TPU v7x, 32 devices: a whole 2x2x4 slice. The times are simulated.
32 devices in a mesh: pb: 4 (over z), ka: 8 (over y, x, core).
Axes of the slice: x: 2, y: 2, z: 4, core: 2. Of those that a mesh axis runs over, the one named last changes fastest.
Arguments:
- queries: bfloat16 [4096, 2048], P('pb'), may hold values from -8 to 8
- keys: bfloat16 [4096, 2048], P(('ka', 'pb')), may hold values from -8 to 8
- values: bfloat16 [4096, 2048], P(('ka', 'pb')), may hold values from -6 to 6
- block_mask: int32 [32, 32], P('pb', 'ka'), may hold values from 0 to 1, as said below
Outputs:
- attended: bfloat16 [4096, 2048], P('pb')
Inputs may be any that keep to these rules, and one draw needn't show every extreme that they name: `block_mask`: 1 where the two blocks are equal or adjacent, in the first 2 block rows and block columns, and for 3 block columns drawn for each block row; 0 elsewhere.
All inputs are finite; a program needn't handle non-finite values.
Results may differ from a plain program's by a relative error of at most 0.0047.
Values may be sent and summed in bfloat16 or wider, within the bound.
No kernel may reach another device: no remote copies, remote signals or barrier semaphores. Data moves between devices by JAX's collectives and lax.ppermute only.
A program may use at most 128 MiB of HBM per device.

v0:
```python
import jax
import jax.numpy as jnp
from jax import lax
from jax.sharding import PartitionSpec as P

HEADS = 16
HEAD_DIM = 128
BLOCK = 128


NEG = -1e30


def normalize_rows(numer, totals):
    row_count = numer.shape[0]
    shaped = numer.reshape(row_count, HEADS, HEAD_DIM) / totals[:, :, None]
    return shaped.reshape(row_count, HEADS * HEAD_DIM).astype(jnp.bfloat16)


def local(queries, keys, values, block_mask):
    key_panel, value_panel = (
        lax.all_gather(keys, "pb", axis=0, tiled=True),
        lax.all_gather(values, "pb", axis=0, tiled=True),
    )
    query_rows = queries.shape[0]
    allowed = jnp.repeat(jnp.repeat(block_mask > 0, BLOCK, axis=0), BLOCK, axis=1)
    scale = HEAD_DIM ** (-0.5)

    def head_scores(head_index):
        start = head_index * HEAD_DIM
        q_head = lax.dynamic_slice_in_dim(queries, start, HEAD_DIM, 1)
        k_head = lax.dynamic_slice_in_dim(key_panel, start, HEAD_DIM, 1)
        product = lax.dot_general(
            q_head, k_head, (((1,), (1,)), ((), ())), preferred_element_type=jnp.float32
        )
        return product * scale

    def local_top(scores):
        return jnp.max(jnp.where(allowed, scores, NEG), axis=1, keepdims=True)

    def accumulate(head_index, scores, head_top, numer, totals):
        weights = jnp.where(allowed, jnp.exp(scores - head_top), 0.0)
        totals = lax.dynamic_update_slice_in_dim(
            totals, jnp.sum(weights, axis=1, keepdims=True), head_index, 1
        )
        v_head = lax.dynamic_slice_in_dim(value_panel, head_index * HEAD_DIM, HEAD_DIM, 1)
        head_out = jnp.dot(weights.astype(jnp.bfloat16), v_head, preferred_element_type=jnp.float32)
        numer = lax.dynamic_update_slice_in_dim(numer, head_out, head_index * HEAD_DIM, 1)
        return (numer, totals)

    start_numer = jnp.zeros((query_rows, HEADS * HEAD_DIM), jnp.float32)
    start_totals = jnp.zeros((query_rows, HEADS), jnp.float32)

    def top_step(head_index, row_tops):
        largest = local_top(head_scores(head_index))
        return lax.dynamic_update_slice_in_dim(row_tops, largest, head_index, 1)

    row_tops = lax.fori_loop(0, HEADS, top_step, jnp.zeros((query_rows, HEADS), jnp.float32))
    row_tops = lax.pmax(row_tops, "ka")

    def value_step(head_index, carry):
        numer, totals = carry
        scores = head_scores(head_index)
        head_top = lax.dynamic_slice_in_dim(row_tops, head_index, 1, 1)
        return accumulate(head_index, scores, head_top, numer, totals)

    numer, totals = lax.fori_loop(0, HEADS, value_step, (start_numer, start_totals))
    numer, totals = lax.psum((numer, totals), "ka")
    return normalize_rows(numer, totals)


def solution(mesh):
    return jax.shard_map(
        local,
        mesh=mesh,
        in_specs=(P("pb", None), P(("ka", "pb"), None), P(("ka", "pb"), None), P("pb", "ka")),
        out_specs=P("pb", None),
        check_vma=False,
    )
```

profile of v0, /device:TPU:0, one launch (start us, length us, event | category | flops | bytes accessed | tf_op | source)
XLA Modules:
  0.0 382.9 jit_solution(3565778699795455772)
XLA Ops:
  8.8 48.8 %all-gather.3.cloned.1.call-done = bf16[512,2048]{1,0:T(8,128)(2,1)} async-done(((bf16[128,2048]{1,0:T(8,128)(2,1)}), bf16[512,2048]{1,0:T(8,128)(2,1)}) %all-gather.3.cloned.1.call-update) | async-done | bytes 2097168 | tf_op jit(solution)/shard_map/all_gather | solution.py:22
  57.6 25.4 %while.30 = (s32[]{:T(128)}, f32[1024,16]{0,1:T(8,128)S(1)}, bf16[1024,2048]{1,0:T(8,128)(2,1)}, bf16[512,2048]{1,0:T(8,128)(2,1)}, pred[1024,4]{0,1:T(4,128)(4,...) while((s32[]{:T(128)}, f32[1024,16]{0,1:T(8,128)S(1)}, bf16[1024,2048]{1,0:T(8,128)(2,1)}, ...), condition=%wide.region_2.3_spmd.clone, body=%wide.region_0.2_spmd.clone.sunk | while | flops 135789568 | bytes 410775 | solution.py:58
  83.7 20.2 %all-gather.5.cloned.1.call-done = bf16[512,2048]{1,0:T(8,128)(2,1)} async-done(((bf16[128,2048]{1,0:T(8,128)(2,1)}), bf16[512,2048]{1,0:T(8,128)(2,1)}) %all-gather.5.cloned.1.call-update) | async-done | bytes 2097168 | tf_op jit(solution)/shard_map/all_gather | solution.py:23
  103.8 54.3 %all-reduce.4.cloned.1.call-done = f32[1024,16]{0,1:T(8,128)} async-done(((f32[1024,16]{0,1:T(8,128)}), f32[1024,16]{0,1:T(8,128)}) %all-reduce.4.cloned.1.call-update) | async-done | bytes 65552 | tf_op jit(solution)/shard_map/pmax | solution.py:59
  158.2 4.3 %broadcast_in_dim.39 = f32[1024,2048]{1,0:T(8,128)} broadcast(f32[]{:T(128)} %constant.103.clone.1), dimensions={} | broadcast | bytes 8388612 | tf_op jit(solution)/shard_map/broadcast_in_dim | solution.py:51
  162.4 76.1 %while.31 = (s32[]{:T(128)}, f32[1024,2048]{1,0:T(8,128)}, f32[1024,16]{0,1:T(8,128)S(1)}, bf16[1024,2048]{1,0:T(8,128)(2,1)}, bf16[512,2048]{1,0:T(8,128)(2,1)}...) while((s32[]{:T(128)}, f32[1024,2048]{1,0:T(8,128)}, ...), condition=%wide.region_6.7_spmd.clone, body=%wide.region_4.6_spmd.clone.sunk | while | flops 271055872 | bytes 3176627 | solution.py:67
  165.0 2.2 convolution_dynamic-update-slice_fusion.2
  169.7 2.2 convolution_dynamic-update-slice_fusion.2
  174.5 2.2 convolution_dynamic-update-slice_fusion.2
  179.2 2.2 convolution_dynamic-update-slice_fusion.2
  184.0 2.3 convolution_dynamic-update-slice_fusion.2
  193.5 2.2 convolution_dynamic-update-slice_fusion.2
  198.2 2.2 convolution_dynamic-update-slice_fusion.2
  203.0 2.2 convolution_dynamic-update-slice_fusion.2
  207.7 2.2 convolution_dynamic-update-slice_fusion.2
  212.5 2.3 convolution_dynamic-update-slice_fusion.2
  217.3 2.2 convolution_dynamic-update-slice_fusion.2
  222.1 2.2 convolution_dynamic-update-slice_fusion.2
  226.8 2.2 convolution_dynamic-update-slice_fusion.2
  231.5 2.2 convolution_dynamic-update-slice_fusion.2
  236.3 2.2 convolution_dynamic-update-slice_fusion.2
  239.2 127.5 %all-reduce.6.cloned.1.call-done = (f32[1024,2048]{1,0:T(8,128)}, f32[1024,16]{0,1:T(8,128)}) async-done(((f32[1024,2048]{1,0:T(8,128)}, f32[1024,16]{0,1:T(8,128)}), (f32[1024,2048]{1,0:T(8,128)}, f32[1024,16]{0,1:T(8,128)})) %all-reduce.6.cloned.1.call-update) | async-done | bytes 8454160 | tf_op jit(solution)/shard_map/psum | solution.py:68
  367.8 2.3 div.11
  371.2 5.2 %fusion.13 = bf16[1024,2048]{1,0:T(8,128)(2,1)} fusion(f32[1024,2048]{1,0:T(8,128)S(1)} %copy-done, f32[128,8,16,128]{3,2,1,0:T(8,128)S(1)} %bitcast.30), kind=kLoop, calls=%fused_computation.16 | loop fusion | flops 4194304 | bytes 20971520 | tf_op jit(solution)/shard_map/convert_element_type | solution.py:17
  (101 shorter events, 72.8 us)
Async XLA Ops:
  6.5 51.1 %all-gather.3.cloned.1.call-start = ((), (), s32[]{:S(2)}) async-start(), calls=%async_computation | async-start | bytes 2621440 | tf_op jit(solution)/shard_map/all_gather | solution.py:22
  7.3 96.6 %all-gather.5.cloned.1.call-start = ((), (), s32[]{:S(2)}) async-start(), calls=%async_computation.2 | async-start | bytes 2621440 | tf_op jit(solution)/shard_map/all_gather | solution.py:23
  8.0 150.1 %all-reduce.4.cloned.1.call-start = ((), (), s32[]{:S(2)}) async-start(), calls=%async_computation.1 | async-start | bytes 131072 | tf_op jit(solution)/shard_map/pmax | solution.py:59
  83.0 0.6 copy-start.2
  83.6 283.1 %all-reduce.6.cloned.1.call-start = ((), (), s32[]{:S(2)}) async-start(), calls=%async_computation.3 | async-start | bytes 16908288 | tf_op jit(solution)/shard_map/psum | solution.py:68
  238.6 0.6 copy-start.1
  367.8 3.4 copy-start
Sparse Core Ops, SparseCore 0:
  8.9 48.6 all-gather.2
  59.2 44.6 all-gather.4
  106.9 51.2 all-reduce.3
  239.3 127.3 all-reduce.5
where the time goes:
time: 385 us; the launch traced here: 383 us
  waiting for transfers between devices  252 us (65%)
  matrix products  84.9 us (22%)
  local copies, waits for them, and re-layouts  25.8 us (7%)
  between operations  13.2 us (3%)
  other arithmetic  5.87 us (2%)
    psum x1, waiting for transfers between devices, local(): numer, totals = lax.psum((numer, totals), 'ka')  128 us
    pmax x1, waiting for transfers between devices, local(): row_tops = lax.pmax(row_tops, 'ka')  54.3 us
    dot_general x32, matrix products, head_scores(): lax.dot_general(q_head, k_head, (((1,), (1,)), ((), ())), preferred_eleme...  49.2 us
    all_gather x1, waiting for transfers between devices, local(): lax.all_gather(keys, 'pb', axis=0, tiled=True)  48.8 us
    dot_general x16, matrix products, accumulate(): jnp.dot(weights.astype(jnp.bfloat16), v_head, preferred_element_type=jnp....  35.7 us
    all_gather x1, waiting for transfers between devices, local(): lax.all_gather(values, 'pb', axis=0, tiled=True)  20.2 us
    dynamic_slice x16, local copies, waits for them, and re-layouts, value_step(): head_top = lax.dynamic_slice_in_dim(row_tops, head_index, 1, 1)  12.2 us
  transfers between devices with their start and end apart: 4, of which 4 were waited for; matrix products, arithmetic and copies ran while one was open for 7% of the time, Pallas kernels for 0%

commit v1 on v0

v1 whole, which is shorter than its diff:
```python
import functools
import math

import jax
import jax.numpy as jnp
from jax import lax
from jax.experimental import pallas as pl
from jax.experimental.pallas import tpu as pltpu
from jax.sharding import PartitionSpec as P

HEADS = 16
HEAD_DIM = 128
BLOCK = 128
NEG = -1e30
EXP2_SCALE = math.log2(math.e) / math.sqrt(HEAD_DIM)
VMEM_BYTES = 40 * 1024 * 1024

VMEM = pl.BlockSpec(memory_space=pltpu.VMEM)
SMEM = pl.BlockSpec(memory_space=pltpu.SMEM)
ANY = pl.BlockSpec(memory_space=pl.ANY)


def params():
    return pltpu.CompilerParams(vmem_limit_bytes=VMEM_BYTES)


def pack_kernel(n_ka, heads, me_ref, k_ref, v_ref, *out_refs):
    key_blocks = k_ref.shape[0] // BLOCK
    for c in range(heads):
        for k in range(n_ka):
            col = pl.multiple_of(((me_ref[0] ^ k) * heads + c) * HEAD_DIM, HEAD_DIM)
            for t in range(key_blocks):
                rows = slice(t * BLOCK, (t + 1) * BLOCK)
                out_refs[c][k, 0, t] = k_ref[rows, pl.ds(col, HEAD_DIM)]
                out_refs[c][k, 1, t] = v_ref[rows, pl.ds(col, HEAD_DIM)].T


def pack(me, keys, values, n_ka, heads):
    key_blocks = keys.shape[0] // BLOCK
    shape = jax.ShapeDtypeStruct((n_ka, 2, key_blocks, BLOCK, HEAD_DIM), keys.dtype)
    return pl.pallas_call(
        functools.partial(pack_kernel, n_ka, heads),
        out_shape=[shape] * heads,
        in_specs=[SMEM, VMEM, VMEM],
        out_specs=[VMEM] * heads,
        compiler_params=params(),
        name="pack",
    )(me, keys, values)


def attend_kernel(deltas, first, last, n_pb, info_ref, mask_ref, q_ref, *refs):
    n_src = len(deltas)
    kv_refs, refs = refs[:n_src], refs[n_src:]
    if not first:
        (m_in, l_in, acc_in), refs = refs[:3], refs[3:]
    if last:
        (out_ref,), refs = refs[:1], refs[1:]
    else:
        (m_out, l_out, acc_out), refs = refs[:3], refs[3:]
    kv, live, sems = refs
    copies = [pltpu.make_async_copy(kv_refs[s], kv.at[s], sems.at[s]) for s in range(n_src)]
    for copy in copies:
        copy.start()
    rows = q_ref.shape[0] // BLOCK
    n_slots, key_blocks = kv.shape[1], kv.shape[3]
    pb = info_ref[0]
    for copy in copies:
        copy.wait()

    def row_step(r, _):
        count = jnp.int32(0)
        for s, delta in enumerate(deltas):
            j = pb + delta
            inside = ((j >= 0) & (j < n_pb)).astype(jnp.int32)
            j = jnp.clip(j, 0, n_pb - 1)
            for slot in range(n_slots):
                for t in range(key_blocks):
                    live[count] = (s * n_slots + slot) * key_blocks + t
                    column = j * key_blocks + t
                    count += inside * mask_ref[(slot * rows + r) * (n_pb * key_blocks) + column]
        live[count] = 0
        q = q_ref[pl.ds(pl.multiple_of(r * BLOCK, BLOCK), BLOCK), :]

        def block(i):
            index = live[i]
            t, index = index % key_blocks, index // key_blocks
            s, slot = index // n_slots, index % n_slots
            return s, slot, t

        def pair_step(i, carry):
            m, l, acc = carry
            s0, slot0, t0 = block(2 * i)
            s1, slot1, t1 = block(2 * i + 1)
            nt = (((1,), (1,)), ((), ()))
            nn = (((1,), (0,)), ((), ()))
            f32 = jnp.float32
            x0 = lax.dot_general(kv[s0, slot0, 0, t0], q, nt, preferred_element_type=f32)
            x1 = lax.dot_general(kv[s1, slot1, 0, t1], q, nt, preferred_element_type=f32)
            x1 = jnp.where(2 * i + 1 < count, x1, NEG)
            top = jnp.max(jnp.maximum(x0, x1), axis=0, keepdims=True)
            m_new = jnp.maximum(m, top)
            alpha = jnp.exp2((m - m_new) * EXP2_SCALE)
            w0 = jnp.exp2((x0 - m_new) * EXP2_SCALE)
            w1 = jnp.exp2((x1 - m_new) * EXP2_SCALE)
            l = l * alpha + jnp.sum(w0 + w1, axis=0, keepdims=True)
            bf16 = jnp.bfloat16
            acc = acc * alpha
            acc += lax.dot_general(kv[s0, slot0, 1, t0], w0.astype(bf16), nn, preferred_element_type=f32)
            acc += lax.dot_general(kv[s1, slot1, 1, t1], w1.astype(bf16), nn, preferred_element_type=f32)
            return m_new, l, acc

        if first:
            carry = (
                jnp.full((1, BLOCK), NEG, jnp.float32),
                jnp.zeros((1, BLOCK), jnp.float32),
                jnp.zeros((HEAD_DIM, BLOCK), jnp.float32),
            )
        else:
            carry = (m_in[r], l_in[r], acc_in[r])
        m, l, acc = lax.fori_loop(0, (count + 1) // 2, pair_step, carry)
        if last:
            done = (acc / l).T.astype(out_ref.dtype)
            out_ref[pl.ds(pl.multiple_of(r * BLOCK, BLOCK), BLOCK), :] = done
        else:
            m_out[r], l_out[r], acc_out[r] = m, l, acc
        return 0

    lax.fori_loop(0, rows, row_step, 0)


def attend(info, mask, q, sources, deltas, state, last, n_pb, name):
    rows = q.shape[0] // BLOCK
    first = state is None
    state = () if first else state
    stat = jax.ShapeDtypeStruct((rows, 1, BLOCK), jnp.float32)
    if last:
        out_shape = [jax.ShapeDtypeStruct(q.shape, q.dtype)]
    else:
        out_shape = [stat, stat, jax.ShapeDtypeStruct((rows, HEAD_DIM, BLOCK), jnp.float32)]
    shape = sources[0].shape
    blocks = len(deltas) * shape[0] * shape[2]
    return pl.pallas_call(
        functools.partial(attend_kernel, deltas, first, last, n_pb),
        out_shape=out_shape,
        in_specs=[SMEM, SMEM, VMEM] + [ANY] * len(sources) + [VMEM] * len(state),
        out_specs=[VMEM] * len(out_shape),
        scratch_shapes=[
            pltpu.VMEM((len(sources),) + shape, q.dtype),
            pltpu.SMEM((blocks + 1,), jnp.int32),
            pltpu.SemaphoreType.DMA((len(sources),)),
        ],
        compiler_params=params(),
        cost_estimate=pl.CostEstimate(
            flops=rows * blocks * 4 * BLOCK * BLOCK * HEAD_DIM,
            bytes_accessed=4 * q.size,
            transcendentals=rows * blocks * BLOCK * BLOCK,
        ),
        name=name,
    )(info, mask, q, *sources, *state)


def place_kernel(n_ka, heads, c, me_ref, *refs):
    pieces, out_ref, sems = refs[:n_ka], refs[-2], refs[-1]
    copies = []
    for k in range(n_ka):
        col = pl.multiple_of(((me_ref[0] ^ k) * heads + c) * HEAD_DIM, HEAD_DIM)
        copies.append(pltpu.make_async_copy(pieces[k], out_ref.at[:, pl.ds(col, HEAD_DIM)], sems.at[k]))
    for copy in copies:
        copy.start()
    for copy in copies:
        copy.wait()


def place(me, pieces, whole, c, heads):
    n_ka = len(pieces)
    rows = pieces[0].shape[0]
    extra = () if whole is None else (whole,)
    return pl.pallas_call(
        functools.partial(place_kernel, n_ka, heads, c),
        out_shape=jax.ShapeDtypeStruct((rows, HEADS * HEAD_DIM), pieces[0].dtype),
        in_specs=[SMEM] + [ANY] * (n_ka + len(extra)),
        out_specs=ANY,
        scratch_shapes=[pltpu.SemaphoreType.DMA((n_ka,))],
        input_output_aliases={1 + n_ka: 0} if extra else {},
        compiler_params=params(),
        name="place",
    )(me, *pieces, *extra)


def local(n_pb, n_ka, queries, keys, values, block_mask):
    heads = HEADS // n_ka
    me = lax.axis_index("ka").astype(jnp.int32)
    pb = lax.axis_index("pb").astype(jnp.int32)
    me1, pb1 = me[None], pb[None]

    def swap(x, k):
        return lax.ppermute(x, "ka", [(i, i ^ k) for i in range(n_ka)])

    def move(x, step):
        hops = [(i, i + step) for i in range(n_pb) if 0 <= i + step < n_pb]
        return lax.ppermute(x, "pb", hops)

    mask = block_mask[None]
    bit = 1
    while bit < n_ka:
        mask = jnp.concatenate([mask, swap(mask, bit)])
        bit *= 2
    mask = mask.reshape((n_ka // 2, 2) + block_mask.shape).swapaxes(0, 1).reshape(-1)

    packed = pack(me1, keys, values, n_ka, heads)

    outs = None
    whole = None
    owns = []
    for c in range(heads):
        msgs = packed[c]
        mixed = [msgs[:2]] + [swap(msgs[k : k + 2], k) for k in range(2, n_ka, 2)]
        theirs = swap(jnp.stack([x[1] for x in mixed]), 1)
        owns.append(jnp.concatenate([jnp.stack([x[0] for x in mixed]), theirs]))

    for c in range(heads):
        q = lax.dynamic_slice_in_dim(queries, (me * heads + c) * HEAD_DIM, HEAD_DIM, 1)
        own = owns[c]
        from_left, from_right = own, own
        state = None
        sources, deltas = [own], [0]
        for step in range(1, n_pb):
            from_left, from_right = move(from_left, 1), move(from_right, -1)
            sources, deltas = sources + [from_left, from_right], deltas + [-step, step]
            state = attend(
                pb1, mask, q, sources, tuple(deltas), state, step == n_pb - 1, n_pb, f"attend_{c}_{step}"
            )
            sources, deltas = [], []
        (out,) = state
        pieces = [out] + [swap(out, k) for k in range(2, n_ka, 2)]
        others = [swap(x, 1) for x in pieces]
        pieces = [x for two in zip(pieces, others) for x in two]
        whole = place(me1, pieces, whole, c, heads)
    return whole


def solution(mesh):
    n_pb, n_ka = mesh.shape["pb"], mesh.shape["ka"]
    return jax.shard_map(
        functools.partial(local, n_pb, n_ka),
        mesh=mesh,
        in_specs=(P("pb", None), P(("ka", "pb"), None), P(("ka", "pb"), None), P("pb", "ka")),
        out_specs=P("pb", None),
        check_vma=False,
    )
```

time: 385 us -> 154 us (0.40)
  waiting for transfers between devices: 252 us -> 34.8 us
  matrix products: 84.9 us -> 0 us
  starting transfers between devices: 0.12 us -> 58.7 us
  Pallas kernels: 0 us -> 56.6 us
  local copies, waits for them, and re-layouts: 25.8 us -> 3.64 us
  between operations: 13.2 us -> 0.37 us
  other arithmetic: 5.87 us -> 0.09 us
    psum x1 -> x0, waiting for transfers between devices: 128 us -> none  [local(): numer, totals = lax.psum((numer, totals), 'ka')]
    dot_general x48 -> x0, matrix products: 84.9 us -> none  [the longest x32 49.2 us: head_scores(): lax.dot_general(q_head, k_head, (((1,), (1,)), ((), ())), preferred_eleme...]
    all_gather x2 -> x0, waiting for transfers between devices: 68.9 us -> none  [the longest x1 48.8 us: local(): lax.all_gather(keys, 'pb', axis=0, tiled=True)]
    ppermute x0 -> x37, starting transfers between devices: none -> 58.7 us  [the longest x12 37.9 us: move(): return lax.ppermute(x, 'pb', hops)]
    pallas_call x0 -> x9, Pallas kernels: none -> 56.6 us  [the longest x6 53.5 us: attend(): pl.pallas_call(functools.partial(attend_kernel, deltas, first, last, n_pb...]
    pmax x1 -> x0, waiting for transfers between devices: 54.3 us -> none  [local(): row_tops = lax.pmax(row_tops, 'ka')]
    ppermute x0 -> x37, waiting for transfers between devices: none -> 34.8 us  [the longest x25 23.7 us: swap(): return lax.ppermute(x, 'ka', [(i, i ^ k) for i in range(n_ka)])]
    dynamic_slice x16 -> x1, local copies, waits for them, and re-layouts: 12.2 us -> 1.07 us  [local(): lax.dynamic_slice_in_dim(queries, (me * heads + c) * HEAD_DIM, HEAD_DIM, 1)]
  transfers between devices with their start and end apart: 4 -> 37, of which waited for: 4 -> 15; matrix products, arithmetic and copies ran while one was open for 7% -> 1% of each run, Pallas kernels for 0% -> 36%
where the time goes in v1:
time: 154 us
  starting transfers between devices  58.7 us (38%)
  Pallas kernels  56.6 us (37%)
  waiting for transfers between devices  34.8 us (23%)
  local copies, waits for them, and re-layouts  3.64 us (2%)
    pallas_call x6, Pallas kernels, attend(): pl.pallas_call(functools.partial(attend_kernel, deltas, first, last, n_pb...  53.5 us
    ppermute x12, starting transfers between devices, move(): return lax.ppermute(x, 'pb', hops)  37.9 us
    ppermute x25, waiting for transfers between devices, swap(): return lax.ppermute(x, 'ka', [(i, i ^ k) for i in range(n_ka)])  23.7 us
    ppermute x25, starting transfers between devices, swap(): return lax.ppermute(x, 'ka', [(i, i ^ k) for i in range(n_ka)])  20.8 us
    ppermute x12, waiting for transfers between devices, move(): return lax.ppermute(x, 'pb', hops)  11.1 us
  transfers between devices with their start and end apart: 37, of which 15 were waited for; matrix products, arithmetic and copies ran while one was open for 1% of the time, Pallas kernels for 36%

profile of v1, /device:TPU:0, one launch (start us, length us, event | category | flops | bytes accessed | tf_op | source)
XLA Modules:
  0.0 154.2 jit_solution(13296810805737658978)
XLA Ops:
  2.5 4.0 %collective-permute-start.5 = (bf16[2,2,1,128,128]{4,3,2,1,0:T(8,128)(2,1)S(1)}, bf16[2,2,1,128,128]{4,3,2,1,0:T(8,128)(2,1)S(1)}, u32[]{:S(2)}, u32[]{:S(2)}) collective-permute-start(bf16[2,2,1,128,128]{4,3,2,1,0:T(8,128)(2,1)S(1)} %get-tuple-element.42), channel_id=1, source_target_pairs={{0,6},{1,7},{2,4},{3,5},{4,2},{5,3},{6,0},{7,1},{8,14},{9,15},{10,... | collective-permute-start | bytes 393224 | tf_op jit(solution)/shard_map/ppermute | solution.py:197
  7.1 2.9 %collective-permute-start.22 = (bf16[2,2,1,128,128]{4,3,2,1,0:T(8,128)(2,1)S(1)}, bf16[2,2,1,128,128]{4,3,2,1,0:T(8,128)(2,1)S(1)}, u32[]{:S(2)}, u32[]{:S(2)}) collective-permute-start(bf16[2,2,1,128,128]{4,3,2,1,0:T(8,128)(2,1)S(1)} %get-tuple-element.37), channel_id=1, source_target_pairs={{0,6},{1,7},{2,4},{3,5},{4,2},{5,3},{6,0},{7,1},{8,14},{9,15},{10,... | collective-permute-start | bytes 393224 | tf_op jit(solution)/shard_map/ppermute | solution.py:197
  10.5 3.6 %collective-permute-done.3 = bf16[2,2,1,128,128]{4,3,2,1,0:T(8,128)(2,1)S(1)} collective-permute-done((bf16[2,2,1,128,128]{4,3,2,1,0:T(8,128)(2,1)S(1)}, bf16[2,2,1,128,128]{4,3,2,1,0:T(8,128)(2,1)S(1)}, u32[]{:S(2)}, u32[]{:S(2)}) %collective-permute-start.3) | collective-permute-done | bytes 131104 | tf_op jit(solution)/shard_map/ppermute | solution.py:197
  15.8 3.3 %collective-permute-done.20 = bf16[2,2,1,128,128]{4,3,2,1,0:T(8,128)(2,1)S(1)} collective-permute-done((bf16[2,2,1,128,128]{4,3,2,1,0:T(8,128)(2,1)S(1)}, bf16[2,2,1,128,128]{4,3,2,1,0:T(8,128)(2,1)S(1)}, u32[]{:S(2)}, u32[]{:S(2)}) %collective-permute-start.20) | collective-permute-done | bytes 131104 | tf_op jit(solution)/shard_map/ppermute | solution.py:197
  20.7 5.4 %collective-permute-start.7 = (bf16[8,2,1,128,128]{4,3,2,1,0:T(8,128)(2,1)S(1)}, bf16[8,2,1,128,128]{4,3,2,1,0:T(8,128)(2,1)}, u32[]{:S(2)}, u32[]{:S(2)}) collective-permute-start(bf16[8,2,1,128,128]{4,3,2,1,0:T(8,128)(2,1)S(1)} %constant_dynamic-update-slice_fusion.refs_0_), channel_id=1, source_target_pairs={{0,8},{8,16},{16,24},{1,9},{9,17},{17,25},{2,10},{10,18},{18,26},{... | collective-permute-start | bytes 1572872 | tf_op jit(solution)/shard_map/ppermute | solution.py:201
  27.4 5.3 %collective-permute-start.24 = (bf16[8,2,1,128,128]{4,3,2,1,0:T(8,128)(2,1)S(1)}, bf16[8,2,1,128,128]{4,3,2,1,0:T(8,128)(2,1)}, u32[]{:S(2)}, u32[]{:S(2)}) collective-permute-start(bf16[8,2,1,128,128]{4,3,2,1,0:T(8,128)(2,1)S(1)} %constant_dynamic-update-slice_fusion.1.refs_0_), channel_id=1, source_target_pairs={{0,8},{8,16},{16,24},{1,9},{9,17},{17,25},{2,10},{10,18},{18,26},{... | collective-permute-start | bytes 1572872 | tf_op jit(solution)/shard_map/ppermute | solution.py:201
  32.7 3.3 %collective-permute-done.10.refs_2_ = bf16[8,2,1,128,128]{4,3,2,1,0:T(8,128)(2,1)S(1)} collective-permute-done((bf16[8,2,1,128,128]{4,3,2,1,0:T(8,128)(2,1)S(1)}, bf16[8,2,1,128,128]{4,3,2,1,0:T(8,128)(2,1)S(1)}, u32[]{:S(2)}, u32[]{:S(2)}) %collective-permute-start.10) | collective-permute-done | bytes 524320 | tf_op jit(solution)/shard_map/ppermute | solution.py:201
  37.5 5.3 %collective-permute-start.8 = (bf16[8,2,1,128,128]{4,3,2,1,0:T(8,128)(2,1)}, bf16[8,2,1,128,128]{4,3,2,1,0:T(8,128)(2,1)}, u32[]{:S(2)}, u32[]{:S(2)}) collective-permute-start(bf16[8,2,1,128,128]{4,3,2,1,0:T(8,128)(2,1)} %collective-permute-done.7.refs_1_), channel_id=1, source_target_pairs={{0,8},{8,16},{16,24},{1,9},{9,17},{17,25},{2,10},{10,18},{18,26},{... | collective-permute-start | bytes 1572872 | tf_op jit(solution)/shard_map/ppermute | solution.py:201
  42.8 4.6 %collective-permute-done.27.refs_2_ = bf16[8,2,1,128,128]{4,3,2,1,0:T(8,128)(2,1)} collective-permute-done((bf16[8,2,1,128,128]{4,3,2,1,0:T(8,128)(2,1)S(1)}, bf16[8,2,1,128,128]{4,3,2,1,0:T(8,128)(2,1)}, u32[]{:S(2)}, u32[]{:S(2)}) %collective-permute-start.27) | collective-permute-done | bytes 524320 | tf_op jit(solution)/shard_map/ppermute | solution.py:201
  48.7 4.5 %collective-permute-start.25 = (bf16[8,2,1,128,128]{4,3,2,1,0:T(8,128)(2,1)}, bf16[8,2,1,128,128]{4,3,2,1,0:T(8,128)(2,1)S(1)}, u32[]{:S(2)}, u32[]{:S(2)}) collective-permute-start(bf16[8,2,1,128,128]{4,3,2,1,0:T(8,128)(2,1)} %collective-permute-done.24.refs_1_), channel_id=1, source_target_pairs={{0,8},{8,16},{16,24},{1,9},{9,17},{17,25},{2,10},{10,18},{18,26},{... | collective-permute-start | bytes 1572872 | tf_op jit(solution)/shard_map/ppermute | solution.py:201
  56.0 2.1 %collective-permute-done.1 = s32[2,8,4]{1,2,0:T(4,128)S(1)} collective-permute-done((s32[2,8,4]{1,2,0:T(4,128)S(1)}, s32[2,8,4]{1,2,0:T(4,128)S(1)}, u32[]{:S(2)}, u32[]{:S(2)}) %collective-permute-start.1) | collective-permute-done | bytes 288 | tf_op jit(solution)/shard_map/ppermute | solution.py:197
  61.4 5.4 %collective-permute-start.9 = (bf16[8,2,1,128,128]{4,3,2,1,0:T(8,128)(2,1)}, bf16[8,2,1,128,128]{4,3,2,1,0:T(8,128)(2,1)}, u32[]{:S(2)}, u32[]{:S(2)}) collective-permute-start(bf16[8,2,1,128,128]{4,3,2,1,0:T(8,128)(2,1)} %collective-permute-done.8.refs_0_), channel_id=1, source_target_pairs={{0,8},{8,16},{16,24},{1,9},{9,17},{17,25},{2,10},{10,18},{18,26},{... | collective-permute-start | bytes 1572872 | tf_op jit(solution)/shard_map/ppermute | solution.py:201
  67.0 2.7 %collective-permute-done.28.refs_1_ = bf16[8,2,1,128,128]{4,3,2,1,0:T(8,128)(2,1)S(1)} collective-permute-done((bf16[8,2,1,128,128]{4,3,2,1,0:T(8,128)(2,1)}, bf16[8,2,1,128,128]{4,3,2,1,0:T(8,128)(2,1)S(1)}, u32[]{:S(2)}, u32[]{:S(2)}) %collective-permute-start.28) | collective-permute-done | bytes 524320 | tf_op jit(solution)/shard_map/ppermute | solution.py:201
  71.3 4.3 %collective-permute-start.26 = (bf16[8,2,1,128,128]{4,3,2,1,0:T(8,128)(2,1)S(1)}, bf16[8,2,1,128,128]{4,3,2,1,0:T(8,128)(2,1)S(1)}, u32[]{:S(2)}, u32[]{:S(2)}) collective-permute-start(bf16[8,2,1,128,128]{4,3,2,1,0:T(8,128)(2,1)S(1)} %collective-permute-done.25.refs_0_), channel_id=1, source_target_pairs={{0,8},{8,16},{16,24},{1,9},{9,17},{17,25},{2,10},{10,18},{18,26},{... | collective-permute-start | bytes 1572872 | tf_op jit(solution)/shard_map/ppermute | solution.py:201
  75.6 12.8 %attend_1_1.1 = (f32[8,1,128]{2,1,0:T(1,128)S(1)}, f32[8,1,128]{2,1,0:T(1,128)S(1)}, f32[8,128,128]{2,1,0:T(8,128)S(1)}) custom-call(s32[1]{0:T(128)} %bitcast.1.info_ref, s32[256]{0:T(256)S(1)} %reshape.7.mask_ref, bf16[1024,128]{1,0:T(8,128)(2,1)S(1)} %get-tuple-element.34.q_ref, ...), custom_call_target="tpu_custom_call" | custom-call | flops 1610612736 | bytes 524288 | tf_op jit(solution)/shard_map/attend_1_1/pallas_call | solution.py:142
  88.4 12.9 %attend_0_1.1 = (f32[8,1,128]{2,1,0:T(1,128)S(1)}, f32[8,1,128]{2,1,0:T(1,128)S(1)}, f32[8,128,128]{2,1,0:T(8,128)S(1)}) custom-call(s32[1]{0:T(128)} %bitcast.1.info_ref, s32[256]{0:T(256)S(1)} %reshape.7.mask_ref, bf16[1024,128]{1,0:T(8,128)(2,1)S(1)} %get-tuple-element.33.q_ref, ...), custom_call_target="tpu_custom_call" | custom-call | flops 1610612736 | bytes 524288 | tf_op jit(solution)/shard_map/attend_0_1/pallas_call | solution.py:142
  101.3 7.1 %attend_1_2.1 = (f32[8,1,128]{2,1,0:T(1,128)S(1)}, f32[8,1,128]{2,1,0:T(1,128)S(1)}, f32[8,128,128]{2,1,0:T(8,128)S(1)}) custom-call(s32[1]{0:T(128)} %bitcast.1.info_ref, s32[256]{0:T(256)S(1)} %reshape.7.mask_ref, bf16[1024,128]{1,0:T(8,128)(2,1)S(1)} %get-tuple-element.34.q_ref, bf16[8,2,1,128,128]{4,3,2,1,0:T(8,128)(2,1)} %collective-permute-done.8.refs_0_, ...), custom_call_target="tpu_custom_call" | custom-call | flops 1073741824 | bytes 524288 | tf_op jit(solution)/shard_map/attend_1_2/pallas_call | solution.py:142
  108.4 6.0 %attend_0_2.1 = (f32[8,1,128]{2,1,0:T(1,128)S(1)}, f32[8,1,128]{2,1,0:T(1,128)S(1)}, f32[8,128,128]{2,1,0:T(8,128)S(1)}) custom-call(s32[1]{0:T(128)} %bitcast.1.info_ref, s32[256]{0:T(256)S(1)} %reshape.7.mask_ref, bf16[1024,128]{1,0:T(8,128)(2,1)S(1)} %get-tuple-element.33.q_ref, bf16[8,2,1,128,128]{4,3,2,1,0:T(8,128)(2,1)S(1)} %collective-permute-done.25.refs_0_, ...), custom_call_target="tpu_custom_call" | custom-call | flops 1073741824 | bytes 524288 | tf_op jit(solution)/shard_map/attend_0_2/pallas_call | solution.py:142
  114.5 7.9 %attend_1_3.1.refs_0_ = bf16[1024,128]{1,0:T(8,128)(2,1)S(1)} custom-call(s32[1]{0:T(128)} %bitcast.1.info_ref, s32[256]{0:T(256)S(1)} %reshape.7.mask_ref, bf16[1024,128]{1,0:T(8,128)(2,1)S(1)} %get-tuple-element.34.q_ref, bf16[8,2,1,128,128]{4,3,2,1,0:T(8,128)(2,1)} %collective-permute-done.9.refs_0_, ...), custom_call_target="tpu_custom_call" | custom-call | flops 1073741824 | bytes 524288 | tf_op jit(solution)/shard_map/attend_1_3/pallas_call | solution.py:142
  125.4 6.8 %attend_0_3.1.refs_0_ = bf16[1024,128]{1,0:T(8,128)(2,1)S(1)} custom-call(s32[1]{0:T(128)} %bitcast.1.info_ref, s32[256]{0:T(256)S(1)} %reshape.7.mask_ref, bf16[1024,128]{1,0:T(8,128)(2,1)S(1)} %get-tuple-element.33.q_ref, bf16[8,2,1,128,128]{4,3,2,1,0:T(8,128)(2,1)S(1)} %collective-permute-done.26.refs_0_, ...), custom_call_target="tpu_custom_call" | custom-call | flops 1073741824 | bytes 524288 | tf_op jit(solution)/shard_map/attend_0_3/pallas_call | solution.py:142
  136.3 4.4 %collective-permute-done.16.refs_4_ = bf16[1024,128]{1,0:T(8,128)(2,1)S(1)} collective-permute-done((bf16[1024,128]{1,0:T(8,128)(2,1)S(1)}, bf16[1024,128]{1,0:T(8,128)(2,1)S(1)}, u32[]{:S(2)}, u32[]{:S(2)}) %collective-permute-start.16) | collective-permute-done | bytes 262176 | tf_op jit(solution)/shard_map/ppermute | solution.py:197
  140.7 1.7 %collective-permute-done.35.refs_6_ = bf16[1024,128]{1,0:T(8,128)(2,1)S(1)} collective-permute-done((bf16[1024,128]{1,0:T(8,128)(2,1)S(1)}, bf16[1024,128]{1,0:T(8,128)(2,1)S(1)}, u32[]{:S(2)}, u32[]{:S(2)}) %collective-permute-start.35) | collective-permute-done | bytes 262176 | tf_op jit(solution)/shard_map/ppermute | solution.py:197
  142.4 4.7 %collective-permute-done.33.refs_4_ = bf16[1024,128]{1,0:T(8,128)(2,1)S(1)} collective-permute-done((bf16[1024,128]{1,0:T(8,128)(2,1)S(1)}, bf16[1024,128]{1,0:T(8,128)(2,1)S(1)}, u32[]{:S(2)}, u32[]{:S(2)}) %collective-permute-start.33) | collective-permute-done | bytes 262176 | tf_op jit(solution)/shard_map/ppermute | solution.py:197
  147.6 2.2 %collective-permute-done.31.refs_2_ = bf16[1024,128]{1,0:T(8,128)(2,1)S(1)} collective-permute-done((bf16[1024,128]{1,0:T(8,128)(2,1)S(1)}, bf16[1024,128]{1,0:T(8,128)(2,1)S(1)}, u32[]{:S(2)}, u32[]{:S(2)}) %collective-permute-start.31) | collective-permute-done | bytes 262176 | tf_op jit(solution)/shard_map/ppermute | solution.py:197
  (84 shorter events, 30.8 us)
Async XLA Ops:
  2.5 13.2 %collective-permute-start.5 = (bf16[2,2,1,128,128]{4,3,2,1,0:T(8,128)(2,1)S(1)}, bf16[2,2,1,128,128]{4,3,2,1,0:T(8,128)(2,1)S(1)}, u32[]{:S(2)}, u32[]{:S(2)}) collective-permute-start(bf16[2,2,1,128,128]{4,3,2,1,0:T(8,128)(2,1)S(1)} %get-tuple-element.42), channel_id=1, source_target_pairs={{0,6},{1,7},{2,4},{3,5},{4,2},{5,3},{6,0},{7,1},{8,14},{9,15},{10,... | collective-permute-start | bytes 393224 | tf_op jit(solution)/shard_map/ppermute | solution.py:197
  6.4 9.2 %collective-permute-start.4 = (bf16[2,2,1,128,128]{4,3,2,1,0:T(8,128)(2,1)S(1)}, bf16[2,2,1,128,128]{4,3,2,1,0:T(8,128)(2,1)S(1)}, u32[]{:S(2)}, u32[]{:S(2)}) collective-permute-start(bf16[2,2,1,128,128]{4,3,2,1,0:T(8,128)(2,1)S(1)} %get-tuple-element.43), channel_id=1, source_target_pairs={{0,4},{1,5},{2,6},{3,7},{4,0},{5,1},{6,2},{7,3},{8,12},{9,13},{10,... | collective-permute-start | bytes 393224 | tf_op jit(solution)/shard_map/ppermute | solution.py:197
  7.1 12.1 %collective-permute-start.22 = (bf16[2,2,1,128,128]{4,3,2,1,0:T(8,128)(2,1)S(1)}, bf16[2,2,1,128,128]{4,3,2,1,0:T(8,128)(2,1)S(1)}, u32[]{:S(2)}, u32[]{:S(2)}) collective-permute-start(bf16[2,2,1,128,128]{4,3,2,1,0:T(8,128)(2,1)S(1)} %get-tuple-element.37), channel_id=1, source_target_pairs={{0,6},{1,7},{2,4},{3,5},{4,2},{5,3},{6,0},{7,1},{8,14},{9,15},{10,... | collective-permute-start | bytes 393224 | tf_op jit(solution)/shard_map/ppermute | solution.py:197
  10.0 9.1 %collective-permute-start.21 = (bf16[2,2,1,128,128]{4,3,2,1,0:T(8,128)(2,1)S(1)}, bf16[2,2,1,128,128]{4,3,2,1,0:T(8,128)(2,1)S(1)}, u32[]{:S(2)}, u32[]{:S(2)}) collective-permute-start(bf16[2,2,1,128,128]{4,3,2,1,0:T(8,128)(2,1)S(1)} %get-tuple-element.38), channel_id=1, source_target_pairs={{0,4},{1,5},{2,6},{3,7},{4,0},{5,1},{6,2},{7,3},{8,12},{9,13},{10,... | collective-permute-start | bytes 393224 | tf_op jit(solution)/shard_map/ppermute | solution.py:197
  19.4 16.6 %collective-permute-start.10 = (bf16[8,2,1,128,128]{4,3,2,1,0:T(8,128)(2,1)S(1)}, bf16[8,2,1,128,128]{4,3,2,1,0:T(8,128)(2,1)S(1)}, u32[]{:S(2)}, u32[]{:S(2)}) collective-permute-start(bf16[8,2,1,128,128]{4,3,2,1,0:T(8,128)(2,1)S(1)} %constant_dynamic-update-slice_fusion.refs_0_), channel_id=1, source_target_pairs={{8,0},{16,8},{24,16},{9,1},{17,9},{25,17},{10,2},{18,10},{26,18},{... | collective-permute-start | bytes 1572872 | tf_op jit(solution)/shard_map/ppermute | solution.py:201
  20.7 16.8 %collective-permute-start.7 = (bf16[8,2,1,128,128]{4,3,2,1,0:T(8,128)(2,1)S(1)}, bf16[8,2,1,128,128]{4,3,2,1,0:T(8,128)(2,1)}, u32[]{:S(2)}, u32[]{:S(2)}) collective-permute-start(bf16[8,2,1,128,128]{4,3,2,1,0:T(8,128)(2,1)S(1)} %constant_dynamic-update-slice_fusion.refs_0_), channel_id=1, source_target_pairs={{0,8},{8,16},{16,24},{1,9},{9,17},{17,25},{2,10},{10,18},{18,26},{... | collective-permute-start | bytes 1572872 | tf_op jit(solution)/shard_map/ppermute | solution.py:201
  26.1 21.3 %collective-permute-start.27 = (bf16[8,2,1,128,128]{4,3,2,1,0:T(8,128)(2,1)S(1)}, bf16[8,2,1,128,128]{4,3,2,1,0:T(8,128)(2,1)}, u32[]{:S(2)}, u32[]{:S(2)}) collective-permute-start(bf16[8,2,1,128,128]{4,3,2,1,0:T(8,128)(2,1)S(1)} %constant_dynamic-update-slice_fusion.1.refs_0_), channel_id=1, source_target_pairs={{8,0},{16,8},{24,16},{9,1},{17,9},{25,17},{10,2},{18,10},{26,18},{... | collective-permute-start | bytes 1572872 | tf_op jit(solution)/shard_map/ppermute | solution.py:201
  27.4 21.4 %collective-permute-start.24 = (bf16[8,2,1,128,128]{4,3,2,1,0:T(8,128)(2,1)S(1)}, bf16[8,2,1,128,128]{4,3,2,1,0:T(8,128)(2,1)}, u32[]{:S(2)}, u32[]{:S(2)}) collective-permute-start(bf16[8,2,1,128,128]{4,3,2,1,0:T(8,128)(2,1)S(1)} %constant_dynamic-update-slice_fusion.1.refs_0_), channel_id=1, source_target_pairs={{0,8},{8,16},{16,24},{1,9},{9,17},{17,25},{2,10},{10,18},{18,26},{... | collective-permute-start | bytes 1572872 | tf_op jit(solution)/shard_map/ppermute | solution.py:201
  36.0 24.1 %collective-permute-start.11 = (bf16[8,2,1,128,128]{4,3,2,1,0:T(8,128)(2,1)S(1)}, bf16[8,2,1,128,128]{4,3,2,1,0:T(8,128)(2,1)}, u32[]{:S(2)}, u32[]{:S(2)}) collective-permute-start(bf16[8,2,1,128,128]{4,3,2,1,0:T(8,128)(2,1)S(1)} %collective-permute-done.10.refs_2_), channel_id=1, source_target_pairs={{8,0},{16,8},{24,16},{9,1},{17,9},{25,17},{10,2},{18,10},{26,18},{... | collective-permute-start | bytes 1572872 | tf_op jit(solution)/shard_map/ppermute | solution.py:201
  37.5 23.9 %collective-permute-start.8 = (bf16[8,2,1,128,128]{4,3,2,1,0:T(8,128)(2,1)}, bf16[8,2,1,128,128]{4,3,2,1,0:T(8,128)(2,1)}, u32[]{:S(2)}, u32[]{:S(2)}) collective-permute-start(bf16[8,2,1,128,128]{4,3,2,1,0:T(8,128)(2,1)} %collective-permute-done.7.refs_1_), channel_id=1, source_target_pairs={{0,8},{8,16},{16,24},{1,9},{9,17},{17,25},{2,10},{10,18},{18,26},{... | collective-permute-start | bytes 1572872 | tf_op jit(solution)/shard_map/ppermute | solution.py:201
  47.3 22.4 %collective-permute-start.28 = (bf16[8,2,1,128,128]{4,3,2,1,0:T(8,128)(2,1)}, bf16[8,2,1,128,128]{4,3,2,1,0:T(8,128)(2,1)S(1)}, u32[]{:S(2)}, u32[]{:S(2)}) collective-permute-start(bf16[8,2,1,128,128]{4,3,2,1,0:T(8,128)(2,1)} %collective-permute-done.27.refs_2_), channel_id=1, source_target_pairs={{8,0},{16,8},{24,16},{9,1},{17,9},{25,17},{10,2},{18,10},{26,18},{... | collective-permute-start | bytes 1572872 | tf_op jit(solution)/shard_map/ppermute | solution.py:201
  48.7 22.6 %collective-permute-start.25 = (bf16[8,2,1,128,128]{4,3,2,1,0:T(8,128)(2,1)}, bf16[8,2,1,128,128]{4,3,2,1,0:T(8,128)(2,1)S(1)}, u32[]{:S(2)}, u32[]{:S(2)}) collective-permute-start(bf16[8,2,1,128,128]{4,3,2,1,0:T(8,128)(2,1)} %collective-permute-done.24.refs_1_), channel_id=1, source_target_pairs={{0,8},{8,16},{16,24},{1,9},{9,17},{17,25},{2,10},{10,18},{18,26},{... | collective-permute-start | bytes 1572872 | tf_op jit(solution)/shard_map/ppermute | solution.py:201
  58.1 8.7 %collective-permute-start.2 = (s32[4,8,4]{1,2,0:T(4,128)S(1)}, s32[4,8,4]{1,2,0:T(4,128)S(1)}, u32[]{:S(2)}, u32[]{:S(2)}) collective-permute-start(s32[4,8,4]{1,2,0:T(4,128)S(1)} %pad_add_fusion.1), channel_id=1, source_target_pairs={{0,4},{1,5},{2,6},{3,7},{4,0},{5,1},{6,2},{7,3},{8,12},{9,13},{10,... | collective-permute-start | bytes 1544 | tf_op jit(solution)/shard_map/ppermute | solution.py:197
  60.1 54.3 %collective-permute-start.12 = (bf16[8,2,1,128,128]{4,3,2,1,0:T(8,128)(2,1)}, bf16[8,2,1,128,128]{4,3,2,1,0:T(8,128)(2,1)}, u32[]{:S(2)}, u32[]{:S(2)}) collective-permute-start(bf16[8,2,1,128,128]{4,3,2,1,0:T(8,128)(2,1)} %collective-permute-done.11.refs_1_), channel_id=1, source_target_pairs={{8,0},{16,8},{24,16},{9,1},{17,9},{25,17},{10,2},{18,10},{26,18},{... | collective-permute-start | bytes 1572872 | tf_op jit(solution)/shard_map/ppermute | solution.py:201
  61.4 53.0 %collective-permute-start.9 = (bf16[8,2,1,128,128]{4,3,2,1,0:T(8,128)(2,1)}, bf16[8,2,1,128,128]{4,3,2,1,0:T(8,128)(2,1)}, u32[]{:S(2)}, u32[]{:S(2)}) collective-permute-start(bf16[8,2,1,128,128]{4,3,2,1,0:T(8,128)(2,1)} %collective-permute-done.8.refs_0_), channel_id=1, source_target_pairs={{0,8},{8,16},{16,24},{1,9},{9,17},{17,25},{2,10},{10,18},{18,26},{... | collective-permute-start | bytes 1572872 | tf_op jit(solution)/shard_map/ppermute | solution.py:201
  69.7 55.7 %collective-permute-start.29 = (bf16[8,2,1,128,128]{4,3,2,1,0:T(8,128)(2,1)S(1)}, bf16[8,2,1,128,128]{4,3,2,1,0:T(8,128)(2,1)S(1)}, u32[]{:S(2)}, u32[]{:S(2)}) collective-permute-start(bf16[8,2,1,128,128]{4,3,2,1,0:T(8,128)(2,1)S(1)} %collective-permute-done.28.refs_1_), channel_id=1, source_target_pairs={{8,0},{16,8},{24,16},{9,1},{17,9},{25,17},{10,2},{18,10},{26,18},{... | collective-permute-start | bytes 1572872 | tf_op jit(solution)/shard_map/ppermute | solution.py:201
  71.3 54.1 %collective-permute-start.26 = (bf16[8,2,1,128,128]{4,3,2,1,0:T(8,128)(2,1)S(1)}, bf16[8,2,1,128,128]{4,3,2,1,0:T(8,128)(2,1)S(1)}, u32[]{:S(2)}, u32[]{:S(2)}) collective-permute-start(bf16[8,2,1,128,128]{4,3,2,1,0:T(8,128)(2,1)S(1)} %collective-permute-done.25.refs_0_), channel_id=1, source_target_pairs={{0,8},{8,16},{16,24},{1,9},{9,17},{17,25},{2,10},{10,18},{18,26},{... | collective-permute-start | bytes 1572872 | tf_op jit(solution)/shard_map/ppermute | solution.py:201
  122.4 13.4 %collective-permute-start.18 = (bf16[1024,128]{1,0:T(8,128)(2,1)S(1)}, bf16[1024,128]{1,0:T(8,128)(2,1)S(1)}, u32[]{:S(2)}, u32[]{:S(2)}) collective-permute-start(bf16[1024,128]{1,0:T(8,128)(2,1)S(1)} %attend_1_3.1.refs_0_), channel_id=1, source_target_pairs={{0,6},{1,7},{2,4},{3,5},{4,2},{5,3},{6,0},{7,1},{8,14},{9,15},{10,... | collective-permute-start | bytes 786440 | tf_op jit(solution)/shard_map/ppermute | solution.py:197
  123.9 16.9 %collective-permute-start.16 = (bf16[1024,128]{1,0:T(8,128)(2,1)S(1)}, bf16[1024,128]{1,0:T(8,128)(2,1)S(1)}, u32[]{:S(2)}, u32[]{:S(2)}) collective-permute-start(bf16[1024,128]{1,0:T(8,128)(2,1)S(1)} %attend_1_3.1.refs_0_), channel_id=1, source_target_pairs={{0,4},{1,5},{2,6},{3,7},{4,0},{5,1},{6,2},{7,3},{8,12},{9,13},{10,... | collective-permute-start | bytes 786440 | tf_op jit(solution)/shard_map/ppermute | solution.py:197
  132.2 10.2 %collective-permute-start.35 = (bf16[1024,128]{1,0:T(8,128)(2,1)S(1)}, bf16[1024,128]{1,0:T(8,128)(2,1)S(1)}, u32[]{:S(2)}, u32[]{:S(2)}) collective-permute-start(bf16[1024,128]{1,0:T(8,128)(2,1)S(1)} %attend_0_3.1.refs_0_), channel_id=1, source_target_pairs={{0,6},{1,7},{2,4},{3,5},{4,2},{5,3},{6,0},{7,1},{8,14},{9,15},{10,... | collective-permute-start | bytes 786440 | tf_op jit(solution)/shard_map/ppermute | solution.py:197
  133.2 13.9 %collective-permute-start.33 = (bf16[1024,128]{1,0:T(8,128)(2,1)S(1)}, bf16[1024,128]{1,0:T(8,128)(2,1)S(1)}, u32[]{:S(2)}, u32[]{:S(2)}) collective-permute-start(bf16[1024,128]{1,0:T(8,128)(2,1)S(1)} %attend_0_3.1.refs_0_), channel_id=1, source_target_pairs={{0,4},{1,5},{2,6},{3,7},{4,0},{5,1},{6,2},{7,3},{8,12},{9,13},{10,... | collective-permute-start | bytes 786440 | tf_op jit(solution)/shard_map/ppermute | solution.py:197
  134.3 12.8 %collective-permute-start.14 = (bf16[1024,128]{1,0:T(8,128)(2,1)S(1)}, bf16[1024,128]{1,0:T(8,128)(2,1)S(1)}, u32[]{:S(2)}, u32[]{:S(2)}) collective-permute-start(bf16[1024,128]{1,0:T(8,128)(2,1)S(1)} %attend_1_3.1.refs_0_), channel_id=1, source_target_pairs={{0,2},{1,3},{2,0},{3,1},{4,6},{5,7},{6,4},{7,5},{8,10},{9,11},{10,... | collective-permute-start | bytes 786440 | tf_op jit(solution)/shard_map/ppermute | solution.py:197
  135.8 14.1 %collective-permute-start.31 = (bf16[1024,128]{1,0:T(8,128)(2,1)S(1)}, bf16[1024,128]{1,0:T(8,128)(2,1)S(1)}, u32[]{:S(2)}, u32[]{:S(2)}) collective-permute-start(bf16[1024,128]{1,0:T(8,128)(2,1)S(1)} %attend_0_3.1.refs_0_), channel_id=1, source_target_pairs={{0,2},{1,3},{2,0},{3,1},{4,6},{5,7},{6,4},{7,5},{8,10},{9,11},{10,... | collective-permute-start | bytes 786440 | tf_op jit(solution)/shard_map/ppermute | solution.py:197
  140.7 9.2 %collective-permute-start.30 = (bf16[1024,128]{1,0:T(8,128)(2,1)S(1)}, bf16[1024,128]{1,0:T(8,128)(2,1)S(1)}, u32[]{:S(2)}, u32[]{:S(2)}) collective-permute-start(bf16[1024,128]{1,0:T(8,128)(2,1)S(1)} %attend_0_3.1.refs_0_), channel_id=1, source_target_pairs={{0,1},{1,0},{2,3},{3,2},{4,5},{5,4},{6,7},{7,6},{8,9},{9,8},{10,11... | collective-permute-start | bytes 786440 | tf_op jit(solution)/shard_map/ppermute | solution.py:197
  (16 other events, 108.9 us)

commit v2 on v1

v2 whole, which is shorter than its diff:
```python
import functools
import math

import jax
import jax.numpy as jnp
from jax import lax
from jax.experimental import pallas as pl
from jax.experimental.pallas import tpu as pltpu
from jax.sharding import PartitionSpec as P

HEADS = 16
HEAD_DIM = 128
BLOCK = 128
NEG = -1e30
EXP2_SCALE = math.log2(math.e) / math.sqrt(HEAD_DIM)
GROUP = 4
ROW_SHIFT = 16
VMEM_BYTES = 40 * 1024 * 1024

VMEM = pl.BlockSpec(memory_space=pltpu.VMEM)
SMEM = pl.BlockSpec(memory_space=pltpu.SMEM)
ANY = pl.BlockSpec(memory_space=pl.ANY)


def params():
    return pltpu.CompilerParams(vmem_limit_bytes=VMEM_BYTES)


def pack_kernel(n_ka, heads, me_ref, k_ref, v_ref, mask_ref, *out_refs):
    key_blocks = k_ref.shape[0] // BLOCK
    for c in range(heads):
        for k in range(n_ka):
            col = pl.multiple_of(((me_ref[0] ^ k) * heads + c) * HEAD_DIM, HEAD_DIM)
            for t in range(key_blocks):
                rows, at = slice(t * BLOCK, (t + 1) * BLOCK), 2 * t * BLOCK
                out_refs[c][k, at : at + BLOCK] = k_ref[rows, pl.ds(col, HEAD_DIM)]
                out_refs[c][k, at + BLOCK : at + 2 * BLOCK] = v_ref[rows, pl.ds(col, HEAD_DIM)].T
            if c == 0:
                out_refs[c][k, 2 * key_blocks * BLOCK :] = mask_ref[...]


def pack(me, keys, values, mask, n_ka, heads):
    sizes = [2 * keys.shape[0] + (mask.shape[0] if c == 0 else 0) for c in range(heads)]
    return pl.pallas_call(
        functools.partial(pack_kernel, n_ka, heads),
        out_shape=[jax.ShapeDtypeStruct((n_ka, size, HEAD_DIM), keys.dtype) for size in sizes],
        in_specs=[SMEM, VMEM, VMEM, VMEM],
        out_specs=[VMEM] * heads,
        compiler_params=params(),
        name="pack",
    )(me, keys, values, mask)


def plan_kernel(steps, n_pb, n_slots, key_blocks, rows, pb_ref, mask_ref, count_ref, *live_refs):
    pb = pb_ref[0]
    sign = 1 - 2 * (pb & 1)
    for step, (deltas, live) in enumerate(zip(steps, live_refs)):

        def row_step(r, base):
            count = jnp.int32(0)
            for s, delta in enumerate(deltas):
                j = pb + delta * sign
                inside = ((j >= 0) & (j < n_pb)).astype(jnp.int32)
                j = jnp.clip(j, 0, n_pb - 1)
                for slot in range(n_slots):
                    for t in range(key_blocks):
                        live[2 * base + count] = (r << ROW_SHIFT) + (s * n_slots + slot) * key_blocks + t
                        column = j * key_blocks + t
                        count += inside * mask_ref[(slot * rows + r) * (n_pb * key_blocks) + column]
            live[2 * base + count] = -1
            return base + ((count + 1) >> 1)

        total = lax.fori_loop(0, rows, row_step, jnp.int32(0))
        for u in range(GROUP):
            live[2 * (total + u)] = 0
            live[2 * (total + u) + 1] = -1
        count_ref[step] = total


def plan(pb, mask, steps, n_pb, n_slots, key_blocks, rows):
    sizes = [rows * ((len(deltas) * n_slots * key_blocks + 2) // 2) + GROUP for deltas in steps]
    out_shape = [jax.ShapeDtypeStruct((len(steps),), jnp.int32)]
    out_shape += [jax.ShapeDtypeStruct((2 * size,), jnp.int32) for size in sizes]
    return pl.pallas_call(
        functools.partial(plan_kernel, steps, n_pb, n_slots, key_blocks, rows),
        out_shape=out_shape,
        in_specs=[SMEM, SMEM],
        out_specs=[SMEM] * len(out_shape),
        compiler_params=params(),
        name="plan",
    )(pb, mask)


def attend_kernel(n_src, step, first, last, count_ref, live_ref, q_ref, *refs):
    kv_refs, refs = refs[:n_src], refs[n_src:]
    state_in, refs = ((), refs) if first else (refs[:3], refs[3:])
    if last:
        (out_ref, kv, *state, sems) = refs
    else:
        (*state, kv, sems) = refs
    m_ref, l_ref, acc_ref = state
    blocks = kv.shape[0] // n_src
    copies = [
        pltpu.make_async_copy(kv_refs[s], kv.at[pl.ds(s * blocks, blocks)], sems.at[s]) for s in range(n_src)
    ]
    copies += [pltpu.make_async_copy(a, b, sems.at[n_src + i]) for i, (a, b) in enumerate(zip(state_in, state))]
    for copy in copies:
        copy.start()
    if first:
        m_ref[...] = jnp.full(m_ref.shape, NEG, jnp.float32)
        l_ref[...] = jnp.zeros(l_ref.shape, jnp.float32)
        acc_ref[...] = jnp.zeros(acc_ref.shape, jnp.float32)
    for copy in copies:
        copy.wait()
    total = count_ref[step]
    nt = (((1,), (1,)), ((), ()))
    nn = (((1,), (0,)), ((), ()))
    f32, bf16 = jnp.float32, jnp.bfloat16

    def group_step(g, _):
        found = []
        for u in range(GROUP):
            index = g * GROUP + u
            code0, code1 = live_ref[2 * index], live_ref[2 * index + 1]
            r = code0 >> ROW_SHIFT
            b0 = code0 & ((1 << ROW_SHIFT) - 1)
            b1 = jnp.maximum(code1, 0) & ((1 << ROW_SHIFT) - 1)
            q = q_ref[pl.ds(pl.multiple_of(r * BLOCK, BLOCK), BLOCK), :]
            x0 = lax.dot_general(kv[b0, 0], q, nt, preferred_element_type=f32)
            x1 = lax.dot_general(kv[b1, 0], q, nt, preferred_element_type=f32)
            x0 = jnp.where(index < total, x0, NEG)
            x1 = jnp.where(code1 >= 0, x1, NEG)
            top = jnp.max(jnp.maximum(x0, x1), axis=0, keepdims=True)
            w0 = jnp.exp2((x0 - top) * EXP2_SCALE)
            w1 = jnp.exp2((x1 - top) * EXP2_SCALE)
            total_w = jnp.sum(w0 + w1, axis=0, keepdims=True)
            part = lax.dot_general(kv[b0, 1], w0.astype(bf16), nn, preferred_element_type=f32)
            part += lax.dot_general(kv[b1, 1], w1.astype(bf16), nn, preferred_element_type=f32)
            found.append((r, top, total_w, part))
        for r, top, total_w, part in found:
            m = m_ref[r]
            m_new = jnp.maximum(m, top)
            alpha = jnp.exp2((m - m_new) * EXP2_SCALE)
            beta = jnp.exp2((top - m_new) * EXP2_SCALE)
            m_ref[r] = m_new
            l_ref[r] = l_ref[r] * alpha + total_w * beta
            acc_ref[r] = acc_ref[r] * alpha + part * beta
        return 0

    lax.fori_loop(0, (total + GROUP - 1) // GROUP, group_step, 0)
    if last:

        def finish(r, _):
            done = (acc_ref[r] / l_ref[r]).T.astype(out_ref.dtype)
            out_ref[pl.ds(pl.multiple_of(r * BLOCK, BLOCK), BLOCK), :] = done
            return 0

        lax.fori_loop(0, q_ref.shape[0] // BLOCK, finish, 0)


def attend(counts, live, q, sources, state, step, last, name):
    rows = q.shape[0] // BLOCK
    first = state is None
    state = () if first else tuple(state)
    stat = (rows, 1, BLOCK)
    shapes = [stat, stat, (rows, HEAD_DIM, BLOCK)]
    if last:
        out_shape = [jax.ShapeDtypeStruct(q.shape, q.dtype)]
    else:
        out_shape = [jax.ShapeDtypeStruct(shape, jnp.float32) for shape in shapes]
    n_src = len(sources)
    blocks = sources[0].shape[0]
    scratch = [pltpu.VMEM((n_src * blocks,) + sources[0].shape[1:], q.dtype)]
    if last:
        scratch += [pltpu.VMEM(shape, jnp.float32) for shape in shapes]
    scratch.append(pltpu.SemaphoreType.DMA((n_src + 3,)))
    live_blocks = rows * n_src * blocks // 4
    return pl.pallas_call(
        functools.partial(attend_kernel, n_src, step, first, last),
        out_shape=out_shape,
        in_specs=[SMEM, SMEM, VMEM] + [ANY] * (n_src + len(state)),
        out_specs=[VMEM] * len(out_shape),
        scratch_shapes=scratch,
        compiler_params=params(),
        cost_estimate=pl.CostEstimate(
            flops=live_blocks * 4 * BLOCK * BLOCK * HEAD_DIM,
            bytes_accessed=8 * q.size + 2 * n_src * sources[0].size,
            transcendentals=live_blocks * BLOCK * BLOCK,
        ),
        name=name,
    )(counts, live, q, *sources, *state)


def place_kernel(n_ka, heads, c, me_ref, *refs):
    pieces, out_ref, sems = refs[:n_ka], refs[-2], refs[-1]
    copies = []
    for k in range(n_ka):
        col = pl.multiple_of(((me_ref[0] ^ k) * heads + c) * HEAD_DIM, HEAD_DIM)
        copies.append(pltpu.make_async_copy(pieces[k], out_ref.at[:, pl.ds(col, HEAD_DIM)], sems.at[k]))
    for copy in copies:
        copy.start()
    for copy in copies:
        copy.wait()


def place(me, pieces, whole, c, heads):
    n_ka = len(pieces)
    rows = pieces[0].shape[0]
    extra = () if whole is None else (whole,)
    return pl.pallas_call(
        functools.partial(place_kernel, n_ka, heads, c),
        out_shape=jax.ShapeDtypeStruct((rows, HEADS * HEAD_DIM), pieces[0].dtype),
        in_specs=[SMEM] + [ANY] * (n_ka + len(extra)),
        out_specs=ANY,
        scratch_shapes=[pltpu.SemaphoreType.DMA((n_ka,))],
        input_output_aliases={1 + n_ka: 0} if extra else {},
        compiler_params=params(),
        name="place",
    )(me, *pieces, *extra)


def local(n_pb, n_ka, queries, keys, values, block_mask):
    heads = HEADS // n_ka
    key_blocks = keys.shape[0] // BLOCK
    rows = queries.shape[0] // BLOCK
    me = lax.axis_index("ka").astype(jnp.int32)
    pb = lax.axis_index("pb").astype(jnp.int32)
    me1, pb1 = me[None], pb[None]

    def swap(x, k):
        return lax.ppermute(x, "ka", [(i, i ^ k) for i in range(n_ka)])

    def exchange(x, odd, step):
        hops = []
        for low in range(odd, n_pb - 1, 2):
            hops += [(low, low + 1)] if low - (step - 1) >= 0 else []
            hops += [(low + 1, low)] if low + 1 + (step - 1) < n_pb else []
        return lax.ppermute(x, "pb", hops) if hops else None

    pad = (-rows) % 16
    mask = jnp.pad(block_mask.astype(keys.dtype), ((0, pad), (0, BLOCK - block_mask.shape[1])))
    packed = pack(me1, keys, values, mask, n_ka, heads)

    owns = []
    for c in range(heads):
        msgs = packed[c]
        mixed = [msgs[:2]] + [swap(msgs[k : k + 2], k) for k in range(2, n_ka, 2)]
        theirs = swap(jnp.stack([x[1] for x in mixed]), 1)
        all_kv = jnp.concatenate([jnp.stack([x[0] for x in mixed]), theirs])
        if c == 0:
            masks = all_kv[:, 2 * keys.shape[0] :, :][:, :rows, : block_mask.shape[1]]
            masks = masks.astype(jnp.int32).reshape(-1)
        owns.append(all_kv[:, : 2 * keys.shape[0]].reshape(n_ka * key_blocks, 2, BLOCK, HEAD_DIM))

    steps = []
    arrived = [[] for _ in range(heads)]
    state = [None] * heads
    last_even, last_odd = list(owns), list(owns)
    for step in range(1, n_pb):
        deltas = (0,) if step == 1 else ()
        for c in range(heads):
            even, odd = exchange(last_odd[c], 0, step), exchange(last_even[c], 1, step)
            last_even[c], last_odd[c] = even, odd
            arrived[c].append(([owns[c]] if step == 1 else []) + [x for x in (even, odd) if x is not None])
        deltas += (step,) if even is not None else ()
        deltas += (-step,) if odd is not None else ()
        steps.append(deltas)

    counts, *lives = plan(pb1, masks, steps, n_pb, n_ka, key_blocks, rows)

    whole = None
    for step in range(1, n_pb):
        for c in range(heads):
            q = lax.dynamic_slice_in_dim(queries, (me * heads + c) * HEAD_DIM, HEAD_DIM, 1)
            name = f"attend_{c}_{step}"
            last = step == n_pb - 1
            state[c] = attend(counts, lives[step - 1], q, arrived[c][step - 1], state[c], step - 1, last, name)
    for c in range(heads):
        (out,) = state[c]
        pieces = [out] + [swap(out, k) for k in range(2, n_ka, 2)]
        others = [swap(x, 1) for x in pieces]
        pieces = [x for two in zip(pieces, others) for x in two]
        whole = place(me1, pieces, whole, c, heads)
    return whole


def solution(mesh):
    n_pb, n_ka = mesh.shape["pb"], mesh.shape["ka"]
    return jax.shard_map(
        functools.partial(local, n_pb, n_ka),
        mesh=mesh,
        in_specs=(P("pb", None), P(("ka", "pb"), None), P(("ka", "pb"), None), P("pb", "ka")),
        out_specs=P("pb", None),
        check_vma=False,
    )
```

time: 154 us -> 138 us (0.90)
  the two profiles are of different devices: /device:TPU:0 before, /device:TPU:9 now
where the time goes in v2:
time: 138 us
  waiting for transfers between devices  53.7 us (39%)
  starting transfers between devices  39.6 us (29%)
  Pallas kernels  35.2 us (26%)
  local copies, waits for them, and re-layouts  7.28 us (5%)
  other arithmetic  1.49 us (1%)
    pallas_call x6, Pallas kernels, attend(): pl.pallas_call(functools.partial(attend_kernel, n_src, step, first, last)...  29.7 us
    ppermute x10, waiting for transfers between devices, exchange(): return lax.ppermute(x, 'pb', hops) if hops else None  29.2 us
    ppermute x22, waiting for transfers between devices, swap(): return lax.ppermute(x, 'ka', [(i, i ^ k) for i in range(n_ka)])  24.5 us
    ppermute x10, starting transfers between devices, exchange(): return lax.ppermute(x, 'pb', hops) if hops else None  21.4 us
    ppermute x22, starting transfers between devices, swap(): return lax.ppermute(x, 'ka', [(i, i ^ k) for i in range(n_ka)])  18.2 us
    unnamed x14, local copies, waits for them, and re-layouts  5.72 us
  transfers between devices with their start and end apart: 32, of which 13 were waited for; matrix products, arithmetic and copies ran while one was open for 2% of the time, Pallas kernels for 24%

profile of v2, /device:TPU:9, one launch (start us, length us, event | category | flops | bytes accessed | tf_op | source)
XLA Modules:
  0.0 137.6 jit_solution(2876790418706311742)
XLA Ops:
  3.2 2.2 %collective-permute-start.6 = (bf16[2,256,128]{2,1,0:T(8,128)(2,1)S(1)}, bf16[2,256,128]{2,1,0:T(8,128)(2,1)S(1)}, u32[]{:S(2)}, u32[]{:S(2)}) collective-permute-start(bf16[2,256,128]{2,1,0:T(8,128)(2,1)S(1)} %get-tuple-element.50), channel_id=1, source_target_pairs={{0,6},{1,7},{2,4},{3,5},{4,2},{5,3},{6,0},{7,1},{8,14},{9,15},{10,... | collective-permute-start | bytes 393224 | tf_op jit(solution)/shard_map/ppermute | solution.py:231
  6.0 2.2 %collective-permute-start.2 = (bf16[2,272,128]{2,1,0:T(8,128)(2,1)S(1)}, bf16[2,272,128]{2,1,0:T(8,128)(2,1)S(1)}, u32[]{:S(2)}, u32[]{:S(2)}) collective-permute-start(bf16[2,272,128]{2,1,0:T(8,128)(2,1)S(1)} %get-tuple-element.45), channel_id=1, source_target_pairs={{0,6},{1,7},{2,4},{3,5},{4,2},{5,3},{6,0},{7,1},{8,14},{9,15},{10,... | collective-permute-start | bytes 417800 | tf_op jit(solution)/shard_map/ppermute | solution.py:231
  8.5 3.0 %collective-permute-done.4 = bf16[2,256,128]{2,1,0:T(8,128)(2,1)S(1)} collective-permute-done((bf16[2,256,128]{2,1,0:T(8,128)(2,1)S(1)}, bf16[2,256,128]{2,1,0:T(8,128)(2,1)S(1)}, u32[]{:S(2)}, u32[]{:S(2)}) %collective-permute-start.4) | collective-permute-done | bytes 131104 | tf_op jit(solution)/shard_map/ppermute | solution.py:231
  13.8 2.0 %collective-permute-start.7 = (bf16[4,256,128]{2,1,0:T(8,128)(2,1)S(1)}, bf16[4,256,128]{2,1,0:T(8,128)(2,1)S(1)}, u32[]{:S(2)}, u32[]{:S(2)}) collective-permute-start(bf16[4,256,128]{2,1,0:T(8,128)(2,1)S(1)} %pad_maximum_fusion.1), channel_id=1, source_target_pairs={{0,1},{1,0},{2,3},{3,2},{4,5},{5,4},{6,7},{7,6},{8,9},{9,8},{10,11... | collective-permute-start | bytes 786440 | tf_op jit(solution)/shard_map/ppermute | solution.py:231
  21.1 4.1 %collective-permute-start.11 = (bf16[8,2,128,128]{3,2,1,0:T(8,128)(2,1)S(1)}, bf16[8,2,128,128]{3,2,1,0:T(8,128)(2,1)}, u32[]{:S(2)}, u32[]{:S(2)}) collective-permute-start(bf16[8,2,128,128]{3,2,1,0:T(8,128)(2,1)S(1)} %bitcast.8), channel_id=1, source_target_pairs={{8,16},{16,8},{9,17},{17,9},{10,18},{18,10},{11,19},{19,11},{12,20... | collective-permute-start | bytes 1572872 | tf_op jit(solution)/shard_map/ppermute | solution.py:238
  27.2 6.0 %collective-permute-done.8.refs_1_ = bf16[8,2,128,128]{3,2,1,0:T(8,128)(2,1)S(1)} collective-permute-done((bf16[8,2,128,128]{3,2,1,0:T(8,128)(2,1)S(1)}, bf16[8,2,128,128]{3,2,1,0:T(8,128)(2,1)S(1)}, u32[]{:S(2)}, u32[]{:S(2)}) %collective-permute-start.8) | collective-permute-done | bytes 524320 | tf_op jit(solution)/shard_map/ppermute | solution.py:238
  33.1 3.2 %collective-permute-start.9 = (bf16[8,2,128,128]{3,2,1,0:T(8,128)(2,1)S(1)}, bf16[8,2,128,128]{3,2,1,0:T(8,128)(2,1)S(1)}, u32[]{:S(2)}, u32[]{:S(2)}) collective-permute-start(bf16[8,2,128,128]{3,2,1,0:T(8,128)(2,1)S(1)} %collective-permute-done.8.refs_1_), channel_id=1, source_target_pairs={{8,16},{16,8},{9,17},{17,9},{10,18},{18,10},{11,19},{19,11},{12,20... | collective-permute-start | bytes 1572872 | tf_op jit(solution)/shard_map/ppermute | solution.py:238
  37.1 7.1 %collective-permute-done.20.refs_1_ = bf16[8,2,128,128]{3,2,1,0:T(8,128)(2,1)S(1)} collective-permute-done((bf16[8,2,128,128]{3,2,1,0:T(8,128)(2,1)S(1)}, bf16[8,2,128,128]{3,2,1,0:T(8,128)(2,1)S(1)}, u32[]{:S(2)}, u32[]{:S(2)}) %collective-permute-start.20) | collective-permute-done | bytes 524320 | tf_op jit(solution)/shard_map/ppermute | solution.py:238
  44.3 3.2 %collective-permute-start.21 = (bf16[8,2,128,128]{3,2,1,0:T(8,128)(2,1)S(1)}, bf16[8,2,128,128]{3,2,1,0:T(8,128)(2,1)S(1)}, u32[]{:S(2)}, u32[]{:S(2)}) collective-permute-start(bf16[8,2,128,128]{3,2,1,0:T(8,128)(2,1)S(1)} %collective-permute-done.20.refs_1_), channel_id=1, source_target_pairs={{8,16},{16,8},{9,17},{17,9},{10,18},{18,10},{11,19},{19,11},{12,20... | collective-permute-start | bytes 1572872 | tf_op jit(solution)/shard_map/ppermute | solution.py:238
  48.3 2.1 %collective-permute-start.12 = (bf16[8,2,128,128]{3,2,1,0:T(8,128)(2,1)}, bf16[8,2,128,128]{3,2,1,0:T(8,128)(2,1)}, u32[]{:S(2)}, u32[]{:S(2)}) collective-permute-start(bf16[8,2,128,128]{3,2,1,0:T(8,128)(2,1)} %collective-permute-done.11.refs_2_), channel_id=1, source_target_pairs={{8,0},{16,24},{9,1},{17,25},{10,2},{18,26},{11,3},{19,27},{12,4},{... | collective-permute-start | bytes 1572872 | tf_op jit(solution)/shard_map/ppermute | solution.py:238
  50.4 2.1 %collective-permute-start.24 = (bf16[8,2,128,128]{3,2,1,0:T(8,128)(2,1)S(1)}, bf16[8,2,128,128]{3,2,1,0:T(8,128)(2,1)}, u32[]{:S(2)}, u32[]{:S(2)}) collective-permute-start(bf16[8,2,128,128]{3,2,1,0:T(8,128)(2,1)S(1)} %collective-permute-done.23.refs_2_), channel_id=1, source_target_pairs={{8,0},{16,24},{9,1},{17,25},{10,2},{18,26},{11,3},{19,27},{12,4},{... | collective-permute-start | bytes 1572872 | tf_op jit(solution)/shard_map/ppermute | solution.py:238
  52.4 6.9 %collective-permute-done.9.refs_1_ = bf16[8,2,128,128]{3,2,1,0:T(8,128)(2,1)S(1)} collective-permute-done((bf16[8,2,128,128]{3,2,1,0:T(8,128)(2,1)S(1)}, bf16[8,2,128,128]{3,2,1,0:T(8,128)(2,1)S(1)}, u32[]{:S(2)}, u32[]{:S(2)}) %collective-permute-start.9) | collective-permute-done | bytes 524320 | tf_op jit(solution)/shard_map/ppermute | solution.py:238
  59.4 2.1 %collective-permute-start.10 = (bf16[8,2,128,128]{3,2,1,0:T(8,128)(2,1)S(1)}, bf16[8,2,128,128]{3,2,1,0:T(8,128)(2,1)}, u32[]{:S(2)}, u32[]{:S(2)}) collective-permute-start(bf16[8,2,128,128]{3,2,1,0:T(8,128)(2,1)S(1)} %collective-permute-done.9.refs_1_), channel_id=1, source_target_pairs={{8,0},{16,24},{9,1},{17,25},{10,2},{18,26},{11,3},{19,27},{12,4},{... | collective-permute-start | bytes 1572872 | tf_op jit(solution)/shard_map/ppermute | solution.py:238
  61.5 9.1 %collective-permute-done.21.refs_1_ = bf16[8,2,128,128]{3,2,1,0:T(8,128)(2,1)S(1)} collective-permute-done((bf16[8,2,128,128]{3,2,1,0:T(8,128)(2,1)S(1)}, bf16[8,2,128,128]{3,2,1,0:T(8,128)(2,1)S(1)}, u32[]{:S(2)}, u32[]{:S(2)}) %collective-permute-start.21) | collective-permute-done | bytes 524320 | tf_op jit(solution)/shard_map/ppermute | solution.py:238
  70.6 2.1 %collective-permute-start.22 = (bf16[8,2,128,128]{3,2,1,0:T(8,128)(2,1)S(1)}, bf16[8,2,128,128]{3,2,1,0:T(8,128)(2,1)}, u32[]{:S(2)}, u32[]{:S(2)}) collective-permute-start(bf16[8,2,128,128]{3,2,1,0:T(8,128)(2,1)S(1)} %collective-permute-done.21.refs_1_), channel_id=1, source_target_pairs={{8,0},{16,24},{9,1},{17,25},{10,2},{18,26},{11,3},{19,27},{12,4},{... | collective-permute-start | bytes 1572872 | tf_op jit(solution)/shard_map/ppermute | solution.py:238
  74.6 2.4 %plan.1 = (s32[3]{0:T(128)S(1)}, s32[216]{0:T(256)S(1)}, s32[152]{0:T(256)S(1)}, s32[88]{0:T(128)S(1)}) custom-call(s32[1]{0:T(128)} %bitcast.1.pb_ref, s32[256]{0:T(256)S(1)} %reshape.16.mask_ref), custom_call_target="tpu_custom_call" | custom-call | tf_op jit(solution)/shard_map/plan/pallas_call | solution.py:84
  78.1 9.1 %attend_1_1.1 = (f32[8,1,128]{2,1,0:T(1,128)S(1)}, f32[8,1,128]{2,1,0:T(1,128)S(1)}, f32[8,128,128]{2,1,0:T(8,128)S(1)}) custom-call(s32[3]{0:T(128)S(1)} %get-tuple-element.24.count_ref, s32[216]{0:T(256)S(1)} %get-tuple-element.28.live_ref, bf16[1024,128]{1,0:T(8,128)(2,1)S(1)} %get-tuple-element.42.q_ref, bf16[8,2,128,128]{3,2,1,0:T(8,128)(2,1)S(1)} %bitcast.9, ...), custom_call_target="tpu_custom_call" | custom-call | flops 402653184 | bytes 2621440 | tf_op jit(solution)/shard_map/attend_1_1/pallas_call | solution.py:178
  88.2 8.1 %attend_0_1.1 = (f32[8,1,128]{2,1,0:T(1,128)S(1)}, f32[8,1,128]{2,1,0:T(1,128)S(1)}, f32[8,128,128]{2,1,0:T(8,128)S(1)}) custom-call(s32[3]{0:T(128)S(1)} %get-tuple-element.24.count_ref, s32[216]{0:T(256)S(1)} %get-tuple-element.28.live_ref, bf16[1024,128]{1,0:T(8,128)(2,1)S(1)} %get-tuple-element.41.q_ref, bf16[8,2,128,128]{3,2,1,0:T(8,128)(2,1)S(1)} %bitcast.6, ...), custom_call_target="tpu_custom_call" | custom-call | flops 402653184 | bytes 2621440 | tf_op jit(solution)/shard_map/attend_0_1/pallas_call | solution.py:178
  96.4 3.7 %attend_1_2.1 = (f32[8,1,128]{2,1,0:T(1,128)S(1)}, f32[8,1,128]{2,1,0:T(1,128)S(1)}, f32[8,128,128]{2,1,0:T(8,128)S(1)}) custom-call(s32[3]{0:T(128)S(1)} %get-tuple-element.24.count_ref, s32[152]{0:T(256)S(1)} %get-tuple-element.27.live_ref, bf16[1024,128]{1,0:T(8,128)(2,1)S(1)} %get-tuple-element.42.q_ref, ...), custom_call_target="tpu_custom_call" | custom-call | flops 268435456 | bytes 2097152 | tf_op jit(solution)/shard_map/attend_1_2/pallas_call | solution.py:178
  100.1 3.7 %attend_0_2.1 = (f32[8,1,128]{2,1,0:T(1,128)S(1)}, f32[8,1,128]{2,1,0:T(1,128)S(1)}, f32[8,128,128]{2,1,0:T(8,128)S(1)}) custom-call(s32[3]{0:T(128)S(1)} %get-tuple-element.24.count_ref, s32[152]{0:T(256)S(1)} %get-tuple-element.27.live_ref, bf16[1024,128]{1,0:T(8,128)(2,1)S(1)} %get-tuple-element.41.q_ref, ...), custom_call_target="tpu_custom_call" | custom-call | flops 268435456 | bytes 2097152 | tf_op jit(solution)/shard_map/attend_0_2/pallas_call | solution.py:178
  103.9 2.5 %attend_1_3.1.refs_0_ = bf16[1024,128]{1,0:T(8,128)(2,1)S(1)} custom-call(s32[3]{0:T(128)S(1)} %get-tuple-element.24.count_ref, s32[88]{0:T(128)S(1)} %get-tuple-element.25.live_ref, bf16[1024,128]{1,0:T(8,128)(2,1)S(1)} %get-tuple-element.42.q_ref, bf16[8,2,128,128]{3,2,1,0:T(8,128)(2,1)} %collective-permute-done.10.refs_0_, ...), custom_call_target="tpu_custom_call" | custom-call | flops 134217728 | bytes 1572864 | tf_op jit(solution)/shard_map/attend_1_3/pallas_call | solution.py:178
  108.8 2.5 %attend_0_3.1.refs_0_ = bf16[1024,128]{1,0:T(8,128)(2,1)S(1)} custom-call(s32[3]{0:T(128)S(1)} %get-tuple-element.24.count_ref, s32[88]{0:T(128)S(1)} %get-tuple-element.25.live_ref, bf16[1024,128]{1,0:T(8,128)(2,1)S(1)} %get-tuple-element.41.q_ref, bf16[8,2,128,128]{3,2,1,0:T(8,128)(2,1)} %collective-permute-done.22.refs_0_, ...), custom_call_target="tpu_custom_call" | custom-call | flops 134217728 | bytes 1572864 | tf_op jit(solution)/shard_map/attend_0_3/pallas_call | solution.py:178
  115.2 11.6 %collective-permute-done.16.refs_4_ = bf16[1024,128]{1,0:T(8,128)(2,1)S(1)} collective-permute-done((bf16[1024,128]{1,0:T(8,128)(2,1)S(1)}, bf16[1024,128]{1,0:T(8,128)(2,1)S(1)}, u32[]{:S(2)}, u32[]{:S(2)}) %collective-permute-start.16) | collective-permute-done | bytes 262176 | tf_op jit(solution)/shard_map/ppermute | solution.py:231
  127.4 5.0 %collective-permute-done.28.refs_4_ = bf16[1024,128]{1,0:T(8,128)(2,1)S(1)} collective-permute-done((bf16[1024,128]{1,0:T(8,128)(2,1)S(1)}, bf16[1024,128]{1,0:T(8,128)(2,1)S(1)}, u32[]{:S(2)}, u32[]{:S(2)}) %collective-permute-start.28) | collective-permute-done | bytes 262176 | tf_op jit(solution)/shard_map/ppermute | solution.py:231
  (85 shorter events, 31.2 us)
Async XLA Ops:
  3.2 10.5 %collective-permute-start.6 = (bf16[2,256,128]{2,1,0:T(8,128)(2,1)S(1)}, bf16[2,256,128]{2,1,0:T(8,128)(2,1)S(1)}, u32[]{:S(2)}, u32[]{:S(2)}) collective-permute-start(bf16[2,256,128]{2,1,0:T(8,128)(2,1)S(1)} %get-tuple-element.50), channel_id=1, source_target_pairs={{0,6},{1,7},{2,4},{3,5},{4,2},{5,3},{6,0},{7,1},{8,14},{9,15},{10,... | collective-permute-start | bytes 393224 | tf_op jit(solution)/shard_map/ppermute | solution.py:231
  5.5 8.2 %collective-permute-start.5 = (bf16[2,256,128]{2,1,0:T(8,128)(2,1)S(1)}, bf16[2,256,128]{2,1,0:T(8,128)(2,1)S(1)}, u32[]{:S(2)}, u32[]{:S(2)}) collective-permute-start(bf16[2,256,128]{2,1,0:T(8,128)(2,1)S(1)} %get-tuple-element.51), channel_id=1, source_target_pairs={{0,4},{1,5},{2,6},{3,7},{4,0},{5,1},{6,2},{7,3},{8,12},{9,13},{10,... | collective-permute-start | bytes 393224 | tf_op jit(solution)/shard_map/ppermute | solution.py:231
  5.7 5.7 %collective-permute-start.4 = (bf16[2,256,128]{2,1,0:T(8,128)(2,1)S(1)}, bf16[2,256,128]{2,1,0:T(8,128)(2,1)S(1)}, u32[]{:S(2)}, u32[]{:S(2)}) collective-permute-start(bf16[2,256,128]{2,1,0:T(8,128)(2,1)S(1)} %get-tuple-element.52), channel_id=1, source_target_pairs={{0,2},{1,3},{2,0},{3,1},{4,6},{5,7},{6,4},{7,5},{8,10},{9,11},{10,... | collective-permute-start | bytes 393224 | tf_op jit(solution)/shard_map/ppermute | solution.py:231
  6.0 12.4 %collective-permute-start.2 = (bf16[2,272,128]{2,1,0:T(8,128)(2,1)S(1)}, bf16[2,272,128]{2,1,0:T(8,128)(2,1)S(1)}, u32[]{:S(2)}, u32[]{:S(2)}) collective-permute-start(bf16[2,272,128]{2,1,0:T(8,128)(2,1)S(1)} %get-tuple-element.45), channel_id=1, source_target_pairs={{0,6},{1,7},{2,4},{3,5},{4,2},{5,3},{6,0},{7,1},{8,14},{9,15},{10,... | collective-permute-start | bytes 417800 | tf_op jit(solution)/shard_map/ppermute | solution.py:231
  8.2 10.2 %collective-permute-start.1 = (bf16[2,272,128]{2,1,0:T(8,128)(2,1)S(1)}, bf16[2,272,128]{2,1,0:T(8,128)(2,1)S(1)}, u32[]{:S(2)}, u32[]{:S(2)}) collective-permute-start(bf16[2,272,128]{2,1,0:T(8,128)(2,1)S(1)} %get-tuple-element.46), channel_id=1, source_target_pairs={{0,4},{1,5},{2,6},{3,7},{4,0},{5,1},{6,2},{7,3},{8,12},{9,13},{10,... | collective-permute-start | bytes 417800 | tf_op jit(solution)/shard_map/ppermute | solution.py:231
  11.4 5.6 %collective-permute-start = (bf16[2,272,128]{2,1,0:T(8,128)(2,1)S(1)}, bf16[2,272,128]{2,1,0:T(8,128)(2,1)S(1)}, u32[]{:S(2)}, u32[]{:S(2)}) collective-permute-start(bf16[2,272,128]{2,1,0:T(8,128)(2,1)S(1)} %get-tuple-element.47), channel_id=1, source_target_pairs={{0,2},{1,3},{2,0},{3,1},{4,6},{5,7},{6,4},{7,5},{8,10},{9,11},{10,... | collective-permute-start | bytes 417800 | tf_op jit(solution)/shard_map/ppermute | solution.py:231
  19.4 13.7 %collective-permute-start.8 = (bf16[8,2,128,128]{3,2,1,0:T(8,128)(2,1)S(1)}, bf16[8,2,128,128]{3,2,1,0:T(8,128)(2,1)S(1)}, u32[]{:S(2)}, u32[]{:S(2)}) collective-permute-start(bf16[8,2,128,128]{3,2,1,0:T(8,128)(2,1)S(1)} %bitcast.7), channel_id=1, source_target_pairs={{0,8},{8,0},{16,24},{24,16},{1,9},{9,1},{17,25},{25,17},{2,10},{10... | collective-permute-start | bytes 1572872 | tf_op jit(solution)/shard_map/ppermute | solution.py:238
  20.7 23.6 %collective-permute-start.20 = (bf16[8,2,128,128]{3,2,1,0:T(8,128)(2,1)S(1)}, bf16[8,2,128,128]{3,2,1,0:T(8,128)(2,1)S(1)}, u32[]{:S(2)}, u32[]{:S(2)}) collective-permute-start(bf16[8,2,128,128]{3,2,1,0:T(8,128)(2,1)S(1)} %bitcast.4), channel_id=1, source_target_pairs={{0,8},{8,0},{16,24},{24,16},{1,9},{9,1},{17,25},{25,17},{2,10},{10... | collective-permute-start | bytes 1572872 | tf_op jit(solution)/shard_map/ppermute | solution.py:238
  21.1 27.1 %collective-permute-start.11 = (bf16[8,2,128,128]{3,2,1,0:T(8,128)(2,1)S(1)}, bf16[8,2,128,128]{3,2,1,0:T(8,128)(2,1)}, u32[]{:S(2)}, u32[]{:S(2)}) collective-permute-start(bf16[8,2,128,128]{3,2,1,0:T(8,128)(2,1)S(1)} %bitcast.8), channel_id=1, source_target_pairs={{8,16},{16,8},{9,17},{17,9},{10,18},{18,10},{11,19},{19,11},{12,20... | collective-permute-start | bytes 1572872 | tf_op jit(solution)/shard_map/ppermute | solution.py:238
  25.2 25.1 %collective-permute-start.23 = (bf16[8,2,128,128]{3,2,1,0:T(8,128)(2,1)S(1)}, bf16[8,2,128,128]{3,2,1,0:T(8,128)(2,1)S(1)}, u32[]{:S(2)}, u32[]{:S(2)}) collective-permute-start(bf16[8,2,128,128]{3,2,1,0:T(8,128)(2,1)S(1)} %bitcast.5), channel_id=1, source_target_pairs={{8,16},{16,8},{9,17},{17,9},{10,18},{18,10},{11,19},{19,11},{12,20... | collective-permute-start | bytes 1572872 | tf_op jit(solution)/shard_map/ppermute | solution.py:238
  33.1 26.2 %collective-permute-start.9 = (bf16[8,2,128,128]{3,2,1,0:T(8,128)(2,1)S(1)}, bf16[8,2,128,128]{3,2,1,0:T(8,128)(2,1)S(1)}, u32[]{:S(2)}, u32[]{:S(2)}) collective-permute-start(bf16[8,2,128,128]{3,2,1,0:T(8,128)(2,1)S(1)} %collective-permute-done.8.refs_1_), channel_id=1, source_target_pairs={{8,16},{16,8},{9,17},{17,9},{10,18},{18,10},{11,19},{19,11},{12,20... | collective-permute-start | bytes 1572872 | tf_op jit(solution)/shard_map/ppermute | solution.py:238
  44.3 26.3 %collective-permute-start.21 = (bf16[8,2,128,128]{3,2,1,0:T(8,128)(2,1)S(1)}, bf16[8,2,128,128]{3,2,1,0:T(8,128)(2,1)S(1)}, u32[]{:S(2)}, u32[]{:S(2)}) collective-permute-start(bf16[8,2,128,128]{3,2,1,0:T(8,128)(2,1)S(1)} %collective-permute-done.20.refs_1_), channel_id=1, source_target_pairs={{8,16},{16,8},{9,17},{17,9},{10,18},{18,10},{11,19},{19,11},{12,20... | collective-permute-start | bytes 1572872 | tf_op jit(solution)/shard_map/ppermute | solution.py:238
  48.3 48.1 %collective-permute-start.12 = (bf16[8,2,128,128]{3,2,1,0:T(8,128)(2,1)}, bf16[8,2,128,128]{3,2,1,0:T(8,128)(2,1)}, u32[]{:S(2)}, u32[]{:S(2)}) collective-permute-start(bf16[8,2,128,128]{3,2,1,0:T(8,128)(2,1)} %collective-permute-done.11.refs_2_), channel_id=1, source_target_pairs={{8,0},{16,24},{9,1},{17,25},{10,2},{18,26},{11,3},{19,27},{12,4},{... | collective-permute-start | bytes 1572872 | tf_op jit(solution)/shard_map/ppermute | solution.py:238
  50.4 49.7 %collective-permute-start.24 = (bf16[8,2,128,128]{3,2,1,0:T(8,128)(2,1)S(1)}, bf16[8,2,128,128]{3,2,1,0:T(8,128)(2,1)}, u32[]{:S(2)}, u32[]{:S(2)}) collective-permute-start(bf16[8,2,128,128]{3,2,1,0:T(8,128)(2,1)S(1)} %collective-permute-done.23.refs_2_), channel_id=1, source_target_pairs={{8,0},{16,24},{9,1},{17,25},{10,2},{18,26},{11,3},{19,27},{12,4},{... | collective-permute-start | bytes 1572872 | tf_op jit(solution)/shard_map/ppermute | solution.py:238
  59.4 44.5 %collective-permute-start.10 = (bf16[8,2,128,128]{3,2,1,0:T(8,128)(2,1)S(1)}, bf16[8,2,128,128]{3,2,1,0:T(8,128)(2,1)}, u32[]{:S(2)}, u32[]{:S(2)}) collective-permute-start(bf16[8,2,128,128]{3,2,1,0:T(8,128)(2,1)S(1)} %collective-permute-done.9.refs_1_), channel_id=1, source_target_pairs={{8,0},{16,24},{9,1},{17,25},{10,2},{18,26},{11,3},{19,27},{12,4},{... | collective-permute-start | bytes 1572872 | tf_op jit(solution)/shard_map/ppermute | solution.py:238
  70.6 38.2 %collective-permute-start.22 = (bf16[8,2,128,128]{3,2,1,0:T(8,128)(2,1)S(1)}, bf16[8,2,128,128]{3,2,1,0:T(8,128)(2,1)}, u32[]{:S(2)}, u32[]{:S(2)}) collective-permute-start(bf16[8,2,128,128]{3,2,1,0:T(8,128)(2,1)S(1)} %collective-permute-done.21.refs_1_), channel_id=1, source_target_pairs={{8,0},{16,24},{9,1},{17,25},{10,2},{18,26},{11,3},{19,27},{12,4},{... | collective-permute-start | bytes 1572872 | tf_op jit(solution)/shard_map/ppermute | solution.py:238
  106.4 7.7 %collective-permute-start.18 = (bf16[1024,128]{1,0:T(8,128)(2,1)S(1)}, bf16[1024,128]{1,0:T(8,128)(2,1)S(1)}, u32[]{:S(2)}, u32[]{:S(2)}) collective-permute-start(bf16[1024,128]{1,0:T(8,128)(2,1)S(1)} %attend_1_3.1.refs_0_), channel_id=1, source_target_pairs={{0,6},{1,7},{2,4},{3,5},{4,2},{5,3},{6,0},{7,1},{8,14},{9,15},{10,... | collective-permute-start | bytes 786440 | tf_op jit(solution)/shard_map/ppermute | solution.py:231
  107.6 19.2 %collective-permute-start.16 = (bf16[1024,128]{1,0:T(8,128)(2,1)S(1)}, bf16[1024,128]{1,0:T(8,128)(2,1)S(1)}, u32[]{:S(2)}, u32[]{:S(2)}) collective-permute-start(bf16[1024,128]{1,0:T(8,128)(2,1)S(1)} %attend_1_3.1.refs_0_), channel_id=1, source_target_pairs={{0,4},{1,5},{2,6},{3,7},{4,0},{5,1},{6,2},{7,3},{8,12},{9,13},{10,... | collective-permute-start | bytes 786440 | tf_op jit(solution)/shard_map/ppermute | solution.py:231
  111.3 16.1 %collective-permute-start.30 = (bf16[1024,128]{1,0:T(8,128)(2,1)S(1)}, bf16[1024,128]{1,0:T(8,128)(2,1)S(1)}, u32[]{:S(2)}, u32[]{:S(2)}) collective-permute-start(bf16[1024,128]{1,0:T(8,128)(2,1)S(1)} %attend_0_3.1.refs_0_), channel_id=1, source_target_pairs={{0,6},{1,7},{2,4},{3,5},{4,2},{5,3},{6,0},{7,1},{8,14},{9,15},{10,... | collective-permute-start | bytes 786440 | tf_op jit(solution)/shard_map/ppermute | solution.py:231
  112.3 20.1 %collective-permute-start.28 = (bf16[1024,128]{1,0:T(8,128)(2,1)S(1)}, bf16[1024,128]{1,0:T(8,128)(2,1)S(1)}, u32[]{:S(2)}, u32[]{:S(2)}) collective-permute-start(bf16[1024,128]{1,0:T(8,128)(2,1)S(1)} %attend_0_3.1.refs_0_), channel_id=1, source_target_pairs={{0,4},{1,5},{2,6},{3,7},{4,0},{5,1},{6,2},{7,3},{8,12},{9,13},{10,... | collective-permute-start | bytes 786440 | tf_op jit(solution)/shard_map/ppermute | solution.py:231
  112.8 20.1 %collective-permute-start.14 = (bf16[1024,128]{1,0:T(8,128)(2,1)S(1)}, bf16[1024,128]{1,0:T(8,128)(2,1)S(1)}, u32[]{:S(2)}, u32[]{:S(2)}) collective-permute-start(bf16[1024,128]{1,0:T(8,128)(2,1)S(1)} %attend_1_3.1.refs_0_), channel_id=1, source_target_pairs={{0,2},{1,3},{2,0},{3,1},{4,6},{5,7},{6,4},{7,5},{8,10},{9,11},{10,... | collective-permute-start | bytes 786440 | tf_op jit(solution)/shard_map/ppermute | solution.py:231
  114.0 18.9 %collective-permute-start.26 = (bf16[1024,128]{1,0:T(8,128)(2,1)S(1)}, bf16[1024,128]{1,0:T(8,128)(2,1)S(1)}, u32[]{:S(2)}, u32[]{:S(2)}) collective-permute-start(bf16[1024,128]{1,0:T(8,128)(2,1)S(1)} %attend_0_3.1.refs_0_), channel_id=1, source_target_pairs={{0,2},{1,3},{2,0},{3,1},{4,6},{5,7},{6,4},{7,5},{8,10},{9,11},{10,... | collective-permute-start | bytes 786440 | tf_op jit(solution)/shard_map/ppermute | solution.py:231
  126.8 6.6 %collective-permute-start.25 = (bf16[1024,128]{1,0:T(8,128)(2,1)S(1)}, bf16[1024,128]{1,0:T(8,128)(2,1)S(1)}, u32[]{:S(2)}, u32[]{:S(2)}) collective-permute-start(bf16[1024,128]{1,0:T(8,128)(2,1)S(1)} %attend_0_3.1.refs_0_), channel_id=1, source_target_pairs={{0,1},{1,0},{2,3},{3,2},{4,5},{5,4},{6,7},{7,6},{8,9},{9,8},{10,11... | collective-permute-start | bytes 786440 | tf_op jit(solution)/shard_map/ppermute | solution.py:231
  127.4 6.1 %collective-permute-start.31 = (bf16[1024,128]{1,0:T(8,128)(2,1)S(1)}, bf16[1024,128]{1,0:T(8,128)(2,1)S(1)}, u32[]{:S(2)}, u32[]{:S(2)}) collective-permute-start(bf16[1024,128]{1,0:T(8,128)(2,1)S(1)} %collective-permute-done.30.refs_6_), channel_id=1, source_target_pairs={{0,1},{1,0},{2,3},{3,2},{4,5},{5,4},{6,7},{7,6},{8,9},{9,8},{10,11... | collective-permute-start | bytes 786440 | tf_op jit(solution)/shard_map/ppermute | solution.py:231
  (15 other events, 34.5 us)

commit v3 on v2

--- a/solution.py
+++ b/solution.py
@@ -24,6 +24,10 @@
 
 def params():
     return pltpu.CompilerParams(vmem_limit_bytes=VMEM_BYTES)
+
+
+def mask_rows(rows):
+    return -(-rows // 16) * 16
 
 
 def pack_kernel(n_ka, heads, me_ref, k_ref, v_ref, mask_ref, *out_refs):
@@ -35,16 +39,24 @@
                 rows, at = slice(t * BLOCK, (t + 1) * BLOCK), 2 * t * BLOCK
                 out_refs[c][k, at : at + BLOCK] = k_ref[rows, pl.ds(col, HEAD_DIM)]
                 out_refs[c][k, at + BLOCK : at + 2 * BLOCK] = v_ref[rows, pl.ds(col, HEAD_DIM)].T
-            if c == 0:
-                out_refs[c][k, 2 * key_blocks * BLOCK :] = mask_ref[...]
+    rows = mask_rows(mask_ref.shape[0])
+    row = lax.broadcasted_iota(jnp.int32, (rows, HEAD_DIM), 0)
+    column = lax.broadcasted_iota(jnp.int32, (rows, HEAD_DIM), 1)
+    mask = jnp.zeros((rows, HEAD_DIM), jnp.int32)
+    for i in range(mask_ref.shape[0]):
+        for j in range(mask_ref.shape[1]):
+            mask = jnp.where((row == i) & (column == j), mask_ref[i, j], mask)
+    mask = mask.astype(jnp.float32).astype(k_ref.dtype)
+    for k in range(n_ka):
+        out_refs[0][k, 2 * key_blocks * BLOCK :] = mask
 
 
 def pack(me, keys, values, mask, n_ka, heads):
-    sizes = [2 * keys.shape[0] + (mask.shape[0] if c == 0 else 0) for c in range(heads)]
+    sizes = [2 * keys.shape[0] + (mask_rows(mask.shape[0]) if c == 0 else 0) for c in range(heads)]
     return pl.pallas_call(
         functools.partial(pack_kernel, n_ka, heads),
         out_shape=[jax.ShapeDtypeStruct((n_ka, size, HEAD_DIM), keys.dtype) for size in sizes],
-        in_specs=[SMEM, VMEM, VMEM, VMEM],
+        in_specs=[SMEM, VMEM, VMEM, SMEM],
         out_specs=[VMEM] * heads,
         compiler_params=params(),
         name="pack",
@@ -91,19 +103,21 @@
     )(pb, mask)
 
 
-def attend_kernel(n_src, step, first, last, count_ref, live_ref, q_ref, *refs):
+def attend_kernel(n_src, step, first, last, count_ref, live_ref, head_ref, q_all, *refs):
     kv_refs, refs = refs[:n_src], refs[n_src:]
     state_in, refs = ((), refs) if first else (refs[:3], refs[3:])
     if last:
-        (out_ref, kv, *state, sems) = refs
+        (out_ref, kv, q_ref, *state, sems) = refs
     else:
-        (*state, kv, sems) = refs
+        (*state, kv, q_ref, sems) = refs
     m_ref, l_ref, acc_ref = state
     blocks = kv.shape[0] // n_src
     copies = [
         pltpu.make_async_copy(kv_refs[s], kv.at[pl.ds(s * blocks, blocks)], sems.at[s]) for s in range(n_src)
     ]
     copies += [pltpu.make_async_copy(a, b, sems.at[n_src + i]) for i, (a, b) in enumerate(zip(state_in, state))]
+    column = pl.multiple_of(head_ref[0] * HEAD_DIM, HEAD_DIM)
+    copies.append(pltpu.make_async_copy(q_all.at[:, pl.ds(column, HEAD_DIM)], q_ref, sems.at[n_src + 3]))
     for copy in copies:
         copy.start()
     if first:
@@ -158,7 +172,8 @@
         lax.fori_loop(0, q_ref.shape[0] // BLOCK, finish, 0)
 
 
-def attend(counts, live, q, sources, state, step, last, name):
+def attend(counts, live, head, queries, sources, state, step, last, name):
+    q = jax.ShapeDtypeStruct((queries.shape[0], HEAD_DIM), queries.dtype)
     rows = q.shape[0] // BLOCK
     first = state is None
     state = () if first else tuple(state)
@@ -170,15 +185,15 @@
         out_shape = [jax.ShapeDtypeStruct(shape, jnp.float32) for shape in shapes]
     n_src = len(sources)
     blocks = sources[0].shape[0]
-    scratch = [pltpu.VMEM((n_src * blocks,) + sources[0].shape[1:], q.dtype)]
+    scratch = [pltpu.VMEM((n_src * blocks,) + sources[0].shape[1:], q.dtype), pltpu.VMEM(q.shape, q.dtype)]
     if last:
         scratch += [pltpu.VMEM(shape, jnp.float32) for shape in shapes]
-    scratch.append(pltpu.SemaphoreType.DMA((n_src + 3,)))
+    scratch.append(pltpu.SemaphoreType.DMA((n_src + 4,)))
     live_blocks = rows * n_src * blocks // 4
     return pl.pallas_call(
         functools.partial(attend_kernel, n_src, step, first, last),
         out_shape=out_shape,
-        in_specs=[SMEM, SMEM, VMEM] + [ANY] * (n_src + len(state)),
+        in_specs=[SMEM, SMEM, SMEM, ANY] + [ANY] * (n_src + len(state)),
         out_specs=[VMEM] * len(out_shape),
         scratch_shapes=scratch,
         compiler_params=params(),
@@ -188,7 +203,7 @@
             transcendentals=live_blocks * BLOCK * BLOCK,
         ),
         name=name,
-    )(counts, live, q, *sources, *state)
+    )(counts, live, head, queries, *sources, *state)
 
 
 def place_kernel(n_ka, heads, c, me_ref, *refs):
@@ -230,16 +245,18 @@
     def swap(x, k):
         return lax.ppermute(x, "ka", [(i, i ^ k) for i in range(n_ka)])
 
+    def hops(odd, step):
+        found = []
+        for low in range(odd, n_pb - 1, 2):
+            found += [(low, low + 1)] if low - (step - 1) >= 0 else []
+            found += [(low + 1, low)] if low + 1 + (step - 1) < n_pb else []
+        return found
+
     def exchange(x, odd, step):
-        hops = []
-        for low in range(odd, n_pb - 1, 2):
-            hops += [(low, low + 1)] if low - (step - 1) >= 0 else []
-            hops += [(low + 1, low)] if low + 1 + (step - 1) < n_pb else []
-        return lax.ppermute(x, "pb", hops) if hops else None
-
-    pad = (-rows) % 16
-    mask = jnp.pad(block_mask.astype(keys.dtype), ((0, pad), (0, BLOCK - block_mask.shape[1])))
-    packed = pack(me1, keys, values, mask, n_ka, heads)
+        found = hops(odd, step)
+        return lax.ppermute(x, "pb", found) if found else None
+
+    packed = pack(me1, keys, values, block_mask, n_ka, heads)
 
     owns = []
     for c in range(heads):
@@ -252,29 +269,39 @@
             masks = masks.astype(jnp.int32).reshape(-1)
         owns.append(all_kv[:, : 2 * keys.shape[0]].reshape(n_ka * key_blocks, 2, BLOCK, HEAD_DIM))
 
-    steps = []
-    arrived = [[] for _ in range(heads)]
+    steps = [(0,)]
+    for step in range(1, n_pb):
+        even, odd = hops(0, step), hops(1, step)
+        steps.append(((step,) if even else ()) + ((-step,) if odd else ()))
+    counts, *lives = plan(pb1, masks, steps, n_pb, n_ka, key_blocks, rows)
+
+    def run(c, step, sources):
+        last = step == n_pb - 1
+        head = me1 * heads + c
+        return attend(counts, lives[step], head, queries, sources, state[c], step, last, f"attend_{c}_{step}")
+
+    def after(arrays, done):
+        if done is None:
+            return arrays
+        return lax.optimization_barrier((arrays, done[0]))[0]
+
     state = [None] * heads
-    last_even, last_odd = list(owns), list(owns)
-    for step in range(1, n_pb):
-        deltas = (0,) if step == 1 else ()
-        for c in range(heads):
-            even, odd = exchange(last_odd[c], 0, step), exchange(last_even[c], 1, step)
-            last_even[c], last_odd[c] = even, odd
-            arrived[c].append(([owns[c]] if step == 1 else []) + [x for x in (even, odd) if x is not None])
-        deltas += (step,) if even is not None else ()
-        deltas += (-step,) if odd is not None else ()
-        steps.append(deltas)
-
-    counts, *lives = plan(pb1, masks, steps, n_pb, n_ka, key_blocks, rows)
-
-    whole = None
+    over_even, over_odd = [None] * heads, [None] * heads
+    done = None
     for step in range(1, n_pb):
         for c in range(heads):
-            q = lax.dynamic_slice_in_dim(queries, (me * heads + c) * HEAD_DIM, HEAD_DIM, 1)
-            name = f"attend_{c}_{step}"
-            last = step == n_pb - 1
-            state[c] = attend(counts, lives[step - 1], q, arrived[c][step - 1], state[c], step - 1, last, name)
+            if step == 1:
+                owns[c] = after(owns[c], done)
+                even, odd = owns[c], owns[c]
+            else:
+                even, odd = after((over_odd[c], over_even[c]), done)
+            over_even[c], over_odd[c] = exchange(even, 0, step), exchange(odd, 1, step)
+            sources = [owns[c]] if step == 1 else [x for x in (odd, even) if x is not None]
+            done = state[c] = run(c, step - 1, sources)
+    for c in range(heads):
+        state[c] = run(c, n_pb - 1, [x for x in (over_even[c], over_odd[c]) if x is not None])
+
+    whole = None
     for c in range(heads):
         (out,) = state[c]
         pieces = [out] + [swap(out, k) for k in range(2, n_ka, 2)]

time: 138 us -> 128 us (0.928)
  the two profiles are of different devices: /device:TPU:9 before, /device:TPU:0 now
where the time goes in v3:
time: 128 us; the launch traced here: 127 us
  Pallas kernels  47.7 us (37%)
  waiting for transfers between devices  42 us (33%)
  starting transfers between devices  31.7 us (25%)
  local copies, waits for them, and re-layouts  5.41 us (4%)
    pallas_call x8, Pallas kernels, attend(): pl.pallas_call(functools.partial(attend_kernel, n_src, step, first, last)...  41.6 us
    ppermute x22, waiting for transfers between devices, swap(): return lax.ppermute(x, 'ka', [(i, i ^ k) for i in range(n_ka)])  22.1 us
    ppermute x10, waiting for transfers between devices, exchange(): return lax.ppermute(x, 'pb', found) if found else None  19.9 us
    ppermute x22, starting transfers between devices, swap(): return lax.ppermute(x, 'ka', [(i, i ^ k) for i in range(n_ka)])  18.7 us
    ppermute x10, starting transfers between devices, exchange(): return lax.ppermute(x, 'pb', found) if found else None  12.9 us
    unnamed x9, local copies, waits for them, and re-layouts  5.02 us
    pallas_call x2, Pallas kernels, place(): pl.pallas_call(functools.partial(place_kernel, n_ka, heads, c), out_shape...  2.76 us
  transfers between devices with their start and end apart: 32, of which 13 were waited for; matrix products, arithmetic and copies ran while one was open for 0% of the time, Pallas kernels for 36%

profile of v3, /device:TPU:0, one launch (start us, length us, event | category | flops | bytes accessed | tf_op | source)
XLA Modules:
  0.0 127.3 jit_solution(9899366591504924870)
XLA Ops:
  3.8 4.0 %collective-permute-start.6 = (bf16[2,256,128]{2,1,0:T(8,128)(2,1)S(1)}, bf16[2,256,128]{2,1,0:T(8,128)(2,1)S(1)}, u32[]{:S(2)}, u32[]{:S(2)}) collective-permute-start(bf16[2,256,128]{2,1,0:T(8,128)(2,1)S(1)} %get-tuple-element.80), channel_id=1, source_target_pairs={{0,6},{1,7},{2,4},{3,5},{4,2},{5,3},{6,0},{7,1},{8,14},{9,15},{10,... | collective-permute-start | bytes 393224 | tf_op jit(solution)/shard_map/ppermute | solution.py:246
  8.4 2.9 %collective-permute-start.2 = (bf16[2,272,128]{2,1,0:T(8,128)(2,1)S(1)}, bf16[2,272,128]{2,1,0:T(8,128)(2,1)S(1)}, u32[]{:S(2)}, u32[]{:S(2)}) collective-permute-start(bf16[2,272,128]{2,1,0:T(8,128)(2,1)S(1)} %get-tuple-element.75), channel_id=1, source_target_pairs={{0,6},{1,7},{2,4},{3,5},{4,2},{5,3},{6,0},{7,1},{8,14},{9,15},{10,... | collective-permute-start | bytes 417800 | tf_op jit(solution)/shard_map/ppermute | solution.py:246
  11.9 3.6 %collective-permute-done.4 = bf16[2,256,128]{2,1,0:T(8,128)(2,1)S(1)} collective-permute-done((bf16[2,256,128]{2,1,0:T(8,128)(2,1)S(1)}, bf16[2,256,128]{2,1,0:T(8,128)(2,1)S(1)}, u32[]{:S(2)}, u32[]{:S(2)}) %collective-permute-start.4) | collective-permute-done | bytes 131104 | tf_op jit(solution)/shard_map/ppermute | solution.py:246
  17.2 3.4 %collective-permute-done = bf16[2,272,128]{2,1,0:T(8,128)(2,1)S(1)} collective-permute-done((bf16[2,272,128]{2,1,0:T(8,128)(2,1)S(1)}, bf16[2,272,128]{2,1,0:T(8,128)(2,1)S(1)}, u32[]{:S(2)}, u32[]{:S(2)}) %collective-permute-start) | collective-permute-done | bytes 139296 | tf_op jit(solution)/shard_map/ppermute | solution.py:246
  22.4 1.6 %collective-permute-start.11 = (bf16[8,2,128,128]{3,2,1,0:T(8,128)(2,1)S(1)}, bf16[8,2,128,128]{3,2,1,0:T(8,128)(2,1)S(1)}, u32[]{:S(2)}, u32[]{:S(2)}) collective-permute-start(bf16[8,2,128,128]{3,2,1,0:T(8,128)(2,1)S(1)} %bitcast.4), channel_id=1, source_target_pairs={{0,8},{8,0},{16,24},{24,16},{1,9},{9,1},{17,25},{25,17},{2,10},{10... | collective-permute-start | bytes 1572872 | tf_op jit(solution)/shard_map/ppermute | solution.py:257
  24.8 2.5 %plan.1 = (s32[4]{0:T(128)S(1)}, s32[88]{0:T(128)S(1)}, s32[152]{0:T(256)S(1)}, s32[152]{0:T(256)S(1)}, s32[88]{0:T(128)S(1)}) custom-call(s32[1]{0:T(128)} %bitcast.1.pb_ref, s32[256]{0:T(256)S(1)} %reshape.16.mask_ref), custom_call_target="tpu_custom_call" | custom-call | tf_op jit(solution)/shard_map/plan/pallas_call | solution.py:96
  27.3 2.2 %copy-done = bf16[1024,2048]{1,0:T(8,128)(2,1)S(1)} copy-done((bf16[1024,2048]{1,0:T(8,128)(2,1)S(1)}, bf16[1024,2048]{1,0:T(8,128)(2,1)}, u32[]{:S(2)}) %copy-start) | copy-done | bytes 4194328
  29.5 4.9 %attend_0_0.1 = (f32[8,1,128]{2,1,0:T(1,128)S(1)}, f32[8,1,128]{2,1,0:T(1,128)S(1)}, f32[8,128,128]{2,1,0:T(8,128)S(1)}) custom-call(s32[4]{0:T(128)S(1)} %get-tuple-element.40.count_ref, s32[88]{0:T(128)S(1)} %get-tuple-element.43.live_ref, s32[1]{0:T(128)S(6)} %mul.2.head_ref, bf16[1024,2048]{1,0:T(8,128)(2,1)S(1)} %copy-done, ...), custom_call_target="tpu_custom_call" | custom-call | flops 134217728 | bytes 1572864 | tf_op jit(solution)/shard_map/attend_0_0/pallas_call | solution.py:193
  34.5 3.4 %collective-permute-start.9 = (bf16[8,2,128,128]{3,2,1,0:T(8,128)(2,1)S(1)}, bf16[8,2,128,128]{3,2,1,0:T(8,128)(2,1)S(1)}, u32[]{:S(2)}, u32[]{:S(2)}) collective-permute-start(bf16[8,2,128,128]{3,2,1,0:T(8,128)(2,1)S(1)} %bitcast.7), channel_id=1, source_target_pairs={{0,8},{8,0},{16,24},{24,16},{1,9},{9,1},{17,25},{25,17},{2,10},{10... | collective-permute-start | bytes 1572872 | tf_op jit(solution)/shard_map/ppermute | solution.py:257
  38.5 4.9 %attend_1_0.1 = (f32[8,1,128]{2,1,0:T(1,128)S(1)}, f32[8,1,128]{2,1,0:T(1,128)S(1)}, f32[8,128,128]{2,1,0:T(8,128)S(1)}) custom-call(s32[4]{0:T(128)S(1)} %get-tuple-element.40.count_ref, s32[88]{0:T(128)S(1)} %get-tuple-element.43.live_ref, s32[1]{0:T(128)S(6)} %add.2.head_ref, bf16[1024,2048]{1,0:T(8,128)(2,1)S(1)} %copy-done.1, ...), custom_call_target="tpu_custom_call" | custom-call | flops 134217728 | bytes 1572864 | tf_op jit(solution)/shard_map/attend_1_0/pallas_call | solution.py:193
  45.5 5.0 %attend_0_1.1 = (f32[8,1,128]{2,1,0:T(1,128)S(1)}, f32[8,1,128]{2,1,0:T(1,128)S(1)}, f32[8,128,128]{2,1,0:T(8,128)S(1)}) custom-call(s32[4]{0:T(128)S(1)} %get-tuple-element.40.count_ref, s32[152]{0:T(256)S(1)} %get-tuple-element.46.live_ref, s32[1]{0:T(128)S(6)} %mul.2.head_ref, bf16[1024,2048]{1,0:T(8,128)(2,1)S(1)} %copy-done.1, ...), custom_call_target="tpu_custom_call" | custom-call | flops 268435456 | bytes 2097152 | tf_op jit(solution)/shard_map/attend_0_1/pallas_call | solution.py:193
  52.6 5.0 %attend_1_1.1 = (f32[8,1,128]{2,1,0:T(1,128)S(1)}, f32[8,1,128]{2,1,0:T(1,128)S(1)}, f32[8,128,128]{2,1,0:T(8,128)S(1)}) custom-call(s32[4]{0:T(128)S(1)} %get-tuple-element.40.count_ref, s32[152]{0:T(256)S(1)} %get-tuple-element.46.live_ref, s32[1]{0:T(128)S(6)} %add.2.head_ref, bf16[1024,2048]{1,0:T(8,128)(2,1)S(1)} %copy-done.1, ...), custom_call_target="tpu_custom_call" | custom-call | flops 268435456 | bytes 2097152 | tf_op jit(solution)/shard_map/attend_1_1/pallas_call | solution.py:193
  57.7 4.2 %collective-permute-done.15.refs_0_ = bf16[8,2,128,128]{3,2,1,0:T(8,128)(2,1)S(1)} collective-permute-done((bf16[8,2,128,128]{3,2,1,0:T(8,128)(2,1)S(1)}, bf16[8,2,128,128]{3,2,1,0:T(8,128)(2,1)S(1)}, u32[]{:S(2)}, u32[]{:S(2)}) %collective-permute-start.15) | collective-permute-done | bytes 524320 | tf_op jit(solution)/shard_map/ppermute | solution.py:257
  61.9 5.0 %attend_0_2.1 = (f32[8,1,128]{2,1,0:T(1,128)S(1)}, f32[8,1,128]{2,1,0:T(1,128)S(1)}, f32[8,128,128]{2,1,0:T(8,128)S(1)}) custom-call(s32[4]{0:T(128)S(1)} %get-tuple-element.40.count_ref, s32[152]{0:T(256)S(1)} %get-tuple-element.55.live_ref, s32[1]{0:T(128)S(6)} %mul.2.head_ref, bf16[1024,2048]{1,0:T(8,128)(2,1)S(1)} %copy-done.1, ...), custom_call_target="tpu_custom_call" | custom-call | flops 268435456 | bytes 2097152 | tf_op jit(solution)/shard_map/attend_0_2/pallas_call | solution.py:193
  66.9 5.1 %collective-permute-done.13.refs_0_ = bf16[8,2,128,128]{3,2,1,0:T(8,128)(2,1)S(1)} collective-permute-done((bf16[8,2,128,128]{3,2,1,0:T(8,128)(2,1)S(1)}, bf16[8,2,128,128]{3,2,1,0:T(8,128)(2,1)S(1)}, u32[]{:S(2)}, u32[]{:S(2)}) %collective-permute-start.13) | collective-permute-done | bytes 524320 | tf_op jit(solution)/shard_map/ppermute | solution.py:257
  74.6 5.0 %attend_1_2.1 = (f32[8,1,128]{2,1,0:T(1,128)S(1)}, f32[8,1,128]{2,1,0:T(1,128)S(1)}, f32[8,128,128]{2,1,0:T(8,128)S(1)}) custom-call(s32[4]{0:T(128)S(1)} %get-tuple-element.40.count_ref, s32[152]{0:T(256)S(1)} %get-tuple-element.55.live_ref, s32[1]{0:T(128)S(6)} %add.2.head_ref, bf16[1024,2048]{1,0:T(8,128)(2,1)S(1)} %copy-done.1, ...), custom_call_target="tpu_custom_call" | custom-call | flops 268435456 | bytes 2097152 | tf_op jit(solution)/shard_map/attend_1_2/pallas_call | solution.py:193
  79.6 10.1 %collective-permute-done.16.refs_0_ = bf16[8,2,128,128]{3,2,1,0:T(8,128)(2,1)S(1)} collective-permute-done((bf16[8,2,128,128]{3,2,1,0:T(8,128)(2,1)S(1)}, bf16[8,2,128,128]{3,2,1,0:T(8,128)(2,1)S(1)}, u32[]{:S(2)}, u32[]{:S(2)}) %collective-permute-start.16) | collective-permute-done | bytes 524320 | tf_op jit(solution)/shard_map/ppermute | solution.py:257
  89.7 5.8 %attend_1_3.1.refs_0_ = bf16[1024,128]{1,0:T(8,128)(2,1)S(1)} custom-call(s32[4]{0:T(128)S(1)} %get-tuple-element.40.count_ref, s32[88]{0:T(128)S(1)} %get-tuple-element.41.live_ref, s32[1]{0:T(128)S(6)} %add.2.head_ref, bf16[1024,2048]{1,0:T(8,128)(2,1)S(1)} %copy-done.1, bf16[8,2,128,128]{3,2,1,0:T(8,128)(2,1)S(1)} %collective-permute-done.16.refs_0_, ...), custom_call_target="tpu_custom_call" | custom-call | flops 134217728 | bytes 1572864 | tf_op jit(solution)/shard_map/attend_1_3/pallas_call | solution.py:193
  98.9 5.8 %attend_0_3.1.refs_0_ = bf16[1024,128]{1,0:T(8,128)(2,1)S(1)} custom-call(s32[4]{0:T(128)S(1)} %get-tuple-element.40.count_ref, s32[88]{0:T(128)S(1)} %get-tuple-element.41.live_ref, s32[1]{0:T(128)S(6)} %mul.2.head_ref, bf16[1024,2048]{1,0:T(8,128)(2,1)S(1)} %copy-done.1, bf16[8,2,128,128]{3,2,1,0:T(8,128)(2,1)S(1)} %collective-permute-done.24.refs_0_, ...), custom_call_target="tpu_custom_call" | custom-call | flops 134217728 | bytes 1572864 | tf_op jit(solution)/shard_map/attend_0_3/pallas_call | solution.py:193
  106.2 1.5 %collective-permute-start.28 = (bf16[1024,128]{1,0:T(8,128)(2,1)S(1)}, bf16[1024,128]{1,0:T(8,128)(2,1)S(1)}, u32[]{:S(2)}, u32[]{:S(2)}) collective-permute-start(bf16[1024,128]{1,0:T(8,128)(2,1)S(1)} %attend_0_3.1.refs_0_), channel_id=1, source_target_pairs={{0,4},{1,5},{2,6},{3,7},{4,0},{5,1},{6,2},{7,3},{8,12},{9,13},{10,... | collective-permute-start | bytes 786440 | tf_op jit(solution)/shard_map/ppermute | solution.py:246
  109.8 5.2 %collective-permute-done.30.refs_6_ = bf16[1024,128]{1,0:T(8,128)(2,1)S(1)} collective-permute-done((bf16[1024,128]{1,0:T(8,128)(2,1)S(1)}, bf16[1024,128]{1,0:T(8,128)(2,1)S(1)}, u32[]{:S(2)}, u32[]{:S(2)}) %collective-permute-start.30) | collective-permute-done | bytes 262176 | tf_op jit(solution)/shard_map/ppermute | solution.py:246
  114.9 2.6 %collective-permute-done.28.refs_4_ = bf16[1024,128]{1,0:T(8,128)(2,1)S(1)} collective-permute-done((bf16[1024,128]{1,0:T(8,128)(2,1)S(1)}, bf16[1024,128]{1,0:T(8,128)(2,1)S(1)}, u32[]{:S(2)}, u32[]{:S(2)}) %collective-permute-start.28) | collective-permute-done | bytes 262176 | tf_op jit(solution)/shard_map/ppermute | solution.py:246
  117.5 2.6 %collective-permute-done.18.refs_2_ = bf16[1024,128]{1,0:T(8,128)(2,1)S(1)} collective-permute-done((bf16[1024,128]{1,0:T(8,128)(2,1)S(1)}, bf16[1024,128]{1,0:T(8,128)(2,1)S(1)}, u32[]{:S(2)}, u32[]{:S(2)}) %collective-permute-start.18) | collective-permute-done | bytes 262176 | tf_op jit(solution)/shard_map/ppermute | solution.py:246
  120.2 2.8 %collective-permute-done.26.refs_2_ = bf16[1024,128]{1,0:T(8,128)(2,1)S(1)} collective-permute-done((bf16[1024,128]{1,0:T(8,128)(2,1)S(1)}, bf16[1024,128]{1,0:T(8,128)(2,1)S(1)}, u32[]{:S(2)}, u32[]{:S(2)}) %collective-permute-start.26) | collective-permute-done | bytes 262176 | tf_op jit(solution)/shard_map/ppermute | solution.py:246
  (78 shorter events, 27.7 us)
Async XLA Ops:
  3.8 13.2 %collective-permute-start.6 = (bf16[2,256,128]{2,1,0:T(8,128)(2,1)S(1)}, bf16[2,256,128]{2,1,0:T(8,128)(2,1)S(1)}, u32[]{:S(2)}, u32[]{:S(2)}) collective-permute-start(bf16[2,256,128]{2,1,0:T(8,128)(2,1)S(1)} %get-tuple-element.80), channel_id=1, source_target_pairs={{0,6},{1,7},{2,4},{3,5},{4,2},{5,3},{6,0},{7,1},{8,14},{9,15},{10,... | collective-permute-start | bytes 393224 | tf_op jit(solution)/shard_map/ppermute | solution.py:246
  7.8 9.2 %collective-permute-start.5 = (bf16[2,256,128]{2,1,0:T(8,128)(2,1)S(1)}, bf16[2,256,128]{2,1,0:T(8,128)(2,1)S(1)}, u32[]{:S(2)}, u32[]{:S(2)}) collective-permute-start(bf16[2,256,128]{2,1,0:T(8,128)(2,1)S(1)} %get-tuple-element.81), channel_id=1, source_target_pairs={{0,4},{1,5},{2,6},{3,7},{4,0},{5,1},{6,2},{7,3},{8,12},{9,13},{10,... | collective-permute-start | bytes 393224 | tf_op jit(solution)/shard_map/ppermute | solution.py:246
  8.3 7.2 %collective-permute-start.4 = (bf16[2,256,128]{2,1,0:T(8,128)(2,1)S(1)}, bf16[2,256,128]{2,1,0:T(8,128)(2,1)S(1)}, u32[]{:S(2)}, u32[]{:S(2)}) collective-permute-start(bf16[2,256,128]{2,1,0:T(8,128)(2,1)S(1)} %get-tuple-element.82), channel_id=1, source_target_pairs={{0,2},{1,3},{2,0},{3,1},{4,6},{5,7},{6,4},{7,5},{8,10},{9,11},{10,... | collective-permute-start | bytes 393224 | tf_op jit(solution)/shard_map/ppermute | solution.py:246
  8.4 12.1 %collective-permute-start.2 = (bf16[2,272,128]{2,1,0:T(8,128)(2,1)S(1)}, bf16[2,272,128]{2,1,0:T(8,128)(2,1)S(1)}, u32[]{:S(2)}, u32[]{:S(2)}) collective-permute-start(bf16[2,272,128]{2,1,0:T(8,128)(2,1)S(1)} %get-tuple-element.75), channel_id=1, source_target_pairs={{0,6},{1,7},{2,4},{3,5},{4,2},{5,3},{6,0},{7,1},{8,14},{9,15},{10,... | collective-permute-start | bytes 417800 | tf_op jit(solution)/shard_map/ppermute | solution.py:246
  11.4 9.2 %collective-permute-start.1 = (bf16[2,272,128]{2,1,0:T(8,128)(2,1)S(1)}, bf16[2,272,128]{2,1,0:T(8,128)(2,1)S(1)}, u32[]{:S(2)}, u32[]{:S(2)}) collective-permute-start(bf16[2,272,128]{2,1,0:T(8,128)(2,1)S(1)} %get-tuple-element.76), channel_id=1, source_target_pairs={{0,4},{1,5},{2,6},{3,7},{4,0},{5,1},{6,2},{7,3},{8,12},{9,13},{10,... | collective-permute-start | bytes 417800 | tf_op jit(solution)/shard_map/ppermute | solution.py:246
  22.4 21.1 %collective-permute-start.11 = (bf16[8,2,128,128]{3,2,1,0:T(8,128)(2,1)S(1)}, bf16[8,2,128,128]{3,2,1,0:T(8,128)(2,1)S(1)}, u32[]{:S(2)}, u32[]{:S(2)}) collective-permute-start(bf16[8,2,128,128]{3,2,1,0:T(8,128)(2,1)S(1)} %bitcast.4), channel_id=1, source_target_pairs={{0,8},{8,0},{16,24},{24,16},{1,9},{9,1},{17,25},{25,17},{2,10},{10... | collective-permute-start | bytes 1572872 | tf_op jit(solution)/shard_map/ppermute | solution.py:257
  24.0 19.5 %collective-permute-start.10 = (bf16[8,2,128,128]{3,2,1,0:T(8,128)(2,1)S(1)}, bf16[8,2,128,128]{3,2,1,0:T(8,128)(2,1)S(1)}, u32[]{:S(2)}, u32[]{:S(2)}) collective-permute-start(bf16[8,2,128,128]{3,2,1,0:T(8,128)(2,1)S(1)} %bitcast.5), channel_id=1, source_target_pairs={{8,16},{16,8},{9,17},{17,9},{10,18},{18,10},{11,19},{19,11},{12,20... | collective-permute-start | bytes 1572872 | tf_op jit(solution)/shard_map/ppermute | solution.py:257
  34.5 16.2 %collective-permute-start.9 = (bf16[8,2,128,128]{3,2,1,0:T(8,128)(2,1)S(1)}, bf16[8,2,128,128]{3,2,1,0:T(8,128)(2,1)S(1)}, u32[]{:S(2)}, u32[]{:S(2)}) collective-permute-start(bf16[8,2,128,128]{3,2,1,0:T(8,128)(2,1)S(1)} %bitcast.7), channel_id=1, source_target_pairs={{0,8},{8,0},{16,24},{24,16},{1,9},{9,1},{17,25},{25,17},{2,10},{10... | collective-permute-start | bytes 1572872 | tf_op jit(solution)/shard_map/ppermute | solution.py:257
  37.8 12.8 %collective-permute-start.8 = (bf16[8,2,128,128]{3,2,1,0:T(8,128)(2,1)S(1)}, bf16[8,2,128,128]{3,2,1,0:T(8,128)(2,1)S(1)}, u32[]{:S(2)}, u32[]{:S(2)}) collective-permute-start(bf16[8,2,128,128]{3,2,1,0:T(8,128)(2,1)S(1)} %bitcast.8), channel_id=1, source_target_pairs={{8,16},{16,8},{9,17},{17,9},{10,18},{18,10},{11,19},{19,11},{12,20... | collective-permute-start | bytes 1572872 | tf_op jit(solution)/shard_map/ppermute | solution.py:257
  43.5 14.2 %collective-permute-start.14 = (bf16[8,2,128,128]{3,2,1,0:T(8,128)(2,1)S(1)}, bf16[8,2,128,128]{3,2,1,0:T(8,128)(2,1)S(1)}, u32[]{:S(2)}, u32[]{:S(2)}) collective-permute-start(bf16[8,2,128,128]{3,2,1,0:T(8,128)(2,1)S(1)} %collective-permute-done.11.refs_0_), channel_id=1, source_target_pairs={{8,16},{16,8},{9,17},{17,9},{10,18},{18,10},{11,19},{19,11},{12,20... | collective-permute-start | bytes 1572872 | tf_op jit(solution)/shard_map/ppermute | solution.py:257
  44.2 17.7 %collective-permute-start.15 = (bf16[8,2,128,128]{3,2,1,0:T(8,128)(2,1)S(1)}, bf16[8,2,128,128]{3,2,1,0:T(8,128)(2,1)S(1)}, u32[]{:S(2)}, u32[]{:S(2)}) collective-permute-start(bf16[8,2,128,128]{3,2,1,0:T(8,128)(2,1)S(1)} %collective-permute-done.10.refs_1_), channel_id=1, source_target_pairs={{8,0},{16,24},{9,1},{17,25},{10,2},{18,26},{11,3},{19,27},{12,4},{... | collective-permute-start | bytes 1572872 | tf_op jit(solution)/shard_map/ppermute | solution.py:257
  50.6 16.2 %collective-permute-start.12 = (bf16[8,2,128,128]{3,2,1,0:T(8,128)(2,1)S(1)}, bf16[8,2,128,128]{3,2,1,0:T(8,128)(2,1)S(1)}, u32[]{:S(2)}, u32[]{:S(2)}) collective-permute-start(bf16[8,2,128,128]{3,2,1,0:T(8,128)(2,1)S(1)} %collective-permute-done.9.refs_0_), channel_id=1, source_target_pairs={{8,16},{16,8},{9,17},{17,9},{10,18},{18,10},{11,19},{19,11},{12,20... | collective-permute-start | bytes 1572872 | tf_op jit(solution)/shard_map/ppermute | solution.py:257
  51.3 20.6 %collective-permute-start.13 = (bf16[8,2,128,128]{3,2,1,0:T(8,128)(2,1)S(1)}, bf16[8,2,128,128]{3,2,1,0:T(8,128)(2,1)S(1)}, u32[]{:S(2)}, u32[]{:S(2)}) collective-permute-start(bf16[8,2,128,128]{3,2,1,0:T(8,128)(2,1)S(1)} %collective-permute-done.8.refs_1_), channel_id=1, source_target_pairs={{8,0},{16,24},{9,1},{17,25},{10,2},{18,26},{11,3},{19,27},{12,4},{... | collective-permute-start | bytes 1572872 | tf_op jit(solution)/shard_map/ppermute | solution.py:257
  72.0 17.8 %collective-permute-start.16 = (bf16[8,2,128,128]{3,2,1,0:T(8,128)(2,1)S(1)}, bf16[8,2,128,128]{3,2,1,0:T(8,128)(2,1)S(1)}, u32[]{:S(2)}, u32[]{:S(2)}) collective-permute-start(bf16[8,2,128,128]{3,2,1,0:T(8,128)(2,1)S(1)} %collective-permute-done.12.refs_1_), channel_id=1, source_target_pairs={{8,0},{16,24},{9,1},{17,25},{10,2},{18,26},{11,3},{19,27},{12,4},{... | collective-permute-start | bytes 1572872 | tf_op jit(solution)/shard_map/ppermute | solution.py:257
  73.3 25.6 %collective-permute-start.24 = (bf16[8,2,128,128]{3,2,1,0:T(8,128)(2,1)S(1)}, bf16[8,2,128,128]{3,2,1,0:T(8,128)(2,1)S(1)}, u32[]{:S(2)}, u32[]{:S(2)}) collective-permute-start(bf16[8,2,128,128]{3,2,1,0:T(8,128)(2,1)S(1)} %collective-permute-done.14.refs_1_), channel_id=1, source_target_pairs={{8,0},{16,24},{9,1},{17,25},{10,2},{18,26},{11,3},{19,27},{12,4},{... | collective-permute-start | bytes 1572872 | tf_op jit(solution)/shard_map/ppermute | solution.py:257
  95.6 12.7 %collective-permute-start.22 = (bf16[1024,128]{1,0:T(8,128)(2,1)S(1)}, bf16[1024,128]{1,0:T(8,128)(2,1)S(1)}, u32[]{:S(2)}, u32[]{:S(2)}) collective-permute-start(bf16[1024,128]{1,0:T(8,128)(2,1)S(1)} %attend_1_3.1.refs_0_), channel_id=1, source_target_pairs={{0,6},{1,7},{2,4},{3,5},{4,2},{5,3},{6,0},{7,1},{8,14},{9,15},{10,... | collective-permute-start | bytes 786440 | tf_op jit(solution)/shard_map/ppermute | solution.py:246
  97.1 12.7 %collective-permute-start.20 = (bf16[1024,128]{1,0:T(8,128)(2,1)S(1)}, bf16[1024,128]{1,0:T(8,128)(2,1)S(1)}, u32[]{:S(2)}, u32[]{:S(2)}) collective-permute-start(bf16[1024,128]{1,0:T(8,128)(2,1)S(1)} %attend_1_3.1.refs_0_), channel_id=1, source_target_pairs={{0,4},{1,5},{2,6},{3,7},{4,0},{5,1},{6,2},{7,3},{8,12},{9,13},{10,... | collective-permute-start | bytes 786440 | tf_op jit(solution)/shard_map/ppermute | solution.py:246
  104.7 10.2 %collective-permute-start.30 = (bf16[1024,128]{1,0:T(8,128)(2,1)S(1)}, bf16[1024,128]{1,0:T(8,128)(2,1)S(1)}, u32[]{:S(2)}, u32[]{:S(2)}) collective-permute-start(bf16[1024,128]{1,0:T(8,128)(2,1)S(1)} %attend_0_3.1.refs_0_), channel_id=1, source_target_pairs={{0,6},{1,7},{2,4},{3,5},{4,2},{5,3},{6,0},{7,1},{8,14},{9,15},{10,... | collective-permute-start | bytes 786440 | tf_op jit(solution)/shard_map/ppermute | solution.py:246
  106.2 11.3 %collective-permute-start.28 = (bf16[1024,128]{1,0:T(8,128)(2,1)S(1)}, bf16[1024,128]{1,0:T(8,128)(2,1)S(1)}, u32[]{:S(2)}, u32[]{:S(2)}) collective-permute-start(bf16[1024,128]{1,0:T(8,128)(2,1)S(1)} %attend_0_3.1.refs_0_), channel_id=1, source_target_pairs={{0,4},{1,5},{2,6},{3,7},{4,0},{5,1},{6,2},{7,3},{8,12},{9,13},{10,... | collective-permute-start | bytes 786440 | tf_op jit(solution)/shard_map/ppermute | solution.py:246
  107.7 12.4 %collective-permute-start.18 = (bf16[1024,128]{1,0:T(8,128)(2,1)S(1)}, bf16[1024,128]{1,0:T(8,128)(2,1)S(1)}, u32[]{:S(2)}, u32[]{:S(2)}) collective-permute-start(bf16[1024,128]{1,0:T(8,128)(2,1)S(1)} %attend_1_3.1.refs_0_), channel_id=1, source_target_pairs={{0,2},{1,3},{2,0},{3,1},{4,6},{5,7},{6,4},{7,5},{8,10},{9,11},{10,... | collective-permute-start | bytes 786440 | tf_op jit(solution)/shard_map/ppermute | solution.py:246
  108.3 14.7 %collective-permute-start.26 = (bf16[1024,128]{1,0:T(8,128)(2,1)S(1)}, bf16[1024,128]{1,0:T(8,128)(2,1)S(1)}, u32[]{:S(2)}, u32[]{:S(2)}) collective-permute-start(bf16[1024,128]{1,0:T(8,128)(2,1)S(1)} %attend_0_3.1.refs_0_), channel_id=1, source_target_pairs={{0,2},{1,3},{2,0},{3,1},{4,6},{5,7},{6,4},{7,5},{8,10},{9,11},{10,... | collective-permute-start | bytes 786440 | tf_op jit(solution)/shard_map/ppermute | solution.py:246
  109.8 13.2 %collective-permute-start.25 = (bf16[1024,128]{1,0:T(8,128)(2,1)S(1)}, bf16[1024,128]{1,0:T(8,128)(2,1)S(1)}, u32[]{:S(2)}, u32[]{:S(2)}) collective-permute-start(bf16[1024,128]{1,0:T(8,128)(2,1)S(1)} %attend_0_3.1.refs_0_), channel_id=1, source_target_pairs={{0,1},{1,0},{2,3},{3,2},{4,5},{5,4},{6,7},{7,6},{8,9},{9,8},{10,11... | collective-permute-start | bytes 786440 | tf_op jit(solution)/shard_map/ppermute | solution.py:246
  114.9 8.6 %collective-permute-start.31 = (bf16[1024,128]{1,0:T(8,128)(2,1)S(1)}, bf16[1024,128]{1,0:T(8,128)(2,1)S(1)}, u32[]{:S(2)}, u32[]{:S(2)}) collective-permute-start(bf16[1024,128]{1,0:T(8,128)(2,1)S(1)} %collective-permute-done.30.refs_6_), channel_id=1, source_target_pairs={{0,1},{1,0},{2,3},{3,2},{4,5},{5,4},{6,7},{7,6},{8,9},{9,8},{10,11... | collective-permute-start | bytes 786440 | tf_op jit(solution)/shard_map/ppermute | solution.py:246
  117.5 6.0 %collective-permute-start.29 = (bf16[1024,128]{1,0:T(8,128)(2,1)S(1)}, bf16[1024,128]{1,0:T(8,128)(2,1)S(1)}, u32[]{:S(2)}, u32[]{:S(2)}) collective-permute-start(bf16[1024,128]{1,0:T(8,128)(2,1)S(1)} %collective-permute-done.28.refs_4_), channel_id=1, source_target_pairs={{0,1},{1,0},{2,3},{3,2},{4,5},{5,4},{6,7},{7,6},{8,9},{9,8},{10,11... | collective-permute-start | bytes 786440 | tf_op jit(solution)/shard_map/ppermute | solution.py:246
  (12 other events, 38.6 us)

commit v4 on v3

--- a/solution.py
+++ b/solution.py
@@ -13,7 +13,7 @@
 BLOCK = 128
 NEG = -1e30
 EXP2_SCALE = math.log2(math.e) / math.sqrt(HEAD_DIM)
-GROUP = 4
+GROUP = 8
 ROW_SHIFT = 16
 VMEM_BYTES = 40 * 1024 * 1024
 
@@ -107,9 +107,9 @@
     kv_refs, refs = refs[:n_src], refs[n_src:]
     state_in, refs = ((), refs) if first else (refs[:3], refs[3:])
     if last:
-        (out_ref, kv, q_ref, *state, sems) = refs
+        (out_ref, kv, q_ref, qt_ref, *state, sems) = refs
     else:
-        (*state, kv, q_ref, sems) = refs
+        (*state, kv, q_ref, qt_ref, sems) = refs
     m_ref, l_ref, acc_ref = state
     blocks = kv.shape[0] // n_src
     copies = [
@@ -127,6 +127,12 @@
     for copy in copies:
         copy.wait()
     total = count_ref[step]
+
+    def turn(r, _):
+        qt_ref[r] = q_ref[pl.ds(pl.multiple_of(r * BLOCK, BLOCK), BLOCK), :].T
+        return 0
+
+    lax.fori_loop(0, q_ref.shape[0] // BLOCK, turn, 0, unroll=True)
     nt = (((1,), (1,)), ((), ()))
     nn = (((1,), (0,)), ((), ()))
     f32, bf16 = jnp.float32, jnp.bfloat16
@@ -139,17 +145,17 @@
             r = code0 >> ROW_SHIFT
             b0 = code0 & ((1 << ROW_SHIFT) - 1)
             b1 = jnp.maximum(code1, 0) & ((1 << ROW_SHIFT) - 1)
-            q = q_ref[pl.ds(pl.multiple_of(r * BLOCK, BLOCK), BLOCK), :]
-            x0 = lax.dot_general(kv[b0, 0], q, nt, preferred_element_type=f32)
-            x1 = lax.dot_general(kv[b1, 0], q, nt, preferred_element_type=f32)
+            q = qt_ref[r]
+            x = lax.dot_general(jnp.concatenate([kv[b0, 0], kv[b1, 0]]), q, nn, preferred_element_type=f32)
+            x0, x1 = x[:BLOCK], x[BLOCK:]
             x0 = jnp.where(index < total, x0, NEG)
             x1 = jnp.where(code1 >= 0, x1, NEG)
             top = jnp.max(jnp.maximum(x0, x1), axis=0, keepdims=True)
             w0 = jnp.exp2((x0 - top) * EXP2_SCALE)
             w1 = jnp.exp2((x1 - top) * EXP2_SCALE)
             total_w = jnp.sum(w0 + w1, axis=0, keepdims=True)
-            part = lax.dot_general(kv[b0, 1], w0.astype(bf16), nn, preferred_element_type=f32)
-            part += lax.dot_general(kv[b1, 1], w1.astype(bf16), nn, preferred_element_type=f32)
+            w = jnp.concatenate([w0.astype(bf16), w1.astype(bf16)])
+            part = lax.dot_general(jnp.concatenate([kv[b0, 1], kv[b1, 1]], axis=1), w, nn, preferred_element_type=f32)
             found.append((r, top, total_w, part))
         for r, top, total_w, part in found:
             m = m_ref[r]
@@ -185,7 +191,7 @@
         out_shape = [jax.ShapeDtypeStruct(shape, jnp.float32) for shape in shapes]
     n_src = len(sources)
     blocks = sources[0].shape[0]
-    scratch = [pltpu.VMEM((n_src * blocks,) + sources[0].shape[1:], q.dtype), pltpu.VMEM(q.shape, q.dtype)]
+    scratch = [pltpu.VMEM((n_src * blocks,) + sources[0].shape[1:], q.dtype), pltpu.VMEM(q.shape, q.dtype), pltpu.VMEM((rows, HEAD_DIM, BLOCK), q.dtype)]
     if last:
         scratch += [pltpu.VMEM(shape, jnp.float32) for shape in shapes]
     scratch.append(pltpu.SemaphoreType.DMA((n_src + 4,)))

time: 128 us -> 125 us (0.977)
  Pallas kernels: 47.7 us -> 25.3 us
  waiting for transfers between devices: 42 us -> 61.1 us
    pallas_call x8, Pallas kernels: 41.6 us -> 19 us  [attend(): pl.pallas_call(functools.partial(attend_kernel, n_src, step, first, last)...]
    ppermute x10, waiting for transfers between devices: 19.9 us -> 38.3 us  [exchange(): return lax.ppermute(x, 'pb', found) if found else None]
  transfers between devices with their start and end apart: 32 -> 32, of which waited for: 13 -> 13; matrix products, arithmetic and copies ran while one was open for 0% -> 0% of each run, Pallas kernels for 36% -> 18%
where the time goes in v4:
time: 125 us
  waiting for transfers between devices  61.1 us (49%)
  starting transfers between devices  32.7 us (26%)
  Pallas kernels  25.3 us (20%)
  local copies, waits for them, and re-layouts  5.41 us (4%)
    ppermute x10, waiting for transfers between devices, exchange(): return lax.ppermute(x, 'pb', found) if found else None  38.3 us
    ppermute x22, waiting for transfers between devices, swap(): return lax.ppermute(x, 'ka', [(i, i ^ k) for i in range(n_ka)])  22.8 us
    pallas_call x8, Pallas kernels, attend(): pl.pallas_call(functools.partial(attend_kernel, n_src, step, first, last)...  19 us
    ppermute x22, starting transfers between devices, swap(): return lax.ppermute(x, 'ka', [(i, i ^ k) for i in range(n_ka)])  18.8 us
    ppermute x10, starting transfers between devices, exchange(): return lax.ppermute(x, 'pb', found) if found else None  14 us
    unnamed x9, local copies, waits for them, and re-layouts  5.02 us
    pallas_call x2, Pallas kernels, place(): pl.pallas_call(functools.partial(place_kernel, n_ka, heads, c), out_shape...  2.76 us
    pallas_call x1, Pallas kernels, plan(): pl.pallas_call(functools.partial(plan_kernel, steps, n_pb, n_slots, key_b...  2.53 us
  transfers between devices with their start and end apart: 32, of which 13 were waited for; matrix products, arithmetic and copies ran while one was open for 0% of the time, Pallas kernels for 18%

profile of v4, /device:TPU:0, one launch (start us, length us, event | category | flops | bytes accessed | tf_op | source)
XLA Modules:
  0.0 125.0 jit_solution(3608803710389691725)
XLA Ops:
  3.8 4.0 %collective-permute-start.6 = (bf16[2,256,128]{2,1,0:T(8,128)(2,1)S(1)}, bf16[2,256,128]{2,1,0:T(8,128)(2,1)S(1)}, u32[]{:S(2)}, u32[]{:S(2)}) collective-permute-start(bf16[2,256,128]{2,1,0:T(8,128)(2,1)S(1)} %get-tuple-element.80), channel_id=1, source_target_pairs={{0,6},{1,7},{2,4},{3,5},{4,2},{5,3},{6,0},{7,1},{8,14},{9,15},{10,... | collective-permute-start | bytes 393224 | tf_op jit(solution)/shard_map/ppermute | solution.py:252
  8.4 2.9 %collective-permute-start.2 = (bf16[2,272,128]{2,1,0:T(8,128)(2,1)S(1)}, bf16[2,272,128]{2,1,0:T(8,128)(2,1)S(1)}, u32[]{:S(2)}, u32[]{:S(2)}) collective-permute-start(bf16[2,272,128]{2,1,0:T(8,128)(2,1)S(1)} %get-tuple-element.75), channel_id=1, source_target_pairs={{0,6},{1,7},{2,4},{3,5},{4,2},{5,3},{6,0},{7,1},{8,14},{9,15},{10,... | collective-permute-start | bytes 417800 | tf_op jit(solution)/shard_map/ppermute | solution.py:252
  11.9 3.6 %collective-permute-done.4 = bf16[2,256,128]{2,1,0:T(8,128)(2,1)S(1)} collective-permute-done((bf16[2,256,128]{2,1,0:T(8,128)(2,1)S(1)}, bf16[2,256,128]{2,1,0:T(8,128)(2,1)S(1)}, u32[]{:S(2)}, u32[]{:S(2)}) %collective-permute-start.4) | collective-permute-done | bytes 131104 | tf_op jit(solution)/shard_map/ppermute | solution.py:252
  17.2 3.4 %collective-permute-done = bf16[2,272,128]{2,1,0:T(8,128)(2,1)S(1)} collective-permute-done((bf16[2,272,128]{2,1,0:T(8,128)(2,1)S(1)}, bf16[2,272,128]{2,1,0:T(8,128)(2,1)S(1)}, u32[]{:S(2)}, u32[]{:S(2)}) %collective-permute-start) | collective-permute-done | bytes 139296 | tf_op jit(solution)/shard_map/ppermute | solution.py:252
  24.8 2.5 %plan.1 = (s32[4]{0:T(128)S(1)}, s32[96]{0:T(128)S(1)}, s32[160]{0:T(256)S(1)}, s32[160]{0:T(256)S(1)}, s32[96]{0:T(128)S(1)}) custom-call(s32[1]{0:T(128)} %bitcast.1.pb_ref, s32[256]{0:T(256)S(1)} %reshape.16.mask_ref), custom_call_target="tpu_custom_call" | custom-call | tf_op jit(solution)/shard_map/plan/pallas_call | solution.py:96
  27.4 2.2 %copy-done = bf16[1024,2048]{1,0:T(8,128)(2,1)S(1)} copy-done((bf16[1024,2048]{1,0:T(8,128)(2,1)S(1)}, bf16[1024,2048]{1,0:T(8,128)(2,1)}, u32[]{:S(2)}) %copy-start) | copy-done | bytes 4194328
  29.6 2.1 %attend_0_0.1 = (f32[8,1,128]{2,1,0:T(1,128)S(1)}, f32[8,1,128]{2,1,0:T(1,128)S(1)}, f32[8,128,128]{2,1,0:T(8,128)S(1)}) custom-call(s32[4]{0:T(128)S(1)} %get-tuple-element.40.count_ref, s32[96]{0:T(128)S(1)} %get-tuple-element.43.live_ref, s32[1]{0:T(128)S(6)} %mul.2.head_ref, bf16[1024,2048]{1,0:T(8,128)(2,1)S(1)} %copy-done, ...), custom_call_target="tpu_custom_call" | custom-call | flops 134217728 | bytes 1572864 | tf_op jit(solution)/shard_map/attend_0_0/pallas_call | solution.py:199
  31.7 4.4 %collective-permute-start.9 = (bf16[8,2,128,128]{3,2,1,0:T(8,128)(2,1)S(1)}, bf16[8,2,128,128]{3,2,1,0:T(8,128)(2,1)S(1)}, u32[]{:S(2)}, u32[]{:S(2)}) collective-permute-start(bf16[8,2,128,128]{3,2,1,0:T(8,128)(2,1)S(1)} %bitcast.7), channel_id=1, source_target_pairs={{0,8},{8,0},{16,24},{24,16},{1,9},{9,1},{17,25},{25,17},{2,10},{10... | collective-permute-start | bytes 1572872 | tf_op jit(solution)/shard_map/ppermute | solution.py:263
  36.8 2.1 %attend_1_0.1 = (f32[8,1,128]{2,1,0:T(1,128)S(1)}, f32[8,1,128]{2,1,0:T(1,128)S(1)}, f32[8,128,128]{2,1,0:T(8,128)S(1)}) custom-call(s32[4]{0:T(128)S(1)} %get-tuple-element.40.count_ref, s32[96]{0:T(128)S(1)} %get-tuple-element.43.live_ref, s32[1]{0:T(128)S(6)} %add.2.head_ref, bf16[1024,2048]{1,0:T(8,128)(2,1)S(1)} %copy-done.1, ...), custom_call_target="tpu_custom_call" | custom-call | flops 134217728 | bytes 1572864 | tf_op jit(solution)/shard_map/attend_1_0/pallas_call | solution.py:199
  41.0 2.2 %attend_0_1.1 = (f32[8,1,128]{2,1,0:T(1,128)S(1)}, f32[8,1,128]{2,1,0:T(1,128)S(1)}, f32[8,128,128]{2,1,0:T(8,128)S(1)}) custom-call(s32[4]{0:T(128)S(1)} %get-tuple-element.40.count_ref, s32[160]{0:T(256)S(1)} %get-tuple-element.46.live_ref, s32[1]{0:T(128)S(6)} %mul.2.head_ref, bf16[1024,2048]{1,0:T(8,128)(2,1)S(1)} %copy-done.1, ...), custom_call_target="tpu_custom_call" | custom-call | flops 268435456 | bytes 2097152 | tf_op jit(solution)/shard_map/attend_0_1/pallas_call | solution.py:199
  43.2 5.7 %collective-permute-done.9.refs_0_ = bf16[8,2,128,128]{3,2,1,0:T(8,128)(2,1)S(1)} collective-permute-done((bf16[8,2,128,128]{3,2,1,0:T(8,128)(2,1)S(1)}, bf16[8,2,128,128]{3,2,1,0:T(8,128)(2,1)S(1)}, u32[]{:S(2)}, u32[]{:S(2)}) %collective-permute-start.9) | collective-permute-done | bytes 524320 | tf_op jit(solution)/shard_map/ppermute | solution.py:263
  50.9 2.2 %attend_1_1.1 = (f32[8,1,128]{2,1,0:T(1,128)S(1)}, f32[8,1,128]{2,1,0:T(1,128)S(1)}, f32[8,128,128]{2,1,0:T(8,128)S(1)}) custom-call(s32[4]{0:T(128)S(1)} %get-tuple-element.40.count_ref, s32[160]{0:T(256)S(1)} %get-tuple-element.46.live_ref, s32[1]{0:T(128)S(6)} %add.2.head_ref, bf16[1024,2048]{1,0:T(8,128)(2,1)S(1)} %copy-done.1, ...), custom_call_target="tpu_custom_call" | custom-call | flops 268435456 | bytes 2097152 | tf_op jit(solution)/shard_map/attend_1_1/pallas_call | solution.py:199
  53.1 7.0 %collective-permute-done.15.refs_0_ = bf16[8,2,128,128]{3,2,1,0:T(8,128)(2,1)S(1)} collective-permute-done((bf16[8,2,128,128]{3,2,1,0:T(8,128)(2,1)S(1)}, bf16[8,2,128,128]{3,2,1,0:T(8,128)(2,1)S(1)}, u32[]{:S(2)}, u32[]{:S(2)}) %collective-permute-start.15) | collective-permute-done | bytes 524320 | tf_op jit(solution)/shard_map/ppermute | solution.py:263
  60.2 2.2 %attend_0_2.1 = (f32[8,1,128]{2,1,0:T(1,128)S(1)}, f32[8,1,128]{2,1,0:T(1,128)S(1)}, f32[8,128,128]{2,1,0:T(8,128)S(1)}) custom-call(s32[4]{0:T(128)S(1)} %get-tuple-element.40.count_ref, s32[160]{0:T(256)S(1)} %get-tuple-element.55.live_ref, s32[1]{0:T(128)S(6)} %mul.2.head_ref, bf16[1024,2048]{1,0:T(8,128)(2,1)S(1)} %copy-done.1, ...), custom_call_target="tpu_custom_call" | custom-call | flops 268435456 | bytes 2097152 | tf_op jit(solution)/shard_map/attend_0_2/pallas_call | solution.py:199
  62.4 7.9 %collective-permute-done.13.refs_0_ = bf16[8,2,128,128]{3,2,1,0:T(8,128)(2,1)S(1)} collective-permute-done((bf16[8,2,128,128]{3,2,1,0:T(8,128)(2,1)S(1)}, bf16[8,2,128,128]{3,2,1,0:T(8,128)(2,1)S(1)}, u32[]{:S(2)}, u32[]{:S(2)}) %collective-permute-start.13) | collective-permute-done | bytes 524320 | tf_op jit(solution)/shard_map/ppermute | solution.py:263
  72.8 2.2 %attend_1_2.1 = (f32[8,1,128]{2,1,0:T(1,128)S(1)}, f32[8,1,128]{2,1,0:T(1,128)S(1)}, f32[8,128,128]{2,1,0:T(8,128)S(1)}) custom-call(s32[4]{0:T(128)S(1)} %get-tuple-element.40.count_ref, s32[160]{0:T(256)S(1)} %get-tuple-element.55.live_ref, s32[1]{0:T(128)S(6)} %add.2.head_ref, bf16[1024,2048]{1,0:T(8,128)(2,1)S(1)} %copy-done.1, ...), custom_call_target="tpu_custom_call" | custom-call | flops 268435456 | bytes 2097152 | tf_op jit(solution)/shard_map/attend_1_2/pallas_call | solution.py:199
  75.0 13.7 %collective-permute-done.16.refs_0_ = bf16[8,2,128,128]{3,2,1,0:T(8,128)(2,1)S(1)} collective-permute-done((bf16[8,2,128,128]{3,2,1,0:T(8,128)(2,1)S(1)}, bf16[8,2,128,128]{3,2,1,0:T(8,128)(2,1)S(1)}, u32[]{:S(2)}, u32[]{:S(2)}) %collective-permute-start.16) | collective-permute-done | bytes 524320 | tf_op jit(solution)/shard_map/ppermute | solution.py:263
  88.8 3.0 %attend_1_3.1.refs_0_ = bf16[1024,128]{1,0:T(8,128)(2,1)S(1)} custom-call(s32[4]{0:T(128)S(1)} %get-tuple-element.40.count_ref, s32[96]{0:T(128)S(1)} %get-tuple-element.41.live_ref, s32[1]{0:T(128)S(6)} %add.2.head_ref, bf16[1024,2048]{1,0:T(8,128)(2,1)S(1)} %copy-done.1, bf16[8,2,128,128]{3,2,1,0:T(8,128)(2,1)S(1)} %collective-permute-done.16.refs_0_, ...), custom_call_target="tpu_custom_call" | custom-call | flops 134217728 | bytes 1572864 | tf_op jit(solution)/shard_map/attend_1_3/pallas_call | solution.py:199
  94.8 3.9 %collective-permute-done.24.refs_0_ = bf16[8,2,128,128]{3,2,1,0:T(8,128)(2,1)S(1)} collective-permute-done((bf16[8,2,128,128]{3,2,1,0:T(8,128)(2,1)S(1)}, bf16[8,2,128,128]{3,2,1,0:T(8,128)(2,1)S(1)}, u32[]{:S(2)}, u32[]{:S(2)}) %collective-permute-start.24) | collective-permute-done | bytes 524320 | tf_op jit(solution)/shard_map/ppermute | solution.py:263
  98.7 3.0 %attend_0_3.1.refs_0_ = bf16[1024,128]{1,0:T(8,128)(2,1)S(1)} custom-call(s32[4]{0:T(128)S(1)} %get-tuple-element.40.count_ref, s32[96]{0:T(128)S(1)} %get-tuple-element.41.live_ref, s32[1]{0:T(128)S(6)} %mul.2.head_ref, bf16[1024,2048]{1,0:T(8,128)(2,1)S(1)} %copy-done.1, bf16[8,2,128,128]{3,2,1,0:T(8,128)(2,1)S(1)} %collective-permute-done.24.refs_0_, ...), custom_call_target="tpu_custom_call" | custom-call | flops 134217728 | bytes 1572864 | tf_op jit(solution)/shard_map/attend_0_3/pallas_call | solution.py:199
  106.7 5.2 %collective-permute-done.30.refs_6_ = bf16[1024,128]{1,0:T(8,128)(2,1)S(1)} collective-permute-done((bf16[1024,128]{1,0:T(8,128)(2,1)S(1)}, bf16[1024,128]{1,0:T(8,128)(2,1)S(1)}, u32[]{:S(2)}, u32[]{:S(2)}) %collective-permute-start.30) | collective-permute-done | bytes 262176 | tf_op jit(solution)/shard_map/ppermute | solution.py:252
  111.9 3.3 %collective-permute-done.28.refs_4_ = bf16[1024,128]{1,0:T(8,128)(2,1)S(1)} collective-permute-done((bf16[1024,128]{1,0:T(8,128)(2,1)S(1)}, bf16[1024,128]{1,0:T(8,128)(2,1)S(1)}, u32[]{:S(2)}, u32[]{:S(2)}) %collective-permute-start.28) | collective-permute-done | bytes 262176 | tf_op jit(solution)/shard_map/ppermute | solution.py:252
  115.3 2.0 %collective-permute-done.18.refs_2_ = bf16[1024,128]{1,0:T(8,128)(2,1)S(1)} collective-permute-done((bf16[1024,128]{1,0:T(8,128)(2,1)S(1)}, bf16[1024,128]{1,0:T(8,128)(2,1)S(1)}, u32[]{:S(2)}, u32[]{:S(2)}) %collective-permute-start.18) | collective-permute-done | bytes 262176 | tf_op jit(solution)/shard_map/ppermute | solution.py:252
  117.3 3.4 %collective-permute-done.26.refs_2_ = bf16[1024,128]{1,0:T(8,128)(2,1)S(1)} collective-permute-done((bf16[1024,128]{1,0:T(8,128)(2,1)S(1)}, bf16[1024,128]{1,0:T(8,128)(2,1)S(1)}, u32[]{:S(2)}, u32[]{:S(2)}) %collective-permute-start.26) | collective-permute-done | bytes 262176 | tf_op jit(solution)/shard_map/ppermute | solution.py:252
  (78 shorter events, 30.5 us)
Async XLA Ops:
  3.8 13.2 %collective-permute-start.6 = (bf16[2,256,128]{2,1,0:T(8,128)(2,1)S(1)}, bf16[2,256,128]{2,1,0:T(8,128)(2,1)S(1)}, u32[]{:S(2)}, u32[]{:S(2)}) collective-permute-start(bf16[2,256,128]{2,1,0:T(8,128)(2,1)S(1)} %get-tuple-element.80), channel_id=1, source_target_pairs={{0,6},{1,7},{2,4},{3,5},{4,2},{5,3},{6,0},{7,1},{8,14},{9,15},{10,... | collective-permute-start | bytes 393224 | tf_op jit(solution)/shard_map/ppermute | solution.py:252
  7.8 9.2 %collective-permute-start.5 = (bf16[2,256,128]{2,1,0:T(8,128)(2,1)S(1)}, bf16[2,256,128]{2,1,0:T(8,128)(2,1)S(1)}, u32[]{:S(2)}, u32[]{:S(2)}) collective-permute-start(bf16[2,256,128]{2,1,0:T(8,128)(2,1)S(1)} %get-tuple-element.81), channel_id=1, source_target_pairs={{0,4},{1,5},{2,6},{3,7},{4,0},{5,1},{6,2},{7,3},{8,12},{9,13},{10,... | collective-permute-start | bytes 393224 | tf_op jit(solution)/shard_map/ppermute | solution.py:252
  8.3 7.2 %collective-permute-start.4 = (bf16[2,256,128]{2,1,0:T(8,128)(2,1)S(1)}, bf16[2,256,128]{2,1,0:T(8,128)(2,1)S(1)}, u32[]{:S(2)}, u32[]{:S(2)}) collective-permute-start(bf16[2,256,128]{2,1,0:T(8,128)(2,1)S(1)} %get-tuple-element.82), channel_id=1, source_target_pairs={{0,2},{1,3},{2,0},{3,1},{4,6},{5,7},{6,4},{7,5},{8,10},{9,11},{10,... | collective-permute-start | bytes 393224 | tf_op jit(solution)/shard_map/ppermute | solution.py:252
  8.4 12.1 %collective-permute-start.2 = (bf16[2,272,128]{2,1,0:T(8,128)(2,1)S(1)}, bf16[2,272,128]{2,1,0:T(8,128)(2,1)S(1)}, u32[]{:S(2)}, u32[]{:S(2)}) collective-permute-start(bf16[2,272,128]{2,1,0:T(8,128)(2,1)S(1)} %get-tuple-element.75), channel_id=1, source_target_pairs={{0,6},{1,7},{2,4},{3,5},{4,2},{5,3},{6,0},{7,1},{8,14},{9,15},{10,... | collective-permute-start | bytes 417800 | tf_op jit(solution)/shard_map/ppermute | solution.py:252
  11.4 9.2 %collective-permute-start.1 = (bf16[2,272,128]{2,1,0:T(8,128)(2,1)S(1)}, bf16[2,272,128]{2,1,0:T(8,128)(2,1)S(1)}, u32[]{:S(2)}, u32[]{:S(2)}) collective-permute-start(bf16[2,272,128]{2,1,0:T(8,128)(2,1)S(1)} %get-tuple-element.76), channel_id=1, source_target_pairs={{0,4},{1,5},{2,6},{3,7},{4,0},{5,1},{6,2},{7,3},{8,12},{9,13},{10,... | collective-permute-start | bytes 417800 | tf_op jit(solution)/shard_map/ppermute | solution.py:252
  22.4 16.6 %collective-permute-start.11 = (bf16[8,2,128,128]{3,2,1,0:T(8,128)(2,1)S(1)}, bf16[8,2,128,128]{3,2,1,0:T(8,128)(2,1)S(1)}, u32[]{:S(2)}, u32[]{:S(2)}) collective-permute-start(bf16[8,2,128,128]{3,2,1,0:T(8,128)(2,1)S(1)} %bitcast.4), channel_id=1, source_target_pairs={{0,8},{8,0},{16,24},{24,16},{1,9},{9,1},{17,25},{25,17},{2,10},{10... | collective-permute-start | bytes 1572872 | tf_op jit(solution)/shard_map/ppermute | solution.py:263
  24.0 15.0 %collective-permute-start.10 = (bf16[8,2,128,128]{3,2,1,0:T(8,128)(2,1)S(1)}, bf16[8,2,128,128]{3,2,1,0:T(8,128)(2,1)S(1)}, u32[]{:S(2)}, u32[]{:S(2)}) collective-permute-start(bf16[8,2,128,128]{3,2,1,0:T(8,128)(2,1)S(1)} %bitcast.5), channel_id=1, source_target_pairs={{8,16},{16,8},{9,17},{17,9},{10,18},{18,10},{11,19},{19,11},{12,20... | collective-permute-start | bytes 1572872 | tf_op jit(solution)/shard_map/ppermute | solution.py:263
  31.7 17.2 %collective-permute-start.9 = (bf16[8,2,128,128]{3,2,1,0:T(8,128)(2,1)S(1)}, bf16[8,2,128,128]{3,2,1,0:T(8,128)(2,1)S(1)}, u32[]{:S(2)}, u32[]{:S(2)}) collective-permute-start(bf16[8,2,128,128]{3,2,1,0:T(8,128)(2,1)S(1)} %bitcast.7), channel_id=1, source_target_pairs={{0,8},{8,0},{16,24},{24,16},{1,9},{9,1},{17,25},{25,17},{2,10},{10... | collective-permute-start | bytes 1572872 | tf_op jit(solution)/shard_map/ppermute | solution.py:263
  36.1 12.8 %collective-permute-start.8 = (bf16[8,2,128,128]{3,2,1,0:T(8,128)(2,1)S(1)}, bf16[8,2,128,128]{3,2,1,0:T(8,128)(2,1)S(1)}, u32[]{:S(2)}, u32[]{:S(2)}) collective-permute-start(bf16[8,2,128,128]{3,2,1,0:T(8,128)(2,1)S(1)} %bitcast.8), channel_id=1, source_target_pairs={{8,16},{16,8},{9,17},{17,9},{10,18},{18,10},{11,19},{19,11},{12,20... | collective-permute-start | bytes 1572872 | tf_op jit(solution)/shard_map/ppermute | solution.py:263
  39.0 14.1 %collective-permute-start.14 = (bf16[8,2,128,128]{3,2,1,0:T(8,128)(2,1)S(1)}, bf16[8,2,128,128]{3,2,1,0:T(8,128)(2,1)S(1)}, u32[]{:S(2)}, u32[]{:S(2)}) collective-permute-start(bf16[8,2,128,128]{3,2,1,0:T(8,128)(2,1)S(1)} %collective-permute-done.11.refs_0_), channel_id=1, source_target_pairs={{8,16},{16,8},{9,17},{17,9},{10,18},{18,10},{11,19},{19,11},{12,20... | collective-permute-start | bytes 1572872 | tf_op jit(solution)/shard_map/ppermute | solution.py:263
  39.7 20.5 %collective-permute-start.15 = (bf16[8,2,128,128]{3,2,1,0:T(8,128)(2,1)S(1)}, bf16[8,2,128,128]{3,2,1,0:T(8,128)(2,1)S(1)}, u32[]{:S(2)}, u32[]{:S(2)}) collective-permute-start(bf16[8,2,128,128]{3,2,1,0:T(8,128)(2,1)S(1)} %collective-permute-done.10.refs_1_), channel_id=1, source_target_pairs={{8,0},{16,24},{9,1},{17,25},{10,2},{18,26},{11,3},{19,27},{12,4},{... | collective-permute-start | bytes 1572872 | tf_op jit(solution)/shard_map/ppermute | solution.py:263
  48.9 13.4 %collective-permute-start.12 = (bf16[8,2,128,128]{3,2,1,0:T(8,128)(2,1)S(1)}, bf16[8,2,128,128]{3,2,1,0:T(8,128)(2,1)S(1)}, u32[]{:S(2)}, u32[]{:S(2)}) collective-permute-start(bf16[8,2,128,128]{3,2,1,0:T(8,128)(2,1)S(1)} %collective-permute-done.9.refs_0_), channel_id=1, source_target_pairs={{8,16},{16,8},{9,17},{17,9},{10,18},{18,10},{11,19},{19,11},{12,20... | collective-permute-start | bytes 1572872 | tf_op jit(solution)/shard_map/ppermute | solution.py:263
  49.6 20.6 %collective-permute-start.13 = (bf16[8,2,128,128]{3,2,1,0:T(8,128)(2,1)S(1)}, bf16[8,2,128,128]{3,2,1,0:T(8,128)(2,1)S(1)}, u32[]{:S(2)}, u32[]{:S(2)}) collective-permute-start(bf16[8,2,128,128]{3,2,1,0:T(8,128)(2,1)S(1)} %collective-permute-done.8.refs_1_), channel_id=1, source_target_pairs={{8,0},{16,24},{9,1},{17,25},{10,2},{18,26},{11,3},{19,27},{12,4},{... | collective-permute-start | bytes 1572872 | tf_op jit(solution)/shard_map/ppermute | solution.py:263
  70.3 18.5 %collective-permute-start.16 = (bf16[8,2,128,128]{3,2,1,0:T(8,128)(2,1)S(1)}, bf16[8,2,128,128]{3,2,1,0:T(8,128)(2,1)S(1)}, u32[]{:S(2)}, u32[]{:S(2)}) collective-permute-start(bf16[8,2,128,128]{3,2,1,0:T(8,128)(2,1)S(1)} %collective-permute-done.12.refs_1_), channel_id=1, source_target_pairs={{8,0},{16,24},{9,1},{17,25},{10,2},{18,26},{11,3},{19,27},{12,4},{... | collective-permute-start | bytes 1572872 | tf_op jit(solution)/shard_map/ppermute | solution.py:263
  71.5 27.1 %collective-permute-start.24 = (bf16[8,2,128,128]{3,2,1,0:T(8,128)(2,1)S(1)}, bf16[8,2,128,128]{3,2,1,0:T(8,128)(2,1)S(1)}, u32[]{:S(2)}, u32[]{:S(2)}) collective-permute-start(bf16[8,2,128,128]{3,2,1,0:T(8,128)(2,1)S(1)} %collective-permute-done.14.refs_1_), channel_id=1, source_target_pairs={{8,0},{16,24},{9,1},{17,25},{10,2},{18,26},{11,3},{19,27},{12,4},{... | collective-permute-start | bytes 1572872 | tf_op jit(solution)/shard_map/ppermute | solution.py:263
  91.8 13.5 %collective-permute-start.22 = (bf16[1024,128]{1,0:T(8,128)(2,1)S(1)}, bf16[1024,128]{1,0:T(8,128)(2,1)S(1)}, u32[]{:S(2)}, u32[]{:S(2)}) collective-permute-start(bf16[1024,128]{1,0:T(8,128)(2,1)S(1)} %attend_1_3.1.refs_0_), channel_id=1, source_target_pairs={{0,6},{1,7},{2,4},{3,5},{4,2},{5,3},{6,0},{7,1},{8,14},{9,15},{10,... | collective-permute-start | bytes 786440 | tf_op jit(solution)/shard_map/ppermute | solution.py:252
  93.3 13.4 %collective-permute-start.20 = (bf16[1024,128]{1,0:T(8,128)(2,1)S(1)}, bf16[1024,128]{1,0:T(8,128)(2,1)S(1)}, u32[]{:S(2)}, u32[]{:S(2)}) collective-permute-start(bf16[1024,128]{1,0:T(8,128)(2,1)S(1)} %attend_1_3.1.refs_0_), channel_id=1, source_target_pairs={{0,4},{1,5},{2,6},{3,7},{4,0},{5,1},{6,2},{7,3},{8,12},{9,13},{10,... | collective-permute-start | bytes 786440 | tf_op jit(solution)/shard_map/ppermute | solution.py:252
  101.7 10.2 %collective-permute-start.30 = (bf16[1024,128]{1,0:T(8,128)(2,1)S(1)}, bf16[1024,128]{1,0:T(8,128)(2,1)S(1)}, u32[]{:S(2)}, u32[]{:S(2)}) collective-permute-start(bf16[1024,128]{1,0:T(8,128)(2,1)S(1)} %attend_0_3.1.refs_0_), channel_id=1, source_target_pairs={{0,6},{1,7},{2,4},{3,5},{4,2},{5,3},{6,0},{7,1},{8,14},{9,15},{10,... | collective-permute-start | bytes 786440 | tf_op jit(solution)/shard_map/ppermute | solution.py:252
  103.2 12.1 %collective-permute-start.28 = (bf16[1024,128]{1,0:T(8,128)(2,1)S(1)}, bf16[1024,128]{1,0:T(8,128)(2,1)S(1)}, u32[]{:S(2)}, u32[]{:S(2)}) collective-permute-start(bf16[1024,128]{1,0:T(8,128)(2,1)S(1)} %attend_0_3.1.refs_0_), channel_id=1, source_target_pairs={{0,4},{1,5},{2,6},{3,7},{4,0},{5,1},{6,2},{7,3},{8,12},{9,13},{10,... | collective-permute-start | bytes 786440 | tf_op jit(solution)/shard_map/ppermute | solution.py:252
  104.7 12.6 %collective-permute-start.18 = (bf16[1024,128]{1,0:T(8,128)(2,1)S(1)}, bf16[1024,128]{1,0:T(8,128)(2,1)S(1)}, u32[]{:S(2)}, u32[]{:S(2)}) collective-permute-start(bf16[1024,128]{1,0:T(8,128)(2,1)S(1)} %attend_1_3.1.refs_0_), channel_id=1, source_target_pairs={{0,2},{1,3},{2,0},{3,1},{4,6},{5,7},{6,4},{7,5},{8,10},{9,11},{10,... | collective-permute-start | bytes 786440 | tf_op jit(solution)/shard_map/ppermute | solution.py:252
  105.2 15.4 %collective-permute-start.26 = (bf16[1024,128]{1,0:T(8,128)(2,1)S(1)}, bf16[1024,128]{1,0:T(8,128)(2,1)S(1)}, u32[]{:S(2)}, u32[]{:S(2)}) collective-permute-start(bf16[1024,128]{1,0:T(8,128)(2,1)S(1)} %attend_0_3.1.refs_0_), channel_id=1, source_target_pairs={{0,2},{1,3},{2,0},{3,1},{4,6},{5,7},{6,4},{7,5},{8,10},{9,11},{10,... | collective-permute-start | bytes 786440 | tf_op jit(solution)/shard_map/ppermute | solution.py:252
  106.7 13.9 %collective-permute-start.25 = (bf16[1024,128]{1,0:T(8,128)(2,1)S(1)}, bf16[1024,128]{1,0:T(8,128)(2,1)S(1)}, u32[]{:S(2)}, u32[]{:S(2)}) collective-permute-start(bf16[1024,128]{1,0:T(8,128)(2,1)S(1)} %attend_0_3.1.refs_0_), channel_id=1, source_target_pairs={{0,1},{1,0},{2,3},{3,2},{4,5},{5,4},{6,7},{7,6},{8,9},{9,8},{10,11... | collective-permute-start | bytes 786440 | tf_op jit(solution)/shard_map/ppermute | solution.py:252
  111.9 9.3 %collective-permute-start.31 = (bf16[1024,128]{1,0:T(8,128)(2,1)S(1)}, bf16[1024,128]{1,0:T(8,128)(2,1)S(1)}, u32[]{:S(2)}, u32[]{:S(2)}) collective-permute-start(bf16[1024,128]{1,0:T(8,128)(2,1)S(1)} %collective-permute-done.30.refs_6_), channel_id=1, source_target_pairs={{0,1},{1,0},{2,3},{3,2},{4,5},{5,4},{6,7},{7,6},{8,9},{9,8},{10,11... | collective-permute-start | bytes 786440 | tf_op jit(solution)/shard_map/ppermute | solution.py:252
  117.3 6.3 %collective-permute-start.17 = (bf16[1024,128]{1,0:T(8,128)(2,1)S(1)}, bf16[1024,128]{1,0:T(8,128)(2,1)S(1)}, u32[]{:S(2)}, u32[]{:S(2)}) collective-permute-start(bf16[1024,128]{1,0:T(8,128)(2,1)S(1)} %attend_1_3.1.refs_0_), channel_id=1, source_target_pairs={{0,1},{1,0},{2,3},{3,2},{4,5},{5,4},{6,7},{7,6},{8,9},{9,8},{10,11... | collective-permute-start | bytes 786440 | tf_op jit(solution)/shard_map/ppermute | solution.py:252
  (12 other events, 37.1 us)

commit v5 on v4

v5 whole, which is shorter than its diff:
```python
import functools
import math

import jax
import jax.numpy as jnp
from jax import lax
from jax.experimental import pallas as pl
from jax.experimental.pallas import tpu as pltpu
from jax.sharding import PartitionSpec as P

HEADS = 16
HEAD_DIM = 128
BLOCK = 128
NEG = -1e30
EXP2_SCALE = math.log2(math.e) / math.sqrt(HEAD_DIM)
GROUP = 8
ROW_SHIFT = 16
VMEM_BYTES = 40 * 1024 * 1024

VMEM = pl.BlockSpec(memory_space=pltpu.VMEM)
SMEM = pl.BlockSpec(memory_space=pltpu.SMEM)
ANY = pl.BlockSpec(memory_space=pl.ANY)


def params():
    return pltpu.CompilerParams(vmem_limit_bytes=VMEM_BYTES)


def mask_rows(rows):
    return -(-rows // 16) * 16


def pack_kernel(n_ka, heads, me_ref, k_ref, v_ref, mask_ref, *out_refs):
    key_blocks = k_ref.shape[0] // BLOCK
    for c in range(heads):
        for k in range(n_ka):
            col = pl.multiple_of(((me_ref[0] ^ k) * heads + c) * HEAD_DIM, HEAD_DIM)
            for t in range(key_blocks):
                rows, at = slice(t * BLOCK, (t + 1) * BLOCK), 2 * t * BLOCK
                out_refs[c][k, at : at + BLOCK] = k_ref[rows, pl.ds(col, HEAD_DIM)]
                out_refs[c][k, at + BLOCK : at + 2 * BLOCK] = v_ref[rows, pl.ds(col, HEAD_DIM)].T
    rows = mask_rows(mask_ref.shape[0])
    row = lax.broadcasted_iota(jnp.int32, (rows, HEAD_DIM), 0)
    column = lax.broadcasted_iota(jnp.int32, (rows, HEAD_DIM), 1)
    mask = jnp.zeros((rows, HEAD_DIM), jnp.int32)
    for i in range(mask_ref.shape[0]):
        for j in range(mask_ref.shape[1]):
            mask = jnp.where((row == i) & (column == j), mask_ref[i, j], mask)
    mask = mask.astype(jnp.float32).astype(k_ref.dtype)
    for k in range(n_ka):
        out_refs[0][k, 2 * key_blocks * BLOCK :] = mask


def pack(me, keys, values, mask, n_ka, heads):
    sizes = [2 * keys.shape[0] + (mask_rows(mask.shape[0]) if c == 0 else 0) for c in range(heads)]
    return pl.pallas_call(
        functools.partial(pack_kernel, n_ka, heads),
        out_shape=[jax.ShapeDtypeStruct((n_ka, size, HEAD_DIM), keys.dtype) for size in sizes],
        in_specs=[SMEM, VMEM, VMEM, SMEM],
        out_specs=[VMEM] * heads,
        compiler_params=params(),
        name="pack",
    )(me, keys, values, mask)


def plan_kernel(steps, n_pb, n_slots, key_blocks, rows, relay, pb_ref, *refs):
    mask_refs, count_ref, live_refs = refs[: -len(steps) - 1], refs[-len(steps) - 1], refs[-len(steps) :]
    pb = pb_ref[0]
    sign = 1 - 2 * (pb & 1)
    inner = ((pb > 0) & (pb < n_pb - 1)).astype(jnp.int32)
    for step, (sources, live) in enumerate(zip(steps, live_refs)):
        total = jnp.int32(0)
        for guest, mask_ref in enumerate(mask_refs):

            def row_step(r, base, guest=guest, mask_ref=mask_ref):
                count = jnp.int32(0)
                for s, (delta, open_to_guests) in enumerate(sources):
                    if guest and not open_to_guests:
                        continue
                    j = pb + delta * sign
                    inside = ((j >= 0) & (j < n_pb)).astype(jnp.int32)
                    if relay and abs(delta) > 1:
                        inside = inside * inner
                    j = jnp.clip(j, 0, n_pb - 1)
                    for slot in range(n_slots):
                        for t in range(key_blocks):
                            block = (s * n_slots + slot) * key_blocks + t
                            live[2 * base + count] = ((r + guest * rows) << ROW_SHIFT) + block
                            column = j * key_blocks + t
                            count += inside * mask_ref[(slot * rows + r) * (n_pb * key_blocks) + column]
                live[2 * base + count] = -1
                return base + ((count + 1) >> 1)

            total = lax.fori_loop(0, rows, row_step, total)
        for u in range(GROUP):
            live[2 * (total + u)] = 0
            live[2 * (total + u) + 1] = -1
        count_ref[step] = total


def plan(pb, masks, steps, n_pb, n_slots, key_blocks, rows, relay):
    sizes = [len(masks) * rows * ((len(step) * n_slots * key_blocks + 2) // 2) + GROUP for step in steps]
    out_shape = [jax.ShapeDtypeStruct((len(steps),), jnp.int32)]
    out_shape += [jax.ShapeDtypeStruct((2 * size,), jnp.int32) for size in sizes]
    counts, *lives = pl.pallas_call(
        functools.partial(plan_kernel, steps, n_pb, n_slots, key_blocks, rows, relay),
        out_shape=out_shape,
        in_specs=[SMEM] * (1 + len(masks)),
        out_specs=[SMEM] * len(out_shape),
        compiler_params=params(),
        name="plan",
    )(pb, *masks)
    return [(counts, i, live) for i, live in enumerate(lives)]


def attend_kernel(n_src, entry, first, mode, guests, count_ref, live_ref, head_ref, q_all, *refs):
    n_kv = n_src
    guest_ref, refs = (refs[0], refs[1:]) if guests else (None, refs)
    kv_refs, refs = refs[:n_kv], refs[n_kv:]
    state_in, refs = ((), refs) if first else (refs[:3], refs[3:])
    if mode == "last":
        (out_ref, kv, q_ref, qt_ref, *state, sems) = refs
    elif mode == "send":
        (*state, part_ref, stat_ref, kv, q_ref, qt_ref, sems) = refs
    else:
        (*state, kv, q_ref, qt_ref, sems) = refs
    m_ref, l_ref, acc_ref = state
    blocks = kv.shape[0] // n_src
    tokens = q_all.shape[0]
    rows = tokens // BLOCK
    copies = [
        pltpu.make_async_copy(kv_refs[s], kv.at[pl.ds(s * blocks, blocks)], sems.at[s]) for s in range(n_src)
    ]
    copies += [pltpu.make_async_copy(a, b, sems.at[n_src + i]) for i, (a, b) in enumerate(zip(state_in, state))]
    column = pl.multiple_of(head_ref[0] * HEAD_DIM, HEAD_DIM)
    q_own = q_all.at[:, pl.ds(column, HEAD_DIM)]
    copies.append(pltpu.make_async_copy(q_own, q_ref.at[pl.ds(0, tokens)], sems.at[n_src + 3]))
    if guests:
        copies.append(pltpu.make_async_copy(guest_ref, q_ref.at[pl.ds(tokens, tokens)], sems.at[n_src + 4]))
    for copy in copies:
        copy.start()
    if first:
        m_ref[...] = jnp.full(m_ref.shape, NEG, jnp.float32)
        l_ref[...] = jnp.zeros(l_ref.shape, jnp.float32)
        acc_ref[...] = jnp.zeros(acc_ref.shape, jnp.float32)
    for copy in copies:
        copy.wait()
    total = count_ref[entry]

    for r in range(rows * (2 if guests else 1)):
        qt_ref[r] = q_ref[r * BLOCK : (r + 1) * BLOCK, :].T
    nn = (((1,), (0,)), ((), ()))
    f32, bf16 = jnp.float32, jnp.bfloat16

    def group_step(g, _):
        found = []
        for u in range(GROUP):
            index = g * GROUP + u
            code0, code1 = live_ref[2 * index], live_ref[2 * index + 1]
            r = code0 >> ROW_SHIFT
            b0 = code0 & ((1 << ROW_SHIFT) - 1)
            b1 = jnp.maximum(code1, 0) & ((1 << ROW_SHIFT) - 1)
            x = lax.dot_general(jnp.concatenate([kv[b0, 0], kv[b1, 0]]), qt_ref[r], nn, preferred_element_type=f32)
            x0 = jnp.where(index < total, x[:BLOCK], NEG)
            x1 = jnp.where(code1 >= 0, x[BLOCK:], NEG)
            top = jnp.max(jnp.maximum(x0, x1), axis=0, keepdims=True)
            w0 = jnp.exp2((x0 - top) * EXP2_SCALE)
            w1 = jnp.exp2((x1 - top) * EXP2_SCALE)
            total_w = jnp.sum(w0 + w1, axis=0, keepdims=True)
            w = jnp.concatenate([w0.astype(bf16), w1.astype(bf16)])
            v = jnp.concatenate([kv[b0, 1], kv[b1, 1]], axis=1)
            found.append((r, top, total_w, lax.dot_general(v, w, nn, preferred_element_type=f32)))
        for r, top, total_w, part in found:
            m = m_ref[r]
            m_new = jnp.maximum(m, top)
            alpha = jnp.exp2((m - m_new) * EXP2_SCALE)
            beta = jnp.exp2((top - m_new) * EXP2_SCALE)
            m_ref[r] = m_new
            l_ref[r] = l_ref[r] * alpha + total_w * beta
            acc_ref[r] = acc_ref[r] * alpha + part * beta
        return 0

    lax.fori_loop(0, (total + GROUP - 1) // GROUP, group_step, 0)
    if mode == "last":
        for r in range(rows):
            out_ref[r * BLOCK : (r + 1) * BLOCK, :] = (acc_ref[r] / l_ref[r]).T.astype(out_ref.dtype)
    if mode == "send":
        for r in range(rows):
            l = l_ref[rows + r]
            part_ref[r] = (acc_ref[rows + r] / jnp.where(l > 0, l, 1.0)).astype(part_ref.dtype)
            stat_ref[0, r], stat_ref[1, r] = m_ref[rows + r], l


def attend(listed, head, queries, guest, sources, state, mode, sets, name):
    counts, entry, live = listed
    tokens, dtype = queries.shape[0], queries.dtype
    rows = tokens // BLOCK
    first = state is None
    state = () if first else tuple(state)
    stat = (sets * rows, 1, BLOCK)
    shapes = [stat, stat, (sets * rows, HEAD_DIM, BLOCK)]
    if mode == "last":
        out_shape = [jax.ShapeDtypeStruct((tokens, HEAD_DIM), dtype)]
    else:
        out_shape = [jax.ShapeDtypeStruct(shape, jnp.float32) for shape in shapes]
    if mode == "send":
        out_shape.append(jax.ShapeDtypeStruct((rows, HEAD_DIM, BLOCK), dtype))
        out_shape.append(jax.ShapeDtypeStruct((2, rows, 1, BLOCK), jnp.float32))
    n_src = len(sources)
    blocks = sources[0].shape[0]
    guests = () if guest is None else (guest,)
    met = (1 + len(guests)) * rows
    scratch = [pltpu.VMEM((n_src * blocks,) + sources[0].shape[1:], dtype)]
    scratch += [pltpu.VMEM((met * BLOCK, HEAD_DIM), dtype), pltpu.VMEM((met, HEAD_DIM, BLOCK), dtype)]
    if mode == "last":
        scratch += [pltpu.VMEM(shape, jnp.float32) for shape in shapes]
    scratch.append(pltpu.SemaphoreType.DMA((n_src + 5,)))
    live_blocks = rows * n_src * blocks // 4
    return pl.pallas_call(
        functools.partial(attend_kernel, n_src, entry, first, mode, bool(guests)),
        out_shape=out_shape,
        in_specs=[SMEM, SMEM, SMEM, ANY] + [ANY] * (len(guests) + n_src + len(state)),
        out_specs=[VMEM] * len(out_shape),
        scratch_shapes=scratch,
        compiler_params=params(),
        cost_estimate=pl.CostEstimate(
            flops=live_blocks * 4 * BLOCK * BLOCK * HEAD_DIM,
            bytes_accessed=8 * tokens * HEAD_DIM + 2 * n_src * sources[0].size,
            transcendentals=live_blocks * BLOCK * BLOCK,
        ),
        name=name,
    )(counts, live, head, queries, *guests, *sources, *state)


def merge_kernel(outer_ref, m_ref, l_ref, acc_ref, part_ref, stat_ref, out_ref):
    outer = outer_ref[0] > 0
    for r in range(part_ref.shape[0]):
        m, l = m_ref[r], l_ref[r]
        extra = jnp.where(outer, stat_ref[1, r], 0.0)
        top = jnp.where(outer, stat_ref[0, r], NEG)
        m_new = jnp.maximum(m, top)
        alpha = jnp.exp2((m - m_new) * EXP2_SCALE)
        beta = jnp.exp2((top - m_new) * EXP2_SCALE) * extra
        done = (acc_ref[r] * alpha + part_ref[r].astype(jnp.float32) * beta) / (l * alpha + beta)
        out_ref[r * BLOCK : (r + 1) * BLOCK, :] = done.T.astype(out_ref.dtype)


def merge(outer, state, part, stat, name):
    rows = part.shape[0]
    half = lambda x: pl.BlockSpec((rows,) + x.shape[1:], lambda i: (0, 0, 0))
    return pl.pallas_call(
        merge_kernel,
        out_shape=jax.ShapeDtypeStruct((rows * BLOCK, HEAD_DIM), part.dtype),
        grid=(1,),
        in_specs=[SMEM] + [half(x) for x in state] + [VMEM, VMEM],
        out_specs=VMEM,
        compiler_params=params(),
        name=name,
    )(outer, *state, part, stat)


def place_kernel(n_ka, heads, c, me_ref, *refs):
    pieces, out_ref, sems = refs[:n_ka], refs[-2], refs[-1]
    copies = []
    for k in range(n_ka):
        col = pl.multiple_of(((me_ref[0] ^ k) * heads + c) * HEAD_DIM, HEAD_DIM)
        copies.append(pltpu.make_async_copy(pieces[k], out_ref.at[:, pl.ds(col, HEAD_DIM)], sems.at[k]))
    for copy in copies:
        copy.start()
    for copy in copies:
        copy.wait()


def place(me, pieces, whole, c, heads):
    n_ka = len(pieces)
    rows = pieces[0].shape[0]
    extra = () if whole is None else (whole,)
    return pl.pallas_call(
        functools.partial(place_kernel, n_ka, heads, c),
        out_shape=jax.ShapeDtypeStruct((rows, HEADS * HEAD_DIM), pieces[0].dtype),
        in_specs=[SMEM] + [ANY] * (n_ka + len(extra)),
        out_specs=ANY,
        scratch_shapes=[pltpu.SemaphoreType.DMA((n_ka,))],
        input_output_aliases={1 + n_ka: 0} if extra else {},
        compiler_params=params(),
        name="place",
    )(me, *pieces, *extra)


def local(n_pb, n_ka, queries, keys, values, block_mask):
    heads = HEADS // n_ka
    shard = keys.shape[0]
    key_blocks = shard // BLOCK
    rows = queries.shape[0] // BLOCK
    me = lax.axis_index("ka").astype(jnp.int32)
    pb = lax.axis_index("pb").astype(jnp.int32)
    me1, pb1 = me[None], pb[None]
    relay = n_pb >= 4 and n_pb % 2 == 0
    early = heads - 1 if heads > 1 and n_pb > 1 else None

    def swap(x, k):
        return lax.ppermute(x, "ka", [(i, i ^ k) for i in range(n_ka)])

    def hops(odd, step):
        found = []
        for low in range(odd, n_pb - 1, 2):
            found += [(low, low + 1)] if low - (step - 1) >= 0 else []
            found += [(low + 1, low)] if low + 1 + (step - 1) < n_pb else []
        if relay and step > 1:
            found = [(i, j) for i, j in found if 0 < j < n_pb - 1]
        return found

    def exchange(x, odd, step):
        found = hops(odd, step)
        return lax.ppermute(x, "pb", found) if found else None

    def inward(x):
        return lax.ppermute(x, "pb", [(0, 1), (n_pb - 1, n_pb - 2)])

    def outward(x):
        return lax.ppermute(x, "pb", [(1, 0), (n_pb - 2, n_pb - 1)])

    def sort(parts):
        mixed = []
        for k in range(0, n_ka, 2):
            two = [x[k : k + 2] for x in parts]
            joined = jnp.concatenate(two) if len(two) > 1 else two[0]
            joined = swap(joined, k) if k else joined
            mixed.append(joined.reshape((len(parts), 2) + joined.shape[1:]))
        theirs = swap(jnp.stack([x[:, 1] for x in mixed], axis=1), 1)
        return [jnp.concatenate([jnp.stack([x[i, 0] for x in mixed]), theirs[i]]) for i in range(len(parts))]

    def blocks(x):
        return x[:, : 2 * shard].reshape(n_ka * key_blocks, 2, BLOCK, HEAD_DIM)

    def after(arrays, done):
        return arrays if done is None else lax.optimization_barrier((arrays, done))[0]

    def flags(x):
        return x[:, :rows, : block_mask.shape[1]].astype(jnp.int32).reshape(-1)

    packed = pack(me1, keys, values, block_mask, n_ka, heads)
    ahead = [exchange(packed[early], odd, 1) for odd in (0, 1)] if early is not None else []
    ahead_from = [i for i, x in enumerate(ahead) if x is not None]

    owns = []
    for c in range(heads):
        (own,) = sort([packed[c]])
        owns.append(blocks(own))
        if c == 0:
            marks = own[:, 2 * shard :]
    masks = [flags(marks)]

    steps = [((0, False),)]
    for step in range(1, n_pb):
        found = (((step, False),) if hops(0, step) else ()) + (((-step, True),) if hops(1, step) else ())
        if found:
            steps.append(found)
    last = len(steps) - 1
    sets = 2 if relay else 1
    lists = plan(pb1, masks, steps[:1], n_pb, n_ka, key_blocks, rows, relay)
    if relay:
        masks.append(flags(inward(marks)))
    lists += plan(pb1, masks, steps[1:], n_pb, n_ka, key_blocks, rows, relay) if last else []
    guest = [None] * heads
    state = [None] * heads
    over = [None] * heads
    mode = "send" if relay else "last"

    def run(c, step, sources):
        head = me1 * heads + c
        kind = mode if step == last else "keep"
        seen = guest[c] if step else None
        name = f"attend_{c}_{step}"
        return attend(lists[step], head, queries, seen, sources, state[c], kind, sets, name)

    done = None
    for step in range(1, last + 1):
        for c in range(heads):
            if step == 1 and c == early:
                sorted_ahead = sort([ahead[i] for i in ahead_from])
                arrived = [None, None]
                for i, x in zip(ahead_from, sorted_ahead):
                    arrived[i] = blocks(x)
            elif step == 1:
                arrived = [exchange(owns[c], odd, 1) for odd in (0, 1)]
            else:
                over[c] = after(over[c], done)
                arrived = [exchange(over[c][1], 0, step), exchange(over[c][0], 1, step)]
            sources = [owns[c]] if step == 1 else [x for x in over[c] if x is not None]
            if relay and step == (2 if c else 1):
                q = lax.dynamic_slice_in_dim(queries, (me * heads + c) * HEAD_DIM, HEAD_DIM, 1)
                guest[c] = inward(after(q, done if c else arrived[0]))
            state[c] = run(c, step - 1, sources)
            done = state[c][0]
            over[c] = arrived

    whole = None
    for c in range(heads):
        sources = [x for x in over[c] if x is not None] if last else [owns[c]]
        found = run(c, last, sources)
        if relay:
            outer = ((pb == 0) | (pb == n_pb - 1)).astype(jnp.int32)[None]
            out = merge(outer, found[:3], outward(found[3]), outward(found[4]), f"merge_{c}")
        else:
            out = found[0]
        pieces = [out] + [swap(out, k) for k in range(2, n_ka, 2)]
        others = [swap(x, 1) for x in pieces]
        pieces = [x for two in zip(pieces, others) for x in two]
        whole = place(me1, pieces, whole, c, heads)
    return whole


def solution(mesh):
    n_pb, n_ka = mesh.shape["pb"], mesh.shape["ka"]
    return jax.shard_map(
        functools.partial(local, n_pb, n_ka),
        mesh=mesh,
        in_specs=(P("pb", None), P(("ka", "pb"), None), P(("ka", "pb"), None), P("pb", "ka")),
        out_specs=P("pb", None),
        check_vma=False,
    )
```

time: 125 us -> 142 us (1.14)
  the two profiles are of different devices: /device:TPU:0 before, /device:TPU:9 now
where the time goes in v5:
time: 142 us
  starting transfers between devices  58.5 us (41%)
  waiting for transfers between devices  41.2 us (29%)
  Pallas kernels  29.6 us (21%)
  local copies, waits for them, and re-layouts  11.4 us (8%)
    ppermute x26, starting transfers between devices, swap(): return lax.ppermute(x, 'ka', [(i, i ^ k) for i in range(n_ka)])  36.8 us
    ppermute x26, waiting for transfers between devices, swap(): return lax.ppermute(x, 'ka', [(i, i ^ k) for i in range(n_ka)])  33.2 us
    pallas_call x6, Pallas kernels, attend(): pl.pallas_call(functools.partial(attend_kernel, n_src, entry, first, mode...  21.1 us
    ppermute x6, starting transfers between devices, exchange(): return lax.ppermute(x, 'pb', found) if found else None  11.9 us
    ppermute x3, waiting for transfers between devices, inward(): return lax.ppermute(x, 'pb', [(0, 1), (n_pb - 1, n_pb - 2)])  7.95 us
    ppermute x4, starting transfers between devices, outward(): return lax.ppermute(x, 'pb', [(1, 0), (n_pb - 2, n_pb - 1)])  5.99 us
    unnamed x25, local copies, waits for them, and re-layouts  5.22 us
    ppermute x3, starting transfers between devices, inward(): return lax.ppermute(x, 'pb', [(0, 1), (n_pb - 1, n_pb - 2)])  3.88 us
  transfers between devices with their start and end apart: 39, of which 14 were waited for; matrix products, arithmetic and copies ran while one was open for 5% of the time, Pallas kernels for 19%

profile of v5, /device:TPU:9, one launch (start us, length us, event | category | flops | bytes accessed | tf_op | source)
XLA Modules:
  0.0 141.6 jit_solution(11706235212731221677)
XLA Ops:
  4.6 4.5 %collective-permute-start.14 = (bf16[8,256,128]{2,1,0:T(8,128)(2,1)}, bf16[8,256,128]{2,1,0:T(8,128)(2,1)}, u32[]{:S(2)}, u32[]{:S(2)}) collective-permute-start(bf16[8,256,128]{2,1,0:T(8,128)(2,1)} %get-tuple-element.47), channel_id=1, source_target_pairs={{8,16},{16,8},{9,17},{17,9},{10,18},{18,10},{11,19},{19,11},{12,20... | collective-permute-start | bytes 1572872 | tf_op jit(solution)/shard_map/ppermute | solution.py:315
  9.1 2.2 %collective-permute-start.2 = (bf16[2,272,128]{2,1,0:T(8,128)(2,1)S(1)}, bf16[2,272,128]{2,1,0:T(8,128)(2,1)S(1)}, u32[]{:S(2)}, u32[]{:S(2)}) collective-permute-start(bf16[2,272,128]{2,1,0:T(8,128)(2,1)S(1)} %get-tuple-element.77), channel_id=1, source_target_pairs={{0,6},{1,7},{2,4},{3,5},{4,2},{5,3},{6,0},{7,1},{8,14},{9,15},{10,... | collective-permute-start | bytes 417800 | tf_op jit(solution)/shard_map/ppermute | solution.py:302
  18.8 3.9 %collective-permute-done.9 = bf16[2,256,128]{2,1,0:T(8,128)(2,1)S(1)} collective-permute-done((bf16[2,256,128]{2,1,0:T(8,128)(2,1)S(1)}, bf16[2,256,128]{2,1,0:T(8,128)(2,1)S(1)}, u32[]{:S(2)}, u32[]{:S(2)}) %collective-permute-start.9) | collective-permute-done | bytes 131104 | tf_op jit(solution)/shard_map/ppermute | solution.py:302
  24.4 2.3 %collective-permute-done.8 = bf16[2,256,128]{2,1,0:T(8,128)(2,1)S(1)} collective-permute-done((bf16[2,256,128]{2,1,0:T(8,128)(2,1)S(1)}, bf16[2,256,128]{2,1,0:T(8,128)(2,1)S(1)}, u32[]{:S(2)}, u32[]{:S(2)}) %collective-permute-start.8) | collective-permute-done | bytes 131104 | tf_op jit(solution)/shard_map/ppermute | solution.py:302
  28.3 3.1 %collective-permute-start.11 = (bf16[1,4,256,128]{3,2,1,0:T(8,128)(2,1)S(1)}, bf16[1,4,256,128]{3,2,1,0:T(8,128)(2,1)S(1)}, u32[]{:S(2)}, u32[]{:S(2)}) collective-permute-start(bf16[1,4,256,128]{3,2,1,0:T(8,128)(2,1)S(1)} %pad_maximum_fusion.2), channel_id=1, source_target_pairs={{0,1},{1,0},{2,3},{3,2},{4,5},{5,4},{6,7},{7,6},{8,9},{9,8},{10,11... | collective-permute-start | bytes 786440 | tf_op jit(solution)/shard_map/ppermute | solution.py:302
  31.5 4.8 %collective-permute-start.3 = (bf16[1,4,272,128]{3,2,1,0:T(8,128)(2,1)S(1)}, bf16[1,4,272,128]{3,2,1,0:T(8,128)(2,1)S(1)}, u32[]{:S(2)}, u32[]{:S(2)}) collective-permute-start(bf16[1,4,272,128]{3,2,1,0:T(8,128)(2,1)S(1)} %pad_maximum_fusion.1), channel_id=1, source_target_pairs={{0,1},{1,0},{2,3},{3,2},{4,5},{5,4},{6,7},{7,6},{8,9},{9,8},{10,11... | collective-permute-start | bytes 835592 | tf_op jit(solution)/shard_map/ppermute | solution.py:302
  38.9 1.9 %collective-permute-start.7 = (bf16[8,2,128,128]{3,2,1,0:T(8,128)(2,1)S(1)}, bf16[8,2,128,128]{3,2,1,0:T(8,128)(2,1)}, u32[]{:S(2)}, u32[]{:S(2)}) collective-permute-start(bf16[8,2,128,128]{3,2,1,0:T(8,128)(2,1)S(1)} %bitcast.51), channel_id=1, source_target_pairs={{8,16},{16,8},{9,17},{17,9},{10,18},{18,10},{11,19},{19,11},{12,20... | collective-permute-start | bytes 1572872 | tf_op jit(solution)/shard_map/ppermute | solution.py:315
  44.0 2.2 %copy-done = bf16[1024,2048]{1,0:T(8,128)(2,1)S(1)} copy-done((bf16[1024,2048]{1,0:T(8,128)(2,1)S(1)}, bf16[1024,2048]{1,0:T(8,128)(2,1)}, u32[]{:S(2)}) %copy-start) | copy-done | bytes 4194328
  46.1 2.9 %attend_0_0.1 = (f32[16,1,128]{2,1,0:T(1,128)S(1)}, f32[16,1,128]{2,1,0:T(1,128)S(1)}, f32[16,128,128]{2,1,0:T(8,128)S(1)}) custom-call(s32[1]{0:T(128)} %get-tuple-element.45.count_ref, s32[96]{0:T(128)S(1)} %get-tuple-element.46.live_ref, s32[1]{0:T(128)S(6)} %mul.8.head_ref, bf16[1024,2048]{1,0:T(8,128)(2,1)S(1)} %copy-done, ...), custom_call_target="tpu_custom_call" | custom-call | flops 134217728 | bytes 1572864 | tf_op jit(solution)/shard_map/attend_0_0/pallas_call | solution.py:219
  49.0 2.9 %attend_1_0.1 = (f32[16,1,128]{2,1,0:T(1,128)S(1)}, f32[16,1,128]{2,1,0:T(1,128)S(1)}, f32[16,128,128]{2,1,0:T(8,128)S(1)}) custom-call(s32[1]{0:T(128)} %get-tuple-element.45.count_ref, s32[96]{0:T(128)S(1)} %get-tuple-element.46.live_ref, s32[1]{0:T(128)S(6)} %add.14.head_ref, bf16[1024,2048]{1,0:T(8,128)(2,1)S(1)} %copy-done, ...), custom_call_target="tpu_custom_call" | custom-call | flops 134217728 | bytes 1572864 | tf_op jit(solution)/shard_map/attend_1_0/pallas_call | solution.py:219
  52.0 2.3 %plan.2 = (s32[2]{0:T(128)S(1)}, s32[304]{0:T(512)S(1)}, s32[176]{0:T(256)S(1)}) custom-call(s32[1]{0:T(128)} %bitcast.2.pb_ref, s32[256]{0:T(256)S(1)} %reshape.101.refs_0_, s32[256]{0:T(256)S(1)} %reshape.103.refs_1_), custom_call_target="tpu_custom_call" | custom-call | tf_op jit(solution)/shard_map/plan/pallas_call | solution.py:105
  60.0 3.9 %collective-permute-done.15 = bf16[4,256,128]{2,1,0:T(8,128)(2,1)S(1)} collective-permute-done((bf16[4,256,128]{2,1,0:T(8,128)(2,1)S(1)}, bf16[4,256,128]{2,1,0:T(8,128)(2,1)S(1)}, u32[]{:S(2)}, u32[]{:S(2)}) %collective-permute-start.15) | collective-permute-done | bytes 262176 | tf_op jit(solution)/shard_map/ppermute | solution.py:302
  64.2 6.6 %collective-permute-done.17 = bf16[4,256,128]{2,1,0:T(8,128)(2,1)S(1)} collective-permute-done((bf16[4,256,128]{2,1,0:T(8,128)(2,1)S(1)}, bf16[4,256,128]{2,1,0:T(8,128)(2,1)S(1)}, u32[]{:S(2)}, u32[]{:S(2)}) %collective-permute-start.17) | collective-permute-done | bytes 262176 | tf_op jit(solution)/shard_map/ppermute | solution.py:302
  76.2 6.5 %collective-permute-done.6.refs_0_ = bf16[1024,128]{1,0:T(8,128)(2,1)S(1)} collective-permute-done((bf16[1024,128]{1,0:T(8,128)(2,1)S(1)}, bf16[1024,128]{1,0:T(8,128)(2,1)S(1)}, u32[]{:S(2)}, u32[]{:S(2)}) %collective-permute-start.6) | collective-permute-done | bytes 262176 | tf_op jit(solution)/shard_map/ppermute | solution.py:318
  82.7 5.2 %attend_0_1.1 = (f32[16,1,128]{2,1,0:T(1,128)S(1)}, f32[16,1,128]{2,1,0:T(1,128)S(1)}, f32[16,128,128]{2,1,0:T(8,128)S(1)}) custom-call(s32[2]{0:T(128)S(1)} %get-tuple-element.41.count_ref, s32[304]{0:T(512)S(1)} %get-tuple-element.43.live_ref, s32[1]{0:T(128)S(6)} %mul.8.head_ref, bf16[1024,2048]{1,0:T(8,128)(2,1)S(1)} %copy-done.1, ...), custom_call_target="tpu_custom_call" | custom-call | flops 268435456 | bytes 2097152 | tf_op jit(solution)/shard_map/attend_0_1/pallas_call | solution.py:219
  91.3 3.0 %attend_0_2.1 = (f32[16,1,128]{2,1,0:T(1,128)S(1)}, f32[16,1,128]{2,1,0:T(1,128)S(1)}, f32[16,128,128]{2,1,0:T(8,128)S(1)}, bf16[8,128,128]{2,1,0:T(8,128)(2,1)S(1)}, f32[2,8,1,128]{3,2,1,0:T(1,128)S(1)}) custom-call(s32[2]{0:T(128)S(1)} %get-tuple-element.41.count_ref, s32[176]{0:T(256)S(1)} %get-tuple-element.42.live_ref, s32[1]{0:T(128)S(6)} %mul.8.head_ref, ...), custom_call_target="tpu_custom_call" | custom-call | flops 134217728 | bytes 1572864 | tf_op jit(solution)/shard_map/attend_0_2/pallas_call | solution.py:219
  94.3 2.1 %collective-permute-start.30 = (bf16[8,128,128]{2,1,0:T(8,128)(2,1)S(1)}, bf16[8,128,128]{2,1,0:T(8,128)(2,1)S(1)}, u32[]{:S(2)}, u32[]{:S(2)}) collective-permute-start(bf16[8,128,128]{2,1,0:T(8,128)(2,1)S(1)} %get-tuple-element.73), channel_id=1, source_target_pairs={{8,0},{16,24},{9,1},{17,25},{10,2},{18,26},{11,3},{19,27},{12,4},{... | collective-permute-start | bytes 786440 | tf_op jit(solution)/shard_map/ppermute | solution.py:321
  99.1 4.2 %attend_1_1.1 = (f32[16,1,128]{2,1,0:T(1,128)S(1)}, f32[16,1,128]{2,1,0:T(1,128)S(1)}, f32[16,128,128]{2,1,0:T(8,128)S(1)}) custom-call(s32[2]{0:T(128)S(1)} %get-tuple-element.41.count_ref, s32[304]{0:T(512)S(1)} %get-tuple-element.43.live_ref, s32[1]{0:T(128)S(6)} %add.14.head_ref, bf16[1024,2048]{1,0:T(8,128)(2,1)S(1)} %copy-done.1, ...), custom_call_target="tpu_custom_call" | custom-call | flops 268435456 | bytes 2097152 | tf_op jit(solution)/shard_map/attend_1_1/pallas_call | solution.py:219
  103.4 3.0 %attend_1_2.1 = (f32[16,1,128]{2,1,0:T(1,128)S(1)}, f32[16,1,128]{2,1,0:T(1,128)S(1)}, f32[16,128,128]{2,1,0:T(8,128)S(1)}, bf16[8,128,128]{2,1,0:T(8,128)(2,1)S(1)}, f32[2,8,1,128]{3,2,1,0:T(1,128)S(1)}) custom-call(s32[2]{0:T(128)S(1)} %get-tuple-element.41.count_ref, s32[176]{0:T(256)S(1)} %get-tuple-element.42.live_ref, s32[1]{0:T(128)S(6)} %add.14.head_ref, ...), custom_call_target="tpu_custom_call" | custom-call | flops 134217728 | bytes 1572864 | tf_op jit(solution)/shard_map/attend_1_2/pallas_call | solution.py:219
  112.0 2.5 %collective-permute-start.32 = (bf16[1024,128]{1,0:T(8,128)(2,1)S(1)}, bf16[1024,128]{1,0:T(8,128)(2,1)S(1)}, u32[]{:S(2)}, u32[]{:S(2)}) collective-permute-start(bf16[1024,128]{1,0:T(8,128)(2,1)S(1)} %merge_0.1.refs_0_), channel_id=1, source_target_pairs={{0,1},{1,0},{2,3},{3,2},{4,5},{5,4},{6,7},{7,6},{8,9},{9,8},{10,11... | collective-permute-start | bytes 786440 | tf_op jit(solution)/shard_map/ppermute | solution.py:302
  115.0 4.8 %collective-permute-start.38 = (bf16[1024,128]{1,0:T(8,128)(2,1)S(1)}, bf16[1024,128]{1,0:T(8,128)(2,1)S(1)}, u32[]{:S(2)}, u32[]{:S(2)}) collective-permute-start(bf16[1024,128]{1,0:T(8,128)(2,1)S(1)} %collective-permute-done.37.refs_6_), channel_id=1, source_target_pairs={{0,1},{1,0},{2,3},{3,2},{4,5},{5,4},{6,7},{7,6},{8,9},{9,8},{10,11... | collective-permute-start | bytes 786440 | tf_op jit(solution)/shard_map/ppermute | solution.py:302
  119.8 2.9 %collective-permute-done.35.refs_4_ = bf16[1024,128]{1,0:T(8,128)(2,1)S(1)} collective-permute-done((bf16[1024,128]{1,0:T(8,128)(2,1)S(1)}, bf16[1024,128]{1,0:T(8,128)(2,1)S(1)}, u32[]{:S(2)}, u32[]{:S(2)}) %collective-permute-start.35) | collective-permute-done | bytes 262176 | tf_op jit(solution)/shard_map/ppermute | solution.py:302
  127.1 5.3 %collective-permute-done.27.refs_6_ = bf16[1024,128]{1,0:T(8,128)(2,1)S(1)} collective-permute-done((bf16[1024,128]{1,0:T(8,128)(2,1)S(1)}, bf16[1024,128]{1,0:T(8,128)(2,1)S(1)}, u32[]{:S(2)}, u32[]{:S(2)}) %collective-permute-start.27) | collective-permute-done | bytes 262176 | tf_op jit(solution)/shard_map/ppermute | solution.py:302
  133.5 4.7 %collective-permute-done.25.refs_4_ = bf16[1024,128]{1,0:T(8,128)(2,1)S(1)} collective-permute-done((bf16[1024,128]{1,0:T(8,128)(2,1)S(1)}, bf16[1024,128]{1,0:T(8,128)(2,1)S(1)}, u32[]{:S(2)}, u32[]{:S(2)}) %collective-permute-start.25) | collective-permute-done | bytes 262176 | tf_op jit(solution)/shard_map/ppermute | solution.py:302
  (130 shorter events, 53.2 us)
Async XLA Ops:
  4.6 49.8 %collective-permute-start.13 = (bf16[8,256,128]{2,1,0:T(8,128)(2,1)}, bf16[8,256,128]{2,1,0:T(8,128)(2,1)}, u32[]{:S(2)}, u32[]{:S(2)}) collective-permute-start(bf16[8,256,128]{2,1,0:T(8,128)(2,1)} %get-tuple-element.47), channel_id=1, source_target_pairs={{0,8},{8,0},{16,24},{24,16},{1,9},{9,1},{17,25},{25,17},{2,10},{10... | collective-permute-start | bytes 1572872 | tf_op jit(solution)/shard_map/ppermute | solution.py:315
  4.6 51.1 %collective-permute-start.14 = (bf16[8,256,128]{2,1,0:T(8,128)(2,1)}, bf16[8,256,128]{2,1,0:T(8,128)(2,1)}, u32[]{:S(2)}, u32[]{:S(2)}) collective-permute-start(bf16[8,256,128]{2,1,0:T(8,128)(2,1)} %get-tuple-element.47), channel_id=1, source_target_pairs={{8,16},{16,8},{9,17},{17,9},{10,18},{18,10},{11,19},{19,11},{12,20... | collective-permute-start | bytes 1572872 | tf_op jit(solution)/shard_map/ppermute | solution.py:315
  9.1 19.2 %collective-permute-start.2 = (bf16[2,272,128]{2,1,0:T(8,128)(2,1)S(1)}, bf16[2,272,128]{2,1,0:T(8,128)(2,1)S(1)}, u32[]{:S(2)}, u32[]{:S(2)}) collective-permute-start(bf16[2,272,128]{2,1,0:T(8,128)(2,1)S(1)} %get-tuple-element.77), channel_id=1, source_target_pairs={{0,6},{1,7},{2,4},{3,5},{4,2},{5,3},{6,0},{7,1},{8,14},{9,15},{10,... | collective-permute-start | bytes 417800 | tf_op jit(solution)/shard_map/ppermute | solution.py:302
  11.3 20.1 %collective-permute-start.1 = (bf16[2,272,128]{2,1,0:T(8,128)(2,1)S(1)}, bf16[2,272,128]{2,1,0:T(8,128)(2,1)S(1)}, u32[]{:S(2)}, u32[]{:S(2)}) collective-permute-start(bf16[2,272,128]{2,1,0:T(8,128)(2,1)S(1)} %get-tuple-element.78), channel_id=1, source_target_pairs={{0,4},{1,5},{2,6},{3,7},{4,0},{5,1},{6,2},{7,3},{8,12},{9,13},{10,... | collective-permute-start | bytes 417800 | tf_op jit(solution)/shard_map/ppermute | solution.py:302
  37.5 14.3 %collective-permute-start.4 = (bf16[8,16,128]{2,1,0:T(8,128)(2,1)S(1)}, bf16[8,16,128]{2,1,0:T(8,128)(2,1)S(1)}, u32[]{:S(2)}, u32[]{:S(2)}) collective-permute-start(bf16[8,16,128]{2,1,0:T(8,128)(2,1)S(1)} %slice.210), channel_id=1, source_target_pairs={{0,8},{24,16},{1,9},{25,17},{2,10},{26,18},{3,11},{27,19},{4,12},{... | collective-permute-start | bytes 98312 | tf_op jit(solution)/shard_map/ppermute | solution.py:318
  38.9 35.4 %collective-permute-start.7 = (bf16[8,2,128,128]{3,2,1,0:T(8,128)(2,1)S(1)}, bf16[8,2,128,128]{3,2,1,0:T(8,128)(2,1)}, u32[]{:S(2)}, u32[]{:S(2)}) collective-permute-start(bf16[8,2,128,128]{3,2,1,0:T(8,128)(2,1)S(1)} %bitcast.51), channel_id=1, source_target_pairs={{8,16},{16,8},{9,17},{17,9},{10,18},{18,10},{11,19},{19,11},{12,20... | collective-permute-start | bytes 1572872 | tf_op jit(solution)/shard_map/ppermute | solution.py:315
  40.8 32.1 %collective-permute-start.5 = (bf16[8,2,128,128]{3,2,1,0:T(8,128)(2,1)S(1)}, bf16[8,2,128,128]{3,2,1,0:T(8,128)(2,1)}, u32[]{:S(2)}, u32[]{:S(2)}) collective-permute-start(bf16[8,2,128,128]{3,2,1,0:T(8,128)(2,1)S(1)} %bitcast.52), channel_id=1, source_target_pairs={{0,8},{8,0},{16,24},{24,16},{1,9},{9,1},{17,25},{25,17},{2,10},{10... | collective-permute-start | bytes 1572872 | tf_op jit(solution)/shard_map/ppermute | solution.py:315
  58.8 12.1 %collective-permute-start.17 = (bf16[4,256,128]{2,1,0:T(8,128)(2,1)S(1)}, bf16[4,256,128]{2,1,0:T(8,128)(2,1)S(1)}, u32[]{:S(2)}, u32[]{:S(2)}) collective-permute-start(bf16[4,256,128]{2,1,0:T(8,128)(2,1)S(1)} %pad_maximum_fusion.6), channel_id=1, source_target_pairs={{0,6},{1,7},{2,4},{3,5},{4,2},{5,3},{6,0},{7,1},{8,14},{9,15},{10,... | collective-permute-start | bytes 786440 | tf_op jit(solution)/shard_map/ppermute | solution.py:302
  70.9 17.0 %collective-permute-start.18 = (bf16[2,4,256,128]{3,2,1,0:T(8,128)(2,1)S(1)}, bf16[2,4,256,128]{3,2,1,0:T(8,128)(2,1)S(1)}, u32[]{:S(2)}, u32[]{:S(2)}) collective-permute-start(bf16[2,4,256,128]{3,2,1,0:T(8,128)(2,1)S(1)} %pad_maximum_fusion), channel_id=1, source_target_pairs={{0,1},{1,0},{2,3},{3,2},{4,5},{5,4},{6,7},{7,6},{8,9},{9,8},{10,11... | collective-permute-start | bytes 1572872 | tf_op jit(solution)/shard_map/ppermute | solution.py:302
  72.9 9.8 %collective-permute-start.6 = (bf16[1024,128]{1,0:T(8,128)(2,1)S(1)}, bf16[1024,128]{1,0:T(8,128)(2,1)S(1)}, u32[]{:S(2)}, u32[]{:S(2)}) collective-permute-start(bf16[1024,128]{1,0:T(8,128)(2,1)S(1)} %get-tuple-element.44), channel_id=1, source_target_pairs={{0,8},{24,16},{1,9},{25,17},{2,10},{26,18},{3,11},{27,19},{4,12},{... | collective-permute-start | bytes 786440 | tf_op jit(solution)/shard_map/ppermute | solution.py:318
  74.3 17.0 %collective-permute-start.29 = (bf16[8,2,128,128]{3,2,1,0:T(8,128)(2,1)}, bf16[8,2,128,128]{3,2,1,0:T(8,128)(2,1)S(1)}, u32[]{:S(2)}, u32[]{:S(2)}) collective-permute-start(bf16[8,2,128,128]{3,2,1,0:T(8,128)(2,1)} %collective-permute-done.5.refs_1_), channel_id=1, source_target_pairs={{8,16},{16,8},{9,17},{17,9},{10,18},{18,10},{11,19},{19,11},{12,20... | collective-permute-start | bytes 1572872 | tf_op jit(solution)/shard_map/ppermute | solution.py:315
  88.1 15.3 %collective-permute-start.19 = (bf16[8,2,128,128]{3,2,1,0:T(8,128)(2,1)S(1)}, bf16[8,2,128,128]{3,2,1,0:T(8,128)(2,1)S(1)}, u32[]{:S(2)}, u32[]{:S(2)}) collective-permute-start(bf16[8,2,128,128]{3,2,1,0:T(8,128)(2,1)S(1)} %get-tuple-element.56.refs_1_), channel_id=1, source_target_pairs={{8,16},{16,8},{9,17},{17,9},{10,18},{18,10},{11,19},{19,11},{12,20... | collective-permute-start | bytes 1572872 | tf_op jit(solution)/shard_map/ppermute | solution.py:315
  90.0 9.1 %collective-permute-start.12 = (bf16[1024,128]{1,0:T(8,128)(2,1)}, bf16[1024,128]{1,0:T(8,128)(2,1)S(1)}, u32[]{:S(2)}, u32[]{:S(2)}) collective-permute-start(bf16[1024,128]{1,0:T(8,128)(2,1)} %get-tuple-element.55), channel_id=1, source_target_pairs={{0,8},{24,16},{1,9},{25,17},{2,10},{26,18},{3,11},{27,19},{4,12},{... | collective-permute-start | bytes 786440 | tf_op jit(solution)/shard_map/ppermute | solution.py:318
  94.3 13.4 %collective-permute-start.30 = (bf16[8,128,128]{2,1,0:T(8,128)(2,1)S(1)}, bf16[8,128,128]{2,1,0:T(8,128)(2,1)S(1)}, u32[]{:S(2)}, u32[]{:S(2)}) collective-permute-start(bf16[8,128,128]{2,1,0:T(8,128)(2,1)S(1)} %get-tuple-element.73), channel_id=1, source_target_pairs={{8,0},{16,24},{9,1},{17,25},{10,2},{18,26},{11,3},{19,27},{12,4},{... | collective-permute-start | bytes 786440 | tf_op jit(solution)/shard_map/ppermute | solution.py:321
  96.4 11.3 %collective-permute-start.31 = (f32[2,8,1,128]{3,2,1,0:T(1,128)S(1)}, f32[2,8,1,128]{3,2,1,0:T(1,128)S(1)}, u32[]{:S(2)}, u32[]{:S(2)}) collective-permute-start(f32[2,8,1,128]{3,2,1,0:T(1,128)S(1)} %get-tuple-element.74), channel_id=1, source_target_pairs={{8,0},{16,24},{9,1},{17,25},{10,2},{18,26},{11,3},{19,27},{12,4},{... | collective-permute-start | bytes 24584 | tf_op jit(solution)/shard_map/ppermute | solution.py:321
  109.6 13.1 %collective-permute-start.35 = (bf16[1024,128]{1,0:T(8,128)(2,1)S(1)}, bf16[1024,128]{1,0:T(8,128)(2,1)S(1)}, u32[]{:S(2)}, u32[]{:S(2)}) collective-permute-start(bf16[1024,128]{1,0:T(8,128)(2,1)S(1)} %merge_0.1.refs_0_), channel_id=1, source_target_pairs={{0,4},{1,5},{2,6},{3,7},{4,0},{5,1},{6,2},{7,3},{8,12},{9,13},{10,... | collective-permute-start | bytes 786440 | tf_op jit(solution)/shard_map/ppermute | solution.py:302
  109.6 13.6 %collective-permute-start.20 = (bf16[8,128,128]{2,1,0:T(8,128)(2,1)S(1)}, bf16[8,128,128]{2,1,0:T(8,128)(2,1)S(1)}, u32[]{:S(2)}, u32[]{:S(2)}) collective-permute-start(bf16[8,128,128]{2,1,0:T(8,128)(2,1)S(1)} %get-tuple-element.66), channel_id=1, source_target_pairs={{8,0},{16,24},{9,1},{17,25},{10,2},{18,26},{11,3},{19,27},{12,4},{... | collective-permute-start | bytes 786440 | tf_op jit(solution)/shard_map/ppermute | solution.py:321
  110.9 14.1 %collective-permute-start.33 = (bf16[1024,128]{1,0:T(8,128)(2,1)S(1)}, bf16[1024,128]{1,0:T(8,128)(2,1)S(1)}, u32[]{:S(2)}, u32[]{:S(2)}) collective-permute-start(bf16[1024,128]{1,0:T(8,128)(2,1)S(1)} %merge_0.1.refs_0_), channel_id=1, source_target_pairs={{0,2},{1,3},{2,0},{3,1},{4,6},{5,7},{6,4},{7,5},{8,10},{9,11},{10,... | collective-permute-start | bytes 786440 | tf_op jit(solution)/shard_map/ppermute | solution.py:302
  112.0 13.1 %collective-permute-start.32 = (bf16[1024,128]{1,0:T(8,128)(2,1)S(1)}, bf16[1024,128]{1,0:T(8,128)(2,1)S(1)}, u32[]{:S(2)}, u32[]{:S(2)}) collective-permute-start(bf16[1024,128]{1,0:T(8,128)(2,1)S(1)} %merge_0.1.refs_0_), channel_id=1, source_target_pairs={{0,1},{1,0},{2,3},{3,2},{4,5},{5,4},{6,7},{7,6},{8,9},{9,8},{10,11... | collective-permute-start | bytes 786440 | tf_op jit(solution)/shard_map/ppermute | solution.py:302
  115.0 11.1 %collective-permute-start.38 = (bf16[1024,128]{1,0:T(8,128)(2,1)S(1)}, bf16[1024,128]{1,0:T(8,128)(2,1)S(1)}, u32[]{:S(2)}, u32[]{:S(2)}) collective-permute-start(bf16[1024,128]{1,0:T(8,128)(2,1)S(1)} %collective-permute-done.37.refs_6_), channel_id=1, source_target_pairs={{0,1},{1,0},{2,3},{3,2},{4,5},{5,4},{6,7},{7,6},{8,9},{9,8},{10,11... | collective-permute-start | bytes 786440 | tf_op jit(solution)/shard_map/ppermute | solution.py:302
  124.9 13.3 %collective-permute-start.25 = (bf16[1024,128]{1,0:T(8,128)(2,1)S(1)}, bf16[1024,128]{1,0:T(8,128)(2,1)S(1)}, u32[]{:S(2)}, u32[]{:S(2)}) collective-permute-start(bf16[1024,128]{1,0:T(8,128)(2,1)S(1)} %merge_1.1.refs_0_), channel_id=1, source_target_pairs={{0,4},{1,5},{2,6},{3,7},{4,0},{5,1},{6,2},{7,3},{8,12},{9,13},{10,... | collective-permute-start | bytes 786440 | tf_op jit(solution)/shard_map/ppermute | solution.py:302
  125.1 13.6 %collective-permute-start.23 = (bf16[1024,128]{1,0:T(8,128)(2,1)S(1)}, bf16[1024,128]{1,0:T(8,128)(2,1)S(1)}, u32[]{:S(2)}, u32[]{:S(2)}) collective-permute-start(bf16[1024,128]{1,0:T(8,128)(2,1)S(1)} %merge_1.1.refs_0_), channel_id=1, source_target_pairs={{0,2},{1,3},{2,0},{3,1},{4,6},{5,7},{6,4},{7,5},{8,10},{9,11},{10,... | collective-permute-start | bytes 786440 | tf_op jit(solution)/shard_map/ppermute | solution.py:302
  126.1 12.6 %collective-permute-start.34 = (bf16[1024,128]{1,0:T(8,128)(2,1)S(1)}, bf16[1024,128]{1,0:T(8,128)(2,1)S(1)}, u32[]{:S(2)}, u32[]{:S(2)}) collective-permute-start(bf16[1024,128]{1,0:T(8,128)(2,1)S(1)} %collective-permute-done.33.refs_2_), channel_id=1, source_target_pairs={{0,1},{1,0},{2,3},{3,2},{4,5},{5,4},{6,7},{7,6},{8,9},{9,8},{10,11... | collective-permute-start | bytes 786440 | tf_op jit(solution)/shard_map/ppermute | solution.py:302
  127.0 13.2 %collective-permute-start.22 = (bf16[1024,128]{1,0:T(8,128)(2,1)S(1)}, bf16[1024,128]{1,0:T(8,128)(2,1)S(1)}, u32[]{:S(2)}, u32[]{:S(2)}) collective-permute-start(bf16[1024,128]{1,0:T(8,128)(2,1)S(1)} %merge_1.1.refs_0_), channel_id=1, source_target_pairs={{0,1},{1,0},{2,3},{3,2},{4,5},{5,4},{6,7},{7,6},{8,9},{9,8},{10,11... | collective-permute-start | bytes 786440 | tf_op jit(solution)/shard_map/ppermute | solution.py:302
  (19 other events, 116.6 us)

commit v6 on v5

--- a/solution.py
+++ b/solution.py
@@ -14,6 +14,7 @@
 NEG = -1e30
 EXP2_SCALE = math.log2(math.e) / math.sqrt(HEAD_DIM)
 GROUP = 8
+STAT_ROWS = 16
 ROW_SHIFT = 16
 VMEM_BYTES = 40 * 1024 * 1024
 
@@ -30,7 +31,7 @@
     return -(-rows // 16) * 16
 
 
-def pack_kernel(n_ka, heads, me_ref, k_ref, v_ref, mask_ref, *out_refs):
+def pack_kernel(n_ka, heads, marked, me_ref, k_ref, v_ref, mask_ref, *out_refs):
     key_blocks = k_ref.shape[0] // BLOCK
     for c in range(heads):
         for k in range(n_ka):
@@ -47,14 +48,15 @@
         for j in range(mask_ref.shape[1]):
             mask = jnp.where((row == i) & (column == j), mask_ref[i, j], mask)
     mask = mask.astype(jnp.float32).astype(k_ref.dtype)
-    for k in range(n_ka):
-        out_refs[0][k, 2 * key_blocks * BLOCK :] = mask
-
-
-def pack(me, keys, values, mask, n_ka, heads):
-    sizes = [2 * keys.shape[0] + (mask_rows(mask.shape[0]) if c == 0 else 0) for c in range(heads)]
+    for c in marked:
+        for k in range(n_ka):
+            out_refs[c][k, 2 * key_blocks * BLOCK :] = mask
+
+
+def pack(me, keys, values, mask, n_ka, heads, marked):
+    sizes = [2 * keys.shape[0] + (mask_rows(mask.shape[0]) if c in marked else 0) for c in range(heads)]
     return pl.pallas_call(
-        functools.partial(pack_kernel, n_ka, heads),
+        functools.partial(pack_kernel, n_ka, heads, marked),
         out_shape=[jax.ShapeDtypeStruct((n_ka, size, HEAD_DIM), keys.dtype) for size in sizes],
         in_specs=[SMEM, VMEM, VMEM, SMEM],
         out_specs=[VMEM] * heads,
@@ -68,6 +70,7 @@
     pb = pb_ref[0]
     sign = 1 - 2 * (pb & 1)
     inner = ((pb > 0) & (pb < n_pb - 1)).astype(jnp.int32)
+    helper = ((pb == 1) | (pb == n_pb - 2)).astype(jnp.int32)
     for step, (sources, live) in enumerate(zip(steps, live_refs)):
         total = jnp.int32(0)
         for guest, mask_ref in enumerate(mask_refs):
@@ -81,6 +84,8 @@
                     inside = ((j >= 0) & (j < n_pb)).astype(jnp.int32)
                     if relay and abs(delta) > 1:
                         inside = inside * inner
+                    if guest:
+                        inside = inside * helper
                     j = jnp.clip(j, 0, n_pb - 1)
                     for slot in range(n_slots):
                         for t in range(key_blocks):
@@ -113,6 +118,14 @@
     return [(counts, i, live) for i, live in enumerate(lives)]
 
 
+def in_parts(x):
+    found = []
+    for _ in range(3):
+        found.append(x.astype(jnp.bfloat16).astype(jnp.float32))
+        x = x - found[-1]
+    return found
+
+
 def attend_kernel(n_src, entry, first, mode, guests, count_ref, live_ref, head_ref, q_all, *refs):
     n_kv = n_src
     guest_ref, refs = (refs[0], refs[1:]) if guests else (None, refs)
@@ -121,7 +134,7 @@
     if mode == "last":
         (out_ref, kv, q_ref, qt_ref, *state, sems) = refs
     elif mode == "send":
-        (*state, part_ref, stat_ref, kv, q_ref, qt_ref, sems) = refs
+        (*state, part_ref, kv, q_ref, qt_ref, sems) = refs
     else:
         (*state, kv, q_ref, qt_ref, sems) = refs
     m_ref, l_ref, acc_ref = state
@@ -187,8 +200,10 @@
     if mode == "send":
         for r in range(rows):
             l = l_ref[rows + r]
-            part_ref[r] = (acc_ref[rows + r] / jnp.where(l > 0, l, 1.0)).astype(part_ref.dtype)
-            stat_ref[0, r], stat_ref[1, r] = m_ref[rows + r], l
+            part_ref[r, :HEAD_DIM] = (acc_ref[rows + r] / jnp.where(l > 0, l, 1.0)).astype(part_ref.dtype)
+            words = in_parts(m_ref[rows + r]) + in_parts(l)
+            words.append(jnp.zeros((STAT_ROWS - len(words), BLOCK), f32))
+            part_ref[r, HEAD_DIM:] = jnp.concatenate(words).astype(part_ref.dtype)
 
 
 def attend(listed, head, queries, guest, sources, state, mode, sets, name):
@@ -204,8 +219,7 @@
     else:
         out_shape = [jax.ShapeDtypeStruct(shape, jnp.float32) for shape in shapes]
     if mode == "send":
-        out_shape.append(jax.ShapeDtypeStruct((rows, HEAD_DIM, BLOCK), dtype))
-        out_shape.append(jax.ShapeDtypeStruct((2, rows, 1, BLOCK), jnp.float32))
+        out_shape.append(jax.ShapeDtypeStruct((rows, HEAD_DIM + STAT_ROWS, BLOCK), dtype))
     n_src = len(sources)
     blocks = sources[0].shape[0]
     guests = () if guest is None else (guest,)
@@ -215,7 +229,6 @@
     if mode == "last":
         scratch += [pltpu.VMEM(shape, jnp.float32) for shape in shapes]
     scratch.append(pltpu.SemaphoreType.DMA((n_src + 5,)))
-    live_blocks = rows * n_src * blocks // 4
     return pl.pallas_call(
         functools.partial(attend_kernel, n_src, entry, first, mode, bool(guests)),
         out_shape=out_shape,
@@ -223,40 +236,37 @@
         out_specs=[VMEM] * len(out_shape),
         scratch_shapes=scratch,
         compiler_params=params(),
-        cost_estimate=pl.CostEstimate(
-            flops=live_blocks * 4 * BLOCK * BLOCK * HEAD_DIM,
-            bytes_accessed=8 * tokens * HEAD_DIM + 2 * n_src * sources[0].size,
-            transcendentals=live_blocks * BLOCK * BLOCK,
-        ),
+        cost_estimate=pl.CostEstimate(flops=0, bytes_accessed=tokens * HEAD_DIM, transcendentals=0),
         name=name,
     )(counts, live, head, queries, *guests, *sources, *state)
 
 
-def merge_kernel(outer_ref, m_ref, l_ref, acc_ref, part_ref, stat_ref, out_ref):
+def merge_kernel(outer_ref, m_ref, l_ref, acc_ref, part_ref, out_ref):
     outer = outer_ref[0] > 0
     for r in range(part_ref.shape[0]):
         m, l = m_ref[r], l_ref[r]
-        extra = jnp.where(outer, stat_ref[1, r], 0.0)
-        top = jnp.where(outer, stat_ref[0, r], NEG)
+        words = part_ref[r, HEAD_DIM:].astype(jnp.float32)
+        top = jnp.where(outer, words[0:1] + words[1:2] + words[2:3], NEG)
+        extra = jnp.where(outer, words[3:4] + words[4:5] + words[5:6], 0.0)
         m_new = jnp.maximum(m, top)
         alpha = jnp.exp2((m - m_new) * EXP2_SCALE)
         beta = jnp.exp2((top - m_new) * EXP2_SCALE) * extra
-        done = (acc_ref[r] * alpha + part_ref[r].astype(jnp.float32) * beta) / (l * alpha + beta)
+        done = (acc_ref[r] * alpha + part_ref[r, :HEAD_DIM].astype(jnp.float32) * beta) / (l * alpha + beta)
         out_ref[r * BLOCK : (r + 1) * BLOCK, :] = done.T.astype(out_ref.dtype)
 
 
-def merge(outer, state, part, stat, name):
+def merge(outer, state, part, name):
     rows = part.shape[0]
     half = lambda x: pl.BlockSpec((rows,) + x.shape[1:], lambda i: (0, 0, 0))
     return pl.pallas_call(
         merge_kernel,
         out_shape=jax.ShapeDtypeStruct((rows * BLOCK, HEAD_DIM), part.dtype),
         grid=(1,),
-        in_specs=[SMEM] + [half(x) for x in state] + [VMEM, VMEM],
+        in_specs=[SMEM] + [half(x) for x in state] + [VMEM],
         out_specs=VMEM,
         compiler_params=params(),
         name=name,
-    )(outer, *state, part, stat)
+    )(outer, *state, part)
 
 
 def place_kernel(n_ka, heads, c, me_ref, *refs):
@@ -339,16 +349,13 @@
     def flags(x):
         return x[:, :rows, : block_mask.shape[1]].astype(jnp.int32).reshape(-1)
 
-    packed = pack(me1, keys, values, block_mask, n_ka, heads)
+    packed = pack(me1, keys, values, block_mask, n_ka, heads, (0,) if early is None else (0, early))
     ahead = [exchange(packed[early], odd, 1) for odd in (0, 1)] if early is not None else []
     ahead_from = [i for i, x in enumerate(ahead) if x is not None]
 
-    owns = []
-    for c in range(heads):
-        (own,) = sort([packed[c]])
-        owns.append(blocks(own))
-        if c == 0:
-            marks = own[:, 2 * shard :]
+    owns = [None if c == early else sort([packed[c]])[0] for c in range(heads)]
+    marks = owns[0][:, 2 * shard :]
+    owns = [own if own is None else blocks(own) for own in owns]
     masks = [flags(marks)]
 
     steps = [((0, False),)]
@@ -359,8 +366,15 @@
     last = len(steps) - 1
     sets = 2 if relay else 1
     lists = plan(pb1, masks, steps[:1], n_pb, n_ka, key_blocks, rows, relay)
+    arrived_early = [None, None]
+    if early is not None:
+        first_over = exchange(owns[0], 0, 1), exchange(owns[0], 1, 1)
+        own_early, *sorted_ahead = sort([packed[early]] + [ahead[i] for i in ahead_from])
+        owns[early] = blocks(own_early)
+        for i, x in zip(ahead_from, sorted_ahead):
+            arrived_early[i] = blocks(x)
     if relay:
-        masks.append(flags(inward(marks)))
+        masks.append(flags(sorted_ahead[0][:, 2 * shard :] if early is not None else inward(marks)))
     lists += plan(pb1, masks, steps[1:], n_pb, n_ka, key_blocks, rows, relay) if last else []
     guest = [None] * heads
     state = [None] * heads
@@ -378,12 +392,9 @@
     for step in range(1, last + 1):
         for c in range(heads):
             if step == 1 and c == early:
-                sorted_ahead = sort([ahead[i] for i in ahead_from])
-                arrived = [None, None]
-                for i, x in zip(ahead_from, sorted_ahead):
-                    arrived[i] = blocks(x)
+                arrived = arrived_early
             elif step == 1:
-                arrived = [exchange(owns[c], odd, 1) for odd in (0, 1)]
+                arrived = [exchange(owns[c], odd, 1) for odd in (0, 1)] if c or early is None else list(first_over)
             else:
                 over[c] = after(over[c], done)
                 arrived = [exchange(over[c][1], 0, step), exchange(over[c][0], 1, step)]
@@ -398,10 +409,10 @@
     whole = None
     for c in range(heads):
         sources = [x for x in over[c] if x is not None] if last else [owns[c]]
-        found = run(c, last, sources)
+        found = run(c, last, sources if whole is None else after(sources, out))
         if relay:
             outer = ((pb == 0) | (pb == n_pb - 1)).astype(jnp.int32)[None]
-            out = merge(outer, found[:3], outward(found[3]), outward(found[4]), f"merge_{c}")
+            out = merge(outer, found[:3], outward(found[3]), f"merge_{c}")
         else:
             out = found[0]
         pieces = [out] + [swap(out, k) for k in range(2, n_ka, 2)]

time: 142 us -> 136 us (0.958)
  starting transfers between devices: 58.5 us -> 43.4 us
  local copies, waits for them, and re-layouts: 11.4 us -> 14.9 us
  waiting for transfers between devices: 41.2 us -> 44.5 us
  Pallas kernels: 29.6 us -> 31.4 us
  other arithmetic: 0.26 us -> 1.89 us
    ppermute x26 -> x22, starting transfers between devices: 36.8 us -> 28.3 us  [swap(): return lax.ppermute(x, 'ka', [(i, i ^ k) for i in range(n_ka)])]
    unnamed x25 -> x33, local copies, waits for them, and re-layouts: 5.22 us -> 12.3 us
    slice x4, local copies, waits for them, and re-layouts: 3.77 us -> 0.15 us  [sort(): two = [x[k:k + 2] for x in parts]]
    ppermute x4 -> x2, starting transfers between devices: 5.99 us -> 2.6 us  [outward(): return lax.ppermute(x, 'pb', [(1, 0), (n_pb - 2, n_pb - 1)])]
    ppermute x3 -> x2, waiting for transfers between devices: 7.95 us -> 10.8 us  [inward(): return lax.ppermute(x, 'pb', [(0, 1), (n_pb - 1, n_pb - 2)])]
    ppermute x6, waiting for transfers between devices: 0.02 us -> 2.83 us  [exchange(): return lax.ppermute(x, 'pb', found) if found else None]
    pallas_call x6, Pallas kernels: 21.1 us -> 23.6 us  [attend(): pl.pallas_call(functools.partial(attend_kernel, n_src, entry, first, mode...]
    ppermute x26 -> x22, waiting for transfers between devices: 33.2 us -> 30.9 us  [swap(): return lax.ppermute(x, 'ka', [(i, i ^ k) for i in range(n_ka)])]
  transfers between devices with their start and end apart: 39 -> 32, of which waited for: 14 -> 14; matrix products, arithmetic and copies ran while one was open for 5% -> 5% of each run, Pallas kernels for 19% -> 19%
where the time goes in v6:
time: 136 us; the launch traced here: 137 us
  waiting for transfers between devices  44.5 us (33%)
  starting transfers between devices  43.4 us (32%)
  Pallas kernels  31.4 us (23%)
  local copies, waits for them, and re-layouts  14.9 us (11%)
  other arithmetic  1.89 us (1%)
    ppermute x22, waiting for transfers between devices, swap(): return lax.ppermute(x, 'ka', [(i, i ^ k) for i in range(n_ka)])  30.9 us
    ppermute x22, starting transfers between devices, swap(): return lax.ppermute(x, 'ka', [(i, i ^ k) for i in range(n_ka)])  28.3 us
    pallas_call x6, Pallas kernels, attend(): pl.pallas_call(functools.partial(attend_kernel, n_src, entry, first, mode...  23.6 us
    unnamed x33, local copies, waits for them, and re-layouts  12.3 us
    ppermute x2, waiting for transfers between devices, inward(): return lax.ppermute(x, 'pb', [(0, 1), (n_pb - 1, n_pb - 2)])  10.8 us
    ppermute x6, starting transfers between devices, exchange(): return lax.ppermute(x, 'pb', found) if found else None  9.88 us
    pallas_call x2, Pallas kernels, plan(): pl.pallas_call(functools.partial(plan_kernel, steps, n_pb, n_slots, key_b...  3.69 us
    ppermute x6, waiting for transfers between devices, exchange(): return lax.ppermute(x, 'pb', found) if found else None  2.83 us
  transfers between devices with their start and end apart: 32, of which 14 were waited for; matrix products, arithmetic and copies ran while one was open for 5% of the time, Pallas kernels for 19%

profile of v6, /device:TPU:9, one launch (start us, length us, event | category | flops | bytes accessed | tf_op | source)
XLA Modules:
  0.0 136.6 jit_solution(384982696562259585)
XLA Ops:
  3.8 3.2 %collective-permute-start.5 = (bf16[8,272,128]{2,1,0:T(8,128)(2,1)S(1)}, bf16[8,272,128]{2,1,0:T(8,128)(2,1)S(1)}, u32[]{:S(2)}, u32[]{:S(2)}) collective-permute-start(bf16[8,272,128]{2,1,0:T(8,128)(2,1)S(1)} %get-tuple-element.40), channel_id=1, source_target_pairs={{8,16},{16,8},{9,17},{17,9},{10,18},{18,10},{11,19},{19,11},{12,20... | collective-permute-start | bytes 1671176 | tf_op jit(solution)/shard_map/ppermute | solution.py:325
  7.1 2.2 %collective-permute-start.2 = (bf16[2,272,128]{2,1,0:T(8,128)(2,1)S(1)}, bf16[2,272,128]{2,1,0:T(8,128)(2,1)S(1)}, u32[]{:S(2)}, u32[]{:S(2)}) collective-permute-start(bf16[2,272,128]{2,1,0:T(8,128)(2,1)S(1)} %get-tuple-element.90), channel_id=1, source_target_pairs={{0,6},{1,7},{2,4},{3,5},{4,2},{5,3},{6,0},{7,1},{8,14},{9,15},{10,... | collective-permute-start | bytes 417800 | tf_op jit(solution)/shard_map/ppermute | solution.py:312
  9.9 2.4 %collective-permute-done.2 = bf16[2,272,128]{2,1,0:T(8,128)(2,1)S(1)} collective-permute-done((bf16[2,272,128]{2,1,0:T(8,128)(2,1)S(1)}, bf16[2,272,128]{2,1,0:T(8,128)(2,1)S(1)}, u32[]{:S(2)}, u32[]{:S(2)}) %collective-permute-start.2) | collective-permute-done | bytes 139296 | tf_op jit(solution)/shard_map/ppermute | solution.py:312
  12.3 4.2 %collective-permute-done.1 = bf16[2,272,128]{2,1,0:T(8,128)(2,1)S(1)} collective-permute-done((bf16[2,272,128]{2,1,0:T(8,128)(2,1)S(1)}, bf16[2,272,128]{2,1,0:T(8,128)(2,1)S(1)}, u32[]{:S(2)}, u32[]{:S(2)}) %collective-permute-start.1) | collective-permute-done | bytes 139296 | tf_op jit(solution)/shard_map/ppermute | solution.py:312
  24.8 2.2 %collective-permute-start.12 = (bf16[8,2,128,128]{3,2,1,0:T(8,128)(2,1)S(1)}, bf16[8,2,128,128]{3,2,1,0:T(8,128)(2,1)S(1)}, u32[]{:S(2)}, u32[]{:S(2)}) collective-permute-start(bf16[8,2,128,128]{3,2,1,0:T(8,128)(2,1)S(1)} %bitcast.97), channel_id=1, source_target_pairs={{8,16},{16,8},{9,17},{17,9},{10,18},{18,10},{11,19},{19,11},{12,20... | collective-permute-start | bytes 1572872 | tf_op jit(solution)/shard_map/ppermute | solution.py:325
  29.7 2.9 %collective-permute-done.7 = bf16[6,272,128]{2,1,0:T(8,128)(2,1)S(1)} collective-permute-done((bf16[6,272,128]{2,1,0:T(8,128)(2,1)}, bf16[6,272,128]{2,1,0:T(8,128)(2,1)S(1)}, u32[]{:S(2)}, u32[]{:S(2)}) %collective-permute-start.7) | collective-permute-done | bytes 417824 | tf_op jit(solution)/shard_map/ppermute | solution.py:312
  32.6 7.1 %collective-permute-done.8 = bf16[6,272,128]{2,1,0:T(8,128)(2,1)} collective-permute-done((bf16[6,272,128]{2,1,0:T(8,128)(2,1)}, bf16[6,272,128]{2,1,0:T(8,128)(2,1)}, u32[]{:S(2)}, u32[]{:S(2)}) %collective-permute-start.8) | collective-permute-done | bytes 417824 | tf_op jit(solution)/shard_map/ppermute | solution.py:312
  40.8 4.7 %collective-permute-start.9 = (bf16[3,4,272,128]{3,2,1,0:T(8,128)(2,1)S(1)}, bf16[3,4,272,128]{3,2,1,0:T(8,128)(2,1)S(1)}, u32[]{:S(2)}, u32[]{:S(2)}) collective-permute-start(bf16[3,4,272,128]{3,2,1,0:T(8,128)(2,1)S(1)} %pad_maximum_fusion), channel_id=1, source_target_pairs={{0,1},{1,0},{2,3},{3,2},{4,5},{5,4},{6,7},{7,6},{8,9},{9,8},{10,11... | collective-permute-start | bytes 2506760 | tf_op jit(solution)/shard_map/ppermute | solution.py:312
  48.7 2.8 %attend_1_0.1 = (f32[16,1,128]{2,1,0:T(1,128)S(1)}, f32[16,1,128]{2,1,0:T(1,128)S(1)}, f32[16,128,128]{2,1,0:T(8,128)S(1)}) custom-call(s32[1]{0:T(128)} %get-tuple-element.45.count_ref, s32[96]{0:T(128)S(1)} %get-tuple-element.46.live_ref, s32[1]{0:T(128)S(6)} %add.14.head_ref, bf16[1024,2048]{1,0:T(8,128)(2,1)S(1)} %copy-done, ...), custom_call_target="tpu_custom_call" | custom-call | bytes 131072 | tf_op jit(solution)/shard_map/attend_1_0/pallas_call | solution.py:232
  55.7 2.8 %attend_0_0.1 = (f32[16,1,128]{2,1,0:T(1,128)S(1)}, f32[16,1,128]{2,1,0:T(1,128)S(1)}, f32[16,128,128]{2,1,0:T(8,128)S(1)}) custom-call(s32[1]{0:T(128)} %get-tuple-element.45.count_ref, s32[96]{0:T(128)S(1)} %get-tuple-element.46.live_ref, s32[1]{0:T(128)S(6)} %mul.8.head_ref, bf16[1024,2048]{1,0:T(8,128)(2,1)S(1)} %copy-done, ...), custom_call_target="tpu_custom_call" | custom-call | bytes 131072 | tf_op jit(solution)/shard_map/attend_0_0/pallas_call | solution.py:232
  58.7 2.3 %plan.2 = (s32[2]{0:T(128)S(1)}, s32[304]{0:T(512)S(1)}, s32[176]{0:T(256)S(1)}) custom-call(s32[1]{0:T(128)} %bitcast.2.pb_ref, s32[256]{0:T(256)S(1)} %reshape.64.refs_0_, s32[256]{0:T(256)S(1)} %reshape.66.refs_1_), custom_call_target="tpu_custom_call" | custom-call | tf_op jit(solution)/shard_map/plan/pallas_call | solution.py:110
  61.0 3.5 %collective-permute-done.11.refs_0_ = bf16[1024,128]{1,0:T(8,128)(2,1)S(1)} collective-permute-done((bf16[1024,128]{1,0:T(8,128)(2,1)}, bf16[1024,128]{1,0:T(8,128)(2,1)S(1)}, u32[]{:S(2)}, u32[]{:S(2)}) %collective-permute-start.11) | collective-permute-done | bytes 262176 | tf_op jit(solution)/shard_map/ppermute | solution.py:328
  67.7 5.0 %attend_0_1.1 = (f32[16,1,128]{2,1,0:T(1,128)S(1)}, f32[16,1,128]{2,1,0:T(1,128)S(1)}, f32[16,128,128]{2,1,0:T(8,128)S(1)}) custom-call(s32[2]{0:T(128)S(1)} %get-tuple-element.41.count_ref, s32[304]{0:T(512)S(1)} %get-tuple-element.43.live_ref, s32[1]{0:T(128)S(6)} %mul.8.head_ref, bf16[1024,2048]{1,0:T(8,128)(2,1)S(1)} %copy-done.1, ...), custom_call_target="tpu_custom_call" | custom-call | bytes 131072 | tf_op jit(solution)/shard_map/attend_0_1/pallas_call | solution.py:232
  72.7 2.4 %collective-permute-start.14 = (bf16[8,2,128,128]{3,2,1,0:T(8,128)(2,1)S(1)}, bf16[8,2,128,128]{3,2,1,0:T(8,128)(2,1)S(1)}, u32[]{:S(2)}, u32[]{:S(2)}) collective-permute-start(bf16[8,2,128,128]{3,2,1,0:T(8,128)(2,1)S(1)} %bitcast.94), channel_id=1, source_target_pairs={{8,16},{16,8},{9,17},{17,9},{10,18},{18,10},{11,19},{19,11},{12,20... | collective-permute-start | bytes 1572872 | tf_op jit(solution)/shard_map/ppermute | solution.py:325
  75.2 5.2 %attend_0_2.1 = (f32[16,1,128]{2,1,0:T(1,128)S(1)}, f32[16,1,128]{2,1,0:T(1,128)S(1)}, f32[16,128,128]{2,1,0:T(8,128)S(1)}, bf16[8,144,128]{2,1,0:T(8,128)(2,1)}) custom-call(s32[2]{0:T(128)S(1)} %get-tuple-element.41.count_ref, s32[176]{0:T(256)S(1)} %get-tuple-element.42.live_ref, s32[1]{0:T(128)S(6)} %mul.8.head_ref, bf16[1024,2048]{1,0:T(8,128)(2,1)S(1)} %copy-done.1, ...), custom_call_target="tpu_custom_call" | custom-call | bytes 131072 | tf_op jit(solution)/shard_map/attend_0_2/pallas_call | solution.py:232
  83.9 7.3 %collective-permute-done.13.refs_0_ = bf16[1024,128]{1,0:T(8,128)(2,1)S(1)} collective-permute-done((bf16[1024,128]{1,0:T(8,128)(2,1)}, bf16[1024,128]{1,0:T(8,128)(2,1)S(1)}, u32[]{:S(2)}, u32[]{:S(2)}) %collective-permute-start.13) | collective-permute-done | bytes 262176 | tf_op jit(solution)/shard_map/ppermute | solution.py:328
  91.2 2.2 %copy-done.2 = bf16[1024,2048]{1,0:T(8,128)(2,1)S(1)} copy-done((bf16[1024,2048]{1,0:T(8,128)(2,1)S(1)}, bf16[1024,2048]{1,0:T(8,128)(2,1)}, u32[]{:S(2)}) %copy-start.2) | copy-done | bytes 4194328
  93.4 4.2 %attend_1_1.1 = (f32[16,1,128]{2,1,0:T(1,128)S(1)}, f32[16,1,128]{2,1,0:T(1,128)S(1)}, f32[16,128,128]{2,1,0:T(8,128)S(1)}) custom-call(s32[2]{0:T(128)S(1)} %get-tuple-element.41.count_ref, s32[304]{0:T(512)S(1)} %get-tuple-element.43.live_ref, s32[1]{0:T(128)S(6)} %add.14.head_ref, bf16[1024,2048]{1,0:T(8,128)(2,1)S(1)} %copy-done.2, ...), custom_call_target="tpu_custom_call" | custom-call | bytes 131072 | tf_op jit(solution)/shard_map/attend_1_1/pallas_call | solution.py:232
  97.9 3.6 %attend_1_2.1 = (f32[16,1,128]{2,1,0:T(1,128)S(1)}, f32[16,1,128]{2,1,0:T(1,128)S(1)}, f32[16,128,128]{2,1,0:T(8,128)S(1)}, bf16[8,144,128]{2,1,0:T(8,128)(2,1)S(1)}) custom-call(s32[2]{0:T(128)S(1)} %get-tuple-element.41.count_ref, s32[176]{0:T(256)S(1)} %get-tuple-element.42.live_ref, s32[1]{0:T(128)S(6)} %add.14.head_ref, ...), custom_call_target="tpu_custom_call" | custom-call | bytes 131072 | tf_op jit(solution)/shard_map/attend_1_2/pallas_call | solution.py:232
  105.6 3.1 %collective-permute-start.25 = (bf16[1024,128]{1,0:T(8,128)(2,1)S(1)}, bf16[1024,128]{1,0:T(8,128)(2,1)S(1)}, u32[]{:S(2)}, u32[]{:S(2)}) collective-permute-start(bf16[1024,128]{1,0:T(8,128)(2,1)S(1)} %merge_0.1.refs_0_), channel_id=1, source_target_pairs={{0,1},{1,0},{2,3},{3,2},{4,5},{5,4},{6,7},{7,6},{8,9},{9,8},{10,11... | collective-permute-start | bytes 786440 | tf_op jit(solution)/shard_map/ppermute | solution.py:312
  109.5 5.8 %collective-permute-start.31 = (bf16[1024,128]{1,0:T(8,128)(2,1)S(1)}, bf16[1024,128]{1,0:T(8,128)(2,1)S(1)}, u32[]{:S(2)}, u32[]{:S(2)}) collective-permute-start(bf16[1024,128]{1,0:T(8,128)(2,1)S(1)} %collective-permute-done.30.refs_6_), channel_id=1, source_target_pairs={{0,1},{1,0},{2,3},{3,2},{4,5},{5,4},{6,7},{7,6},{8,9},{9,8},{10,11... | collective-permute-start | bytes 786440 | tf_op jit(solution)/shard_map/ppermute | solution.py:312
  115.3 2.3 %collective-permute-done.28.refs_4_ = bf16[1024,128]{1,0:T(8,128)(2,1)S(1)} collective-permute-done((bf16[1024,128]{1,0:T(8,128)(2,1)S(1)}, bf16[1024,128]{1,0:T(8,128)(2,1)S(1)}, u32[]{:S(2)}, u32[]{:S(2)}) %collective-permute-start.28) | collective-permute-done | bytes 262176 | tf_op jit(solution)/shard_map/ppermute | solution.py:312
  122.0 5.3 %collective-permute-done.23.refs_6_ = bf16[1024,128]{1,0:T(8,128)(2,1)S(1)} collective-permute-done((bf16[1024,128]{1,0:T(8,128)(2,1)S(1)}, bf16[1024,128]{1,0:T(8,128)(2,1)S(1)}, u32[]{:S(2)}, u32[]{:S(2)}) %collective-permute-start.23) | collective-permute-done | bytes 262176 | tf_op jit(solution)/shard_map/ppermute | solution.py:312
  128.5 4.7 %collective-permute-done.21.refs_4_ = bf16[1024,128]{1,0:T(8,128)(2,1)S(1)} collective-permute-done((bf16[1024,128]{1,0:T(8,128)(2,1)S(1)}, bf16[1024,128]{1,0:T(8,128)(2,1)S(1)}, u32[]{:S(2)}, u32[]{:S(2)}) %collective-permute-start.21) | collective-permute-done | bytes 262176 | tf_op jit(solution)/shard_map/ppermute | solution.py:312
  (115 shorter events, 44.6 us)
Async XLA Ops:
  3.8 15.4 %collective-permute-start.5 = (bf16[8,272,128]{2,1,0:T(8,128)(2,1)S(1)}, bf16[8,272,128]{2,1,0:T(8,128)(2,1)S(1)}, u32[]{:S(2)}, u32[]{:S(2)}) collective-permute-start(bf16[8,272,128]{2,1,0:T(8,128)(2,1)S(1)} %get-tuple-element.40), channel_id=1, source_target_pairs={{8,16},{16,8},{9,17},{17,9},{10,18},{18,10},{11,19},{19,11},{12,20... | collective-permute-start | bytes 1671176 | tf_op jit(solution)/shard_map/ppermute | solution.py:325
  7.0 13.2 %collective-permute-start.4 = (bf16[8,272,128]{2,1,0:T(8,128)(2,1)S(1)}, bf16[8,272,128]{2,1,0:T(8,128)(2,1)S(1)}, u32[]{:S(2)}, u32[]{:S(2)}) collective-permute-start(bf16[8,272,128]{2,1,0:T(8,128)(2,1)S(1)} %get-tuple-element.40), channel_id=1, source_target_pairs={{0,8},{8,0},{16,24},{24,16},{1,9},{9,1},{17,25},{25,17},{2,10},{10... | collective-permute-start | bytes 1671176 | tf_op jit(solution)/shard_map/ppermute | solution.py:325
  16.6 8.1 %collective-permute-start.3 = (bf16[1,4,272,128]{3,2,1,0:T(8,128)(2,1)S(1)}, bf16[1,4,272,128]{3,2,1,0:T(8,128)(2,1)S(1)}, u32[]{:S(2)}, u32[]{:S(2)}) collective-permute-start(bf16[1,4,272,128]{3,2,1,0:T(8,128)(2,1)S(1)} %pad_maximum_fusion.5), channel_id=1, source_target_pairs={{0,1},{1,0},{2,3},{3,2},{4,5},{5,4},{6,7},{7,6},{8,9},{9,8},{10,11... | collective-permute-start | bytes 835592 | tf_op jit(solution)/shard_map/ppermute | solution.py:312
  20.3 9.3 %collective-permute-start.6 = (bf16[6,272,128]{2,1,0:T(8,128)(2,1)S(1)}, bf16[6,272,128]{2,1,0:T(8,128)(2,1)S(1)}, u32[]{:S(2)}, u32[]{:S(2)}) collective-permute-start(bf16[6,272,128]{2,1,0:T(8,128)(2,1)S(1)} %pad_maximum_fusion.2), channel_id=1, source_target_pairs={{0,2},{1,3},{2,0},{3,1},{4,6},{5,7},{6,4},{7,5},{8,10},{9,11},{10,... | collective-permute-start | bytes 1253384 | tf_op jit(solution)/shard_map/ppermute | solution.py:312
  22.4 10.2 %collective-permute-start.7 = (bf16[6,272,128]{2,1,0:T(8,128)(2,1)}, bf16[6,272,128]{2,1,0:T(8,128)(2,1)S(1)}, u32[]{:S(2)}, u32[]{:S(2)}) collective-permute-start(bf16[6,272,128]{2,1,0:T(8,128)(2,1)} %pad_maximum_fusion.3), channel_id=1, source_target_pairs={{0,4},{1,5},{2,6},{3,7},{4,0},{5,1},{6,2},{7,3},{8,12},{9,13},{10,... | collective-permute-start | bytes 1253384 | tf_op jit(solution)/shard_map/ppermute | solution.py:312
  24.5 15.2 %collective-permute-start.8 = (bf16[6,272,128]{2,1,0:T(8,128)(2,1)}, bf16[6,272,128]{2,1,0:T(8,128)(2,1)}, u32[]{:S(2)}, u32[]{:S(2)}) collective-permute-start(bf16[6,272,128]{2,1,0:T(8,128)(2,1)} %pad_maximum_fusion.4), channel_id=1, source_target_pairs={{0,6},{1,7},{2,4},{3,5},{4,2},{5,3},{6,0},{7,1},{8,14},{9,15},{10,... | collective-permute-start | bytes 1253384 | tf_op jit(solution)/shard_map/ppermute | solution.py:312
  24.8 26.7 %collective-permute-start.12 = (bf16[8,2,128,128]{3,2,1,0:T(8,128)(2,1)S(1)}, bf16[8,2,128,128]{3,2,1,0:T(8,128)(2,1)S(1)}, u32[]{:S(2)}, u32[]{:S(2)}) collective-permute-start(bf16[8,2,128,128]{3,2,1,0:T(8,128)(2,1)S(1)} %bitcast.97), channel_id=1, source_target_pairs={{8,16},{16,8},{9,17},{17,9},{10,18},{18,10},{11,19},{19,11},{12,20... | collective-permute-start | bytes 1572872 | tf_op jit(solution)/shard_map/ppermute | solution.py:325
  27.0 24.5 %collective-permute-start.10 = (bf16[8,2,128,128]{3,2,1,0:T(8,128)(2,1)S(1)}, bf16[8,2,128,128]{3,2,1,0:T(8,128)(2,1)}, u32[]{:S(2)}, u32[]{:S(2)}) collective-permute-start(bf16[8,2,128,128]{3,2,1,0:T(8,128)(2,1)S(1)} %bitcast.98), channel_id=1, source_target_pairs={{0,8},{8,0},{16,24},{24,16},{1,9},{9,1},{17,25},{25,17},{2,10},{10... | collective-permute-start | bytes 1572872 | tf_op jit(solution)/shard_map/ppermute | solution.py:325
  51.5 23.7 %collective-permute-start.15 = (bf16[8,2,128,128]{3,2,1,0:T(8,128)(2,1)}, bf16[8,2,128,128]{3,2,1,0:T(8,128)(2,1)}, u32[]{:S(2)}, u32[]{:S(2)}) collective-permute-start(bf16[8,2,128,128]{3,2,1,0:T(8,128)(2,1)} %collective-permute-done.10.refs_1_), channel_id=1, source_target_pairs={{8,16},{16,8},{9,17},{17,9},{10,18},{18,10},{11,19},{19,11},{12,20... | collective-permute-start | bytes 1572872 | tf_op jit(solution)/shard_map/ppermute | solution.py:325
  54.4 10.1 %collective-permute-start.11 = (bf16[1024,128]{1,0:T(8,128)(2,1)}, bf16[1024,128]{1,0:T(8,128)(2,1)S(1)}, u32[]{:S(2)}, u32[]{:S(2)}) collective-permute-start(bf16[1024,128]{1,0:T(8,128)(2,1)} %get-tuple-element.44), channel_id=1, source_target_pairs={{0,8},{24,16},{1,9},{25,17},{2,10},{26,18},{3,11},{27,19},{4,12},{... | collective-permute-start | bytes 786440 | tf_op jit(solution)/shard_map/ppermute | solution.py:328
  72.7 25.2 %collective-permute-start.14 = (bf16[8,2,128,128]{3,2,1,0:T(8,128)(2,1)S(1)}, bf16[8,2,128,128]{3,2,1,0:T(8,128)(2,1)S(1)}, u32[]{:S(2)}, u32[]{:S(2)}) collective-permute-start(bf16[8,2,128,128]{3,2,1,0:T(8,128)(2,1)S(1)} %bitcast.94), channel_id=1, source_target_pairs={{8,16},{16,8},{9,17},{17,9},{10,18},{18,10},{11,19},{19,11},{12,20... | collective-permute-start | bytes 1572872 | tf_op jit(solution)/shard_map/ppermute | solution.py:325
  81.3 16.4 %collective-permute-start.16 = (bf16[8,144,128]{2,1,0:T(8,128)(2,1)}, bf16[8,144,128]{2,1,0:T(8,128)(2,1)S(1)}, u32[]{:S(2)}, u32[]{:S(2)}) collective-permute-start(bf16[8,144,128]{2,1,0:T(8,128)(2,1)} %get-tuple-element.61), channel_id=1, source_target_pairs={{8,0},{16,24},{9,1},{17,25},{10,2},{18,26},{11,3},{19,27},{12,4},{... | collective-permute-start | bytes 884744 | tf_op jit(solution)/shard_map/ppermute | solution.py:331
  82.6 8.6 %collective-permute-start.13 = (bf16[1024,128]{1,0:T(8,128)(2,1)}, bf16[1024,128]{1,0:T(8,128)(2,1)S(1)}, u32[]{:S(2)}, u32[]{:S(2)}) collective-permute-start(bf16[1024,128]{1,0:T(8,128)(2,1)} %get-tuple-element.54), channel_id=1, source_target_pairs={{0,8},{24,16},{1,9},{25,17},{2,10},{26,18},{3,11},{27,19},{4,12},{... | collective-permute-start | bytes 786440 | tf_op jit(solution)/shard_map/ppermute | solution.py:328
  101.6 16.6 %collective-permute-start.17 = (bf16[8,144,128]{2,1,0:T(8,128)(2,1)S(1)}, bf16[8,144,128]{2,1,0:T(8,128)(2,1)S(1)}, u32[]{:S(2)}, u32[]{:S(2)}) collective-permute-start(bf16[8,144,128]{2,1,0:T(8,128)(2,1)S(1)} %get-tuple-element.72), channel_id=1, source_target_pairs={{8,0},{16,24},{9,1},{17,25},{10,2},{18,26},{11,3},{19,27},{12,4},{... | collective-permute-start | bytes 884744 | tf_op jit(solution)/shard_map/ppermute | solution.py:331
  104.1 13.5 %collective-permute-start.28 = (bf16[1024,128]{1,0:T(8,128)(2,1)S(1)}, bf16[1024,128]{1,0:T(8,128)(2,1)S(1)}, u32[]{:S(2)}, u32[]{:S(2)}) collective-permute-start(bf16[1024,128]{1,0:T(8,128)(2,1)S(1)} %merge_0.1.refs_0_), channel_id=1, source_target_pairs={{0,4},{1,5},{2,6},{3,7},{4,0},{5,1},{6,2},{7,3},{8,12},{9,13},{10,... | collective-permute-start | bytes 786440 | tf_op jit(solution)/shard_map/ppermute | solution.py:312
  104.4 15.3 %collective-permute-start.26 = (bf16[1024,128]{1,0:T(8,128)(2,1)S(1)}, bf16[1024,128]{1,0:T(8,128)(2,1)S(1)}, u32[]{:S(2)}, u32[]{:S(2)}) collective-permute-start(bf16[1024,128]{1,0:T(8,128)(2,1)S(1)} %merge_0.1.refs_0_), channel_id=1, source_target_pairs={{0,2},{1,3},{2,0},{3,1},{4,6},{5,7},{6,4},{7,5},{8,10},{9,11},{10,... | collective-permute-start | bytes 786440 | tf_op jit(solution)/shard_map/ppermute | solution.py:312
  105.6 14.3 %collective-permute-start.25 = (bf16[1024,128]{1,0:T(8,128)(2,1)S(1)}, bf16[1024,128]{1,0:T(8,128)(2,1)S(1)}, u32[]{:S(2)}, u32[]{:S(2)}) collective-permute-start(bf16[1024,128]{1,0:T(8,128)(2,1)S(1)} %merge_0.1.refs_0_), channel_id=1, source_target_pairs={{0,1},{1,0},{2,3},{3,2},{4,5},{5,4},{6,7},{7,6},{8,9},{9,8},{10,11... | collective-permute-start | bytes 786440 | tf_op jit(solution)/shard_map/ppermute | solution.py:312
  109.5 11.6 %collective-permute-start.31 = (bf16[1024,128]{1,0:T(8,128)(2,1)S(1)}, bf16[1024,128]{1,0:T(8,128)(2,1)S(1)}, u32[]{:S(2)}, u32[]{:S(2)}) collective-permute-start(bf16[1024,128]{1,0:T(8,128)(2,1)S(1)} %collective-permute-done.30.refs_6_), channel_id=1, source_target_pairs={{0,1},{1,0},{2,3},{3,2},{4,5},{5,4},{6,7},{7,6},{8,9},{9,8},{10,11... | collective-permute-start | bytes 786440 | tf_op jit(solution)/shard_map/ppermute | solution.py:312
  118.4 8.9 %collective-permute-start.23 = (bf16[1024,128]{1,0:T(8,128)(2,1)S(1)}, bf16[1024,128]{1,0:T(8,128)(2,1)S(1)}, u32[]{:S(2)}, u32[]{:S(2)}) collective-permute-start(bf16[1024,128]{1,0:T(8,128)(2,1)S(1)} %merge_1.1.refs_0_), channel_id=1, source_target_pairs={{0,6},{1,7},{2,4},{3,5},{4,2},{5,3},{6,0},{7,1},{8,14},{9,15},{10,... | collective-permute-start | bytes 786440 | tf_op jit(solution)/shard_map/ppermute | solution.py:312
  119.6 13.6 %collective-permute-start.21 = (bf16[1024,128]{1,0:T(8,128)(2,1)S(1)}, bf16[1024,128]{1,0:T(8,128)(2,1)S(1)}, u32[]{:S(2)}, u32[]{:S(2)}) collective-permute-start(bf16[1024,128]{1,0:T(8,128)(2,1)S(1)} %merge_1.1.refs_0_), channel_id=1, source_target_pairs={{0,4},{1,5},{2,6},{3,7},{4,0},{5,1},{6,2},{7,3},{8,12},{9,13},{10,... | collective-permute-start | bytes 786440 | tf_op jit(solution)/shard_map/ppermute | solution.py:312
  119.9 13.8 %collective-permute-start.19 = (bf16[1024,128]{1,0:T(8,128)(2,1)S(1)}, bf16[1024,128]{1,0:T(8,128)(2,1)S(1)}, u32[]{:S(2)}, u32[]{:S(2)}) collective-permute-start(bf16[1024,128]{1,0:T(8,128)(2,1)S(1)} %merge_1.1.refs_0_), channel_id=1, source_target_pairs={{0,2},{1,3},{2,0},{3,1},{4,6},{5,7},{6,4},{7,5},{8,10},{9,11},{10,... | collective-permute-start | bytes 786440 | tf_op jit(solution)/shard_map/ppermute | solution.py:312
  121.1 12.6 %collective-permute-start.27 = (bf16[1024,128]{1,0:T(8,128)(2,1)S(1)}, bf16[1024,128]{1,0:T(8,128)(2,1)S(1)}, u32[]{:S(2)}, u32[]{:S(2)}) collective-permute-start(bf16[1024,128]{1,0:T(8,128)(2,1)S(1)} %collective-permute-done.26.refs_2_), channel_id=1, source_target_pairs={{0,1},{1,0},{2,3},{3,2},{4,5},{5,4},{6,7},{7,6},{8,9},{9,8},{10,11... | collective-permute-start | bytes 786440 | tf_op jit(solution)/shard_map/ppermute | solution.py:312
  122.0 13.2 %collective-permute-start.18 = (bf16[1024,128]{1,0:T(8,128)(2,1)S(1)}, bf16[1024,128]{1,0:T(8,128)(2,1)S(1)}, u32[]{:S(2)}, u32[]{:S(2)}) collective-permute-start(bf16[1024,128]{1,0:T(8,128)(2,1)S(1)} %merge_1.1.refs_0_), channel_id=1, source_target_pairs={{0,1},{1,0},{2,3},{3,2},{4,5},{5,4},{6,7},{7,6},{8,9},{9,8},{10,11... | collective-permute-start | bytes 786440 | tf_op jit(solution)/shard_map/ppermute | solution.py:312
  127.3 7.8 %collective-permute-start.24 = (bf16[1024,128]{1,0:T(8,128)(2,1)S(1)}, bf16[1024,128]{1,0:T(8,128)(2,1)S(1)}, u32[]{:S(2)}, u32[]{:S(2)}) collective-permute-start(bf16[1024,128]{1,0:T(8,128)(2,1)S(1)} %collective-permute-done.23.refs_6_), channel_id=1, source_target_pairs={{0,1},{1,0},{2,3},{3,2},{4,5},{5,4},{6,7},{7,6},{8,9},{9,8},{10,11... | collective-permute-start | bytes 786440 | tf_op jit(solution)/shard_map/ppermute | solution.py:312
  (20 other events, 102.9 us)

commit v7 on v6

v7 whole, which is shorter than its diff:
```python
import functools
import math

import jax
import jax.numpy as jnp
from jax import lax
from jax.experimental import pallas as pl
from jax.experimental.pallas import tpu as pltpu
from jax.sharding import PartitionSpec as P

HEADS = 16
HEAD_DIM = 128
BLOCK = 128
NEG = -1e30
EXP2_SCALE = math.log2(math.e) / math.sqrt(HEAD_DIM)
GROUP = 8
STAT_ROWS = 16
ROW_SHIFT = 16
VMEM_BYTES = 40 * 1024 * 1024
MOST_VMEM_BYTES = 60 * 1024 * 1024

VMEM = pl.BlockSpec(memory_space=pltpu.VMEM)
SMEM = pl.BlockSpec(memory_space=pltpu.SMEM)
ANY = pl.BlockSpec(memory_space=pl.ANY)


def params(size=VMEM_BYTES):
    return pltpu.CompilerParams(vmem_limit_bytes=size)


def mask_rows(rows):
    return -(-rows // 16) * 16


def pack_kernel(n_ka, heads, me_ref, mask_ref, k_all, v_all, *refs):
    out_refs, (k_ref, v_ref, sems) = refs[:heads], refs[heads:]
    key_blocks = k_ref.shape[0] // BLOCK
    parts = sems.shape[1]
    width = k_ref.shape[1] // parts
    copies = []
    for i in range(parts):
        at = slice(i * width, (i + 1) * width)
        copies.append(pltpu.make_async_copy(k_all.at[:, at], k_ref.at[:, at], sems.at[0, i]))
        copies.append(pltpu.make_async_copy(v_all.at[:, at], v_ref.at[:, at], sems.at[1, i]))
    for copy in copies:
        copy.start()
    rows, used = mask_rows(mask_ref.shape[0]), mask_ref.shape[0]
    column = lax.broadcasted_iota(jnp.int32, (used, HEAD_DIM), 1)
    mask = jnp.zeros((used, HEAD_DIM), jnp.float32)
    for j in range(mask_ref.shape[1]):
        mask = jnp.where(column == j, mask_ref[:, j : j + 1].astype(jnp.float32), mask)
    if rows > used:
        mask = jnp.concatenate([mask, jnp.zeros((rows - used, HEAD_DIM), jnp.float32)])
    mask = mask.astype(k_ref.dtype)
    for k in range(n_ka):
        out_refs[0][k, 2 * key_blocks * BLOCK :] = mask
    for copy in copies:
        copy.wait()
    for c in range(heads):
        for k in range(n_ka):
            col = pl.multiple_of(((me_ref[0] ^ k) * heads + c) * HEAD_DIM, HEAD_DIM)
            for t in range(key_blocks):
                rows, at = slice(t * BLOCK, (t + 1) * BLOCK), 2 * t * BLOCK
                out_refs[c][k, at : at + BLOCK] = k_ref[rows, pl.ds(col, HEAD_DIM)]
                out_refs[c][k, at + BLOCK : at + 2 * BLOCK] = v_ref[rows, pl.ds(col, HEAD_DIM)].T


def mask_rows(rows):
    return -(-rows // 16) * 16


def pack(me, keys, values, mask, n_ka, heads):
    sizes = [2 * keys.shape[0] + (mask_rows(mask.shape[0]) if c == 0 else 0) for c in range(heads)]
    parts = 4
    return pl.pallas_call(
        functools.partial(pack_kernel, n_ka, heads),
        out_shape=[jax.ShapeDtypeStruct((n_ka, size, HEAD_DIM), keys.dtype) for size in sizes],
        in_specs=[SMEM, VMEM, ANY, ANY],
        out_specs=[VMEM] * heads,
        scratch_shapes=[
            pltpu.VMEM(keys.shape, keys.dtype),
            pltpu.VMEM(values.shape, values.dtype),
            pltpu.SemaphoreType.DMA((2, parts)),
        ],
        compiler_params=params(MOST_VMEM_BYTES),
        name="pack",
    )(me, mask, keys, values)


def turn_kernel(heads, me_ref, q_all, *refs):
    out_refs, (q_ref, sem) = refs[:heads], refs[heads:]
    column = pl.multiple_of(me_ref[0] * heads * HEAD_DIM, HEAD_DIM)
    copy = pltpu.make_async_copy(q_all.at[:, pl.ds(column, heads * HEAD_DIM)], q_ref, sem)
    copy.start()
    copy.wait()
    for c in range(heads):
        for r in range(out_refs[c].shape[0]):
            out_refs[c][r] = q_ref[r * BLOCK : (r + 1) * BLOCK, c * HEAD_DIM : (c + 1) * HEAD_DIM].T


def turn(me, queries, heads):
    tokens = queries.shape[0]
    shape = jax.ShapeDtypeStruct((tokens // BLOCK, HEAD_DIM, BLOCK), queries.dtype)
    return pl.pallas_call(
        functools.partial(turn_kernel, heads),
        out_shape=[shape] * heads,
        in_specs=[SMEM, ANY],
        out_specs=[VMEM] * heads,
        scratch_shapes=[pltpu.VMEM((tokens, heads * HEAD_DIM), queries.dtype), pltpu.SemaphoreType.DMA],
        compiler_params=params(MOST_VMEM_BYTES),
        name="turn",
    )(me, queries)


def plan_kernel(steps, n_pb, n_slots, key_blocks, rows, relay, pb_ref, *refs):
    mask_refs, count_ref, live_refs = refs[: -len(steps) - 1], refs[-len(steps) - 1], refs[-len(steps) :]
    pb = pb_ref[0]
    sign = 1 - 2 * (pb & 1)
    inner = ((pb > 0) & (pb < n_pb - 1)).astype(jnp.int32)
    helper = ((pb == 1) | (pb == n_pb - 2)).astype(jnp.int32)
    for step, (sources, live) in enumerate(zip(steps, live_refs)):
        total = jnp.int32(0)
        for guest, mask_ref in enumerate(mask_refs):

            def row_step(r, base, guest=guest, mask_ref=mask_ref):
                count = jnp.int32(0)
                for s, (delta, open_to_guests) in enumerate(sources):
                    if guest and not open_to_guests:
                        continue
                    j = pb + delta * sign
                    inside = ((j >= 0) & (j < n_pb)).astype(jnp.int32)
                    if relay and abs(delta) > 1:
                        inside = inside * inner
                    if guest:
                        inside = inside * helper
                    j = jnp.clip(j, 0, n_pb - 1)
                    for slot in range(n_slots):
                        for t in range(key_blocks):
                            block = (s * n_slots + slot) * key_blocks + t
                            live[2 * base + count] = ((r + guest * rows) << ROW_SHIFT) + block
                            column = j * key_blocks + t
                            count += inside * mask_ref[(slot * rows + r) * (n_pb * key_blocks) + column]
                live[2 * base + count] = -1
                return base + ((count + 1) >> 1)

            total = lax.fori_loop(0, rows, row_step, total)
        for u in range(GROUP):
            live[2 * (total + u)] = 0
            live[2 * (total + u) + 1] = -1
        count_ref[step] = total


def plan(pb, masks, steps, n_pb, n_slots, key_blocks, rows, relay):
    sizes = [len(masks) * rows * ((len(step) * n_slots * key_blocks + 2) // 2) + GROUP for step in steps]
    out_shape = [jax.ShapeDtypeStruct((len(steps),), jnp.int32)]
    out_shape += [jax.ShapeDtypeStruct((2 * size,), jnp.int32) for size in sizes]
    counts, *lives = pl.pallas_call(
        functools.partial(plan_kernel, steps, n_pb, n_slots, key_blocks, rows, relay),
        out_shape=out_shape,
        in_specs=[SMEM] * (1 + len(masks)),
        out_specs=[SMEM] * len(out_shape),
        compiler_params=params(),
        name="plan",
    )(pb, *masks)
    return [(counts, i, live) for i, live in enumerate(lives)]


def in_parts(x):
    found = []
    for _ in range(3):
        found.append(x.astype(jnp.bfloat16).astype(jnp.float32))
        x = x - found[-1]
    return found


def attend_kernel(n_src, entry, first, mode, guests, count_ref, live_ref, q_own, *refs):
    n_kv = n_src
    guest_ref, refs = (refs[0], refs[1:]) if guests else (None, refs)
    kv_refs, refs = refs[:n_kv], refs[n_kv:]
    state_in, refs = ((), refs) if first else (refs[:3], refs[3:])
    if mode == "last":
        (out_ref, kv, q_ref, *state, sems) = refs
    elif mode == "send":
        (*state, part_ref, kv, q_ref, sems) = refs
    else:
        (*state, kv, q_ref, sems) = refs
    m_ref, l_ref, acc_ref = state
    blocks = kv.shape[0] // n_src
    rows = q_own.shape[0]
    copies = [
        pltpu.make_async_copy(kv_refs[s], kv.at[pl.ds(s * blocks, blocks)], sems.at[s]) for s in range(n_src)
    ]
    copies += [pltpu.make_async_copy(a, b, sems.at[n_src + i]) for i, (a, b) in enumerate(zip(state_in, state))]
    copies.append(pltpu.make_async_copy(q_own, q_ref.at[pl.ds(0, rows)], sems.at[n_src + 3]))
    if guests:
        copies.append(pltpu.make_async_copy(guest_ref.at[pl.ds(0, rows)], q_ref.at[pl.ds(rows, rows)], sems.at[n_src + 4]))
    for copy in copies:
        copy.start()
    if first:
        m_ref[...] = jnp.full(m_ref.shape, NEG, jnp.float32)
        l_ref[...] = jnp.zeros(l_ref.shape, jnp.float32)
        acc_ref[...] = jnp.zeros(acc_ref.shape, jnp.float32)
    for copy in copies:
        copy.wait()
    total = count_ref[entry]
    nn = (((1,), (0,)), ((), ()))
    f32, bf16 = jnp.float32, jnp.bfloat16

    def group_step(g, _):
        found = []
        for u in range(GROUP):
            index = g * GROUP + u
            code0, code1 = live_ref[2 * index], live_ref[2 * index + 1]
            r = code0 >> ROW_SHIFT
            b0 = code0 & ((1 << ROW_SHIFT) - 1)
            b1 = jnp.maximum(code1, 0) & ((1 << ROW_SHIFT) - 1)
            x = lax.dot_general(jnp.concatenate([kv[b0, 0], kv[b1, 0]]), q_ref[r], nn, preferred_element_type=f32)
            x0 = jnp.where(index < total, x[:BLOCK], NEG)
            x1 = jnp.where(code1 >= 0, x[BLOCK:], NEG)
            top = jnp.max(jnp.maximum(x0, x1), axis=0, keepdims=True)
            w0 = jnp.exp2((x0 - top) * EXP2_SCALE)
            w1 = jnp.exp2((x1 - top) * EXP2_SCALE)
            total_w = jnp.sum(w0 + w1, axis=0, keepdims=True)
            w = jnp.concatenate([w0.astype(bf16), w1.astype(bf16)])
            v = jnp.concatenate([kv[b0, 1], kv[b1, 1]], axis=1)
            found.append((r, top, total_w, lax.dot_general(v, w, nn, preferred_element_type=f32)))
        for r, top, total_w, part in found:
            m = m_ref[r]
            m_new = jnp.maximum(m, top)
            alpha = jnp.exp2((m - m_new) * EXP2_SCALE)
            beta = jnp.exp2((top - m_new) * EXP2_SCALE)
            m_ref[r] = m_new
            l_ref[r] = l_ref[r] * alpha + total_w * beta
            acc_ref[r] = acc_ref[r] * alpha + part * beta
        return 0

    lax.fori_loop(0, (total + GROUP - 1) // GROUP, group_step, 0)
    if mode == "last":
        for r in range(rows):
            out_ref[r * BLOCK : (r + 1) * BLOCK, :] = (acc_ref[r] / l_ref[r]).T.astype(out_ref.dtype)
    if mode == "send":
        for r in range(rows):
            l = l_ref[rows + r]
            part_ref[r, :HEAD_DIM] = (acc_ref[rows + r] / jnp.where(l > 0, l, 1.0)).astype(part_ref.dtype)
            words = in_parts(m_ref[rows + r]) + in_parts(l)
            words.append(jnp.zeros((STAT_ROWS - len(words), BLOCK), f32))
            part_ref[r, HEAD_DIM:] = jnp.concatenate(words).astype(part_ref.dtype)


def attend(listed, q, guest, sources, state, mode, sets, name):
    counts, entry, live = listed
    rows, dtype = q.shape[0], q.dtype
    first = state is None
    state = () if first else tuple(state)
    stat = (sets * rows, 1, BLOCK)
    shapes = [stat, stat, (sets * rows, HEAD_DIM, BLOCK)]
    if mode == "last":
        out_shape = [jax.ShapeDtypeStruct((rows * BLOCK, HEAD_DIM), dtype)]
    else:
        out_shape = [jax.ShapeDtypeStruct(shape, jnp.float32) for shape in shapes]
    if mode == "send":
        out_shape.append(jax.ShapeDtypeStruct((rows, HEAD_DIM + STAT_ROWS, BLOCK), dtype))
    n_src = len(sources)
    blocks = sources[0].shape[0]
    guests = () if guest is None else (guest,)
    scratch = [pltpu.VMEM((n_src * blocks,) + sources[0].shape[1:], dtype)]
    scratch += [pltpu.VMEM(((1 + len(guests)) * rows, HEAD_DIM, BLOCK), dtype)]
    if mode == "last":
        scratch += [pltpu.VMEM(shape, jnp.float32) for shape in shapes]
    scratch.append(pltpu.SemaphoreType.DMA((n_src + 5,)))
    return pl.pallas_call(
        functools.partial(attend_kernel, n_src, entry, first, mode, bool(guests)),
        out_shape=out_shape,
        in_specs=[SMEM, SMEM, ANY] + [ANY] * (len(guests) + n_src + len(state)),
        out_specs=[VMEM] * len(out_shape),
        scratch_shapes=scratch,
        compiler_params=params(),
        cost_estimate=pl.CostEstimate(flops=0, bytes_accessed=q.size, transcendentals=0),
        name=name,
    )(counts, live, q, *guests, *sources, *state)


def merge_kernel(outer_ref, m_ref, l_ref, acc_ref, part_ref, out_ref):
    outer = outer_ref[0] > 0
    for r in range(part_ref.shape[0]):
        m, l = m_ref[r], l_ref[r]
        words = part_ref[r, HEAD_DIM:].astype(jnp.float32)
        top = jnp.where(outer, words[0:1] + words[1:2] + words[2:3], NEG)
        extra = jnp.where(outer, words[3:4] + words[4:5] + words[5:6], 0.0)
        m_new = jnp.maximum(m, top)
        alpha = jnp.exp2((m - m_new) * EXP2_SCALE)
        beta = jnp.exp2((top - m_new) * EXP2_SCALE) * extra
        done = (acc_ref[r] * alpha + part_ref[r, :HEAD_DIM].astype(jnp.float32) * beta) / (l * alpha + beta)
        out_ref[r * BLOCK : (r + 1) * BLOCK, :] = done.T.astype(out_ref.dtype)


def merge(outer, state, part, name):
    rows = part.shape[0]
    half = lambda x: pl.BlockSpec((rows,) + x.shape[1:], lambda i: (0, 0, 0))
    return pl.pallas_call(
        merge_kernel,
        out_shape=jax.ShapeDtypeStruct((rows * BLOCK, HEAD_DIM), part.dtype),
        grid=(1,),
        in_specs=[SMEM] + [half(x) for x in state] + [VMEM],
        out_specs=VMEM,
        compiler_params=params(),
        name=name,
    )(outer, *state, part)


def place_kernel(n_ka, heads, me_ref, *refs):
    pieces, out_ref, sems = refs[: n_ka * heads], refs[-2], refs[-1]
    copies = []
    for k in range(n_ka):
        for c in range(heads):
            col = pl.multiple_of(((me_ref[0] ^ k) * heads + c) * HEAD_DIM, HEAD_DIM)
            copies.append(
                pltpu.make_async_copy(pieces[c * n_ka + k], out_ref.at[:, pl.ds(col, HEAD_DIM)], sems.at[c, k])
            )
    for copy in copies:
        copy.start()
    for copy in copies:
        copy.wait()


def place(me, pieces, n_ka, heads):
    rows = pieces[0].shape[0]
    return pl.pallas_call(
        functools.partial(place_kernel, n_ka, heads),
        out_shape=jax.ShapeDtypeStruct((rows, HEADS * HEAD_DIM), pieces[0].dtype),
        in_specs=[SMEM] + [ANY] * (n_ka * heads),
        out_specs=ANY,
        scratch_shapes=[pltpu.SemaphoreType.DMA((heads, n_ka))],
        compiler_params=params(),
        name="place",
    )(me, *pieces)


def local(n_pb, n_ka, queries, keys, values, block_mask):
    heads = HEADS // n_ka
    shard = keys.shape[0]
    key_blocks = shard // BLOCK
    rows = queries.shape[0] // BLOCK
    me = lax.axis_index("ka").astype(jnp.int32)
    pb = lax.axis_index("pb").astype(jnp.int32)
    me1, pb1 = me[None], pb[None]
    relay = n_pb >= 4 and n_pb % 2 == 0
    def swap(x, k):
        return lax.ppermute(x, "ka", [(i, i ^ k) for i in range(n_ka)])

    def hops(odd, step):
        found = []
        for low in range(odd, n_pb - 1, 2):
            found += [(low, low + 1)] if low - (step - 1) >= 0 else []
            found += [(low + 1, low)] if low + 1 + (step - 1) < n_pb else []
        if relay and step > 1:
            found = [(i, j) for i, j in found if 0 < j < n_pb - 1]
        return found

    def exchange(x, odd, step):
        found = hops(odd, step)
        return lax.ppermute(x, "pb", found) if found else None

    def inward(x):
        return lax.ppermute(x, "pb", [(0, 1), (n_pb - 1, n_pb - 2)])

    def outward(x):
        return lax.ppermute(x, "pb", [(1, 0), (n_pb - 2, n_pb - 1)])

    def sort(x):
        mixed = [x[:2]] + [swap(x[k : k + 2], k) for k in range(2, n_ka, 2)]
        theirs = swap(jnp.stack([x[1] for x in mixed]), 1)
        return jnp.concatenate([jnp.stack([x[0] for x in mixed]), theirs]), mixed[-1]

    def blocks(x):
        return x[:, : 2 * shard].reshape(n_ka * key_blocks, 2, BLOCK, HEAD_DIM)

    def after(arrays, done):
        return arrays if done is None else lax.optimization_barrier((arrays, done))[0]

    def flags(x):
        return x[:, :rows, : block_mask.shape[1]].astype(jnp.int32).reshape(-1)

    packed = pack(me1, keys, values, block_mask, n_ka, heads)
    owns, moved = [], None
    for c in range(heads):
        own, moved = sort(after(packed[c], moved))
        owns.append(blocks(own))
        if c == 0:
            marks = own[:, 2 * shard :]
    q = turn(me1, queries, heads)

    steps = [((0, False),)]
    for step in range(1, n_pb):
        found = (((step, False),) if hops(0, step) else ()) + (((-step, True),) if hops(1, step) else ())
        if step == 1:
            steps[0] += found
        elif found:
            steps.append(found)
    last = len(steps) - 1
    over = [[exchange(own, odd, 1) for odd in (0, 1)] for own in owns]
    masks = [flags(marks)]
    guest = [None] * heads
    if relay:
        first = jnp.concatenate([q[0], marks.reshape(-1, HEAD_DIM, BLOCK)])
        first = inward(after(first, over[0][0]))
        masks.append(flags(first[rows:].reshape(marks.shape)))
        guest = [first] + [inward(after(x, first)) for x in q[1:]]
    lists = plan(pb1, masks, steps, n_pb, n_ka, key_blocks, rows, relay)
    state = [None] * heads

    def run(c, step, sources):
        kind = "keep" if step < last else "send" if relay else "last"
        sources = [x for x in sources if x is not None]
        name = f"attend_{c}_{step}"
        return attend(lists[step], q[c], guest[c], sources, state[c], kind, 2 if relay else 1, name)

    for step in range(last):
        for c in range(heads):
            sources = ([owns[c]] if step == 0 else []) + over[c]
            over[c] = [exchange(over[c][1], 0, step + 2), exchange(over[c][0], 1, step + 2)]
            state[c] = run(c, step, sources)

    pieces = []
    out = None
    for c in range(heads):
        found = run(c, last, ([] if last else [owns[c]]) + after(over[c], out))
        if relay:
            outer = ((pb == 0) | (pb == n_pb - 1)).astype(jnp.int32)[None]
            out = merge(outer, found[:3], outward(found[3]), f"merge_{c}")
        else:
            out = found[0]
        mine = [out] + [swap(out, k) for k in range(2, n_ka, 2)]
        others = [swap(x, 1) for x in mine]
        pieces += [x for two in zip(mine, others) for x in two]
    return place(me1, pieces, n_ka, heads)


def solution(mesh):
    n_pb, n_ka = mesh.shape["pb"], mesh.shape["ka"]
    return jax.shard_map(
        functools.partial(local, n_pb, n_ka),
        mesh=mesh,
        in_specs=(P("pb", None), P(("ka", "pb"), None), P(("ka", "pb"), None), P("pb", "ka")),
        out_specs=P("pb", None),
        check_vma=False,
    )
```

time: 136 us -> 122 us (0.90); the launches traced: 137 us -> 121 us
  local copies, waits for them, and re-layouts: 14.9 us -> 6.65 us
  waiting for transfers between devices: 44.5 us -> 39 us
  Pallas kernels: 31.4 us -> 27 us
  starting transfers between devices: 43.4 us -> 46.4 us
    ppermute x22, waiting for transfers between devices: 30.9 us -> 19.5 us  [swap(): return lax.ppermute(x, 'ka', [(i, i ^ k) for i in range(n_ka)])]
    unnamed x33 -> x7, local copies, waits for them, and re-layouts: 12.3 us -> 2.29 us
    pallas_call x6 -> x4, Pallas kernels: 23.6 us -> 16.8 us  [attend(): pl.pallas_call(functools.partial(attend_kernel, n_src, entry, first, mode...]
    ppermute x6, waiting for transfers between devices: 2.83 us -> 9.56 us  [exchange(): return lax.ppermute(x, 'pb', found) if found else None]
    pallas_call x3, Pallas kernels: 3.67 us -> 7.37 us  [the longest x1 3.27 us: pack(): pl.pallas_call(functools.partial(pack_kernel, n_ka, heads), out_shape=[ja...]
    ppermute x6, starting transfers between devices: 9.88 us -> 13.4 us  [exchange(): return lax.ppermute(x, 'pb', found) if found else None]
    slice x12, local copies, waits for them, and re-layouts: 1.17 us -> 4.04 us  [the longest x2 2.13 us: sort(): mixed = [x[:2]] + [swap(x[k:k + 2], k) for k in range(2, n_ka, 2)]]
    pallas_call x2 -> x1, Pallas kernels: 3.69 us -> 2.43 us  [plan(): pl.pallas_call(functools.partial(plan_kernel, steps, n_pb, n_slots, key_b...]
  transfers between devices with their start and end apart: 32 -> 32, of which waited for: 14 -> 13; matrix products, arithmetic and copies ran while one was open for 5% -> 4% of each run, Pallas kernels for 19% -> 15%
where the time goes in v7:
time: 122 us; the launch traced here: 121 us
  starting transfers between devices  46.4 us (38%)
  waiting for transfers between devices  39 us (32%)
  Pallas kernels  27 us (22%)
  local copies, waits for them, and re-layouts  6.65 us (5%)
  other arithmetic  1.79 us (1%)
    ppermute x22, starting transfers between devices, swap(): return lax.ppermute(x, 'ka', [(i, i ^ k) for i in range(n_ka)])  27.8 us
    ppermute x22, waiting for transfers between devices, swap(): return lax.ppermute(x, 'ka', [(i, i ^ k) for i in range(n_ka)])  19.5 us
    pallas_call x4, Pallas kernels, attend(): pl.pallas_call(functools.partial(attend_kernel, n_src, entry, first, mode...  16.8 us
    ppermute x6, starting transfers between devices, exchange(): return lax.ppermute(x, 'pb', found) if found else None  13.4 us
    ppermute x2, waiting for transfers between devices, inward(): return lax.ppermute(x, 'pb', [(0, 1), (n_pb - 1, n_pb - 2)])  9.88 us
    ppermute x6, waiting for transfers between devices, exchange(): return lax.ppermute(x, 'pb', found) if found else None  9.56 us
    pallas_call x1, Pallas kernels, pack(): pl.pallas_call(functools.partial(pack_kernel, n_ka, heads), out_shape=[ja...  3.27 us
    ppermute x2, starting transfers between devices, outward(): return lax.ppermute(x, 'pb', [(1, 0), (n_pb - 2, n_pb - 1)])  2.62 us
  transfers between devices with their start and end apart: 32, of which 13 were waited for; matrix products, arithmetic and copies ran while one was open for 4% of the time, Pallas kernels for 15%

profile of v7, /device:TPU:9, one launch (start us, length us, event | category | flops | bytes accessed | tf_op | source)
XLA Modules:
  0.0 121.1 jit_solution(4151977199438226575)
XLA Ops:
  1.3 3.3 %pack.1 = (bf16[8,272,128]{2,1,0:T(8,128)(2,1)}, bf16[8,256,128]{2,1,0:T(8,128)(2,1)}) custom-call(s32[1]{0:T(128)} %bitcast.me_ref, s32[8,4]{1,0:T(8,128)} %copy.6.mask_ref, bf16[128,2048]{1,0:T(8,128)(2,1)} %k_all.1, bf16[128,2048]{1,0:T(8,128)(2,1)} %v_all.1), custom_call_target="tpu_custom_call" | custom-call | tf_op jit(solution)/shard_map/pack/pallas_call | solution.py:75
  5.7 2.2 %collective-permute-start.2 = (bf16[2,272,128]{2,1,0:T(8,128)(2,1)S(1)}, bf16[2,272,128]{2,1,0:T(8,128)(2,1)S(1)}, u32[]{:S(2)}, u32[]{:S(2)}) collective-permute-start(bf16[2,272,128]{2,1,0:T(8,128)(2,1)S(1)} %get-tuple-element.57), channel_id=1, source_target_pairs={{0,6},{1,7},{2,4},{3,5},{4,2},{5,3},{6,0},{7,1},{8,14},{9,15},{10,... | collective-permute-start | bytes 417800 | tf_op jit(solution)/shard_map/ppermute | solution.py:349
  12.3 2.3 %collective-permute-start.19 = (bf16[2,256,128]{2,1,0:T(8,128)(2,1)S(1)}, bf16[2,256,128]{2,1,0:T(8,128)(2,1)S(1)}, u32[]{:S(2)}, u32[]{:S(2)}) collective-permute-start(bf16[2,256,128]{2,1,0:T(8,128)(2,1)S(1)} %get-tuple-element.62), channel_id=1, source_target_pairs={{0,6},{1,7},{2,4},{3,5},{4,2},{5,3},{6,0},{7,1},{8,14},{9,15},{10,... | collective-permute-start | bytes 393224 | tf_op jit(solution)/shard_map/ppermute | solution.py:349
  15.3 3.0 %collective-permute-start.3 = (bf16[4,272,128]{2,1,0:T(8,128)(2,1)S(1)}, bf16[4,272,128]{2,1,0:T(8,128)(2,1)S(1)}, u32[]{:S(2)}, u32[]{:S(2)}) collective-permute-start(bf16[4,272,128]{2,1,0:T(8,128)(2,1)S(1)} %pad_maximum_fusion.1), channel_id=1, source_target_pairs={{0,1},{1,0},{2,3},{3,2},{4,5},{5,4},{6,7},{7,6},{8,9},{9,8},{10,11... | collective-permute-start | bytes 835592 | tf_op jit(solution)/shard_map/ppermute | solution.py:349
  19.3 3.8 %collective-permute-start.20 = (bf16[4,256,128]{2,1,0:T(8,128)(2,1)S(1)}, bf16[4,256,128]{2,1,0:T(8,128)(2,1)S(1)}, u32[]{:S(2)}, u32[]{:S(2)}) collective-permute-start(bf16[4,256,128]{2,1,0:T(8,128)(2,1)S(1)} %pad_maximum_fusion.2), channel_id=1, source_target_pairs={{0,1},{1,0},{2,3},{3,2},{4,5},{5,4},{6,7},{7,6},{8,9},{9,8},{10,11... | collective-permute-start | bytes 786440 | tf_op jit(solution)/shard_map/ppermute | solution.py:349
  26.9 4.2 %collective-permute-start.7 = (bf16[8,2,128,128]{3,2,1,0:T(8,128)(2,1)S(1)}, bf16[8,2,128,128]{3,2,1,0:T(8,128)(2,1)S(1)}, u32[]{:S(2)}, u32[]{:S(2)}) collective-permute-start(bf16[8,2,128,128]{3,2,1,0:T(8,128)(2,1)S(1)} %bitcast.8), channel_id=1, source_target_pairs={{8,16},{16,8},{9,17},{17,9},{10,18},{18,10},{11,19},{19,11},{12,20... | collective-permute-start | bytes 1572872 | tf_op jit(solution)/shard_map/ppermute | solution.py:362
  31.0 5.8 %collective-permute-done.4.refs_2_ = bf16[8,2,128,128]{3,2,1,0:T(8,128)(2,1)S(1)} collective-permute-done((bf16[8,2,128,128]{3,2,1,0:T(8,128)(2,1)S(1)}, bf16[8,2,128,128]{3,2,1,0:T(8,128)(2,1)S(1)}, u32[]{:S(2)}, u32[]{:S(2)}) %collective-permute-start.4) | collective-permute-done | bytes 524320 | tf_op jit(solution)/shard_map/ppermute | solution.py:362
  36.8 3.2 %collective-permute-start.6 = (bf16[8,2,128,128]{3,2,1,0:T(8,128)(2,1)S(1)}, bf16[8,2,128,128]{3,2,1,0:T(8,128)(2,1)S(1)}, u32[]{:S(2)}, u32[]{:S(2)}) collective-permute-start(bf16[8,2,128,128]{3,2,1,0:T(8,128)(2,1)S(1)} %collective-permute-done.4.refs_2_), channel_id=1, source_target_pairs={{8,16},{16,8},{9,17},{17,9},{10,18},{18,10},{11,19},{19,11},{12,20... | collective-permute-start | bytes 1572872 | tf_op jit(solution)/shard_map/ppermute | solution.py:362
  44.4 3.8 %collective-permute-done.21.refs_2_ = bf16[8,2,128,128]{3,2,1,0:T(8,128)(2,1)} collective-permute-done((bf16[8,2,128,128]{3,2,1,0:T(8,128)(2,1)S(1)}, bf16[8,2,128,128]{3,2,1,0:T(8,128)(2,1)}, u32[]{:S(2)}, u32[]{:S(2)}) %collective-permute-start.21) | collective-permute-done | bytes 524320 | tf_op jit(solution)/shard_map/ppermute | solution.py:362
  48.2 3.2 %collective-permute-start.22 = (bf16[8,2,128,128]{3,2,1,0:T(8,128)(2,1)}, bf16[8,2,128,128]{3,2,1,0:T(8,128)(2,1)}, u32[]{:S(2)}, u32[]{:S(2)}) collective-permute-start(bf16[8,2,128,128]{3,2,1,0:T(8,128)(2,1)} %collective-permute-done.21.refs_2_), channel_id=1, source_target_pairs={{8,16},{16,8},{9,17},{17,9},{10,18},{18,10},{11,19},{19,11},{12,20... | collective-permute-start | bytes 1572872 | tf_op jit(solution)/shard_map/ppermute | solution.py:362
  52.2 2.2 %collective-permute-done.5.refs_0_ = bf16[9,128,128]{2,1,0:T(8,128)(2,1)S(1)} collective-permute-done((bf16[9,128,128]{2,1,0:T(8,128)(2,1)S(1)}, bf16[9,128,128]{2,1,0:T(8,128)(2,1)S(1)}, u32[]{:S(2)}, u32[]{:S(2)}) %collective-permute-start.5) | collective-permute-done | bytes 294944 | tf_op jit(solution)/shard_map/ppermute | solution.py:365
  54.5 2.4 %plan.1 = (s32[2]{0:T(128)S(1)}, s32[432]{0:T(512)S(1)}, s32[176]{0:T(256)S(1)}) custom-call(s32[1]{0:T(128)} %bitcast.2.pb_ref, s32[256]{0:T(256)S(1)} %reshape.32.refs_0_, s32[256]{0:T(256)S(1)} %reshape.34.refs_1_), custom_call_target="tpu_custom_call" | custom-call | tf_op jit(solution)/shard_map/plan/pallas_call | solution.py:157
  57.9 4.7 %attend_0_0.1 = (f32[16,1,128]{2,1,0:T(1,128)S(1)}, f32[16,1,128]{2,1,0:T(1,128)S(1)}, f32[16,128,128]{2,1,0:T(8,128)S(1)}) custom-call(s32[2]{0:T(128)S(1)} %get-tuple-element.33.count_ref, s32[432]{0:T(512)S(1)} %get-tuple-element.35.live_ref, bf16[8,128,128]{2,1,0:T(8,128)(2,1)S(1)} %copy-done, bf16[9,128,128]{2,1,0:T(8,128)(2,1)S(1)} %collective-permute-done.5.refs_0_, ...), custom_call_target="tpu_custom_call" | custom-call | bytes 131072 | tf_op jit(solution)/shard_map/attend_0_0/pallas_call | solution.py:271
  62.6 2.8 %attend_0_1.1 = (f32[16,1,128]{2,1,0:T(1,128)S(1)}, f32[16,1,128]{2,1,0:T(1,128)S(1)}, f32[16,128,128]{2,1,0:T(8,128)S(1)}, bf16[8,144,128]{2,1,0:T(8,128)(2,1)S(1)}) custom-call(s32[2]{0:T(128)S(1)} %get-tuple-element.33.count_ref, s32[176]{0:T(256)S(1)} %get-tuple-element.34.live_ref, bf16[8,128,128]{2,1,0:T(8,128)(2,1)S(1)} %copy-done, ...), custom_call_target="tpu_custom_call" | custom-call | bytes 131072 | tf_op jit(solution)/shard_map/attend_0_1/pallas_call | solution.py:271
  68.1 7.7 %collective-permute-done.16.refs_0_ = bf16[8,128,128]{2,1,0:T(8,128)(2,1)S(1)} collective-permute-done((bf16[8,128,128]{2,1,0:T(8,128)(2,1)S(1)}, bf16[8,128,128]{2,1,0:T(8,128)(2,1)S(1)}, u32[]{:S(2)}, u32[]{:S(2)}) %collective-permute-start.16) | collective-permute-done | bytes 262176 | tf_op jit(solution)/shard_map/ppermute | solution.py:365
  75.8 5.7 %attend_1_0.1 = (f32[16,1,128]{2,1,0:T(1,128)S(1)}, f32[16,1,128]{2,1,0:T(1,128)S(1)}, f32[16,128,128]{2,1,0:T(8,128)S(1)}) custom-call(s32[2]{0:T(128)S(1)} %get-tuple-element.33.count_ref, s32[432]{0:T(512)S(1)} %get-tuple-element.35.live_ref, bf16[8,128,128]{2,1,0:T(8,128)(2,1)S(1)} %copy-done.1, ...), custom_call_target="tpu_custom_call" | custom-call | bytes 131072 | tf_op jit(solution)/shard_map/attend_1_0/pallas_call | solution.py:271
  81.7 3.6 %attend_1_1.1 = (f32[16,1,128]{2,1,0:T(1,128)S(1)}, f32[16,1,128]{2,1,0:T(1,128)S(1)}, f32[16,128,128]{2,1,0:T(8,128)S(1)}, bf16[8,144,128]{2,1,0:T(8,128)(2,1)S(1)}) custom-call(s32[2]{0:T(128)S(1)} %get-tuple-element.33.count_ref, s32[176]{0:T(256)S(1)} %get-tuple-element.34.live_ref, bf16[8,128,128]{2,1,0:T(8,128)(2,1)S(1)} %copy-done.1, ...), custom_call_target="tpu_custom_call" | custom-call | bytes 131072 | tf_op jit(solution)/shard_map/attend_1_1/pallas_call | solution.py:271
  89.4 2.4 %collective-permute-start.9 = (bf16[1024,128]{1,0:T(8,128)(2,1)S(1)}, bf16[1024,128]{1,0:T(8,128)(2,1)S(1)}, u32[]{:S(2)}, u32[]{:S(2)}) collective-permute-start(bf16[1024,128]{1,0:T(8,128)(2,1)S(1)} %merge_0.1.refs_0_), channel_id=1, source_target_pairs={{0,1},{1,0},{2,3},{3,2},{4,5},{5,4},{6,7},{7,6},{8,9},{9,8},{10,11... | collective-permute-start | bytes 786440 | tf_op jit(solution)/shard_map/ppermute | solution.py:349
  91.8 2.1 %collective-permute-done.14.refs_6_ = bf16[1024,128]{1,0:T(8,128)(2,1)S(1)} collective-permute-done((bf16[1024,128]{1,0:T(8,128)(2,1)S(1)}, bf16[1024,128]{1,0:T(8,128)(2,1)S(1)}, u32[]{:S(2)}, u32[]{:S(2)}) %collective-permute-start.14) | collective-permute-done | bytes 262176 | tf_op jit(solution)/shard_map/ppermute | solution.py:349
  93.9 4.6 %collective-permute-start.15 = (bf16[1024,128]{1,0:T(8,128)(2,1)S(1)}, bf16[1024,128]{1,0:T(8,128)(2,1)S(1)}, u32[]{:S(2)}, u32[]{:S(2)}) collective-permute-start(bf16[1024,128]{1,0:T(8,128)(2,1)S(1)} %collective-permute-done.14.refs_6_), channel_id=1, source_target_pairs={{0,1},{1,0},{2,3},{3,2},{4,5},{5,4},{6,7},{7,6},{8,9},{9,8},{10,11... | collective-permute-start | bytes 786440 | tf_op jit(solution)/shard_map/ppermute | solution.py:349
  98.5 3.0 %collective-permute-done.12.refs_4_ = bf16[1024,128]{1,0:T(8,128)(2,1)S(1)} collective-permute-done((bf16[1024,128]{1,0:T(8,128)(2,1)S(1)}, bf16[1024,128]{1,0:T(8,128)(2,1)S(1)}, u32[]{:S(2)}, u32[]{:S(2)}) %collective-permute-start.12) | collective-permute-done | bytes 262176 | tf_op jit(solution)/shard_map/ppermute | solution.py:349
  105.8 5.3 %collective-permute-done.30.refs_14_ = bf16[1024,128]{1,0:T(8,128)(2,1)S(1)} collective-permute-done((bf16[1024,128]{1,0:T(8,128)(2,1)S(1)}, bf16[1024,128]{1,0:T(8,128)(2,1)S(1)}, u32[]{:S(2)}, u32[]{:S(2)}) %collective-permute-start.30) | collective-permute-done | bytes 262176 | tf_op jit(solution)/shard_map/ppermute | solution.py:349
  112.3 4.7 %collective-permute-done.28.refs_12_ = bf16[1024,128]{1,0:T(8,128)(2,1)S(1)} collective-permute-done((bf16[1024,128]{1,0:T(8,128)(2,1)S(1)}, bf16[1024,128]{1,0:T(8,128)(2,1)S(1)}, u32[]{:S(2)}, u32[]{:S(2)}) %collective-permute-start.28) | collective-permute-done | bytes 262176 | tf_op jit(solution)/shard_map/ppermute | solution.py:349
  119.0 2.1 %place.1 = bf16[1024,2048]{1,0:T(8,128)(2,1)} custom-call(s32[1]{0:T(128)} %bitcast.me_ref, bf16[1024,128]{1,0:T(8,128)(2,1)S(1)} %merge_0.1.refs_0_, bf16[1024,128]{1,0:T(8,128)(2,1)S(1)} %collective-permute-done.9.refs_1_, bf16[1024,128]{1,0:T(8,128)(2,1)S(1)} %collective-permute-done.10.refs_2_, bf16[1024,128]{1,0:T(8,128)(2,1)S(1)} %collective-permute-done.11.refs_3_, ...), custom_call_target="tpu_custom_call" | custom-call | tf_op jit(solution)/shard_map/place/pallas_call | solution.py:328
  (79 shorter events, 32.7 us)
Async XLA Ops:
  7.9 7.3 %collective-permute-start.1 = (bf16[2,272,128]{2,1,0:T(8,128)(2,1)S(1)}, bf16[2,272,128]{2,1,0:T(8,128)(2,1)S(1)}, u32[]{:S(2)}, u32[]{:S(2)}) collective-permute-start(bf16[2,272,128]{2,1,0:T(8,128)(2,1)S(1)} %get-tuple-element.58), channel_id=1, source_target_pairs={{0,4},{1,5},{2,6},{3,7},{4,0},{5,1},{6,2},{7,3},{8,12},{9,13},{10,... | collective-permute-start | bytes 417800 | tf_op jit(solution)/shard_map/ppermute | solution.py:349
  8.2 6.8 %collective-permute-start = (bf16[2,272,128]{2,1,0:T(8,128)(2,1)S(1)}, bf16[2,272,128]{2,1,0:T(8,128)(2,1)S(1)}, u32[]{:S(2)}, u32[]{:S(2)}) collective-permute-start(bf16[2,272,128]{2,1,0:T(8,128)(2,1)S(1)} %get-tuple-element.59), channel_id=1, source_target_pairs={{0,2},{1,3},{2,0},{3,1},{4,6},{5,7},{6,4},{7,5},{8,10},{9,11},{10,... | collective-permute-start | bytes 417800 | tf_op jit(solution)/shard_map/ppermute | solution.py:349
  12.3 7.0 %collective-permute-start.19 = (bf16[2,256,128]{2,1,0:T(8,128)(2,1)S(1)}, bf16[2,256,128]{2,1,0:T(8,128)(2,1)S(1)}, u32[]{:S(2)}, u32[]{:S(2)}) collective-permute-start(bf16[2,256,128]{2,1,0:T(8,128)(2,1)S(1)} %get-tuple-element.62), channel_id=1, source_target_pairs={{0,6},{1,7},{2,4},{3,5},{4,2},{5,3},{6,0},{7,1},{8,14},{9,15},{10,... | collective-permute-start | bytes 393224 | tf_op jit(solution)/shard_map/ppermute | solution.py:349
  15.3 7.8 %collective-permute-start.3 = (bf16[4,272,128]{2,1,0:T(8,128)(2,1)S(1)}, bf16[4,272,128]{2,1,0:T(8,128)(2,1)S(1)}, u32[]{:S(2)}, u32[]{:S(2)}) collective-permute-start(bf16[4,272,128]{2,1,0:T(8,128)(2,1)S(1)} %pad_maximum_fusion.1), channel_id=1, source_target_pairs={{0,1},{1,0},{2,3},{3,2},{4,5},{5,4},{6,7},{7,6},{8,9},{9,8},{10,11... | collective-permute-start | bytes 835592 | tf_op jit(solution)/shard_map/ppermute | solution.py:349
  23.2 13.6 %collective-permute-start.4 = (bf16[8,2,128,128]{3,2,1,0:T(8,128)(2,1)S(1)}, bf16[8,2,128,128]{3,2,1,0:T(8,128)(2,1)S(1)}, u32[]{:S(2)}, u32[]{:S(2)}) collective-permute-start(bf16[8,2,128,128]{3,2,1,0:T(8,128)(2,1)S(1)} %bitcast.7), channel_id=1, source_target_pairs={{0,8},{8,0},{16,24},{24,16},{1,9},{9,1},{17,25},{25,17},{2,10},{10... | collective-permute-start | bytes 1572872 | tf_op jit(solution)/shard_map/ppermute | solution.py:362
  24.3 23.8 %collective-permute-start.21 = (bf16[8,2,128,128]{3,2,1,0:T(8,128)(2,1)S(1)}, bf16[8,2,128,128]{3,2,1,0:T(8,128)(2,1)}, u32[]{:S(2)}, u32[]{:S(2)}) collective-permute-start(bf16[8,2,128,128]{3,2,1,0:T(8,128)(2,1)S(1)} %bitcast.10), channel_id=1, source_target_pairs={{0,8},{8,0},{16,24},{24,16},{1,9},{9,1},{17,25},{25,17},{2,10},{10... | collective-permute-start | bytes 1572872 | tf_op jit(solution)/shard_map/ppermute | solution.py:362
  26.9 30.1 %collective-permute-start.7 = (bf16[8,2,128,128]{3,2,1,0:T(8,128)(2,1)S(1)}, bf16[8,2,128,128]{3,2,1,0:T(8,128)(2,1)S(1)}, u32[]{:S(2)}, u32[]{:S(2)}) collective-permute-start(bf16[8,2,128,128]{3,2,1,0:T(8,128)(2,1)S(1)} %bitcast.8), channel_id=1, source_target_pairs={{8,16},{16,8},{9,17},{17,9},{10,18},{18,10},{11,19},{19,11},{12,20... | collective-permute-start | bytes 1572872 | tf_op jit(solution)/shard_map/ppermute | solution.py:362
  36.8 25.8 %collective-permute-start.6 = (bf16[8,2,128,128]{3,2,1,0:T(8,128)(2,1)S(1)}, bf16[8,2,128,128]{3,2,1,0:T(8,128)(2,1)S(1)}, u32[]{:S(2)}, u32[]{:S(2)}) collective-permute-start(bf16[8,2,128,128]{3,2,1,0:T(8,128)(2,1)S(1)} %collective-permute-done.4.refs_2_), channel_id=1, source_target_pairs={{8,16},{16,8},{9,17},{17,9},{10,18},{18,10},{11,19},{19,11},{12,20... | collective-permute-start | bytes 1572872 | tf_op jit(solution)/shard_map/ppermute | solution.py:362
  41.0 13.4 %collective-permute-start.5 = (bf16[9,128,128]{2,1,0:T(8,128)(2,1)S(1)}, bf16[9,128,128]{2,1,0:T(8,128)(2,1)S(1)}, u32[]{:S(2)}, u32[]{:S(2)}) collective-permute-start(bf16[9,128,128]{2,1,0:T(8,128)(2,1)S(1)} %pad_maximum_fusion), channel_id=1, source_target_pairs={{0,8},{24,16},{1,9},{25,17},{2,10},{26,18},{3,11},{27,19},{4,12},{... | collective-permute-start | bytes 884744 | tf_op jit(solution)/shard_map/ppermute | solution.py:365
  42.3 25.7 %collective-permute-start.23 = (bf16[8,2,128,128]{3,2,1,0:T(8,128)(2,1)S(1)}, bf16[8,2,128,128]{3,2,1,0:T(8,128)(2,1)}, u32[]{:S(2)}, u32[]{:S(2)}) collective-permute-start(bf16[8,2,128,128]{3,2,1,0:T(8,128)(2,1)S(1)} %bitcast.11), channel_id=1, source_target_pairs={{8,16},{16,8},{9,17},{17,9},{10,18},{18,10},{11,19},{19,11},{12,20... | collective-permute-start | bytes 1572872 | tf_op jit(solution)/shard_map/ppermute | solution.py:362
  48.2 33.5 %collective-permute-start.22 = (bf16[8,2,128,128]{3,2,1,0:T(8,128)(2,1)}, bf16[8,2,128,128]{3,2,1,0:T(8,128)(2,1)}, u32[]{:S(2)}, u32[]{:S(2)}) collective-permute-start(bf16[8,2,128,128]{3,2,1,0:T(8,128)(2,1)} %collective-permute-done.21.refs_2_), channel_id=1, source_target_pairs={{8,16},{16,8},{9,17},{17,9},{10,18},{18,10},{11,19},{19,11},{12,20... | collective-permute-start | bytes 1572872 | tf_op jit(solution)/shard_map/ppermute | solution.py:362
  65.4 16.1 %collective-permute-start.8 = (bf16[8,144,128]{2,1,0:T(8,128)(2,1)S(1)}, bf16[8,144,128]{2,1,0:T(8,128)(2,1)S(1)}, u32[]{:S(2)}, u32[]{:S(2)}) collective-permute-start(bf16[8,144,128]{2,1,0:T(8,128)(2,1)S(1)} %get-tuple-element.42), channel_id=1, source_target_pairs={{8,0},{16,24},{9,1},{17,25},{10,2},{18,26},{11,3},{19,27},{12,4},{... | collective-permute-start | bytes 884744 | tf_op jit(solution)/shard_map/ppermute | solution.py:368
  66.7 9.0 %collective-permute-start.16 = (bf16[8,128,128]{2,1,0:T(8,128)(2,1)S(1)}, bf16[8,128,128]{2,1,0:T(8,128)(2,1)S(1)}, u32[]{:S(2)}, u32[]{:S(2)}) collective-permute-start(bf16[8,128,128]{2,1,0:T(8,128)(2,1)S(1)} %copy-done.1), channel_id=1, source_target_pairs={{0,8},{24,16},{1,9},{25,17},{2,10},{26,18},{3,11},{27,19},{4,12},{... | collective-permute-start | bytes 786440 | tf_op jit(solution)/shard_map/ppermute | solution.py:365
  85.3 16.6 %collective-permute-start.24 = (bf16[8,144,128]{2,1,0:T(8,128)(2,1)S(1)}, bf16[8,144,128]{2,1,0:T(8,128)(2,1)S(1)}, u32[]{:S(2)}, u32[]{:S(2)}) collective-permute-start(bf16[8,144,128]{2,1,0:T(8,128)(2,1)S(1)} %get-tuple-element.54), channel_id=1, source_target_pairs={{8,0},{16,24},{9,1},{17,25},{10,2},{18,26},{11,3},{19,27},{12,4},{... | collective-permute-start | bytes 884744 | tf_op jit(solution)/shard_map/ppermute | solution.py:368
  86.6 7.2 %collective-permute-start.14 = (bf16[1024,128]{1,0:T(8,128)(2,1)S(1)}, bf16[1024,128]{1,0:T(8,128)(2,1)S(1)}, u32[]{:S(2)}, u32[]{:S(2)}) collective-permute-start(bf16[1024,128]{1,0:T(8,128)(2,1)S(1)} %merge_0.1.refs_0_), channel_id=1, source_target_pairs={{0,6},{1,7},{2,4},{3,5},{4,2},{5,3},{6,0},{7,1},{8,14},{9,15},{10,... | collective-permute-start | bytes 786440 | tf_op jit(solution)/shard_map/ppermute | solution.py:349
  87.9 13.5 %collective-permute-start.12 = (bf16[1024,128]{1,0:T(8,128)(2,1)S(1)}, bf16[1024,128]{1,0:T(8,128)(2,1)S(1)}, u32[]{:S(2)}, u32[]{:S(2)}) collective-permute-start(bf16[1024,128]{1,0:T(8,128)(2,1)S(1)} %merge_0.1.refs_0_), channel_id=1, source_target_pairs={{0,4},{1,5},{2,6},{3,7},{4,0},{5,1},{6,2},{7,3},{8,12},{9,13},{10,... | collective-permute-start | bytes 786440 | tf_op jit(solution)/shard_map/ppermute | solution.py:349
  88.5 14.9 %collective-permute-start.10 = (bf16[1024,128]{1,0:T(8,128)(2,1)S(1)}, bf16[1024,128]{1,0:T(8,128)(2,1)S(1)}, u32[]{:S(2)}, u32[]{:S(2)}) collective-permute-start(bf16[1024,128]{1,0:T(8,128)(2,1)S(1)} %merge_0.1.refs_0_), channel_id=1, source_target_pairs={{0,2},{1,3},{2,0},{3,1},{4,6},{5,7},{6,4},{7,5},{8,10},{9,11},{10,... | collective-permute-start | bytes 786440 | tf_op jit(solution)/shard_map/ppermute | solution.py:349
  89.4 14.7 %collective-permute-start.9 = (bf16[1024,128]{1,0:T(8,128)(2,1)S(1)}, bf16[1024,128]{1,0:T(8,128)(2,1)S(1)}, u32[]{:S(2)}, u32[]{:S(2)}) collective-permute-start(bf16[1024,128]{1,0:T(8,128)(2,1)S(1)} %merge_0.1.refs_0_), channel_id=1, source_target_pairs={{0,1},{1,0},{2,3},{3,2},{4,5},{5,4},{6,7},{7,6},{8,9},{9,8},{10,11... | collective-permute-start | bytes 786440 | tf_op jit(solution)/shard_map/ppermute | solution.py:349
  93.9 11.0 %collective-permute-start.15 = (bf16[1024,128]{1,0:T(8,128)(2,1)S(1)}, bf16[1024,128]{1,0:T(8,128)(2,1)S(1)}, u32[]{:S(2)}, u32[]{:S(2)}) collective-permute-start(bf16[1024,128]{1,0:T(8,128)(2,1)S(1)} %collective-permute-done.14.refs_6_), channel_id=1, source_target_pairs={{0,1},{1,0},{2,3},{3,2},{4,5},{5,4},{6,7},{7,6},{8,9},{9,8},{10,11... | collective-permute-start | bytes 786440 | tf_op jit(solution)/shard_map/ppermute | solution.py:349
  102.2 8.9 %collective-permute-start.30 = (bf16[1024,128]{1,0:T(8,128)(2,1)S(1)}, bf16[1024,128]{1,0:T(8,128)(2,1)S(1)}, u32[]{:S(2)}, u32[]{:S(2)}) collective-permute-start(bf16[1024,128]{1,0:T(8,128)(2,1)S(1)} %merge_1.1.refs_8_), channel_id=1, source_target_pairs={{0,6},{1,7},{2,4},{3,5},{4,2},{5,3},{6,0},{7,1},{8,14},{9,15},{10,... | collective-permute-start | bytes 786440 | tf_op jit(solution)/shard_map/ppermute | solution.py:349
  103.4 13.6 %collective-permute-start.28 = (bf16[1024,128]{1,0:T(8,128)(2,1)S(1)}, bf16[1024,128]{1,0:T(8,128)(2,1)S(1)}, u32[]{:S(2)}, u32[]{:S(2)}) collective-permute-start(bf16[1024,128]{1,0:T(8,128)(2,1)S(1)} %merge_1.1.refs_8_), channel_id=1, source_target_pairs={{0,4},{1,5},{2,6},{3,7},{4,0},{5,1},{6,2},{7,3},{8,12},{9,13},{10,... | collective-permute-start | bytes 786440 | tf_op jit(solution)/shard_map/ppermute | solution.py:349
  104.1 13.4 %collective-permute-start.26 = (bf16[1024,128]{1,0:T(8,128)(2,1)S(1)}, bf16[1024,128]{1,0:T(8,128)(2,1)S(1)}, u32[]{:S(2)}, u32[]{:S(2)}) collective-permute-start(bf16[1024,128]{1,0:T(8,128)(2,1)S(1)} %merge_1.1.refs_8_), channel_id=1, source_target_pairs={{0,2},{1,3},{2,0},{3,1},{4,6},{5,7},{6,4},{7,5},{8,10},{9,11},{10,... | collective-permute-start | bytes 786440 | tf_op jit(solution)/shard_map/ppermute | solution.py:349
  104.9 12.6 %collective-permute-start.11 = (bf16[1024,128]{1,0:T(8,128)(2,1)S(1)}, bf16[1024,128]{1,0:T(8,128)(2,1)S(1)}, u32[]{:S(2)}, u32[]{:S(2)}) collective-permute-start(bf16[1024,128]{1,0:T(8,128)(2,1)S(1)} %collective-permute-done.10.refs_2_), channel_id=1, source_target_pairs={{0,1},{1,0},{2,3},{3,2},{4,5},{5,4},{6,7},{7,6},{8,9},{9,8},{10,11... | collective-permute-start | bytes 786440 | tf_op jit(solution)/shard_map/ppermute | solution.py:349
  105.7 11.8 %collective-permute-start.25 = (bf16[1024,128]{1,0:T(8,128)(2,1)S(1)}, bf16[1024,128]{1,0:T(8,128)(2,1)S(1)}, u32[]{:S(2)}, u32[]{:S(2)}) collective-permute-start(bf16[1024,128]{1,0:T(8,128)(2,1)S(1)} %merge_1.1.refs_8_), channel_id=1, source_target_pairs={{0,1},{1,0},{2,3},{3,2},{4,5},{5,4},{6,7},{7,6},{8,9},{9,8},{10,11... | collective-permute-start | bytes 786440 | tf_op jit(solution)/shard_map/ppermute | solution.py:349
  (11 other events, 91.1 us)

commit v8 on v7

--- a/solution.py
+++ b/solution.py
@@ -32,82 +32,77 @@
     return -(-rows // 16) * 16
 
 
-def pack_kernel(n_ka, heads, me_ref, mask_ref, k_all, v_all, *refs):
-    out_refs, (k_ref, v_ref, sems) = refs[:heads], refs[heads:]
-    key_blocks = k_ref.shape[0] // BLOCK
-    parts = sems.shape[1]
-    width = k_ref.shape[1] // parts
+def pack_kernel(n_ka, heads, c, marked, me_ref, *refs):
+    mask_ref, refs = (refs[0], refs[1:]) if marked else (None, refs)
+    k_all, v_all, *out_refs, v_ref, sems = refs
+    key_blocks = k_all.shape[0] // BLOCK
     copies = []
-    for i in range(parts):
-        at = slice(i * width, (i + 1) * width)
-        copies.append(pltpu.make_async_copy(k_all.at[:, at], k_ref.at[:, at], sems.at[0, i]))
-        copies.append(pltpu.make_async_copy(v_all.at[:, at], v_ref.at[:, at], sems.at[1, i]))
-    for copy in copies:
-        copy.start()
-    rows, used = mask_rows(mask_ref.shape[0]), mask_ref.shape[0]
-    column = lax.broadcasted_iota(jnp.int32, (used, HEAD_DIM), 1)
-    mask = jnp.zeros((used, HEAD_DIM), jnp.float32)
-    for j in range(mask_ref.shape[1]):
-        mask = jnp.where(column == j, mask_ref[:, j : j + 1].astype(jnp.float32), mask)
-    if rows > used:
-        mask = jnp.concatenate([mask, jnp.zeros((rows - used, HEAD_DIM), jnp.float32)])
-    mask = mask.astype(k_ref.dtype)
     for k in range(n_ka):
-        out_refs[0][k, 2 * key_blocks * BLOCK :] = mask
-    for copy in copies:
-        copy.wait()
-    for c in range(heads):
+        out_ref = out_refs[k // 2]
+        col = pl.multiple_of(((me_ref[0] ^ k) * heads + c) * HEAD_DIM, HEAD_DIM)
+        for t in range(key_blocks):
+            rows, at = pl.ds(t * BLOCK, BLOCK), pl.ds(2 * t * BLOCK, BLOCK)
+            sem = sems.at[k * key_blocks + t]
+            copies.append(
+                (
+                    pltpu.make_async_copy(k_all.at[rows, pl.ds(col, HEAD_DIM)], out_ref.at[k % 2, at], sem.at[0]),
+                    pltpu.make_async_copy(v_all.at[rows, pl.ds(col, HEAD_DIM)], v_ref.at[k, t], sem.at[1]),
+                )
+            )
+    for pair in copies:
+        for copy in pair:
+            copy.start()
+    if marked:
         for k in range(n_ka):
-            col = pl.multiple_of(((me_ref[0] ^ k) * heads + c) * HEAD_DIM, HEAD_DIM)
-            for t in range(key_blocks):
-                rows, at = slice(t * BLOCK, (t + 1) * BLOCK), 2 * t * BLOCK
-                out_refs[c][k, at : at + BLOCK] = k_ref[rows, pl.ds(col, HEAD_DIM)]
-                out_refs[c][k, at + BLOCK : at + 2 * BLOCK] = v_ref[rows, pl.ds(col, HEAD_DIM)].T
-
-
-def mask_rows(rows):
-    return -(-rows // 16) * 16
-
-
-def pack(me, keys, values, mask, n_ka, heads):
-    sizes = [2 * keys.shape[0] + (mask_rows(mask.shape[0]) if c == 0 else 0) for c in range(heads)]
-    parts = 4
+            out_refs[k // 2][k % 2, 2 * key_blocks * BLOCK :] = mask_ref[...]
+    for k in range(n_ka):
+        for t in range(key_blocks):
+            copies[k * key_blocks + t][1].wait()
+            out_refs[k // 2][k % 2, (2 * t + 1) * BLOCK : (2 * t + 2) * BLOCK] = v_ref[k, t].T
+    for pair in copies:
+        pair[0].wait()
+
+
+def pack(me, keys, values, mask, n_ka, heads, c):
+    key_blocks = keys.shape[0] // BLOCK
+    size = 2 * keys.shape[0] + (0 if mask is None else mask.shape[0])
+    masks = () if mask is None else (mask,)
     return pl.pallas_call(
-        functools.partial(pack_kernel, n_ka, heads),
-        out_shape=[jax.ShapeDtypeStruct((n_ka, size, HEAD_DIM), keys.dtype) for size in sizes],
-        in_specs=[SMEM, VMEM, ANY, ANY],
-        out_specs=[VMEM] * heads,
+        functools.partial(pack_kernel, n_ka, heads, c, bool(masks)),
+        out_shape=[jax.ShapeDtypeStruct((2, size, HEAD_DIM), keys.dtype)] * (n_ka // 2),
+        in_specs=[SMEM] + [VMEM] * len(masks) + [ANY, ANY],
+        out_specs=[VMEM] * (n_ka // 2),
         scratch_shapes=[
-            pltpu.VMEM(keys.shape, keys.dtype),
-            pltpu.VMEM(values.shape, values.dtype),
-            pltpu.SemaphoreType.DMA((2, parts)),
+            pltpu.VMEM((n_ka, key_blocks, BLOCK, HEAD_DIM), values.dtype),
+            pltpu.SemaphoreType.DMA((n_ka * key_blocks, 2)),
         ],
         compiler_params=params(MOST_VMEM_BYTES),
-        name="pack",
-    )(me, mask, keys, values)
-
-
-def turn_kernel(heads, me_ref, q_all, *refs):
-    out_refs, (q_ref, sem) = refs[:heads], refs[heads:]
+        cost_estimate=pl.CostEstimate(flops=0, bytes_accessed=keys.size, transcendentals=0),
+        name=f"pack_{c}",
+    )(me, *masks, keys, values)
+
+
+def turn_kernel(heads, me_ref, q_all, out_ref, q_ref, sem):
     column = pl.multiple_of(me_ref[0] * heads * HEAD_DIM, HEAD_DIM)
     copy = pltpu.make_async_copy(q_all.at[:, pl.ds(column, heads * HEAD_DIM)], q_ref, sem)
     copy.start()
     copy.wait()
+    rows = out_ref.shape[1]
     for c in range(heads):
-        for r in range(out_refs[c].shape[0]):
-            out_refs[c][r] = q_ref[r * BLOCK : (r + 1) * BLOCK, c * HEAD_DIM : (c + 1) * HEAD_DIM].T
+        for r in range(rows):
+            out_ref[c, r] = q_ref[r * BLOCK : (r + 1) * BLOCK, c * HEAD_DIM : (c + 1) * HEAD_DIM].T
 
 
 def turn(me, queries, heads):
     tokens = queries.shape[0]
-    shape = jax.ShapeDtypeStruct((tokens // BLOCK, HEAD_DIM, BLOCK), queries.dtype)
     return pl.pallas_call(
         functools.partial(turn_kernel, heads),
-        out_shape=[shape] * heads,
+        out_shape=jax.ShapeDtypeStruct((heads, tokens // BLOCK, HEAD_DIM, BLOCK), queries.dtype),
         in_specs=[SMEM, ANY],
-        out_specs=[VMEM] * heads,
+        out_specs=VMEM,
         scratch_shapes=[pltpu.VMEM((tokens, heads * HEAD_DIM), queries.dtype), pltpu.SemaphoreType.DMA],
         compiler_params=params(MOST_VMEM_BYTES),
+        cost_estimate=pl.CostEstimate(flops=0, bytes_accessed=queries.size // HEADS, transcendentals=0),
         name="turn",
     )(me, queries)
 
@@ -139,7 +134,7 @@
                             block = (s * n_slots + slot) * key_blocks + t
                             live[2 * base + count] = ((r + guest * rows) << ROW_SHIFT) + block
                             column = j * key_blocks + t
-                            count += inside * mask_ref[(slot * rows + r) * (n_pb * key_blocks) + column]
+                            count += inside * mask_ref[(slot * n_pb * key_blocks + column) * rows + r]
                 live[2 * base + count] = -1
                 return base + ((count + 1) >> 1)
 
@@ -173,7 +168,7 @@
     return found
 
 
-def attend_kernel(n_src, entry, first, mode, guests, count_ref, live_ref, q_own, *refs):
+def attend_kernel(c, n_src, entry, first, mode, guests, count_ref, live_ref, q_own, *refs):
     n_kv = n_src
     guest_ref, refs = (refs[0], refs[1:]) if guests else (None, refs)
     kv_refs, refs = refs[:n_kv], refs[n_kv:]
@@ -186,14 +181,14 @@
         (*state, kv, q_ref, sems) = refs
     m_ref, l_ref, acc_ref = state
     blocks = kv.shape[0] // n_src
-    rows = q_own.shape[0]
+    rows = q_own.shape[1]
     copies = [
         pltpu.make_async_copy(kv_refs[s], kv.at[pl.ds(s * blocks, blocks)], sems.at[s]) for s in range(n_src)
     ]
     copies += [pltpu.make_async_copy(a, b, sems.at[n_src + i]) for i, (a, b) in enumerate(zip(state_in, state))]
-    copies.append(pltpu.make_async_copy(q_own, q_ref.at[pl.ds(0, rows)], sems.at[n_src + 3]))
+    copies.append(pltpu.make_async_copy(q_own.at[c], q_ref.at[pl.ds(0, rows)], sems.at[n_src + 3]))
     if guests:
-        copies.append(pltpu.make_async_copy(guest_ref.at[pl.ds(0, rows)], q_ref.at[pl.ds(rows, rows)], sems.at[n_src + 4]))
+        copies.append(pltpu.make_async_copy(guest_ref.at[c], q_ref.at[pl.ds(rows, rows)], sems.at[n_src + 4]))
     for copy in copies:
         copy.start()
     if first:
@@ -247,9 +242,9 @@
             part_ref[r, HEAD_DIM:] = jnp.concatenate(words).astype(part_ref.dtype)
 
 
-def attend(listed, q, guest, sources, state, mode, sets, name):
+def attend(c, listed, q, guest, sources, state, mode, sets, name):
     counts, entry, live = listed
-    rows, dtype = q.shape[0], q.dtype
+    rows, dtype = q.shape[1], q.dtype
     first = state is None
     state = () if first else tuple(state)
     stat = (sets * rows, 1, BLOCK)
@@ -269,13 +264,13 @@
         scratch += [pltpu.VMEM(shape, jnp.float32) for shape in shapes]
     scratch.append(pltpu.SemaphoreType.DMA((n_src + 5,)))
     return pl.pallas_call(
-        functools.partial(attend_kernel, n_src, entry, first, mode, bool(guests)),
+        functools.partial(attend_kernel, c, n_src, entry, first, mode, bool(guests)),
         out_shape=out_shape,
         in_specs=[SMEM, SMEM, ANY] + [ANY] * (len(guests) + n_src + len(state)),
         out_specs=[VMEM] * len(out_shape),
         scratch_shapes=scratch,
         compiler_params=params(),
-        cost_estimate=pl.CostEstimate(flops=0, bytes_accessed=q.size, transcendentals=0),
+        cost_estimate=pl.CostEstimate(flops=0, bytes_accessed=HEAD_DIM * BLOCK, transcendentals=0),
         name=name,
     )(counts, live, q, *guests, *sources, *state)
 
@@ -368,9 +363,9 @@
         return lax.ppermute(x, "pb", [(1, 0), (n_pb - 2, n_pb - 1)])
 
     def sort(x):
-        mixed = [x[:2]] + [swap(x[k : k + 2], k) for k in range(2, n_ka, 2)]
-        theirs = swap(jnp.stack([x[1] for x in mixed]), 1)
-        return jnp.concatenate([jnp.stack([x[0] for x in mixed]), theirs]), mixed[-1]
+        mixed = [y if i == 0 else swap(y, 2 * i) for i, y in enumerate(x)]
+        theirs = swap(jnp.stack([y[1] for y in mixed]), 1)
+        return jnp.concatenate([jnp.stack([y[0] for y in mixed]), theirs]), theirs
 
     def blocks(x):
         return x[:, : 2 * shard].reshape(n_ka * key_blocks, 2, BLOCK, HEAD_DIM)
@@ -379,16 +374,20 @@
         return arrays if done is None else lax.optimization_barrier((arrays, done))[0]
 
     def flags(x):
-        return x[:, :rows, : block_mask.shape[1]].astype(jnp.int32).reshape(-1)
-
-    packed = pack(me1, keys, values, block_mask, n_ka, heads)
+        return x[:, : block_mask.shape[1], :rows].astype(jnp.int32).reshape(-1)
+
+    columns = block_mask.shape[1]
+    mask = jnp.pad(block_mask.T.astype(keys.dtype), ((0, mask_rows(columns) - columns), (0, HEAD_DIM - rows)))
     owns, moved = [], None
     for c in range(heads):
-        own, moved = sort(after(packed[c], moved))
+        packed = pack(after(me1, q) if c else me1, keys, values, None if c else mask, n_ka, heads, c)
+        if c == 0:
+            q = turn(after(me1, packed), queries, heads)
+            guest = inward(q) if relay else None
+        own, moved = sort(after(packed, (moved, guest) if c else None))
         owns.append(blocks(own))
         if c == 0:
             marks = own[:, 2 * shard :]
-    q = turn(me1, queries, heads)
 
     steps = [((0, False),)]
     for step in range(1, n_pb):
@@ -398,39 +397,43 @@
         elif found:
             steps.append(found)
     last = len(steps) - 1
-    over = [[exchange(own, odd, 1) for odd in (0, 1)] for own in owns]
     masks = [flags(marks)]
-    guest = [None] * heads
+    guest_marks = inward(marks) if relay else None
     if relay:
-        first = jnp.concatenate([q[0], marks.reshape(-1, HEAD_DIM, BLOCK)])
-        first = inward(after(first, over[0][0]))
-        masks.append(flags(first[rows:].reshape(marks.shape)))
-        guest = [first] + [inward(after(x, first)) for x in q[1:]]
+        masks.append(flags(guest_marks))
     lists = plan(pb1, masks, steps, n_pb, n_ka, key_blocks, rows, relay)
+    over = []
+    for c in range(heads):
+        own = after(owns[c], (over[0][1], guest_marks) if c else None)
+        over.append([exchange(own, odd, 1) for odd in (0, 1)])
     state = [None] * heads
 
     def run(c, step, sources):
         kind = "keep" if step < last else "send" if relay else "last"
         sources = [x for x in sources if x is not None]
         name = f"attend_{c}_{step}"
-        return attend(lists[step], q[c], guest[c], sources, state[c], kind, 2 if relay else 1, name)
+        return attend(c, lists[step], q, guest, sources, state[c], kind, 2 if relay else 1, name)
 
     for step in range(last):
         for c in range(heads):
             sources = ([owns[c]] if step == 0 else []) + over[c]
-            over[c] = [exchange(over[c][1], 0, step + 2), exchange(over[c][0], 1, step + 2)]
+            even, odd = over[c]
+            if even is not None and odd is not None:
+                even, odd = lax.optimization_barrier((even, odd))
+            over[c] = [exchange(odd, 0, step + 2), exchange(even, 1, step + 2)]
             state[c] = run(c, step, sources)
 
     pieces = []
-    out = None
+    sent = far = None
     for c in range(heads):
-        found = run(c, last, ([] if last else [owns[c]]) + after(over[c], out))
+        found = run(c, last, ([] if last else [owns[c]]) + after(over[c], sent))
         if relay:
             outer = ((pb == 0) | (pb == n_pb - 1)).astype(jnp.int32)[None]
-            out = merge(outer, found[:3], outward(found[3]), f"merge_{c}")
+            out = merge(outer, found[:3], outward(after(found[3], far)), f"merge_{c}")
         else:
             out = found[0]
         mine = [out] + [swap(out, k) for k in range(2, n_ka, 2)]
+        sent, far = mine[: n_ka // 4 + 1], mine[n_ka // 4 + 1 :]
         others = [swap(x, 1) for x in mine]
         pieces += [x for two in zip(mine, others) for x in two]
     return place(me1, pieces, n_ka, heads)

time: 122 us -> 111 us (0.910)
  the two profiles are of different devices: /device:TPU:9 before, /device:TPU:0 now
where the time goes in v8:
time: 111 us; the launch traced here: 110 us
  waiting for transfers between devices  41.9 us (38%)
  starting transfers between devices  41.1 us (37%)
  Pallas kernels  23.4 us (21%)
  local copies, waits for them, and re-layouts  1.9 us (2%)
  other arithmetic  1.49 us (1%)
    ppermute x22, waiting for transfers between devices, swap(): return lax.ppermute(x, 'ka', [(i, i ^ k) for i in range(n_ka)])  19.9 us
    ppermute x2, waiting for transfers between devices, outward(): return lax.ppermute(x, 'pb', [(1, 0), (n_pb - 2, n_pb - 1)])  17.3 us
    ppermute x22, starting transfers between devices, swap(): return lax.ppermute(x, 'ka', [(i, i ^ k) for i in range(n_ka)])  16.9 us
    ppermute x6, starting transfers between devices, exchange(): return lax.ppermute(x, 'pb', found) if found else None  13.2 us
    pallas_call x4, Pallas kernels, attend(): pl.pallas_call(functools.partial(attend_kernel, c, n_src, entry, first, m...  11.1 us
    ppermute x2, starting transfers between devices, inward(): return lax.ppermute(x, 'pb', [(0, 1), (n_pb - 1, n_pb - 2)])  8.38 us
    pallas_call x2, Pallas kernels, pack(): pl.pallas_call(functools.partial(pack_kernel, n_ka, heads, c, bool(masks)...  5.3 us
    ppermute x2, waiting for transfers between devices, inward(): return lax.ppermute(x, 'pb', [(0, 1), (n_pb - 1, n_pb - 2)])  3.99 us
  transfers between devices with their start and end apart: 32, of which 15 were waited for; matrix products, arithmetic and copies ran while one was open for 2% of the time, Pallas kernels for 17%

profile of v8, /device:TPU:0, one launch (start us, length us, event | category | flops | bytes accessed | tf_op | source)
XLA Modules:
  0.0 110.1 jit_solution(12957568868172649404)
XLA Ops:
  1.3 3.0 %pack_0.1 = (bf16[2,272,128]{2,1,0:T(8,128)(2,1)}, bf16[2,272,128]{2,1,0:T(8,128)(2,1)}, bf16[2,272,128]{2,1,0:T(8,128)(2,1)}, bf16[2,272,128]{2,1,0:T(8,128)(2,1)}) custom-call(s32[1]{0:T(128)} %bitcast.me_ref, bf16[16,128]{1,0:T(8,128)(2,1)} %pad.4.refs_0_, bf16[128,2048]{1,0:T(8,128)(2,1)} %refs_0_.1, bf16[128,2048]{1,0:T(8,128)(2,1)} %refs_1_.3), custom_call_target="tpu_custom_call" | custom-call | bytes 262144 | tf_op jit(solution)/shard_map/pack_0/pallas_call | solution.py:70
  4.3 3.0 %collective-permute-start = (bf16[2,272,128]{2,1,0:T(8,128)(2,1)}, bf16[2,272,128]{2,1,0:T(8,128)(2,1)S(1)}, u32[]{:S(2)}, u32[]{:S(2)}) collective-permute-start(bf16[2,272,128]{2,1,0:T(8,128)(2,1)} %get-tuple-element.42), channel_id=1, source_target_pairs={{0,2},{1,3},{2,0},{3,1},{4,6},{5,7},{6,4},{7,5},{8,10},{9,11},{10,... | collective-permute-start | bytes 417800 | tf_op jit(solution)/shard_map/ppermute | solution.py:344
  8.8 2.0 %turn.1.q_own = bf16[2,8,128,128]{3,2,1,0:T(8,128)(2,1)} custom-call(s32[1]{0:T(128)} %bitcast.me_ref, bf16[1024,2048]{1,0:T(8,128)(2,1)} %q_all.1), custom_call_target="tpu_custom_call" | custom-call | bytes 131072 | tf_op jit(solution)/shard_map/turn/pallas_call | solution.py:98
  10.9 4.1 %collective-permute-start.5 = (bf16[2,8,128,128]{3,2,1,0:T(8,128)(2,1)}, bf16[2,8,128,128]{3,2,1,0:T(8,128)(2,1)S(1)}, u32[]{:S(2)}, u32[]{:S(2)}) collective-permute-start(bf16[2,8,128,128]{3,2,1,0:T(8,128)(2,1)} %turn.1.q_own), channel_id=1, source_target_pairs={{0,8},{24,16},{1,9},{25,17},{2,10},{26,18},{3,11},{27,19},{4,12},{... | collective-permute-start | bytes 1572872 | tf_op jit(solution)/shard_map/ppermute | solution.py:360
  15.8 2.3 %pack_1.1 = (bf16[2,256,128]{2,1,0:T(8,128)(2,1)}, bf16[2,256,128]{2,1,0:T(8,128)(2,1)}, bf16[2,256,128]{2,1,0:T(8,128)(2,1)}, bf16[2,256,128]{2,1,0:T(8,128)(2,1)}) custom-call(s32[1]{0:T(128)} %bitcast.me_ref, bf16[128,2048]{1,0:T(8,128)(2,1)} %refs_0_.1, bf16[128,2048]{1,0:T(8,128)(2,1)} %refs_1_.3), custom_call_target="tpu_custom_call" | custom-call | bytes 262144 | tf_op jit(solution)/shard_map/pack_1/pallas_call | solution.py:70
  18.9 4.4 %collective-permute-start.6 = (bf16[8,2,128,128]{3,2,1,0:T(8,128)(2,1)S(1)}, bf16[8,2,128,128]{3,2,1,0:T(8,128)(2,1)S(1)}, u32[]{:S(2)}, u32[]{:S(2)}) collective-permute-start(bf16[8,2,128,128]{3,2,1,0:T(8,128)(2,1)S(1)} %bitcast.8), channel_id=1, source_target_pairs={{0,8},{8,0},{16,24},{24,16},{1,9},{9,1},{17,25},{25,17},{2,10},{10... | collective-permute-start | bytes 1572872 | tf_op jit(solution)/shard_map/ppermute | solution.py:357
  23.4 4.0 %collective-permute-done.5.refs_0_ = bf16[2,8,128,128]{3,2,1,0:T(8,128)(2,1)S(1)} collective-permute-done((bf16[2,8,128,128]{3,2,1,0:T(8,128)(2,1)}, bf16[2,8,128,128]{3,2,1,0:T(8,128)(2,1)S(1)}, u32[]{:S(2)}, u32[]{:S(2)}) %collective-permute-start.5) | collective-permute-done | bytes 524320 | tf_op jit(solution)/shard_map/ppermute | solution.py:360
  27.3 1.8 %collective-permute-start.17 = (bf16[2,256,128]{2,1,0:T(8,128)(2,1)}, bf16[2,256,128]{2,1,0:T(8,128)(2,1)S(1)}, u32[]{:S(2)}, u32[]{:S(2)}) collective-permute-start(bf16[2,256,128]{2,1,0:T(8,128)(2,1)} %get-tuple-element.63), channel_id=1, source_target_pairs={{0,2},{1,3},{2,0},{3,1},{4,6},{5,7},{6,4},{7,5},{8,10},{9,11},{10,... | collective-permute-start | bytes 393224 | tf_op jit(solution)/shard_map/ppermute | solution.py:344
  32.5 1.8 %collective-permute-done.18 = bf16[2,256,128]{2,1,0:T(8,128)(2,1)S(1)} collective-permute-done((bf16[2,256,128]{2,1,0:T(8,128)(2,1)}, bf16[2,256,128]{2,1,0:T(8,128)(2,1)S(1)}, u32[]{:S(2)}, u32[]{:S(2)}) %collective-permute-start.18) | collective-permute-done | bytes 131104 | tf_op jit(solution)/shard_map/ppermute | solution.py:344
  34.3 2.4 %collective-permute-done.19 = bf16[2,256,128]{2,1,0:T(8,128)(2,1)S(1)} collective-permute-done((bf16[2,256,128]{2,1,0:T(8,128)(2,1)}, bf16[2,256,128]{2,1,0:T(8,128)(2,1)S(1)}, u32[]{:S(2)}, u32[]{:S(2)}) %collective-permute-start.19) | collective-permute-done | bytes 131104 | tf_op jit(solution)/shard_map/ppermute | solution.py:344
  36.9 4.3 %collective-permute-start.4 = (bf16[8,16,128]{2,1,0:T(8,128)(2,1)S(1)}, bf16[8,16,128]{2,1,0:T(8,128)(2,1)S(1)}, u32[]{:S(2)}, u32[]{:S(2)}) collective-permute-start(bf16[8,16,128]{2,1,0:T(8,128)(2,1)S(1)} %slice.88), channel_id=1, source_target_pairs={{0,8},{24,16},{1,9},{25,17},{2,10},{26,18},{3,11},{27,19},{4,12},{... | collective-permute-start | bytes 98312 | tf_op jit(solution)/shard_map/ppermute | solution.py:360
  44.2 4.4 %collective-permute-start.21 = (bf16[8,2,128,128]{3,2,1,0:T(8,128)(2,1)S(1)}, bf16[8,2,128,128]{3,2,1,0:T(8,128)(2,1)}, u32[]{:S(2)}, u32[]{:S(2)}) collective-permute-start(bf16[8,2,128,128]{3,2,1,0:T(8,128)(2,1)S(1)} %bitcast.11), channel_id=1, source_target_pairs={{0,8},{8,0},{16,24},{24,16},{1,9},{9,1},{17,25},{25,17},{2,10},{10... | collective-permute-start | bytes 1572872 | tf_op jit(solution)/shard_map/ppermute | solution.py:357
  49.6 2.4 %plan.1 = (s32[2]{0:T(128)S(1)}, s32[432]{0:T(512)S(1)}, s32[176]{0:T(256)S(1)}) custom-call(s32[1]{0:T(128)} %bitcast.2.pb_ref, s32[256]{0:T(256)S(1)} %reshape.24.refs_0_, s32[256]{0:T(256)S(1)} %reshape.26.refs_1_), custom_call_target="tpu_custom_call" | custom-call | tf_op jit(solution)/shard_map/plan/pallas_call | solution.py:152
  51.9 3.4 %attend_0_0.1 = (f32[16,1,128]{2,1,0:T(1,128)S(1)}, f32[16,1,128]{2,1,0:T(1,128)S(1)}, f32[16,128,128]{2,1,0:T(8,128)S(1)}) custom-call(s32[2]{0:T(128)S(1)} %get-tuple-element.45.count_ref, s32[432]{0:T(512)S(1)} %get-tuple-element.49.live_ref, bf16[2,8,128,128]{3,2,1,0:T(8,128)(2,1)S(1)} %copy-done, ...), custom_call_target="tpu_custom_call" | custom-call | bytes 16384 | tf_op jit(solution)/shard_map/attend_0_0/pallas_call | solution.py:266
  55.4 2.4 %attend_0_1.1 = (f32[16,1,128]{2,1,0:T(1,128)S(1)}, f32[16,1,128]{2,1,0:T(1,128)S(1)}, f32[16,128,128]{2,1,0:T(8,128)S(1)}, bf16[8,144,128]{2,1,0:T(8,128)(2,1)}) custom-call(s32[2]{0:T(128)S(1)} %get-tuple-element.45.count_ref, s32[176]{0:T(256)S(1)} %get-tuple-element.46.live_ref, bf16[2,8,128,128]{3,2,1,0:T(8,128)(2,1)S(1)} %copy-done, ...), custom_call_target="tpu_custom_call" | custom-call | bytes 16384 | tf_op jit(solution)/shard_map/attend_0_1/pallas_call | solution.py:266
  60.6 9.0 %collective-permute-done.9.part_ref = bf16[8,144,128]{2,1,0:T(8,128)(2,1)S(1)} collective-permute-done((bf16[8,144,128]{2,1,0:T(8,128)(2,1)}, bf16[8,144,128]{2,1,0:T(8,128)(2,1)S(1)}, u32[]{:S(2)}, u32[]{:S(2)}) %collective-permute-start.9) | collective-permute-done | bytes 294944 | tf_op jit(solution)/shard_map/ppermute | solution.py:363
  70.4 3.0 %collective-permute-start.15 = (bf16[1024,128]{1,0:T(8,128)(2,1)S(1)}, bf16[1024,128]{1,0:T(8,128)(2,1)S(1)}, u32[]{:S(2)}, u32[]{:S(2)}) collective-permute-start(bf16[1024,128]{1,0:T(8,128)(2,1)S(1)} %merge_0.1.refs_0_), channel_id=1, source_target_pairs={{0,6},{1,7},{2,4},{3,5},{4,2},{5,3},{6,0},{7,1},{8,14},{9,15},{10,... | collective-permute-start | bytes 786440 | tf_op jit(solution)/shard_map/ppermute | solution.py:344
  73.3 4.4 %attend_1_0.1 = (f32[16,1,128]{2,1,0:T(1,128)S(1)}, f32[16,1,128]{2,1,0:T(1,128)S(1)}, f32[16,128,128]{2,1,0:T(8,128)S(1)}) custom-call(s32[2]{0:T(128)S(1)} %get-tuple-element.45.count_ref, s32[432]{0:T(512)S(1)} %get-tuple-element.49.live_ref, bf16[2,8,128,128]{3,2,1,0:T(8,128)(2,1)S(1)} %copy-done, ...), custom_call_target="tpu_custom_call" | custom-call | bytes 16384 | tf_op jit(solution)/shard_map/attend_1_0/pallas_call | solution.py:266
  80.5 3.0 %collective-permute-done.15.refs_6_ = bf16[1024,128]{1,0:T(8,128)(2,1)S(1)} collective-permute-done((bf16[1024,128]{1,0:T(8,128)(2,1)S(1)}, bf16[1024,128]{1,0:T(8,128)(2,1)S(1)}, u32[]{:S(2)}, u32[]{:S(2)}) %collective-permute-start.15) | collective-permute-done | bytes 262176 | tf_op jit(solution)/shard_map/ppermute | solution.py:344
  85.5 8.3 %collective-permute-done.24.part_ref = bf16[8,144,128]{2,1,0:T(8,128)(2,1)S(1)} collective-permute-done((bf16[8,144,128]{2,1,0:T(8,128)(2,1)S(1)}, bf16[8,144,128]{2,1,0:T(8,128)(2,1)S(1)}, u32[]{:S(2)}, u32[]{:S(2)}) %collective-permute-start.24) | collective-permute-done | bytes 294944 | tf_op jit(solution)/shard_map/ppermute | solution.py:363
  94.1 2.0 %collective-permute-start.28 = (bf16[1024,128]{1,0:T(8,128)(2,1)S(1)}, bf16[1024,128]{1,0:T(8,128)(2,1)S(1)}, u32[]{:S(2)}, u32[]{:S(2)}) collective-permute-start(bf16[1024,128]{1,0:T(8,128)(2,1)S(1)} %merge_1.1.refs_8_), channel_id=1, source_target_pairs={{0,4},{1,5},{2,6},{3,7},{4,0},{5,1},{6,2},{7,3},{8,12},{9,13},{10,... | collective-permute-start | bytes 786440 | tf_op jit(solution)/shard_map/ppermute | solution.py:344
  98.0 6.1 %collective-permute-done.30.refs_14_ = bf16[1024,128]{1,0:T(8,128)(2,1)S(1)} collective-permute-done((bf16[1024,128]{1,0:T(8,128)(2,1)S(1)}, bf16[1024,128]{1,0:T(8,128)(2,1)S(1)}, u32[]{:S(2)}, u32[]{:S(2)}) %collective-permute-start.30) | collective-permute-done | bytes 262176 | tf_op jit(solution)/shard_map/ppermute | solution.py:344
  104.2 1.9 %collective-permute-done.28.refs_12_ = bf16[1024,128]{1,0:T(8,128)(2,1)S(1)} collective-permute-done((bf16[1024,128]{1,0:T(8,128)(2,1)S(1)}, bf16[1024,128]{1,0:T(8,128)(2,1)S(1)}, u32[]{:S(2)}, u32[]{:S(2)}) %collective-permute-start.28) | collective-permute-done | bytes 262176 | tf_op jit(solution)/shard_map/ppermute | solution.py:344
  108.0 2.1 %place.1 = bf16[1024,2048]{1,0:T(8,128)(2,1)} custom-call(s32[1]{0:T(128)} %bitcast.me_ref, bf16[1024,128]{1,0:T(8,128)(2,1)S(1)} %merge_0.1.refs_0_, bf16[1024,128]{1,0:T(8,128)(2,1)S(1)} %collective-permute-done.10.refs_1_, bf16[1024,128]{1,0:T(8,128)(2,1)S(1)} %collective-permute-done.11.refs_2_, bf16[1024,128]{1,0:T(8,128)(2,1)S(1)} %collective-permute-done.12.refs_3_, ...), custom_call_target="tpu_custom_call" | custom-call | tf_op jit(solution)/shard_map/place/pallas_call | solution.py:323
  (77 shorter events, 24.1 us)
Async XLA Ops:
  4.3 10.7 %collective-permute-start = (bf16[2,272,128]{2,1,0:T(8,128)(2,1)}, bf16[2,272,128]{2,1,0:T(8,128)(2,1)S(1)}, u32[]{:S(2)}, u32[]{:S(2)}) collective-permute-start(bf16[2,272,128]{2,1,0:T(8,128)(2,1)} %get-tuple-element.42), channel_id=1, source_target_pairs={{0,2},{1,3},{2,0},{3,1},{4,6},{5,7},{6,4},{7,5},{8,10},{9,11},{10,... | collective-permute-start | bytes 417800 | tf_op jit(solution)/shard_map/ppermute | solution.py:344
  7.3 8.3 %collective-permute-start.1 = (bf16[2,272,128]{2,1,0:T(8,128)(2,1)}, bf16[2,272,128]{2,1,0:T(8,128)(2,1)S(1)}, u32[]{:S(2)}, u32[]{:S(2)}) collective-permute-start(bf16[2,272,128]{2,1,0:T(8,128)(2,1)} %get-tuple-element.43), channel_id=1, source_target_pairs={{0,4},{1,5},{2,6},{3,7},{4,0},{5,1},{6,2},{7,3},{8,12},{9,13},{10,... | collective-permute-start | bytes 417800 | tf_op jit(solution)/shard_map/ppermute | solution.py:344
  8.8 6.8 %collective-permute-start.2 = (bf16[2,272,128]{2,1,0:T(8,128)(2,1)}, bf16[2,272,128]{2,1,0:T(8,128)(2,1)S(1)}, u32[]{:S(2)}, u32[]{:S(2)}) collective-permute-start(bf16[2,272,128]{2,1,0:T(8,128)(2,1)} %get-tuple-element.44), channel_id=1, source_target_pairs={{0,6},{1,7},{2,4},{3,5},{4,2},{5,3},{6,0},{7,1},{8,14},{9,15},{10,... | collective-permute-start | bytes 417800 | tf_op jit(solution)/shard_map/ppermute | solution.py:344
  10.9 16.4 %collective-permute-start.5 = (bf16[2,8,128,128]{3,2,1,0:T(8,128)(2,1)}, bf16[2,8,128,128]{3,2,1,0:T(8,128)(2,1)S(1)}, u32[]{:S(2)}, u32[]{:S(2)}) collective-permute-start(bf16[2,8,128,128]{3,2,1,0:T(8,128)(2,1)} %turn.1.q_own), channel_id=1, source_target_pairs={{0,8},{24,16},{1,9},{25,17},{2,10},{26,18},{3,11},{27,19},{4,12},{... | collective-permute-start | bytes 1572872 | tf_op jit(solution)/shard_map/ppermute | solution.py:360
  18.2 22.9 %collective-permute-start.7 = (bf16[8,2,128,128]{3,2,1,0:T(8,128)(2,1)S(1)}, bf16[8,2,128,128]{3,2,1,0:T(8,128)(2,1)S(1)}, u32[]{:S(2)}, u32[]{:S(2)}) collective-permute-start(bf16[8,2,128,128]{3,2,1,0:T(8,128)(2,1)S(1)} %bitcast.7), channel_id=1, source_target_pairs={{8,16},{16,8},{9,17},{17,9},{10,18},{18,10},{11,19},{19,11},{12,20... | collective-permute-start | bytes 1572872 | tf_op jit(solution)/shard_map/ppermute | solution.py:357
  18.9 22.2 %collective-permute-start.6 = (bf16[8,2,128,128]{3,2,1,0:T(8,128)(2,1)S(1)}, bf16[8,2,128,128]{3,2,1,0:T(8,128)(2,1)S(1)}, u32[]{:S(2)}, u32[]{:S(2)}) collective-permute-start(bf16[8,2,128,128]{3,2,1,0:T(8,128)(2,1)S(1)} %bitcast.8), channel_id=1, source_target_pairs={{0,8},{8,0},{16,24},{24,16},{1,9},{9,1},{17,25},{25,17},{2,10},{10... | collective-permute-start | bytes 1572872 | tf_op jit(solution)/shard_map/ppermute | solution.py:357
  30.7 6.1 %collective-permute-start.19 = (bf16[2,256,128]{2,1,0:T(8,128)(2,1)}, bf16[2,256,128]{2,1,0:T(8,128)(2,1)S(1)}, u32[]{:S(2)}, u32[]{:S(2)}) collective-permute-start(bf16[2,256,128]{2,1,0:T(8,128)(2,1)} %get-tuple-element.65), channel_id=1, source_target_pairs={{0,6},{1,7},{2,4},{3,5},{4,2},{5,3},{6,0},{7,1},{8,14},{9,15},{10,... | collective-permute-start | bytes 393224 | tf_op jit(solution)/shard_map/ppermute | solution.py:344
  41.2 14.2 %collective-permute-start.8 = (bf16[8,2,128,128]{3,2,1,0:T(8,128)(2,1)S(1)}, bf16[8,2,128,128]{3,2,1,0:T(8,128)(2,1)}, u32[]{:S(2)}, u32[]{:S(2)}) collective-permute-start(bf16[8,2,128,128]{3,2,1,0:T(8,128)(2,1)S(1)} %collective-permute-done.6.refs_2_), channel_id=1, source_target_pairs={{8,16},{16,8},{9,17},{17,9},{10,18},{18,10},{11,19},{19,11},{12,20... | collective-permute-start | bytes 1572872 | tf_op jit(solution)/shard_map/ppermute | solution.py:357
  42.8 16.4 %collective-permute-start.22 = (bf16[8,2,128,128]{3,2,1,0:T(8,128)(2,1)S(1)}, bf16[8,2,128,128]{3,2,1,0:T(8,128)(2,1)}, u32[]{:S(2)}, u32[]{:S(2)}) collective-permute-start(bf16[8,2,128,128]{3,2,1,0:T(8,128)(2,1)S(1)} %bitcast.10), channel_id=1, source_target_pairs={{8,16},{16,8},{9,17},{17,9},{10,18},{18,10},{11,19},{19,11},{12,20... | collective-permute-start | bytes 1572872 | tf_op jit(solution)/shard_map/ppermute | solution.py:357
  44.2 15.6 %collective-permute-start.21 = (bf16[8,2,128,128]{3,2,1,0:T(8,128)(2,1)S(1)}, bf16[8,2,128,128]{3,2,1,0:T(8,128)(2,1)}, u32[]{:S(2)}, u32[]{:S(2)}) collective-permute-start(bf16[8,2,128,128]{3,2,1,0:T(8,128)(2,1)S(1)} %bitcast.11), channel_id=1, source_target_pairs={{0,8},{8,0},{16,24},{24,16},{1,9},{9,1},{17,25},{25,17},{2,10},{10... | collective-permute-start | bytes 1572872 | tf_op jit(solution)/shard_map/ppermute | solution.py:357
  57.8 11.8 %collective-permute-start.9 = (bf16[8,144,128]{2,1,0:T(8,128)(2,1)}, bf16[8,144,128]{2,1,0:T(8,128)(2,1)S(1)}, u32[]{:S(2)}, u32[]{:S(2)}) collective-permute-start(bf16[8,144,128]{2,1,0:T(8,128)(2,1)} %get-tuple-element.56), channel_id=1, source_target_pairs={{8,0},{16,24},{9,1},{17,25},{10,2},{18,26},{11,3},{19,27},{12,4},{... | collective-permute-start | bytes 884744 | tf_op jit(solution)/shard_map/ppermute | solution.py:363
  59.9 17.9 %collective-permute-start.23 = (bf16[8,2,128,128]{3,2,1,0:T(8,128)(2,1)}, bf16[8,2,128,128]{3,2,1,0:T(8,128)(2,1)S(1)}, u32[]{:S(2)}, u32[]{:S(2)}) collective-permute-start(bf16[8,2,128,128]{3,2,1,0:T(8,128)(2,1)} %collective-permute-done.21.refs_2_), channel_id=1, source_target_pairs={{8,16},{16,8},{9,17},{17,9},{10,18},{18,10},{11,19},{19,11},{12,20... | collective-permute-start | bytes 1572872 | tf_op jit(solution)/shard_map/ppermute | solution.py:357
  69.8 8.4 %collective-permute-start.13 = (bf16[1024,128]{1,0:T(8,128)(2,1)S(1)}, bf16[1024,128]{1,0:T(8,128)(2,1)S(1)}, u32[]{:S(2)}, u32[]{:S(2)}) collective-permute-start(bf16[1024,128]{1,0:T(8,128)(2,1)S(1)} %merge_0.1.refs_0_), channel_id=1, source_target_pairs={{0,4},{1,5},{2,6},{3,7},{4,0},{5,1},{6,2},{7,3},{8,12},{9,13},{10,... | collective-permute-start | bytes 786440 | tf_op jit(solution)/shard_map/ppermute | solution.py:344
  70.4 9.2 %collective-permute-start.11 = (bf16[1024,128]{1,0:T(8,128)(2,1)S(1)}, bf16[1024,128]{1,0:T(8,128)(2,1)S(1)}, u32[]{:S(2)}, u32[]{:S(2)}) collective-permute-start(bf16[1024,128]{1,0:T(8,128)(2,1)S(1)} %merge_0.1.refs_0_), channel_id=1, source_target_pairs={{0,2},{1,3},{2,0},{3,1},{4,6},{5,7},{6,4},{7,5},{8,10},{9,11},{10,... | collective-permute-start | bytes 786440 | tf_op jit(solution)/shard_map/ppermute | solution.py:344
  70.4 13.1 %collective-permute-start.15 = (bf16[1024,128]{1,0:T(8,128)(2,1)S(1)}, bf16[1024,128]{1,0:T(8,128)(2,1)S(1)}, u32[]{:S(2)}, u32[]{:S(2)}) collective-permute-start(bf16[1024,128]{1,0:T(8,128)(2,1)S(1)} %merge_0.1.refs_0_), channel_id=1, source_target_pairs={{0,6},{1,7},{2,4},{3,5},{4,2},{5,3},{6,0},{7,1},{8,14},{9,15},{10,... | collective-permute-start | bytes 786440 | tf_op jit(solution)/shard_map/ppermute | solution.py:344
  83.5 10.3 %collective-permute-start.24 = (bf16[8,144,128]{2,1,0:T(8,128)(2,1)S(1)}, bf16[8,144,128]{2,1,0:T(8,128)(2,1)S(1)}, u32[]{:S(2)}, u32[]{:S(2)}) collective-permute-start(bf16[8,144,128]{2,1,0:T(8,128)(2,1)S(1)} %get-tuple-element.76), channel_id=1, source_target_pairs={{8,0},{16,24},{9,1},{17,25},{10,2},{18,26},{11,3},{19,27},{12,4},{... | collective-permute-start | bytes 884744 | tf_op jit(solution)/shard_map/ppermute | solution.py:363
  84.8 11.2 %collective-permute-start.10 = (bf16[1024,128]{1,0:T(8,128)(2,1)S(1)}, bf16[1024,128]{1,0:T(8,128)(2,1)S(1)}, u32[]{:S(2)}, u32[]{:S(2)}) collective-permute-start(bf16[1024,128]{1,0:T(8,128)(2,1)S(1)} %merge_0.1.refs_0_), channel_id=1, source_target_pairs={{0,1},{1,0},{2,3},{3,2},{4,5},{5,4},{6,7},{7,6},{8,9},{9,8},{10,11... | collective-permute-start | bytes 786440 | tf_op jit(solution)/shard_map/ppermute | solution.py:344
  84.9 12.7 %collective-permute-start.16 = (bf16[1024,128]{1,0:T(8,128)(2,1)S(1)}, bf16[1024,128]{1,0:T(8,128)(2,1)S(1)}, u32[]{:S(2)}, u32[]{:S(2)}) collective-permute-start(bf16[1024,128]{1,0:T(8,128)(2,1)S(1)} %collective-permute-done.15.refs_6_), channel_id=1, source_target_pairs={{0,1},{1,0},{2,3},{3,2},{4,5},{5,4},{6,7},{7,6},{8,9},{9,8},{10,11... | collective-permute-start | bytes 786440 | tf_op jit(solution)/shard_map/ppermute | solution.py:344
  85.4 12.2 %collective-permute-start.14 = (bf16[1024,128]{1,0:T(8,128)(2,1)S(1)}, bf16[1024,128]{1,0:T(8,128)(2,1)S(1)}, u32[]{:S(2)}, u32[]{:S(2)}) collective-permute-start(bf16[1024,128]{1,0:T(8,128)(2,1)S(1)} %collective-permute-done.13.refs_4_), channel_id=1, source_target_pairs={{0,1},{1,0},{2,3},{3,2},{4,5},{5,4},{6,7},{7,6},{8,9},{9,8},{10,11... | collective-permute-start | bytes 786440 | tf_op jit(solution)/shard_map/ppermute | solution.py:344
  94.0 10.2 %collective-permute-start.30 = (bf16[1024,128]{1,0:T(8,128)(2,1)S(1)}, bf16[1024,128]{1,0:T(8,128)(2,1)S(1)}, u32[]{:S(2)}, u32[]{:S(2)}) collective-permute-start(bf16[1024,128]{1,0:T(8,128)(2,1)S(1)} %merge_1.1.refs_8_), channel_id=1, source_target_pairs={{0,6},{1,7},{2,4},{3,5},{4,2},{5,3},{6,0},{7,1},{8,14},{9,15},{10,... | collective-permute-start | bytes 786440 | tf_op jit(solution)/shard_map/ppermute | solution.py:344
  94.1 12.1 %collective-permute-start.28 = (bf16[1024,128]{1,0:T(8,128)(2,1)S(1)}, bf16[1024,128]{1,0:T(8,128)(2,1)S(1)}, u32[]{:S(2)}, u32[]{:S(2)}) collective-permute-start(bf16[1024,128]{1,0:T(8,128)(2,1)S(1)} %merge_1.1.refs_8_), channel_id=1, source_target_pairs={{0,4},{1,5},{2,6},{3,7},{4,0},{5,1},{6,2},{7,3},{8,12},{9,13},{10,... | collective-permute-start | bytes 786440 | tf_op jit(solution)/shard_map/ppermute | solution.py:344
  96.0 10.1 %collective-permute-start.26 = (bf16[1024,128]{1,0:T(8,128)(2,1)S(1)}, bf16[1024,128]{1,0:T(8,128)(2,1)S(1)}, u32[]{:S(2)}, u32[]{:S(2)}) collective-permute-start(bf16[1024,128]{1,0:T(8,128)(2,1)S(1)} %merge_1.1.refs_8_), channel_id=1, source_target_pairs={{0,2},{1,3},{2,0},{3,1},{4,6},{5,7},{6,4},{7,5},{8,10},{9,11},{10,... | collective-permute-start | bytes 786440 | tf_op jit(solution)/shard_map/ppermute | solution.py:344
  97.5 9.1 %collective-permute-start.12 = (bf16[1024,128]{1,0:T(8,128)(2,1)S(1)}, bf16[1024,128]{1,0:T(8,128)(2,1)S(1)}, u32[]{:S(2)}, u32[]{:S(2)}) collective-permute-start(bf16[1024,128]{1,0:T(8,128)(2,1)S(1)} %collective-permute-done.11.refs_2_), channel_id=1, source_target_pairs={{0,1},{1,0},{2,3},{3,2},{4,5},{5,4},{6,7},{7,6},{8,9},{9,8},{10,11... | collective-permute-start | bytes 786440 | tf_op jit(solution)/shard_map/ppermute | solution.py:344
  97.5 9.1 %collective-permute-start.25 = (bf16[1024,128]{1,0:T(8,128)(2,1)S(1)}, bf16[1024,128]{1,0:T(8,128)(2,1)S(1)}, u32[]{:S(2)}, u32[]{:S(2)}) collective-permute-start(bf16[1024,128]{1,0:T(8,128)(2,1)S(1)} %merge_1.1.refs_8_), channel_id=1, source_target_pairs={{0,1},{1,0},{2,3},{3,2},{4,5},{5,4},{6,7},{7,6},{8,9},{9,8},{10,11... | collective-permute-start | bytes 786440 | tf_op jit(solution)/shard_map/ppermute | solution.py:344
  (11 other events, 106.8 us)

commit v9 on v8

--- a/solution.py
+++ b/solution.py
@@ -53,8 +53,15 @@
         for copy in pair:
             copy.start()
     if marked:
+        shape = (mask_rows(mask_ref.shape[0]), HEAD_DIM)
+        row, column = (lax.broadcasted_iota(jnp.int32, shape, i) for i in (0, 1))
+        mask = jnp.zeros(shape, jnp.int32)
+        for i in range(mask_ref.shape[0]):
+            for j in range(mask_ref.shape[1]):
+                mask = jnp.where((row == i) & (column == j), mask_ref[i, j], mask)
+        mask = mask.astype(jnp.float32).astype(k_all.dtype)
         for k in range(n_ka):
-            out_refs[k // 2][k % 2, 2 * key_blocks * BLOCK :] = mask_ref[...]
+            out_refs[k // 2][k % 2, 2 * key_blocks * BLOCK :] = mask
     for k in range(n_ka):
         for t in range(key_blocks):
             copies[k * key_blocks + t][1].wait()
@@ -65,12 +72,12 @@
 
 def pack(me, keys, values, mask, n_ka, heads, c):
     key_blocks = keys.shape[0] // BLOCK
-    size = 2 * keys.shape[0] + (0 if mask is None else mask.shape[0])
+    size = 2 * keys.shape[0] + (0 if mask is None else mask_rows(mask.shape[0]))
     masks = () if mask is None else (mask,)
     return pl.pallas_call(
         functools.partial(pack_kernel, n_ka, heads, c, bool(masks)),
         out_shape=[jax.ShapeDtypeStruct((2, size, HEAD_DIM), keys.dtype)] * (n_ka // 2),
-        in_specs=[SMEM] + [VMEM] * len(masks) + [ANY, ANY],
+        in_specs=[SMEM] + [SMEM] * len(masks) + [ANY, ANY],
         out_specs=[VMEM] * (n_ka // 2),
         scratch_shapes=[
             pltpu.VMEM((n_ka, key_blocks, BLOCK, HEAD_DIM), values.dtype),
@@ -362,8 +369,9 @@
     def outward(x):
         return lax.ppermute(x, "pb", [(1, 0), (n_pb - 2, n_pb - 1)])
 
-    def sort(x):
+    def sort(x, before=None):
         mixed = [y if i == 0 else swap(y, 2 * i) for i, y in enumerate(x)]
+        mixed = after(mixed, before)
         theirs = swap(jnp.stack([y[1] for y in mixed]), 1)
         return jnp.concatenate([jnp.stack([y[0] for y in mixed]), theirs]), theirs
 
@@ -376,18 +384,20 @@
     def flags(x):
         return x[:, : block_mask.shape[1], :rows].astype(jnp.int32).reshape(-1)
 
-    columns = block_mask.shape[1]
-    mask = jnp.pad(block_mask.T.astype(keys.dtype), ((0, mask_rows(columns) - columns), (0, HEAD_DIM - rows)))
-    owns, moved = [], None
+    owns, over = [], []
     for c in range(heads):
-        packed = pack(after(me1, q) if c else me1, keys, values, None if c else mask, n_ka, heads, c)
+        packed = pack(after(me1, q) if c else me1, keys, values, None if c else block_mask.T, n_ka, heads, c)
         if c == 0:
             q = turn(after(me1, packed), queries, heads)
             guest = inward(q) if relay else None
-        own, moved = sort(after(packed, (moved, guest) if c else None))
+            own, moved = sort(packed, q)
+            marks = own[:, 2 * shard :]
+            guest_marks = inward(marks) if relay else None
+        else:
+            own, moved = sort(after(packed, (moved, guest)), over[0])
         owns.append(blocks(own))
-        if c == 0:
-            marks = own[:, 2 * shard :]
+        own = after(owns[c], (over[0][1], guest_marks) if c else None)
+        over.append([exchange(own, odd, 1) for odd in (0, 1)])
 
     steps = [((0, False),)]
     for step in range(1, n_pb):
@@ -398,14 +408,9 @@
             steps.append(found)
     last = len(steps) - 1
     masks = [flags(marks)]
-    guest_marks = inward(marks) if relay else None
     if relay:
         masks.append(flags(guest_marks))
     lists = plan(pb1, masks, steps, n_pb, n_ka, key_blocks, rows, relay)
-    over = []
-    for c in range(heads):
-        own = after(owns[c], (over[0][1], guest_marks) if c else None)
-        over.append([exchange(own, odd, 1) for odd in (0, 1)])
     state = [None] * heads
 
     def run(c, step, sources):

time: 111 us -> 117 us (1.054)
  waiting for transfers between devices: 41.9 us -> 52.2 us
  starting transfers between devices: 41.1 us -> 38.5 us
    ppermute x22, waiting for transfers between devices: 19.9 us -> 25.3 us  [swap(): return lax.ppermute(x, 'ka', [(i, i ^ k) for i in range(n_ka)])]
    ppermute x2, waiting for transfers between devices: 3.99 us -> 6.97 us  [inward(): return lax.ppermute(x, 'pb', [(0, 1), (n_pb - 1, n_pb - 2)])]
    ppermute x6, starting transfers between devices: 13.2 us -> 11.2 us  [exchange(): return lax.ppermute(x, 'pb', found) if found else None]
    ppermute x6, waiting for transfers between devices: 0.74 us -> 2.61 us  [exchange(): return lax.ppermute(x, 'pb', found) if found else None]
  transfers between devices with their start and end apart: 32 -> 32, of which waited for: 15 -> 18; matrix products, arithmetic and copies ran while one was open for 2% -> 1% of each run, Pallas kernels for 17% -> 16%
where the time goes in v9:
time: 117 us
  waiting for transfers between devices  52.2 us (45%)
  starting transfers between devices  38.5 us (33%)
  Pallas kernels  23.4 us (20%)
  local copies, waits for them, and re-layouts  1.31 us (1%)
    ppermute x22, waiting for transfers between devices, swap(): return lax.ppermute(x, 'ka', [(i, i ^ k) for i in range(n_ka)])  25.3 us
    ppermute x2, waiting for transfers between devices, outward(): return lax.ppermute(x, 'pb', [(1, 0), (n_pb - 2, n_pb - 1)])  17.3 us
    ppermute x22, starting transfers between devices, swap(): return lax.ppermute(x, 'ka', [(i, i ^ k) for i in range(n_ka)])  16.9 us
    ppermute x6, starting transfers between devices, exchange(): return lax.ppermute(x, 'pb', found) if found else None  11.2 us
    pallas_call x4, Pallas kernels, attend(): pl.pallas_call(functools.partial(attend_kernel, c, n_src, entry, first, m...  11.1 us
    ppermute x2, starting transfers between devices, inward(): return lax.ppermute(x, 'pb', [(0, 1), (n_pb - 1, n_pb - 2)])  7.9 us
    ppermute x2, waiting for transfers between devices, inward(): return lax.ppermute(x, 'pb', [(0, 1), (n_pb - 1, n_pb - 2)])  6.97 us
    pallas_call x2, Pallas kernels, pack(): pl.pallas_call(functools.partial(pack_kernel, n_ka, heads, c, bool(masks)...  5.31 us
  transfers between devices with their start and end apart: 32, of which 18 were waited for; matrix products, arithmetic and copies ran while one was open for 1% of the time, Pallas kernels for 16%

profile of v9, /device:TPU:0, one launch (start us, length us, event | category | flops | bytes accessed | tf_op | source)
XLA Modules:
  0.0 116.6 jit_solution(7709010728668853132)
XLA Ops:
  0.0 3.0 %pack_0.1 = (bf16[2,272,128]{2,1,0:T(8,128)(2,1)}, bf16[2,272,128]{2,1,0:T(8,128)(2,1)}, bf16[2,272,128]{2,1,0:T(8,128)(2,1)}, bf16[2,272,128]{2,1,0:T(8,128)(2,1)}) custom-call(s32[1]{0:T(128)} %bitcast.me_ref, s32[4,8]{1,0:T(4,128)} %bitcast.12, bf16[128,2048]{1,0:T(8,128)(2,1)} %refs_0_.1, bf16[128,2048]{1,0:T(8,128)(2,1)} %refs_1_.3), custom_call_target="tpu_custom_call" | custom-call | bytes 262144 | tf_op jit(solution)/shard_map/pack_0/pallas_call | solution.py:77
  3.0 3.0 %collective-permute-start = (bf16[2,272,128]{2,1,0:T(8,128)(2,1)}, bf16[2,272,128]{2,1,0:T(8,128)(2,1)S(1)}, u32[]{:S(2)}, u32[]{:S(2)}) collective-permute-start(bf16[2,272,128]{2,1,0:T(8,128)(2,1)} %get-tuple-element.50), channel_id=1, source_target_pairs={{0,2},{1,3},{2,0},{3,1},{4,6},{5,7},{6,4},{7,5},{8,10},{9,11},{10,... | collective-permute-start | bytes 417800 | tf_op jit(solution)/shard_map/ppermute | solution.py:351
  7.6 2.0 %turn.1.q_own = bf16[2,8,128,128]{3,2,1,0:T(8,128)(2,1)} custom-call(s32[1]{0:T(128)} %bitcast.me_ref, bf16[1024,2048]{1,0:T(8,128)(2,1)} %q_all.1), custom_call_target="tpu_custom_call" | custom-call | bytes 131072 | tf_op jit(solution)/shard_map/turn/pallas_call | solution.py:105
  10.4 3.9 %collective-permute-done.1 = bf16[2,272,128]{2,1,0:T(8,128)(2,1)S(1)} collective-permute-done((bf16[2,272,128]{2,1,0:T(8,128)(2,1)}, bf16[2,272,128]{2,1,0:T(8,128)(2,1)S(1)}, u32[]{:S(2)}, u32[]{:S(2)}) %collective-permute-start.1) | collective-permute-done | bytes 139296 | tf_op jit(solution)/shard_map/ppermute | solution.py:351
  14.6 3.5 %collective-permute-start.5 = (bf16[2,8,128,128]{3,2,1,0:T(8,128)(2,1)}, bf16[2,8,128,128]{3,2,1,0:T(8,128)(2,1)S(1)}, u32[]{:S(2)}, u32[]{:S(2)}) collective-permute-start(bf16[2,8,128,128]{3,2,1,0:T(8,128)(2,1)} %turn.1.q_own), channel_id=1, source_target_pairs={{0,8},{24,16},{1,9},{25,17},{2,10},{26,18},{3,11},{27,19},{4,12},{... | collective-permute-start | bytes 1572872 | tf_op jit(solution)/shard_map/ppermute | solution.py:367
  18.9 2.4 %collective-permute-start.6 = (bf16[8,2,128,128]{3,2,1,0:T(8,128)(2,1)S(1)}, bf16[8,2,128,128]{3,2,1,0:T(8,128)(2,1)S(1)}, u32[]{:S(2)}, u32[]{:S(2)}) collective-permute-start(bf16[8,2,128,128]{3,2,1,0:T(8,128)(2,1)S(1)} %bitcast.7), channel_id=1, source_target_pairs={{0,8},{8,0},{16,24},{24,16},{1,9},{9,1},{17,25},{25,17},{2,10},{10... | collective-permute-start | bytes 1572872 | tf_op jit(solution)/shard_map/ppermute | solution.py:364
  21.3 2.3 %pack_1.1 = (bf16[2,256,128]{2,1,0:T(8,128)(2,1)}, bf16[2,256,128]{2,1,0:T(8,128)(2,1)}, bf16[2,256,128]{2,1,0:T(8,128)(2,1)}, bf16[2,256,128]{2,1,0:T(8,128)(2,1)}) custom-call(s32[1]{0:T(128)} %bitcast.me_ref, bf16[128,2048]{1,0:T(8,128)(2,1)} %refs_0_.1, bf16[128,2048]{1,0:T(8,128)(2,1)} %refs_1_.3), custom_call_target="tpu_custom_call" | custom-call | bytes 262144 | tf_op jit(solution)/shard_map/pack_1/pallas_call | solution.py:77
  23.7 6.9 %collective-permute-done.5.refs_0_ = bf16[2,8,128,128]{3,2,1,0:T(8,128)(2,1)S(1)} collective-permute-done((bf16[2,8,128,128]{3,2,1,0:T(8,128)(2,1)}, bf16[2,8,128,128]{3,2,1,0:T(8,128)(2,1)S(1)}, u32[]{:S(2)}, u32[]{:S(2)}) %collective-permute-start.5) | collective-permute-done | bytes 524320 | tf_op jit(solution)/shard_map/ppermute | solution.py:367
  34.1 2.7 %collective-permute-done.17 = bf16[2,256,128]{2,1,0:T(8,128)(2,1)S(1)} collective-permute-done((bf16[2,256,128]{2,1,0:T(8,128)(2,1)}, bf16[2,256,128]{2,1,0:T(8,128)(2,1)S(1)}, u32[]{:S(2)}, u32[]{:S(2)}) %collective-permute-start.17) | collective-permute-done | bytes 131104 | tf_op jit(solution)/shard_map/ppermute | solution.py:351
  36.8 2.7 %collective-permute-done.18 = bf16[2,256,128]{2,1,0:T(8,128)(2,1)S(1)} collective-permute-done((bf16[2,256,128]{2,1,0:T(8,128)(2,1)}, bf16[2,256,128]{2,1,0:T(8,128)(2,1)S(1)}, u32[]{:S(2)}, u32[]{:S(2)}) %collective-permute-start.18) | collective-permute-done | bytes 131104 | tf_op jit(solution)/shard_map/ppermute | solution.py:351
  39.4 1.9 %collective-permute-done.6.refs_2_ = bf16[8,2,128,128]{3,2,1,0:T(8,128)(2,1)S(1)} collective-permute-done((bf16[8,2,128,128]{3,2,1,0:T(8,128)(2,1)S(1)}, bf16[8,2,128,128]{3,2,1,0:T(8,128)(2,1)S(1)}, u32[]{:S(2)}, u32[]{:S(2)}) %collective-permute-start.6) | collective-permute-done | bytes 524320 | tf_op jit(solution)/shard_map/ppermute | solution.py:364
  42.4 4.4 %collective-permute-start.4 = (bf16[8,16,128]{2,1,0:T(8,128)(2,1)S(1)}, bf16[8,16,128]{2,1,0:T(8,128)(2,1)S(1)}, u32[]{:S(2)}, u32[]{:S(2)}) collective-permute-start(bf16[8,16,128]{2,1,0:T(8,128)(2,1)S(1)} %slice.82), channel_id=1, source_target_pairs={{0,8},{24,16},{1,9},{25,17},{2,10},{26,18},{3,11},{27,19},{4,12},{... | collective-permute-start | bytes 98312 | tf_op jit(solution)/shard_map/ppermute | solution.py:367
  49.9 4.4 %collective-permute-start.21 = (bf16[8,2,128,128]{3,2,1,0:T(8,128)(2,1)S(1)}, bf16[8,2,128,128]{3,2,1,0:T(8,128)(2,1)}, u32[]{:S(2)}, u32[]{:S(2)}) collective-permute-start(bf16[8,2,128,128]{3,2,1,0:T(8,128)(2,1)S(1)} %bitcast.10), channel_id=1, source_target_pairs={{0,8},{8,0},{16,24},{24,16},{1,9},{9,1},{17,25},{25,17},{2,10},{10... | collective-permute-start | bytes 1572872 | tf_op jit(solution)/shard_map/ppermute | solution.py:364
  55.2 2.4 %plan.1 = (s32[2]{0:T(128)S(1)}, s32[432]{0:T(512)S(1)}, s32[176]{0:T(256)S(1)}) custom-call(s32[1]{0:T(128)} %bitcast.2.pb_ref, s32[256]{0:T(256)S(1)} %reshape.24.refs_0_, s32[256]{0:T(256)S(1)} %reshape.26.refs_1_), custom_call_target="tpu_custom_call" | custom-call | tf_op jit(solution)/shard_map/plan/pallas_call | solution.py:159
  57.6 3.4 %attend_0_0.1 = (f32[16,1,128]{2,1,0:T(1,128)S(1)}, f32[16,1,128]{2,1,0:T(1,128)S(1)}, f32[16,128,128]{2,1,0:T(8,128)S(1)}) custom-call(s32[2]{0:T(128)S(1)} %get-tuple-element.58.count_ref, s32[432]{0:T(512)S(1)} %get-tuple-element.61.live_ref, bf16[2,8,128,128]{3,2,1,0:T(8,128)(2,1)S(1)} %copy-done, ...), custom_call_target="tpu_custom_call" | custom-call | bytes 16384 | tf_op jit(solution)/shard_map/attend_0_0/pallas_call | solution.py:273
  61.0 2.4 %attend_0_1.1 = (f32[16,1,128]{2,1,0:T(1,128)S(1)}, f32[16,1,128]{2,1,0:T(1,128)S(1)}, f32[16,128,128]{2,1,0:T(8,128)S(1)}, bf16[8,144,128]{2,1,0:T(8,128)(2,1)}) custom-call(s32[2]{0:T(128)S(1)} %get-tuple-element.58.count_ref, s32[176]{0:T(256)S(1)} %get-tuple-element.59.live_ref, bf16[2,8,128,128]{3,2,1,0:T(8,128)(2,1)S(1)} %copy-done, ...), custom_call_target="tpu_custom_call" | custom-call | bytes 16384 | tf_op jit(solution)/shard_map/attend_0_1/pallas_call | solution.py:273
  66.2 9.0 %collective-permute-done.9.part_ref = bf16[8,144,128]{2,1,0:T(8,128)(2,1)S(1)} collective-permute-done((bf16[8,144,128]{2,1,0:T(8,128)(2,1)}, bf16[8,144,128]{2,1,0:T(8,128)(2,1)S(1)}, u32[]{:S(2)}, u32[]{:S(2)}) %collective-permute-start.9) | collective-permute-done | bytes 294944 | tf_op jit(solution)/shard_map/ppermute | solution.py:370
  78.9 4.4 %attend_1_0.1 = (f32[16,1,128]{2,1,0:T(1,128)S(1)}, f32[16,1,128]{2,1,0:T(1,128)S(1)}, f32[16,128,128]{2,1,0:T(8,128)S(1)}) custom-call(s32[2]{0:T(128)S(1)} %get-tuple-element.58.count_ref, s32[432]{0:T(512)S(1)} %get-tuple-element.61.live_ref, bf16[2,8,128,128]{3,2,1,0:T(8,128)(2,1)S(1)} %copy-done, ...), custom_call_target="tpu_custom_call" | custom-call | bytes 16384 | tf_op jit(solution)/shard_map/attend_1_0/pallas_call | solution.py:273
  83.8 2.4 %collective-permute-done.11.refs_2_ = bf16[1024,128]{1,0:T(8,128)(2,1)S(1)} collective-permute-done((bf16[1024,128]{1,0:T(8,128)(2,1)S(1)}, bf16[1024,128]{1,0:T(8,128)(2,1)S(1)}, u32[]{:S(2)}, u32[]{:S(2)}) %collective-permute-start.11) | collective-permute-done | bytes 262176 | tf_op jit(solution)/shard_map/ppermute | solution.py:351
  87.1 2.0 %collective-permute-done.15.refs_6_ = bf16[1024,128]{1,0:T(8,128)(2,1)S(1)} collective-permute-done((bf16[1024,128]{1,0:T(8,128)(2,1)S(1)}, bf16[1024,128]{1,0:T(8,128)(2,1)S(1)}, u32[]{:S(2)}, u32[]{:S(2)}) %collective-permute-start.15) | collective-permute-done | bytes 262176 | tf_op jit(solution)/shard_map/ppermute | solution.py:351
  91.0 8.3 %collective-permute-done.24.part_ref = bf16[8,144,128]{2,1,0:T(8,128)(2,1)S(1)} collective-permute-done((bf16[8,144,128]{2,1,0:T(8,128)(2,1)S(1)}, bf16[8,144,128]{2,1,0:T(8,128)(2,1)S(1)}, u32[]{:S(2)}, u32[]{:S(2)}) %collective-permute-start.24) | collective-permute-done | bytes 294944 | tf_op jit(solution)/shard_map/ppermute | solution.py:370
  103.6 6.1 %collective-permute-done.30.refs_14_ = bf16[1024,128]{1,0:T(8,128)(2,1)S(1)} collective-permute-done((bf16[1024,128]{1,0:T(8,128)(2,1)S(1)}, bf16[1024,128]{1,0:T(8,128)(2,1)S(1)}, u32[]{:S(2)}, u32[]{:S(2)}) %collective-permute-start.30) | collective-permute-done | bytes 262176 | tf_op jit(solution)/shard_map/ppermute | solution.py:351
  109.7 2.8 %collective-permute-done.28.refs_12_ = bf16[1024,128]{1,0:T(8,128)(2,1)S(1)} collective-permute-done((bf16[1024,128]{1,0:T(8,128)(2,1)S(1)}, bf16[1024,128]{1,0:T(8,128)(2,1)S(1)}, u32[]{:S(2)}, u32[]{:S(2)}) %collective-permute-start.28) | collective-permute-done | bytes 262176 | tf_op jit(solution)/shard_map/ppermute | solution.py:351
  114.4 2.1 %place.1 = bf16[1024,2048]{1,0:T(8,128)(2,1)} custom-call(s32[1]{0:T(128)} %bitcast.me_ref, bf16[1024,128]{1,0:T(8,128)(2,1)S(1)} %merge_0.1.refs_0_, bf16[1024,128]{1,0:T(8,128)(2,1)S(1)} %collective-permute-done.10.refs_1_, bf16[1024,128]{1,0:T(8,128)(2,1)S(1)} %collective-permute-done.11.refs_2_, bf16[1024,128]{1,0:T(8,128)(2,1)S(1)} %collective-permute-done.12.refs_3_, ...), custom_call_target="tpu_custom_call" | custom-call | tf_op jit(solution)/shard_map/place/pallas_call | solution.py:330
  (75 shorter events, 27.7 us)
Async XLA Ops:
  3.0 7.4 %collective-permute-start = (bf16[2,272,128]{2,1,0:T(8,128)(2,1)}, bf16[2,272,128]{2,1,0:T(8,128)(2,1)S(1)}, u32[]{:S(2)}, u32[]{:S(2)}) collective-permute-start(bf16[2,272,128]{2,1,0:T(8,128)(2,1)} %get-tuple-element.50), channel_id=1, source_target_pairs={{0,2},{1,3},{2,0},{3,1},{4,6},{5,7},{6,4},{7,5},{8,10},{9,11},{10,... | collective-permute-start | bytes 417800 | tf_op jit(solution)/shard_map/ppermute | solution.py:351
  6.0 8.3 %collective-permute-start.1 = (bf16[2,272,128]{2,1,0:T(8,128)(2,1)}, bf16[2,272,128]{2,1,0:T(8,128)(2,1)S(1)}, u32[]{:S(2)}, u32[]{:S(2)}) collective-permute-start(bf16[2,272,128]{2,1,0:T(8,128)(2,1)} %get-tuple-element.51), channel_id=1, source_target_pairs={{0,4},{1,5},{2,6},{3,7},{4,0},{5,1},{6,2},{7,3},{8,12},{9,13},{10,... | collective-permute-start | bytes 417800 | tf_op jit(solution)/shard_map/ppermute | solution.py:351
  7.5 6.8 %collective-permute-start.2 = (bf16[2,272,128]{2,1,0:T(8,128)(2,1)}, bf16[2,272,128]{2,1,0:T(8,128)(2,1)S(1)}, u32[]{:S(2)}, u32[]{:S(2)}) collective-permute-start(bf16[2,272,128]{2,1,0:T(8,128)(2,1)} %get-tuple-element.52), channel_id=1, source_target_pairs={{0,6},{1,7},{2,4},{3,5},{4,2},{5,3},{6,0},{7,1},{8,14},{9,15},{10,... | collective-permute-start | bytes 417800 | tf_op jit(solution)/shard_map/ppermute | solution.py:351
  14.6 16.0 %collective-permute-start.5 = (bf16[2,8,128,128]{3,2,1,0:T(8,128)(2,1)}, bf16[2,8,128,128]{3,2,1,0:T(8,128)(2,1)S(1)}, u32[]{:S(2)}, u32[]{:S(2)}) collective-permute-start(bf16[2,8,128,128]{3,2,1,0:T(8,128)(2,1)} %turn.1.q_own), channel_id=1, source_target_pairs={{0,8},{24,16},{1,9},{25,17},{2,10},{26,18},{3,11},{27,19},{4,12},{... | collective-permute-start | bytes 1572872 | tf_op jit(solution)/shard_map/ppermute | solution.py:367
  18.2 21.2 %collective-permute-start.7 = (bf16[8,2,128,128]{3,2,1,0:T(8,128)(2,1)S(1)}, bf16[8,2,128,128]{3,2,1,0:T(8,128)(2,1)S(1)}, u32[]{:S(2)}, u32[]{:S(2)}) collective-permute-start(bf16[8,2,128,128]{3,2,1,0:T(8,128)(2,1)S(1)} %bitcast.6), channel_id=1, source_target_pairs={{8,16},{16,8},{9,17},{17,9},{10,18},{18,10},{11,19},{19,11},{12,20... | collective-permute-start | bytes 1572872 | tf_op jit(solution)/shard_map/ppermute | solution.py:364
  18.9 22.4 %collective-permute-start.6 = (bf16[8,2,128,128]{3,2,1,0:T(8,128)(2,1)S(1)}, bf16[8,2,128,128]{3,2,1,0:T(8,128)(2,1)S(1)}, u32[]{:S(2)}, u32[]{:S(2)}) collective-permute-start(bf16[8,2,128,128]{3,2,1,0:T(8,128)(2,1)S(1)} %bitcast.7), channel_id=1, source_target_pairs={{0,8},{8,0},{16,24},{24,16},{1,9},{9,1},{17,25},{25,17},{2,10},{10... | collective-permute-start | bytes 1572872 | tf_op jit(solution)/shard_map/ppermute | solution.py:364
  31.8 7.6 %collective-permute-start.18 = (bf16[2,256,128]{2,1,0:T(8,128)(2,1)}, bf16[2,256,128]{2,1,0:T(8,128)(2,1)S(1)}, u32[]{:S(2)}, u32[]{:S(2)}) collective-permute-start(bf16[2,256,128]{2,1,0:T(8,128)(2,1)} %get-tuple-element.76), channel_id=1, source_target_pairs={{0,4},{1,5},{2,6},{3,7},{4,0},{5,1},{6,2},{7,3},{8,12},{9,13},{10,... | collective-permute-start | bytes 393224 | tf_op jit(solution)/shard_map/ppermute | solution.py:351
  46.8 14.2 %collective-permute-start.8 = (bf16[8,2,128,128]{3,2,1,0:T(8,128)(2,1)S(1)}, bf16[8,2,128,128]{3,2,1,0:T(8,128)(2,1)}, u32[]{:S(2)}, u32[]{:S(2)}) collective-permute-start(bf16[8,2,128,128]{3,2,1,0:T(8,128)(2,1)S(1)} %collective-permute-done.6.refs_2_), channel_id=1, source_target_pairs={{8,16},{16,8},{9,17},{17,9},{10,18},{18,10},{11,19},{19,11},{12,20... | collective-permute-start | bytes 1572872 | tf_op jit(solution)/shard_map/ppermute | solution.py:364
  48.4 16.4 %collective-permute-start.22 = (bf16[8,2,128,128]{3,2,1,0:T(8,128)(2,1)S(1)}, bf16[8,2,128,128]{3,2,1,0:T(8,128)(2,1)}, u32[]{:S(2)}, u32[]{:S(2)}) collective-permute-start(bf16[8,2,128,128]{3,2,1,0:T(8,128)(2,1)S(1)} %bitcast.9), channel_id=1, source_target_pairs={{8,16},{16,8},{9,17},{17,9},{10,18},{18,10},{11,19},{19,11},{12,20... | collective-permute-start | bytes 1572872 | tf_op jit(solution)/shard_map/ppermute | solution.py:364
  49.9 15.6 %collective-permute-start.21 = (bf16[8,2,128,128]{3,2,1,0:T(8,128)(2,1)S(1)}, bf16[8,2,128,128]{3,2,1,0:T(8,128)(2,1)}, u32[]{:S(2)}, u32[]{:S(2)}) collective-permute-start(bf16[8,2,128,128]{3,2,1,0:T(8,128)(2,1)S(1)} %bitcast.10), channel_id=1, source_target_pairs={{0,8},{8,0},{16,24},{24,16},{1,9},{9,1},{17,25},{25,17},{2,10},{10... | collective-permute-start | bytes 1572872 | tf_op jit(solution)/shard_map/ppermute | solution.py:364
  63.4 11.7 %collective-permute-start.9 = (bf16[8,144,128]{2,1,0:T(8,128)(2,1)}, bf16[8,144,128]{2,1,0:T(8,128)(2,1)S(1)}, u32[]{:S(2)}, u32[]{:S(2)}) collective-permute-start(bf16[8,144,128]{2,1,0:T(8,128)(2,1)} %get-tuple-element.68), channel_id=1, source_target_pairs={{8,0},{16,24},{9,1},{17,25},{10,2},{18,26},{11,3},{19,27},{12,4},{... | collective-permute-start | bytes 884744 | tf_op jit(solution)/shard_map/ppermute | solution.py:370
  65.5 20.7 %collective-permute-start.23 = (bf16[8,2,128,128]{3,2,1,0:T(8,128)(2,1)}, bf16[8,2,128,128]{3,2,1,0:T(8,128)(2,1)S(1)}, u32[]{:S(2)}, u32[]{:S(2)}) collective-permute-start(bf16[8,2,128,128]{3,2,1,0:T(8,128)(2,1)} %collective-permute-done.21.refs_2_), channel_id=1, source_target_pairs={{8,16},{16,8},{9,17},{17,9},{10,18},{18,10},{11,19},{19,11},{12,20... | collective-permute-start | bytes 1572872 | tf_op jit(solution)/shard_map/ppermute | solution.py:364
  75.4 8.4 %collective-permute-start.13 = (bf16[1024,128]{1,0:T(8,128)(2,1)S(1)}, bf16[1024,128]{1,0:T(8,128)(2,1)S(1)}, u32[]{:S(2)}, u32[]{:S(2)}) collective-permute-start(bf16[1024,128]{1,0:T(8,128)(2,1)S(1)} %merge_0.1.refs_0_), channel_id=1, source_target_pairs={{0,4},{1,5},{2,6},{3,7},{4,0},{5,1},{6,2},{7,3},{8,12},{9,13},{10,... | collective-permute-start | bytes 786440 | tf_op jit(solution)/shard_map/ppermute | solution.py:351
  77.0 9.2 %collective-permute-start.11 = (bf16[1024,128]{1,0:T(8,128)(2,1)S(1)}, bf16[1024,128]{1,0:T(8,128)(2,1)S(1)}, u32[]{:S(2)}, u32[]{:S(2)}) collective-permute-start(bf16[1024,128]{1,0:T(8,128)(2,1)S(1)} %merge_0.1.refs_0_), channel_id=1, source_target_pairs={{0,2},{1,3},{2,0},{3,1},{4,6},{5,7},{6,4},{7,5},{8,10},{9,11},{10,... | collective-permute-start | bytes 786440 | tf_op jit(solution)/shard_map/ppermute | solution.py:351
  77.5 11.6 %collective-permute-start.15 = (bf16[1024,128]{1,0:T(8,128)(2,1)S(1)}, bf16[1024,128]{1,0:T(8,128)(2,1)S(1)}, u32[]{:S(2)}, u32[]{:S(2)}) collective-permute-start(bf16[1024,128]{1,0:T(8,128)(2,1)S(1)} %merge_0.1.refs_0_), channel_id=1, source_target_pairs={{0,6},{1,7},{2,4},{3,5},{4,2},{5,3},{6,0},{7,1},{8,14},{9,15},{10,... | collective-permute-start | bytes 786440 | tf_op jit(solution)/shard_map/ppermute | solution.py:351
  89.1 10.3 %collective-permute-start.24 = (bf16[8,144,128]{2,1,0:T(8,128)(2,1)S(1)}, bf16[8,144,128]{2,1,0:T(8,128)(2,1)S(1)}, u32[]{:S(2)}, u32[]{:S(2)}) collective-permute-start(bf16[8,144,128]{2,1,0:T(8,128)(2,1)S(1)} %get-tuple-element.92), channel_id=1, source_target_pairs={{8,0},{16,24},{9,1},{17,25},{10,2},{18,26},{11,3},{19,27},{12,4},{... | collective-permute-start | bytes 884744 | tf_op jit(solution)/shard_map/ppermute | solution.py:370
  90.4 11.9 %collective-permute-start.10 = (bf16[1024,128]{1,0:T(8,128)(2,1)S(1)}, bf16[1024,128]{1,0:T(8,128)(2,1)S(1)}, u32[]{:S(2)}, u32[]{:S(2)}) collective-permute-start(bf16[1024,128]{1,0:T(8,128)(2,1)S(1)} %merge_0.1.refs_0_), channel_id=1, source_target_pairs={{0,1},{1,0},{2,3},{3,2},{4,5},{5,4},{6,7},{7,6},{8,9},{9,8},{10,11... | collective-permute-start | bytes 786440 | tf_op jit(solution)/shard_map/ppermute | solution.py:351
  90.5 12.7 %collective-permute-start.16 = (bf16[1024,128]{1,0:T(8,128)(2,1)S(1)}, bf16[1024,128]{1,0:T(8,128)(2,1)S(1)}, u32[]{:S(2)}, u32[]{:S(2)}) collective-permute-start(bf16[1024,128]{1,0:T(8,128)(2,1)S(1)} %collective-permute-done.15.refs_6_), channel_id=1, source_target_pairs={{0,1},{1,0},{2,3},{3,2},{4,5},{5,4},{6,7},{7,6},{8,9},{9,8},{10,11... | collective-permute-start | bytes 786440 | tf_op jit(solution)/shard_map/ppermute | solution.py:351
  91.0 12.2 %collective-permute-start.14 = (bf16[1024,128]{1,0:T(8,128)(2,1)S(1)}, bf16[1024,128]{1,0:T(8,128)(2,1)S(1)}, u32[]{:S(2)}, u32[]{:S(2)}) collective-permute-start(bf16[1024,128]{1,0:T(8,128)(2,1)S(1)} %collective-permute-done.13.refs_4_), channel_id=1, source_target_pairs={{0,1},{1,0},{2,3},{3,2},{4,5},{5,4},{6,7},{7,6},{8,9},{9,8},{10,11... | collective-permute-start | bytes 786440 | tf_op jit(solution)/shard_map/ppermute | solution.py:351
  99.6 10.2 %collective-permute-start.30 = (bf16[1024,128]{1,0:T(8,128)(2,1)S(1)}, bf16[1024,128]{1,0:T(8,128)(2,1)S(1)}, u32[]{:S(2)}, u32[]{:S(2)}) collective-permute-start(bf16[1024,128]{1,0:T(8,128)(2,1)S(1)} %merge_1.1.refs_8_), channel_id=1, source_target_pairs={{0,6},{1,7},{2,4},{3,5},{4,2},{5,3},{6,0},{7,1},{8,14},{9,15},{10,... | collective-permute-start | bytes 786440 | tf_op jit(solution)/shard_map/ppermute | solution.py:351
  101.1 11.4 %collective-permute-start.28 = (bf16[1024,128]{1,0:T(8,128)(2,1)S(1)}, bf16[1024,128]{1,0:T(8,128)(2,1)S(1)}, u32[]{:S(2)}, u32[]{:S(2)}) collective-permute-start(bf16[1024,128]{1,0:T(8,128)(2,1)S(1)} %merge_1.1.refs_8_), channel_id=1, source_target_pairs={{0,4},{1,5},{2,6},{3,7},{4,0},{5,1},{6,2},{7,3},{8,12},{9,13},{10,... | collective-permute-start | bytes 786440 | tf_op jit(solution)/shard_map/ppermute | solution.py:351
  102.3 10.3 %collective-permute-start.26 = (bf16[1024,128]{1,0:T(8,128)(2,1)S(1)}, bf16[1024,128]{1,0:T(8,128)(2,1)S(1)}, u32[]{:S(2)}, u32[]{:S(2)}) collective-permute-start(bf16[1024,128]{1,0:T(8,128)(2,1)S(1)} %merge_1.1.refs_8_), channel_id=1, source_target_pairs={{0,2},{1,3},{2,0},{3,1},{4,6},{5,7},{6,4},{7,5},{8,10},{9,11},{10,... | collective-permute-start | bytes 786440 | tf_op jit(solution)/shard_map/ppermute | solution.py:351
  103.1 9.9 %collective-permute-start.12 = (bf16[1024,128]{1,0:T(8,128)(2,1)S(1)}, bf16[1024,128]{1,0:T(8,128)(2,1)S(1)}, u32[]{:S(2)}, u32[]{:S(2)}) collective-permute-start(bf16[1024,128]{1,0:T(8,128)(2,1)S(1)} %collective-permute-done.11.refs_2_), channel_id=1, source_target_pairs={{0,1},{1,0},{2,3},{3,2},{4,5},{5,4},{6,7},{7,6},{8,9},{9,8},{10,11... | collective-permute-start | bytes 786440 | tf_op jit(solution)/shard_map/ppermute | solution.py:351
  103.1 9.9 %collective-permute-start.25 = (bf16[1024,128]{1,0:T(8,128)(2,1)S(1)}, bf16[1024,128]{1,0:T(8,128)(2,1)S(1)}, u32[]{:S(2)}, u32[]{:S(2)}) collective-permute-start(bf16[1024,128]{1,0:T(8,128)(2,1)S(1)} %merge_1.1.refs_8_), channel_id=1, source_target_pairs={{0,1},{1,0},{2,3},{3,2},{4,5},{5,4},{6,7},{7,6},{8,9},{9,8},{10,11... | collective-permute-start | bytes 786440 | tf_op jit(solution)/shard_map/ppermute | solution.py:351
  (11 other events, 124.7 us)

commit v10 on v9

--- a/solution.py
+++ b/solution.py
@@ -32,8 +32,8 @@
     return -(-rows // 16) * 16
 
 
-def pack_kernel(n_ka, heads, c, marked, me_ref, *refs):
-    mask_ref, refs = (refs[0], refs[1:]) if marked else (None, refs)
+def pack_kernel(n_ka, heads, c, n_masks, me_ref, *refs):
+    mask_refs, refs = refs[:n_masks], refs[n_masks:]
     k_all, v_all, *out_refs, v_ref, sems = refs
     key_blocks = k_all.shape[0] // BLOCK
     copies = []
@@ -52,16 +52,17 @@
     for pair in copies:
         for copy in pair:
             copy.start()
-    if marked:
-        shape = (mask_rows(mask_ref.shape[0]), HEAD_DIM)
-        row, column = (lax.broadcasted_iota(jnp.int32, shape, i) for i in (0, 1))
-        mask = jnp.zeros(shape, jnp.int32)
-        for i in range(mask_ref.shape[0]):
-            for j in range(mask_ref.shape[1]):
-                mask = jnp.where((row == i) & (column == j), mask_ref[i, j], mask)
+    for i, mask_ref in enumerate(mask_refs):
+        size = mask_rows(mask_ref.shape[0])
+        row, column = (lax.broadcasted_iota(jnp.int32, (size, HEAD_DIM), axis) for axis in (0, 1))
+        mask = jnp.zeros((size, HEAD_DIM), jnp.int32)
+        for a in range(mask_ref.shape[0]):
+            for b in range(mask_ref.shape[1]):
+                mask = jnp.where((row == a) & (column == b), mask_ref[a, b], mask)
         mask = mask.astype(jnp.float32).astype(k_all.dtype)
+        at = 2 * key_blocks * BLOCK + i * size
         for k in range(n_ka):
-            out_refs[k // 2][k % 2, 2 * key_blocks * BLOCK :] = mask
+            out_refs[k // 2][k % 2, at : at + size] = mask
     for k in range(n_ka):
         for t in range(key_blocks):
             copies[k * key_blocks + t][1].wait()
@@ -70,12 +71,11 @@
         pair[0].wait()
 
 
-def pack(me, keys, values, mask, n_ka, heads, c):
+def pack(me, keys, values, masks, n_ka, heads, c):
     key_blocks = keys.shape[0] // BLOCK
-    size = 2 * keys.shape[0] + (0 if mask is None else mask_rows(mask.shape[0]))
-    masks = () if mask is None else (mask,)
+    size = 2 * keys.shape[0] + sum(mask_rows(mask.shape[0]) for mask in masks)
     return pl.pallas_call(
-        functools.partial(pack_kernel, n_ka, heads, c, bool(masks)),
+        functools.partial(pack_kernel, n_ka, heads, c, len(masks)),
         out_shape=[jax.ShapeDtypeStruct((2, size, HEAD_DIM), keys.dtype)] * (n_ka // 2),
         in_specs=[SMEM] + [SMEM] * len(masks) + [ANY, ANY],
         out_specs=[VMEM] * (n_ka // 2),
@@ -89,24 +89,24 @@
     )(me, *masks, keys, values)
 
 
-def turn_kernel(heads, me_ref, q_all, out_ref, q_ref, sem):
+def turn_kernel(heads, me_ref, q_all, *refs):
+    out_refs, (q_ref, sem) = refs[:heads], refs[heads:]
     column = pl.multiple_of(me_ref[0] * heads * HEAD_DIM, HEAD_DIM)
     copy = pltpu.make_async_copy(q_all.at[:, pl.ds(column, heads * HEAD_DIM)], q_ref, sem)
     copy.start()
     copy.wait()
-    rows = out_ref.shape[1]
     for c in range(heads):
-        for r in range(rows):
-            out_ref[c, r] = q_ref[r * BLOCK : (r + 1) * BLOCK, c * HEAD_DIM : (c + 1) * HEAD_DIM].T
+        for r in range(out_refs[c].shape[0]):
+            out_refs[c][r] = q_ref[r * BLOCK : (r + 1) * BLOCK, c * HEAD_DIM : (c + 1) * HEAD_DIM].T
 
 
 def turn(me, queries, heads):
     tokens = queries.shape[0]
     return pl.pallas_call(
         functools.partial(turn_kernel, heads),
-        out_shape=jax.ShapeDtypeStruct((heads, tokens // BLOCK, HEAD_DIM, BLOCK), queries.dtype),
+        out_shape=[jax.ShapeDtypeStruct((tokens // BLOCK, HEAD_DIM, BLOCK), queries.dtype)] * heads,
         in_specs=[SMEM, ANY],
-        out_specs=VMEM,
+        out_specs=[VMEM] * heads,
         scratch_shapes=[pltpu.VMEM((tokens, heads * HEAD_DIM), queries.dtype), pltpu.SemaphoreType.DMA],
         compiler_params=params(MOST_VMEM_BYTES),
         cost_estimate=pl.CostEstimate(flops=0, bytes_accessed=queries.size // HEADS, transcendentals=0),
@@ -175,7 +175,7 @@
     return found
 
 
-def attend_kernel(c, n_src, entry, first, mode, guests, count_ref, live_ref, q_own, *refs):
+def attend_kernel(n_src, entry, first, mode, guests, count_ref, live_ref, q_own, *refs):
     n_kv = n_src
     guest_ref, refs = (refs[0], refs[1:]) if guests else (None, refs)
     kv_refs, refs = refs[:n_kv], refs[n_kv:]
@@ -188,14 +188,14 @@
         (*state, kv, q_ref, sems) = refs
     m_ref, l_ref, acc_ref = state
     blocks = kv.shape[0] // n_src
-    rows = q_own.shape[1]
+    rows = q_own.shape[0]
     copies = [
         pltpu.make_async_copy(kv_refs[s], kv.at[pl.ds(s * blocks, blocks)], sems.at[s]) for s in range(n_src)
     ]
     copies += [pltpu.make_async_copy(a, b, sems.at[n_src + i]) for i, (a, b) in enumerate(zip(state_in, state))]
-    copies.append(pltpu.make_async_copy(q_own.at[c], q_ref.at[pl.ds(0, rows)], sems.at[n_src + 3]))
+    copies.append(pltpu.make_async_copy(q_own, q_ref.at[pl.ds(0, rows)], sems.at[n_src + 3]))
     if guests:
-        copies.append(pltpu.make_async_copy(guest_ref.at[c], q_ref.at[pl.ds(rows, rows)], sems.at[n_src + 4]))
+        copies.append(pltpu.make_async_copy(guest_ref, q_ref.at[pl.ds(rows, rows)], sems.at[n_src + 4]))
     for copy in copies:
         copy.start()
     if first:
@@ -249,9 +249,9 @@
             part_ref[r, HEAD_DIM:] = jnp.concatenate(words).astype(part_ref.dtype)
 
 
-def attend(c, listed, q, guest, sources, state, mode, sets, name):
+def attend(listed, q, guest, sources, state, mode, sets, name):
     counts, entry, live = listed
-    rows, dtype = q.shape[1], q.dtype
+    rows, dtype = q.shape[0], q.dtype
     first = state is None
     state = () if first else tuple(state)
     stat = (sets * rows, 1, BLOCK)
@@ -271,7 +271,7 @@
         scratch += [pltpu.VMEM(shape, jnp.float32) for shape in shapes]
     scratch.append(pltpu.SemaphoreType.DMA((n_src + 5,)))
     return pl.pallas_call(
-        functools.partial(attend_kernel, c, n_src, entry, first, mode, bool(guests)),
+        functools.partial(attend_kernel, n_src, entry, first, mode, bool(guests)),
         out_shape=out_shape,
         in_specs=[SMEM, SMEM, ANY] + [ANY] * (len(guests) + n_src + len(state)),
         out_specs=[VMEM] * len(out_shape),
@@ -373,7 +373,7 @@
         mixed = [y if i == 0 else swap(y, 2 * i) for i, y in enumerate(x)]
         mixed = after(mixed, before)
         theirs = swap(jnp.stack([y[1] for y in mixed]), 1)
-        return jnp.concatenate([jnp.stack([y[0] for y in mixed]), theirs]), theirs
+        return jnp.concatenate([jnp.stack([y[0] for y in mixed]), theirs])
 
     def blocks(x):
         return x[:, : 2 * shard].reshape(n_ka * key_blocks, 2, BLOCK, HEAD_DIM)
@@ -384,20 +384,22 @@
     def flags(x):
         return x[:, : block_mask.shape[1], :rows].astype(jnp.int32).reshape(-1)
 
-    owns, over = [], []
+    parts = (block_mask.T,) + ((inward(block_mask.T),) if relay else ())
+    owns, over, guest = [], [], [None] * heads
     for c in range(heads):
-        packed = pack(after(me1, q) if c else me1, keys, values, None if c else block_mask.T, n_ka, heads, c)
+        place_of = after(me1, (q, owns[0])) if c else me1
+        packed = pack(place_of, keys, values, parts if c == heads - 1 else (), n_ka, heads, c)
         if c == 0:
             q = turn(after(me1, packed), queries, heads)
-            guest = inward(q) if relay else None
-            own, moved = sort(packed, q)
-            marks = own[:, 2 * shard :]
-            guest_marks = inward(marks) if relay else None
+            own = sort(packed, (q, parts))
         else:
-            own, moved = sort(after(packed, (moved, guest)), over[0])
+            own = sort(packed, over[0])
         owns.append(blocks(own))
-        own = after(owns[c], (over[0][1], guest_marks) if c else None)
-        over.append([exchange(own, odd, 1) for odd in (0, 1)])
+        over.append([exchange(after(owns[c], (over[0][1], guest[0]) if c else None), odd, 1) for odd in (0, 1)])
+        if relay:
+            guest[c] = inward(after(q[c], over[c]))
+    size = mask_rows(block_mask.shape[1])
+    masks = [flags(own[:, 2 * shard + i * size :]) for i in range(len(parts))]
 
     steps = [((0, False),)]
     for step in range(1, n_pb):
@@ -407,9 +409,6 @@
         elif found:
             steps.append(found)
     last = len(steps) - 1
-    masks = [flags(marks)]
-    if relay:
-        masks.append(flags(guest_marks))
     lists = plan(pb1, masks, steps, n_pb, n_ka, key_blocks, rows, relay)
     state = [None] * heads
 
@@ -417,7 +416,7 @@
         kind = "keep" if step < last else "send" if relay else "last"
         sources = [x for x in sources if x is not None]
         name = f"attend_{c}_{step}"
-        return attend(c, lists[step], q, guest, sources, state[c], kind, 2 if relay else 1, name)
+        return attend(lists[step], q[c], guest[c], sources, state[c], kind, 2 if relay else 1, name)
 
     for step in range(last):
         for c in range(heads):

time: 117 us -> 108 us (0.923)
  waiting for transfers between devices: 52.2 us -> 35.2 us
  starting transfers between devices: 38.5 us -> 46.2 us
    ppermute x2, waiting for transfers between devices: 17.3 us -> 7.1 us  [outward(): return lax.ppermute(x, 'pb', [(1, 0), (n_pb - 2, n_pb - 1)])]
    ppermute x2 -> x3, starting transfers between devices: 7.9 us -> 14.5 us  [inward(): return lax.ppermute(x, 'pb', [(0, 1), (n_pb - 1, n_pb - 2)])]
    ppermute x22, waiting for transfers between devices: 25.3 us -> 21.4 us  [swap(): return lax.ppermute(x, 'ka', [(i, i ^ k) for i in range(n_ka)])]
    ppermute x6, waiting for transfers between devices: 2.61 us -> 1.09 us  [exchange(): return lax.ppermute(x, 'pb', found) if found else None]
    ppermute x2 -> x3, waiting for transfers between devices: 6.97 us -> 5.52 us  [inward(): return lax.ppermute(x, 'pb', [(0, 1), (n_pb - 1, n_pb - 2)])]
  transfers between devices with their start and end apart: 32 -> 33, of which waited for: 18 -> 16; matrix products, arithmetic and copies ran while one was open for 1% -> 1% of each run, Pallas kernels for 16% -> 18%
where the time goes in v10:
time: 108 us; the launch traced here: 107 us
  starting transfers between devices  46.2 us (43%)
  waiting for transfers between devices  35.2 us (33%)
  Pallas kernels  23.3 us (22%)
  local copies, waits for them, and re-layouts  1.37 us (1%)
    ppermute x22, waiting for transfers between devices, swap(): return lax.ppermute(x, 'ka', [(i, i ^ k) for i in range(n_ka)])  21.4 us
    ppermute x22, starting transfers between devices, swap(): return lax.ppermute(x, 'ka', [(i, i ^ k) for i in range(n_ka)])  16.9 us
    ppermute x3, starting transfers between devices, inward(): return lax.ppermute(x, 'pb', [(0, 1), (n_pb - 1, n_pb - 2)])  14.5 us
    ppermute x6, starting transfers between devices, exchange(): return lax.ppermute(x, 'pb', found) if found else None  12.3 us
    pallas_call x4, Pallas kernels, attend(): pl.pallas_call(functools.partial(attend_kernel, n_src, entry, first, mode...  11 us
    ppermute x2, waiting for transfers between devices, outward(): return lax.ppermute(x, 'pb', [(1, 0), (n_pb - 2, n_pb - 1)])  7.1 us
    ppermute x3, waiting for transfers between devices, inward(): return lax.ppermute(x, 'pb', [(0, 1), (n_pb - 1, n_pb - 2)])  5.52 us
    pallas_call x2, Pallas kernels, pack(): pl.pallas_call(functools.partial(pack_kernel, n_ka, heads, c, len(masks))...  5.38 us
  transfers between devices with their start and end apart: 33, of which 16 were waited for; matrix products, arithmetic and copies ran while one was open for 1% of the time, Pallas kernels for 18%

profile of v10, /device:TPU:0, one launch (start us, length us, event | category | flops | bytes accessed | tf_op | source)
XLA Modules:
  0.0 107.2 jit_solution(8855783265564725458)
XLA Ops:
  0.0 2.3 %pack_0.1 = (bf16[2,256,128]{2,1,0:T(8,128)(2,1)}, bf16[2,256,128]{2,1,0:T(8,128)(2,1)}, bf16[2,256,128]{2,1,0:T(8,128)(2,1)}, bf16[2,256,128]{2,1,0:T(8,128)(2,1)}) custom-call(s32[1]{0:T(128)} %bitcast.me_ref, bf16[128,2048]{1,0:T(8,128)(2,1)} %refs_2_.1, bf16[128,2048]{1,0:T(8,128)(2,1)} %refs_3_.1), custom_call_target="tpu_custom_call" | custom-call | bytes 262144 | tf_op jit(solution)/shard_map/pack_0/pallas_call | solution.py:77
  2.3 3.0 %collective-permute-start = (bf16[2,256,128]{2,1,0:T(8,128)(2,1)}, bf16[2,256,128]{2,1,0:T(8,128)(2,1)S(1)}, u32[]{:S(2)}, u32[]{:S(2)}) collective-permute-start(bf16[2,256,128]{2,1,0:T(8,128)(2,1)} %get-tuple-element.50), channel_id=1, source_target_pairs={{0,2},{1,3},{2,0},{3,1},{4,6},{5,7},{6,4},{7,5},{8,10},{9,11},{10,... | collective-permute-start | bytes 393224 | tf_op jit(solution)/shard_map/ppermute | solution.py:351
  6.9 3.9 %collective-permute-start.3 = (s32[4,8]{1,0:T(4,128)}, s32[4,8]{1,0:T(4,128)S(1)}, u32[]{:S(2)}, u32[]{:S(2)}) collective-permute-start(s32[4,8]{1,0:T(4,128)} %bitcast.12), channel_id=1, source_target_pairs={{0,8},{24,16},{1,9},{25,17},{2,10},{26,18},{3,11},{27,19},{4,12},{... | collective-permute-start | bytes 392 | tf_op jit(solution)/shard_map/ppermute | solution.py:367
  10.8 2.0 %turn.1 = (bf16[8,128,128]{2,1,0:T(8,128)(2,1)}, bf16[8,128,128]{2,1,0:T(8,128)(2,1)}) custom-call(s32[1]{0:T(128)} %bitcast.me_ref, bf16[1024,2048]{1,0:T(8,128)(2,1)} %q_all.1), custom_call_target="tpu_custom_call" | custom-call | bytes 131072 | tf_op jit(solution)/shard_map/turn/pallas_call | solution.py:105
  15.9 4.4 %collective-permute-start.8 = (bf16[8,2,128,128]{3,2,1,0:T(8,128)(2,1)S(1)}, bf16[8,2,128,128]{3,2,1,0:T(8,128)(2,1)S(1)}, u32[]{:S(2)}, u32[]{:S(2)}) collective-permute-start(bf16[8,2,128,128]{3,2,1,0:T(8,128)(2,1)S(1)} %bitcast.10), channel_id=1, source_target_pairs={{0,8},{8,0},{16,24},{24,16},{1,9},{9,1},{17,25},{25,17},{2,10},{10... | collective-permute-start | bytes 1572872 | tf_op jit(solution)/shard_map/ppermute | solution.py:364
  20.4 3.1 %pack_1.1 = (bf16[2,288,128]{2,1,0:T(8,128)(2,1)}, bf16[2,288,128]{2,1,0:T(8,128)(2,1)}, bf16[2,288,128]{2,1,0:T(8,128)(2,1)}, bf16[2,288,128]{2,1,0:T(8,128)(2,1)}) custom-call(s32[1]{0:T(128)} %bitcast.me_ref, s32[4,8]{1,0:T(4,128)} %bitcast.13, s32[4,8]{1,0:T(4,128)} %copy-done.4, bf16[128,2048]{1,0:T(8,128)(2,1)} %refs_2_.1, bf16[128,2048]{1,0:T(8,128)(2,1)} %refs_3_.1), custom_call_target="tpu_custom_call" | custom-call | bytes 262144 | tf_op jit(solution)/shard_map/pack_1/pallas_call | solution.py:77
  27.0 3.1 %collective-permute-done.5 = bf16[2,288,128]{2,1,0:T(8,128)(2,1)S(1)} collective-permute-done((bf16[2,288,128]{2,1,0:T(8,128)(2,1)}, bf16[2,288,128]{2,1,0:T(8,128)(2,1)S(1)}, u32[]{:S(2)}, u32[]{:S(2)}) %collective-permute-start.5) | collective-permute-done | bytes 147488 | tf_op jit(solution)/shard_map/ppermute | solution.py:351
  30.1 3.1 %collective-permute-done.6 = bf16[2,288,128]{2,1,0:T(8,128)(2,1)S(1)} collective-permute-done((bf16[2,288,128]{2,1,0:T(8,128)(2,1)}, bf16[2,288,128]{2,1,0:T(8,128)(2,1)S(1)}, u32[]{:S(2)}, u32[]{:S(2)}) %collective-permute-start.6) | collective-permute-done | bytes 147488 | tf_op jit(solution)/shard_map/ppermute | solution.py:351
  34.4 2.7 %collective-permute-start.11 = (bf16[8,128,128]{2,1,0:T(8,128)(2,1)S(1)}, bf16[8,128,128]{2,1,0:T(8,128)(2,1)S(1)}, u32[]{:S(2)}, u32[]{:S(2)}) collective-permute-start(bf16[8,128,128]{2,1,0:T(8,128)(2,1)S(1)} %copy-done.1), channel_id=1, source_target_pairs={{0,8},{24,16},{1,9},{25,17},{2,10},{26,18},{3,11},{27,19},{4,12},{... | collective-permute-start | bytes 786440 | tf_op jit(solution)/shard_map/ppermute | solution.py:367
  38.7 4.6 %collective-permute-done.11.refs_0_ = bf16[8,128,128]{2,1,0:T(8,128)(2,1)S(1)} collective-permute-done((bf16[8,128,128]{2,1,0:T(8,128)(2,1)S(1)}, bf16[8,128,128]{2,1,0:T(8,128)(2,1)S(1)}, u32[]{:S(2)}, u32[]{:S(2)}) %collective-permute-start.11) | collective-permute-done | bytes 262176 | tf_op jit(solution)/shard_map/ppermute | solution.py:367
  44.8 3.4 %collective-permute-start.21 = (bf16[8,2,128,128]{3,2,1,0:T(8,128)(2,1)S(1)}, bf16[8,2,128,128]{3,2,1,0:T(8,128)(2,1)S(1)}, u32[]{:S(2)}, u32[]{:S(2)}) collective-permute-start(bf16[8,2,128,128]{3,2,1,0:T(8,128)(2,1)S(1)} %bitcast.7), channel_id=1, source_target_pairs={{0,8},{8,0},{16,24},{24,16},{1,9},{9,1},{17,25},{25,17},{2,10},{10... | collective-permute-start | bytes 1572872 | tf_op jit(solution)/shard_map/ppermute | solution.py:364
  49.1 2.4 %plan.1 = (s32[2]{0:T(128)S(1)}, s32[432]{0:T(512)S(1)}, s32[176]{0:T(256)S(1)}) custom-call(s32[1]{0:T(128)} %bitcast.2.pb_ref, s32[256]{0:T(256)S(1)} %reshape.24.refs_0_, s32[256]{0:T(256)S(1)} %reshape.26.refs_1_), custom_call_target="tpu_custom_call" | custom-call | tf_op jit(solution)/shard_map/plan/pallas_call | solution.py:159
  51.5 3.4 %attend_0_0.1 = (f32[16,1,128]{2,1,0:T(1,128)S(1)}, f32[16,1,128]{2,1,0:T(1,128)S(1)}, f32[16,128,128]{2,1,0:T(8,128)S(1)}) custom-call(s32[2]{0:T(128)S(1)} %get-tuple-element.69.count_ref, s32[432]{0:T(512)S(1)} %get-tuple-element.73.live_ref, bf16[8,128,128]{2,1,0:T(8,128)(2,1)S(1)} %copy-done.1, ...), custom_call_target="tpu_custom_call" | custom-call | bytes 16384 | tf_op jit(solution)/shard_map/attend_0_0/pallas_call | solution.py:273
  55.0 2.4 %attend_0_1.1 = (f32[16,1,128]{2,1,0:T(1,128)S(1)}, f32[16,1,128]{2,1,0:T(1,128)S(1)}, f32[16,128,128]{2,1,0:T(8,128)S(1)}, bf16[8,144,128]{2,1,0:T(8,128)(2,1)}) custom-call(s32[2]{0:T(128)S(1)} %get-tuple-element.69.count_ref, s32[176]{0:T(256)S(1)} %get-tuple-element.70.live_ref, bf16[8,128,128]{2,1,0:T(8,128)(2,1)S(1)} %copy-done.1, ...), custom_call_target="tpu_custom_call" | custom-call | bytes 16384 | tf_op jit(solution)/shard_map/attend_0_1/pallas_call | solution.py:273
  60.5 7.8 %collective-permute-start.23 = (bf16[8,128,128]{2,1,0:T(8,128)(2,1)S(1)}, bf16[8,128,128]{2,1,0:T(8,128)(2,1)S(1)}, u32[]{:S(2)}, u32[]{:S(2)}) collective-permute-start(bf16[8,128,128]{2,1,0:T(8,128)(2,1)S(1)} %copy-done), channel_id=1, source_target_pairs={{0,8},{24,16},{1,9},{25,17},{2,10},{26,18},{3,11},{27,19},{4,12},{... | collective-permute-start | bytes 786440 | tf_op jit(solution)/shard_map/ppermute | solution.py:367
  69.0 1.6 %collective-permute-start.17 = (bf16[1024,128]{1,0:T(8,128)(2,1)S(1)}, bf16[1024,128]{1,0:T(8,128)(2,1)S(1)}, u32[]{:S(2)}, u32[]{:S(2)}) collective-permute-start(bf16[1024,128]{1,0:T(8,128)(2,1)S(1)} %merge_0.1.refs_0_), channel_id=1, source_target_pairs={{0,4},{1,5},{2,6},{3,7},{4,0},{5,1},{6,2},{7,3},{8,12},{9,13},{10,... | collective-permute-start | bytes 786440 | tf_op jit(solution)/shard_map/ppermute | solution.py:351
  73.5 4.3 %attend_1_0.1 = (f32[16,1,128]{2,1,0:T(1,128)S(1)}, f32[16,1,128]{2,1,0:T(1,128)S(1)}, f32[16,128,128]{2,1,0:T(8,128)S(1)}) custom-call(s32[2]{0:T(128)S(1)} %get-tuple-element.69.count_ref, s32[432]{0:T(512)S(1)} %get-tuple-element.73.live_ref, bf16[8,128,128]{2,1,0:T(8,128)(2,1)S(1)} %copy-done, bf16[8,128,128]{2,1,0:T(8,128)(2,1)S(1)} %collective-permute-done.23.refs_0_, ...), custom_call_target="tpu_custom_call" | custom-call | bytes 16384 | tf_op jit(solution)/shard_map/attend_1_0/pallas_call | solution.py:273
  77.8 2.0 %collective-permute-done.15.refs_2_ = bf16[1024,128]{1,0:T(8,128)(2,1)S(1)} collective-permute-done((bf16[1024,128]{1,0:T(8,128)(2,1)S(1)}, bf16[1024,128]{1,0:T(8,128)(2,1)S(1)}, u32[]{:S(2)}, u32[]{:S(2)}) %collective-permute-start.15) | collective-permute-done | bytes 262176 | tf_op jit(solution)/shard_map/ppermute | solution.py:351
  80.7 2.3 %collective-permute-done.19.refs_6_ = bf16[1024,128]{1,0:T(8,128)(2,1)S(1)} collective-permute-done((bf16[1024,128]{1,0:T(8,128)(2,1)S(1)}, bf16[1024,128]{1,0:T(8,128)(2,1)S(1)}, u32[]{:S(2)}, u32[]{:S(2)}) %collective-permute-start.19) | collective-permute-done | bytes 262176 | tf_op jit(solution)/shard_map/ppermute | solution.py:351
  84.9 6.7 %collective-permute-done.25.part_ref = bf16[8,144,128]{2,1,0:T(8,128)(2,1)S(1)} collective-permute-done((bf16[8,144,128]{2,1,0:T(8,128)(2,1)S(1)}, bf16[8,144,128]{2,1,0:T(8,128)(2,1)S(1)}, u32[]{:S(2)}, u32[]{:S(2)}) %collective-permute-start.25) | collective-permute-done | bytes 294944 | tf_op jit(solution)/shard_map/ppermute | solution.py:370
  91.8 2.2 %collective-permute-start.31 = (bf16[1024,128]{1,0:T(8,128)(2,1)S(1)}, bf16[1024,128]{1,0:T(8,128)(2,1)S(1)}, u32[]{:S(2)}, u32[]{:S(2)}) collective-permute-start(bf16[1024,128]{1,0:T(8,128)(2,1)S(1)} %merge_1.1.refs_8_), channel_id=1, source_target_pairs={{0,6},{1,7},{2,4},{3,5},{4,2},{5,3},{6,0},{7,1},{8,14},{9,15},{10,... | collective-permute-start | bytes 786440 | tf_op jit(solution)/shard_map/ppermute | solution.py:351
  95.9 4.6 %collective-permute-done.31.refs_14_ = bf16[1024,128]{1,0:T(8,128)(2,1)S(1)} collective-permute-done((bf16[1024,128]{1,0:T(8,128)(2,1)S(1)}, bf16[1024,128]{1,0:T(8,128)(2,1)S(1)}, u32[]{:S(2)}, u32[]{:S(2)}) %collective-permute-start.31) | collective-permute-done | bytes 262176 | tf_op jit(solution)/shard_map/ppermute | solution.py:351
  100.5 2.7 %collective-permute-done.29.refs_12_ = bf16[1024,128]{1,0:T(8,128)(2,1)S(1)} collective-permute-done((bf16[1024,128]{1,0:T(8,128)(2,1)S(1)}, bf16[1024,128]{1,0:T(8,128)(2,1)S(1)}, u32[]{:S(2)}, u32[]{:S(2)}) %collective-permute-start.29) | collective-permute-done | bytes 262176 | tf_op jit(solution)/shard_map/ppermute | solution.py:351
  105.1 2.1 %place.1 = bf16[1024,2048]{1,0:T(8,128)(2,1)} custom-call(s32[1]{0:T(128)} %bitcast.me_ref, bf16[1024,128]{1,0:T(8,128)(2,1)S(1)} %merge_0.1.refs_0_, bf16[1024,128]{1,0:T(8,128)(2,1)S(1)} %collective-permute-done.14.refs_1_, bf16[1024,128]{1,0:T(8,128)(2,1)S(1)} %collective-permute-done.15.refs_2_, bf16[1024,128]{1,0:T(8,128)(2,1)S(1)} %collective-permute-done.16.refs_3_, ...), custom_call_target="tpu_custom_call" | custom-call | tf_op jit(solution)/shard_map/place/pallas_call | solution.py:330
  (79 shorter events, 26.5 us)
Async XLA Ops:
  2.3 10.5 %collective-permute-start = (bf16[2,256,128]{2,1,0:T(8,128)(2,1)}, bf16[2,256,128]{2,1,0:T(8,128)(2,1)S(1)}, u32[]{:S(2)}, u32[]{:S(2)}) collective-permute-start(bf16[2,256,128]{2,1,0:T(8,128)(2,1)} %get-tuple-element.50), channel_id=1, source_target_pairs={{0,2},{1,3},{2,0},{3,1},{4,6},{5,7},{6,4},{7,5},{8,10},{9,11},{10,... | collective-permute-start | bytes 393224 | tf_op jit(solution)/shard_map/ppermute | solution.py:351
  5.3 8.0 %collective-permute-start.1 = (bf16[2,256,128]{2,1,0:T(8,128)(2,1)}, bf16[2,256,128]{2,1,0:T(8,128)(2,1)S(1)}, u32[]{:S(2)}, u32[]{:S(2)}) collective-permute-start(bf16[2,256,128]{2,1,0:T(8,128)(2,1)} %get-tuple-element.51), channel_id=1, source_target_pairs={{0,4},{1,5},{2,6},{3,7},{4,0},{5,1},{6,2},{7,3},{8,12},{9,13},{10,... | collective-permute-start | bytes 393224 | tf_op jit(solution)/shard_map/ppermute | solution.py:351
  15.1 18.1 %collective-permute-start.9 = (bf16[8,2,128,128]{3,2,1,0:T(8,128)(2,1)S(1)}, bf16[8,2,128,128]{3,2,1,0:T(8,128)(2,1)S(1)}, u32[]{:S(2)}, u32[]{:S(2)}) collective-permute-start(bf16[8,2,128,128]{3,2,1,0:T(8,128)(2,1)S(1)} %bitcast.9), channel_id=1, source_target_pairs={{8,16},{16,8},{9,17},{17,9},{10,18},{18,10},{11,19},{19,11},{12,20... | collective-permute-start | bytes 1572872 | tf_op jit(solution)/shard_map/ppermute | solution.py:364
  15.9 17.3 %collective-permute-start.8 = (bf16[8,2,128,128]{3,2,1,0:T(8,128)(2,1)S(1)}, bf16[8,2,128,128]{3,2,1,0:T(8,128)(2,1)S(1)}, u32[]{:S(2)}, u32[]{:S(2)}) collective-permute-start(bf16[8,2,128,128]{3,2,1,0:T(8,128)(2,1)S(1)} %bitcast.10), channel_id=1, source_target_pairs={{0,8},{8,0},{16,24},{24,16},{1,9},{9,1},{17,25},{25,17},{2,10},{10... | collective-permute-start | bytes 1572872 | tf_op jit(solution)/shard_map/ppermute | solution.py:364
  24.7 8.5 %collective-permute-start.6 = (bf16[2,288,128]{2,1,0:T(8,128)(2,1)}, bf16[2,288,128]{2,1,0:T(8,128)(2,1)S(1)}, u32[]{:S(2)}, u32[]{:S(2)}) collective-permute-start(bf16[2,288,128]{2,1,0:T(8,128)(2,1)} %get-tuple-element.63), channel_id=1, source_target_pairs={{0,4},{1,5},{2,6},{3,7},{4,0},{5,1},{6,2},{7,3},{8,12},{9,13},{10,... | collective-permute-start | bytes 442376 | tf_op jit(solution)/shard_map/ppermute | solution.py:351
  34.4 8.9 %collective-permute-start.11 = (bf16[8,128,128]{2,1,0:T(8,128)(2,1)S(1)}, bf16[8,128,128]{2,1,0:T(8,128)(2,1)S(1)}, u32[]{:S(2)}, u32[]{:S(2)}) collective-permute-start(bf16[8,128,128]{2,1,0:T(8,128)(2,1)S(1)} %copy-done.1), channel_id=1, source_target_pairs={{0,8},{24,16},{1,9},{25,17},{2,10},{26,18},{3,11},{27,19},{4,12},{... | collective-permute-start | bytes 786440 | tf_op jit(solution)/shard_map/ppermute | solution.py:367
  37.1 17.8 %collective-permute-start.12 = (bf16[8,2,128,128]{3,2,1,0:T(8,128)(2,1)S(1)}, bf16[8,2,128,128]{3,2,1,0:T(8,128)(2,1)}, u32[]{:S(2)}, u32[]{:S(2)}) collective-permute-start(bf16[8,2,128,128]{3,2,1,0:T(8,128)(2,1)S(1)} %collective-permute-done.8.refs_2_), channel_id=1, source_target_pairs={{8,16},{16,8},{9,17},{17,9},{10,18},{18,10},{11,19},{19,11},{12,20... | collective-permute-start | bytes 1572872 | tf_op jit(solution)/shard_map/ppermute | solution.py:364
  43.3 15.4 %collective-permute-start.22 = (bf16[8,2,128,128]{3,2,1,0:T(8,128)(2,1)S(1)}, bf16[8,2,128,128]{3,2,1,0:T(8,128)(2,1)}, u32[]{:S(2)}, u32[]{:S(2)}) collective-permute-start(bf16[8,2,128,128]{3,2,1,0:T(8,128)(2,1)S(1)} %bitcast.6), channel_id=1, source_target_pairs={{8,16},{16,8},{9,17},{17,9},{10,18},{18,10},{11,19},{19,11},{12,20... | collective-permute-start | bytes 1572872 | tf_op jit(solution)/shard_map/ppermute | solution.py:364
  44.8 15.1 %collective-permute-start.21 = (bf16[8,2,128,128]{3,2,1,0:T(8,128)(2,1)S(1)}, bf16[8,2,128,128]{3,2,1,0:T(8,128)(2,1)S(1)}, u32[]{:S(2)}, u32[]{:S(2)}) collective-permute-start(bf16[8,2,128,128]{3,2,1,0:T(8,128)(2,1)S(1)} %bitcast.7), channel_id=1, source_target_pairs={{0,8},{8,0},{16,24},{24,16},{1,9},{9,1},{17,25},{25,17},{2,10},{10... | collective-permute-start | bytes 1572872 | tf_op jit(solution)/shard_map/ppermute | solution.py:364
  57.4 11.4 %collective-permute-start.13 = (bf16[8,144,128]{2,1,0:T(8,128)(2,1)}, bf16[8,144,128]{2,1,0:T(8,128)(2,1)S(1)}, u32[]{:S(2)}, u32[]{:S(2)}) collective-permute-start(bf16[8,144,128]{2,1,0:T(8,128)(2,1)} %get-tuple-element.80), channel_id=1, source_target_pairs={{8,0},{16,24},{9,1},{17,25},{10,2},{18,26},{11,3},{19,27},{12,4},{... | collective-permute-start | bytes 884744 | tf_op jit(solution)/shard_map/ppermute | solution.py:370
  59.8 20.0 %collective-permute-start.24 = (bf16[8,2,128,128]{3,2,1,0:T(8,128)(2,1)S(1)}, bf16[8,2,128,128]{3,2,1,0:T(8,128)(2,1)S(1)}, u32[]{:S(2)}, u32[]{:S(2)}) collective-permute-start(bf16[8,2,128,128]{3,2,1,0:T(8,128)(2,1)S(1)} %collective-permute-done.21.refs_2_), channel_id=1, source_target_pairs={{8,16},{16,8},{9,17},{17,9},{10,18},{18,10},{11,19},{19,11},{12,20... | collective-permute-start | bytes 1572872 | tf_op jit(solution)/shard_map/ppermute | solution.py:364
  60.5 12.9 %collective-permute-start.23 = (bf16[8,128,128]{2,1,0:T(8,128)(2,1)S(1)}, bf16[8,128,128]{2,1,0:T(8,128)(2,1)S(1)}, u32[]{:S(2)}, u32[]{:S(2)}) collective-permute-start(bf16[8,128,128]{2,1,0:T(8,128)(2,1)S(1)} %copy-done), channel_id=1, source_target_pairs={{0,8},{24,16},{1,9},{25,17},{2,10},{26,18},{3,11},{27,19},{4,12},{... | collective-permute-start | bytes 786440 | tf_op jit(solution)/shard_map/ppermute | solution.py:367
  69.0 8.8 %collective-permute-start.17 = (bf16[1024,128]{1,0:T(8,128)(2,1)S(1)}, bf16[1024,128]{1,0:T(8,128)(2,1)S(1)}, u32[]{:S(2)}, u32[]{:S(2)}) collective-permute-start(bf16[1024,128]{1,0:T(8,128)(2,1)S(1)} %merge_0.1.refs_0_), channel_id=1, source_target_pairs={{0,4},{1,5},{2,6},{3,7},{4,0},{5,1},{6,2},{7,3},{8,12},{9,13},{10,... | collective-permute-start | bytes 786440 | tf_op jit(solution)/shard_map/ppermute | solution.py:351
  70.6 9.2 %collective-permute-start.15 = (bf16[1024,128]{1,0:T(8,128)(2,1)S(1)}, bf16[1024,128]{1,0:T(8,128)(2,1)S(1)}, u32[]{:S(2)}, u32[]{:S(2)}) collective-permute-start(bf16[1024,128]{1,0:T(8,128)(2,1)S(1)} %merge_0.1.refs_0_), channel_id=1, source_target_pairs={{0,2},{1,3},{2,0},{3,1},{4,6},{5,7},{6,4},{7,5},{8,10},{9,11},{10,... | collective-permute-start | bytes 786440 | tf_op jit(solution)/shard_map/ppermute | solution.py:351
  71.8 11.2 %collective-permute-start.19 = (bf16[1024,128]{1,0:T(8,128)(2,1)S(1)}, bf16[1024,128]{1,0:T(8,128)(2,1)S(1)}, u32[]{:S(2)}, u32[]{:S(2)}) collective-permute-start(bf16[1024,128]{1,0:T(8,128)(2,1)S(1)} %merge_0.1.refs_0_), channel_id=1, source_target_pairs={{0,6},{1,7},{2,4},{3,5},{4,2},{5,3},{6,0},{7,1},{8,14},{9,15},{10,... | collective-permute-start | bytes 786440 | tf_op jit(solution)/shard_map/ppermute | solution.py:351
  83.0 8.6 %collective-permute-start.25 = (bf16[8,144,128]{2,1,0:T(8,128)(2,1)S(1)}, bf16[8,144,128]{2,1,0:T(8,128)(2,1)S(1)}, u32[]{:S(2)}, u32[]{:S(2)}) collective-permute-start(bf16[8,144,128]{2,1,0:T(8,128)(2,1)S(1)} %get-tuple-element.92), channel_id=1, source_target_pairs={{8,0},{16,24},{9,1},{17,25},{10,2},{18,26},{11,3},{19,27},{12,4},{... | collective-permute-start | bytes 884744 | tf_op jit(solution)/shard_map/ppermute | solution.py:370
  84.3 10.3 %collective-permute-start.14 = (bf16[1024,128]{1,0:T(8,128)(2,1)S(1)}, bf16[1024,128]{1,0:T(8,128)(2,1)S(1)}, u32[]{:S(2)}, u32[]{:S(2)}) collective-permute-start(bf16[1024,128]{1,0:T(8,128)(2,1)S(1)} %merge_0.1.refs_0_), channel_id=1, source_target_pairs={{0,1},{1,0},{2,3},{3,2},{4,5},{5,4},{6,7},{7,6},{8,9},{9,8},{10,11... | collective-permute-start | bytes 786440 | tf_op jit(solution)/shard_map/ppermute | solution.py:351
  84.4 11.0 %collective-permute-start.20 = (bf16[1024,128]{1,0:T(8,128)(2,1)S(1)}, bf16[1024,128]{1,0:T(8,128)(2,1)S(1)}, u32[]{:S(2)}, u32[]{:S(2)}) collective-permute-start(bf16[1024,128]{1,0:T(8,128)(2,1)S(1)} %collective-permute-done.19.refs_6_), channel_id=1, source_target_pairs={{0,1},{1,0},{2,3},{3,2},{4,5},{5,4},{6,7},{7,6},{8,9},{9,8},{10,11... | collective-permute-start | bytes 786440 | tf_op jit(solution)/shard_map/ppermute | solution.py:351
  84.9 10.5 %collective-permute-start.18 = (bf16[1024,128]{1,0:T(8,128)(2,1)S(1)}, bf16[1024,128]{1,0:T(8,128)(2,1)S(1)}, u32[]{:S(2)}, u32[]{:S(2)}) collective-permute-start(bf16[1024,128]{1,0:T(8,128)(2,1)S(1)} %collective-permute-done.17.refs_4_), channel_id=1, source_target_pairs={{0,1},{1,0},{2,3},{3,2},{4,5},{5,4},{6,7},{7,6},{8,9},{9,8},{10,11... | collective-permute-start | bytes 786440 | tf_op jit(solution)/shard_map/ppermute | solution.py:351
  91.8 8.7 %collective-permute-start.31 = (bf16[1024,128]{1,0:T(8,128)(2,1)S(1)}, bf16[1024,128]{1,0:T(8,128)(2,1)S(1)}, u32[]{:S(2)}, u32[]{:S(2)}) collective-permute-start(bf16[1024,128]{1,0:T(8,128)(2,1)S(1)} %merge_1.1.refs_8_), channel_id=1, source_target_pairs={{0,6},{1,7},{2,4},{3,5},{4,2},{5,3},{6,0},{7,1},{8,14},{9,15},{10,... | collective-permute-start | bytes 786440 | tf_op jit(solution)/shard_map/ppermute | solution.py:351
  94.0 9.1 %collective-permute-start.29 = (bf16[1024,128]{1,0:T(8,128)(2,1)S(1)}, bf16[1024,128]{1,0:T(8,128)(2,1)S(1)}, u32[]{:S(2)}, u32[]{:S(2)}) collective-permute-start(bf16[1024,128]{1,0:T(8,128)(2,1)S(1)} %merge_1.1.refs_8_), channel_id=1, source_target_pairs={{0,4},{1,5},{2,6},{3,7},{4,0},{5,1},{6,2},{7,3},{8,12},{9,13},{10,... | collective-permute-start | bytes 786440 | tf_op jit(solution)/shard_map/ppermute | solution.py:351
  94.6 8.8 %collective-permute-start.27 = (bf16[1024,128]{1,0:T(8,128)(2,1)S(1)}, bf16[1024,128]{1,0:T(8,128)(2,1)S(1)}, u32[]{:S(2)}, u32[]{:S(2)}) collective-permute-start(bf16[1024,128]{1,0:T(8,128)(2,1)S(1)} %merge_1.1.refs_8_), channel_id=1, source_target_pairs={{0,2},{1,3},{2,0},{3,1},{4,6},{5,7},{6,4},{7,5},{8,10},{9,11},{10,... | collective-permute-start | bytes 786440 | tf_op jit(solution)/shard_map/ppermute | solution.py:351
  95.4 8.3 %collective-permute-start.16 = (bf16[1024,128]{1,0:T(8,128)(2,1)S(1)}, bf16[1024,128]{1,0:T(8,128)(2,1)S(1)}, u32[]{:S(2)}, u32[]{:S(2)}) collective-permute-start(bf16[1024,128]{1,0:T(8,128)(2,1)S(1)} %collective-permute-done.15.refs_2_), channel_id=1, source_target_pairs={{0,1},{1,0},{2,3},{3,2},{4,5},{5,4},{6,7},{7,6},{8,9},{9,8},{10,11... | collective-permute-start | bytes 786440 | tf_op jit(solution)/shard_map/ppermute | solution.py:351
  95.4 8.3 %collective-permute-start.26 = (bf16[1024,128]{1,0:T(8,128)(2,1)S(1)}, bf16[1024,128]{1,0:T(8,128)(2,1)S(1)}, u32[]{:S(2)}, u32[]{:S(2)}) collective-permute-start(bf16[1024,128]{1,0:T(8,128)(2,1)S(1)} %merge_1.1.refs_8_), channel_id=1, source_target_pairs={{0,1},{1,0},{2,3},{3,2},{4,5},{5,4},{6,7},{7,6},{8,9},{9,8},{10,11... | collective-permute-start | bytes 786440 | tf_op jit(solution)/shard_map/ppermute | solution.py:351
  (14 other events, 128.7 us)

commit v11 on v10

--- a/solution.py
+++ b/solution.py
@@ -395,9 +395,11 @@
         else:
             own = sort(packed, over[0])
         owns.append(blocks(own))
-        over.append([exchange(after(owns[c], (over[0][1], guest[0]) if c else None), odd, 1) for odd in (0, 1)])
+        even = exchange(owns[c], 0, 1)
+        odd = exchange(after(owns[c], (over[0], even) if c else None), 1, 1)
+        over.append([even, odd])
         if relay:
-            guest[c] = inward(after(q[c], over[c]))
+            guest[c] = inward(after(q[c], even if c else over[0]))
     size = mask_rows(block_mask.shape[1])
     masks = [flags(own[:, 2 * shard + i * size :]) for i in range(len(parts))]
 
@@ -409,6 +411,10 @@
         elif found:
             steps.append(found)
     last = len(steps) - 1
+    late = relay and last == 1
+    if late:
+        (own_source, even_source, odd_source), far_sources = steps
+        steps += [(own_source, even_source), (odd_source,) + far_sources]
     lists = plan(pb1, masks, steps, n_pb, n_ka, key_blocks, rows, relay)
     state = [None] * heads
 
@@ -416,15 +422,23 @@
         kind = "keep" if step < last else "send" if relay else "last"
         sources = [x for x in sources if x is not None]
         name = f"attend_{c}_{step}"
-        return attend(lists[step], q[c], guest[c], sources, state[c], kind, 2 if relay else 1, name)
-
+        listed = lists[step + (2 if late and c else 0)]
+        seen = None if late and c and step == 0 else guest[c]
+        return attend(listed, q[c], seen, sources, state[c], kind, 2 if relay else 1, name)
+
+    if late and heads > 1:
+        guest[0] = after(guest[0], over[1][0])
     for step in range(last):
         for c in range(heads):
             sources = ([owns[c]] if step == 0 else []) + over[c]
             even, odd = over[c]
-            if even is not None and odd is not None:
-                even, odd = lax.optimization_barrier((even, odd))
-            over[c] = [exchange(odd, 0, step + 2), exchange(even, 1, step + 2)]
+            if late and c:
+                sources = sources[:2]
+                over[c] = [odd, exchange(even, 1, step + 2)]
+            else:
+                if even is not None and odd is not None:
+                    even, odd = lax.optimization_barrier((even, odd))
+                over[c] = [exchange(odd, 0, step + 2), exchange(even, 1, step + 2)]
             state[c] = run(c, step, sources)
 
     pieces = []

time: 108 us -> 114 us (1.056)
  waiting for transfers between devices: 35.2 us -> 46.7 us
  starting transfers between devices: 46.2 us -> 37.9 us
  Pallas kernels: 23.3 us -> 25.4 us
    ppermute x2, waiting for transfers between devices: 7.1 us -> 17.7 us  [outward(): return lax.ppermute(x, 'pb', [(1, 0), (n_pb - 2, n_pb - 1)])]
    ppermute x6, waiting for transfers between devices: 1.09 us -> 7.66 us  [exchange(): return lax.ppermute(x, 'pb', found) if found else None]
    ppermute x3, waiting for transfers between devices: 5.52 us -> 0.01 us  [inward(): return lax.ppermute(x, 'pb', [(0, 1), (n_pb - 1, n_pb - 2)])]
    ppermute x3, starting transfers between devices: 14.5 us -> 9.31 us  [inward(): return lax.ppermute(x, 'pb', [(0, 1), (n_pb - 1, n_pb - 2)])]
    ppermute x6, starting transfers between devices: 12.3 us -> 8.95 us  [exchange(): return lax.ppermute(x, 'pb', found) if found else None]
    pallas_call x1, Pallas kernels: 2.37 us -> 3.65 us  [plan(): pl.pallas_call(functools.partial(plan_kernel, steps, n_pb, n_slots, key_b...]
  transfers between devices with their start and end apart: 33 -> 33, of which waited for: 16 -> 14; matrix products, arithmetic and copies ran while one was open for 1% -> 1% of each run, Pallas kernels for 18% -> 19%
where the time goes in v11:
time: 114 us; the launch traced here: 113 us
  waiting for transfers between devices  46.7 us (41%)
  starting transfers between devices  37.9 us (33%)
  Pallas kernels  25.4 us (22%)
  local copies, waits for them, and re-layouts  1.37 us (1%)
    ppermute x22, waiting for transfers between devices, swap(): return lax.ppermute(x, 'ka', [(i, i ^ k) for i in range(n_ka)])  21.4 us
    ppermute x2, waiting for transfers between devices, outward(): return lax.ppermute(x, 'pb', [(1, 0), (n_pb - 2, n_pb - 1)])  17.7 us
    ppermute x22, starting transfers between devices, swap(): return lax.ppermute(x, 'ka', [(i, i ^ k) for i in range(n_ka)])  17.1 us
    pallas_call x4, Pallas kernels, attend(): pl.pallas_call(functools.partial(attend_kernel, n_src, entry, first, mode...  11 us
    ppermute x3, starting transfers between devices, inward(): return lax.ppermute(x, 'pb', [(0, 1), (n_pb - 1, n_pb - 2)])  9.31 us
    ppermute x6, starting transfers between devices, exchange(): return lax.ppermute(x, 'pb', found) if found else None  8.95 us
    ppermute x6, waiting for transfers between devices, exchange(): return lax.ppermute(x, 'pb', found) if found else None  7.66 us
    pallas_call x2, Pallas kernels, pack(): pl.pallas_call(functools.partial(pack_kernel, n_ka, heads, c, len(masks))...  5.31 us
  transfers between devices with their start and end apart: 33, of which 14 were waited for; matrix products, arithmetic and copies ran while one was open for 1% of the time, Pallas kernels for 19%

profile of v11, /device:TPU:0, one launch (start us, length us, event | category | flops | bytes accessed | tf_op | source)
XLA Modules:
  0.0 112.6 jit_solution(6520294663993309912)
XLA Ops:
  0.0 2.3 %pack_0.1 = (bf16[2,256,128]{2,1,0:T(8,128)(2,1)}, bf16[2,256,128]{2,1,0:T(8,128)(2,1)}, bf16[2,256,128]{2,1,0:T(8,128)(2,1)}, bf16[2,256,128]{2,1,0:T(8,128)(2,1)}) custom-call(s32[1]{0:T(128)} %bitcast.me_ref, bf16[128,2048]{1,0:T(8,128)(2,1)} %refs_2_.1, bf16[128,2048]{1,0:T(8,128)(2,1)} %refs_3_.1), custom_call_target="tpu_custom_call" | custom-call | bytes 262144 | tf_op jit(solution)/shard_map/pack_0/pallas_call | solution.py:77
  2.3 3.0 %collective-permute-start = (bf16[2,256,128]{2,1,0:T(8,128)(2,1)}, bf16[2,256,128]{2,1,0:T(8,128)(2,1)S(1)}, u32[]{:S(2)}, u32[]{:S(2)}) collective-permute-start(bf16[2,256,128]{2,1,0:T(8,128)(2,1)} %get-tuple-element.53), channel_id=1, source_target_pairs={{0,2},{1,3},{2,0},{3,1},{4,6},{5,7},{6,4},{7,5},{8,10},{9,11},{10,... | collective-permute-start | bytes 393224 | tf_op jit(solution)/shard_map/ppermute | solution.py:351
  6.8 3.9 %collective-permute-start.3 = (s32[4,8]{1,0:T(4,128)}, s32[4,8]{1,0:T(4,128)S(1)}, u32[]{:S(2)}, u32[]{:S(2)}) collective-permute-start(s32[4,8]{1,0:T(4,128)} %bitcast.12), channel_id=1, source_target_pairs={{0,8},{24,16},{1,9},{25,17},{2,10},{26,18},{3,11},{27,19},{4,12},{... | collective-permute-start | bytes 392 | tf_op jit(solution)/shard_map/ppermute | solution.py:367
  10.8 2.0 %turn.1 = (bf16[8,128,128]{2,1,0:T(8,128)(2,1)}, bf16[8,128,128]{2,1,0:T(8,128)(2,1)}) custom-call(s32[1]{0:T(128)} %bitcast.me_ref, bf16[1024,2048]{1,0:T(8,128)(2,1)} %q_all.1), custom_call_target="tpu_custom_call" | custom-call | bytes 131072 | tf_op jit(solution)/shard_map/turn/pallas_call | solution.py:105
  15.8 4.4 %collective-permute-start.8 = (bf16[8,2,128,128]{3,2,1,0:T(8,128)(2,1)S(1)}, bf16[8,2,128,128]{3,2,1,0:T(8,128)(2,1)}, u32[]{:S(2)}, u32[]{:S(2)}) collective-permute-start(bf16[8,2,128,128]{3,2,1,0:T(8,128)(2,1)S(1)} %bitcast.10), channel_id=1, source_target_pairs={{0,8},{8,0},{16,24},{24,16},{1,9},{9,1},{17,25},{25,17},{2,10},{10... | collective-permute-start | bytes 1572872 | tf_op jit(solution)/shard_map/ppermute | solution.py:364
  20.2 3.0 %pack_1.1 = (bf16[2,288,128]{2,1,0:T(8,128)(2,1)}, bf16[2,288,128]{2,1,0:T(8,128)(2,1)}, bf16[2,288,128]{2,1,0:T(8,128)(2,1)}, bf16[2,288,128]{2,1,0:T(8,128)(2,1)}) custom-call(s32[1]{0:T(128)} %bitcast.me_ref, s32[4,8]{1,0:T(4,128)} %bitcast.13, s32[4,8]{1,0:T(4,128)} %copy-done.4, bf16[128,2048]{1,0:T(8,128)(2,1)} %refs_2_.1, bf16[128,2048]{1,0:T(8,128)(2,1)} %refs_3_.1), custom_call_target="tpu_custom_call" | custom-call | bytes 262144 | tf_op jit(solution)/shard_map/pack_1/pallas_call | solution.py:77
  26.8 3.1 %collective-permute-done.5 = bf16[2,288,128]{2,1,0:T(8,128)(2,1)S(1)} collective-permute-done((bf16[2,288,128]{2,1,0:T(8,128)(2,1)}, bf16[2,288,128]{2,1,0:T(8,128)(2,1)S(1)}, u32[]{:S(2)}, u32[]{:S(2)}) %collective-permute-start.5) | collective-permute-done | bytes 147488 | tf_op jit(solution)/shard_map/ppermute | solution.py:351
  29.9 3.1 %collective-permute-done.6 = bf16[2,288,128]{2,1,0:T(8,128)(2,1)S(1)} collective-permute-done((bf16[2,288,128]{2,1,0:T(8,128)(2,1)}, bf16[2,288,128]{2,1,0:T(8,128)(2,1)S(1)}, u32[]{:S(2)}, u32[]{:S(2)}) %collective-permute-start.6) | collective-permute-done | bytes 147488 | tf_op jit(solution)/shard_map/ppermute | solution.py:351
  34.2 1.6 %collective-permute-done.10 = bf16[4,288,128]{2,1,0:T(8,128)(2,1)S(1)} collective-permute-done((bf16[4,288,128]{2,1,0:T(8,128)(2,1)S(1)}, bf16[4,288,128]{2,1,0:T(8,128)(2,1)S(1)}, u32[]{:S(2)}, u32[]{:S(2)}) %collective-permute-start.10) | collective-permute-done | bytes 294944 | tf_op jit(solution)/shard_map/ppermute | solution.py:351
  38.3 3.9 %collective-permute-start.11 = (bf16[8,128,128]{2,1,0:T(8,128)(2,1)S(1)}, bf16[8,128,128]{2,1,0:T(8,128)(2,1)S(1)}, u32[]{:S(2)}, u32[]{:S(2)}) collective-permute-start(bf16[8,128,128]{2,1,0:T(8,128)(2,1)S(1)} %copy-done.1), channel_id=1, source_target_pairs={{0,8},{24,16},{1,9},{25,17},{2,10},{26,18},{3,11},{27,19},{4,12},{... | collective-permute-start | bytes 786440 | tf_op jit(solution)/shard_map/ppermute | solution.py:367
  42.3 7.6 %collective-permute-done.12.refs_1_ = bf16[8,2,128,128]{3,2,1,0:T(8,128)(2,1)S(1)} collective-permute-done((bf16[8,2,128,128]{3,2,1,0:T(8,128)(2,1)S(1)}, bf16[8,2,128,128]{3,2,1,0:T(8,128)(2,1)S(1)}, u32[]{:S(2)}, u32[]{:S(2)}) %collective-permute-start.12) | collective-permute-done | bytes 524320 | tf_op jit(solution)/shard_map/ppermute | solution.py:364
  51.5 3.7 %plan.1 = (s32[4]{0:T(128)S(1)}, s32[432]{0:T(512)S(1)}, s32[176]{0:T(256)S(1)}, s32[304]{0:T(512)S(1)}, s32[304]{0:T(512)S(1)}) custom-call(s32[1]{0:T(128)} %bitcast.2.pb_ref, s32[256]{0:T(256)S(1)} %reshape.24.refs_0_, s32[256]{0:T(256)S(1)} %reshape.26.refs_1_), custom_call_target="tpu_custom_call" | custom-call | tf_op jit(solution)/shard_map/plan/pallas_call | solution.py:159
  55.2 4.3 %attend_0_0.1 = (f32[16,1,128]{2,1,0:T(1,128)S(1)}, f32[16,1,128]{2,1,0:T(1,128)S(1)}, f32[16,128,128]{2,1,0:T(8,128)S(1)}) custom-call(s32[4]{0:T(128)S(1)} %get-tuple-element.72.count_ref, s32[432]{0:T(512)S(1)} %get-tuple-element.77.live_ref, bf16[8,128,128]{2,1,0:T(8,128)(2,1)S(1)} %copy-done.1, ...), custom_call_target="tpu_custom_call" | custom-call | bytes 16384 | tf_op jit(solution)/shard_map/attend_0_0/pallas_call | solution.py:273
  59.5 2.4 %attend_0_1.1 = (f32[16,1,128]{2,1,0:T(1,128)S(1)}, f32[16,1,128]{2,1,0:T(1,128)S(1)}, f32[16,128,128]{2,1,0:T(8,128)S(1)}, bf16[8,144,128]{2,1,0:T(8,128)(2,1)}) custom-call(s32[4]{0:T(128)S(1)} %get-tuple-element.72.count_ref, s32[176]{0:T(256)S(1)} %get-tuple-element.73.live_ref, bf16[8,128,128]{2,1,0:T(8,128)(2,1)S(1)} %copy-done.1, ...), custom_call_target="tpu_custom_call" | custom-call | bytes 16384 | tf_op jit(solution)/shard_map/attend_0_1/pallas_call | solution.py:273
  64.0 11.0 %collective-permute-done.14.part_ref = bf16[8,144,128]{2,1,0:T(8,128)(2,1)} collective-permute-done((bf16[8,144,128]{2,1,0:T(8,128)(2,1)}, bf16[8,144,128]{2,1,0:T(8,128)(2,1)}, u32[]{:S(2)}, u32[]{:S(2)}) %collective-permute-start.14) | collective-permute-done | bytes 294944 | tf_op jit(solution)/shard_map/ppermute | solution.py:370
  76.1 1.6 %collective-permute-start.18 = (bf16[1024,128]{1,0:T(8,128)(2,1)S(1)}, bf16[1024,128]{1,0:T(8,128)(2,1)S(1)}, u32[]{:S(2)}, u32[]{:S(2)}) collective-permute-start(bf16[1024,128]{1,0:T(8,128)(2,1)S(1)} %merge_0.1.refs_0_), channel_id=1, source_target_pairs={{0,4},{1,5},{2,6},{3,7},{4,0},{5,1},{6,2},{7,3},{8,12},{9,13},{10,... | collective-permute-start | bytes 786440 | tf_op jit(solution)/shard_map/ppermute | solution.py:351
  81.2 3.4 %attend_1_0.1 = (f32[16,1,128]{2,1,0:T(1,128)S(1)}, f32[16,1,128]{2,1,0:T(1,128)S(1)}, f32[16,128,128]{2,1,0:T(8,128)S(1)}) custom-call(s32[4]{0:T(128)S(1)} %get-tuple-element.72.count_ref, s32[304]{0:T(512)S(1)} %get-tuple-element.90.live_ref, bf16[8,128,128]{2,1,0:T(8,128)(2,1)S(1)} %copy-done, bf16[8,2,128,128]{3,2,1,0:T(8,128)(2,1)S(1)} %bitcast.8, ...), custom_call_target="tpu_custom_call" | custom-call | bytes 16384 | tf_op jit(solution)/shard_map/attend_1_0/pallas_call | solution.py:273
  84.6 1.5 %collective-permute-done.16.refs_2_ = bf16[1024,128]{1,0:T(8,128)(2,1)S(1)} collective-permute-done((bf16[1024,128]{1,0:T(8,128)(2,1)S(1)}, bf16[1024,128]{1,0:T(8,128)(2,1)S(1)}, u32[]{:S(2)}, u32[]{:S(2)}) %collective-permute-start.16) | collective-permute-done | bytes 262176 | tf_op jit(solution)/shard_map/ppermute | solution.py:351
  87.1 2.3 %collective-permute-done.20.refs_6_ = bf16[1024,128]{1,0:T(8,128)(2,1)S(1)} collective-permute-done((bf16[1024,128]{1,0:T(8,128)(2,1)S(1)}, bf16[1024,128]{1,0:T(8,128)(2,1)S(1)}, u32[]{:S(2)}, u32[]{:S(2)}) %collective-permute-start.20) | collective-permute-done | bytes 262176 | tf_op jit(solution)/shard_map/ppermute | solution.py:351
  91.3 6.7 %collective-permute-done.25.part_ref = bf16[8,144,128]{2,1,0:T(8,128)(2,1)S(1)} collective-permute-done((bf16[8,144,128]{2,1,0:T(8,128)(2,1)S(1)}, bf16[8,144,128]{2,1,0:T(8,128)(2,1)S(1)}, u32[]{:S(2)}, u32[]{:S(2)}) %collective-permute-start.25) | collective-permute-done | bytes 294944 | tf_op jit(solution)/shard_map/ppermute | solution.py:370
  98.2 1.8 %collective-permute-start.31 = (bf16[1024,128]{1,0:T(8,128)(2,1)S(1)}, bf16[1024,128]{1,0:T(8,128)(2,1)S(1)}, u32[]{:S(2)}, u32[]{:S(2)}) collective-permute-start(bf16[1024,128]{1,0:T(8,128)(2,1)S(1)} %merge_1.1.refs_8_), channel_id=1, source_target_pairs={{0,6},{1,7},{2,4},{3,5},{4,2},{5,3},{6,0},{7,1},{8,14},{9,15},{10,... | collective-permute-start | bytes 786440 | tf_op jit(solution)/shard_map/ppermute | solution.py:351
  102.3 3.6 %collective-permute-done.31.refs_14_ = bf16[1024,128]{1,0:T(8,128)(2,1)S(1)} collective-permute-done((bf16[1024,128]{1,0:T(8,128)(2,1)S(1)}, bf16[1024,128]{1,0:T(8,128)(2,1)S(1)}, u32[]{:S(2)}, u32[]{:S(2)}) %collective-permute-start.31) | collective-permute-done | bytes 262176 | tf_op jit(solution)/shard_map/ppermute | solution.py:351
  105.9 2.7 %collective-permute-done.29.refs_12_ = bf16[1024,128]{1,0:T(8,128)(2,1)S(1)} collective-permute-done((bf16[1024,128]{1,0:T(8,128)(2,1)S(1)}, bf16[1024,128]{1,0:T(8,128)(2,1)S(1)}, u32[]{:S(2)}, u32[]{:S(2)}) %collective-permute-start.29) | collective-permute-done | bytes 262176 | tf_op jit(solution)/shard_map/ppermute | solution.py:351
  110.5 2.1 %place.1 = bf16[1024,2048]{1,0:T(8,128)(2,1)} custom-call(s32[1]{0:T(128)} %bitcast.me_ref, bf16[1024,128]{1,0:T(8,128)(2,1)S(1)} %merge_0.1.refs_0_, bf16[1024,128]{1,0:T(8,128)(2,1)S(1)} %collective-permute-done.15.refs_1_, bf16[1024,128]{1,0:T(8,128)(2,1)S(1)} %collective-permute-done.16.refs_2_, bf16[1024,128]{1,0:T(8,128)(2,1)S(1)} %collective-permute-done.17.refs_3_, ...), custom_call_target="tpu_custom_call" | custom-call | tf_op jit(solution)/shard_map/place/pallas_call | solution.py:330
  (79 shorter events, 27.2 us)
Async XLA Ops:
  2.3 10.5 %collective-permute-start = (bf16[2,256,128]{2,1,0:T(8,128)(2,1)}, bf16[2,256,128]{2,1,0:T(8,128)(2,1)S(1)}, u32[]{:S(2)}, u32[]{:S(2)}) collective-permute-start(bf16[2,256,128]{2,1,0:T(8,128)(2,1)} %get-tuple-element.53), channel_id=1, source_target_pairs={{0,2},{1,3},{2,0},{3,1},{4,6},{5,7},{6,4},{7,5},{8,10},{9,11},{10,... | collective-permute-start | bytes 393224 | tf_op jit(solution)/shard_map/ppermute | solution.py:351
  5.3 8.0 %collective-permute-start.1 = (bf16[2,256,128]{2,1,0:T(8,128)(2,1)}, bf16[2,256,128]{2,1,0:T(8,128)(2,1)S(1)}, u32[]{:S(2)}, u32[]{:S(2)}) collective-permute-start(bf16[2,256,128]{2,1,0:T(8,128)(2,1)} %get-tuple-element.54), channel_id=1, source_target_pairs={{0,4},{1,5},{2,6},{3,7},{4,0},{5,1},{6,2},{7,3},{8,12},{9,13},{10,... | collective-permute-start | bytes 393224 | tf_op jit(solution)/shard_map/ppermute | solution.py:351
  15.1 18.0 %collective-permute-start.9 = (bf16[8,2,128,128]{3,2,1,0:T(8,128)(2,1)S(1)}, bf16[8,2,128,128]{3,2,1,0:T(8,128)(2,1)S(1)}, u32[]{:S(2)}, u32[]{:S(2)}) collective-permute-start(bf16[8,2,128,128]{3,2,1,0:T(8,128)(2,1)S(1)} %bitcast.9), channel_id=1, source_target_pairs={{8,16},{16,8},{9,17},{17,9},{10,18},{18,10},{11,19},{19,11},{12,20... | collective-permute-start | bytes 1572872 | tf_op jit(solution)/shard_map/ppermute | solution.py:364
  15.8 17.3 %collective-permute-start.8 = (bf16[8,2,128,128]{3,2,1,0:T(8,128)(2,1)S(1)}, bf16[8,2,128,128]{3,2,1,0:T(8,128)(2,1)}, u32[]{:S(2)}, u32[]{:S(2)}) collective-permute-start(bf16[8,2,128,128]{3,2,1,0:T(8,128)(2,1)S(1)} %bitcast.10), channel_id=1, source_target_pairs={{0,8},{8,0},{16,24},{24,16},{1,9},{9,1},{17,25},{25,17},{2,10},{10... | collective-permute-start | bytes 1572872 | tf_op jit(solution)/shard_map/ppermute | solution.py:364
  24.5 8.5 %collective-permute-start.6 = (bf16[2,288,128]{2,1,0:T(8,128)(2,1)}, bf16[2,288,128]{2,1,0:T(8,128)(2,1)S(1)}, u32[]{:S(2)}, u32[]{:S(2)}) collective-permute-start(bf16[2,288,128]{2,1,0:T(8,128)(2,1)} %get-tuple-element.66), channel_id=1, source_target_pairs={{0,4},{1,5},{2,6},{3,7},{4,0},{5,1},{6,2},{7,3},{8,12},{9,13},{10,... | collective-permute-start | bytes 442376 | tf_op jit(solution)/shard_map/ppermute | solution.py:351
  35.9 14.0 %collective-permute-start.12 = (bf16[8,2,128,128]{3,2,1,0:T(8,128)(2,1)S(1)}, bf16[8,2,128,128]{3,2,1,0:T(8,128)(2,1)S(1)}, u32[]{:S(2)}, u32[]{:S(2)}) collective-permute-start(bf16[8,2,128,128]{3,2,1,0:T(8,128)(2,1)S(1)} %bitcast.6), channel_id=1, source_target_pairs={{0,8},{8,0},{16,24},{24,16},{1,9},{9,1},{17,25},{25,17},{2,10},{10... | collective-permute-start | bytes 1572872 | tf_op jit(solution)/shard_map/ppermute | solution.py:364
  36.9 22.6 %collective-permute-start.13 = (bf16[8,2,128,128]{3,2,1,0:T(8,128)(2,1)}, bf16[8,2,128,128]{3,2,1,0:T(8,128)(2,1)}, u32[]{:S(2)}, u32[]{:S(2)}) collective-permute-start(bf16[8,2,128,128]{3,2,1,0:T(8,128)(2,1)} %collective-permute-done.8.refs_2_), channel_id=1, source_target_pairs={{8,16},{16,8},{9,17},{17,9},{10,18},{18,10},{11,19},{19,11},{12,20... | collective-permute-start | bytes 1572872 | tf_op jit(solution)/shard_map/ppermute | solution.py:364
  38.3 16.9 %collective-permute-start.11 = (bf16[8,128,128]{2,1,0:T(8,128)(2,1)S(1)}, bf16[8,128,128]{2,1,0:T(8,128)(2,1)S(1)}, u32[]{:S(2)}, u32[]{:S(2)}) collective-permute-start(bf16[8,128,128]{2,1,0:T(8,128)(2,1)S(1)} %copy-done.1), channel_id=1, source_target_pairs={{0,8},{24,16},{1,9},{25,17},{2,10},{26,18},{3,11},{27,19},{4,12},{... | collective-permute-start | bytes 786440 | tf_op jit(solution)/shard_map/ppermute | solution.py:367
  49.9 30.5 %collective-permute-start.23 = (bf16[8,2,128,128]{3,2,1,0:T(8,128)(2,1)S(1)}, bf16[8,2,128,128]{3,2,1,0:T(8,128)(2,1)S(1)}, u32[]{:S(2)}, u32[]{:S(2)}) collective-permute-start(bf16[8,2,128,128]{3,2,1,0:T(8,128)(2,1)S(1)} %bitcast.7), channel_id=1, source_target_pairs={{8,16},{16,8},{9,17},{17,9},{10,18},{18,10},{11,19},{19,11},{12,20... | collective-permute-start | bytes 1572872 | tf_op jit(solution)/shard_map/ppermute | solution.py:364
  62.0 13.0 %collective-permute-start.14 = (bf16[8,144,128]{2,1,0:T(8,128)(2,1)}, bf16[8,144,128]{2,1,0:T(8,128)(2,1)}, u32[]{:S(2)}, u32[]{:S(2)}) collective-permute-start(bf16[8,144,128]{2,1,0:T(8,128)(2,1)} %get-tuple-element.84), channel_id=1, source_target_pairs={{8,0},{16,24},{9,1},{17,25},{10,2},{18,26},{11,3},{19,27},{12,4},{... | collective-permute-start | bytes 884744 | tf_op jit(solution)/shard_map/ppermute | solution.py:370
  63.3 21.3 %collective-permute-start.24 = (bf16[8,2,128,128]{3,2,1,0:T(8,128)(2,1)S(1)}, bf16[8,2,128,128]{3,2,1,0:T(8,128)(2,1)S(1)}, u32[]{:S(2)}, u32[]{:S(2)}) collective-permute-start(bf16[8,2,128,128]{3,2,1,0:T(8,128)(2,1)S(1)} %collective-permute-done.12.refs_1_), channel_id=1, source_target_pairs={{8,16},{16,8},{9,17},{17,9},{10,18},{18,10},{11,19},{19,11},{12,20... | collective-permute-start | bytes 1572872 | tf_op jit(solution)/shard_map/ppermute | solution.py:364
  76.1 8.5 %collective-permute-start.18 = (bf16[1024,128]{1,0:T(8,128)(2,1)S(1)}, bf16[1024,128]{1,0:T(8,128)(2,1)S(1)}, u32[]{:S(2)}, u32[]{:S(2)}) collective-permute-start(bf16[1024,128]{1,0:T(8,128)(2,1)S(1)} %merge_0.1.refs_0_), channel_id=1, source_target_pairs={{0,4},{1,5},{2,6},{3,7},{4,0},{5,1},{6,2},{7,3},{8,12},{9,13},{10,... | collective-permute-start | bytes 786440 | tf_op jit(solution)/shard_map/ppermute | solution.py:351
  77.7 8.4 %collective-permute-start.16 = (bf16[1024,128]{1,0:T(8,128)(2,1)S(1)}, bf16[1024,128]{1,0:T(8,128)(2,1)S(1)}, u32[]{:S(2)}, u32[]{:S(2)}) collective-permute-start(bf16[1024,128]{1,0:T(8,128)(2,1)S(1)} %merge_0.1.refs_0_), channel_id=1, source_target_pairs={{0,2},{1,3},{2,0},{3,1},{4,6},{5,7},{6,4},{7,5},{8,10},{9,11},{10,... | collective-permute-start | bytes 786440 | tf_op jit(solution)/shard_map/ppermute | solution.py:351
  78.9 7.2 %collective-permute-start.22 = (bf16[8,128,128]{2,1,0:T(8,128)(2,1)S(1)}, bf16[8,128,128]{2,1,0:T(8,128)(2,1)S(1)}, u32[]{:S(2)}, u32[]{:S(2)}) collective-permute-start(bf16[8,128,128]{2,1,0:T(8,128)(2,1)S(1)} %copy-done), channel_id=1, source_target_pairs={{0,8},{24,16},{1,9},{25,17},{2,10},{26,18},{3,11},{27,19},{4,12},{... | collective-permute-start | bytes 786440 | tf_op jit(solution)/shard_map/ppermute | solution.py:367
  80.4 9.0 %collective-permute-start.20 = (bf16[1024,128]{1,0:T(8,128)(2,1)S(1)}, bf16[1024,128]{1,0:T(8,128)(2,1)S(1)}, u32[]{:S(2)}, u32[]{:S(2)}) collective-permute-start(bf16[1024,128]{1,0:T(8,128)(2,1)S(1)} %merge_0.1.refs_0_), channel_id=1, source_target_pairs={{0,6},{1,7},{2,4},{3,5},{4,2},{5,3},{6,0},{7,1},{8,14},{9,15},{10,... | collective-permute-start | bytes 786440 | tf_op jit(solution)/shard_map/ppermute | solution.py:351
  89.4 8.6 %collective-permute-start.25 = (bf16[8,144,128]{2,1,0:T(8,128)(2,1)S(1)}, bf16[8,144,128]{2,1,0:T(8,128)(2,1)S(1)}, u32[]{:S(2)}, u32[]{:S(2)}) collective-permute-start(bf16[8,144,128]{2,1,0:T(8,128)(2,1)S(1)} %get-tuple-element.98), channel_id=1, source_target_pairs={{8,0},{16,24},{9,1},{17,25},{10,2},{18,26},{11,3},{19,27},{12,4},{... | collective-permute-start | bytes 884744 | tf_op jit(solution)/shard_map/ppermute | solution.py:370
  90.7 9.9 %collective-permute-start.15 = (bf16[1024,128]{1,0:T(8,128)(2,1)S(1)}, bf16[1024,128]{1,0:T(8,128)(2,1)S(1)}, u32[]{:S(2)}, u32[]{:S(2)}) collective-permute-start(bf16[1024,128]{1,0:T(8,128)(2,1)S(1)} %merge_0.1.refs_0_), channel_id=1, source_target_pairs={{0,1},{1,0},{2,3},{3,2},{4,5},{5,4},{6,7},{7,6},{8,9},{9,8},{10,11... | collective-permute-start | bytes 786440 | tf_op jit(solution)/shard_map/ppermute | solution.py:351
  90.7 11.0 %collective-permute-start.21 = (bf16[1024,128]{1,0:T(8,128)(2,1)S(1)}, bf16[1024,128]{1,0:T(8,128)(2,1)S(1)}, u32[]{:S(2)}, u32[]{:S(2)}) collective-permute-start(bf16[1024,128]{1,0:T(8,128)(2,1)S(1)} %collective-permute-done.20.refs_6_), channel_id=1, source_target_pairs={{0,1},{1,0},{2,3},{3,2},{4,5},{5,4},{6,7},{7,6},{8,9},{9,8},{10,11... | collective-permute-start | bytes 786440 | tf_op jit(solution)/shard_map/ppermute | solution.py:351
  91.2 10.5 %collective-permute-start.19 = (bf16[1024,128]{1,0:T(8,128)(2,1)S(1)}, bf16[1024,128]{1,0:T(8,128)(2,1)S(1)}, u32[]{:S(2)}, u32[]{:S(2)}) collective-permute-start(bf16[1024,128]{1,0:T(8,128)(2,1)S(1)} %collective-permute-done.18.refs_4_), channel_id=1, source_target_pairs={{0,1},{1,0},{2,3},{3,2},{4,5},{5,4},{6,7},{7,6},{8,9},{9,8},{10,11... | collective-permute-start | bytes 786440 | tf_op jit(solution)/shard_map/ppermute | solution.py:351
  98.2 7.7 %collective-permute-start.31 = (bf16[1024,128]{1,0:T(8,128)(2,1)S(1)}, bf16[1024,128]{1,0:T(8,128)(2,1)S(1)}, u32[]{:S(2)}, u32[]{:S(2)}) collective-permute-start(bf16[1024,128]{1,0:T(8,128)(2,1)S(1)} %merge_1.1.refs_8_), channel_id=1, source_target_pairs={{0,6},{1,7},{2,4},{3,5},{4,2},{5,3},{6,0},{7,1},{8,14},{9,15},{10,... | collective-permute-start | bytes 786440 | tf_op jit(solution)/shard_map/ppermute | solution.py:351
  99.9 8.6 %collective-permute-start.29 = (bf16[1024,128]{1,0:T(8,128)(2,1)S(1)}, bf16[1024,128]{1,0:T(8,128)(2,1)S(1)}, u32[]{:S(2)}, u32[]{:S(2)}) collective-permute-start(bf16[1024,128]{1,0:T(8,128)(2,1)S(1)} %merge_1.1.refs_8_), channel_id=1, source_target_pairs={{0,4},{1,5},{2,6},{3,7},{4,0},{5,1},{6,2},{7,3},{8,12},{9,13},{10,... | collective-permute-start | bytes 786440 | tf_op jit(solution)/shard_map/ppermute | solution.py:351
  100.5 8.1 %collective-permute-start.27 = (bf16[1024,128]{1,0:T(8,128)(2,1)S(1)}, bf16[1024,128]{1,0:T(8,128)(2,1)S(1)}, u32[]{:S(2)}, u32[]{:S(2)}) collective-permute-start(bf16[1024,128]{1,0:T(8,128)(2,1)S(1)} %merge_1.1.refs_8_), channel_id=1, source_target_pairs={{0,2},{1,3},{2,0},{3,1},{4,6},{5,7},{6,4},{7,5},{8,10},{9,11},{10,... | collective-permute-start | bytes 786440 | tf_op jit(solution)/shard_map/ppermute | solution.py:351
  101.7 7.4 %collective-permute-start.17 = (bf16[1024,128]{1,0:T(8,128)(2,1)S(1)}, bf16[1024,128]{1,0:T(8,128)(2,1)S(1)}, u32[]{:S(2)}, u32[]{:S(2)}) collective-permute-start(bf16[1024,128]{1,0:T(8,128)(2,1)S(1)} %collective-permute-done.16.refs_2_), channel_id=1, source_target_pairs={{0,1},{1,0},{2,3},{3,2},{4,5},{5,4},{6,7},{7,6},{8,9},{9,8},{10,11... | collective-permute-start | bytes 786440 | tf_op jit(solution)/shard_map/ppermute | solution.py:351
  101.7 7.4 %collective-permute-start.26 = (bf16[1024,128]{1,0:T(8,128)(2,1)S(1)}, bf16[1024,128]{1,0:T(8,128)(2,1)S(1)}, u32[]{:S(2)}, u32[]{:S(2)}) collective-permute-start(bf16[1024,128]{1,0:T(8,128)(2,1)S(1)} %merge_1.1.refs_8_), channel_id=1, source_target_pairs={{0,1},{1,0},{2,3},{3,2},{4,5},{5,4},{6,7},{7,6},{8,9},{9,8},{10,11... | collective-permute-start | bytes 786440 | tf_op jit(solution)/shard_map/ppermute | solution.py:351
  (14 other events, 139.0 us)

commit v12 on v10

--- a/solution.py
+++ b/solution.py
@@ -384,22 +384,19 @@
     def flags(x):
         return x[:, : block_mask.shape[1], :rows].astype(jnp.int32).reshape(-1)
 
-    parts = (block_mask.T,) + ((inward(block_mask.T),) if relay else ())
-    owns, over, guest = [], [], [None] * heads
+    owns, over = [], []
     for c in range(heads):
-        place_of = after(me1, (q, owns[0])) if c else me1
-        packed = pack(place_of, keys, values, parts if c == heads - 1 else (), n_ka, heads, c)
+        packed = pack(after(me1, packed) if c else me1, keys, values, () if c else (block_mask.T,), n_ka, heads, c)
+        own = sort(packed, owns[-1] if c else None)
+        owns.append(blocks(own))
+        over.append([exchange(owns[c], odd, 1) for odd in (0, 1)])
         if c == 0:
-            q = turn(after(me1, packed), queries, heads)
-            own = sort(packed, (q, parts))
-        else:
-            own = sort(packed, over[0])
-        owns.append(blocks(own))
-        over.append([exchange(after(owns[c], (over[0][1], guest[0]) if c else None), odd, 1) for odd in (0, 1)])
-        if relay:
-            guest[c] = inward(after(q[c], over[c]))
-    size = mask_rows(block_mask.shape[1])
-    masks = [flags(own[:, 2 * shard + i * size :]) for i in range(len(parts))]
+            marks = own[:, 2 * shard :]
+    q = turn(after(me1, owns), queries, heads)
+    masks, guest = [flags(marks)], [None] * heads
+    if relay:
+        masks.append(flags(inward(marks)))
+        guest = [inward(x) for x in q]
 
     steps = [((0, False),)]
     for step in range(1, n_pb):
@@ -416,6 +413,7 @@
         kind = "keep" if step < last else "send" if relay else "last"
         sources = [x for x in sources if x is not None]
         name = f"attend_{c}_{step}"
+        sources = after(sources, state[c - 1][0] if c else None)
         return attend(lists[step], q[c], guest[c], sources, state[c], kind, 2 if relay else 1, name)
 
     for step in range(last):
@@ -428,16 +426,14 @@
             state[c] = run(c, step, sources)
 
     pieces = []
-    sent = far = None
     for c in range(heads):
-        found = run(c, last, ([] if last else [owns[c]]) + after(over[c], sent))
+        found = state[c] = run(c, last, ([] if last else [owns[c]]) + over[c])
         if relay:
             outer = ((pb == 0) | (pb == n_pb - 1)).astype(jnp.int32)[None]
-            out = merge(outer, found[:3], outward(after(found[3], far)), f"merge_{c}")
+            out = merge(outer, found[:3], outward(found[3]), f"merge_{c}")
         else:
             out = found[0]
         mine = [out] + [swap(out, k) for k in range(2, n_ka, 2)]
-        sent, far = mine[: n_ka // 4 + 1], mine[n_ka // 4 + 1 :]
         others = [swap(x, 1) for x in mine]
         pieces += [x for two in zip(mine, others) for x in two]
     return place(me1, pieces, n_ka, heads)

time: 108 us -> 120 us (1.11)
  the two profiles are of different devices: /device:TPU:0 before, /device:TPU:9 now
where the time goes in v12:
time: 120 us
  starting transfers between devices  42.6 us (36%)
  waiting for transfers between devices  41.6 us (35%)
  Pallas kernels  31.3 us (26%)
  local copies, waits for them, and re-layouts  3.16 us (3%)
    ppermute x22, waiting for transfers between devices, swap(): return lax.ppermute(x, 'ka', [(i, i ^ k) for i in range(n_ka)])  26.2 us
    ppermute x22, starting transfers between devices, swap(): return lax.ppermute(x, 'ka', [(i, i ^ k) for i in range(n_ka)])  25.6 us
    pallas_call x4, Pallas kernels, attend(): pl.pallas_call(functools.partial(attend_kernel, n_src, entry, first, mode...  18.2 us
    ppermute x6, waiting for transfers between devices, exchange(): return lax.ppermute(x, 'pb', found) if found else None  15.4 us
    ppermute x6, starting transfers between devices, exchange(): return lax.ppermute(x, 'pb', found) if found else None  9.74 us
    pallas_call x2, Pallas kernels, pack(): pl.pallas_call(functools.partial(pack_kernel, n_ka, heads, c, len(masks))...  5.28 us
    ppermute x3, starting transfers between devices, inward(): return lax.ppermute(x, 'pb', [(0, 1), (n_pb - 1, n_pb - 2)])  4.01 us
    ppermute x2, starting transfers between devices, outward(): return lax.ppermute(x, 'pb', [(1, 0), (n_pb - 2, n_pb - 1)])  3.33 us
  transfers between devices with their start and end apart: 33, of which 16 were waited for; matrix products, arithmetic and copies ran while one was open for 2% of the time, Pallas kernels for 22%

profile of v12, /device:TPU:9, one launch (start us, length us, event | category | flops | bytes accessed | tf_op | source)
XLA Modules:
  0.0 119.8 jit_solution(8682944212454784615)
XLA Ops:
  0.0 3.0 %pack_0.1 = (bf16[2,272,128]{2,1,0:T(8,128)(2,1)}, bf16[2,272,128]{2,1,0:T(8,128)(2,1)}, bf16[2,272,128]{2,1,0:T(8,128)(2,1)}, bf16[2,272,128]{2,1,0:T(8,128)(2,1)}) custom-call(s32[1]{0:T(128)} %bitcast.me_ref, s32[4,8]{1,0:T(4,128)} %bitcast.12, bf16[128,2048]{1,0:T(8,128)(2,1)} %refs_0_.1, bf16[128,2048]{1,0:T(8,128)(2,1)} %refs_1_.3), custom_call_target="tpu_custom_call" | custom-call | bytes 262144 | tf_op jit(solution)/shard_map/pack_0/pallas_call | solution.py:77
  8.7 3.1 %collective-permute-done.2 = bf16[2,272,128]{2,1,0:T(8,128)(2,1)S(1)} collective-permute-done((bf16[2,272,128]{2,1,0:T(8,128)(2,1)}, bf16[2,272,128]{2,1,0:T(8,128)(2,1)S(1)}, u32[]{:S(2)}, u32[]{:S(2)}) %collective-permute-start.2) | collective-permute-done | bytes 139296 | tf_op jit(solution)/shard_map/ppermute | solution.py:351
  13.7 2.3 %pack_1.1 = (bf16[2,256,128]{2,1,0:T(8,128)(2,1)}, bf16[2,256,128]{2,1,0:T(8,128)(2,1)}, bf16[2,256,128]{2,1,0:T(8,128)(2,1)}, bf16[2,256,128]{2,1,0:T(8,128)(2,1)}) custom-call(s32[1]{0:T(128)} %bitcast.me_ref, bf16[128,2048]{1,0:T(8,128)(2,1)} %refs_0_.1, bf16[128,2048]{1,0:T(8,128)(2,1)} %refs_1_.3), custom_call_target="tpu_custom_call" | custom-call | bytes 262144 | tf_op jit(solution)/shard_map/pack_1/pallas_call | solution.py:77
  18.8 2.6 %collective-permute-done.5 = bf16[2,256,128]{2,1,0:T(8,128)(2,1)S(1)} collective-permute-done((bf16[2,256,128]{2,1,0:T(8,128)(2,1)}, bf16[2,256,128]{2,1,0:T(8,128)(2,1)S(1)}, u32[]{:S(2)}, u32[]{:S(2)}) %collective-permute-start.5) | collective-permute-done | bytes 131104 | tf_op jit(solution)/shard_map/ppermute | solution.py:351
  22.0 3.2 %collective-permute-done.7 = bf16[2,256,128]{2,1,0:T(8,128)(2,1)S(1)} collective-permute-done((bf16[2,256,128]{2,1,0:T(8,128)(2,1)}, bf16[2,256,128]{2,1,0:T(8,128)(2,1)S(1)}, u32[]{:S(2)}, u32[]{:S(2)}) %collective-permute-start.7) | collective-permute-done | bytes 131104 | tf_op jit(solution)/shard_map/ppermute | solution.py:351
  27.0 3.2 %collective-permute-start.11 = (bf16[8,2,128,128]{3,2,1,0:T(8,128)(2,1)S(1)}, bf16[8,2,128,128]{3,2,1,0:T(8,128)(2,1)S(1)}, u32[]{:S(2)}, u32[]{:S(2)}) collective-permute-start(bf16[8,2,128,128]{3,2,1,0:T(8,128)(2,1)S(1)} %bitcast.6), channel_id=1, source_target_pairs={{8,16},{16,8},{9,17},{17,9},{10,18},{18,10},{11,19},{19,11},{12,20... | collective-permute-start | bytes 1572872 | tf_op jit(solution)/shard_map/ppermute | solution.py:364
  30.4 2.1 %collective-permute-start.23 = (bf16[8,2,128,128]{3,2,1,0:T(8,128)(2,1)S(1)}, bf16[8,2,128,128]{3,2,1,0:T(8,128)(2,1)S(1)}, u32[]{:S(2)}, u32[]{:S(2)}) collective-permute-start(bf16[8,2,128,128]{3,2,1,0:T(8,128)(2,1)S(1)} %bitcast.9), channel_id=1, source_target_pairs={{8,16},{16,8},{9,17},{17,9},{10,18},{18,10},{11,19},{19,11},{12,20... | collective-permute-start | bytes 1572872 | tf_op jit(solution)/shard_map/ppermute | solution.py:364
  32.6 9.9 %collective-permute-done.11.refs_3_ = bf16[8,2,128,128]{3,2,1,0:T(8,128)(2,1)S(1)} collective-permute-done((bf16[8,2,128,128]{3,2,1,0:T(8,128)(2,1)S(1)}, bf16[8,2,128,128]{3,2,1,0:T(8,128)(2,1)S(1)}, u32[]{:S(2)}, u32[]{:S(2)}) %collective-permute-start.11) | collective-permute-done | bytes 524320 | tf_op jit(solution)/shard_map/ppermute | solution.py:364
  43.5 2.1 %collective-permute-start.12 = (bf16[8,2,128,128]{3,2,1,0:T(8,128)(2,1)S(1)}, bf16[8,2,128,128]{3,2,1,0:T(8,128)(2,1)}, u32[]{:S(2)}, u32[]{:S(2)}) collective-permute-start(bf16[8,2,128,128]{3,2,1,0:T(8,128)(2,1)S(1)} %collective-permute-done.10.refs_2_), channel_id=1, source_target_pairs={{8,16},{16,8},{9,17},{17,9},{10,18},{18,10},{11,19},{19,11},{12,20... | collective-permute-start | bytes 1572872 | tf_op jit(solution)/shard_map/ppermute | solution.py:364
  47.0 2.0 %turn.1 = (bf16[8,128,128]{2,1,0:T(8,128)(2,1)}, bf16[8,128,128]{2,1,0:T(8,128)(2,1)}) custom-call(s32[1]{0:T(128)} %bitcast.me_ref, bf16[1024,2048]{1,0:T(8,128)(2,1)} %q_all.1), custom_call_target="tpu_custom_call" | custom-call | bytes 131072 | tf_op jit(solution)/shard_map/turn/pallas_call | solution.py:105
  50.4 3.4 %collective-permute-done.23.refs_3_ = bf16[8,2,128,128]{3,2,1,0:T(8,128)(2,1)S(1)} collective-permute-done((bf16[8,2,128,128]{3,2,1,0:T(8,128)(2,1)S(1)}, bf16[8,2,128,128]{3,2,1,0:T(8,128)(2,1)S(1)}, u32[]{:S(2)}, u32[]{:S(2)}) %collective-permute-start.23) | collective-permute-done | bytes 524320 | tf_op jit(solution)/shard_map/ppermute | solution.py:364
  54.9 2.1 %collective-permute-start.24 = (bf16[8,2,128,128]{3,2,1,0:T(8,128)(2,1)}, bf16[8,2,128,128]{3,2,1,0:T(8,128)(2,1)}, u32[]{:S(2)}, u32[]{:S(2)}) collective-permute-start(bf16[8,2,128,128]{3,2,1,0:T(8,128)(2,1)} %collective-permute-done.22.refs_2_), channel_id=1, source_target_pairs={{8,16},{16,8},{9,17},{17,9},{10,18},{18,10},{11,19},{19,11},{12,20... | collective-permute-start | bytes 1572872 | tf_op jit(solution)/shard_map/ppermute | solution.py:364
  57.9 2.4 %plan.1 = (s32[2]{0:T(128)S(1)}, s32[432]{0:T(512)S(1)}, s32[176]{0:T(256)S(1)}) custom-call(s32[1]{0:T(128)} %bitcast.2.pb_ref, s32[256]{0:T(256)S(1)} %reshape.24.refs_0_, s32[256]{0:T(256)S(1)} %reshape.26.refs_1_), custom_call_target="tpu_custom_call" | custom-call | tf_op jit(solution)/shard_map/plan/pallas_call | solution.py:159
  62.6 4.7 %attend_0_0.1 = (f32[16,1,128]{2,1,0:T(1,128)S(1)}, f32[16,1,128]{2,1,0:T(1,128)S(1)}, f32[16,128,128]{2,1,0:T(8,128)S(1)}) custom-call(s32[2]{0:T(128)S(1)} %get-tuple-element.48.count_ref, s32[432]{0:T(512)S(1)} %get-tuple-element.62.live_ref, bf16[8,128,128]{2,1,0:T(8,128)(2,1)S(1)} %copy-done.1, bf16[8,128,128]{2,1,0:T(8,128)(2,1)S(1)} %collective-permute-done.9.refs_0_, ...), custom_call_target="tpu_custom_call" | custom-call | bytes 16384 | tf_op jit(solution)/shard_map/attend_0_0/pallas_call | solution.py:273
  67.3 4.3 %attend_0_1.1 = (f32[16,1,128]{2,1,0:T(1,128)S(1)}, f32[16,1,128]{2,1,0:T(1,128)S(1)}, f32[16,128,128]{2,1,0:T(8,128)S(1)}, bf16[8,144,128]{2,1,0:T(8,128)(2,1)}) custom-call(s32[2]{0:T(128)S(1)} %get-tuple-element.48.count_ref, s32[176]{0:T(256)S(1)} %get-tuple-element.49.live_ref, bf16[8,128,128]{2,1,0:T(8,128)(2,1)S(1)} %copy-done.1, ...), custom_call_target="tpu_custom_call" | custom-call | bytes 16384 | tf_op jit(solution)/shard_map/attend_0_1/pallas_call | solution.py:273
  71.6 2.0 %collective-permute-start.13 = (bf16[8,144,128]{2,1,0:T(8,128)(2,1)}, bf16[8,144,128]{2,1,0:T(8,128)(2,1)}, u32[]{:S(2)}, u32[]{:S(2)}) collective-permute-start(bf16[8,144,128]{2,1,0:T(8,128)(2,1)} %get-tuple-element.69), channel_id=1, source_target_pairs={{8,0},{16,24},{9,1},{17,25},{10,2},{18,26},{11,3},{19,27},{12,4},{... | collective-permute-start | bytes 884744 | tf_op jit(solution)/shard_map/ppermute | solution.py:370
  73.7 5.5 %attend_1_0.1 = (f32[16,1,128]{2,1,0:T(1,128)S(1)}, f32[16,1,128]{2,1,0:T(1,128)S(1)}, f32[16,128,128]{2,1,0:T(8,128)S(1)}) custom-call(s32[2]{0:T(128)S(1)} %get-tuple-element.48.count_ref, s32[432]{0:T(512)S(1)} %get-tuple-element.62.live_ref, bf16[8,128,128]{2,1,0:T(8,128)(2,1)S(1)} %copy-done, bf16[8,128,128]{2,1,0:T(8,128)(2,1)S(1)} %collective-permute-done.21.refs_0_, ...), custom_call_target="tpu_custom_call" | custom-call | bytes 16384 | tf_op jit(solution)/shard_map/attend_1_0/pallas_call | solution.py:273
  79.2 3.6 %attend_1_1.1 = (f32[16,1,128]{2,1,0:T(1,128)S(1)}, f32[16,1,128]{2,1,0:T(1,128)S(1)}, f32[16,128,128]{2,1,0:T(8,128)S(1)}, bf16[8,144,128]{2,1,0:T(8,128)(2,1)S(1)}) custom-call(s32[2]{0:T(128)S(1)} %get-tuple-element.48.count_ref, s32[176]{0:T(256)S(1)} %get-tuple-element.49.live_ref, bf16[8,128,128]{2,1,0:T(8,128)(2,1)S(1)} %copy-done, ...), custom_call_target="tpu_custom_call" | custom-call | bytes 16384 | tf_op jit(solution)/shard_map/attend_1_1/pallas_call | solution.py:273
  88.0 3.0 %collective-permute-start.14 = (bf16[1024,128]{1,0:T(8,128)(2,1)S(1)}, bf16[1024,128]{1,0:T(8,128)(2,1)S(1)}, u32[]{:S(2)}, u32[]{:S(2)}) collective-permute-start(bf16[1024,128]{1,0:T(8,128)(2,1)S(1)} %merge_0.1.refs_0_), channel_id=1, source_target_pairs={{0,1},{1,0},{2,3},{3,2},{4,5},{5,4},{6,7},{7,6},{8,9},{9,8},{10,11... | collective-permute-start | bytes 786440 | tf_op jit(solution)/shard_map/ppermute | solution.py:351
  92.0 5.7 %collective-permute-start.20 = (bf16[1024,128]{1,0:T(8,128)(2,1)S(1)}, bf16[1024,128]{1,0:T(8,128)(2,1)S(1)}, u32[]{:S(2)}, u32[]{:S(2)}) collective-permute-start(bf16[1024,128]{1,0:T(8,128)(2,1)S(1)} %collective-permute-done.19.refs_6_), channel_id=1, source_target_pairs={{0,1},{1,0},{2,3},{3,2},{4,5},{5,4},{6,7},{7,6},{8,9},{9,8},{10,11... | collective-permute-start | bytes 786440 | tf_op jit(solution)/shard_map/ppermute | solution.py:351
  97.7 2.3 %collective-permute-done.17.refs_4_ = bf16[1024,128]{1,0:T(8,128)(2,1)S(1)} collective-permute-done((bf16[1024,128]{1,0:T(8,128)(2,1)S(1)}, bf16[1024,128]{1,0:T(8,128)(2,1)S(1)}, u32[]{:S(2)}, u32[]{:S(2)}) %collective-permute-start.17) | collective-permute-done | bytes 262176 | tf_op jit(solution)/shard_map/ppermute | solution.py:351
  104.5 5.3 %collective-permute-done.31.refs_14_ = bf16[1024,128]{1,0:T(8,128)(2,1)S(1)} collective-permute-done((bf16[1024,128]{1,0:T(8,128)(2,1)S(1)}, bf16[1024,128]{1,0:T(8,128)(2,1)S(1)}, u32[]{:S(2)}, u32[]{:S(2)}) %collective-permute-start.31) | collective-permute-done | bytes 262176 | tf_op jit(solution)/shard_map/ppermute | solution.py:351
  110.9 4.7 %collective-permute-done.29.refs_12_ = bf16[1024,128]{1,0:T(8,128)(2,1)S(1)} collective-permute-done((bf16[1024,128]{1,0:T(8,128)(2,1)S(1)}, bf16[1024,128]{1,0:T(8,128)(2,1)S(1)}, u32[]{:S(2)}, u32[]{:S(2)}) %collective-permute-start.29) | collective-permute-done | bytes 262176 | tf_op jit(solution)/shard_map/ppermute | solution.py:351
  117.7 2.1 %place.1 = bf16[1024,2048]{1,0:T(8,128)(2,1)} custom-call(s32[1]{0:T(128)} %bitcast.me_ref, bf16[1024,128]{1,0:T(8,128)(2,1)S(1)} %merge_0.1.refs_0_, bf16[1024,128]{1,0:T(8,128)(2,1)S(1)} %collective-permute-done.14.refs_1_, bf16[1024,128]{1,0:T(8,128)(2,1)S(1)} %collective-permute-done.15.refs_2_, bf16[1024,128]{1,0:T(8,128)(2,1)S(1)} %collective-permute-done.16.refs_3_, ...), custom_call_target="tpu_custom_call" | custom-call | tf_op jit(solution)/shard_map/place/pallas_call | solution.py:330
  (77 shorter events, 35.0 us)
Async XLA Ops:
  11.8 6.9 %collective-permute-start.3 = (bf16[4,272,128]{2,1,0:T(8,128)(2,1)S(1)}, bf16[4,272,128]{2,1,0:T(8,128)(2,1)S(1)}, u32[]{:S(2)}, u32[]{:S(2)}) collective-permute-start(bf16[4,272,128]{2,1,0:T(8,128)(2,1)S(1)} %pad_maximum_fusion), channel_id=1, source_target_pairs={{0,1},{1,0},{2,3},{3,2},{4,5},{5,4},{6,7},{7,6},{8,9},{9,8},{10,11... | collective-permute-start | bytes 835592 | tf_op jit(solution)/shard_map/ppermute | solution.py:351
  17.6 7.6 %collective-permute-start.7 = (bf16[2,256,128]{2,1,0:T(8,128)(2,1)}, bf16[2,256,128]{2,1,0:T(8,128)(2,1)S(1)}, u32[]{:S(2)}, u32[]{:S(2)}) collective-permute-start(bf16[2,256,128]{2,1,0:T(8,128)(2,1)} %get-tuple-element.54), channel_id=1, source_target_pairs={{0,6},{1,7},{2,4},{3,5},{4,2},{5,3},{6,0},{7,1},{8,14},{9,15},{10,... | collective-permute-start | bytes 393224 | tf_op jit(solution)/shard_map/ppermute | solution.py:351
  27.0 15.4 %collective-permute-start.11 = (bf16[8,2,128,128]{3,2,1,0:T(8,128)(2,1)S(1)}, bf16[8,2,128,128]{3,2,1,0:T(8,128)(2,1)S(1)}, u32[]{:S(2)}, u32[]{:S(2)}) collective-permute-start(bf16[8,2,128,128]{3,2,1,0:T(8,128)(2,1)S(1)} %bitcast.6), channel_id=1, source_target_pairs={{8,16},{16,8},{9,17},{17,9},{10,18},{18,10},{11,19},{19,11},{12,20... | collective-permute-start | bytes 1572872 | tf_op jit(solution)/shard_map/ppermute | solution.py:364
  30.2 13.3 %collective-permute-start.10 = (bf16[8,2,128,128]{3,2,1,0:T(8,128)(2,1)S(1)}, bf16[8,2,128,128]{3,2,1,0:T(8,128)(2,1)S(1)}, u32[]{:S(2)}, u32[]{:S(2)}) collective-permute-start(bf16[8,2,128,128]{3,2,1,0:T(8,128)(2,1)S(1)} %bitcast.7), channel_id=1, source_target_pairs={{0,8},{8,0},{16,24},{24,16},{1,9},{9,1},{17,25},{25,17},{2,10},{10... | collective-permute-start | bytes 1572872 | tf_op jit(solution)/shard_map/ppermute | solution.py:364
  30.4 23.4 %collective-permute-start.23 = (bf16[8,2,128,128]{3,2,1,0:T(8,128)(2,1)S(1)}, bf16[8,2,128,128]{3,2,1,0:T(8,128)(2,1)S(1)}, u32[]{:S(2)}, u32[]{:S(2)}) collective-permute-start(bf16[8,2,128,128]{3,2,1,0:T(8,128)(2,1)S(1)} %bitcast.9), channel_id=1, source_target_pairs={{8,16},{16,8},{9,17},{17,9},{10,18},{18,10},{11,19},{19,11},{12,20... | collective-permute-start | bytes 1572872 | tf_op jit(solution)/shard_map/ppermute | solution.py:364
  32.5 22.4 %collective-permute-start.22 = (bf16[8,2,128,128]{3,2,1,0:T(8,128)(2,1)S(1)}, bf16[8,2,128,128]{3,2,1,0:T(8,128)(2,1)}, u32[]{:S(2)}, u32[]{:S(2)}) collective-permute-start(bf16[8,2,128,128]{3,2,1,0:T(8,128)(2,1)S(1)} %bitcast.10), channel_id=1, source_target_pairs={{0,8},{8,0},{16,24},{24,16},{1,9},{9,1},{17,25},{25,17},{2,10},{10... | collective-permute-start | bytes 1572872 | tf_op jit(solution)/shard_map/ppermute | solution.py:364
  43.5 23.8 %collective-permute-start.12 = (bf16[8,2,128,128]{3,2,1,0:T(8,128)(2,1)S(1)}, bf16[8,2,128,128]{3,2,1,0:T(8,128)(2,1)}, u32[]{:S(2)}, u32[]{:S(2)}) collective-permute-start(bf16[8,2,128,128]{3,2,1,0:T(8,128)(2,1)S(1)} %collective-permute-done.10.refs_2_), channel_id=1, source_target_pairs={{8,16},{16,8},{9,17},{17,9},{10,18},{18,10},{11,19},{19,11},{12,20... | collective-permute-start | bytes 1572872 | tf_op jit(solution)/shard_map/ppermute | solution.py:364
  45.7 12.2 %collective-permute-start.4 = (bf16[8,16,128]{2,1,0:T(8,128)(2,1)S(1)}, bf16[8,16,128]{2,1,0:T(8,128)(2,1)S(1)}, u32[]{:S(2)}, u32[]{:S(2)}) collective-permute-start(bf16[8,16,128]{2,1,0:T(8,128)(2,1)S(1)} %slice.88), channel_id=1, source_target_pairs={{0,8},{24,16},{1,9},{25,17},{2,10},{26,18},{3,11},{27,19},{4,12},{... | collective-permute-start | bytes 98312 | tf_op jit(solution)/shard_map/ppermute | solution.py:367
  49.0 12.6 %collective-permute-start.9 = (bf16[8,128,128]{2,1,0:T(8,128)(2,1)}, bf16[8,128,128]{2,1,0:T(8,128)(2,1)S(1)}, u32[]{:S(2)}, u32[]{:S(2)}) collective-permute-start(bf16[8,128,128]{2,1,0:T(8,128)(2,1)} %get-tuple-element.60.q_own), channel_id=1, source_target_pairs={{0,8},{24,16},{1,9},{25,17},{2,10},{26,18},{3,11},{27,19},{4,12},{... | collective-permute-start | bytes 786440 | tf_op jit(solution)/shard_map/ppermute | solution.py:367
  54.9 24.3 %collective-permute-start.24 = (bf16[8,2,128,128]{3,2,1,0:T(8,128)(2,1)}, bf16[8,2,128,128]{3,2,1,0:T(8,128)(2,1)}, u32[]{:S(2)}, u32[]{:S(2)}) collective-permute-start(bf16[8,2,128,128]{3,2,1,0:T(8,128)(2,1)} %collective-permute-done.22.refs_2_), channel_id=1, source_target_pairs={{8,16},{16,8},{9,17},{17,9},{10,18},{18,10},{11,19},{19,11},{12,20... | collective-permute-start | bytes 1572872 | tf_op jit(solution)/shard_map/ppermute | solution.py:364
  60.3 13.3 %collective-permute-start.21 = (bf16[8,128,128]{2,1,0:T(8,128)(2,1)}, bf16[8,128,128]{2,1,0:T(8,128)(2,1)S(1)}, u32[]{:S(2)}, u32[]{:S(2)}) collective-permute-start(bf16[8,128,128]{2,1,0:T(8,128)(2,1)} %get-tuple-element.70.q_own), channel_id=1, source_target_pairs={{0,8},{24,16},{1,9},{25,17},{2,10},{26,18},{3,11},{27,19},{4,12},{... | collective-permute-start | bytes 786440 | tf_op jit(solution)/shard_map/ppermute | solution.py:367
  71.6 12.5 %collective-permute-start.13 = (bf16[8,144,128]{2,1,0:T(8,128)(2,1)}, bf16[8,144,128]{2,1,0:T(8,128)(2,1)}, u32[]{:S(2)}, u32[]{:S(2)}) collective-permute-start(bf16[8,144,128]{2,1,0:T(8,128)(2,1)} %get-tuple-element.69), channel_id=1, source_target_pairs={{8,0},{16,24},{9,1},{17,25},{10,2},{18,26},{11,3},{19,27},{12,4},{... | collective-permute-start | bytes 884744 | tf_op jit(solution)/shard_map/ppermute | solution.py:370
  82.8 17.8 %collective-permute-start.25 = (bf16[8,144,128]{2,1,0:T(8,128)(2,1)S(1)}, bf16[8,144,128]{2,1,0:T(8,128)(2,1)S(1)}, u32[]{:S(2)}, u32[]{:S(2)}) collective-permute-start(bf16[8,144,128]{2,1,0:T(8,128)(2,1)S(1)} %get-tuple-element.82), channel_id=1, source_target_pairs={{8,0},{16,24},{9,1},{17,25},{10,2},{18,26},{11,3},{19,27},{12,4},{... | collective-permute-start | bytes 884744 | tf_op jit(solution)/shard_map/ppermute | solution.py:370
  85.3 6.7 %collective-permute-start.19 = (bf16[1024,128]{1,0:T(8,128)(2,1)S(1)}, bf16[1024,128]{1,0:T(8,128)(2,1)S(1)}, u32[]{:S(2)}, u32[]{:S(2)}) collective-permute-start(bf16[1024,128]{1,0:T(8,128)(2,1)S(1)} %merge_0.1.refs_0_), channel_id=1, source_target_pairs={{0,6},{1,7},{2,4},{3,5},{4,2},{5,3},{6,0},{7,1},{8,14},{9,15},{10,... | collective-permute-start | bytes 786440 | tf_op jit(solution)/shard_map/ppermute | solution.py:351
  86.8 13.1 %collective-permute-start.17 = (bf16[1024,128]{1,0:T(8,128)(2,1)S(1)}, bf16[1024,128]{1,0:T(8,128)(2,1)S(1)}, u32[]{:S(2)}, u32[]{:S(2)}) collective-permute-start(bf16[1024,128]{1,0:T(8,128)(2,1)S(1)} %merge_0.1.refs_0_), channel_id=1, source_target_pairs={{0,4},{1,5},{2,6},{3,7},{4,0},{5,1},{6,2},{7,3},{8,12},{9,13},{10,... | collective-permute-start | bytes 786440 | tf_op jit(solution)/shard_map/ppermute | solution.py:351
  87.1 15.3 %collective-permute-start.15 = (bf16[1024,128]{1,0:T(8,128)(2,1)S(1)}, bf16[1024,128]{1,0:T(8,128)(2,1)S(1)}, u32[]{:S(2)}, u32[]{:S(2)}) collective-permute-start(bf16[1024,128]{1,0:T(8,128)(2,1)S(1)} %merge_0.1.refs_0_), channel_id=1, source_target_pairs={{0,2},{1,3},{2,0},{3,1},{4,6},{5,7},{6,4},{7,5},{8,10},{9,11},{10,... | collective-permute-start | bytes 786440 | tf_op jit(solution)/shard_map/ppermute | solution.py:351
  88.0 14.6 %collective-permute-start.14 = (bf16[1024,128]{1,0:T(8,128)(2,1)S(1)}, bf16[1024,128]{1,0:T(8,128)(2,1)S(1)}, u32[]{:S(2)}, u32[]{:S(2)}) collective-permute-start(bf16[1024,128]{1,0:T(8,128)(2,1)S(1)} %merge_0.1.refs_0_), channel_id=1, source_target_pairs={{0,1},{1,0},{2,3},{3,2},{4,5},{5,4},{6,7},{7,6},{8,9},{9,8},{10,11... | collective-permute-start | bytes 786440 | tf_op jit(solution)/shard_map/ppermute | solution.py:351
  92.0 11.6 %collective-permute-start.20 = (bf16[1024,128]{1,0:T(8,128)(2,1)S(1)}, bf16[1024,128]{1,0:T(8,128)(2,1)S(1)}, u32[]{:S(2)}, u32[]{:S(2)}) collective-permute-start(bf16[1024,128]{1,0:T(8,128)(2,1)S(1)} %collective-permute-done.19.refs_6_), channel_id=1, source_target_pairs={{0,1},{1,0},{2,3},{3,2},{4,5},{5,4},{6,7},{7,6},{8,9},{9,8},{10,11... | collective-permute-start | bytes 786440 | tf_op jit(solution)/shard_map/ppermute | solution.py:351
  100.8 8.9 %collective-permute-start.31 = (bf16[1024,128]{1,0:T(8,128)(2,1)S(1)}, bf16[1024,128]{1,0:T(8,128)(2,1)S(1)}, u32[]{:S(2)}, u32[]{:S(2)}) collective-permute-start(bf16[1024,128]{1,0:T(8,128)(2,1)S(1)} %merge_1.1.refs_8_), channel_id=1, source_target_pairs={{0,6},{1,7},{2,4},{3,5},{4,2},{5,3},{6,0},{7,1},{8,14},{9,15},{10,... | collective-permute-start | bytes 786440 | tf_op jit(solution)/shard_map/ppermute | solution.py:351
  102.4 13.3 %collective-permute-start.29 = (bf16[1024,128]{1,0:T(8,128)(2,1)S(1)}, bf16[1024,128]{1,0:T(8,128)(2,1)S(1)}, u32[]{:S(2)}, u32[]{:S(2)}) collective-permute-start(bf16[1024,128]{1,0:T(8,128)(2,1)S(1)} %merge_1.1.refs_8_), channel_id=1, source_target_pairs={{0,4},{1,5},{2,6},{3,7},{4,0},{5,1},{6,2},{7,3},{8,12},{9,13},{10,... | collective-permute-start | bytes 786440 | tf_op jit(solution)/shard_map/ppermute | solution.py:351
  102.6 13.5 %collective-permute-start.27 = (bf16[1024,128]{1,0:T(8,128)(2,1)S(1)}, bf16[1024,128]{1,0:T(8,128)(2,1)S(1)}, u32[]{:S(2)}, u32[]{:S(2)}) collective-permute-start(bf16[1024,128]{1,0:T(8,128)(2,1)S(1)} %merge_1.1.refs_8_), channel_id=1, source_target_pairs={{0,2},{1,3},{2,0},{3,1},{4,6},{5,7},{6,4},{7,5},{8,10},{9,11},{10,... | collective-permute-start | bytes 786440 | tf_op jit(solution)/shard_map/ppermute | solution.py:351
  103.6 12.6 %collective-permute-start.16 = (bf16[1024,128]{1,0:T(8,128)(2,1)S(1)}, bf16[1024,128]{1,0:T(8,128)(2,1)S(1)}, u32[]{:S(2)}, u32[]{:S(2)}) collective-permute-start(bf16[1024,128]{1,0:T(8,128)(2,1)S(1)} %collective-permute-done.15.refs_2_), channel_id=1, source_target_pairs={{0,1},{1,0},{2,3},{3,2},{4,5},{5,4},{6,7},{7,6},{8,9},{9,8},{10,11... | collective-permute-start | bytes 786440 | tf_op jit(solution)/shard_map/ppermute | solution.py:351
  104.4 11.8 %collective-permute-start.26 = (bf16[1024,128]{1,0:T(8,128)(2,1)S(1)}, bf16[1024,128]{1,0:T(8,128)(2,1)S(1)}, u32[]{:S(2)}, u32[]{:S(2)}) collective-permute-start(bf16[1024,128]{1,0:T(8,128)(2,1)S(1)} %merge_1.1.refs_8_), channel_id=1, source_target_pairs={{0,1},{1,0},{2,3},{3,2},{4,5},{5,4},{6,7},{7,6},{8,9},{9,8},{10,11... | collective-permute-start | bytes 786440 | tf_op jit(solution)/shard_map/ppermute | solution.py:351
  109.8 6.4 %collective-permute-start.32 = (bf16[1024,128]{1,0:T(8,128)(2,1)S(1)}, bf16[1024,128]{1,0:T(8,128)(2,1)S(1)}, u32[]{:S(2)}, u32[]{:S(2)}) collective-permute-start(bf16[1024,128]{1,0:T(8,128)(2,1)S(1)} %collective-permute-done.31.refs_14_), channel_id=1, source_target_pairs={{0,1},{1,0},{2,3},{3,2},{4,5},{5,4},{6,7},{7,6},{8,9},{9,8},{10,11... | collective-permute-start | bytes 786440 | tf_op jit(solution)/shard_map/ppermute | solution.py:351
  (12 other events, 91.5 us)

commit v13 on v10

--- a/solution.py
+++ b/solution.py
@@ -373,7 +373,7 @@
         mixed = [y if i == 0 else swap(y, 2 * i) for i, y in enumerate(x)]
         mixed = after(mixed, before)
         theirs = swap(jnp.stack([y[1] for y in mixed]), 1)
-        return jnp.concatenate([jnp.stack([y[0] for y in mixed]), theirs])
+        return jnp.concatenate([jnp.stack([y[0] for y in mixed]), theirs]), mixed
 
     def blocks(x):
         return x[:, : 2 * shard].reshape(n_ka * key_blocks, 2, BLOCK, HEAD_DIM)
@@ -387,17 +387,18 @@
     parts = (block_mask.T,) + ((inward(block_mask.T),) if relay else ())
     owns, over, guest = [], [], [None] * heads
     for c in range(heads):
-        place_of = after(me1, (q, owns[0])) if c else me1
+        place_of = after(me1, (q, mixed)) if c else me1
         packed = pack(place_of, keys, values, parts if c == heads - 1 else (), n_ka, heads, c)
         if c == 0:
             q = turn(after(me1, packed), queries, heads)
-            own = sort(packed, (q, parts))
+            own, mixed = sort(packed, (q, parts))
         else:
-            own = sort(packed, over[0])
+            own, mixed = sort(after(packed, owns[0]), over[0])
         owns.append(blocks(own))
-        over.append([exchange(after(owns[c], (over[0][1], guest[0]) if c else None), odd, 1) for odd in (0, 1)])
+        before = ((over[0], guest[0]), over[0]) if c else (None, None)
+        over.append([exchange(after(owns[c], before[odd]), odd, 1) for odd in (0, 1)])
         if relay:
-            guest[c] = inward(after(q[c], over[c]))
+            guest[c] = inward(after(q[c], over[0]))
     size = mask_rows(block_mask.shape[1])
     masks = [flags(own[:, 2 * shard + i * size :]) for i in range(len(parts))]
 
@@ -423,7 +424,7 @@
             sources = ([owns[c]] if step == 0 else []) + over[c]
             even, odd = over[c]
             if even is not None and odd is not None:
-                even, odd = lax.optimization_barrier((even, odd))
+                even, odd = after((even, odd), guest[c] if c else (even, odd))
             over[c] = [exchange(odd, 0, step + 2), exchange(even, 1, step + 2)]
             state[c] = run(c, step, sources)
 

time: 108 us -> 106 us (0.981)
  starting transfers between devices: 46.2 us -> 40.2 us
  waiting for transfers between devices: 35.2 us -> 40 us
    ppermute x3, starting transfers between devices: 14.5 us -> 9.46 us  [inward(): return lax.ppermute(x, 'pb', [(0, 1), (n_pb - 1, n_pb - 2)])]
    ppermute x2, waiting for transfers between devices: 7.1 us -> 12 us  [outward(): return lax.ppermute(x, 'pb', [(1, 0), (n_pb - 2, n_pb - 1)])]
    ppermute x3, waiting for transfers between devices: 5.52 us -> 7.26 us  [inward(): return lax.ppermute(x, 'pb', [(0, 1), (n_pb - 1, n_pb - 2)])]
  transfers between devices with their start and end apart: 33 -> 33, of which waited for: 16 -> 16; matrix products, arithmetic and copies ran while one was open for 1% -> 1% of each run, Pallas kernels for 18% -> 17%
where the time goes in v13:
time: 106 us; the launch traced here: 105 us
  starting transfers between devices  40.2 us (38%)
  waiting for transfers between devices  40 us (38%)
  Pallas kernels  22.7 us (21%)
  local copies, waits for them, and re-layouts  1.37 us (1%)
    ppermute x22, waiting for transfers between devices, swap(): return lax.ppermute(x, 'ka', [(i, i ^ k) for i in range(n_ka)])  20.7 us
    ppermute x22, starting transfers between devices, swap(): return lax.ppermute(x, 'ka', [(i, i ^ k) for i in range(n_ka)])  16.9 us
    ppermute x2, waiting for transfers between devices, outward(): return lax.ppermute(x, 'pb', [(1, 0), (n_pb - 2, n_pb - 1)])  12 us
    ppermute x6, starting transfers between devices, exchange(): return lax.ppermute(x, 'pb', found) if found else None  11.2 us
    pallas_call x4, Pallas kernels, attend(): pl.pallas_call(functools.partial(attend_kernel, n_src, entry, first, mode...  10.4 us
    ppermute x3, starting transfers between devices, inward(): return lax.ppermute(x, 'pb', [(0, 1), (n_pb - 1, n_pb - 2)])  9.46 us
    ppermute x3, waiting for transfers between devices, inward(): return lax.ppermute(x, 'pb', [(0, 1), (n_pb - 1, n_pb - 2)])  7.26 us
    pallas_call x2, Pallas kernels, pack(): pl.pallas_call(functools.partial(pack_kernel, n_ka, heads, c, len(masks))...  5.38 us
  transfers between devices with their start and end apart: 33, of which 16 were waited for; matrix products, arithmetic and copies ran while one was open for 1% of the time, Pallas kernels for 17%

profile of v13, /device:TPU:0, one launch (start us, length us, event | category | flops | bytes accessed | tf_op | source)
XLA Modules:
  0.0 105.4 jit_solution(11270654987884412177)
XLA Ops:
  0.0 2.3 %pack_0.1 = (bf16[2,256,128]{2,1,0:T(8,128)(2,1)}, bf16[2,256,128]{2,1,0:T(8,128)(2,1)}, bf16[2,256,128]{2,1,0:T(8,128)(2,1)}, bf16[2,256,128]{2,1,0:T(8,128)(2,1)}) custom-call(s32[1]{0:T(128)} %bitcast.me_ref, bf16[128,2048]{1,0:T(8,128)(2,1)} %refs_2_.1, bf16[128,2048]{1,0:T(8,128)(2,1)} %refs_3_.1), custom_call_target="tpu_custom_call" | custom-call | bytes 262144 | tf_op jit(solution)/shard_map/pack_0/pallas_call | solution.py:77
  2.3 3.0 %collective-permute-start = (bf16[2,256,128]{2,1,0:T(8,128)(2,1)}, bf16[2,256,128]{2,1,0:T(8,128)(2,1)S(1)}, u32[]{:S(2)}, u32[]{:S(2)}) collective-permute-start(bf16[2,256,128]{2,1,0:T(8,128)(2,1)} %get-tuple-element.55), channel_id=1, source_target_pairs={{0,2},{1,3},{2,0},{3,1},{4,6},{5,7},{6,4},{7,5},{8,10},{9,11},{10,... | collective-permute-start | bytes 393224 | tf_op jit(solution)/shard_map/ppermute | solution.py:351
  6.9 3.9 %collective-permute-start.3 = (s32[4,8]{1,0:T(4,128)}, s32[4,8]{1,0:T(4,128)S(1)}, u32[]{:S(2)}, u32[]{:S(2)}) collective-permute-start(s32[4,8]{1,0:T(4,128)} %bitcast.12), channel_id=1, source_target_pairs={{0,8},{24,16},{1,9},{25,17},{2,10},{26,18},{3,11},{27,19},{4,12},{... | collective-permute-start | bytes 392 | tf_op jit(solution)/shard_map/ppermute | solution.py:367
  10.8 2.0 %turn.1 = (bf16[8,128,128]{2,1,0:T(8,128)(2,1)}, bf16[8,128,128]{2,1,0:T(8,128)(2,1)}) custom-call(s32[1]{0:T(128)} %bitcast.me_ref, bf16[1024,2048]{1,0:T(8,128)(2,1)} %q_all.1), custom_call_target="tpu_custom_call" | custom-call | bytes 131072 | tf_op jit(solution)/shard_map/turn/pallas_call | solution.py:105
  15.8 4.4 %collective-permute-start.8 = (bf16[8,2,128,128]{3,2,1,0:T(8,128)(2,1)S(1)}, bf16[8,2,128,128]{3,2,1,0:T(8,128)(2,1)S(1)}, u32[]{:S(2)}, u32[]{:S(2)}) collective-permute-start(bf16[8,2,128,128]{3,2,1,0:T(8,128)(2,1)S(1)} %bitcast.10), channel_id=1, source_target_pairs={{0,8},{8,0},{16,24},{24,16},{1,9},{9,1},{17,25},{25,17},{2,10},{10... | collective-permute-start | bytes 1572872 | tf_op jit(solution)/shard_map/ppermute | solution.py:364
  20.2 3.1 %pack_1.1 = (bf16[2,288,128]{2,1,0:T(8,128)(2,1)}, bf16[2,288,128]{2,1,0:T(8,128)(2,1)}, bf16[2,288,128]{2,1,0:T(8,128)(2,1)}, bf16[2,288,128]{2,1,0:T(8,128)(2,1)}) custom-call(s32[1]{0:T(128)} %bitcast.me_ref, s32[4,8]{1,0:T(4,128)} %bitcast.13, s32[4,8]{1,0:T(4,128)} %copy-done.4, bf16[128,2048]{1,0:T(8,128)(2,1)} %refs_2_.1, bf16[128,2048]{1,0:T(8,128)(2,1)} %refs_3_.1), custom_call_target="tpu_custom_call" | custom-call | bytes 262144 | tf_op jit(solution)/shard_map/pack_1/pallas_call | solution.py:77
  26.9 3.1 %collective-permute-done.5 = bf16[2,288,128]{2,1,0:T(8,128)(2,1)S(1)} collective-permute-done((bf16[2,288,128]{2,1,0:T(8,128)(2,1)}, bf16[2,288,128]{2,1,0:T(8,128)(2,1)S(1)}, u32[]{:S(2)}, u32[]{:S(2)}) %collective-permute-start.5) | collective-permute-done | bytes 147488 | tf_op jit(solution)/shard_map/ppermute | solution.py:351
  30.0 3.1 %collective-permute-done.6 = bf16[2,288,128]{2,1,0:T(8,128)(2,1)S(1)} collective-permute-done((bf16[2,288,128]{2,1,0:T(8,128)(2,1)}, bf16[2,288,128]{2,1,0:T(8,128)(2,1)S(1)}, u32[]{:S(2)}, u32[]{:S(2)}) %collective-permute-start.6) | collective-permute-done | bytes 147488 | tf_op jit(solution)/shard_map/ppermute | solution.py:351
  34.3 2.7 %collective-permute-start.11 = (bf16[8,128,128]{2,1,0:T(8,128)(2,1)S(1)}, bf16[8,128,128]{2,1,0:T(8,128)(2,1)S(1)}, u32[]{:S(2)}, u32[]{:S(2)}) collective-permute-start(bf16[8,128,128]{2,1,0:T(8,128)(2,1)S(1)} %copy-done.1), channel_id=1, source_target_pairs={{0,8},{24,16},{1,9},{25,17},{2,10},{26,18},{3,11},{27,19},{4,12},{... | collective-permute-start | bytes 786440 | tf_op jit(solution)/shard_map/ppermute | solution.py:367
  38.6 4.6 %collective-permute-done.11.refs_0_ = bf16[8,128,128]{2,1,0:T(8,128)(2,1)S(1)} collective-permute-done((bf16[8,128,128]{2,1,0:T(8,128)(2,1)S(1)}, bf16[8,128,128]{2,1,0:T(8,128)(2,1)S(1)}, u32[]{:S(2)}, u32[]{:S(2)}) %collective-permute-start.11) | collective-permute-done | bytes 262176 | tf_op jit(solution)/shard_map/ppermute | solution.py:367
  43.2 2.5 %collective-permute-start.22 = (bf16[8,2,128,128]{3,2,1,0:T(8,128)(2,1)S(1)}, bf16[8,2,128,128]{3,2,1,0:T(8,128)(2,1)}, u32[]{:S(2)}, u32[]{:S(2)}) collective-permute-start(bf16[8,2,128,128]{3,2,1,0:T(8,128)(2,1)S(1)} %bitcast.6), channel_id=1, source_target_pairs={{0,8},{8,0},{16,24},{24,16},{1,9},{9,1},{17,25},{25,17},{2,10},{10... | collective-permute-start | bytes 1572872 | tf_op jit(solution)/shard_map/ppermute | solution.py:364
  47.1 2.8 %collective-permute-start.21 = (bf16[8,128,128]{2,1,0:T(8,128)(2,1)S(1)}, bf16[8,128,128]{2,1,0:T(8,128)(2,1)S(1)}, u32[]{:S(2)}, u32[]{:S(2)}) collective-permute-start(bf16[8,128,128]{2,1,0:T(8,128)(2,1)S(1)} %copy-done), channel_id=1, source_target_pairs={{0,8},{24,16},{1,9},{25,17},{2,10},{26,18},{3,11},{27,19},{4,12},{... | collective-permute-start | bytes 786440 | tf_op jit(solution)/shard_map/ppermute | solution.py:367
  50.9 2.4 %plan.1 = (s32[2]{0:T(128)S(1)}, s32[432]{0:T(512)S(1)}, s32[176]{0:T(256)S(1)}) custom-call(s32[1]{0:T(128)} %bitcast.2.pb_ref, s32[256]{0:T(256)S(1)} %reshape.24.refs_0_, s32[256]{0:T(256)S(1)} %reshape.26.refs_1_), custom_call_target="tpu_custom_call" | custom-call | tf_op jit(solution)/shard_map/plan/pallas_call | solution.py:159
  53.3 3.4 %attend_0_0.1 = (f32[16,1,128]{2,1,0:T(1,128)S(1)}, f32[16,1,128]{2,1,0:T(1,128)S(1)}, f32[16,128,128]{2,1,0:T(8,128)S(1)}) custom-call(s32[2]{0:T(128)S(1)} %get-tuple-element.78.count_ref, s32[432]{0:T(512)S(1)} %get-tuple-element.82.live_ref, bf16[8,128,128]{2,1,0:T(8,128)(2,1)S(1)} %copy-done.1, ...), custom_call_target="tpu_custom_call" | custom-call | bytes 16384 | tf_op jit(solution)/shard_map/attend_0_0/pallas_call | solution.py:273
  59.8 2.7 %collective-permute-done.21.refs_0_ = bf16[8,128,128]{2,1,0:T(8,128)(2,1)S(1)} collective-permute-done((bf16[8,128,128]{2,1,0:T(8,128)(2,1)S(1)}, bf16[8,128,128]{2,1,0:T(8,128)(2,1)S(1)}, u32[]{:S(2)}, u32[]{:S(2)}) %collective-permute-start.21) | collective-permute-done | bytes 262176 | tf_op jit(solution)/shard_map/ppermute | solution.py:367
  63.1 5.4 %collective-permute-done.13.part_ref = bf16[8,144,128]{2,1,0:T(8,128)(2,1)S(1)} collective-permute-done((bf16[8,144,128]{2,1,0:T(8,128)(2,1)S(1)}, bf16[8,144,128]{2,1,0:T(8,128)(2,1)S(1)}, u32[]{:S(2)}, u32[]{:S(2)}) %collective-permute-start.13) | collective-permute-done | bytes 294944 | tf_op jit(solution)/shard_map/ppermute | solution.py:370
  72.3 4.4 %attend_1_0.1 = (f32[16,1,128]{2,1,0:T(1,128)S(1)}, f32[16,1,128]{2,1,0:T(1,128)S(1)}, f32[16,128,128]{2,1,0:T(8,128)S(1)}) custom-call(s32[2]{0:T(128)S(1)} %get-tuple-element.78.count_ref, s32[432]{0:T(512)S(1)} %get-tuple-element.82.live_ref, bf16[8,128,128]{2,1,0:T(8,128)(2,1)S(1)} %copy-done, bf16[8,128,128]{2,1,0:T(8,128)(2,1)S(1)} %collective-permute-done.21.refs_0_, ...), custom_call_target="tpu_custom_call" | custom-call | bytes 16384 | tf_op jit(solution)/shard_map/attend_1_0/pallas_call | solution.py:273
  77.1 2.2 %collective-permute-done.15.refs_2_ = bf16[1024,128]{1,0:T(8,128)(2,1)S(1)} collective-permute-done((bf16[1024,128]{1,0:T(8,128)(2,1)S(1)}, bf16[1024,128]{1,0:T(8,128)(2,1)S(1)}, u32[]{:S(2)}, u32[]{:S(2)}) %collective-permute-start.15) | collective-permute-done | bytes 262176 | tf_op jit(solution)/shard_map/ppermute | solution.py:351
  80.2 1.9 %collective-permute-done.19.refs_6_ = bf16[1024,128]{1,0:T(8,128)(2,1)S(1)} collective-permute-done((bf16[1024,128]{1,0:T(8,128)(2,1)S(1)}, bf16[1024,128]{1,0:T(8,128)(2,1)S(1)}, u32[]{:S(2)}, u32[]{:S(2)}) %collective-permute-start.19) | collective-permute-done | bytes 262176 | tf_op jit(solution)/shard_map/ppermute | solution.py:351
  84.0 6.7 %collective-permute-done.25.part_ref = bf16[8,144,128]{2,1,0:T(8,128)(2,1)S(1)} collective-permute-done((bf16[8,144,128]{2,1,0:T(8,128)(2,1)S(1)}, bf16[8,144,128]{2,1,0:T(8,128)(2,1)S(1)}, u32[]{:S(2)}, u32[]{:S(2)}) %collective-permute-start.25) | collective-permute-done | bytes 294944 | tf_op jit(solution)/shard_map/ppermute | solution.py:370
  90.9 2.2 %collective-permute-start.31 = (bf16[1024,128]{1,0:T(8,128)(2,1)S(1)}, bf16[1024,128]{1,0:T(8,128)(2,1)S(1)}, u32[]{:S(2)}, u32[]{:S(2)}) collective-permute-start(bf16[1024,128]{1,0:T(8,128)(2,1)S(1)} %merge_1.1.refs_8_), channel_id=1, source_target_pairs={{0,6},{1,7},{2,4},{3,5},{4,2},{5,3},{6,0},{7,1},{8,14},{9,15},{10,... | collective-permute-start | bytes 786440 | tf_op jit(solution)/shard_map/ppermute | solution.py:351
  95.0 3.7 %collective-permute-done.31.refs_14_ = bf16[1024,128]{1,0:T(8,128)(2,1)S(1)} collective-permute-done((bf16[1024,128]{1,0:T(8,128)(2,1)S(1)}, bf16[1024,128]{1,0:T(8,128)(2,1)S(1)}, u32[]{:S(2)}, u32[]{:S(2)}) %collective-permute-start.31) | collective-permute-done | bytes 262176 | tf_op jit(solution)/shard_map/ppermute | solution.py:351
  98.7 2.7 %collective-permute-done.29.refs_12_ = bf16[1024,128]{1,0:T(8,128)(2,1)S(1)} collective-permute-done((bf16[1024,128]{1,0:T(8,128)(2,1)S(1)}, bf16[1024,128]{1,0:T(8,128)(2,1)S(1)}, u32[]{:S(2)}, u32[]{:S(2)}) %collective-permute-start.29) | collective-permute-done | bytes 262176 | tf_op jit(solution)/shard_map/ppermute | solution.py:351
  103.3 2.1 %place.1 = bf16[1024,2048]{1,0:T(8,128)(2,1)} custom-call(s32[1]{0:T(128)} %bitcast.me_ref, bf16[1024,128]{1,0:T(8,128)(2,1)S(1)} %merge_0.1.refs_0_, bf16[1024,128]{1,0:T(8,128)(2,1)S(1)} %collective-permute-done.14.refs_1_, bf16[1024,128]{1,0:T(8,128)(2,1)S(1)} %collective-permute-done.15.refs_2_, bf16[1024,128]{1,0:T(8,128)(2,1)S(1)} %collective-permute-done.16.refs_3_, ...), custom_call_target="tpu_custom_call" | custom-call | tf_op jit(solution)/shard_map/place/pallas_call | solution.py:330
  (79 shorter events, 27.7 us)
Async XLA Ops:
  2.3 10.5 %collective-permute-start = (bf16[2,256,128]{2,1,0:T(8,128)(2,1)}, bf16[2,256,128]{2,1,0:T(8,128)(2,1)S(1)}, u32[]{:S(2)}, u32[]{:S(2)}) collective-permute-start(bf16[2,256,128]{2,1,0:T(8,128)(2,1)} %get-tuple-element.55), channel_id=1, source_target_pairs={{0,2},{1,3},{2,0},{3,1},{4,6},{5,7},{6,4},{7,5},{8,10},{9,11},{10,... | collective-permute-start | bytes 393224 | tf_op jit(solution)/shard_map/ppermute | solution.py:351
  5.3 8.0 %collective-permute-start.1 = (bf16[2,256,128]{2,1,0:T(8,128)(2,1)}, bf16[2,256,128]{2,1,0:T(8,128)(2,1)S(1)}, u32[]{:S(2)}, u32[]{:S(2)}) collective-permute-start(bf16[2,256,128]{2,1,0:T(8,128)(2,1)} %get-tuple-element.56), channel_id=1, source_target_pairs={{0,4},{1,5},{2,6},{3,7},{4,0},{5,1},{6,2},{7,3},{8,12},{9,13},{10,... | collective-permute-start | bytes 393224 | tf_op jit(solution)/shard_map/ppermute | solution.py:351
  15.1 18.0 %collective-permute-start.9 = (bf16[8,2,128,128]{3,2,1,0:T(8,128)(2,1)S(1)}, bf16[8,2,128,128]{3,2,1,0:T(8,128)(2,1)S(1)}, u32[]{:S(2)}, u32[]{:S(2)}) collective-permute-start(bf16[8,2,128,128]{3,2,1,0:T(8,128)(2,1)S(1)} %bitcast.9), channel_id=1, source_target_pairs={{8,16},{16,8},{9,17},{17,9},{10,18},{18,10},{11,19},{19,11},{12,20... | collective-permute-start | bytes 1572872 | tf_op jit(solution)/shard_map/ppermute | solution.py:364
  15.8 17.3 %collective-permute-start.8 = (bf16[8,2,128,128]{3,2,1,0:T(8,128)(2,1)S(1)}, bf16[8,2,128,128]{3,2,1,0:T(8,128)(2,1)S(1)}, u32[]{:S(2)}, u32[]{:S(2)}) collective-permute-start(bf16[8,2,128,128]{3,2,1,0:T(8,128)(2,1)S(1)} %bitcast.10), channel_id=1, source_target_pairs={{0,8},{8,0},{16,24},{24,16},{1,9},{9,1},{17,25},{25,17},{2,10},{10... | collective-permute-start | bytes 1572872 | tf_op jit(solution)/shard_map/ppermute | solution.py:364
  24.6 8.5 %collective-permute-start.6 = (bf16[2,288,128]{2,1,0:T(8,128)(2,1)}, bf16[2,288,128]{2,1,0:T(8,128)(2,1)S(1)}, u32[]{:S(2)}, u32[]{:S(2)}) collective-permute-start(bf16[2,288,128]{2,1,0:T(8,128)(2,1)} %get-tuple-element.72), channel_id=1, source_target_pairs={{0,4},{1,5},{2,6},{3,7},{4,0},{5,1},{6,2},{7,3},{8,12},{9,13},{10,... | collective-permute-start | bytes 442376 | tf_op jit(solution)/shard_map/ppermute | solution.py:351
  34.3 8.9 %collective-permute-start.11 = (bf16[8,128,128]{2,1,0:T(8,128)(2,1)S(1)}, bf16[8,128,128]{2,1,0:T(8,128)(2,1)S(1)}, u32[]{:S(2)}, u32[]{:S(2)}) collective-permute-start(bf16[8,128,128]{2,1,0:T(8,128)(2,1)S(1)} %copy-done.1), channel_id=1, source_target_pairs={{0,8},{24,16},{1,9},{25,17},{2,10},{26,18},{3,11},{27,19},{4,12},{... | collective-permute-start | bytes 786440 | tf_op jit(solution)/shard_map/ppermute | solution.py:367
  37.0 19.7 %collective-permute-start.12 = (bf16[8,2,128,128]{3,2,1,0:T(8,128)(2,1)S(1)}, bf16[8,2,128,128]{3,2,1,0:T(8,128)(2,1)}, u32[]{:S(2)}, u32[]{:S(2)}) collective-permute-start(bf16[8,2,128,128]{3,2,1,0:T(8,128)(2,1)S(1)} %collective-permute-done.8.refs_2_), channel_id=1, source_target_pairs={{8,16},{16,8},{9,17},{17,9},{10,18},{18,10},{11,19},{19,11},{12,20... | collective-permute-start | bytes 1572872 | tf_op jit(solution)/shard_map/ppermute | solution.py:364
  43.2 19.2 %collective-permute-start.22 = (bf16[8,2,128,128]{3,2,1,0:T(8,128)(2,1)S(1)}, bf16[8,2,128,128]{3,2,1,0:T(8,128)(2,1)}, u32[]{:S(2)}, u32[]{:S(2)}) collective-permute-start(bf16[8,2,128,128]{3,2,1,0:T(8,128)(2,1)S(1)} %bitcast.6), channel_id=1, source_target_pairs={{0,8},{8,0},{16,24},{24,16},{1,9},{9,1},{17,25},{25,17},{2,10},{10... | collective-permute-start | bytes 1572872 | tf_op jit(solution)/shard_map/ppermute | solution.py:364
  45.6 16.8 %collective-permute-start.23 = (bf16[8,2,128,128]{3,2,1,0:T(8,128)(2,1)S(1)}, bf16[8,2,128,128]{3,2,1,0:T(8,128)(2,1)}, u32[]{:S(2)}, u32[]{:S(2)}) collective-permute-start(bf16[8,2,128,128]{3,2,1,0:T(8,128)(2,1)S(1)} %bitcast.7), channel_id=1, source_target_pairs={{8,16},{16,8},{9,17},{17,9},{10,18},{18,10},{11,19},{19,11},{12,20... | collective-permute-start | bytes 1572872 | tf_op jit(solution)/shard_map/ppermute | solution.py:364
  47.1 15.3 %collective-permute-start.21 = (bf16[8,128,128]{2,1,0:T(8,128)(2,1)S(1)}, bf16[8,128,128]{2,1,0:T(8,128)(2,1)S(1)}, u32[]{:S(2)}, u32[]{:S(2)}) collective-permute-start(bf16[8,128,128]{2,1,0:T(8,128)(2,1)S(1)} %copy-done), channel_id=1, source_target_pairs={{0,8},{24,16},{1,9},{25,17},{2,10},{26,18},{3,11},{27,19},{4,12},{... | collective-permute-start | bytes 786440 | tf_op jit(solution)/shard_map/ppermute | solution.py:367
  58.5 10.0 %collective-permute-start.13 = (bf16[8,144,128]{2,1,0:T(8,128)(2,1)S(1)}, bf16[8,144,128]{2,1,0:T(8,128)(2,1)S(1)}, u32[]{:S(2)}, u32[]{:S(2)}) collective-permute-start(bf16[8,144,128]{2,1,0:T(8,128)(2,1)S(1)} %get-tuple-element.89), channel_id=1, source_target_pairs={{8,0},{16,24},{9,1},{17,25},{10,2},{18,26},{11,3},{19,27},{12,4},{... | collective-permute-start | bytes 884744 | tf_op jit(solution)/shard_map/ppermute | solution.py:370
  62.4 16.9 %collective-permute-start.24 = (bf16[8,2,128,128]{3,2,1,0:T(8,128)(2,1)}, bf16[8,2,128,128]{3,2,1,0:T(8,128)(2,1)S(1)}, u32[]{:S(2)}, u32[]{:S(2)}) collective-permute-start(bf16[8,2,128,128]{3,2,1,0:T(8,128)(2,1)} %collective-permute-done.22.refs_2_), channel_id=1, source_target_pairs={{8,16},{16,8},{9,17},{17,9},{10,18},{18,10},{11,19},{19,11},{12,20... | collective-permute-start | bytes 1572872 | tf_op jit(solution)/shard_map/ppermute | solution.py:364
  68.7 8.4 %collective-permute-start.17 = (bf16[1024,128]{1,0:T(8,128)(2,1)S(1)}, bf16[1024,128]{1,0:T(8,128)(2,1)S(1)}, u32[]{:S(2)}, u32[]{:S(2)}) collective-permute-start(bf16[1024,128]{1,0:T(8,128)(2,1)S(1)} %merge_0.1.refs_0_), channel_id=1, source_target_pairs={{0,4},{1,5},{2,6},{3,7},{4,0},{5,1},{6,2},{7,3},{8,12},{9,13},{10,... | collective-permute-start | bytes 786440 | tf_op jit(solution)/shard_map/ppermute | solution.py:351
  70.3 9.1 %collective-permute-start.15 = (bf16[1024,128]{1,0:T(8,128)(2,1)S(1)}, bf16[1024,128]{1,0:T(8,128)(2,1)S(1)}, u32[]{:S(2)}, u32[]{:S(2)}) collective-permute-start(bf16[1024,128]{1,0:T(8,128)(2,1)S(1)} %merge_0.1.refs_0_), channel_id=1, source_target_pairs={{0,2},{1,3},{2,0},{3,1},{4,6},{5,7},{6,4},{7,5},{8,10},{9,11},{10,... | collective-permute-start | bytes 786440 | tf_op jit(solution)/shard_map/ppermute | solution.py:351
  71.5 10.6 %collective-permute-start.19 = (bf16[1024,128]{1,0:T(8,128)(2,1)S(1)}, bf16[1024,128]{1,0:T(8,128)(2,1)S(1)}, u32[]{:S(2)}, u32[]{:S(2)}) collective-permute-start(bf16[1024,128]{1,0:T(8,128)(2,1)S(1)} %merge_0.1.refs_0_), channel_id=1, source_target_pairs={{0,6},{1,7},{2,4},{3,5},{4,2},{5,3},{6,0},{7,1},{8,14},{9,15},{10,... | collective-permute-start | bytes 786440 | tf_op jit(solution)/shard_map/ppermute | solution.py:351
  82.1 8.6 %collective-permute-start.25 = (bf16[8,144,128]{2,1,0:T(8,128)(2,1)S(1)}, bf16[8,144,128]{2,1,0:T(8,128)(2,1)S(1)}, u32[]{:S(2)}, u32[]{:S(2)}) collective-permute-start(bf16[8,144,128]{2,1,0:T(8,128)(2,1)S(1)} %get-tuple-element.102), channel_id=1, source_target_pairs={{8,0},{16,24},{9,1},{17,25},{10,2},{18,26},{11,3},{19,27},{12,4},{... | collective-permute-start | bytes 884744 | tf_op jit(solution)/shard_map/ppermute | solution.py:370
  83.4 10.3 %collective-permute-start.14 = (bf16[1024,128]{1,0:T(8,128)(2,1)S(1)}, bf16[1024,128]{1,0:T(8,128)(2,1)S(1)}, u32[]{:S(2)}, u32[]{:S(2)}) collective-permute-start(bf16[1024,128]{1,0:T(8,128)(2,1)S(1)} %merge_0.1.refs_0_), channel_id=1, source_target_pairs={{0,1},{1,0},{2,3},{3,2},{4,5},{5,4},{6,7},{7,6},{8,9},{9,8},{10,11... | collective-permute-start | bytes 786440 | tf_op jit(solution)/shard_map/ppermute | solution.py:351
  83.5 11.0 %collective-permute-start.20 = (bf16[1024,128]{1,0:T(8,128)(2,1)S(1)}, bf16[1024,128]{1,0:T(8,128)(2,1)S(1)}, u32[]{:S(2)}, u32[]{:S(2)}) collective-permute-start(bf16[1024,128]{1,0:T(8,128)(2,1)S(1)} %collective-permute-done.19.refs_6_), channel_id=1, source_target_pairs={{0,1},{1,0},{2,3},{3,2},{4,5},{5,4},{6,7},{7,6},{8,9},{9,8},{10,11... | collective-permute-start | bytes 786440 | tf_op jit(solution)/shard_map/ppermute | solution.py:351
  84.0 10.5 %collective-permute-start.18 = (bf16[1024,128]{1,0:T(8,128)(2,1)S(1)}, bf16[1024,128]{1,0:T(8,128)(2,1)S(1)}, u32[]{:S(2)}, u32[]{:S(2)}) collective-permute-start(bf16[1024,128]{1,0:T(8,128)(2,1)S(1)} %collective-permute-done.17.refs_4_), channel_id=1, source_target_pairs={{0,1},{1,0},{2,3},{3,2},{4,5},{5,4},{6,7},{7,6},{8,9},{9,8},{10,11... | collective-permute-start | bytes 786440 | tf_op jit(solution)/shard_map/ppermute | solution.py:351
  90.9 7.8 %collective-permute-start.31 = (bf16[1024,128]{1,0:T(8,128)(2,1)S(1)}, bf16[1024,128]{1,0:T(8,128)(2,1)S(1)}, u32[]{:S(2)}, u32[]{:S(2)}) collective-permute-start(bf16[1024,128]{1,0:T(8,128)(2,1)S(1)} %merge_1.1.refs_8_), channel_id=1, source_target_pairs={{0,6},{1,7},{2,4},{3,5},{4,2},{5,3},{6,0},{7,1},{8,14},{9,15},{10,... | collective-permute-start | bytes 786440 | tf_op jit(solution)/shard_map/ppermute | solution.py:351
  93.1 8.3 %collective-permute-start.29 = (bf16[1024,128]{1,0:T(8,128)(2,1)S(1)}, bf16[1024,128]{1,0:T(8,128)(2,1)S(1)}, u32[]{:S(2)}, u32[]{:S(2)}) collective-permute-start(bf16[1024,128]{1,0:T(8,128)(2,1)S(1)} %merge_1.1.refs_8_), channel_id=1, source_target_pairs={{0,4},{1,5},{2,6},{3,7},{4,0},{5,1},{6,2},{7,3},{8,12},{9,13},{10,... | collective-permute-start | bytes 786440 | tf_op jit(solution)/shard_map/ppermute | solution.py:351
  93.7 7.8 %collective-permute-start.27 = (bf16[1024,128]{1,0:T(8,128)(2,1)S(1)}, bf16[1024,128]{1,0:T(8,128)(2,1)S(1)}, u32[]{:S(2)}, u32[]{:S(2)}) collective-permute-start(bf16[1024,128]{1,0:T(8,128)(2,1)S(1)} %merge_1.1.refs_8_), channel_id=1, source_target_pairs={{0,2},{1,3},{2,0},{3,1},{4,6},{5,7},{6,4},{7,5},{8,10},{9,11},{10,... | collective-permute-start | bytes 786440 | tf_op jit(solution)/shard_map/ppermute | solution.py:351
  94.5 7.5 %collective-permute-start.16 = (bf16[1024,128]{1,0:T(8,128)(2,1)S(1)}, bf16[1024,128]{1,0:T(8,128)(2,1)S(1)}, u32[]{:S(2)}, u32[]{:S(2)}) collective-permute-start(bf16[1024,128]{1,0:T(8,128)(2,1)S(1)} %collective-permute-done.15.refs_2_), channel_id=1, source_target_pairs={{0,1},{1,0},{2,3},{3,2},{4,5},{5,4},{6,7},{7,6},{8,9},{9,8},{10,11... | collective-permute-start | bytes 786440 | tf_op jit(solution)/shard_map/ppermute | solution.py:351
  94.5 7.5 %collective-permute-start.26 = (bf16[1024,128]{1,0:T(8,128)(2,1)S(1)}, bf16[1024,128]{1,0:T(8,128)(2,1)S(1)}, u32[]{:S(2)}, u32[]{:S(2)}) collective-permute-start(bf16[1024,128]{1,0:T(8,128)(2,1)S(1)} %merge_1.1.refs_8_), channel_id=1, source_target_pairs={{0,1},{1,0},{2,3},{3,2},{4,5},{5,4},{6,7},{7,6},{8,9},{9,8},{10,11... | collective-permute-start | bytes 786440 | tf_op jit(solution)/shard_map/ppermute | solution.py:351
  (14 other events, 119.9 us)

commit v14 on v13

--- a/solution.py
+++ b/solution.py
@@ -90,23 +90,23 @@
 
 
 def turn_kernel(heads, me_ref, q_all, *refs):
-    out_refs, (q_ref, sem) = refs[:heads], refs[heads:]
+    out_ref, q_ref, sem = refs
     column = pl.multiple_of(me_ref[0] * heads * HEAD_DIM, HEAD_DIM)
     copy = pltpu.make_async_copy(q_all.at[:, pl.ds(column, heads * HEAD_DIM)], q_ref, sem)
     copy.start()
     copy.wait()
     for c in range(heads):
-        for r in range(out_refs[c].shape[0]):
-            out_refs[c][r] = q_ref[r * BLOCK : (r + 1) * BLOCK, c * HEAD_DIM : (c + 1) * HEAD_DIM].T
+        for r in range(out_ref.shape[1]):
+            out_ref[c, r] = q_ref[r * BLOCK : (r + 1) * BLOCK, c * HEAD_DIM : (c + 1) * HEAD_DIM].T
 
 
 def turn(me, queries, heads):
     tokens = queries.shape[0]
     return pl.pallas_call(
         functools.partial(turn_kernel, heads),
-        out_shape=[jax.ShapeDtypeStruct((tokens // BLOCK, HEAD_DIM, BLOCK), queries.dtype)] * heads,
+        out_shape=jax.ShapeDtypeStruct((heads, tokens // BLOCK, HEAD_DIM, BLOCK), queries.dtype),
         in_specs=[SMEM, ANY],
-        out_specs=[VMEM] * heads,
+        out_specs=VMEM,
         scratch_shapes=[pltpu.VMEM((tokens, heads * HEAD_DIM), queries.dtype), pltpu.SemaphoreType.DMA],
         compiler_params=params(MOST_VMEM_BYTES),
         cost_estimate=pl.CostEstimate(flops=0, bytes_accessed=queries.size // HEADS, transcendentals=0),
@@ -175,7 +175,7 @@
     return found
 
 
-def attend_kernel(n_src, entry, first, mode, guests, count_ref, live_ref, q_own, *refs):
+def attend_kernel(c, n_src, entry, first, mode, guests, count_ref, live_ref, q_own, *refs):
     n_kv = n_src
     guest_ref, refs = (refs[0], refs[1:]) if guests else (None, refs)
     kv_refs, refs = refs[:n_kv], refs[n_kv:]
@@ -188,14 +188,14 @@
         (*state, kv, q_ref, sems) = refs
     m_ref, l_ref, acc_ref = state
     blocks = kv.shape[0] // n_src
-    rows = q_own.shape[0]
+    rows = q_own.shape[1]
     copies = [
         pltpu.make_async_copy(kv_refs[s], kv.at[pl.ds(s * blocks, blocks)], sems.at[s]) for s in range(n_src)
     ]
     copies += [pltpu.make_async_copy(a, b, sems.at[n_src + i]) for i, (a, b) in enumerate(zip(state_in, state))]
-    copies.append(pltpu.make_async_copy(q_own, q_ref.at[pl.ds(0, rows)], sems.at[n_src + 3]))
+    copies.append(pltpu.make_async_copy(q_own.at[c], q_ref.at[pl.ds(0, rows)], sems.at[n_src + 3]))
     if guests:
-        copies.append(pltpu.make_async_copy(guest_ref, q_ref.at[pl.ds(rows, rows)], sems.at[n_src + 4]))
+        copies.append(pltpu.make_async_copy(guest_ref.at[c], q_ref.at[pl.ds(rows, rows)], sems.at[n_src + 4]))
     for copy in copies:
         copy.start()
     if first:
@@ -249,9 +249,9 @@
             part_ref[r, HEAD_DIM:] = jnp.concatenate(words).astype(part_ref.dtype)
 
 
-def attend(listed, q, guest, sources, state, mode, sets, name):
+def attend(c, listed, q, guest, sources, state, mode, sets, name):
     counts, entry, live = listed
-    rows, dtype = q.shape[0], q.dtype
+    rows, dtype = q.shape[1], q.dtype
     first = state is None
     state = () if first else tuple(state)
     stat = (sets * rows, 1, BLOCK)
@@ -271,7 +271,7 @@
         scratch += [pltpu.VMEM(shape, jnp.float32) for shape in shapes]
     scratch.append(pltpu.SemaphoreType.DMA((n_src + 5,)))
     return pl.pallas_call(
-        functools.partial(attend_kernel, n_src, entry, first, mode, bool(guests)),
+        functools.partial(attend_kernel, c, n_src, entry, first, mode, bool(guests)),
         out_shape=out_shape,
         in_specs=[SMEM, SMEM, ANY] + [ANY] * (len(guests) + n_src + len(state)),
         out_specs=[VMEM] * len(out_shape),
@@ -363,6 +363,10 @@
         found = hops(odd, step)
         return lax.ppermute(x, "pb", found) if found else None
 
+    def relayed(arrived, step, before):
+        even, odd = after(tuple(arrived), before)
+        return [exchange(odd, 0, step), exchange(even, 1, step)]
+
     def inward(x):
         return lax.ppermute(x, "pb", [(0, 1), (n_pb - 1, n_pb - 2)])
 
@@ -384,8 +388,16 @@
     def flags(x):
         return x[:, : block_mask.shape[1], :rows].astype(jnp.int32).reshape(-1)
 
+    steps = [((0, False),)]
+    for step in range(1, n_pb):
+        found = (((step, False),) if hops(0, step) else ()) + (((-step, True),) if hops(1, step) else ())
+        if step == 1:
+            steps[0] += found
+        elif found:
+            steps.append(found)
+    last = len(steps) - 1
     parts = (block_mask.T,) + ((inward(block_mask.T),) if relay else ())
-    owns, over, guest = [], [], [None] * heads
+    owns, over, guest = [], [], None
     for c in range(heads):
         place_of = after(me1, (q, mixed)) if c else me1
         packed = pack(place_of, keys, values, parts if c == heads - 1 else (), n_ka, heads, c)
@@ -395,37 +407,27 @@
         else:
             own, mixed = sort(after(packed, owns[0]), over[0])
         owns.append(blocks(own))
-        before = ((over[0], guest[0]), over[0]) if c else (None, None)
+        if c == heads - 1:
+            size = mask_rows(block_mask.shape[1])
+            masks = [flags(own[:, 2 * shard + i * size :]) for i in range(len(parts))]
+            lists = plan(pb1, masks, steps, n_pb, n_ka, key_blocks, rows, relay)
+        before = ((second, guest, lists[0][0] if c == heads - 1 else None), over[0]) if c else (None, None)
         over.append([exchange(after(owns[c], before[odd]), odd, 1) for odd in (0, 1)])
-        if relay:
-            guest[c] = inward(after(q[c], over[0]))
-    size = mask_rows(block_mask.shape[1])
-    masks = [flags(own[:, 2 * shard + i * size :]) for i in range(len(parts))]
-
-    steps = [((0, False),)]
-    for step in range(1, n_pb):
-        found = (((step, False),) if hops(0, step) else ()) + (((-step, True),) if hops(1, step) else ())
-        if step == 1:
-            steps[0] += found
-        elif found:
-            steps.append(found)
-    last = len(steps) - 1
-    lists = plan(pb1, masks, steps, n_pb, n_ka, key_blocks, rows, relay)
+        if c == 0:
+            guest = inward(after(q, over[0])) if relay else None
+            second = relayed(over[0], 2, over[0])
     state = [None] * heads
 
     def run(c, step, sources):
         kind = "keep" if step < last else "send" if relay else "last"
         sources = [x for x in sources if x is not None]
         name = f"attend_{c}_{step}"
-        return attend(lists[step], q[c], guest[c], sources, state[c], kind, 2 if relay else 1, name)
+        return attend(c, lists[step], q, guest, sources, state[c], kind, 2 if relay else 1, name)
 
     for step in range(last):
         for c in range(heads):
             sources = ([owns[c]] if step == 0 else []) + over[c]
-            even, odd = over[c]
-            if even is not None and odd is not None:
-                even, odd = after((even, odd), guest[c] if c else (even, odd))
-            over[c] = [exchange(odd, 0, step + 2), exchange(even, 1, step + 2)]
+            over[c] = relayed(over[c], step + 2, over[c]) if step or c else second
             state[c] = run(c, step, sources)
 
     pieces = []

time: 106 us -> 113 us (1.066)
  local copies, waits for them, and re-layouts: 1.37 us -> 7.43 us
  waiting for transfers between devices: 40 us -> 42.8 us
  starting transfers between devices: 40.2 us -> 38.5 us
    ppermute x6, waiting for transfers between devices: 0.02 us -> 4.15 us  [exchange(): return lax.ppermute(x, 'pb', found) if found else None]
    ppermute x3 -> x2, waiting for transfers between devices: 7.26 us -> 4.45 us  [inward(): return lax.ppermute(x, 'pb', [(0, 1), (n_pb - 1, n_pb - 2)])]
    ppermute x3 -> x2, starting transfers between devices: 9.46 us -> 6.7 us  [inward(): return lax.ppermute(x, 'pb', [(0, 1), (n_pb - 1, n_pb - 2)])]
    slice x8, local copies, waits for them, and re-layouts: 1.05 us -> 3.55 us  [sort(): theirs = swap(jnp.stack([y[1] for y in mixed]), 1)]
    unnamed x10, local copies, waits for them, and re-layouts: 0.03 us -> 1.84 us
    ppermute x22, waiting for transfers between devices: 20.7 us -> 22.3 us  [swap(): return lax.ppermute(x, 'ka', [(i, i ^ k) for i in range(n_ka)])]
  transfers between devices with their start and end apart: 33 -> 32, of which waited for: 16 -> 15; matrix products, arithmetic and copies ran while one was open for 1% -> 2% of each run, Pallas kernels for 17% -> 17%
where the time goes in v14:
time: 113 us
  waiting for transfers between devices  42.8 us (38%)
  starting transfers between devices  38.5 us (34%)
  Pallas kernels  23.2 us (21%)
  local copies, waits for them, and re-layouts  7.43 us (7%)
    ppermute x22, waiting for transfers between devices, swap(): return lax.ppermute(x, 'ka', [(i, i ^ k) for i in range(n_ka)])  22.3 us
    ppermute x22, starting transfers between devices, swap(): return lax.ppermute(x, 'ka', [(i, i ^ k) for i in range(n_ka)])  16.9 us
    ppermute x6, starting transfers between devices, exchange(): return lax.ppermute(x, 'pb', found) if found else None  12.3 us
    ppermute x2, waiting for transfers between devices, outward(): return lax.ppermute(x, 'pb', [(1, 0), (n_pb - 2, n_pb - 1)])  11.9 us
    pallas_call x4, Pallas kernels, attend(): pl.pallas_call(functools.partial(attend_kernel, c, n_src, entry, first, m...  11 us
    ppermute x2, starting transfers between devices, inward(): return lax.ppermute(x, 'pb', [(0, 1), (n_pb - 1, n_pb - 2)])  6.7 us
    pallas_call x2, Pallas kernels, pack(): pl.pallas_call(functools.partial(pack_kernel, n_ka, heads, c, len(masks))...  5.31 us
    ppermute x2, waiting for transfers between devices, inward(): return lax.ppermute(x, 'pb', [(0, 1), (n_pb - 1, n_pb - 2)])  4.45 us
  transfers between devices with their start and end apart: 32, of which 15 were waited for; matrix products, arithmetic and copies ran while one was open for 2% of the time, Pallas kernels for 17%

profile of v14, /device:TPU:0, one launch (start us, length us, event | category | flops | bytes accessed | tf_op | source)
XLA Modules:
  0.0 113.1 jit_solution(3479607189730222767)
XLA Ops:
  0.0 2.3 %pack_0.1 = (bf16[2,256,128]{2,1,0:T(8,128)(2,1)}, bf16[2,256,128]{2,1,0:T(8,128)(2,1)}, bf16[2,256,128]{2,1,0:T(8,128)(2,1)}, bf16[2,256,128]{2,1,0:T(8,128)(2,1)}) custom-call(s32[1]{0:T(128)} %bitcast.me_ref, bf16[128,2048]{1,0:T(8,128)(2,1)} %refs_2_.1, bf16[128,2048]{1,0:T(8,128)(2,1)} %refs_3_.1), custom_call_target="tpu_custom_call" | custom-call | bytes 262144 | tf_op jit(solution)/shard_map/pack_0/pallas_call | solution.py:77
  2.3 3.0 %collective-permute-start = (bf16[2,256,128]{2,1,0:T(8,128)(2,1)}, bf16[2,256,128]{2,1,0:T(8,128)(2,1)S(1)}, u32[]{:S(2)}, u32[]{:S(2)}) collective-permute-start(bf16[2,256,128]{2,1,0:T(8,128)(2,1)} %get-tuple-element.52), channel_id=1, source_target_pairs={{0,2},{1,3},{2,0},{3,1},{4,6},{5,7},{6,4},{7,5},{8,10},{9,11},{10,... | collective-permute-start | bytes 393224 | tf_op jit(solution)/shard_map/ppermute | solution.py:351
  6.8 3.9 %collective-permute-start.3 = (s32[4,8]{1,0:T(4,128)}, s32[4,8]{1,0:T(4,128)S(1)}, u32[]{:S(2)}, u32[]{:S(2)}) collective-permute-start(s32[4,8]{1,0:T(4,128)} %bitcast.12), channel_id=1, source_target_pairs={{0,8},{24,16},{1,9},{25,17},{2,10},{26,18},{3,11},{27,19},{4,12},{... | collective-permute-start | bytes 392 | tf_op jit(solution)/shard_map/ppermute | solution.py:371
  10.8 2.0 %turn.1.q_own = bf16[2,8,128,128]{3,2,1,0:T(8,128)(2,1)} custom-call(s32[1]{0:T(128)} %bitcast.me_ref, bf16[1024,2048]{1,0:T(8,128)(2,1)} %q_all.1), custom_call_target="tpu_custom_call" | custom-call | bytes 131072 | tf_op jit(solution)/shard_map/turn/pallas_call | solution.py:105
  15.8 4.4 %collective-permute-start.8 = (bf16[8,2,128,128]{3,2,1,0:T(8,128)(2,1)S(1)}, bf16[8,2,128,128]{3,2,1,0:T(8,128)(2,1)S(1)}, u32[]{:S(2)}, u32[]{:S(2)}) collective-permute-start(bf16[8,2,128,128]{3,2,1,0:T(8,128)(2,1)S(1)} %bitcast.10), channel_id=1, source_target_pairs={{0,8},{8,0},{16,24},{24,16},{1,9},{9,1},{17,25},{25,17},{2,10},{10... | collective-permute-start | bytes 1572872 | tf_op jit(solution)/shard_map/ppermute | solution.py:364
  20.2 3.0 %pack_1.1 = (bf16[2,288,128]{2,1,0:T(8,128)(2,1)}, bf16[2,288,128]{2,1,0:T(8,128)(2,1)}, bf16[2,288,128]{2,1,0:T(8,128)(2,1)}, bf16[2,288,128]{2,1,0:T(8,128)(2,1)}) custom-call(s32[1]{0:T(128)} %bitcast.me_ref, s32[4,8]{1,0:T(4,128)} %bitcast.13, s32[4,8]{1,0:T(4,128)} %copy-done.4, bf16[128,2048]{1,0:T(8,128)(2,1)} %refs_2_.1, bf16[128,2048]{1,0:T(8,128)(2,1)} %refs_3_.1), custom_call_target="tpu_custom_call" | custom-call | bytes 262144 | tf_op jit(solution)/shard_map/pack_1/pallas_call | solution.py:77
  26.8 3.1 %collective-permute-done.5 = bf16[2,288,128]{2,1,0:T(8,128)(2,1)S(1)} collective-permute-done((bf16[2,288,128]{2,1,0:T(8,128)(2,1)}, bf16[2,288,128]{2,1,0:T(8,128)(2,1)S(1)}, u32[]{:S(2)}, u32[]{:S(2)}) %collective-permute-start.5) | collective-permute-done | bytes 147488 | tf_op jit(solution)/shard_map/ppermute | solution.py:351
  29.9 3.1 %collective-permute-done.6 = bf16[2,288,128]{2,1,0:T(8,128)(2,1)S(1)} collective-permute-done((bf16[2,288,128]{2,1,0:T(8,128)(2,1)}, bf16[2,288,128]{2,1,0:T(8,128)(2,1)S(1)}, u32[]{:S(2)}, u32[]{:S(2)}) %collective-permute-start.6) | collective-permute-done | bytes 147488 | tf_op jit(solution)/shard_map/ppermute | solution.py:351
  36.7 2.8 %collective-permute-start.11 = (bf16[2,8,128,128]{3,2,1,0:T(8,128)(2,1)S(1)}, bf16[2,8,128,128]{3,2,1,0:T(8,128)(2,1)S(1)}, u32[]{:S(2)}, u32[]{:S(2)}) collective-permute-start(bf16[2,8,128,128]{3,2,1,0:T(8,128)(2,1)S(1)} %copy-done), channel_id=1, source_target_pairs={{0,8},{24,16},{1,9},{25,17},{2,10},{26,18},{3,11},{27,19},{4,12},{... | collective-permute-start | bytes 1572872 | tf_op jit(solution)/shard_map/ppermute | solution.py:371
  44.4 2.4 %plan.1 = (s32[2]{0:T(128)S(1)}, s32[432]{0:T(512)S(1)}, s32[176]{0:T(256)S(1)}) custom-call(s32[1]{0:T(128)} %bitcast.2.pb_ref, s32[256]{0:T(256)S(1)} %reshape.24.refs_0_, s32[256]{0:T(256)S(1)} %reshape.26.refs_1_), custom_call_target="tpu_custom_call" | custom-call | tf_op jit(solution)/shard_map/plan/pallas_call | solution.py:159
  46.8 4.4 %collective-permute-done.11.refs_0_ = bf16[2,8,128,128]{3,2,1,0:T(8,128)(2,1)S(1)} collective-permute-done((bf16[2,8,128,128]{3,2,1,0:T(8,128)(2,1)S(1)}, bf16[2,8,128,128]{3,2,1,0:T(8,128)(2,1)S(1)}, u32[]{:S(2)}, u32[]{:S(2)}) %collective-permute-start.11) | collective-permute-done | bytes 524320 | tf_op jit(solution)/shard_map/ppermute | solution.py:371
  51.2 4.3 %collective-permute-start.21 = (bf16[8,2,128,128]{3,2,1,0:T(8,128)(2,1)S(1)}, bf16[8,2,128,128]{3,2,1,0:T(8,128)(2,1)}, u32[]{:S(2)}, u32[]{:S(2)}) collective-permute-start(bf16[8,2,128,128]{3,2,1,0:T(8,128)(2,1)S(1)} %bitcast.7), channel_id=1, source_target_pairs={{0,8},{8,0},{16,24},{24,16},{1,9},{9,1},{17,25},{25,17},{2,10},{10... | collective-permute-start | bytes 1572872 | tf_op jit(solution)/shard_map/ppermute | solution.py:364
  55.5 3.4 %attend_0_0.1 = (f32[16,1,128]{2,1,0:T(1,128)S(1)}, f32[16,1,128]{2,1,0:T(1,128)S(1)}, f32[16,128,128]{2,1,0:T(8,128)S(1)}) custom-call(s32[2]{0:T(128)S(1)} %get-tuple-element.73.count_ref, s32[432]{0:T(512)S(1)} %get-tuple-element.77.live_ref, bf16[2,8,128,128]{3,2,1,0:T(8,128)(2,1)S(1)} %copy-done, ...), custom_call_target="tpu_custom_call" | custom-call | bytes 16384 | tf_op jit(solution)/shard_map/attend_0_0/pallas_call | solution.py:273
  59.0 2.4 %attend_0_1.1 = (f32[16,1,128]{2,1,0:T(1,128)S(1)}, f32[16,1,128]{2,1,0:T(1,128)S(1)}, f32[16,128,128]{2,1,0:T(8,128)S(1)}, bf16[8,144,128]{2,1,0:T(8,128)(2,1)}) custom-call(s32[2]{0:T(128)S(1)} %get-tuple-element.73.count_ref, s32[176]{0:T(256)S(1)} %get-tuple-element.74.live_ref, bf16[2,8,128,128]{3,2,1,0:T(8,128)(2,1)S(1)} %copy-done, ...), custom_call_target="tpu_custom_call" | custom-call | bytes 16384 | tf_op jit(solution)/shard_map/attend_0_1/pallas_call | solution.py:273
  63.5 4.1 %collective-permute-done.21.refs_2_ = bf16[8,2,128,128]{3,2,1,0:T(8,128)(2,1)} collective-permute-done((bf16[8,2,128,128]{3,2,1,0:T(8,128)(2,1)S(1)}, bf16[8,2,128,128]{3,2,1,0:T(8,128)(2,1)}, u32[]{:S(2)}, u32[]{:S(2)}) %collective-permute-start.21) | collective-permute-done | bytes 524320 | tf_op jit(solution)/shard_map/ppermute | solution.py:364
  68.4 4.9 %collective-permute-done.13.part_ref = bf16[8,144,128]{2,1,0:T(8,128)(2,1)S(1)} collective-permute-done((bf16[8,144,128]{2,1,0:T(8,128)(2,1)}, bf16[8,144,128]{2,1,0:T(8,128)(2,1)S(1)}, u32[]{:S(2)}, u32[]{:S(2)}) %collective-permute-start.13) | collective-permute-done | bytes 294944 | tf_op jit(solution)/shard_map/ppermute | solution.py:374
  78.0 4.2 %attend_1_0.1 = (f32[16,1,128]{2,1,0:T(1,128)S(1)}, f32[16,1,128]{2,1,0:T(1,128)S(1)}, f32[16,128,128]{2,1,0:T(8,128)S(1)}) custom-call(s32[2]{0:T(128)S(1)} %get-tuple-element.73.count_ref, s32[432]{0:T(512)S(1)} %get-tuple-element.77.live_ref, bf16[2,8,128,128]{3,2,1,0:T(8,128)(2,1)S(1)} %copy-done, ...), custom_call_target="tpu_custom_call" | custom-call | bytes 16384 | tf_op jit(solution)/shard_map/attend_1_0/pallas_call | solution.py:273
  82.3 2.0 %collective-permute-done.15.refs_2_ = bf16[1024,128]{1,0:T(8,128)(2,1)S(1)} collective-permute-done((bf16[1024,128]{1,0:T(8,128)(2,1)S(1)}, bf16[1024,128]{1,0:T(8,128)(2,1)S(1)}, u32[]{:S(2)}, u32[]{:S(2)}) %collective-permute-start.15) | collective-permute-done | bytes 262176 | tf_op jit(solution)/shard_map/ppermute | solution.py:351
  85.1 2.8 %collective-permute-done.19.refs_6_ = bf16[1024,128]{1,0:T(8,128)(2,1)S(1)} collective-permute-done((bf16[1024,128]{1,0:T(8,128)(2,1)S(1)}, bf16[1024,128]{1,0:T(8,128)(2,1)S(1)}, u32[]{:S(2)}, u32[]{:S(2)}) %collective-permute-start.19) | collective-permute-done | bytes 262176 | tf_op jit(solution)/shard_map/ppermute | solution.py:351
  89.8 7.0 %collective-permute-done.24.part_ref = bf16[8,144,128]{2,1,0:T(8,128)(2,1)S(1)} collective-permute-done((bf16[8,144,128]{2,1,0:T(8,128)(2,1)S(1)}, bf16[8,144,128]{2,1,0:T(8,128)(2,1)S(1)}, u32[]{:S(2)}, u32[]{:S(2)}) %collective-permute-start.24) | collective-permute-done | bytes 294944 | tf_op jit(solution)/shard_map/ppermute | solution.py:374
  97.0 2.2 %collective-permute-start.30 = (bf16[1024,128]{1,0:T(8,128)(2,1)S(1)}, bf16[1024,128]{1,0:T(8,128)(2,1)S(1)}, u32[]{:S(2)}, u32[]{:S(2)}) collective-permute-start(bf16[1024,128]{1,0:T(8,128)(2,1)S(1)} %merge_1.1.refs_8_), channel_id=1, source_target_pairs={{0,6},{1,7},{2,4},{3,5},{4,2},{5,3},{6,0},{7,1},{8,14},{9,15},{10,... | collective-permute-start | bytes 786440 | tf_op jit(solution)/shard_map/ppermute | solution.py:351
  101.1 5.3 %collective-permute-done.30.refs_14_ = bf16[1024,128]{1,0:T(8,128)(2,1)S(1)} collective-permute-done((bf16[1024,128]{1,0:T(8,128)(2,1)S(1)}, bf16[1024,128]{1,0:T(8,128)(2,1)S(1)}, u32[]{:S(2)}, u32[]{:S(2)}) %collective-permute-start.30) | collective-permute-done | bytes 262176 | tf_op jit(solution)/shard_map/ppermute | solution.py:351
  106.4 2.7 %collective-permute-done.28.refs_12_ = bf16[1024,128]{1,0:T(8,128)(2,1)S(1)} collective-permute-done((bf16[1024,128]{1,0:T(8,128)(2,1)S(1)}, bf16[1024,128]{1,0:T(8,128)(2,1)S(1)}, u32[]{:S(2)}, u32[]{:S(2)}) %collective-permute-start.28) | collective-permute-done | bytes 262176 | tf_op jit(solution)/shard_map/ppermute | solution.py:351
  111.0 2.1 %place.1 = bf16[1024,2048]{1,0:T(8,128)(2,1)} custom-call(s32[1]{0:T(128)} %bitcast.me_ref, bf16[1024,128]{1,0:T(8,128)(2,1)S(1)} %merge_0.1.refs_0_, bf16[1024,128]{1,0:T(8,128)(2,1)S(1)} %collective-permute-done.14.refs_1_, bf16[1024,128]{1,0:T(8,128)(2,1)S(1)} %collective-permute-done.15.refs_2_, bf16[1024,128]{1,0:T(8,128)(2,1)S(1)} %collective-permute-done.16.refs_3_, ...), custom_call_target="tpu_custom_call" | custom-call | tf_op jit(solution)/shard_map/place/pallas_call | solution.py:330
  (77 shorter events, 30.8 us)
Async XLA Ops:
  2.3 10.6 %collective-permute-start = (bf16[2,256,128]{2,1,0:T(8,128)(2,1)}, bf16[2,256,128]{2,1,0:T(8,128)(2,1)S(1)}, u32[]{:S(2)}, u32[]{:S(2)}) collective-permute-start(bf16[2,256,128]{2,1,0:T(8,128)(2,1)} %get-tuple-element.52), channel_id=1, source_target_pairs={{0,2},{1,3},{2,0},{3,1},{4,6},{5,7},{6,4},{7,5},{8,10},{9,11},{10,... | collective-permute-start | bytes 393224 | tf_op jit(solution)/shard_map/ppermute | solution.py:351
  5.3 8.0 %collective-permute-start.1 = (bf16[2,256,128]{2,1,0:T(8,128)(2,1)}, bf16[2,256,128]{2,1,0:T(8,128)(2,1)S(1)}, u32[]{:S(2)}, u32[]{:S(2)}) collective-permute-start(bf16[2,256,128]{2,1,0:T(8,128)(2,1)} %get-tuple-element.53), channel_id=1, source_target_pairs={{0,4},{1,5},{2,6},{3,7},{4,0},{5,1},{6,2},{7,3},{8,12},{9,13},{10,... | collective-permute-start | bytes 393224 | tf_op jit(solution)/shard_map/ppermute | solution.py:351
  15.1 18.0 %collective-permute-start.9 = (bf16[8,2,128,128]{3,2,1,0:T(8,128)(2,1)S(1)}, bf16[8,2,128,128]{3,2,1,0:T(8,128)(2,1)S(1)}, u32[]{:S(2)}, u32[]{:S(2)}) collective-permute-start(bf16[8,2,128,128]{3,2,1,0:T(8,128)(2,1)S(1)} %bitcast.9), channel_id=1, source_target_pairs={{8,16},{16,8},{9,17},{17,9},{10,18},{18,10},{11,19},{19,11},{12,20... | collective-permute-start | bytes 1572872 | tf_op jit(solution)/shard_map/ppermute | solution.py:364
  15.8 17.3 %collective-permute-start.8 = (bf16[8,2,128,128]{3,2,1,0:T(8,128)(2,1)S(1)}, bf16[8,2,128,128]{3,2,1,0:T(8,128)(2,1)S(1)}, u32[]{:S(2)}, u32[]{:S(2)}) collective-permute-start(bf16[8,2,128,128]{3,2,1,0:T(8,128)(2,1)S(1)} %bitcast.10), channel_id=1, source_target_pairs={{0,8},{8,0},{16,24},{24,16},{1,9},{9,1},{17,25},{25,17},{2,10},{10... | collective-permute-start | bytes 1572872 | tf_op jit(solution)/shard_map/ppermute | solution.py:364
  24.5 8.5 %collective-permute-start.6 = (bf16[2,288,128]{2,1,0:T(8,128)(2,1)}, bf16[2,288,128]{2,1,0:T(8,128)(2,1)S(1)}, u32[]{:S(2)}, u32[]{:S(2)}) collective-permute-start(bf16[2,288,128]{2,1,0:T(8,128)(2,1)} %get-tuple-element.67), channel_id=1, source_target_pairs={{0,4},{1,5},{2,6},{3,7},{4,0},{5,1},{6,2},{7,3},{8,12},{9,13},{10,... | collective-permute-start | bytes 442376 | tf_op jit(solution)/shard_map/ppermute | solution.py:351
  26.0 7.0 %collective-permute-start.7 = (bf16[2,288,128]{2,1,0:T(8,128)(2,1)}, bf16[2,288,128]{2,1,0:T(8,128)(2,1)S(1)}, u32[]{:S(2)}, u32[]{:S(2)}) collective-permute-start(bf16[2,288,128]{2,1,0:T(8,128)(2,1)} %get-tuple-element.68), channel_id=1, source_target_pairs={{0,6},{1,7},{2,4},{3,5},{4,2},{5,3},{6,0},{7,1},{8,14},{9,15},{10,... | collective-permute-start | bytes 442376 | tf_op jit(solution)/shard_map/ppermute | solution.py:351
  36.7 14.6 %collective-permute-start.11 = (bf16[2,8,128,128]{3,2,1,0:T(8,128)(2,1)S(1)}, bf16[2,8,128,128]{3,2,1,0:T(8,128)(2,1)S(1)}, u32[]{:S(2)}, u32[]{:S(2)}) collective-permute-start(bf16[2,8,128,128]{3,2,1,0:T(8,128)(2,1)S(1)} %copy-done), channel_id=1, source_target_pairs={{0,8},{24,16},{1,9},{25,17},{2,10},{26,18},{3,11},{27,19},{4,12},{... | collective-permute-start | bytes 1572872 | tf_op jit(solution)/shard_map/ppermute | solution.py:371
  39.5 11.8 %collective-permute-start.12 = (bf16[8,2,128,128]{3,2,1,0:T(8,128)(2,1)S(1)}, bf16[8,2,128,128]{3,2,1,0:T(8,128)(2,1)}, u32[]{:S(2)}, u32[]{:S(2)}) collective-permute-start(bf16[8,2,128,128]{3,2,1,0:T(8,128)(2,1)S(1)} %collective-permute-done.8.refs_2_), channel_id=1, source_target_pairs={{8,16},{16,8},{9,17},{17,9},{10,18},{18,10},{11,19},{19,11},{12,20... | collective-permute-start | bytes 1572872 | tf_op jit(solution)/shard_map/ppermute | solution.py:364
  43.7 19.0 %collective-permute-start.22 = (bf16[8,2,128,128]{3,2,1,0:T(8,128)(2,1)S(1)}, bf16[8,2,128,128]{3,2,1,0:T(8,128)(2,1)S(1)}, u32[]{:S(2)}, u32[]{:S(2)}) collective-permute-start(bf16[8,2,128,128]{3,2,1,0:T(8,128)(2,1)S(1)} %bitcast.6), channel_id=1, source_target_pairs={{8,16},{16,8},{9,17},{17,9},{10,18},{18,10},{11,19},{19,11},{12,20... | collective-permute-start | bytes 1572872 | tf_op jit(solution)/shard_map/ppermute | solution.py:364
  51.2 16.4 %collective-permute-start.21 = (bf16[8,2,128,128]{3,2,1,0:T(8,128)(2,1)S(1)}, bf16[8,2,128,128]{3,2,1,0:T(8,128)(2,1)}, u32[]{:S(2)}, u32[]{:S(2)}) collective-permute-start(bf16[8,2,128,128]{3,2,1,0:T(8,128)(2,1)S(1)} %bitcast.7), channel_id=1, source_target_pairs={{0,8},{8,0},{16,24},{24,16},{1,9},{9,1},{17,25},{25,17},{2,10},{10... | collective-permute-start | bytes 1572872 | tf_op jit(solution)/shard_map/ppermute | solution.py:364
  61.4 11.8 %collective-permute-start.13 = (bf16[8,144,128]{2,1,0:T(8,128)(2,1)}, bf16[8,144,128]{2,1,0:T(8,128)(2,1)S(1)}, u32[]{:S(2)}, u32[]{:S(2)}) collective-permute-start(bf16[8,144,128]{2,1,0:T(8,128)(2,1)} %get-tuple-element.84), channel_id=1, source_target_pairs={{8,0},{16,24},{9,1},{17,25},{10,2},{18,26},{11,3},{19,27},{12,4},{... | collective-permute-start | bytes 884744 | tf_op jit(solution)/shard_map/ppermute | solution.py:374
  67.7 16.6 %collective-permute-start.23 = (bf16[8,2,128,128]{3,2,1,0:T(8,128)(2,1)}, bf16[8,2,128,128]{3,2,1,0:T(8,128)(2,1)S(1)}, u32[]{:S(2)}, u32[]{:S(2)}) collective-permute-start(bf16[8,2,128,128]{3,2,1,0:T(8,128)(2,1)} %collective-permute-done.21.refs_2_), channel_id=1, source_target_pairs={{8,16},{16,8},{9,17},{17,9},{10,18},{18,10},{11,19},{19,11},{12,20... | collective-permute-start | bytes 1572872 | tf_op jit(solution)/shard_map/ppermute | solution.py:364
  73.4 8.9 %collective-permute-start.17 = (bf16[1024,128]{1,0:T(8,128)(2,1)S(1)}, bf16[1024,128]{1,0:T(8,128)(2,1)S(1)}, u32[]{:S(2)}, u32[]{:S(2)}) collective-permute-start(bf16[1024,128]{1,0:T(8,128)(2,1)S(1)} %merge_0.1.refs_0_), channel_id=1, source_target_pairs={{0,4},{1,5},{2,6},{3,7},{4,0},{5,1},{6,2},{7,3},{8,12},{9,13},{10,... | collective-permute-start | bytes 786440 | tf_op jit(solution)/shard_map/ppermute | solution.py:351
  75.0 9.2 %collective-permute-start.15 = (bf16[1024,128]{1,0:T(8,128)(2,1)S(1)}, bf16[1024,128]{1,0:T(8,128)(2,1)S(1)}, u32[]{:S(2)}, u32[]{:S(2)}) collective-permute-start(bf16[1024,128]{1,0:T(8,128)(2,1)S(1)} %merge_0.1.refs_0_), channel_id=1, source_target_pairs={{0,2},{1,3},{2,0},{3,1},{4,6},{5,7},{6,4},{7,5},{8,10},{9,11},{10,... | collective-permute-start | bytes 786440 | tf_op jit(solution)/shard_map/ppermute | solution.py:351
  76.2 11.6 %collective-permute-start.19 = (bf16[1024,128]{1,0:T(8,128)(2,1)S(1)}, bf16[1024,128]{1,0:T(8,128)(2,1)S(1)}, u32[]{:S(2)}, u32[]{:S(2)}) collective-permute-start(bf16[1024,128]{1,0:T(8,128)(2,1)S(1)} %merge_0.1.refs_0_), channel_id=1, source_target_pairs={{0,6},{1,7},{2,4},{3,5},{4,2},{5,3},{6,0},{7,1},{8,14},{9,15},{10,... | collective-permute-start | bytes 786440 | tf_op jit(solution)/shard_map/ppermute | solution.py:351
  87.9 9.0 %collective-permute-start.24 = (bf16[8,144,128]{2,1,0:T(8,128)(2,1)S(1)}, bf16[8,144,128]{2,1,0:T(8,128)(2,1)S(1)}, u32[]{:S(2)}, u32[]{:S(2)}) collective-permute-start(bf16[8,144,128]{2,1,0:T(8,128)(2,1)S(1)} %get-tuple-element.96), channel_id=1, source_target_pairs={{8,0},{16,24},{9,1},{17,25},{10,2},{18,26},{11,3},{19,27},{12,4},{... | collective-permute-start | bytes 884744 | tf_op jit(solution)/shard_map/ppermute | solution.py:374
  89.1 10.6 %collective-permute-start.14 = (bf16[1024,128]{1,0:T(8,128)(2,1)S(1)}, bf16[1024,128]{1,0:T(8,128)(2,1)S(1)}, u32[]{:S(2)}, u32[]{:S(2)}) collective-permute-start(bf16[1024,128]{1,0:T(8,128)(2,1)S(1)} %merge_0.1.refs_0_), channel_id=1, source_target_pairs={{0,1},{1,0},{2,3},{3,2},{4,5},{5,4},{6,7},{7,6},{8,9},{9,8},{10,11... | collective-permute-start | bytes 786440 | tf_op jit(solution)/shard_map/ppermute | solution.py:351
  89.2 11.3 %collective-permute-start.20 = (bf16[1024,128]{1,0:T(8,128)(2,1)S(1)}, bf16[1024,128]{1,0:T(8,128)(2,1)S(1)}, u32[]{:S(2)}, u32[]{:S(2)}) collective-permute-start(bf16[1024,128]{1,0:T(8,128)(2,1)S(1)} %collective-permute-done.19.refs_6_), channel_id=1, source_target_pairs={{0,1},{1,0},{2,3},{3,2},{4,5},{5,4},{6,7},{7,6},{8,9},{9,8},{10,11... | collective-permute-start | bytes 786440 | tf_op jit(solution)/shard_map/ppermute | solution.py:351
  89.7 10.9 %collective-permute-start.18 = (bf16[1024,128]{1,0:T(8,128)(2,1)S(1)}, bf16[1024,128]{1,0:T(8,128)(2,1)S(1)}, u32[]{:S(2)}, u32[]{:S(2)}) collective-permute-start(bf16[1024,128]{1,0:T(8,128)(2,1)S(1)} %collective-permute-done.17.refs_4_), channel_id=1, source_target_pairs={{0,1},{1,0},{2,3},{3,2},{4,5},{5,4},{6,7},{7,6},{8,9},{9,8},{10,11... | collective-permute-start | bytes 786440 | tf_op jit(solution)/shard_map/ppermute | solution.py:351
  97.0 9.4 %collective-permute-start.30 = (bf16[1024,128]{1,0:T(8,128)(2,1)S(1)}, bf16[1024,128]{1,0:T(8,128)(2,1)S(1)}, u32[]{:S(2)}, u32[]{:S(2)}) collective-permute-start(bf16[1024,128]{1,0:T(8,128)(2,1)S(1)} %merge_1.1.refs_8_), channel_id=1, source_target_pairs={{0,6},{1,7},{2,4},{3,5},{4,2},{5,3},{6,0},{7,1},{8,14},{9,15},{10,... | collective-permute-start | bytes 786440 | tf_op jit(solution)/shard_map/ppermute | solution.py:351
  99.3 9.8 %collective-permute-start.28 = (bf16[1024,128]{1,0:T(8,128)(2,1)S(1)}, bf16[1024,128]{1,0:T(8,128)(2,1)S(1)}, u32[]{:S(2)}, u32[]{:S(2)}) collective-permute-start(bf16[1024,128]{1,0:T(8,128)(2,1)S(1)} %merge_1.1.refs_8_), channel_id=1, source_target_pairs={{0,4},{1,5},{2,6},{3,7},{4,0},{5,1},{6,2},{7,3},{8,12},{9,13},{10,... | collective-permute-start | bytes 786440 | tf_op jit(solution)/shard_map/ppermute | solution.py:351
  99.8 9.4 %collective-permute-start.26 = (bf16[1024,128]{1,0:T(8,128)(2,1)S(1)}, bf16[1024,128]{1,0:T(8,128)(2,1)S(1)}, u32[]{:S(2)}, u32[]{:S(2)}) collective-permute-start(bf16[1024,128]{1,0:T(8,128)(2,1)S(1)} %merge_1.1.refs_8_), channel_id=1, source_target_pairs={{0,2},{1,3},{2,0},{3,1},{4,6},{5,7},{6,4},{7,5},{8,10},{9,11},{10,... | collective-permute-start | bytes 786440 | tf_op jit(solution)/shard_map/ppermute | solution.py:351
  100.6 9.0 %collective-permute-start.16 = (bf16[1024,128]{1,0:T(8,128)(2,1)S(1)}, bf16[1024,128]{1,0:T(8,128)(2,1)S(1)}, u32[]{:S(2)}, u32[]{:S(2)}) collective-permute-start(bf16[1024,128]{1,0:T(8,128)(2,1)S(1)} %collective-permute-done.15.refs_2_), channel_id=1, source_target_pairs={{0,1},{1,0},{2,3},{3,2},{4,5},{5,4},{6,7},{7,6},{8,9},{9,8},{10,11... | collective-permute-start | bytes 786440 | tf_op jit(solution)/shard_map/ppermute | solution.py:351
  100.6 9.0 %collective-permute-start.25 = (bf16[1024,128]{1,0:T(8,128)(2,1)S(1)}, bf16[1024,128]{1,0:T(8,128)(2,1)S(1)}, u32[]{:S(2)}, u32[]{:S(2)}) collective-permute-start(bf16[1024,128]{1,0:T(8,128)(2,1)S(1)} %merge_1.1.refs_8_), channel_id=1, source_target_pairs={{0,1},{1,0},{2,3},{3,2},{4,5},{5,4},{6,7},{7,6},{8,9},{9,8},{10,11... | collective-permute-start | bytes 786440 | tf_op jit(solution)/shard_map/ppermute | solution.py:351
  (13 other events, 75.7 us)

commit v15 on v10

--- a/solution.py
+++ b/solution.py
@@ -28,65 +28,44 @@
     return pltpu.CompilerParams(vmem_limit_bytes=size)
 
 
-def mask_rows(rows):
-    return -(-rows // 16) * 16
-
-
-def pack_kernel(n_ka, heads, c, n_masks, me_ref, *refs):
-    mask_refs, refs = refs[:n_masks], refs[n_masks:]
+def pack_kernel(n_ka, heads, me_ref, *refs):
     k_all, v_all, *out_refs, v_ref, sems = refs
     key_blocks = k_all.shape[0] // BLOCK
+    pieces = [(k, c, t) for k in range(n_ka) for c in range(heads) for t in range(key_blocks)]
     copies = []
-    for k in range(n_ka):
-        out_ref = out_refs[k // 2]
+    for i, (k, c, t) in enumerate(pieces):
         col = pl.multiple_of(((me_ref[0] ^ k) * heads + c) * HEAD_DIM, HEAD_DIM)
-        for t in range(key_blocks):
-            rows, at = pl.ds(t * BLOCK, BLOCK), pl.ds(2 * t * BLOCK, BLOCK)
-            sem = sems.at[k * key_blocks + t]
-            copies.append(
-                (
-                    pltpu.make_async_copy(k_all.at[rows, pl.ds(col, HEAD_DIM)], out_ref.at[k % 2, at], sem.at[0]),
-                    pltpu.make_async_copy(v_all.at[rows, pl.ds(col, HEAD_DIM)], v_ref.at[k, t], sem.at[1]),
-                )
+        rows, at = pl.ds(t * BLOCK, BLOCK), pl.ds(2 * t * BLOCK, BLOCK)
+        to = out_refs[k // 2].at[c, k % 2, at]
+        copies.append(
+            (
+                pltpu.make_async_copy(k_all.at[rows, pl.ds(col, HEAD_DIM)], to, sems.at[i, 0]),
+                pltpu.make_async_copy(v_all.at[rows, pl.ds(col, HEAD_DIM)], v_ref.at[i], sems.at[i, 1]),
             )
+        )
     for pair in copies:
         for copy in pair:
             copy.start()
-    for i, mask_ref in enumerate(mask_refs):
-        size = mask_rows(mask_ref.shape[0])
-        row, column = (lax.broadcasted_iota(jnp.int32, (size, HEAD_DIM), axis) for axis in (0, 1))
-        mask = jnp.zeros((size, HEAD_DIM), jnp.int32)
-        for a in range(mask_ref.shape[0]):
-            for b in range(mask_ref.shape[1]):
-                mask = jnp.where((row == a) & (column == b), mask_ref[a, b], mask)
-        mask = mask.astype(jnp.float32).astype(k_all.dtype)
-        at = 2 * key_blocks * BLOCK + i * size
-        for k in range(n_ka):
-            out_refs[k // 2][k % 2, at : at + size] = mask
-    for k in range(n_ka):
-        for t in range(key_blocks):
-            copies[k * key_blocks + t][1].wait()
-            out_refs[k // 2][k % 2, (2 * t + 1) * BLOCK : (2 * t + 2) * BLOCK] = v_ref[k, t].T
+    for i, (k, c, t) in enumerate(pieces):
+        copies[i][1].wait()
+        out_refs[k // 2][c, k % 2, (2 * t + 1) * BLOCK : (2 * t + 2) * BLOCK] = v_ref[i].T
     for pair in copies:
         pair[0].wait()
 
 
-def pack(me, keys, values, masks, n_ka, heads, c):
-    key_blocks = keys.shape[0] // BLOCK
-    size = 2 * keys.shape[0] + sum(mask_rows(mask.shape[0]) for mask in masks)
+def pack(me, keys, values, n_ka, heads):
+    count = n_ka * heads * (keys.shape[0] // BLOCK)
+    shape = (heads, 2, 2 * keys.shape[0], HEAD_DIM)
     return pl.pallas_call(
-        functools.partial(pack_kernel, n_ka, heads, c, len(masks)),
-        out_shape=[jax.ShapeDtypeStruct((2, size, HEAD_DIM), keys.dtype)] * (n_ka // 2),
-        in_specs=[SMEM] + [SMEM] * len(masks) + [ANY, ANY],
+        functools.partial(pack_kernel, n_ka, heads),
+        out_shape=[jax.ShapeDtypeStruct(shape, keys.dtype)] * (n_ka // 2),
+        in_specs=[SMEM, ANY, ANY],
         out_specs=[VMEM] * (n_ka // 2),
-        scratch_shapes=[
-            pltpu.VMEM((n_ka, key_blocks, BLOCK, HEAD_DIM), values.dtype),
-            pltpu.SemaphoreType.DMA((n_ka * key_blocks, 2)),
-        ],
+        scratch_shapes=[pltpu.VMEM((count, BLOCK, HEAD_DIM), values.dtype), pltpu.SemaphoreType.DMA((count, 2))],
         compiler_params=params(MOST_VMEM_BYTES),
         cost_estimate=pl.CostEstimate(flops=0, bytes_accessed=keys.size, transcendentals=0),
-        name=f"pack_{c}",
-    )(me, *masks, keys, values)
+        name="pack",
+    )(me, keys, values)
 
 
 def turn_kernel(heads, me_ref, q_all, *refs):
@@ -369,37 +348,28 @@
     def outward(x):
         return lax.ppermute(x, "pb", [(1, 0), (n_pb - 2, n_pb - 1)])
 
-    def sort(x, before=None):
-        mixed = [y if i == 0 else swap(y, 2 * i) for i, y in enumerate(x)]
-        mixed = after(mixed, before)
-        theirs = swap(jnp.stack([y[1] for y in mixed]), 1)
-        return jnp.concatenate([jnp.stack([y[0] for y in mixed]), theirs])
-
-    def blocks(x):
-        return x[:, : 2 * shard].reshape(n_ka * key_blocks, 2, BLOCK, HEAD_DIM)
+    def sort(x, before):
+        mixed = after([y if i == 0 else swap(y, 2 * i) for i, y in enumerate(x)], before)
+        theirs = swap(jnp.stack([y[:, 1] for y in mixed], axis=1), 1)
+        found = [jnp.concatenate([jnp.stack([y[c, 0] for y in mixed]), theirs[c]]) for c in range(heads)]
+        return [y.reshape(n_ka * key_blocks, 2, BLOCK, HEAD_DIM) for y in found]
 
     def after(arrays, done):
         return arrays if done is None else lax.optimization_barrier((arrays, done))[0]
 
-    def flags(x):
-        return x[:, : block_mask.shape[1], :rows].astype(jnp.int32).reshape(-1)
-
-    parts = (block_mask.T,) + ((inward(block_mask.T),) if relay else ())
-    owns, over, guest = [], [], [None] * heads
-    for c in range(heads):
-        place_of = after(me1, (q, owns[0])) if c else me1
-        packed = pack(place_of, keys, values, parts if c == heads - 1 else (), n_ka, heads, c)
-        if c == 0:
-            q = turn(after(me1, packed), queries, heads)
-            own = sort(packed, (q, parts))
-        else:
-            own = sort(packed, over[0])
-        owns.append(blocks(own))
-        over.append([exchange(after(owns[c], (over[0][1], guest[0]) if c else None), odd, 1) for odd in (0, 1)])
-        if relay:
-            guest[c] = inward(after(q[c], over[c]))
-    size = mask_rows(block_mask.shape[1])
-    masks = [flags(own[:, 2 * shard + i * size :]) for i in range(len(parts))]
+    packed = pack(me1, keys, values, n_ka, heads)
+    q = turn(after(me1, packed), queries, heads)
+    owns = sort(packed, q)
+    over = [[exchange(own, odd, 1) for odd in (0, 1)] for own in owns]
+
+    marks = jnp.stack([block_mask.T] + ([inward(block_mask.T)] if relay else []))[None]
+    bit = 1
+    while bit < n_ka:
+        marks = jnp.concatenate([marks, swap(marks, bit)])
+        bit *= 2
+    marks = marks.reshape((n_ka // 2, 2) + marks.shape[1:]).swapaxes(0, 1).reshape(marks.shape)
+    masks = [marks[:, i].reshape(-1) for i in range(marks.shape[1])]
+    guest = [inward(after(x, over[0])) if relay else None for x in q]
 
     steps = [((0, False),)]
     for step in range(1, n_pb):
@@ -421,9 +391,7 @@
     for step in range(last):
         for c in range(heads):
             sources = ([owns[c]] if step == 0 else []) + over[c]
-            even, odd = over[c]
-            if even is not None and odd is not None:
-                even, odd = lax.optimization_barrier((even, odd))
+            even, odd = after(tuple(over[c]), over[c]) if step else after(tuple(over[c]), lists[0][0])
             over[c] = [exchange(odd, 0, step + 2), exchange(even, 1, step + 2)]
             state[c] = run(c, step, sources)
 

time: 108 us -> 121 us (1.12)
  waiting for transfers between devices: 35.2 us -> 52.3 us
  Pallas kernels: 23.3 us -> 21.1 us
    ppermute x6, waiting for transfers between devices: 1.09 us -> 9.38 us  [exchange(): return lax.ppermute(x, 'pb', found) if found else None]
    ppermute x3, waiting for transfers between devices: 5.52 us -> 13.4 us  [inward(): return lax.ppermute(x, 'pb', [(0, 1), (n_pb - 1, n_pb - 2)])]
    pallas_call x2 -> x1, Pallas kernels: 5.38 us -> 3.2 us  [pack(): pl.pallas_call(functools.partial(pack_kernel, n_ka, heads), out_shape=[ja...]
    ppermute x22 -> x21, starting transfers between devices: 16.9 us -> 15.3 us  [swap(): return lax.ppermute(x, 'ka', [(i, i ^ k) for i in range(n_ka)])]
    ppermute x22 -> x21, waiting for transfers between devices: 21.4 us -> 22.3 us  [swap(): return lax.ppermute(x, 'ka', [(i, i ^ k) for i in range(n_ka)])]
  transfers between devices with their start and end apart: 33 -> 32, of which waited for: 16 -> 15; matrix products, arithmetic and copies ran while one was open for 1% -> 0% of each run, Pallas kernels for 18% -> 16%
where the time goes in v15:
time: 121 us
  waiting for transfers between devices  52.3 us (43%)
  starting transfers between devices  45.8 us (38%)
  Pallas kernels  21.1 us (17%)
    ppermute x21, waiting for transfers between devices, swap(): return lax.ppermute(x, 'ka', [(i, i ^ k) for i in range(n_ka)])  22.3 us
    ppermute x21, starting transfers between devices, swap(): return lax.ppermute(x, 'ka', [(i, i ^ k) for i in range(n_ka)])  15.3 us
    ppermute x3, starting transfers between devices, inward(): return lax.ppermute(x, 'pb', [(0, 1), (n_pb - 1, n_pb - 2)])  14.8 us
    ppermute x3, waiting for transfers between devices, inward(): return lax.ppermute(x, 'pb', [(0, 1), (n_pb - 1, n_pb - 2)])  13.4 us
    ppermute x6, starting transfers between devices, exchange(): return lax.ppermute(x, 'pb', found) if found else None  13.1 us
    pallas_call x4, Pallas kernels, attend(): pl.pallas_call(functools.partial(attend_kernel, n_src, entry, first, mode...  11 us
    ppermute x6, waiting for transfers between devices, exchange(): return lax.ppermute(x, 'pb', found) if found else None  9.38 us
    ppermute x2, waiting for transfers between devices, outward(): return lax.ppermute(x, 'pb', [(1, 0), (n_pb - 2, n_pb - 1)])  7.12 us
  transfers between devices with their start and end apart: 32, of which 15 were waited for; matrix products, arithmetic and copies ran while one was open for 0% of the time, Pallas kernels for 16%

profile of v15, /device:TPU:0, one launch (start us, length us, event | category | flops | bytes accessed | tf_op | source)
XLA Modules:
  0.0 120.9 jit_solution(5551111388846982846)
XLA Ops:
  0.0 4.9 %collective-permute-start = (s32[4,8]{1,0:T(4,128)}, s32[4,8]{1,0:T(4,128)S(1)}, u32[]{:S(2)}, u32[]{:S(2)}) collective-permute-start(s32[4,8]{1,0:T(4,128)} %bitcast.39), channel_id=1, source_target_pairs={{0,8},{24,16},{1,9},{25,17},{2,10},{26,18},{3,11},{27,19},{4,12},{... | collective-permute-start | bytes 392 | tf_op jit(solution)/shard_map/ppermute | solution.py:346
  4.9 3.2 %pack.1 = (bf16[2,2,256,128]{3,2,1,0:T(8,128)(2,1)}, bf16[2,2,256,128]{3,2,1,0:T(8,128)(2,1)}, bf16[2,2,256,128]{3,2,1,0:T(8,128)(2,1)}, bf16[2,2,256,128]{3,2,1,0:T(8,128)(2,1)}) custom-call(s32[1]{0:T(128)} %bitcast.me_ref, bf16[128,2048]{1,0:T(8,128)(2,1)} %refs_0_.1, bf16[128,2048]{1,0:T(8,128)(2,1)} %refs_1_.1), custom_call_target="tpu_custom_call" | custom-call | bytes 262144 | tf_op jit(solution)/shard_map/pack/pallas_call | solution.py:59
  12.4 1.6 %collective-permute-start.2 = (s32[2,2,4,8]{3,2,1,0:T(4,128)S(1)}, s32[2,2,4,8]{3,2,1,0:T(4,128)S(1)}, u32[]{:S(2)}, u32[]{:S(2)}) collective-permute-start(s32[2,2,4,8]{3,2,1,0:T(4,128)S(1)} %pad_add_fusion.2), channel_id=1, source_target_pairs={{0,2},{1,3},{2,0},{3,1},{4,6},{5,7},{6,4},{7,5},{8,10},{9,11},{10,... | collective-permute-start | bytes 1544 | tf_op jit(solution)/shard_map/ppermute | solution.py:330
  13.9 9.7 %collective-permute-done.2 = s32[2,2,4,8]{3,2,1,0:T(4,128)S(1)} collective-permute-done((s32[2,2,4,8]{3,2,1,0:T(4,128)S(1)}, s32[2,2,4,8]{3,2,1,0:T(4,128)S(1)}, u32[]{:S(2)}, u32[]{:S(2)}) %collective-permute-start.2) | collective-permute-done | bytes 544 | tf_op jit(solution)/shard_map/ppermute | solution.py:330
  25.2 2.0 %turn.1 = (bf16[8,128,128]{2,1,0:T(8,128)(2,1)}, bf16[8,128,128]{2,1,0:T(8,128)(2,1)}) custom-call(s32[1]{0:T(128)} %bitcast.me_ref, bf16[1024,2048]{1,0:T(8,128)(2,1)} %q_all.1), custom_call_target="tpu_custom_call" | custom-call | bytes 131072 | tf_op jit(solution)/shard_map/turn/pallas_call | solution.py:84
  27.9 1.8 %collective-permute-done.7 = bf16[2,4,256,128]{3,2,1,0:T(8,128)(2,1)S(1)} collective-permute-done((bf16[2,4,256,128]{3,2,1,0:T(8,128)(2,1)S(1)}, bf16[2,4,256,128]{3,2,1,0:T(8,128)(2,1)S(1)}, u32[]{:S(2)}, u32[]{:S(2)}) %collective-permute-start.7) | collective-permute-done | bytes 524320 | tf_op jit(solution)/shard_map/ppermute | solution.py:330
  30.4 3.4 %collective-permute-start.8 = (bf16[8,2,128,128]{3,2,1,0:T(8,128)(2,1)S(1)}, bf16[8,2,128,128]{3,2,1,0:T(8,128)(2,1)}, u32[]{:S(2)}, u32[]{:S(2)}) collective-permute-start(bf16[8,2,128,128]{3,2,1,0:T(8,128)(2,1)S(1)} %constant_dynamic-update-slice_fusion.refs_1_), channel_id=1, source_target_pairs={{0,8},{8,0},{16,24},{24,16},{1,9},{9,1},{17,25},{25,17},{2,10},{10... | collective-permute-start | bytes 1572872 | tf_op jit(solution)/shard_map/ppermute | solution.py:343
  34.0 2.4 %plan.1 = (s32[2]{0:T(128)S(1)}, s32[432]{0:T(512)S(1)}, s32[176]{0:T(256)S(1)}) custom-call(s32[1]{0:T(128)} %bitcast.2.pb_ref, s32[256]{0:T(256)S(1)} %reshape_squeeze.6.refs_0_, s32[256]{0:T(256)S(1)} %reshape_squeeze.7.refs_1_), custom_call_target="tpu_custom_call" | custom-call | tf_op jit(solution)/shard_map/plan/pallas_call | solution.py:138
  36.5 9.4 %collective-permute-done.8.refs_2_ = bf16[8,2,128,128]{3,2,1,0:T(8,128)(2,1)} collective-permute-done((bf16[8,2,128,128]{3,2,1,0:T(8,128)(2,1)S(1)}, bf16[8,2,128,128]{3,2,1,0:T(8,128)(2,1)}, u32[]{:S(2)}, u32[]{:S(2)}) %collective-permute-start.8) | collective-permute-done | bytes 524320 | tf_op jit(solution)/shard_map/ppermute | solution.py:343
  47.3 6.3 %collective-permute-start.21 = (bf16[8,2,128,128]{3,2,1,0:T(8,128)(2,1)S(1)}, bf16[8,2,128,128]{3,2,1,0:T(8,128)(2,1)S(1)}, u32[]{:S(2)}, u32[]{:S(2)}) collective-permute-start(bf16[8,2,128,128]{3,2,1,0:T(8,128)(2,1)S(1)} %constant_dynamic-update-slice_fusion.5.refs_1_), channel_id=1, source_target_pairs={{0,8},{8,0},{16,24},{24,16},{1,9},{9,1},{17,25},{25,17},{2,10},{10... | collective-permute-start | bytes 1572872 | tf_op jit(solution)/shard_map/ppermute | solution.py:343
  53.6 1.9 %collective-permute-start.10 = (bf16[8,128,128]{2,1,0:T(8,128)(2,1)S(1)}, bf16[8,128,128]{2,1,0:T(8,128)(2,1)S(1)}, u32[]{:S(2)}, u32[]{:S(2)}) collective-permute-start(bf16[8,128,128]{2,1,0:T(8,128)(2,1)S(1)} %copy-done.1), channel_id=1, source_target_pairs={{0,8},{24,16},{1,9},{25,17},{2,10},{26,18},{3,11},{27,19},{4,12},{... | collective-permute-start | bytes 786440 | tf_op jit(solution)/shard_map/ppermute | solution.py:346
  55.5 13.4 %collective-permute-done.10.refs_0_ = bf16[8,128,128]{2,1,0:T(8,128)(2,1)S(1)} collective-permute-done((bf16[8,128,128]{2,1,0:T(8,128)(2,1)S(1)}, bf16[8,128,128]{2,1,0:T(8,128)(2,1)S(1)}, u32[]{:S(2)}, u32[]{:S(2)}) %collective-permute-start.10) | collective-permute-done | bytes 262176 | tf_op jit(solution)/shard_map/ppermute | solution.py:346
  68.9 4.3 %attend_0_0.1 = (f32[16,1,128]{2,1,0:T(1,128)S(1)}, f32[16,1,128]{2,1,0:T(1,128)S(1)}, f32[16,128,128]{2,1,0:T(8,128)S(1)}) custom-call(s32[2]{0:T(128)S(1)} %get-tuple-element.39.count_ref, s32[432]{0:T(512)S(1)} %get-tuple-element.54.live_ref, bf16[8,128,128]{2,1,0:T(8,128)(2,1)S(1)} %copy-done.1, ...), custom_call_target="tpu_custom_call" | custom-call | bytes 16384 | tf_op jit(solution)/shard_map/attend_0_0/pallas_call | solution.py:252
  73.2 1.6 %attend_0_1.1 = (f32[16,1,128]{2,1,0:T(1,128)S(1)}, f32[16,1,128]{2,1,0:T(1,128)S(1)}, f32[16,128,128]{2,1,0:T(8,128)S(1)}, bf16[8,144,128]{2,1,0:T(8,128)(2,1)}) custom-call(s32[2]{0:T(128)S(1)} %get-tuple-element.39.count_ref, s32[176]{0:T(256)S(1)} %get-tuple-element.40.live_ref, bf16[8,128,128]{2,1,0:T(8,128)(2,1)S(1)} %copy-done.1, ...), custom_call_target="tpu_custom_call" | custom-call | bytes 16384 | tf_op jit(solution)/shard_map/attend_0_1/pallas_call | solution.py:252
  77.6 7.9 %collective-permute-start.20 = (bf16[8,128,128]{2,1,0:T(8,128)(2,1)S(1)}, bf16[8,128,128]{2,1,0:T(8,128)(2,1)S(1)}, u32[]{:S(2)}, u32[]{:S(2)}) collective-permute-start(bf16[8,128,128]{2,1,0:T(8,128)(2,1)S(1)} %copy-done), channel_id=1, source_target_pairs={{0,8},{24,16},{1,9},{25,17},{2,10},{26,18},{3,11},{27,19},{4,12},{... | collective-permute-start | bytes 786440 | tf_op jit(solution)/shard_map/ppermute | solution.py:346
  86.2 1.6 %collective-permute-start.16 = (bf16[1024,128]{1,0:T(8,128)(2,1)S(1)}, bf16[1024,128]{1,0:T(8,128)(2,1)S(1)}, u32[]{:S(2)}, u32[]{:S(2)}) collective-permute-start(bf16[1024,128]{1,0:T(8,128)(2,1)S(1)} %merge_0.1.refs_0_), channel_id=1, source_target_pairs={{0,4},{1,5},{2,6},{3,7},{4,0},{5,1},{6,2},{7,3},{8,12},{9,13},{10,... | collective-permute-start | bytes 786440 | tf_op jit(solution)/shard_map/ppermute | solution.py:330
  89.8 3.4 %attend_1_0.1 = (f32[16,1,128]{2,1,0:T(1,128)S(1)}, f32[16,1,128]{2,1,0:T(1,128)S(1)}, f32[16,128,128]{2,1,0:T(8,128)S(1)}) custom-call(s32[2]{0:T(128)S(1)} %get-tuple-element.39.count_ref, s32[432]{0:T(512)S(1)} %get-tuple-element.54.live_ref, bf16[8,128,128]{2,1,0:T(8,128)(2,1)S(1)} %copy-done, bf16[8,128,128]{2,1,0:T(8,128)(2,1)S(1)} %collective-permute-done.20.refs_0_, ...), custom_call_target="tpu_custom_call" | custom-call | bytes 16384 | tf_op jit(solution)/shard_map/attend_1_0/pallas_call | solution.py:252
  93.2 1.9 %collective-permute-done.16.refs_4_ = bf16[1024,128]{1,0:T(8,128)(2,1)S(1)} collective-permute-done((bf16[1024,128]{1,0:T(8,128)(2,1)S(1)}, bf16[1024,128]{1,0:T(8,128)(2,1)S(1)}, u32[]{:S(2)}, u32[]{:S(2)}) %collective-permute-start.16) | collective-permute-done | bytes 262176 | tf_op jit(solution)/shard_map/ppermute | solution.py:330
  95.2 1.7 %attend_1_1.1 = (f32[16,1,128]{2,1,0:T(1,128)S(1)}, f32[16,1,128]{2,1,0:T(1,128)S(1)}, f32[16,128,128]{2,1,0:T(8,128)S(1)}, bf16[8,144,128]{2,1,0:T(8,128)(2,1)S(1)}) custom-call(s32[2]{0:T(128)S(1)} %get-tuple-element.39.count_ref, s32[176]{0:T(256)S(1)} %get-tuple-element.40.live_ref, bf16[8,128,128]{2,1,0:T(8,128)(2,1)S(1)} %copy-done, ...), custom_call_target="tpu_custom_call" | custom-call | bytes 16384 | tf_op jit(solution)/shard_map/attend_1_1/pallas_call | solution.py:252
  99.9 6.7 %collective-permute-done.24.part_ref = bf16[8,144,128]{2,1,0:T(8,128)(2,1)S(1)} collective-permute-done((bf16[8,144,128]{2,1,0:T(8,128)(2,1)S(1)}, bf16[8,144,128]{2,1,0:T(8,128)(2,1)S(1)}, u32[]{:S(2)}, u32[]{:S(2)}) %collective-permute-start.24) | collective-permute-done | bytes 294944 | tf_op jit(solution)/shard_map/ppermute | solution.py:349
  106.7 2.5 %collective-permute-start.30 = (bf16[1024,128]{1,0:T(8,128)(2,1)S(1)}, bf16[1024,128]{1,0:T(8,128)(2,1)S(1)}, u32[]{:S(2)}, u32[]{:S(2)}) collective-permute-start(bf16[1024,128]{1,0:T(8,128)(2,1)S(1)} %merge_1.1.refs_8_), channel_id=1, source_target_pairs={{0,6},{1,7},{2,4},{3,5},{4,2},{5,3},{6,0},{7,1},{8,14},{9,15},{10,... | collective-permute-start | bytes 786440 | tf_op jit(solution)/shard_map/ppermute | solution.py:330
  110.8 3.4 %collective-permute-done.30.refs_14_ = bf16[1024,128]{1,0:T(8,128)(2,1)S(1)} collective-permute-done((bf16[1024,128]{1,0:T(8,128)(2,1)S(1)}, bf16[1024,128]{1,0:T(8,128)(2,1)S(1)}, u32[]{:S(2)}, u32[]{:S(2)}) %collective-permute-start.30) | collective-permute-done | bytes 262176 | tf_op jit(solution)/shard_map/ppermute | solution.py:330
  114.2 2.7 %collective-permute-done.28.refs_12_ = bf16[1024,128]{1,0:T(8,128)(2,1)S(1)} collective-permute-done((bf16[1024,128]{1,0:T(8,128)(2,1)S(1)}, bf16[1024,128]{1,0:T(8,128)(2,1)S(1)}, u32[]{:S(2)}, u32[]{:S(2)}) %collective-permute-start.28) | collective-permute-done | bytes 262176 | tf_op jit(solution)/shard_map/ppermute | solution.py:330
  118.8 2.1 %place.1 = bf16[1024,2048]{1,0:T(8,128)(2,1)} custom-call(s32[1]{0:T(128)} %bitcast.me_ref, bf16[1024,128]{1,0:T(8,128)(2,1)S(1)} %merge_0.1.refs_0_, bf16[1024,128]{1,0:T(8,128)(2,1)S(1)} %collective-permute-done.13.refs_1_, bf16[1024,128]{1,0:T(8,128)(2,1)S(1)} %collective-permute-done.14.refs_2_, bf16[1024,128]{1,0:T(8,128)(2,1)S(1)} %collective-permute-done.15.refs_3_, ...), custom_call_target="tpu_custom_call" | custom-call | tf_op jit(solution)/shard_map/place/pallas_call | solution.py:309
  (84 shorter events, 20.8 us)
Async XLA Ops:
  0.0 8.2 %collective-permute-start = (s32[4,8]{1,0:T(4,128)}, s32[4,8]{1,0:T(4,128)S(1)}, u32[]{:S(2)}, u32[]{:S(2)}) collective-permute-start(s32[4,8]{1,0:T(4,128)} %bitcast.39), channel_id=1, source_target_pairs={{0,8},{24,16},{1,9},{25,17},{2,10},{26,18},{3,11},{27,19},{4,12},{... | collective-permute-start | bytes 392 | tf_op jit(solution)/shard_map/ppermute | solution.py:346
  8.9 18.6 %collective-permute-start.4 = (bf16[2,2,256,128]{3,2,1,0:T(8,128)(2,1)}, bf16[2,2,256,128]{3,2,1,0:T(8,128)(2,1)S(1)}, u32[]{:S(2)}, u32[]{:S(2)}) collective-permute-start(bf16[2,2,256,128]{3,2,1,0:T(8,128)(2,1)} %get-tuple-element.42), channel_id=1, source_target_pairs={{0,2},{1,3},{2,0},{3,1},{4,6},{5,7},{6,4},{7,5},{8,10},{9,11},{10,... | collective-permute-start | bytes 786440 | tf_op jit(solution)/shard_map/ppermute | solution.py:330
  10.4 17.1 %collective-permute-start.5 = (bf16[2,2,256,128]{3,2,1,0:T(8,128)(2,1)}, bf16[2,2,256,128]{3,2,1,0:T(8,128)(2,1)S(1)}, u32[]{:S(2)}, u32[]{:S(2)}) collective-permute-start(bf16[2,2,256,128]{3,2,1,0:T(8,128)(2,1)} %get-tuple-element.43), channel_id=1, source_target_pairs={{0,4},{1,5},{2,6},{3,7},{4,0},{5,1},{6,2},{7,3},{8,12},{9,13},{10,... | collective-permute-start | bytes 786440 | tf_op jit(solution)/shard_map/ppermute | solution.py:330
  11.9 15.6 %collective-permute-start.6 = (bf16[2,2,256,128]{3,2,1,0:T(8,128)(2,1)}, bf16[2,2,256,128]{3,2,1,0:T(8,128)(2,1)S(1)}, u32[]{:S(2)}, u32[]{:S(2)}) collective-permute-start(bf16[2,2,256,128]{3,2,1,0:T(8,128)(2,1)} %get-tuple-element.44), channel_id=1, source_target_pairs={{0,6},{1,7},{2,4},{3,5},{4,2},{5,3},{6,0},{7,1},{8,14},{9,15},{10,... | collective-permute-start | bytes 786440 | tf_op jit(solution)/shard_map/ppermute | solution.py:330
  12.4 11.3 %collective-permute-start.2 = (s32[2,2,4,8]{3,2,1,0:T(4,128)S(1)}, s32[2,2,4,8]{3,2,1,0:T(4,128)S(1)}, u32[]{:S(2)}, u32[]{:S(2)}) collective-permute-start(s32[2,2,4,8]{3,2,1,0:T(4,128)S(1)} %pad_add_fusion.2), channel_id=1, source_target_pairs={{0,2},{1,3},{2,0},{3,1},{4,6},{5,7},{6,4},{7,5},{8,10},{9,11},{10,... | collective-permute-start | bytes 1544 | tf_op jit(solution)/shard_map/ppermute | solution.py:330
  30.4 15.4 %collective-permute-start.8 = (bf16[8,2,128,128]{3,2,1,0:T(8,128)(2,1)S(1)}, bf16[8,2,128,128]{3,2,1,0:T(8,128)(2,1)}, u32[]{:S(2)}, u32[]{:S(2)}) collective-permute-start(bf16[8,2,128,128]{3,2,1,0:T(8,128)(2,1)S(1)} %constant_dynamic-update-slice_fusion.refs_1_), channel_id=1, source_target_pairs={{0,8},{8,0},{16,24},{24,16},{1,9},{9,1},{17,25},{25,17},{2,10},{10... | collective-permute-start | bytes 1572872 | tf_op jit(solution)/shard_map/ppermute | solution.py:343
  45.9 27.4 %collective-permute-start.11 = (bf16[8,2,128,128]{3,2,1,0:T(8,128)(2,1)}, bf16[8,2,128,128]{3,2,1,0:T(8,128)(2,1)S(1)}, u32[]{:S(2)}, u32[]{:S(2)}) collective-permute-start(bf16[8,2,128,128]{3,2,1,0:T(8,128)(2,1)} %collective-permute-done.8.refs_2_), channel_id=1, source_target_pairs={{8,16},{16,8},{9,17},{17,9},{10,18},{18,10},{11,19},{19,11},{12,20... | collective-permute-start | bytes 1572872 | tf_op jit(solution)/shard_map/ppermute | solution.py:343
  46.6 29.5 %collective-permute-start.22 = (bf16[8,2,128,128]{3,2,1,0:T(8,128)(2,1)S(1)}, bf16[8,2,128,128]{3,2,1,0:T(8,128)(2,1)S(1)}, u32[]{:S(2)}, u32[]{:S(2)}) collective-permute-start(bf16[8,2,128,128]{3,2,1,0:T(8,128)(2,1)S(1)} %constant_dynamic-update-slice_fusion.5.refs_1_), channel_id=1, source_target_pairs={{8,16},{16,8},{9,17},{17,9},{10,18},{18,10},{11,19},{19,11},{12,20... | collective-permute-start | bytes 1572872 | tf_op jit(solution)/shard_map/ppermute | solution.py:343
  47.3 28.8 %collective-permute-start.21 = (bf16[8,2,128,128]{3,2,1,0:T(8,128)(2,1)S(1)}, bf16[8,2,128,128]{3,2,1,0:T(8,128)(2,1)S(1)}, u32[]{:S(2)}, u32[]{:S(2)}) collective-permute-start(bf16[8,2,128,128]{3,2,1,0:T(8,128)(2,1)S(1)} %constant_dynamic-update-slice_fusion.5.refs_1_), channel_id=1, source_target_pairs={{0,8},{8,0},{16,24},{24,16},{1,9},{9,1},{17,25},{25,17},{2,10},{10... | collective-permute-start | bytes 1572872 | tf_op jit(solution)/shard_map/ppermute | solution.py:343
  53.6 15.4 %collective-permute-start.10 = (bf16[8,128,128]{2,1,0:T(8,128)(2,1)S(1)}, bf16[8,128,128]{2,1,0:T(8,128)(2,1)S(1)}, u32[]{:S(2)}, u32[]{:S(2)}) collective-permute-start(bf16[8,128,128]{2,1,0:T(8,128)(2,1)S(1)} %copy-done.1), channel_id=1, source_target_pairs={{0,8},{24,16},{1,9},{25,17},{2,10},{26,18},{3,11},{27,19},{4,12},{... | collective-permute-start | bytes 786440 | tf_op jit(solution)/shard_map/ppermute | solution.py:346
  74.8 11.2 %collective-permute-start.12 = (bf16[8,144,128]{2,1,0:T(8,128)(2,1)}, bf16[8,144,128]{2,1,0:T(8,128)(2,1)S(1)}, u32[]{:S(2)}, u32[]{:S(2)}) collective-permute-start(bf16[8,144,128]{2,1,0:T(8,128)(2,1)} %get-tuple-element.61), channel_id=1, source_target_pairs={{8,0},{16,24},{9,1},{17,25},{10,2},{18,26},{11,3},{19,27},{12,4},{... | collective-permute-start | bytes 884744 | tf_op jit(solution)/shard_map/ppermute | solution.py:349
  76.1 17.1 %collective-permute-start.23 = (bf16[8,2,128,128]{3,2,1,0:T(8,128)(2,1)S(1)}, bf16[8,2,128,128]{3,2,1,0:T(8,128)(2,1)}, u32[]{:S(2)}, u32[]{:S(2)}) collective-permute-start(bf16[8,2,128,128]{3,2,1,0:T(8,128)(2,1)S(1)} %collective-permute-done.21.refs_2_), channel_id=1, source_target_pairs={{8,16},{16,8},{9,17},{17,9},{10,18},{18,10},{11,19},{19,11},{12,20... | collective-permute-start | bytes 1572872 | tf_op jit(solution)/shard_map/ppermute | solution.py:343
  77.6 12.2 %collective-permute-start.20 = (bf16[8,128,128]{2,1,0:T(8,128)(2,1)S(1)}, bf16[8,128,128]{2,1,0:T(8,128)(2,1)S(1)}, u32[]{:S(2)}, u32[]{:S(2)}) collective-permute-start(bf16[8,128,128]{2,1,0:T(8,128)(2,1)S(1)} %copy-done), channel_id=1, source_target_pairs={{0,8},{24,16},{1,9},{25,17},{2,10},{26,18},{3,11},{27,19},{4,12},{... | collective-permute-start | bytes 786440 | tf_op jit(solution)/shard_map/ppermute | solution.py:346
  86.2 8.9 %collective-permute-start.16 = (bf16[1024,128]{1,0:T(8,128)(2,1)S(1)}, bf16[1024,128]{1,0:T(8,128)(2,1)S(1)}, u32[]{:S(2)}, u32[]{:S(2)}) collective-permute-start(bf16[1024,128]{1,0:T(8,128)(2,1)S(1)} %merge_0.1.refs_0_), channel_id=1, source_target_pairs={{0,4},{1,5},{2,6},{3,7},{4,0},{5,1},{6,2},{7,3},{8,12},{9,13},{10,... | collective-permute-start | bytes 786440 | tf_op jit(solution)/shard_map/ppermute | solution.py:330
  87.8 7.4 %collective-permute-start.14 = (bf16[1024,128]{1,0:T(8,128)(2,1)S(1)}, bf16[1024,128]{1,0:T(8,128)(2,1)S(1)}, u32[]{:S(2)}, u32[]{:S(2)}) collective-permute-start(bf16[1024,128]{1,0:T(8,128)(2,1)S(1)} %merge_0.1.refs_0_), channel_id=1, source_target_pairs={{0,2},{1,3},{2,0},{3,1},{4,6},{5,7},{6,4},{7,5},{8,10},{9,11},{10,... | collective-permute-start | bytes 786440 | tf_op jit(solution)/shard_map/ppermute | solution.py:330
  89.2 8.7 %collective-permute-start.18 = (bf16[1024,128]{1,0:T(8,128)(2,1)S(1)}, bf16[1024,128]{1,0:T(8,128)(2,1)S(1)}, u32[]{:S(2)}, u32[]{:S(2)}) collective-permute-start(bf16[1024,128]{1,0:T(8,128)(2,1)S(1)} %merge_0.1.refs_0_), channel_id=1, source_target_pairs={{0,6},{1,7},{2,4},{3,5},{4,2},{5,3},{6,0},{7,1},{8,14},{9,15},{10,... | collective-permute-start | bytes 786440 | tf_op jit(solution)/shard_map/ppermute | solution.py:330
  97.9 8.6 %collective-permute-start.24 = (bf16[8,144,128]{2,1,0:T(8,128)(2,1)S(1)}, bf16[8,144,128]{2,1,0:T(8,128)(2,1)S(1)}, u32[]{:S(2)}, u32[]{:S(2)}) collective-permute-start(bf16[8,144,128]{2,1,0:T(8,128)(2,1)S(1)} %get-tuple-element.72), channel_id=1, source_target_pairs={{8,0},{16,24},{9,1},{17,25},{10,2},{18,26},{11,3},{19,27},{12,4},{... | collective-permute-start | bytes 884744 | tf_op jit(solution)/shard_map/ppermute | solution.py:349
  99.2 10.5 %collective-permute-start.13 = (bf16[1024,128]{1,0:T(8,128)(2,1)S(1)}, bf16[1024,128]{1,0:T(8,128)(2,1)S(1)}, u32[]{:S(2)}, u32[]{:S(2)}) collective-permute-start(bf16[1024,128]{1,0:T(8,128)(2,1)S(1)} %merge_0.1.refs_0_), channel_id=1, source_target_pairs={{0,1},{1,0},{2,3},{3,2},{4,5},{5,4},{6,7},{7,6},{8,9},{9,8},{10,11... | collective-permute-start | bytes 786440 | tf_op jit(solution)/shard_map/ppermute | solution.py:330
  99.3 11.0 %collective-permute-start.19 = (bf16[1024,128]{1,0:T(8,128)(2,1)S(1)}, bf16[1024,128]{1,0:T(8,128)(2,1)S(1)}, u32[]{:S(2)}, u32[]{:S(2)}) collective-permute-start(bf16[1024,128]{1,0:T(8,128)(2,1)S(1)} %collective-permute-done.18.refs_6_), channel_id=1, source_target_pairs={{0,1},{1,0},{2,3},{3,2},{4,5},{5,4},{6,7},{7,6},{8,9},{9,8},{10,11... | collective-permute-start | bytes 786440 | tf_op jit(solution)/shard_map/ppermute | solution.py:330
  99.8 10.5 %collective-permute-start.17 = (bf16[1024,128]{1,0:T(8,128)(2,1)S(1)}, bf16[1024,128]{1,0:T(8,128)(2,1)S(1)}, u32[]{:S(2)}, u32[]{:S(2)}) collective-permute-start(bf16[1024,128]{1,0:T(8,128)(2,1)S(1)} %collective-permute-done.16.refs_4_), channel_id=1, source_target_pairs={{0,1},{1,0},{2,3},{3,2},{4,5},{5,4},{6,7},{7,6},{8,9},{9,8},{10,11... | collective-permute-start | bytes 786440 | tf_op jit(solution)/shard_map/ppermute | solution.py:330
  106.7 7.4 %collective-permute-start.30 = (bf16[1024,128]{1,0:T(8,128)(2,1)S(1)}, bf16[1024,128]{1,0:T(8,128)(2,1)S(1)}, u32[]{:S(2)}, u32[]{:S(2)}) collective-permute-start(bf16[1024,128]{1,0:T(8,128)(2,1)S(1)} %merge_1.1.refs_8_), channel_id=1, source_target_pairs={{0,6},{1,7},{2,4},{3,5},{4,2},{5,3},{6,0},{7,1},{8,14},{9,15},{10,... | collective-permute-start | bytes 786440 | tf_op jit(solution)/shard_map/ppermute | solution.py:330
  109.2 7.7 %collective-permute-start.28 = (bf16[1024,128]{1,0:T(8,128)(2,1)S(1)}, bf16[1024,128]{1,0:T(8,128)(2,1)S(1)}, u32[]{:S(2)}, u32[]{:S(2)}) collective-permute-start(bf16[1024,128]{1,0:T(8,128)(2,1)S(1)} %merge_1.1.refs_8_), channel_id=1, source_target_pairs={{0,4},{1,5},{2,6},{3,7},{4,0},{5,1},{6,2},{7,3},{8,12},{9,13},{10,... | collective-permute-start | bytes 786440 | tf_op jit(solution)/shard_map/ppermute | solution.py:330
  109.8 7.2 %collective-permute-start.26 = (bf16[1024,128]{1,0:T(8,128)(2,1)S(1)}, bf16[1024,128]{1,0:T(8,128)(2,1)S(1)}, u32[]{:S(2)}, u32[]{:S(2)}) collective-permute-start(bf16[1024,128]{1,0:T(8,128)(2,1)S(1)} %merge_1.1.refs_8_), channel_id=1, source_target_pairs={{0,2},{1,3},{2,0},{3,1},{4,6},{5,7},{6,4},{7,5},{8,10},{9,11},{10,... | collective-permute-start | bytes 786440 | tf_op jit(solution)/shard_map/ppermute | solution.py:330
  110.3 7.1 %collective-permute-start.15 = (bf16[1024,128]{1,0:T(8,128)(2,1)S(1)}, bf16[1024,128]{1,0:T(8,128)(2,1)S(1)}, u32[]{:S(2)}, u32[]{:S(2)}) collective-permute-start(bf16[1024,128]{1,0:T(8,128)(2,1)S(1)} %collective-permute-done.14.refs_2_), channel_id=1, source_target_pairs={{0,1},{1,0},{2,3},{3,2},{4,5},{5,4},{6,7},{7,6},{8,9},{9,8},{10,11... | collective-permute-start | bytes 786440 | tf_op jit(solution)/shard_map/ppermute | solution.py:330
  (11 other events, 125.2 us)

commit v16 on v13

--- a/solution.py
+++ b/solution.py
@@ -424,21 +424,21 @@
             sources = ([owns[c]] if step == 0 else []) + over[c]
             even, odd = over[c]
             if even is not None and odd is not None:
-                even, odd = after((even, odd), guest[c] if c else (even, odd))
+                even, odd = after((even, odd), (even, odd))
             over[c] = [exchange(odd, 0, step + 2), exchange(even, 1, step + 2)]
             state[c] = run(c, step, sources)
 
     pieces = []
-    sent = far = None
+    sent = None
     for c in range(heads):
-        found = run(c, last, ([] if last else [owns[c]]) + after(over[c], sent))
+        found = run(c, last, ([] if last else [owns[c]]) + over[c])
         if relay:
             outer = ((pb == 0) | (pb == n_pb - 1)).astype(jnp.int32)[None]
-            out = merge(outer, found[:3], outward(after(found[3], far)), f"merge_{c}")
+            out = merge(outer, found[:3], outward(after(found[3], sent)), f"merge_{c}")
         else:
             out = found[0]
         mine = [out] + [swap(out, k) for k in range(2, n_ka, 2)]
-        sent, far = mine[: n_ka // 4 + 1], mine[n_ka // 4 + 1 :]
+        sent = mine[: n_ka // 4 + 1]
         others = [swap(x, 1) for x in mine]
         pieces += [x for two in zip(mine, others) for x in two]
     return place(me1, pieces, n_ka, heads)

time: 106 us -> 111 us (1.047)
  the two profiles are of different devices: /device:TPU:0 before, /device:TPU:9 now
where the time goes in v16:
time: 111 us; the launch traced here: 110 us
  starting transfers between devices  39.9 us (36%)
  waiting for transfers between devices  38 us (34%)
  Pallas kernels  29.6 us (27%)
  local copies, waits for them, and re-layouts  1.37 us (1%)
    ppermute x22, starting transfers between devices, swap(): return lax.ppermute(x, 'ka', [(i, i ^ k) for i in range(n_ka)])  23.8 us
    ppermute x22, waiting for transfers between devices, swap(): return lax.ppermute(x, 'ka', [(i, i ^ k) for i in range(n_ka)])  22.3 us
    pallas_call x4, Pallas kernels, attend(): pl.pallas_call(functools.partial(attend_kernel, n_src, entry, first, mode...  17.3 us
    ppermute x3, waiting for transfers between devices, inward(): return lax.ppermute(x, 'pb', [(0, 1), (n_pb - 1, n_pb - 2)])  12.7 us
    ppermute x6, starting transfers between devices, exchange(): return lax.ppermute(x, 'pb', found) if found else None  9.62 us
    pallas_call x2, Pallas kernels, pack(): pl.pallas_call(functools.partial(pack_kernel, n_ka, heads, c, len(masks))...  5.38 us
    ppermute x3, starting transfers between devices, inward(): return lax.ppermute(x, 'pb', [(0, 1), (n_pb - 1, n_pb - 2)])  3.85 us
    ppermute x6, waiting for transfers between devices, exchange(): return lax.ppermute(x, 'pb', found) if found else None  2.89 us
  transfers between devices with their start and end apart: 33, of which 16 were waited for; matrix products, arithmetic and copies ran while one was open for 1% of the time, Pallas kernels for 23%

profile of v16, /device:TPU:9, one launch (start us, length us, event | category | flops | bytes accessed | tf_op | source)
XLA Modules:
  0.0 110.1 jit_solution(12637348595041766370)
XLA Ops:
  0.0 2.3 %pack_0.1 = (bf16[2,256,128]{2,1,0:T(8,128)(2,1)}, bf16[2,256,128]{2,1,0:T(8,128)(2,1)}, bf16[2,256,128]{2,1,0:T(8,128)(2,1)}, bf16[2,256,128]{2,1,0:T(8,128)(2,1)}) custom-call(s32[1]{0:T(128)} %bitcast.me_ref, bf16[128,2048]{1,0:T(8,128)(2,1)} %refs_2_.1, bf16[128,2048]{1,0:T(8,128)(2,1)} %refs_3_.1), custom_call_target="tpu_custom_call" | custom-call | bytes 262144 | tf_op jit(solution)/shard_map/pack_0/pallas_call | solution.py:77
  6.3 2.0 %turn.1 = (bf16[8,128,128]{2,1,0:T(8,128)(2,1)}, bf16[8,128,128]{2,1,0:T(8,128)(2,1)}) custom-call(s32[1]{0:T(128)} %bitcast.me_ref, bf16[1024,2048]{1,0:T(8,128)(2,1)} %q_all.1), custom_call_target="tpu_custom_call" | custom-call | bytes 131072 | tf_op jit(solution)/shard_map/turn/pallas_call | solution.py:105
  10.7 2.0 %collective-permute-start.4 = (bf16[4,256,128]{2,1,0:T(8,128)(2,1)S(1)}, bf16[4,256,128]{2,1,0:T(8,128)(2,1)S(1)}, u32[]{:S(2)}, u32[]{:S(2)}) collective-permute-start(bf16[4,256,128]{2,1,0:T(8,128)(2,1)S(1)} %pad_maximum_fusion.1), channel_id=1, source_target_pairs={{0,1},{1,0},{2,3},{3,2},{4,5},{5,4},{6,7},{7,6},{8,9},{9,8},{10,11... | collective-permute-start | bytes 786440 | tf_op jit(solution)/shard_map/ppermute | solution.py:351
  14.0 3.3 %collective-permute-start.9 = (bf16[8,2,128,128]{3,2,1,0:T(8,128)(2,1)S(1)}, bf16[8,2,128,128]{3,2,1,0:T(8,128)(2,1)S(1)}, u32[]{:S(2)}, u32[]{:S(2)}) collective-permute-start(bf16[8,2,128,128]{3,2,1,0:T(8,128)(2,1)S(1)} %bitcast.9), channel_id=1, source_target_pairs={{8,16},{16,8},{9,17},{17,9},{10,18},{18,10},{11,19},{19,11},{12,20... | collective-permute-start | bytes 1572872 | tf_op jit(solution)/shard_map/ppermute | solution.py:364
  17.4 3.1 %pack_1.1 = (bf16[2,288,128]{2,1,0:T(8,128)(2,1)}, bf16[2,288,128]{2,1,0:T(8,128)(2,1)}, bf16[2,288,128]{2,1,0:T(8,128)(2,1)}, bf16[2,288,128]{2,1,0:T(8,128)(2,1)}) custom-call(s32[1]{0:T(128)} %bitcast.me_ref, s32[4,8]{1,0:T(4,128)} %bitcast.13, s32[4,8]{1,0:T(4,128)} %copy-done.4, bf16[128,2048]{1,0:T(8,128)(2,1)} %refs_2_.1, bf16[128,2048]{1,0:T(8,128)(2,1)} %refs_3_.1), custom_call_target="tpu_custom_call" | custom-call | bytes 262144 | tf_op jit(solution)/shard_map/pack_1/pallas_call | solution.py:77
  23.2 2.3 %collective-permute-done.5 = bf16[2,288,128]{2,1,0:T(8,128)(2,1)S(1)} collective-permute-done((bf16[2,288,128]{2,1,0:T(8,128)(2,1)}, bf16[2,288,128]{2,1,0:T(8,128)(2,1)S(1)}, u32[]{:S(2)}, u32[]{:S(2)}) %collective-permute-start.5) | collective-permute-done | bytes 147488 | tf_op jit(solution)/shard_map/ppermute | solution.py:351
  26.1 3.6 %collective-permute-done.7 = bf16[2,288,128]{2,1,0:T(8,128)(2,1)S(1)} collective-permute-done((bf16[2,288,128]{2,1,0:T(8,128)(2,1)}, bf16[2,288,128]{2,1,0:T(8,128)(2,1)S(1)}, u32[]{:S(2)}, u32[]{:S(2)}) %collective-permute-start.7) | collective-permute-done | bytes 147488 | tf_op jit(solution)/shard_map/ppermute | solution.py:351
  34.1 2.1 %collective-permute-start.12 = (bf16[8,2,128,128]{3,2,1,0:T(8,128)(2,1)S(1)}, bf16[8,2,128,128]{3,2,1,0:T(8,128)(2,1)}, u32[]{:S(2)}, u32[]{:S(2)}) collective-permute-start(bf16[8,2,128,128]{3,2,1,0:T(8,128)(2,1)S(1)} %collective-permute-done.8.refs_2_), channel_id=1, source_target_pairs={{8,16},{16,8},{9,17},{17,9},{10,18},{18,10},{11,19},{19,11},{12,20... | collective-permute-start | bytes 1572872 | tf_op jit(solution)/shard_map/ppermute | solution.py:364
  36.3 6.4 %collective-permute-done.11.refs_0_ = bf16[8,128,128]{2,1,0:T(8,128)(2,1)S(1)} collective-permute-done((bf16[8,128,128]{2,1,0:T(8,128)(2,1)S(1)}, bf16[8,128,128]{2,1,0:T(8,128)(2,1)S(1)}, u32[]{:S(2)}, u32[]{:S(2)}) %collective-permute-start.11) | collective-permute-done | bytes 262176 | tf_op jit(solution)/shard_map/ppermute | solution.py:367
  42.7 2.1 %collective-permute-start.23 = (bf16[8,2,128,128]{3,2,1,0:T(8,128)(2,1)S(1)}, bf16[8,2,128,128]{3,2,1,0:T(8,128)(2,1)}, u32[]{:S(2)}, u32[]{:S(2)}) collective-permute-start(bf16[8,2,128,128]{3,2,1,0:T(8,128)(2,1)S(1)} %bitcast.7), channel_id=1, source_target_pairs={{8,16},{16,8},{9,17},{17,9},{10,18},{18,10},{11,19},{19,11},{12,20... | collective-permute-start | bytes 1572872 | tf_op jit(solution)/shard_map/ppermute | solution.py:364
  45.8 2.4 %plan.1 = (s32[2]{0:T(128)S(1)}, s32[432]{0:T(512)S(1)}, s32[176]{0:T(256)S(1)}) custom-call(s32[1]{0:T(128)} %bitcast.2.pb_ref, s32[256]{0:T(256)S(1)} %reshape.24.refs_0_, s32[256]{0:T(256)S(1)} %reshape.26.refs_1_), custom_call_target="tpu_custom_call" | custom-call | tf_op jit(solution)/shard_map/plan/pallas_call | solution.py:159
  48.1 4.7 %attend_0_0.1 = (f32[16,1,128]{2,1,0:T(1,128)S(1)}, f32[16,1,128]{2,1,0:T(1,128)S(1)}, f32[16,128,128]{2,1,0:T(8,128)S(1)}) custom-call(s32[2]{0:T(128)S(1)} %get-tuple-element.77.count_ref, s32[432]{0:T(512)S(1)} %get-tuple-element.81.live_ref, bf16[8,128,128]{2,1,0:T(8,128)(2,1)S(1)} %copy-done.1, ...), custom_call_target="tpu_custom_call" | custom-call | bytes 16384 | tf_op jit(solution)/shard_map/attend_0_0/pallas_call | solution.py:273
  52.8 4.3 %attend_0_1.1 = (f32[16,1,128]{2,1,0:T(1,128)S(1)}, f32[16,1,128]{2,1,0:T(1,128)S(1)}, f32[16,128,128]{2,1,0:T(8,128)S(1)}, bf16[8,144,128]{2,1,0:T(8,128)(2,1)}) custom-call(s32[2]{0:T(128)S(1)} %get-tuple-element.77.count_ref, s32[176]{0:T(256)S(1)} %get-tuple-element.78.live_ref, bf16[8,128,128]{2,1,0:T(8,128)(2,1)S(1)} %copy-done.1, ...), custom_call_target="tpu_custom_call" | custom-call | bytes 16384 | tf_op jit(solution)/shard_map/attend_0_1/pallas_call | solution.py:273
  58.5 2.4 %collective-permute-done.23.refs_3_ = bf16[8,2,128,128]{3,2,1,0:T(8,128)(2,1)} collective-permute-done((bf16[8,2,128,128]{3,2,1,0:T(8,128)(2,1)S(1)}, bf16[8,2,128,128]{3,2,1,0:T(8,128)(2,1)}, u32[]{:S(2)}, u32[]{:S(2)}) %collective-permute-start.23) | collective-permute-done | bytes 524320 | tf_op jit(solution)/shard_map/ppermute | solution.py:364
  60.9 2.1 %collective-permute-start.24 = (bf16[8,2,128,128]{3,2,1,0:T(8,128)(2,1)S(1)}, bf16[8,2,128,128]{3,2,1,0:T(8,128)(2,1)S(1)}, u32[]{:S(2)}, u32[]{:S(2)}) collective-permute-start(bf16[8,2,128,128]{3,2,1,0:T(8,128)(2,1)S(1)} %collective-permute-done.22.refs_2_), channel_id=1, source_target_pairs={{8,16},{16,8},{9,17},{17,9},{10,18},{18,10},{11,19},{19,11},{12,20... | collective-permute-start | bytes 1572872 | tf_op jit(solution)/shard_map/ppermute | solution.py:364
  66.8 4.7 %collective-permute-done.21.refs_0_ = bf16[8,128,128]{2,1,0:T(8,128)(2,1)S(1)} collective-permute-done((bf16[8,128,128]{2,1,0:T(8,128)(2,1)S(1)}, bf16[8,128,128]{2,1,0:T(8,128)(2,1)S(1)}, u32[]{:S(2)}, u32[]{:S(2)}) %collective-permute-start.21) | collective-permute-done | bytes 262176 | tf_op jit(solution)/shard_map/ppermute | solution.py:367
  71.6 5.5 %attend_1_0.1 = (f32[16,1,128]{2,1,0:T(1,128)S(1)}, f32[16,1,128]{2,1,0:T(1,128)S(1)}, f32[16,128,128]{2,1,0:T(8,128)S(1)}) custom-call(s32[2]{0:T(128)S(1)} %get-tuple-element.77.count_ref, s32[432]{0:T(512)S(1)} %get-tuple-element.81.live_ref, bf16[8,128,128]{2,1,0:T(8,128)(2,1)S(1)} %copy-done, bf16[8,128,128]{2,1,0:T(8,128)(2,1)S(1)} %collective-permute-done.21.refs_0_, ...), custom_call_target="tpu_custom_call" | custom-call | bytes 16384 | tf_op jit(solution)/shard_map/attend_1_0/pallas_call | solution.py:273
  77.1 2.8 %attend_1_1.1 = (f32[16,1,128]{2,1,0:T(1,128)S(1)}, f32[16,1,128]{2,1,0:T(1,128)S(1)}, f32[16,128,128]{2,1,0:T(8,128)S(1)}, bf16[8,144,128]{2,1,0:T(8,128)(2,1)S(1)}) custom-call(s32[2]{0:T(128)S(1)} %get-tuple-element.77.count_ref, s32[176]{0:T(256)S(1)} %get-tuple-element.78.live_ref, bf16[8,128,128]{2,1,0:T(8,128)(2,1)S(1)} %copy-done, ...), custom_call_target="tpu_custom_call" | custom-call | bytes 16384 | tf_op jit(solution)/shard_map/attend_1_1/pallas_call | solution.py:273
  83.2 2.3 %collective-permute-start.14 = (bf16[1024,128]{1,0:T(8,128)(2,1)S(1)}, bf16[1024,128]{1,0:T(8,128)(2,1)S(1)}, u32[]{:S(2)}, u32[]{:S(2)}) collective-permute-start(bf16[1024,128]{1,0:T(8,128)(2,1)S(1)} %merge_0.1.refs_0_), channel_id=1, source_target_pairs={{0,1},{1,0},{2,3},{3,2},{4,5},{5,4},{6,7},{7,6},{8,9},{9,8},{10,11... | collective-permute-start | bytes 786440 | tf_op jit(solution)/shard_map/ppermute | solution.py:351
  85.5 2.5 %collective-permute-done.19.refs_6_ = bf16[1024,128]{1,0:T(8,128)(2,1)S(1)} collective-permute-done((bf16[1024,128]{1,0:T(8,128)(2,1)S(1)}, bf16[1024,128]{1,0:T(8,128)(2,1)S(1)}, u32[]{:S(2)}, u32[]{:S(2)}) %collective-permute-start.19) | collective-permute-done | bytes 262176 | tf_op jit(solution)/shard_map/ppermute | solution.py:351
  88.0 2.9 %collective-permute-start.20 = (bf16[1024,128]{1,0:T(8,128)(2,1)S(1)}, bf16[1024,128]{1,0:T(8,128)(2,1)S(1)}, u32[]{:S(2)}, u32[]{:S(2)}) collective-permute-start(bf16[1024,128]{1,0:T(8,128)(2,1)S(1)} %collective-permute-done.19.refs_6_), channel_id=1, source_target_pairs={{0,1},{1,0},{2,3},{3,2},{4,5},{5,4},{6,7},{7,6},{8,9},{9,8},{10,11... | collective-permute-start | bytes 786440 | tf_op jit(solution)/shard_map/ppermute | solution.py:351
  94.8 5.3 %collective-permute-done.31.refs_14_ = bf16[1024,128]{1,0:T(8,128)(2,1)S(1)} collective-permute-done((bf16[1024,128]{1,0:T(8,128)(2,1)S(1)}, bf16[1024,128]{1,0:T(8,128)(2,1)S(1)}, u32[]{:S(2)}, u32[]{:S(2)}) %collective-permute-start.31) | collective-permute-done | bytes 262176 | tf_op jit(solution)/shard_map/ppermute | solution.py:351
  101.2 4.7 %collective-permute-done.29.refs_12_ = bf16[1024,128]{1,0:T(8,128)(2,1)S(1)} collective-permute-done((bf16[1024,128]{1,0:T(8,128)(2,1)S(1)}, bf16[1024,128]{1,0:T(8,128)(2,1)S(1)}, u32[]{:S(2)}, u32[]{:S(2)}) %collective-permute-start.29) | collective-permute-done | bytes 262176 | tf_op jit(solution)/shard_map/ppermute | solution.py:351
  108.0 2.1 %place.1 = bf16[1024,2048]{1,0:T(8,128)(2,1)} custom-call(s32[1]{0:T(128)} %bitcast.me_ref, bf16[1024,128]{1,0:T(8,128)(2,1)S(1)} %merge_0.1.refs_0_, bf16[1024,128]{1,0:T(8,128)(2,1)S(1)} %collective-permute-done.14.refs_1_, bf16[1024,128]{1,0:T(8,128)(2,1)S(1)} %collective-permute-done.15.refs_2_, bf16[1024,128]{1,0:T(8,128)(2,1)S(1)} %collective-permute-done.16.refs_3_, ...), custom_call_target="tpu_custom_call" | custom-call | tf_op jit(solution)/shard_map/place/pallas_call | solution.py:330
  (79 shorter events, 31.8 us)
Async XLA Ops:
  2.3 7.5 %collective-permute-start = (bf16[2,256,128]{2,1,0:T(8,128)(2,1)}, bf16[2,256,128]{2,1,0:T(8,128)(2,1)S(1)}, u32[]{:S(2)}, u32[]{:S(2)}) collective-permute-start(bf16[2,256,128]{2,1,0:T(8,128)(2,1)} %get-tuple-element.54), channel_id=1, source_target_pairs={{0,2},{1,3},{2,0},{3,1},{4,6},{5,7},{6,4},{7,5},{8,10},{9,11},{10,... | collective-permute-start | bytes 393224 | tf_op jit(solution)/shard_map/ppermute | solution.py:351
  3.6 6.3 %collective-permute-start.1 = (bf16[2,256,128]{2,1,0:T(8,128)(2,1)}, bf16[2,256,128]{2,1,0:T(8,128)(2,1)S(1)}, u32[]{:S(2)}, u32[]{:S(2)}) collective-permute-start(bf16[2,256,128]{2,1,0:T(8,128)(2,1)} %get-tuple-element.55), channel_id=1, source_target_pairs={{0,4},{1,5},{2,6},{3,7},{4,0},{5,1},{6,2},{7,3},{8,12},{9,13},{10,... | collective-permute-start | bytes 393224 | tf_op jit(solution)/shard_map/ppermute | solution.py:351
  14.0 15.7 %collective-permute-start.9 = (bf16[8,2,128,128]{3,2,1,0:T(8,128)(2,1)S(1)}, bf16[8,2,128,128]{3,2,1,0:T(8,128)(2,1)S(1)}, u32[]{:S(2)}, u32[]{:S(2)}) collective-permute-start(bf16[8,2,128,128]{3,2,1,0:T(8,128)(2,1)S(1)} %bitcast.9), channel_id=1, source_target_pairs={{8,16},{16,8},{9,17},{17,9},{10,18},{18,10},{11,19},{19,11},{12,20... | collective-permute-start | bytes 1572872 | tf_op jit(solution)/shard_map/ppermute | solution.py:364
  17.3 12.9 %collective-permute-start.8 = (bf16[8,2,128,128]{3,2,1,0:T(8,128)(2,1)S(1)}, bf16[8,2,128,128]{3,2,1,0:T(8,128)(2,1)S(1)}, u32[]{:S(2)}, u32[]{:S(2)}) collective-permute-start(bf16[8,2,128,128]{3,2,1,0:T(8,128)(2,1)S(1)} %bitcast.10), channel_id=1, source_target_pairs={{0,8},{8,0},{16,24},{24,16},{1,9},{9,1},{17,25},{25,17},{2,10},{10... | collective-permute-start | bytes 1572872 | tf_op jit(solution)/shard_map/ppermute | solution.py:364
  22.7 7.0 %collective-permute-start.7 = (bf16[2,288,128]{2,1,0:T(8,128)(2,1)}, bf16[2,288,128]{2,1,0:T(8,128)(2,1)S(1)}, u32[]{:S(2)}, u32[]{:S(2)}) collective-permute-start(bf16[2,288,128]{2,1,0:T(8,128)(2,1)} %get-tuple-element.72), channel_id=1, source_target_pairs={{0,6},{1,7},{2,4},{3,5},{4,2},{5,3},{6,0},{7,1},{8,14},{9,15},{10,... | collective-permute-start | bytes 442376 | tf_op jit(solution)/shard_map/ppermute | solution.py:351
  32.8 9.9 %collective-permute-start.11 = (bf16[8,128,128]{2,1,0:T(8,128)(2,1)S(1)}, bf16[8,128,128]{2,1,0:T(8,128)(2,1)S(1)}, u32[]{:S(2)}, u32[]{:S(2)}) collective-permute-start(bf16[8,128,128]{2,1,0:T(8,128)(2,1)S(1)} %copy-done.1), channel_id=1, source_target_pairs={{0,8},{24,16},{1,9},{25,17},{2,10},{26,18},{3,11},{27,19},{4,12},{... | collective-permute-start | bytes 786440 | tf_op jit(solution)/shard_map/ppermute | solution.py:367
  34.1 18.7 %collective-permute-start.12 = (bf16[8,2,128,128]{3,2,1,0:T(8,128)(2,1)S(1)}, bf16[8,2,128,128]{3,2,1,0:T(8,128)(2,1)}, u32[]{:S(2)}, u32[]{:S(2)}) collective-permute-start(bf16[8,2,128,128]{3,2,1,0:T(8,128)(2,1)S(1)} %collective-permute-done.8.refs_2_), channel_id=1, source_target_pairs={{8,16},{16,8},{9,17},{17,9},{10,18},{18,10},{11,19},{19,11},{12,20... | collective-permute-start | bytes 1572872 | tf_op jit(solution)/shard_map/ppermute | solution.py:364
  42.7 15.8 %collective-permute-start.22 = (bf16[8,2,128,128]{3,2,1,0:T(8,128)(2,1)S(1)}, bf16[8,2,128,128]{3,2,1,0:T(8,128)(2,1)S(1)}, u32[]{:S(2)}, u32[]{:S(2)}) collective-permute-start(bf16[8,2,128,128]{3,2,1,0:T(8,128)(2,1)S(1)} %bitcast.6), channel_id=1, source_target_pairs={{0,8},{8,0},{16,24},{24,16},{1,9},{9,1},{17,25},{25,17},{2,10},{10... | collective-permute-start | bytes 1572872 | tf_op jit(solution)/shard_map/ppermute | solution.py:364
  42.7 18.1 %collective-permute-start.23 = (bf16[8,2,128,128]{3,2,1,0:T(8,128)(2,1)S(1)}, bf16[8,2,128,128]{3,2,1,0:T(8,128)(2,1)}, u32[]{:S(2)}, u32[]{:S(2)}) collective-permute-start(bf16[8,2,128,128]{3,2,1,0:T(8,128)(2,1)S(1)} %bitcast.7), channel_id=1, source_target_pairs={{8,16},{16,8},{9,17},{17,9},{10,18},{18,10},{11,19},{19,11},{12,20... | collective-permute-start | bytes 1572872 | tf_op jit(solution)/shard_map/ppermute | solution.py:364
  57.2 7.2 %collective-permute-start.13 = (bf16[8,144,128]{2,1,0:T(8,128)(2,1)}, bf16[8,144,128]{2,1,0:T(8,128)(2,1)S(1)}, u32[]{:S(2)}, u32[]{:S(2)}) collective-permute-start(bf16[8,144,128]{2,1,0:T(8,128)(2,1)} %get-tuple-element.88), channel_id=1, source_target_pairs={{8,0},{16,24},{9,1},{17,25},{10,2},{18,26},{11,3},{19,27},{12,4},{... | collective-permute-start | bytes 884744 | tf_op jit(solution)/shard_map/ppermute | solution.py:370
  60.9 16.2 %collective-permute-start.24 = (bf16[8,2,128,128]{3,2,1,0:T(8,128)(2,1)S(1)}, bf16[8,2,128,128]{3,2,1,0:T(8,128)(2,1)S(1)}, u32[]{:S(2)}, u32[]{:S(2)}) collective-permute-start(bf16[8,2,128,128]{3,2,1,0:T(8,128)(2,1)S(1)} %collective-permute-done.22.refs_2_), channel_id=1, source_target_pairs={{8,16},{16,8},{9,17},{17,9},{10,18},{18,10},{11,19},{19,11},{12,20... | collective-permute-start | bytes 1572872 | tf_op jit(solution)/shard_map/ppermute | solution.py:364
  63.0 8.6 %collective-permute-start.21 = (bf16[8,128,128]{2,1,0:T(8,128)(2,1)S(1)}, bf16[8,128,128]{2,1,0:T(8,128)(2,1)S(1)}, u32[]{:S(2)}, u32[]{:S(2)}) collective-permute-start(bf16[8,128,128]{2,1,0:T(8,128)(2,1)S(1)} %copy-done), channel_id=1, source_target_pairs={{0,8},{24,16},{1,9},{25,17},{2,10},{26,18},{3,11},{27,19},{4,12},{... | collective-permute-start | bytes 786440 | tf_op jit(solution)/shard_map/ppermute | solution.py:367
  64.6 15.3 %collective-permute-start.17 = (bf16[1024,128]{1,0:T(8,128)(2,1)S(1)}, bf16[1024,128]{1,0:T(8,128)(2,1)S(1)}, u32[]{:S(2)}, u32[]{:S(2)}) collective-permute-start(bf16[1024,128]{1,0:T(8,128)(2,1)S(1)} %merge_0.1.refs_0_), channel_id=1, source_target_pairs={{0,4},{1,5},{2,6},{3,7},{4,0},{5,1},{6,2},{7,3},{8,12},{9,13},{10,... | collective-permute-start | bytes 786440 | tf_op jit(solution)/shard_map/ppermute | solution.py:351
  65.9 14.0 %collective-permute-start.15 = (bf16[1024,128]{1,0:T(8,128)(2,1)S(1)}, bf16[1024,128]{1,0:T(8,128)(2,1)S(1)}, u32[]{:S(2)}, u32[]{:S(2)}) collective-permute-start(bf16[1024,128]{1,0:T(8,128)(2,1)S(1)} %merge_0.1.refs_0_), channel_id=1, source_target_pairs={{0,2},{1,3},{2,0},{3,1},{4,6},{5,7},{6,4},{7,5},{8,10},{9,11},{10,... | collective-permute-start | bytes 786440 | tf_op jit(solution)/shard_map/ppermute | solution.py:351
  79.9 11.0 %collective-permute-start.25 = (bf16[8,144,128]{2,1,0:T(8,128)(2,1)S(1)}, bf16[8,144,128]{2,1,0:T(8,128)(2,1)S(1)}, u32[]{:S(2)}, u32[]{:S(2)}) collective-permute-start(bf16[8,144,128]{2,1,0:T(8,128)(2,1)S(1)} %get-tuple-element.100), channel_id=1, source_target_pairs={{8,0},{16,24},{9,1},{17,25},{10,2},{18,26},{11,3},{19,27},{12,4},{... | collective-permute-start | bytes 884744 | tf_op jit(solution)/shard_map/ppermute | solution.py:370
  81.2 6.7 %collective-permute-start.19 = (bf16[1024,128]{1,0:T(8,128)(2,1)S(1)}, bf16[1024,128]{1,0:T(8,128)(2,1)S(1)}, u32[]{:S(2)}, u32[]{:S(2)}) collective-permute-start(bf16[1024,128]{1,0:T(8,128)(2,1)S(1)} %merge_0.1.refs_0_), channel_id=1, source_target_pairs={{0,6},{1,7},{2,4},{3,5},{4,2},{5,3},{6,0},{7,1},{8,14},{9,15},{10,... | collective-permute-start | bytes 786440 | tf_op jit(solution)/shard_map/ppermute | solution.py:351
  83.2 10.1 %collective-permute-start.14 = (bf16[1024,128]{1,0:T(8,128)(2,1)S(1)}, bf16[1024,128]{1,0:T(8,128)(2,1)S(1)}, u32[]{:S(2)}, u32[]{:S(2)}) collective-permute-start(bf16[1024,128]{1,0:T(8,128)(2,1)S(1)} %merge_0.1.refs_0_), channel_id=1, source_target_pairs={{0,1},{1,0},{2,3},{3,2},{4,5},{5,4},{6,7},{7,6},{8,9},{9,8},{10,11... | collective-permute-start | bytes 786440 | tf_op jit(solution)/shard_map/ppermute | solution.py:351
  85.5 9.2 %collective-permute-start.18 = (bf16[1024,128]{1,0:T(8,128)(2,1)S(1)}, bf16[1024,128]{1,0:T(8,128)(2,1)S(1)}, u32[]{:S(2)}, u32[]{:S(2)}) collective-permute-start(bf16[1024,128]{1,0:T(8,128)(2,1)S(1)} %collective-permute-done.17.refs_4_), channel_id=1, source_target_pairs={{0,1},{1,0},{2,3},{3,2},{4,5},{5,4},{6,7},{7,6},{8,9},{9,8},{10,11... | collective-permute-start | bytes 786440 | tf_op jit(solution)/shard_map/ppermute | solution.py:351
  91.1 8.9 %collective-permute-start.31 = (bf16[1024,128]{1,0:T(8,128)(2,1)S(1)}, bf16[1024,128]{1,0:T(8,128)(2,1)S(1)}, u32[]{:S(2)}, u32[]{:S(2)}) collective-permute-start(bf16[1024,128]{1,0:T(8,128)(2,1)S(1)} %merge_1.1.refs_8_), channel_id=1, source_target_pairs={{0,6},{1,7},{2,4},{3,5},{4,2},{5,3},{6,0},{7,1},{8,14},{9,15},{10,... | collective-permute-start | bytes 786440 | tf_op jit(solution)/shard_map/ppermute | solution.py:351
  93.1 12.9 %collective-permute-start.29 = (bf16[1024,128]{1,0:T(8,128)(2,1)S(1)}, bf16[1024,128]{1,0:T(8,128)(2,1)S(1)}, u32[]{:S(2)}, u32[]{:S(2)}) collective-permute-start(bf16[1024,128]{1,0:T(8,128)(2,1)S(1)} %merge_1.1.refs_8_), channel_id=1, source_target_pairs={{0,4},{1,5},{2,6},{3,7},{4,0},{5,1},{6,2},{7,3},{8,12},{9,13},{10,... | collective-permute-start | bytes 786440 | tf_op jit(solution)/shard_map/ppermute | solution.py:351
  93.3 13.1 %collective-permute-start.27 = (bf16[1024,128]{1,0:T(8,128)(2,1)S(1)}, bf16[1024,128]{1,0:T(8,128)(2,1)S(1)}, u32[]{:S(2)}, u32[]{:S(2)}) collective-permute-start(bf16[1024,128]{1,0:T(8,128)(2,1)S(1)} %merge_1.1.refs_8_), channel_id=1, source_target_pairs={{0,2},{1,3},{2,0},{3,1},{4,6},{5,7},{6,4},{7,5},{8,10},{9,11},{10,... | collective-permute-start | bytes 786440 | tf_op jit(solution)/shard_map/ppermute | solution.py:351
  93.9 12.7 %collective-permute-start.16 = (bf16[1024,128]{1,0:T(8,128)(2,1)S(1)}, bf16[1024,128]{1,0:T(8,128)(2,1)S(1)}, u32[]{:S(2)}, u32[]{:S(2)}) collective-permute-start(bf16[1024,128]{1,0:T(8,128)(2,1)S(1)} %collective-permute-done.15.refs_2_), channel_id=1, source_target_pairs={{0,1},{1,0},{2,3},{3,2},{4,5},{5,4},{6,7},{7,6},{8,9},{9,8},{10,11... | collective-permute-start | bytes 786440 | tf_op jit(solution)/shard_map/ppermute | solution.py:351
  94.7 11.8 %collective-permute-start.26 = (bf16[1024,128]{1,0:T(8,128)(2,1)S(1)}, bf16[1024,128]{1,0:T(8,128)(2,1)S(1)}, u32[]{:S(2)}, u32[]{:S(2)}) collective-permute-start(bf16[1024,128]{1,0:T(8,128)(2,1)S(1)} %merge_1.1.refs_8_), channel_id=1, source_target_pairs={{0,1},{1,0},{2,3},{3,2},{4,5},{5,4},{6,7},{7,6},{8,9},{9,8},{10,11... | collective-permute-start | bytes 786440 | tf_op jit(solution)/shard_map/ppermute | solution.py:351
  100.1 6.5 %collective-permute-start.32 = (bf16[1024,128]{1,0:T(8,128)(2,1)S(1)}, bf16[1024,128]{1,0:T(8,128)(2,1)S(1)}, u32[]{:S(2)}, u32[]{:S(2)}) collective-permute-start(bf16[1024,128]{1,0:T(8,128)(2,1)S(1)} %collective-permute-done.31.refs_14_), channel_id=1, source_target_pairs={{0,1},{1,0},{2,3},{3,2},{4,5},{5,4},{6,7},{7,6},{8,9},{9,8},{10,11... | collective-permute-start | bytes 786440 | tf_op jit(solution)/shard_map/ppermute | solution.py:351
  (14 other events, 133.2 us)

commit v17 on v16

--- a/solution.py
+++ b/solution.py
@@ -410,6 +410,10 @@
         elif found:
             steps.append(found)
     last = len(steps) - 1
+    late = relay and last == 1
+    if late:
+        (own_source, even_source, odd_source), far_sources = steps
+        steps += [(own_source, even_source), (odd_source,) + far_sources]
     lists = plan(pb1, masks, steps, n_pb, n_ka, key_blocks, rows, relay)
     state = [None] * heads
 
@@ -417,15 +421,20 @@
         kind = "keep" if step < last else "send" if relay else "last"
         sources = [x for x in sources if x is not None]
         name = f"attend_{c}_{step}"
-        return attend(lists[step], q[c], guest[c], sources, state[c], kind, 2 if relay else 1, name)
+        listed = lists[step + (2 if late and c else 0)]
+        seen = None if late and c and step == 0 else guest[c]
+        return attend(listed, q[c], seen, sources, state[c], kind, 2 if relay else 1, name)
 
     for step in range(last):
         for c in range(heads):
             sources = ([owns[c]] if step == 0 else []) + over[c]
             even, odd = over[c]
+            near = odd
             if even is not None and odd is not None:
                 even, odd = after((even, odd), (even, odd))
             over[c] = [exchange(odd, 0, step + 2), exchange(even, 1, step + 2)]
+            if late and c:
+                sources, over[c] = sources[:2], [near, over[c][1]]
             state[c] = run(c, step, sources)
 
     pieces = []
@@ -438,7 +447,7 @@
         else:
             out = found[0]
         mine = [out] + [swap(out, k) for k in range(2, n_ka, 2)]
-        sent = mine[: n_ka // 4 + 1]
+        sent = mine
         others = [swap(x, 1) for x in mine]
         pieces += [x for two in zip(mine, others) for x in two]
     return place(me1, pieces, n_ka, heads)

time: 111 us -> 116 us (1.045)
  the two profiles are of different devices: /device:TPU:9 before, /device:TPU:0 now
where the time goes in v17:
time: 116 us; the launch traced here: 115 us
  starting transfers between devices  46.2 us (40%)
  waiting for transfers between devices  41.1 us (35%)
  Pallas kernels  25.5 us (22%)
  local copies, waits for them, and re-layouts  1.37 us (1%)
    ppermute x22, waiting for transfers between devices, swap(): return lax.ppermute(x, 'ka', [(i, i ^ k) for i in range(n_ka)])  25.6 us
    ppermute x22, starting transfers between devices, swap(): return lax.ppermute(x, 'ka', [(i, i ^ k) for i in range(n_ka)])  16.6 us
    ppermute x3, starting transfers between devices, inward(): return lax.ppermute(x, 'pb', [(0, 1), (n_pb - 1, n_pb - 2)])  14.7 us
    ppermute x6, starting transfers between devices, exchange(): return lax.ppermute(x, 'pb', found) if found else None  12.3 us
    pallas_call x4, Pallas kernels, attend(): pl.pallas_call(functools.partial(attend_kernel, n_src, entry, first, mode...  11 us
    ppermute x2, waiting for transfers between devices, outward(): return lax.ppermute(x, 'pb', [(1, 0), (n_pb - 2, n_pb - 1)])  10.9 us
    pallas_call x2, Pallas kernels, pack(): pl.pallas_call(functools.partial(pack_kernel, n_ka, heads, c, len(masks))...  5.38 us
    ppermute x3, waiting for transfers between devices, inward(): return lax.ppermute(x, 'pb', [(0, 1), (n_pb - 1, n_pb - 2)])  4.61 us
  transfers between devices with their start and end apart: 33, of which 15 were waited for; matrix products, arithmetic and copies ran while one was open for 1% of the time, Pallas kernels for 18%

profile of v17, /device:TPU:0, one launch (start us, length us, event | category | flops | bytes accessed | tf_op | source)
XLA Modules:
  0.0 115.3 jit_solution(5785364834539351398)
XLA Ops:
  0.0 2.3 %pack_0.1 = (bf16[2,256,128]{2,1,0:T(8,128)(2,1)}, bf16[2,256,128]{2,1,0:T(8,128)(2,1)}, bf16[2,256,128]{2,1,0:T(8,128)(2,1)}, bf16[2,256,128]{2,1,0:T(8,128)(2,1)}) custom-call(s32[1]{0:T(128)} %bitcast.me_ref, bf16[128,2048]{1,0:T(8,128)(2,1)} %refs_2_.1, bf16[128,2048]{1,0:T(8,128)(2,1)} %refs_3_.1), custom_call_target="tpu_custom_call" | custom-call | bytes 262144 | tf_op jit(solution)/shard_map/pack_0/pallas_call | solution.py:77
  2.3 3.0 %collective-permute-start = (bf16[2,256,128]{2,1,0:T(8,128)(2,1)}, bf16[2,256,128]{2,1,0:T(8,128)(2,1)S(1)}, u32[]{:S(2)}, u32[]{:S(2)}) collective-permute-start(bf16[2,256,128]{2,1,0:T(8,128)(2,1)} %get-tuple-element.56), channel_id=1, source_target_pairs={{0,2},{1,3},{2,0},{3,1},{4,6},{5,7},{6,4},{7,5},{8,10},{9,11},{10,... | collective-permute-start | bytes 393224 | tf_op jit(solution)/shard_map/ppermute | solution.py:351
  6.9 3.9 %collective-permute-start.3 = (s32[4,8]{1,0:T(4,128)}, s32[4,8]{1,0:T(4,128)S(1)}, u32[]{:S(2)}, u32[]{:S(2)}) collective-permute-start(s32[4,8]{1,0:T(4,128)} %bitcast.12), channel_id=1, source_target_pairs={{0,8},{24,16},{1,9},{25,17},{2,10},{26,18},{3,11},{27,19},{4,12},{... | collective-permute-start | bytes 392 | tf_op jit(solution)/shard_map/ppermute | solution.py:367
  10.8 2.0 %turn.1 = (bf16[8,128,128]{2,1,0:T(8,128)(2,1)}, bf16[8,128,128]{2,1,0:T(8,128)(2,1)}) custom-call(s32[1]{0:T(128)} %bitcast.me_ref, bf16[1024,2048]{1,0:T(8,128)(2,1)} %q_all.1), custom_call_target="tpu_custom_call" | custom-call | bytes 131072 | tf_op jit(solution)/shard_map/turn/pallas_call | solution.py:105
  15.9 4.4 %collective-permute-start.8 = (bf16[8,2,128,128]{3,2,1,0:T(8,128)(2,1)S(1)}, bf16[8,2,128,128]{3,2,1,0:T(8,128)(2,1)}, u32[]{:S(2)}, u32[]{:S(2)}) collective-permute-start(bf16[8,2,128,128]{3,2,1,0:T(8,128)(2,1)S(1)} %bitcast.10), channel_id=1, source_target_pairs={{0,8},{8,0},{16,24},{24,16},{1,9},{9,1},{17,25},{25,17},{2,10},{10... | collective-permute-start | bytes 1572872 | tf_op jit(solution)/shard_map/ppermute | solution.py:364
  20.4 3.1 %pack_1.1 = (bf16[2,288,128]{2,1,0:T(8,128)(2,1)}, bf16[2,288,128]{2,1,0:T(8,128)(2,1)}, bf16[2,288,128]{2,1,0:T(8,128)(2,1)}, bf16[2,288,128]{2,1,0:T(8,128)(2,1)}) custom-call(s32[1]{0:T(128)} %bitcast.me_ref, s32[4,8]{1,0:T(4,128)} %bitcast.13, s32[4,8]{1,0:T(4,128)} %copy-done.4, bf16[128,2048]{1,0:T(8,128)(2,1)} %refs_2_.1, bf16[128,2048]{1,0:T(8,128)(2,1)} %refs_3_.1), custom_call_target="tpu_custom_call" | custom-call | bytes 262144 | tf_op jit(solution)/shard_map/pack_1/pallas_call | solution.py:77
  27.0 3.1 %collective-permute-done.5 = bf16[2,288,128]{2,1,0:T(8,128)(2,1)S(1)} collective-permute-done((bf16[2,288,128]{2,1,0:T(8,128)(2,1)}, bf16[2,288,128]{2,1,0:T(8,128)(2,1)S(1)}, u32[]{:S(2)}, u32[]{:S(2)}) %collective-permute-start.5) | collective-permute-done | bytes 147488 | tf_op jit(solution)/shard_map/ppermute | solution.py:351
  30.1 3.1 %collective-permute-done.6 = bf16[2,288,128]{2,1,0:T(8,128)(2,1)S(1)} collective-permute-done((bf16[2,288,128]{2,1,0:T(8,128)(2,1)}, bf16[2,288,128]{2,1,0:T(8,128)(2,1)S(1)}, u32[]{:S(2)}, u32[]{:S(2)}) %collective-permute-start.6) | collective-permute-done | bytes 147488 | tf_op jit(solution)/shard_map/ppermute | solution.py:351
  34.4 2.8 %collective-permute-start.11 = (bf16[8,128,128]{2,1,0:T(8,128)(2,1)S(1)}, bf16[8,128,128]{2,1,0:T(8,128)(2,1)S(1)}, u32[]{:S(2)}, u32[]{:S(2)}) collective-permute-start(bf16[8,128,128]{2,1,0:T(8,128)(2,1)S(1)} %copy-done.1), channel_id=1, source_target_pairs={{0,8},{24,16},{1,9},{25,17},{2,10},{26,18},{3,11},{27,19},{4,12},{... | collective-permute-start | bytes 786440 | tf_op jit(solution)/shard_map/ppermute | solution.py:367
  38.8 4.6 %collective-permute-done.11.refs_0_ = bf16[8,128,128]{2,1,0:T(8,128)(2,1)S(1)} collective-permute-done((bf16[8,128,128]{2,1,0:T(8,128)(2,1)S(1)}, bf16[8,128,128]{2,1,0:T(8,128)(2,1)S(1)}, u32[]{:S(2)}, u32[]{:S(2)}) %collective-permute-start.11) | collective-permute-done | bytes 262176 | tf_op jit(solution)/shard_map/ppermute | solution.py:367
  44.1 4.2 %collective-permute-start.23 = (bf16[8,2,128,128]{3,2,1,0:T(8,128)(2,1)S(1)}, bf16[8,2,128,128]{3,2,1,0:T(8,128)(2,1)S(1)}, u32[]{:S(2)}, u32[]{:S(2)}) collective-permute-start(bf16[8,2,128,128]{3,2,1,0:T(8,128)(2,1)S(1)} %bitcast.7), channel_id=1, source_target_pairs={{0,8},{8,0},{16,24},{24,16},{1,9},{9,1},{17,25},{25,17},{2,10},{10... | collective-permute-start | bytes 1572872 | tf_op jit(solution)/shard_map/ppermute | solution.py:364
  49.3 3.7 %plan.1 = (s32[4]{0:T(128)S(1)}, s32[432]{0:T(512)S(1)}, s32[176]{0:T(256)S(1)}, s32[304]{0:T(512)S(1)}, s32[304]{0:T(512)S(1)}) custom-call(s32[1]{0:T(128)} %bitcast.2.pb_ref, s32[256]{0:T(256)S(1)} %reshape.24.refs_0_, s32[256]{0:T(256)S(1)} %reshape.26.refs_1_), custom_call_target="tpu_custom_call" | custom-call | tf_op jit(solution)/shard_map/plan/pallas_call | solution.py:159
  52.9 4.3 %attend_0_0.1 = (f32[16,1,128]{2,1,0:T(1,128)S(1)}, f32[16,1,128]{2,1,0:T(1,128)S(1)}, f32[16,128,128]{2,1,0:T(8,128)S(1)}) custom-call(s32[4]{0:T(128)S(1)} %get-tuple-element.79.count_ref, s32[432]{0:T(512)S(1)} %get-tuple-element.83.live_ref, bf16[8,128,128]{2,1,0:T(8,128)(2,1)S(1)} %copy-done.1, ...), custom_call_target="tpu_custom_call" | custom-call | bytes 16384 | tf_op jit(solution)/shard_map/attend_0_0/pallas_call | solution.py:273
  57.2 2.4 %attend_0_1.1 = (f32[16,1,128]{2,1,0:T(1,128)S(1)}, f32[16,1,128]{2,1,0:T(1,128)S(1)}, f32[16,128,128]{2,1,0:T(8,128)S(1)}, bf16[8,144,128]{2,1,0:T(8,128)(2,1)}) custom-call(s32[4]{0:T(128)S(1)} %get-tuple-element.79.count_ref, s32[176]{0:T(256)S(1)} %get-tuple-element.80.live_ref, bf16[8,128,128]{2,1,0:T(8,128)(2,1)S(1)} %copy-done.1, ...), custom_call_target="tpu_custom_call" | custom-call | bytes 16384 | tf_op jit(solution)/shard_map/attend_0_1/pallas_call | solution.py:273
  61.7 8.0 %collective-permute-start.21 = (bf16[8,128,128]{2,1,0:T(8,128)(2,1)S(1)}, bf16[8,128,128]{2,1,0:T(8,128)(2,1)S(1)}, u32[]{:S(2)}, u32[]{:S(2)}) collective-permute-start(bf16[8,128,128]{2,1,0:T(8,128)(2,1)S(1)} %copy-done), channel_id=1, source_target_pairs={{0,8},{24,16},{1,9},{25,17},{2,10},{26,18},{3,11},{27,19},{4,12},{... | collective-permute-start | bytes 786440 | tf_op jit(solution)/shard_map/ppermute | solution.py:367
  69.7 2.1 %collective-permute-done.13.part_ref = bf16[8,144,128]{2,1,0:T(8,128)(2,1)} collective-permute-done((bf16[8,144,128]{2,1,0:T(8,128)(2,1)}, bf16[8,144,128]{2,1,0:T(8,128)(2,1)}, u32[]{:S(2)}, u32[]{:S(2)}) %collective-permute-start.13) | collective-permute-done | bytes 294944 | tf_op jit(solution)/shard_map/ppermute | solution.py:370
  72.9 2.2 %collective-permute-start.19 = (bf16[1024,128]{1,0:T(8,128)(2,1)S(1)}, bf16[1024,128]{1,0:T(8,128)(2,1)S(1)}, u32[]{:S(2)}, u32[]{:S(2)}) collective-permute-start(bf16[1024,128]{1,0:T(8,128)(2,1)S(1)} %merge_0.1.refs_0_), channel_id=1, source_target_pairs={{0,6},{1,7},{2,4},{3,5},{4,2},{5,3},{6,0},{7,1},{8,14},{9,15},{10,... | collective-permute-start | bytes 786440 | tf_op jit(solution)/shard_map/ppermute | solution.py:351
  76.5 3.4 %attend_1_0.1 = (f32[16,1,128]{2,1,0:T(1,128)S(1)}, f32[16,1,128]{2,1,0:T(1,128)S(1)}, f32[16,128,128]{2,1,0:T(8,128)S(1)}) custom-call(s32[4]{0:T(128)S(1)} %get-tuple-element.79.count_ref, s32[304]{0:T(512)S(1)} %get-tuple-element.96.live_ref, bf16[8,128,128]{2,1,0:T(8,128)(2,1)S(1)} %copy-done, bf16[8,2,128,128]{3,2,1,0:T(8,128)(2,1)S(1)} %bitcast.8, ...), custom_call_target="tpu_custom_call" | custom-call | bytes 16384 | tf_op jit(solution)/shard_map/attend_1_0/pallas_call | solution.py:273
  80.8 2.4 %collective-permute-done.19.refs_6_ = bf16[1024,128]{1,0:T(8,128)(2,1)S(1)} collective-permute-done((bf16[1024,128]{1,0:T(8,128)(2,1)S(1)}, bf16[1024,128]{1,0:T(8,128)(2,1)S(1)}, u32[]{:S(2)}, u32[]{:S(2)}) %collective-permute-start.19) | collective-permute-done | bytes 262176 | tf_op jit(solution)/shard_map/ppermute | solution.py:351
  83.2 3.5 %collective-permute-done.17.refs_4_ = bf16[1024,128]{1,0:T(8,128)(2,1)S(1)} collective-permute-done((bf16[1024,128]{1,0:T(8,128)(2,1)S(1)}, bf16[1024,128]{1,0:T(8,128)(2,1)S(1)}, u32[]{:S(2)}, u32[]{:S(2)}) %collective-permute-start.17) | collective-permute-done | bytes 262176 | tf_op jit(solution)/shard_map/ppermute | solution.py:351
  88.7 8.8 %collective-permute-done.25.part_ref = bf16[8,144,128]{2,1,0:T(8,128)(2,1)S(1)} collective-permute-done((bf16[8,144,128]{2,1,0:T(8,128)(2,1)S(1)}, bf16[8,144,128]{2,1,0:T(8,128)(2,1)S(1)}, u32[]{:S(2)}, u32[]{:S(2)}) %collective-permute-start.25) | collective-permute-done | bytes 294944 | tf_op jit(solution)/shard_map/ppermute | solution.py:370
  101.7 6.1 %collective-permute-done.31.refs_14_ = bf16[1024,128]{1,0:T(8,128)(2,1)S(1)} collective-permute-done((bf16[1024,128]{1,0:T(8,128)(2,1)S(1)}, bf16[1024,128]{1,0:T(8,128)(2,1)S(1)}, u32[]{:S(2)}, u32[]{:S(2)}) %collective-permute-start.31) | collective-permute-done | bytes 262176 | tf_op jit(solution)/shard_map/ppermute | solution.py:351
  107.9 3.4 %collective-permute-done.29.refs_12_ = bf16[1024,128]{1,0:T(8,128)(2,1)S(1)} collective-permute-done((bf16[1024,128]{1,0:T(8,128)(2,1)S(1)}, bf16[1024,128]{1,0:T(8,128)(2,1)S(1)}, u32[]{:S(2)}, u32[]{:S(2)}) %collective-permute-start.29) | collective-permute-done | bytes 262176 | tf_op jit(solution)/shard_map/ppermute | solution.py:351
  113.2 2.1 %place.1 = bf16[1024,2048]{1,0:T(8,128)(2,1)} custom-call(s32[1]{0:T(128)} %bitcast.me_ref, bf16[1024,128]{1,0:T(8,128)(2,1)S(1)} %merge_0.1.refs_0_, bf16[1024,128]{1,0:T(8,128)(2,1)S(1)} %collective-permute-done.14.refs_1_, bf16[1024,128]{1,0:T(8,128)(2,1)S(1)} %collective-permute-done.15.refs_2_, bf16[1024,128]{1,0:T(8,128)(2,1)S(1)} %collective-permute-done.16.refs_3_, ...), custom_call_target="tpu_custom_call" | custom-call | tf_op jit(solution)/shard_map/place/pallas_call | solution.py:330
  (79 shorter events, 26.1 us)
Async XLA Ops:
  2.3 10.5 %collective-permute-start = (bf16[2,256,128]{2,1,0:T(8,128)(2,1)}, bf16[2,256,128]{2,1,0:T(8,128)(2,1)S(1)}, u32[]{:S(2)}, u32[]{:S(2)}) collective-permute-start(bf16[2,256,128]{2,1,0:T(8,128)(2,1)} %get-tuple-element.56), channel_id=1, source_target_pairs={{0,2},{1,3},{2,0},{3,1},{4,6},{5,7},{6,4},{7,5},{8,10},{9,11},{10,... | collective-permute-start | bytes 393224 | tf_op jit(solution)/shard_map/ppermute | solution.py:351
  5.3 8.0 %collective-permute-start.1 = (bf16[2,256,128]{2,1,0:T(8,128)(2,1)}, bf16[2,256,128]{2,1,0:T(8,128)(2,1)S(1)}, u32[]{:S(2)}, u32[]{:S(2)}) collective-permute-start(bf16[2,256,128]{2,1,0:T(8,128)(2,1)} %get-tuple-element.57), channel_id=1, source_target_pairs={{0,4},{1,5},{2,6},{3,7},{4,0},{5,1},{6,2},{7,3},{8,12},{9,13},{10,... | collective-permute-start | bytes 393224 | tf_op jit(solution)/shard_map/ppermute | solution.py:351
  15.1 18.2 %collective-permute-start.9 = (bf16[8,2,128,128]{3,2,1,0:T(8,128)(2,1)S(1)}, bf16[8,2,128,128]{3,2,1,0:T(8,128)(2,1)S(1)}, u32[]{:S(2)}, u32[]{:S(2)}) collective-permute-start(bf16[8,2,128,128]{3,2,1,0:T(8,128)(2,1)S(1)} %bitcast.9), channel_id=1, source_target_pairs={{8,16},{16,8},{9,17},{17,9},{10,18},{18,10},{11,19},{19,11},{12,20... | collective-permute-start | bytes 1572872 | tf_op jit(solution)/shard_map/ppermute | solution.py:364
  15.9 17.3 %collective-permute-start.8 = (bf16[8,2,128,128]{3,2,1,0:T(8,128)(2,1)S(1)}, bf16[8,2,128,128]{3,2,1,0:T(8,128)(2,1)}, u32[]{:S(2)}, u32[]{:S(2)}) collective-permute-start(bf16[8,2,128,128]{3,2,1,0:T(8,128)(2,1)S(1)} %bitcast.10), channel_id=1, source_target_pairs={{0,8},{8,0},{16,24},{24,16},{1,9},{9,1},{17,25},{25,17},{2,10},{10... | collective-permute-start | bytes 1572872 | tf_op jit(solution)/shard_map/ppermute | solution.py:364
  24.7 8.5 %collective-permute-start.6 = (bf16[2,288,128]{2,1,0:T(8,128)(2,1)}, bf16[2,288,128]{2,1,0:T(8,128)(2,1)S(1)}, u32[]{:S(2)}, u32[]{:S(2)}) collective-permute-start(bf16[2,288,128]{2,1,0:T(8,128)(2,1)} %get-tuple-element.73), channel_id=1, source_target_pairs={{0,4},{1,5},{2,6},{3,7},{4,0},{5,1},{6,2},{7,3},{8,12},{9,13},{10,... | collective-permute-start | bytes 442376 | tf_op jit(solution)/shard_map/ppermute | solution.py:351
  34.4 9.0 %collective-permute-start.11 = (bf16[8,128,128]{2,1,0:T(8,128)(2,1)S(1)}, bf16[8,128,128]{2,1,0:T(8,128)(2,1)S(1)}, u32[]{:S(2)}, u32[]{:S(2)}) collective-permute-start(bf16[8,128,128]{2,1,0:T(8,128)(2,1)S(1)} %copy-done.1), channel_id=1, source_target_pairs={{0,8},{24,16},{1,9},{25,17},{2,10},{26,18},{3,11},{27,19},{4,12},{... | collective-permute-start | bytes 786440 | tf_op jit(solution)/shard_map/ppermute | solution.py:367
  37.2 20.0 %collective-permute-start.12 = (bf16[8,2,128,128]{3,2,1,0:T(8,128)(2,1)}, bf16[8,2,128,128]{3,2,1,0:T(8,128)(2,1)}, u32[]{:S(2)}, u32[]{:S(2)}) collective-permute-start(bf16[8,2,128,128]{3,2,1,0:T(8,128)(2,1)} %collective-permute-done.8.refs_2_), channel_id=1, source_target_pairs={{8,16},{16,8},{9,17},{17,9},{10,18},{18,10},{11,19},{19,11},{12,20... | collective-permute-start | bytes 1572872 | tf_op jit(solution)/shard_map/ppermute | solution.py:364
  43.4 17.5 %collective-permute-start.22 = (bf16[8,2,128,128]{3,2,1,0:T(8,128)(2,1)S(1)}, bf16[8,2,128,128]{3,2,1,0:T(8,128)(2,1)S(1)}, u32[]{:S(2)}, u32[]{:S(2)}) collective-permute-start(bf16[8,2,128,128]{3,2,1,0:T(8,128)(2,1)S(1)} %bitcast.6), channel_id=1, source_target_pairs={{8,16},{16,8},{9,17},{17,9},{10,18},{18,10},{11,19},{19,11},{12,20... | collective-permute-start | bytes 1572872 | tf_op jit(solution)/shard_map/ppermute | solution.py:364
  44.1 16.9 %collective-permute-start.23 = (bf16[8,2,128,128]{3,2,1,0:T(8,128)(2,1)S(1)}, bf16[8,2,128,128]{3,2,1,0:T(8,128)(2,1)S(1)}, u32[]{:S(2)}, u32[]{:S(2)}) collective-permute-start(bf16[8,2,128,128]{3,2,1,0:T(8,128)(2,1)S(1)} %bitcast.7), channel_id=1, source_target_pairs={{0,8},{8,0},{16,24},{24,16},{1,9},{9,1},{17,25},{25,17},{2,10},{10... | collective-permute-start | bytes 1572872 | tf_op jit(solution)/shard_map/ppermute | solution.py:364
  59.6 12.1 %collective-permute-start.13 = (bf16[8,144,128]{2,1,0:T(8,128)(2,1)}, bf16[8,144,128]{2,1,0:T(8,128)(2,1)}, u32[]{:S(2)}, u32[]{:S(2)}) collective-permute-start(bf16[8,144,128]{2,1,0:T(8,128)(2,1)} %get-tuple-element.90), channel_id=1, source_target_pairs={{8,0},{16,24},{9,1},{17,25},{10,2},{18,26},{11,3},{19,27},{12,4},{... | collective-permute-start | bytes 884744 | tf_op jit(solution)/shard_map/ppermute | solution.py:370
  61.0 18.9 %collective-permute-start.24 = (bf16[8,2,128,128]{3,2,1,0:T(8,128)(2,1)S(1)}, bf16[8,2,128,128]{3,2,1,0:T(8,128)(2,1)S(1)}, u32[]{:S(2)}, u32[]{:S(2)}) collective-permute-start(bf16[8,2,128,128]{3,2,1,0:T(8,128)(2,1)S(1)} %collective-permute-done.23.refs_1_), channel_id=1, source_target_pairs={{8,16},{16,8},{9,17},{17,9},{10,18},{18,10},{11,19},{19,11},{12,20... | collective-permute-start | bytes 1572872 | tf_op jit(solution)/shard_map/ppermute | solution.py:364
  61.7 18.1 %collective-permute-start.21 = (bf16[8,128,128]{2,1,0:T(8,128)(2,1)S(1)}, bf16[8,128,128]{2,1,0:T(8,128)(2,1)S(1)}, u32[]{:S(2)}, u32[]{:S(2)}) collective-permute-start(bf16[8,128,128]{2,1,0:T(8,128)(2,1)S(1)} %copy-done), channel_id=1, source_target_pairs={{0,8},{24,16},{1,9},{25,17},{2,10},{26,18},{3,11},{27,19},{4,12},{... | collective-permute-start | bytes 786440 | tf_op jit(solution)/shard_map/ppermute | solution.py:367
  72.9 10.3 %collective-permute-start.19 = (bf16[1024,128]{1,0:T(8,128)(2,1)S(1)}, bf16[1024,128]{1,0:T(8,128)(2,1)S(1)}, u32[]{:S(2)}, u32[]{:S(2)}) collective-permute-start(bf16[1024,128]{1,0:T(8,128)(2,1)S(1)} %merge_0.1.refs_0_), channel_id=1, source_target_pairs={{0,6},{1,7},{2,4},{3,5},{4,2},{5,3},{6,0},{7,1},{8,14},{9,15},{10,... | collective-permute-start | bytes 786440 | tf_op jit(solution)/shard_map/ppermute | solution.py:351
  75.1 11.5 %collective-permute-start.17 = (bf16[1024,128]{1,0:T(8,128)(2,1)S(1)}, bf16[1024,128]{1,0:T(8,128)(2,1)S(1)}, u32[]{:S(2)}, u32[]{:S(2)}) collective-permute-start(bf16[1024,128]{1,0:T(8,128)(2,1)S(1)} %merge_0.1.refs_0_), channel_id=1, source_target_pairs={{0,4},{1,5},{2,6},{3,7},{4,0},{5,1},{6,2},{7,3},{8,12},{9,13},{10,... | collective-permute-start | bytes 786440 | tf_op jit(solution)/shard_map/ppermute | solution.py:351
  75.7 11.1 %collective-permute-start.15 = (bf16[1024,128]{1,0:T(8,128)(2,1)S(1)}, bf16[1024,128]{1,0:T(8,128)(2,1)S(1)}, u32[]{:S(2)}, u32[]{:S(2)}) collective-permute-start(bf16[1024,128]{1,0:T(8,128)(2,1)S(1)} %merge_0.1.refs_0_), channel_id=1, source_target_pairs={{0,2},{1,3},{2,0},{3,1},{4,6},{5,7},{6,4},{7,5},{8,10},{9,11},{10,... | collective-permute-start | bytes 786440 | tf_op jit(solution)/shard_map/ppermute | solution.py:351
  86.7 10.7 %collective-permute-start.25 = (bf16[8,144,128]{2,1,0:T(8,128)(2,1)S(1)}, bf16[8,144,128]{2,1,0:T(8,128)(2,1)S(1)}, u32[]{:S(2)}, u32[]{:S(2)}) collective-permute-start(bf16[8,144,128]{2,1,0:T(8,128)(2,1)S(1)} %get-tuple-element.104), channel_id=1, source_target_pairs={{8,0},{16,24},{9,1},{17,25},{10,2},{18,26},{11,3},{19,27},{12,4},{... | collective-permute-start | bytes 884744 | tf_op jit(solution)/shard_map/ppermute | solution.py:370
  88.0 12.4 %collective-permute-start.14 = (bf16[1024,128]{1,0:T(8,128)(2,1)S(1)}, bf16[1024,128]{1,0:T(8,128)(2,1)S(1)}, u32[]{:S(2)}, u32[]{:S(2)}) collective-permute-start(bf16[1024,128]{1,0:T(8,128)(2,1)S(1)} %merge_0.1.refs_0_), channel_id=1, source_target_pairs={{0,1},{1,0},{2,3},{3,2},{4,5},{5,4},{6,7},{7,6},{8,9},{9,8},{10,11... | collective-permute-start | bytes 786440 | tf_op jit(solution)/shard_map/ppermute | solution.py:351
  88.1 13.1 %collective-permute-start.20 = (bf16[1024,128]{1,0:T(8,128)(2,1)S(1)}, bf16[1024,128]{1,0:T(8,128)(2,1)S(1)}, u32[]{:S(2)}, u32[]{:S(2)}) collective-permute-start(bf16[1024,128]{1,0:T(8,128)(2,1)S(1)} %collective-permute-done.19.refs_6_), channel_id=1, source_target_pairs={{0,1},{1,0},{2,3},{3,2},{4,5},{5,4},{6,7},{7,6},{8,9},{9,8},{10,11... | collective-permute-start | bytes 786440 | tf_op jit(solution)/shard_map/ppermute | solution.py:351
  88.6 12.6 %collective-permute-start.18 = (bf16[1024,128]{1,0:T(8,128)(2,1)S(1)}, bf16[1024,128]{1,0:T(8,128)(2,1)S(1)}, u32[]{:S(2)}, u32[]{:S(2)}) collective-permute-start(bf16[1024,128]{1,0:T(8,128)(2,1)S(1)} %collective-permute-done.17.refs_4_), channel_id=1, source_target_pairs={{0,1},{1,0},{2,3},{3,2},{4,5},{5,4},{6,7},{7,6},{8,9},{9,8},{10,11... | collective-permute-start | bytes 786440 | tf_op jit(solution)/shard_map/ppermute | solution.py:351
  97.6 10.2 %collective-permute-start.31 = (bf16[1024,128]{1,0:T(8,128)(2,1)S(1)}, bf16[1024,128]{1,0:T(8,128)(2,1)S(1)}, u32[]{:S(2)}, u32[]{:S(2)}) collective-permute-start(bf16[1024,128]{1,0:T(8,128)(2,1)S(1)} %merge_1.1.refs_8_), channel_id=1, source_target_pairs={{0,6},{1,7},{2,4},{3,5},{4,2},{5,3},{6,0},{7,1},{8,14},{9,15},{10,... | collective-permute-start | bytes 786440 | tf_op jit(solution)/shard_map/ppermute | solution.py:351
  99.0 12.3 %collective-permute-start.29 = (bf16[1024,128]{1,0:T(8,128)(2,1)S(1)}, bf16[1024,128]{1,0:T(8,128)(2,1)S(1)}, u32[]{:S(2)}, u32[]{:S(2)}) collective-permute-start(bf16[1024,128]{1,0:T(8,128)(2,1)S(1)} %merge_1.1.refs_8_), channel_id=1, source_target_pairs={{0,4},{1,5},{2,6},{3,7},{4,0},{5,1},{6,2},{7,3},{8,12},{9,13},{10,... | collective-permute-start | bytes 786440 | tf_op jit(solution)/shard_map/ppermute | solution.py:351
  100.4 11.3 %collective-permute-start.27 = (bf16[1024,128]{1,0:T(8,128)(2,1)S(1)}, bf16[1024,128]{1,0:T(8,128)(2,1)S(1)}, u32[]{:S(2)}, u32[]{:S(2)}) collective-permute-start(bf16[1024,128]{1,0:T(8,128)(2,1)S(1)} %merge_1.1.refs_8_), channel_id=1, source_target_pairs={{0,2},{1,3},{2,0},{3,1},{4,6},{5,7},{6,4},{7,5},{8,10},{9,11},{10,... | collective-permute-start | bytes 786440 | tf_op jit(solution)/shard_map/ppermute | solution.py:351
  101.2 10.6 %collective-permute-start.16 = (bf16[1024,128]{1,0:T(8,128)(2,1)S(1)}, bf16[1024,128]{1,0:T(8,128)(2,1)S(1)}, u32[]{:S(2)}, u32[]{:S(2)}) collective-permute-start(bf16[1024,128]{1,0:T(8,128)(2,1)S(1)} %collective-permute-done.15.refs_2_), channel_id=1, source_target_pairs={{0,1},{1,0},{2,3},{3,2},{4,5},{5,4},{6,7},{7,6},{8,9},{9,8},{10,11... | collective-permute-start | bytes 786440 | tf_op jit(solution)/shard_map/ppermute | solution.py:351
  101.2 10.6 %collective-permute-start.26 = (bf16[1024,128]{1,0:T(8,128)(2,1)S(1)}, bf16[1024,128]{1,0:T(8,128)(2,1)S(1)}, u32[]{:S(2)}, u32[]{:S(2)}) collective-permute-start(bf16[1024,128]{1,0:T(8,128)(2,1)S(1)} %merge_1.1.refs_8_), channel_id=1, source_target_pairs={{0,1},{1,0},{2,3},{3,2},{4,5},{5,4},{6,7},{7,6},{8,9},{9,8},{10,11... | collective-permute-start | bytes 786440 | tf_op jit(solution)/shard_map/ppermute | solution.py:351
  (14 other events, 130.5 us)

commit v18 on v13

--- a/solution.py
+++ b/solution.py
@@ -384,6 +384,14 @@
     def flags(x):
         return x[:, : block_mask.shape[1], :rows].astype(jnp.int32).reshape(-1)
 
+    steps = [((0, False),)]
+    for step in range(1, n_pb):
+        found = (((step, False),) if hops(0, step) else ()) + (((-step, True),) if hops(1, step) else ())
+        if step == 1:
+            steps[0] += found
+        elif found:
+            steps.append(found)
+    last = len(steps) - 1
     parts = (block_mask.T,) + ((inward(block_mask.T),) if relay else ())
     owns, over, guest = [], [], [None] * heads
     for c in range(heads):
@@ -395,22 +403,14 @@
         else:
             own, mixed = sort(after(packed, owns[0]), over[0])
         owns.append(blocks(own))
-        before = ((over[0], guest[0]), over[0]) if c else (None, None)
+        if c == heads - 1:
+            size = mask_rows(block_mask.shape[1])
+            masks = [flags(own[:, 2 * shard + i * size :]) for i in range(len(parts))]
+            lists = plan(pb1, masks, steps, n_pb, n_ka, key_blocks, rows, relay)
+        before = ((over[0], guest[0], lists[0][0] if c == heads - 1 else None), over[0]) if c else (None, None)
         over.append([exchange(after(owns[c], before[odd]), odd, 1) for odd in (0, 1)])
         if relay:
             guest[c] = inward(after(q[c], over[0]))
-    size = mask_rows(block_mask.shape[1])
-    masks = [flags(own[:, 2 * shard + i * size :]) for i in range(len(parts))]
-
-    steps = [((0, False),)]
-    for step in range(1, n_pb):
-        found = (((step, False),) if hops(0, step) else ()) + (((-step, True),) if hops(1, step) else ())
-        if step == 1:
-            steps[0] += found
-        elif found:
-            steps.append(found)
-    last = len(steps) - 1
-    lists = plan(pb1, masks, steps, n_pb, n_ka, key_blocks, rows, relay)
     state = [None] * heads
 
     def run(c, step, sources):

time: 106 us -> 109 us (1.028)
  local copies, waits for them, and re-layouts: 1.37 us -> 7.44 us
  waiting for transfers between devices: 40 us -> 37.7 us
    slice x8, local copies, waits for them, and re-layouts: 1.05 us -> 3.55 us  [sort(): theirs = swap(jnp.stack([y[1] for y in mixed]), 1)]
    ppermute x2, waiting for transfers between devices: 12 us -> 10.2 us  [outward(): return lax.ppermute(x, 'pb', [(1, 0), (n_pb - 2, n_pb - 1)])]
    unnamed x10 -> x12, local copies, waits for them, and re-layouts: 0.03 us -> 1.85 us
    ppermute x3, waiting for transfers between devices: 7.26 us -> 5.92 us  [inward(): return lax.ppermute(x, 'pb', [(0, 1), (n_pb - 1, n_pb - 2)])]
    ppermute x6, starting transfers between devices: 11.2 us -> 9.99 us  [exchange(): return lax.ppermute(x, 'pb', found) if found else None]
  transfers between devices with their start and end apart: 33 -> 33, of which waited for: 16 -> 14; matrix products, arithmetic and copies ran while one was open for 1% -> 3% of each run, Pallas kernels for 17% -> 17%
where the time goes in v18:
time: 109 us
  starting transfers between devices  39.8 us (37%)
  waiting for transfers between devices  37.7 us (35%)
  Pallas kernels  22.4 us (21%)
  local copies, waits for them, and re-layouts  7.44 us (7%)
    ppermute x22, waiting for transfers between devices, swap(): return lax.ppermute(x, 'ka', [(i, i ^ k) for i in range(n_ka)])  21.6 us
    ppermute x22, starting transfers between devices, swap(): return lax.ppermute(x, 'ka', [(i, i ^ k) for i in range(n_ka)])  16.9 us
    ppermute x3, starting transfers between devices, inward(): return lax.ppermute(x, 'pb', [(0, 1), (n_pb - 1, n_pb - 2)])  10.3 us
    pallas_call x4, Pallas kernels, attend(): pl.pallas_call(functools.partial(attend_kernel, n_src, entry, first, mode...  10.3 us
    ppermute x2, waiting for transfers between devices, outward(): return lax.ppermute(x, 'pb', [(1, 0), (n_pb - 2, n_pb - 1)])  10.2 us
    ppermute x6, starting transfers between devices, exchange(): return lax.ppermute(x, 'pb', found) if found else None  9.99 us
    ppermute x3, waiting for transfers between devices, inward(): return lax.ppermute(x, 'pb', [(0, 1), (n_pb - 1, n_pb - 2)])  5.92 us
    pallas_call x2, Pallas kernels, pack(): pl.pallas_call(functools.partial(pack_kernel, n_ka, heads, c, len(masks))...  5.3 us
  transfers between devices with their start and end apart: 33, of which 14 were waited for; matrix products, arithmetic and copies ran while one was open for 3% of the time, Pallas kernels for 17%

profile of v18, /device:TPU:0, one launch (start us, length us, event | category | flops | bytes accessed | tf_op | source)
XLA Modules:
  0.0 108.6 jit_solution(18357488924175790069)
XLA Ops:
  0.0 2.3 %pack_0.1 = (bf16[2,256,128]{2,1,0:T(8,128)(2,1)}, bf16[2,256,128]{2,1,0:T(8,128)(2,1)}, bf16[2,256,128]{2,1,0:T(8,128)(2,1)}, bf16[2,256,128]{2,1,0:T(8,128)(2,1)}) custom-call(s32[1]{0:T(128)} %bitcast.me_ref, bf16[128,2048]{1,0:T(8,128)(2,1)} %refs_2_.1, bf16[128,2048]{1,0:T(8,128)(2,1)} %refs_3_.1), custom_call_target="tpu_custom_call" | custom-call | bytes 262144 | tf_op jit(solution)/shard_map/pack_0/pallas_call | solution.py:77
  2.3 3.0 %collective-permute-start = (bf16[2,256,128]{2,1,0:T(8,128)(2,1)}, bf16[2,256,128]{2,1,0:T(8,128)(2,1)S(1)}, u32[]{:S(2)}, u32[]{:S(2)}) collective-permute-start(bf16[2,256,128]{2,1,0:T(8,128)(2,1)} %get-tuple-element.55), channel_id=1, source_target_pairs={{0,2},{1,3},{2,0},{3,1},{4,6},{5,7},{6,4},{7,5},{8,10},{9,11},{10,... | collective-permute-start | bytes 393224 | tf_op jit(solution)/shard_map/ppermute | solution.py:351
  6.8 3.9 %collective-permute-start.3 = (s32[4,8]{1,0:T(4,128)}, s32[4,8]{1,0:T(4,128)S(1)}, u32[]{:S(2)}, u32[]{:S(2)}) collective-permute-start(s32[4,8]{1,0:T(4,128)} %bitcast.12), channel_id=1, source_target_pairs={{0,8},{24,16},{1,9},{25,17},{2,10},{26,18},{3,11},{27,19},{4,12},{... | collective-permute-start | bytes 392 | tf_op jit(solution)/shard_map/ppermute | solution.py:367
  10.8 2.0 %turn.1 = (bf16[8,128,128]{2,1,0:T(8,128)(2,1)}, bf16[8,128,128]{2,1,0:T(8,128)(2,1)}) custom-call(s32[1]{0:T(128)} %bitcast.me_ref, bf16[1024,2048]{1,0:T(8,128)(2,1)} %q_all.1), custom_call_target="tpu_custom_call" | custom-call | bytes 131072 | tf_op jit(solution)/shard_map/turn/pallas_call | solution.py:105
  15.8 4.4 %collective-permute-start.8 = (bf16[8,2,128,128]{3,2,1,0:T(8,128)(2,1)S(1)}, bf16[8,2,128,128]{3,2,1,0:T(8,128)(2,1)S(1)}, u32[]{:S(2)}, u32[]{:S(2)}) collective-permute-start(bf16[8,2,128,128]{3,2,1,0:T(8,128)(2,1)S(1)} %bitcast.10), channel_id=1, source_target_pairs={{0,8},{8,0},{16,24},{24,16},{1,9},{9,1},{17,25},{25,17},{2,10},{10... | collective-permute-start | bytes 1572872 | tf_op jit(solution)/shard_map/ppermute | solution.py:364
  20.2 3.0 %pack_1.1 = (bf16[2,288,128]{2,1,0:T(8,128)(2,1)}, bf16[2,288,128]{2,1,0:T(8,128)(2,1)}, bf16[2,288,128]{2,1,0:T(8,128)(2,1)}, bf16[2,288,128]{2,1,0:T(8,128)(2,1)}) custom-call(s32[1]{0:T(128)} %bitcast.me_ref, s32[4,8]{1,0:T(4,128)} %bitcast.13, s32[4,8]{1,0:T(4,128)} %copy-done.5, bf16[128,2048]{1,0:T(8,128)(2,1)} %refs_2_.1, bf16[128,2048]{1,0:T(8,128)(2,1)} %refs_3_.1), custom_call_target="tpu_custom_call" | custom-call | bytes 262144 | tf_op jit(solution)/shard_map/pack_1/pallas_call | solution.py:77
  26.8 3.1 %collective-permute-done.5 = bf16[2,288,128]{2,1,0:T(8,128)(2,1)S(1)} collective-permute-done((bf16[2,288,128]{2,1,0:T(8,128)(2,1)}, bf16[2,288,128]{2,1,0:T(8,128)(2,1)S(1)}, u32[]{:S(2)}, u32[]{:S(2)}) %collective-permute-start.5) | collective-permute-done | bytes 147488 | tf_op jit(solution)/shard_map/ppermute | solution.py:351
  29.9 3.1 %collective-permute-done.6 = bf16[2,288,128]{2,1,0:T(8,128)(2,1)S(1)} collective-permute-done((bf16[2,288,128]{2,1,0:T(8,128)(2,1)}, bf16[2,288,128]{2,1,0:T(8,128)(2,1)S(1)}, u32[]{:S(2)}, u32[]{:S(2)}) %collective-permute-start.6) | collective-permute-done | bytes 147488 | tf_op jit(solution)/shard_map/ppermute | solution.py:351
  36.7 2.8 %collective-permute-start.11 = (bf16[8,128,128]{2,1,0:T(8,128)(2,1)S(1)}, bf16[8,128,128]{2,1,0:T(8,128)(2,1)S(1)}, u32[]{:S(2)}, u32[]{:S(2)}) collective-permute-start(bf16[8,128,128]{2,1,0:T(8,128)(2,1)S(1)} %copy-done.1), channel_id=1, source_target_pairs={{0,8},{24,16},{1,9},{25,17},{2,10},{26,18},{3,11},{27,19},{4,12},{... | collective-permute-start | bytes 786440 | tf_op jit(solution)/shard_map/ppermute | solution.py:367
  43.7 2.4 %plan.1 = (s32[2]{0:T(128)S(1)}, s32[432]{0:T(512)S(1)}, s32[176]{0:T(256)S(1)}) custom-call(s32[1]{0:T(128)} %bitcast.2.pb_ref, s32[256]{0:T(256)S(1)} %reshape.24.refs_0_, s32[256]{0:T(256)S(1)} %reshape.26.refs_1_), custom_call_target="tpu_custom_call" | custom-call | tf_op jit(solution)/shard_map/plan/pallas_call | solution.py:159
  46.1 2.0 %collective-permute-start.22 = (bf16[8,2,128,128]{3,2,1,0:T(8,128)(2,1)S(1)}, bf16[8,2,128,128]{3,2,1,0:T(8,128)(2,1)}, u32[]{:S(2)}, u32[]{:S(2)}) collective-permute-start(bf16[8,2,128,128]{3,2,1,0:T(8,128)(2,1)S(1)} %bitcast.6), channel_id=1, source_target_pairs={{0,8},{8,0},{16,24},{24,16},{1,9},{9,1},{17,25},{25,17},{2,10},{10... | collective-permute-start | bytes 1572872 | tf_op jit(solution)/shard_map/ppermute | solution.py:364
  48.8 3.6 %collective-permute-start.21 = (bf16[8,128,128]{2,1,0:T(8,128)(2,1)S(1)}, bf16[8,128,128]{2,1,0:T(8,128)(2,1)S(1)}, u32[]{:S(2)}, u32[]{:S(2)}) collective-permute-start(bf16[8,128,128]{2,1,0:T(8,128)(2,1)S(1)} %copy-done), channel_id=1, source_target_pairs={{0,8},{24,16},{1,9},{25,17},{2,10},{26,18},{3,11},{27,19},{4,12},{... | collective-permute-start | bytes 786440 | tf_op jit(solution)/shard_map/ppermute | solution.py:367
  52.5 3.4 %attend_0_0.1 = (f32[16,1,128]{2,1,0:T(1,128)S(1)}, f32[16,1,128]{2,1,0:T(1,128)S(1)}, f32[16,128,128]{2,1,0:T(8,128)S(1)}) custom-call(s32[2]{0:T(128)S(1)} %get-tuple-element.78.count_ref, s32[432]{0:T(512)S(1)} %get-tuple-element.82.live_ref, bf16[8,128,128]{2,1,0:T(8,128)(2,1)S(1)} %copy-done.1, ...), custom_call_target="tpu_custom_call" | custom-call | bytes 16384 | tf_op jit(solution)/shard_map/attend_0_0/pallas_call | solution.py:273
  55.9 1.7 %attend_0_1.1 = (f32[16,1,128]{2,1,0:T(1,128)S(1)}, f32[16,1,128]{2,1,0:T(1,128)S(1)}, f32[16,128,128]{2,1,0:T(8,128)S(1)}, bf16[8,144,128]{2,1,0:T(8,128)(2,1)S(1)}) custom-call(s32[2]{0:T(128)S(1)} %get-tuple-element.78.count_ref, s32[176]{0:T(256)S(1)} %get-tuple-element.79.live_ref, bf16[8,128,128]{2,1,0:T(8,128)(2,1)S(1)} %copy-done.1, ...), custom_call_target="tpu_custom_call" | custom-call | bytes 16384 | tf_op jit(solution)/shard_map/attend_0_1/pallas_call | solution.py:273
  58.9 5.9 %collective-permute-done.21.refs_0_ = bf16[8,128,128]{2,1,0:T(8,128)(2,1)S(1)} collective-permute-done((bf16[8,128,128]{2,1,0:T(8,128)(2,1)S(1)}, bf16[8,128,128]{2,1,0:T(8,128)(2,1)S(1)}, u32[]{:S(2)}, u32[]{:S(2)}) %collective-permute-start.21) | collective-permute-done | bytes 262176 | tf_op jit(solution)/shard_map/ppermute | solution.py:367
  68.0 1.6 %collective-permute-start.17 = (bf16[1024,128]{1,0:T(8,128)(2,1)S(1)}, bf16[1024,128]{1,0:T(8,128)(2,1)S(1)}, u32[]{:S(2)}, u32[]{:S(2)}) collective-permute-start(bf16[1024,128]{1,0:T(8,128)(2,1)S(1)} %merge_0.1.refs_0_), channel_id=1, source_target_pairs={{0,4},{1,5},{2,6},{3,7},{4,0},{5,1},{6,2},{7,3},{8,12},{9,13},{10,... | collective-permute-start | bytes 786440 | tf_op jit(solution)/shard_map/ppermute | solution.py:351
  72.6 4.3 %attend_1_0.1 = (f32[16,1,128]{2,1,0:T(1,128)S(1)}, f32[16,1,128]{2,1,0:T(1,128)S(1)}, f32[16,128,128]{2,1,0:T(8,128)S(1)}) custom-call(s32[2]{0:T(128)S(1)} %get-tuple-element.78.count_ref, s32[432]{0:T(512)S(1)} %get-tuple-element.82.live_ref, bf16[8,128,128]{2,1,0:T(8,128)(2,1)S(1)} %copy-done, bf16[8,128,128]{2,1,0:T(8,128)(2,1)S(1)} %collective-permute-done.21.refs_0_, ...), custom_call_target="tpu_custom_call" | custom-call | bytes 16384 | tf_op jit(solution)/shard_map/attend_1_0/pallas_call | solution.py:273
  76.9 1.9 %collective-permute-done.15.refs_2_ = bf16[1024,128]{1,0:T(8,128)(2,1)S(1)} collective-permute-done((bf16[1024,128]{1,0:T(8,128)(2,1)S(1)}, bf16[1024,128]{1,0:T(8,128)(2,1)S(1)}, u32[]{:S(2)}, u32[]{:S(2)}) %collective-permute-start.15) | collective-permute-done | bytes 262176 | tf_op jit(solution)/shard_map/ppermute | solution.py:351
  79.6 1.9 %collective-permute-done.19.refs_6_ = bf16[1024,128]{1,0:T(8,128)(2,1)S(1)} collective-permute-done((bf16[1024,128]{1,0:T(8,128)(2,1)S(1)}, bf16[1024,128]{1,0:T(8,128)(2,1)S(1)}, u32[]{:S(2)}, u32[]{:S(2)}) %collective-permute-start.19) | collective-permute-done | bytes 262176 | tf_op jit(solution)/shard_map/ppermute | solution.py:351
  83.4 8.8 %collective-permute-done.25.part_ref = bf16[8,144,128]{2,1,0:T(8,128)(2,1)S(1)} collective-permute-done((bf16[8,144,128]{2,1,0:T(8,128)(2,1)S(1)}, bf16[8,144,128]{2,1,0:T(8,128)(2,1)S(1)}, u32[]{:S(2)}, u32[]{:S(2)}) %collective-permute-start.25) | collective-permute-done | bytes 294944 | tf_op jit(solution)/shard_map/ppermute | solution.py:370
  92.4 2.2 %collective-permute-start.31 = (bf16[1024,128]{1,0:T(8,128)(2,1)S(1)}, bf16[1024,128]{1,0:T(8,128)(2,1)S(1)}, u32[]{:S(2)}, u32[]{:S(2)}) collective-permute-start(bf16[1024,128]{1,0:T(8,128)(2,1)S(1)} %merge_1.1.refs_8_), channel_id=1, source_target_pairs={{0,6},{1,7},{2,4},{3,5},{4,2},{5,3},{6,0},{7,1},{8,14},{9,15},{10,... | collective-permute-start | bytes 786440 | tf_op jit(solution)/shard_map/ppermute | solution.py:351
  96.5 5.4 %collective-permute-done.31.refs_14_ = bf16[1024,128]{1,0:T(8,128)(2,1)S(1)} collective-permute-done((bf16[1024,128]{1,0:T(8,128)(2,1)S(1)}, bf16[1024,128]{1,0:T(8,128)(2,1)S(1)}, u32[]{:S(2)}, u32[]{:S(2)}) %collective-permute-start.31) | collective-permute-done | bytes 262176 | tf_op jit(solution)/shard_map/ppermute | solution.py:351
  101.9 2.7 %collective-permute-done.29.refs_12_ = bf16[1024,128]{1,0:T(8,128)(2,1)S(1)} collective-permute-done((bf16[1024,128]{1,0:T(8,128)(2,1)S(1)}, bf16[1024,128]{1,0:T(8,128)(2,1)S(1)}, u32[]{:S(2)}, u32[]{:S(2)}) %collective-permute-start.29) | collective-permute-done | bytes 262176 | tf_op jit(solution)/shard_map/ppermute | solution.py:351
  106.5 2.1 %place.1 = bf16[1024,2048]{1,0:T(8,128)(2,1)} custom-call(s32[1]{0:T(128)} %bitcast.me_ref, bf16[1024,128]{1,0:T(8,128)(2,1)S(1)} %merge_0.1.refs_0_, bf16[1024,128]{1,0:T(8,128)(2,1)S(1)} %collective-permute-done.14.refs_1_, bf16[1024,128]{1,0:T(8,128)(2,1)S(1)} %collective-permute-done.15.refs_2_, bf16[1024,128]{1,0:T(8,128)(2,1)S(1)} %collective-permute-done.16.refs_3_, ...), custom_call_target="tpu_custom_call" | custom-call | tf_op jit(solution)/shard_map/place/pallas_call | solution.py:330
  (81 shorter events, 30.7 us)
Async XLA Ops:
  2.3 10.5 %collective-permute-start = (bf16[2,256,128]{2,1,0:T(8,128)(2,1)}, bf16[2,256,128]{2,1,0:T(8,128)(2,1)S(1)}, u32[]{:S(2)}, u32[]{:S(2)}) collective-permute-start(bf16[2,256,128]{2,1,0:T(8,128)(2,1)} %get-tuple-element.55), channel_id=1, source_target_pairs={{0,2},{1,3},{2,0},{3,1},{4,6},{5,7},{6,4},{7,5},{8,10},{9,11},{10,... | collective-permute-start | bytes 393224 | tf_op jit(solution)/shard_map/ppermute | solution.py:351
  5.3 8.0 %collective-permute-start.1 = (bf16[2,256,128]{2,1,0:T(8,128)(2,1)}, bf16[2,256,128]{2,1,0:T(8,128)(2,1)S(1)}, u32[]{:S(2)}, u32[]{:S(2)}) collective-permute-start(bf16[2,256,128]{2,1,0:T(8,128)(2,1)} %get-tuple-element.56), channel_id=1, source_target_pairs={{0,4},{1,5},{2,6},{3,7},{4,0},{5,1},{6,2},{7,3},{8,12},{9,13},{10,... | collective-permute-start | bytes 393224 | tf_op jit(solution)/shard_map/ppermute | solution.py:351
  15.1 18.0 %collective-permute-start.9 = (bf16[8,2,128,128]{3,2,1,0:T(8,128)(2,1)S(1)}, bf16[8,2,128,128]{3,2,1,0:T(8,128)(2,1)S(1)}, u32[]{:S(2)}, u32[]{:S(2)}) collective-permute-start(bf16[8,2,128,128]{3,2,1,0:T(8,128)(2,1)S(1)} %bitcast.9), channel_id=1, source_target_pairs={{8,16},{16,8},{9,17},{17,9},{10,18},{18,10},{11,19},{19,11},{12,20... | collective-permute-start | bytes 1572872 | tf_op jit(solution)/shard_map/ppermute | solution.py:364
  15.8 17.3 %collective-permute-start.8 = (bf16[8,2,128,128]{3,2,1,0:T(8,128)(2,1)S(1)}, bf16[8,2,128,128]{3,2,1,0:T(8,128)(2,1)S(1)}, u32[]{:S(2)}, u32[]{:S(2)}) collective-permute-start(bf16[8,2,128,128]{3,2,1,0:T(8,128)(2,1)S(1)} %bitcast.10), channel_id=1, source_target_pairs={{0,8},{8,0},{16,24},{24,16},{1,9},{9,1},{17,25},{25,17},{2,10},{10... | collective-permute-start | bytes 1572872 | tf_op jit(solution)/shard_map/ppermute | solution.py:364
  24.5 8.5 %collective-permute-start.6 = (bf16[2,288,128]{2,1,0:T(8,128)(2,1)}, bf16[2,288,128]{2,1,0:T(8,128)(2,1)S(1)}, u32[]{:S(2)}, u32[]{:S(2)}) collective-permute-start(bf16[2,288,128]{2,1,0:T(8,128)(2,1)} %get-tuple-element.72), channel_id=1, source_target_pairs={{0,4},{1,5},{2,6},{3,7},{4,0},{5,1},{6,2},{7,3},{8,12},{9,13},{10,... | collective-permute-start | bytes 442376 | tf_op jit(solution)/shard_map/ppermute | solution.py:351
  36.7 9.4 %collective-permute-start.11 = (bf16[8,128,128]{2,1,0:T(8,128)(2,1)S(1)}, bf16[8,128,128]{2,1,0:T(8,128)(2,1)S(1)}, u32[]{:S(2)}, u32[]{:S(2)}) collective-permute-start(bf16[8,128,128]{2,1,0:T(8,128)(2,1)S(1)} %copy-done.1), channel_id=1, source_target_pairs={{0,8},{24,16},{1,9},{25,17},{2,10},{26,18},{3,11},{27,19},{4,12},{... | collective-permute-start | bytes 786440 | tf_op jit(solution)/shard_map/ppermute | solution.py:367
  39.4 16.5 %collective-permute-start.12 = (bf16[8,2,128,128]{3,2,1,0:T(8,128)(2,1)S(1)}, bf16[8,2,128,128]{3,2,1,0:T(8,128)(2,1)}, u32[]{:S(2)}, u32[]{:S(2)}) collective-permute-start(bf16[8,2,128,128]{3,2,1,0:T(8,128)(2,1)S(1)} %collective-permute-done.8.refs_2_), channel_id=1, source_target_pairs={{8,16},{16,8},{9,17},{17,9},{10,18},{18,10},{11,19},{19,11},{12,20... | collective-permute-start | bytes 1572872 | tf_op jit(solution)/shard_map/ppermute | solution.py:364
  46.1 18.8 %collective-permute-start.22 = (bf16[8,2,128,128]{3,2,1,0:T(8,128)(2,1)S(1)}, bf16[8,2,128,128]{3,2,1,0:T(8,128)(2,1)}, u32[]{:S(2)}, u32[]{:S(2)}) collective-permute-start(bf16[8,2,128,128]{3,2,1,0:T(8,128)(2,1)S(1)} %bitcast.6), channel_id=1, source_target_pairs={{0,8},{8,0},{16,24},{24,16},{1,9},{9,1},{17,25},{25,17},{2,10},{10... | collective-permute-start | bytes 1572872 | tf_op jit(solution)/shard_map/ppermute | solution.py:364
  48.1 16.8 %collective-permute-start.23 = (bf16[8,2,128,128]{3,2,1,0:T(8,128)(2,1)S(1)}, bf16[8,2,128,128]{3,2,1,0:T(8,128)(2,1)S(1)}, u32[]{:S(2)}, u32[]{:S(2)}) collective-permute-start(bf16[8,2,128,128]{3,2,1,0:T(8,128)(2,1)S(1)} %bitcast.7), channel_id=1, source_target_pairs={{8,16},{16,8},{9,17},{17,9},{10,18},{18,10},{11,19},{19,11},{12,20... | collective-permute-start | bytes 1572872 | tf_op jit(solution)/shard_map/ppermute | solution.py:364
  48.8 16.1 %collective-permute-start.21 = (bf16[8,128,128]{2,1,0:T(8,128)(2,1)S(1)}, bf16[8,128,128]{2,1,0:T(8,128)(2,1)S(1)}, u32[]{:S(2)}, u32[]{:S(2)}) collective-permute-start(bf16[8,128,128]{2,1,0:T(8,128)(2,1)S(1)} %copy-done), channel_id=1, source_target_pairs={{0,8},{24,16},{1,9},{25,17},{2,10},{26,18},{3,11},{27,19},{4,12},{... | collective-permute-start | bytes 786440 | tf_op jit(solution)/shard_map/ppermute | solution.py:367
  57.6 10.2 %collective-permute-start.13 = (bf16[8,144,128]{2,1,0:T(8,128)(2,1)S(1)}, bf16[8,144,128]{2,1,0:T(8,128)(2,1)S(1)}, u32[]{:S(2)}, u32[]{:S(2)}) collective-permute-start(bf16[8,144,128]{2,1,0:T(8,128)(2,1)S(1)} %get-tuple-element.89), channel_id=1, source_target_pairs={{8,0},{16,24},{9,1},{17,25},{10,2},{18,26},{11,3},{19,27},{12,4},{... | collective-permute-start | bytes 884744 | tf_op jit(solution)/shard_map/ppermute | solution.py:370
  65.7 13.1 %collective-permute-start.24 = (bf16[8,2,128,128]{3,2,1,0:T(8,128)(2,1)}, bf16[8,2,128,128]{3,2,1,0:T(8,128)(2,1)S(1)}, u32[]{:S(2)}, u32[]{:S(2)}) collective-permute-start(bf16[8,2,128,128]{3,2,1,0:T(8,128)(2,1)} %collective-permute-done.22.refs_2_), channel_id=1, source_target_pairs={{8,16},{16,8},{9,17},{17,9},{10,18},{18,10},{11,19},{19,11},{12,20... | collective-permute-start | bytes 1572872 | tf_op jit(solution)/shard_map/ppermute | solution.py:364
  68.0 8.9 %collective-permute-start.17 = (bf16[1024,128]{1,0:T(8,128)(2,1)S(1)}, bf16[1024,128]{1,0:T(8,128)(2,1)S(1)}, u32[]{:S(2)}, u32[]{:S(2)}) collective-permute-start(bf16[1024,128]{1,0:T(8,128)(2,1)S(1)} %merge_0.1.refs_0_), channel_id=1, source_target_pairs={{0,4},{1,5},{2,6},{3,7},{4,0},{5,1},{6,2},{7,3},{8,12},{9,13},{10,... | collective-permute-start | bytes 786440 | tf_op jit(solution)/shard_map/ppermute | solution.py:351
  69.6 9.2 %collective-permute-start.15 = (bf16[1024,128]{1,0:T(8,128)(2,1)S(1)}, bf16[1024,128]{1,0:T(8,128)(2,1)S(1)}, u32[]{:S(2)}, u32[]{:S(2)}) collective-permute-start(bf16[1024,128]{1,0:T(8,128)(2,1)S(1)} %merge_0.1.refs_0_), channel_id=1, source_target_pairs={{0,2},{1,3},{2,0},{3,1},{4,6},{5,7},{6,4},{7,5},{8,10},{9,11},{10,... | collective-permute-start | bytes 786440 | tf_op jit(solution)/shard_map/ppermute | solution.py:351
  70.8 10.7 %collective-permute-start.19 = (bf16[1024,128]{1,0:T(8,128)(2,1)S(1)}, bf16[1024,128]{1,0:T(8,128)(2,1)S(1)}, u32[]{:S(2)}, u32[]{:S(2)}) collective-permute-start(bf16[1024,128]{1,0:T(8,128)(2,1)S(1)} %merge_0.1.refs_0_), channel_id=1, source_target_pairs={{0,6},{1,7},{2,4},{3,5},{4,2},{5,3},{6,0},{7,1},{8,14},{9,15},{10,... | collective-permute-start | bytes 786440 | tf_op jit(solution)/shard_map/ppermute | solution.py:351
  81.5 10.7 %collective-permute-start.25 = (bf16[8,144,128]{2,1,0:T(8,128)(2,1)S(1)}, bf16[8,144,128]{2,1,0:T(8,128)(2,1)S(1)}, u32[]{:S(2)}, u32[]{:S(2)}) collective-permute-start(bf16[8,144,128]{2,1,0:T(8,128)(2,1)S(1)} %get-tuple-element.102), channel_id=1, source_target_pairs={{8,0},{16,24},{9,1},{17,25},{10,2},{18,26},{11,3},{19,27},{12,4},{... | collective-permute-start | bytes 884744 | tf_op jit(solution)/shard_map/ppermute | solution.py:370
  82.8 12.4 %collective-permute-start.14 = (bf16[1024,128]{1,0:T(8,128)(2,1)S(1)}, bf16[1024,128]{1,0:T(8,128)(2,1)S(1)}, u32[]{:S(2)}, u32[]{:S(2)}) collective-permute-start(bf16[1024,128]{1,0:T(8,128)(2,1)S(1)} %merge_0.1.refs_0_), channel_id=1, source_target_pairs={{0,1},{1,0},{2,3},{3,2},{4,5},{5,4},{6,7},{7,6},{8,9},{9,8},{10,11... | collective-permute-start | bytes 786440 | tf_op jit(solution)/shard_map/ppermute | solution.py:351
  82.9 13.1 %collective-permute-start.20 = (bf16[1024,128]{1,0:T(8,128)(2,1)S(1)}, bf16[1024,128]{1,0:T(8,128)(2,1)S(1)}, u32[]{:S(2)}, u32[]{:S(2)}) collective-permute-start(bf16[1024,128]{1,0:T(8,128)(2,1)S(1)} %collective-permute-done.19.refs_6_), channel_id=1, source_target_pairs={{0,1},{1,0},{2,3},{3,2},{4,5},{5,4},{6,7},{7,6},{8,9},{9,8},{10,11... | collective-permute-start | bytes 786440 | tf_op jit(solution)/shard_map/ppermute | solution.py:351
  83.4 12.6 %collective-permute-start.18 = (bf16[1024,128]{1,0:T(8,128)(2,1)S(1)}, bf16[1024,128]{1,0:T(8,128)(2,1)S(1)}, u32[]{:S(2)}, u32[]{:S(2)}) collective-permute-start(bf16[1024,128]{1,0:T(8,128)(2,1)S(1)} %collective-permute-done.17.refs_4_), channel_id=1, source_target_pairs={{0,1},{1,0},{2,3},{3,2},{4,5},{5,4},{6,7},{7,6},{8,9},{9,8},{10,11... | collective-permute-start | bytes 786440 | tf_op jit(solution)/shard_map/ppermute | solution.py:351
  92.4 9.5 %collective-permute-start.31 = (bf16[1024,128]{1,0:T(8,128)(2,1)S(1)}, bf16[1024,128]{1,0:T(8,128)(2,1)S(1)}, u32[]{:S(2)}, u32[]{:S(2)}) collective-permute-start(bf16[1024,128]{1,0:T(8,128)(2,1)S(1)} %merge_1.1.refs_8_), channel_id=1, source_target_pairs={{0,6},{1,7},{2,4},{3,5},{4,2},{5,3},{6,0},{7,1},{8,14},{9,15},{10,... | collective-permute-start | bytes 786440 | tf_op jit(solution)/shard_map/ppermute | solution.py:351
  94.6 9.9 %collective-permute-start.29 = (bf16[1024,128]{1,0:T(8,128)(2,1)S(1)}, bf16[1024,128]{1,0:T(8,128)(2,1)S(1)}, u32[]{:S(2)}, u32[]{:S(2)}) collective-permute-start(bf16[1024,128]{1,0:T(8,128)(2,1)S(1)} %merge_1.1.refs_8_), channel_id=1, source_target_pairs={{0,4},{1,5},{2,6},{3,7},{4,0},{5,1},{6,2},{7,3},{8,12},{9,13},{10,... | collective-permute-start | bytes 786440 | tf_op jit(solution)/shard_map/ppermute | solution.py:351
  95.1 9.5 %collective-permute-start.27 = (bf16[1024,128]{1,0:T(8,128)(2,1)S(1)}, bf16[1024,128]{1,0:T(8,128)(2,1)S(1)}, u32[]{:S(2)}, u32[]{:S(2)}) collective-permute-start(bf16[1024,128]{1,0:T(8,128)(2,1)S(1)} %merge_1.1.refs_8_), channel_id=1, source_target_pairs={{0,2},{1,3},{2,0},{3,1},{4,6},{5,7},{6,4},{7,5},{8,10},{9,11},{10,... | collective-permute-start | bytes 786440 | tf_op jit(solution)/shard_map/ppermute | solution.py:351
  96.0 9.1 %collective-permute-start.16 = (bf16[1024,128]{1,0:T(8,128)(2,1)S(1)}, bf16[1024,128]{1,0:T(8,128)(2,1)S(1)}, u32[]{:S(2)}, u32[]{:S(2)}) collective-permute-start(bf16[1024,128]{1,0:T(8,128)(2,1)S(1)} %collective-permute-done.15.refs_2_), channel_id=1, source_target_pairs={{0,1},{1,0},{2,3},{3,2},{4,5},{5,4},{6,7},{7,6},{8,9},{9,8},{10,11... | collective-permute-start | bytes 786440 | tf_op jit(solution)/shard_map/ppermute | solution.py:351
  96.0 9.1 %collective-permute-start.26 = (bf16[1024,128]{1,0:T(8,128)(2,1)S(1)}, bf16[1024,128]{1,0:T(8,128)(2,1)S(1)}, u32[]{:S(2)}, u32[]{:S(2)}) collective-permute-start(bf16[1024,128]{1,0:T(8,128)(2,1)S(1)} %merge_1.1.refs_8_), channel_id=1, source_target_pairs={{0,1},{1,0},{2,3},{3,2},{4,5},{5,4},{6,7},{7,6},{8,9},{9,8},{10,11... | collective-permute-start | bytes 786440 | tf_op jit(solution)/shard_map/ppermute | solution.py:351
  (15 other events, 118.8 us)

commit v19 on v18

--- a/solution.py
+++ b/solution.py
@@ -371,12 +371,10 @@
 
     def sort(x, before=None):
         mixed = [y if i == 0 else swap(y, 2 * i) for i, y in enumerate(x)]
-        mixed = after(mixed, before)
-        theirs = swap(jnp.stack([y[1] for y in mixed]), 1)
-        return jnp.concatenate([jnp.stack([y[0] for y in mixed]), theirs]), mixed
-
-    def blocks(x):
-        return x[:, : 2 * shard].reshape(n_ka * key_blocks, 2, BLOCK, HEAD_DIM)
+        theirs = swap(after(jnp.stack([y[1] for y in mixed]), before), 1)
+        rows_of = lambda at: jnp.concatenate([jnp.stack([y[0, at] for y in mixed]), theirs[:, at]])
+        own = rows_of(slice(0, 2 * shard)).reshape(n_ka * key_blocks, 2, BLOCK, HEAD_DIM)
+        return own, rows_of(slice(2 * shard, None)), mixed
 
     def after(arrays, done):
         return arrays if done is None else lax.optimization_barrier((arrays, done))[0]
@@ -392,20 +390,22 @@
         elif found:
             steps.append(found)
     last = len(steps) - 1
-    parts = (block_mask.T,) + ((inward(block_mask.T),) if relay else ())
+    parts = (block_mask.T,) + ((inward(block_mask.T),) if relay and heads == 1 else ())
     owns, over, guest = [], [], [None] * heads
     for c in range(heads):
-        place_of = after(me1, (q, mixed)) if c else me1
+        place_of = after(me1, (q, owns[0])) if c else me1
         packed = pack(place_of, keys, values, parts if c == heads - 1 else (), n_ka, heads, c)
         if c == 0:
+            if relay and heads > 1:
+                parts += (inward(after(block_mask.T, packed)),)
             q = turn(after(me1, packed), queries, heads)
-            own, mixed = sort(packed, (q, parts))
+            own, marks, mixed = sort(packed, (q, parts))
         else:
-            own, mixed = sort(after(packed, owns[0]), over[0])
-        owns.append(blocks(own))
+            own, marks, mixed = sort(after(packed, owns[0]), over[0])
+        owns.append(own)
         if c == heads - 1:
             size = mask_rows(block_mask.shape[1])
-            masks = [flags(own[:, 2 * shard + i * size :]) for i in range(len(parts))]
+            masks = [flags(marks[:, i * size :]) for i in range(len(parts))]
             lists = plan(pb1, masks, steps, n_pb, n_ka, key_blocks, rows, relay)
         before = ((over[0], guest[0], lists[0][0] if c == heads - 1 else None), over[0]) if c else (None, None)
         over.append([exchange(after(owns[c], before[odd]), odd, 1) for odd in (0, 1)])

time: 109 us -> 107 us (0.982)
  local copies, waits for them, and re-layouts: 7.44 us -> 4.7 us
    slice x9 -> x8, local copies, waits for them, and re-layouts: 4.63 us -> 0.97 us  [sort(): theirs = swap(after(jnp.stack([y[1] for y in mixed]), before), 1)]
    unnamed x12 -> x20, local copies, waits for them, and re-layouts: 1.85 us -> 3.46 us
    ppermute x3, waiting for transfers between devices: 5.92 us -> 7.34 us  [inward(): return lax.ppermute(x, 'pb', [(0, 1), (n_pb - 1, n_pb - 2)])]
  transfers between devices with their start and end apart: 33 -> 33, of which waited for: 14 -> 15; matrix products, arithmetic and copies ran while one was open for 3% -> 3% of each run, Pallas kernels for 17% -> 18%
where the time goes in v19:
time: 107 us; the launch traced here: 106 us
  starting transfers between devices  39.7 us (37%)
  waiting for transfers between devices  38.3 us (36%)
  Pallas kernels  23.2 us (22%)
  local copies, waits for them, and re-layouts  4.7 us (4%)
    ppermute x22, waiting for transfers between devices, swap(): return lax.ppermute(x, 'ka', [(i, i ^ k) for i in range(n_ka)])  20.6 us
    ppermute x22, starting transfers between devices, swap(): return lax.ppermute(x, 'ka', [(i, i ^ k) for i in range(n_ka)])  16.9 us
    pallas_call x4, Pallas kernels, attend(): pl.pallas_call(functools.partial(attend_kernel, n_src, entry, first, mode...  11 us
    ppermute x6, starting transfers between devices, exchange(): return lax.ppermute(x, 'pb', found) if found else None  10.5 us
    ppermute x2, waiting for transfers between devices, outward(): return lax.ppermute(x, 'pb', [(1, 0), (n_pb - 2, n_pb - 1)])  10.3 us
    ppermute x3, starting transfers between devices, inward(): return lax.ppermute(x, 'pb', [(0, 1), (n_pb - 1, n_pb - 2)])  9.68 us
    ppermute x3, waiting for transfers between devices, inward(): return lax.ppermute(x, 'pb', [(0, 1), (n_pb - 1, n_pb - 2)])  7.34 us
    pallas_call x2, Pallas kernels, pack(): pl.pallas_call(functools.partial(pack_kernel, n_ka, heads, c, len(masks))...  5.34 us
  transfers between devices with their start and end apart: 33, of which 15 were waited for; matrix products, arithmetic and copies ran while one was open for 3% of the time, Pallas kernels for 18%

profile of v19, /device:TPU:0, one launch (start us, length us, event | category | flops | bytes accessed | tf_op | source)
XLA Modules:
  0.0 106.3 jit_solution(9902019483583175988)
XLA Ops:
  0.0 2.3 %pack_0.1 = (bf16[2,256,128]{2,1,0:T(8,128)(2,1)}, bf16[2,256,128]{2,1,0:T(8,128)(2,1)}, bf16[2,256,128]{2,1,0:T(8,128)(2,1)}, bf16[2,256,128]{2,1,0:T(8,128)(2,1)}) custom-call(s32[1]{0:T(128)} %bitcast.me_ref, bf16[128,2048]{1,0:T(8,128)(2,1)} %refs_2_.1, bf16[128,2048]{1,0:T(8,128)(2,1)} %refs_3_.1), custom_call_target="tpu_custom_call" | custom-call | bytes 262144 | tf_op jit(solution)/shard_map/pack_0/pallas_call | solution.py:77
  2.3 3.0 %collective-permute-start = (bf16[2,256,128]{2,1,0:T(8,128)(2,1)}, bf16[2,256,128]{2,1,0:T(8,128)(2,1)S(1)}, u32[]{:S(2)}, u32[]{:S(2)}) collective-permute-start(bf16[2,256,128]{2,1,0:T(8,128)(2,1)} %get-tuple-element.50), channel_id=1, source_target_pairs={{0,2},{1,3},{2,0},{3,1},{4,6},{5,7},{6,4},{7,5},{8,10},{9,11},{10,... | collective-permute-start | bytes 393224 | tf_op jit(solution)/shard_map/ppermute | solution.py:351
  6.9 3.9 %collective-permute-start.3 = (s32[4,8]{1,0:T(4,128)}, s32[4,8]{1,0:T(4,128)S(1)}, u32[]{:S(2)}, u32[]{:S(2)}) collective-permute-start(s32[4,8]{1,0:T(4,128)} %bitcast.12), channel_id=1, source_target_pairs={{0,8},{24,16},{1,9},{25,17},{2,10},{26,18},{3,11},{27,19},{4,12},{... | collective-permute-start | bytes 392 | tf_op jit(solution)/shard_map/ppermute | solution.py:367
  10.8 2.0 %turn.1 = (bf16[8,128,128]{2,1,0:T(8,128)(2,1)}, bf16[8,128,128]{2,1,0:T(8,128)(2,1)}) custom-call(s32[1]{0:T(128)} %bitcast.me_ref, bf16[1024,2048]{1,0:T(8,128)(2,1)} %q_all.1), custom_call_target="tpu_custom_call" | custom-call | bytes 131072 | tf_op jit(solution)/shard_map/turn/pallas_call | solution.py:105
  15.8 4.4 %collective-permute-start.8 = (bf16[8,2,128,128]{3,2,1,0:T(8,128)(2,1)S(1)}, bf16[8,2,128,128]{3,2,1,0:T(8,128)(2,1)S(1)}, u32[]{:S(2)}, u32[]{:S(2)}) collective-permute-start(bf16[8,2,128,128]{3,2,1,0:T(8,128)(2,1)S(1)} %bitcast.10), channel_id=1, source_target_pairs={{0,8},{8,0},{16,24},{24,16},{1,9},{9,1},{17,25},{25,17},{2,10},{10... | collective-permute-start | bytes 1572872 | tf_op jit(solution)/shard_map/ppermute | solution.py:364
  20.2 3.0 %pack_1.1 = (bf16[2,288,128]{2,1,0:T(8,128)(2,1)}, bf16[2,288,128]{2,1,0:T(8,128)(2,1)}, bf16[2,288,128]{2,1,0:T(8,128)(2,1)}, bf16[2,288,128]{2,1,0:T(8,128)(2,1)}) custom-call(s32[1]{0:T(128)} %bitcast.me_ref, s32[4,8]{1,0:T(4,128)} %bitcast.13, s32[4,8]{1,0:T(4,128)} %copy-done.5, bf16[128,2048]{1,0:T(8,128)(2,1)} %refs_2_.1, bf16[128,2048]{1,0:T(8,128)(2,1)} %refs_3_.1), custom_call_target="tpu_custom_call" | custom-call | bytes 262144 | tf_op jit(solution)/shard_map/pack_1/pallas_call | solution.py:77
  29.2 2.5 %collective-permute-done.5 = bf16[2,288,128]{2,1,0:T(8,128)(2,1)S(1)} collective-permute-done((bf16[2,288,128]{2,1,0:T(8,128)(2,1)}, bf16[2,288,128]{2,1,0:T(8,128)(2,1)S(1)}, u32[]{:S(2)}, u32[]{:S(2)}) %collective-permute-start.5) | collective-permute-done | bytes 147488 | tf_op jit(solution)/shard_map/ppermute | solution.py:351
  31.7 1.9 %collective-permute-done.6 = bf16[2,288,128]{2,1,0:T(8,128)(2,1)S(1)} collective-permute-done((bf16[2,288,128]{2,1,0:T(8,128)(2,1)}, bf16[2,288,128]{2,1,0:T(8,128)(2,1)S(1)}, u32[]{:S(2)}, u32[]{:S(2)}) %collective-permute-start.6) | collective-permute-done | bytes 147488 | tf_op jit(solution)/shard_map/ppermute | solution.py:351
  34.9 2.2 %collective-permute-start.11 = (bf16[8,128,128]{2,1,0:T(8,128)(2,1)S(1)}, bf16[8,128,128]{2,1,0:T(8,128)(2,1)S(1)}, u32[]{:S(2)}, u32[]{:S(2)}) collective-permute-start(bf16[8,128,128]{2,1,0:T(8,128)(2,1)S(1)} %copy-done.1), channel_id=1, source_target_pairs={{0,8},{24,16},{1,9},{25,17},{2,10},{26,18},{3,11},{27,19},{4,12},{... | collective-permute-start | bytes 786440 | tf_op jit(solution)/shard_map/ppermute | solution.py:367
  38.8 2.4 %plan.1 = (s32[2]{0:T(128)S(1)}, s32[432]{0:T(512)S(1)}, s32[176]{0:T(256)S(1)}) custom-call(s32[1]{0:T(128)} %bitcast.2.pb_ref, s32[256]{0:T(256)S(1)} %reshape.24.refs_0_, s32[256]{0:T(256)S(1)} %reshape.26.refs_1_), custom_call_target="tpu_custom_call" | custom-call | tf_op jit(solution)/shard_map/plan/pallas_call | solution.py:159
  41.2 2.0 %collective-permute-done.11.refs_0_ = bf16[8,128,128]{2,1,0:T(8,128)(2,1)S(1)} collective-permute-done((bf16[8,128,128]{2,1,0:T(8,128)(2,1)S(1)}, bf16[8,128,128]{2,1,0:T(8,128)(2,1)S(1)}, u32[]{:S(2)}, u32[]{:S(2)}) %collective-permute-start.11) | collective-permute-done | bytes 262176 | tf_op jit(solution)/shard_map/ppermute | solution.py:367
  43.3 2.5 %collective-permute-start.22 = (bf16[8,2,128,128]{3,2,1,0:T(8,128)(2,1)S(1)}, bf16[8,2,128,128]{3,2,1,0:T(8,128)(2,1)}, u32[]{:S(2)}, u32[]{:S(2)}) collective-permute-start(bf16[8,2,128,128]{3,2,1,0:T(8,128)(2,1)S(1)} %bitcast.6), channel_id=1, source_target_pairs={{0,8},{8,0},{16,24},{24,16},{1,9},{9,1},{17,25},{25,17},{2,10},{10... | collective-permute-start | bytes 1572872 | tf_op jit(solution)/shard_map/ppermute | solution.py:364
  46.5 3.6 %collective-permute-start.21 = (bf16[8,128,128]{2,1,0:T(8,128)(2,1)S(1)}, bf16[8,128,128]{2,1,0:T(8,128)(2,1)S(1)}, u32[]{:S(2)}, u32[]{:S(2)}) collective-permute-start(bf16[8,128,128]{2,1,0:T(8,128)(2,1)S(1)} %copy-done), channel_id=1, source_target_pairs={{0,8},{24,16},{1,9},{25,17},{2,10},{26,18},{3,11},{27,19},{4,12},{... | collective-permute-start | bytes 786440 | tf_op jit(solution)/shard_map/ppermute | solution.py:367
  50.1 3.4 %attend_0_0.1 = (f32[16,1,128]{2,1,0:T(1,128)S(1)}, f32[16,1,128]{2,1,0:T(1,128)S(1)}, f32[16,128,128]{2,1,0:T(8,128)S(1)}) custom-call(s32[2]{0:T(128)S(1)} %get-tuple-element.68.count_ref, s32[432]{0:T(512)S(1)} %get-tuple-element.72.live_ref, bf16[8,128,128]{2,1,0:T(8,128)(2,1)S(1)} %copy-done.1, ...), custom_call_target="tpu_custom_call" | custom-call | bytes 16384 | tf_op jit(solution)/shard_map/attend_0_0/pallas_call | solution.py:273
  53.5 2.4 %attend_0_1.1 = (f32[16,1,128]{2,1,0:T(1,128)S(1)}, f32[16,1,128]{2,1,0:T(1,128)S(1)}, f32[16,128,128]{2,1,0:T(8,128)S(1)}, bf16[8,144,128]{2,1,0:T(8,128)(2,1)}) custom-call(s32[2]{0:T(128)S(1)} %get-tuple-element.68.count_ref, s32[176]{0:T(256)S(1)} %get-tuple-element.69.live_ref, bf16[8,128,128]{2,1,0:T(8,128)(2,1)S(1)} %copy-done.1, ...), custom_call_target="tpu_custom_call" | custom-call | bytes 16384 | tf_op jit(solution)/shard_map/attend_0_1/pallas_call | solution.py:273
  57.2 5.3 %collective-permute-done.21.refs_0_ = bf16[8,128,128]{2,1,0:T(8,128)(2,1)S(1)} collective-permute-done((bf16[8,128,128]{2,1,0:T(8,128)(2,1)S(1)}, bf16[8,128,128]{2,1,0:T(8,128)(2,1)S(1)}, u32[]{:S(2)}, u32[]{:S(2)}) %collective-permute-start.21) | collective-permute-done | bytes 262176 | tf_op jit(solution)/shard_map/ppermute | solution.py:367
  64.0 2.2 %collective-permute-done.13.part_ref = bf16[8,144,128]{2,1,0:T(8,128)(2,1)S(1)} collective-permute-done((bf16[8,144,128]{2,1,0:T(8,128)(2,1)}, bf16[8,144,128]{2,1,0:T(8,128)(2,1)S(1)}, u32[]{:S(2)}, u32[]{:S(2)}) %collective-permute-start.13) | collective-permute-done | bytes 294944 | tf_op jit(solution)/shard_map/ppermute | solution.py:370
  71.0 4.3 %attend_1_0.1 = (f32[16,1,128]{2,1,0:T(1,128)S(1)}, f32[16,1,128]{2,1,0:T(1,128)S(1)}, f32[16,128,128]{2,1,0:T(8,128)S(1)}) custom-call(s32[2]{0:T(128)S(1)} %get-tuple-element.68.count_ref, s32[432]{0:T(512)S(1)} %get-tuple-element.72.live_ref, bf16[8,128,128]{2,1,0:T(8,128)(2,1)S(1)} %copy-done, bf16[8,128,128]{2,1,0:T(8,128)(2,1)S(1)} %collective-permute-done.21.refs_0_, ...), custom_call_target="tpu_custom_call" | custom-call | bytes 16384 | tf_op jit(solution)/shard_map/attend_1_0/pallas_call | solution.py:273
  77.7 2.1 %collective-permute-done.19.refs_6_ = bf16[1024,128]{1,0:T(8,128)(2,1)S(1)} collective-permute-done((bf16[1024,128]{1,0:T(8,128)(2,1)S(1)}, bf16[1024,128]{1,0:T(8,128)(2,1)S(1)}, u32[]{:S(2)}, u32[]{:S(2)}) %collective-permute-start.19) | collective-permute-done | bytes 262176 | tf_op jit(solution)/shard_map/ppermute | solution.py:351
  81.7 8.2 %collective-permute-done.25.part_ref = bf16[8,144,128]{2,1,0:T(8,128)(2,1)S(1)} collective-permute-done((bf16[8,144,128]{2,1,0:T(8,128)(2,1)S(1)}, bf16[8,144,128]{2,1,0:T(8,128)(2,1)S(1)}, u32[]{:S(2)}, u32[]{:S(2)}) %collective-permute-start.25) | collective-permute-done | bytes 294944 | tf_op jit(solution)/shard_map/ppermute | solution.py:370
  90.1 1.8 %collective-permute-start.31 = (bf16[1024,128]{1,0:T(8,128)(2,1)S(1)}, bf16[1024,128]{1,0:T(8,128)(2,1)S(1)}, u32[]{:S(2)}, u32[]{:S(2)}) collective-permute-start(bf16[1024,128]{1,0:T(8,128)(2,1)S(1)} %merge_1.1.refs_8_), channel_id=1, source_target_pairs={{0,6},{1,7},{2,4},{3,5},{4,2},{5,3},{6,0},{7,1},{8,14},{9,15},{10,... | collective-permute-start | bytes 786440 | tf_op jit(solution)/shard_map/ppermute | solution.py:351
  94.2 5.4 %collective-permute-done.31.refs_14_ = bf16[1024,128]{1,0:T(8,128)(2,1)S(1)} collective-permute-done((bf16[1024,128]{1,0:T(8,128)(2,1)S(1)}, bf16[1024,128]{1,0:T(8,128)(2,1)S(1)}, u32[]{:S(2)}, u32[]{:S(2)}) %collective-permute-start.31) | collective-permute-done | bytes 262176 | tf_op jit(solution)/shard_map/ppermute | solution.py:351
  99.6 2.7 %collective-permute-done.29.refs_12_ = bf16[1024,128]{1,0:T(8,128)(2,1)S(1)} collective-permute-done((bf16[1024,128]{1,0:T(8,128)(2,1)S(1)}, bf16[1024,128]{1,0:T(8,128)(2,1)S(1)}, u32[]{:S(2)}, u32[]{:S(2)}) %collective-permute-start.29) | collective-permute-done | bytes 262176 | tf_op jit(solution)/shard_map/ppermute | solution.py:351
  104.2 2.1 %place.1 = bf16[1024,2048]{1,0:T(8,128)(2,1)} custom-call(s32[1]{0:T(128)} %bitcast.me_ref, bf16[1024,128]{1,0:T(8,128)(2,1)S(1)} %merge_0.1.refs_0_, bf16[1024,128]{1,0:T(8,128)(2,1)S(1)} %collective-permute-done.14.refs_1_, bf16[1024,128]{1,0:T(8,128)(2,1)S(1)} %collective-permute-done.15.refs_2_, bf16[1024,128]{1,0:T(8,128)(2,1)S(1)} %collective-permute-done.16.refs_3_, ...), custom_call_target="tpu_custom_call" | custom-call | tf_op jit(solution)/shard_map/place/pallas_call | solution.py:330
  (89 shorter events, 30.4 us)
Async XLA Ops:
  2.3 10.5 %collective-permute-start = (bf16[2,256,128]{2,1,0:T(8,128)(2,1)}, bf16[2,256,128]{2,1,0:T(8,128)(2,1)S(1)}, u32[]{:S(2)}, u32[]{:S(2)}) collective-permute-start(bf16[2,256,128]{2,1,0:T(8,128)(2,1)} %get-tuple-element.50), channel_id=1, source_target_pairs={{0,2},{1,3},{2,0},{3,1},{4,6},{5,7},{6,4},{7,5},{8,10},{9,11},{10,... | collective-permute-start | bytes 393224 | tf_op jit(solution)/shard_map/ppermute | solution.py:351
  5.3 8.0 %collective-permute-start.1 = (bf16[2,256,128]{2,1,0:T(8,128)(2,1)}, bf16[2,256,128]{2,1,0:T(8,128)(2,1)S(1)}, u32[]{:S(2)}, u32[]{:S(2)}) collective-permute-start(bf16[2,256,128]{2,1,0:T(8,128)(2,1)} %get-tuple-element.51), channel_id=1, source_target_pairs={{0,4},{1,5},{2,6},{3,7},{4,0},{5,1},{6,2},{7,3},{8,12},{9,13},{10,... | collective-permute-start | bytes 393224 | tf_op jit(solution)/shard_map/ppermute | solution.py:351
  15.1 19.7 %collective-permute-start.9 = (bf16[8,2,128,128]{3,2,1,0:T(8,128)(2,1)S(1)}, bf16[8,2,128,128]{3,2,1,0:T(8,128)(2,1)S(1)}, u32[]{:S(2)}, u32[]{:S(2)}) collective-permute-start(bf16[8,2,128,128]{3,2,1,0:T(8,128)(2,1)S(1)} %bitcast.9), channel_id=1, source_target_pairs={{8,16},{16,8},{9,17},{17,9},{10,18},{18,10},{11,19},{19,11},{12,20... | collective-permute-start | bytes 1572872 | tf_op jit(solution)/shard_map/ppermute | solution.py:364
  15.8 19.0 %collective-permute-start.8 = (bf16[8,2,128,128]{3,2,1,0:T(8,128)(2,1)S(1)}, bf16[8,2,128,128]{3,2,1,0:T(8,128)(2,1)S(1)}, u32[]{:S(2)}, u32[]{:S(2)}) collective-permute-start(bf16[8,2,128,128]{3,2,1,0:T(8,128)(2,1)S(1)} %bitcast.10), channel_id=1, source_target_pairs={{0,8},{8,0},{16,24},{24,16},{1,9},{9,1},{17,25},{25,17},{2,10},{10... | collective-permute-start | bytes 1572872 | tf_op jit(solution)/shard_map/ppermute | solution.py:364
  26.2 7.4 %collective-permute-start.6 = (bf16[2,288,128]{2,1,0:T(8,128)(2,1)}, bf16[2,288,128]{2,1,0:T(8,128)(2,1)S(1)}, u32[]{:S(2)}, u32[]{:S(2)}) collective-permute-start(bf16[2,288,128]{2,1,0:T(8,128)(2,1)} %get-tuple-element.65), channel_id=1, source_target_pairs={{0,4},{1,5},{2,6},{3,7},{4,0},{5,1},{6,2},{7,3},{8,12},{9,13},{10,... | collective-permute-start | bytes 442376 | tf_op jit(solution)/shard_map/ppermute | solution.py:351
  34.9 8.4 %collective-permute-start.11 = (bf16[8,128,128]{2,1,0:T(8,128)(2,1)S(1)}, bf16[8,128,128]{2,1,0:T(8,128)(2,1)S(1)}, u32[]{:S(2)}, u32[]{:S(2)}) collective-permute-start(bf16[8,128,128]{2,1,0:T(8,128)(2,1)S(1)} %copy-done.1), channel_id=1, source_target_pairs={{0,8},{24,16},{1,9},{25,17},{2,10},{26,18},{3,11},{27,19},{4,12},{... | collective-permute-start | bytes 786440 | tf_op jit(solution)/shard_map/ppermute | solution.py:367
  37.1 16.4 %collective-permute-start.12 = (bf16[8,2,128,128]{3,2,1,0:T(8,128)(2,1)S(1)}, bf16[8,2,128,128]{3,2,1,0:T(8,128)(2,1)}, u32[]{:S(2)}, u32[]{:S(2)}) collective-permute-start(bf16[8,2,128,128]{3,2,1,0:T(8,128)(2,1)S(1)} %collective-permute-done.8.refs_2_), channel_id=1, source_target_pairs={{8,16},{16,8},{9,17},{17,9},{10,18},{18,10},{11,19},{19,11},{12,20... | collective-permute-start | bytes 1572872 | tf_op jit(solution)/shard_map/ppermute | solution.py:364
  43.3 19.3 %collective-permute-start.22 = (bf16[8,2,128,128]{3,2,1,0:T(8,128)(2,1)S(1)}, bf16[8,2,128,128]{3,2,1,0:T(8,128)(2,1)}, u32[]{:S(2)}, u32[]{:S(2)}) collective-permute-start(bf16[8,2,128,128]{3,2,1,0:T(8,128)(2,1)S(1)} %bitcast.6), channel_id=1, source_target_pairs={{0,8},{8,0},{16,24},{24,16},{1,9},{9,1},{17,25},{25,17},{2,10},{10... | collective-permute-start | bytes 1572872 | tf_op jit(solution)/shard_map/ppermute | solution.py:364
  45.8 16.8 %collective-permute-start.23 = (bf16[8,2,128,128]{3,2,1,0:T(8,128)(2,1)S(1)}, bf16[8,2,128,128]{3,2,1,0:T(8,128)(2,1)S(1)}, u32[]{:S(2)}, u32[]{:S(2)}) collective-permute-start(bf16[8,2,128,128]{3,2,1,0:T(8,128)(2,1)S(1)} %bitcast.7), channel_id=1, source_target_pairs={{8,16},{16,8},{9,17},{17,9},{10,18},{18,10},{11,19},{19,11},{12,20... | collective-permute-start | bytes 1572872 | tf_op jit(solution)/shard_map/ppermute | solution.py:364
  46.5 16.1 %collective-permute-start.21 = (bf16[8,128,128]{2,1,0:T(8,128)(2,1)S(1)}, bf16[8,128,128]{2,1,0:T(8,128)(2,1)S(1)}, u32[]{:S(2)}, u32[]{:S(2)}) collective-permute-start(bf16[8,128,128]{2,1,0:T(8,128)(2,1)S(1)} %copy-done), channel_id=1, source_target_pairs={{0,8},{24,16},{1,9},{25,17},{2,10},{26,18},{3,11},{27,19},{4,12},{... | collective-permute-start | bytes 786440 | tf_op jit(solution)/shard_map/ppermute | solution.py:367
  55.9 10.3 %collective-permute-start.13 = (bf16[8,144,128]{2,1,0:T(8,128)(2,1)}, bf16[8,144,128]{2,1,0:T(8,128)(2,1)S(1)}, u32[]{:S(2)}, u32[]{:S(2)}) collective-permute-start(bf16[8,144,128]{2,1,0:T(8,128)(2,1)} %get-tuple-element.79), channel_id=1, source_target_pairs={{8,0},{16,24},{9,1},{17,25},{10,2},{18,26},{11,3},{19,27},{12,4},{... | collective-permute-start | bytes 884744 | tf_op jit(solution)/shard_map/ppermute | solution.py:370
  63.3 13.5 %collective-permute-start.24 = (bf16[8,2,128,128]{3,2,1,0:T(8,128)(2,1)}, bf16[8,2,128,128]{3,2,1,0:T(8,128)(2,1)S(1)}, u32[]{:S(2)}, u32[]{:S(2)}) collective-permute-start(bf16[8,2,128,128]{3,2,1,0:T(8,128)(2,1)} %collective-permute-done.22.refs_2_), channel_id=1, source_target_pairs={{8,16},{16,8},{9,17},{17,9},{10,18},{18,10},{11,19},{19,11},{12,20... | collective-permute-start | bytes 1572872 | tf_op jit(solution)/shard_map/ppermute | solution.py:364
  66.4 8.9 %collective-permute-start.17 = (bf16[1024,128]{1,0:T(8,128)(2,1)S(1)}, bf16[1024,128]{1,0:T(8,128)(2,1)S(1)}, u32[]{:S(2)}, u32[]{:S(2)}) collective-permute-start(bf16[1024,128]{1,0:T(8,128)(2,1)S(1)} %merge_0.1.refs_0_), channel_id=1, source_target_pairs={{0,4},{1,5},{2,6},{3,7},{4,0},{5,1},{6,2},{7,3},{8,12},{9,13},{10,... | collective-permute-start | bytes 786440 | tf_op jit(solution)/shard_map/ppermute | solution.py:351
  67.8 9.1 %collective-permute-start.15 = (bf16[1024,128]{1,0:T(8,128)(2,1)S(1)}, bf16[1024,128]{1,0:T(8,128)(2,1)S(1)}, u32[]{:S(2)}, u32[]{:S(2)}) collective-permute-start(bf16[1024,128]{1,0:T(8,128)(2,1)S(1)} %merge_0.1.refs_0_), channel_id=1, source_target_pairs={{0,2},{1,3},{2,0},{3,1},{4,6},{5,7},{6,4},{7,5},{8,10},{9,11},{10,... | collective-permute-start | bytes 786440 | tf_op jit(solution)/shard_map/ppermute | solution.py:351
  68.8 11.0 %collective-permute-start.19 = (bf16[1024,128]{1,0:T(8,128)(2,1)S(1)}, bf16[1024,128]{1,0:T(8,128)(2,1)S(1)}, u32[]{:S(2)}, u32[]{:S(2)}) collective-permute-start(bf16[1024,128]{1,0:T(8,128)(2,1)S(1)} %merge_0.1.refs_0_), channel_id=1, source_target_pairs={{0,6},{1,7},{2,4},{3,5},{4,2},{5,3},{6,0},{7,1},{8,14},{9,15},{10,... | collective-permute-start | bytes 786440 | tf_op jit(solution)/shard_map/ppermute | solution.py:351
  79.8 10.1 %collective-permute-start.25 = (bf16[8,144,128]{2,1,0:T(8,128)(2,1)S(1)}, bf16[8,144,128]{2,1,0:T(8,128)(2,1)S(1)}, u32[]{:S(2)}, u32[]{:S(2)}) collective-permute-start(bf16[8,144,128]{2,1,0:T(8,128)(2,1)S(1)} %get-tuple-element.92), channel_id=1, source_target_pairs={{8,0},{16,24},{9,1},{17,25},{10,2},{18,26},{11,3},{19,27},{12,4},{... | collective-permute-start | bytes 884744 | tf_op jit(solution)/shard_map/ppermute | solution.py:370
  81.1 11.6 %collective-permute-start.14 = (bf16[1024,128]{1,0:T(8,128)(2,1)S(1)}, bf16[1024,128]{1,0:T(8,128)(2,1)S(1)}, u32[]{:S(2)}, u32[]{:S(2)}) collective-permute-start(bf16[1024,128]{1,0:T(8,128)(2,1)S(1)} %merge_0.1.refs_0_), channel_id=1, source_target_pairs={{0,1},{1,0},{2,3},{3,2},{4,5},{5,4},{6,7},{7,6},{8,9},{9,8},{10,11... | collective-permute-start | bytes 786440 | tf_op jit(solution)/shard_map/ppermute | solution.py:351
  81.2 12.5 %collective-permute-start.20 = (bf16[1024,128]{1,0:T(8,128)(2,1)S(1)}, bf16[1024,128]{1,0:T(8,128)(2,1)S(1)}, u32[]{:S(2)}, u32[]{:S(2)}) collective-permute-start(bf16[1024,128]{1,0:T(8,128)(2,1)S(1)} %collective-permute-done.19.refs_6_), channel_id=1, source_target_pairs={{0,1},{1,0},{2,3},{3,2},{4,5},{5,4},{6,7},{7,6},{8,9},{9,8},{10,11... | collective-permute-start | bytes 786440 | tf_op jit(solution)/shard_map/ppermute | solution.py:351
  81.7 12.0 %collective-permute-start.18 = (bf16[1024,128]{1,0:T(8,128)(2,1)S(1)}, bf16[1024,128]{1,0:T(8,128)(2,1)S(1)}, u32[]{:S(2)}, u32[]{:S(2)}) collective-permute-start(bf16[1024,128]{1,0:T(8,128)(2,1)S(1)} %collective-permute-done.17.refs_4_), channel_id=1, source_target_pairs={{0,1},{1,0},{2,3},{3,2},{4,5},{5,4},{6,7},{7,6},{8,9},{9,8},{10,11... | collective-permute-start | bytes 786440 | tf_op jit(solution)/shard_map/ppermute | solution.py:351
  90.1 9.5 %collective-permute-start.31 = (bf16[1024,128]{1,0:T(8,128)(2,1)S(1)}, bf16[1024,128]{1,0:T(8,128)(2,1)S(1)}, u32[]{:S(2)}, u32[]{:S(2)}) collective-permute-start(bf16[1024,128]{1,0:T(8,128)(2,1)S(1)} %merge_1.1.refs_8_), channel_id=1, source_target_pairs={{0,6},{1,7},{2,4},{3,5},{4,2},{5,3},{6,0},{7,1},{8,14},{9,15},{10,... | collective-permute-start | bytes 786440 | tf_op jit(solution)/shard_map/ppermute | solution.py:351
  92.0 10.3 %collective-permute-start.29 = (bf16[1024,128]{1,0:T(8,128)(2,1)S(1)}, bf16[1024,128]{1,0:T(8,128)(2,1)S(1)}, u32[]{:S(2)}, u32[]{:S(2)}) collective-permute-start(bf16[1024,128]{1,0:T(8,128)(2,1)S(1)} %merge_1.1.refs_8_), channel_id=1, source_target_pairs={{0,4},{1,5},{2,6},{3,7},{4,0},{5,1},{6,2},{7,3},{8,12},{9,13},{10,... | collective-permute-start | bytes 786440 | tf_op jit(solution)/shard_map/ppermute | solution.py:351
  92.7 9.6 %collective-permute-start.27 = (bf16[1024,128]{1,0:T(8,128)(2,1)S(1)}, bf16[1024,128]{1,0:T(8,128)(2,1)S(1)}, u32[]{:S(2)}, u32[]{:S(2)}) collective-permute-start(bf16[1024,128]{1,0:T(8,128)(2,1)S(1)} %merge_1.1.refs_8_), channel_id=1, source_target_pairs={{0,2},{1,3},{2,0},{3,1},{4,6},{5,7},{6,4},{7,5},{8,10},{9,11},{10,... | collective-permute-start | bytes 786440 | tf_op jit(solution)/shard_map/ppermute | solution.py:351
  93.7 9.1 %collective-permute-start.16 = (bf16[1024,128]{1,0:T(8,128)(2,1)S(1)}, bf16[1024,128]{1,0:T(8,128)(2,1)S(1)}, u32[]{:S(2)}, u32[]{:S(2)}) collective-permute-start(bf16[1024,128]{1,0:T(8,128)(2,1)S(1)} %collective-permute-done.15.refs_2_), channel_id=1, source_target_pairs={{0,1},{1,0},{2,3},{3,2},{4,5},{5,4},{6,7},{7,6},{8,9},{9,8},{10,11... | collective-permute-start | bytes 786440 | tf_op jit(solution)/shard_map/ppermute | solution.py:351
  93.7 9.1 %collective-permute-start.26 = (bf16[1024,128]{1,0:T(8,128)(2,1)S(1)}, bf16[1024,128]{1,0:T(8,128)(2,1)S(1)}, u32[]{:S(2)}, u32[]{:S(2)}) collective-permute-start(bf16[1024,128]{1,0:T(8,128)(2,1)S(1)} %merge_1.1.refs_8_), channel_id=1, source_target_pairs={{0,1},{1,0},{2,3},{3,2},{4,5},{5,4},{6,7},{7,6},{8,9},{9,8},{10,11... | collective-permute-start | bytes 786440 | tf_op jit(solution)/shard_map/ppermute | solution.py:351
  (15 other events, 113.8 us)

commit v20 on v19

--- a/solution.py
+++ b/solution.py
@@ -424,7 +424,7 @@
             sources = ([owns[c]] if step == 0 else []) + over[c]
             even, odd = over[c]
             if even is not None and odd is not None:
-                even, odd = after((even, odd), guest[c] if c else (even, odd))
+                even, odd = after((even, odd), (even, odd))
             over[c] = [exchange(odd, 0, step + 2), exchange(even, 1, step + 2)]
             state[c] = run(c, step, sources)
 
@@ -434,7 +434,7 @@
         found = run(c, last, ([] if last else [owns[c]]) + after(over[c], sent))
         if relay:
             outer = ((pb == 0) | (pb == n_pb - 1)).astype(jnp.int32)[None]
-            out = merge(outer, found[:3], outward(after(found[3], far)), f"merge_{c}")
+            out = merge(outer, found[:3], after(outward(after(found[3], far)), guest[c + 1 :]), f"merge_{c}")
         else:
             out = found[0]
         mine = [out] + [swap(out, k) for k in range(2, n_ka, 2)]

time: 107 us -> 109 us (1.019)
  starting transfers between devices: 39.7 us -> 43.9 us
  waiting for transfers between devices: 38.3 us -> 36 us
    ppermute x3, starting transfers between devices: 9.68 us -> 13.2 us  [inward(): return lax.ppermute(x, 'pb', [(0, 1), (n_pb - 1, n_pb - 2)])]
    ppermute x3, waiting for transfers between devices: 7.34 us -> 4.79 us  [inward(): return lax.ppermute(x, 'pb', [(0, 1), (n_pb - 1, n_pb - 2)])]
  transfers between devices with their start and end apart: 33 -> 33, of which waited for: 15 -> 15; matrix products, arithmetic and copies ran while one was open for 3% -> 3% of each run, Pallas kernels for 18% -> 17%
where the time goes in v20:
time: 109 us; the launch traced here: 108 us
  starting transfers between devices  43.9 us (40%)
  waiting for transfers between devices  36 us (33%)
  Pallas kernels  23.2 us (21%)
  local copies, waits for them, and re-layouts  4.69 us (4%)
    ppermute x22, waiting for transfers between devices, swap(): return lax.ppermute(x, 'ka', [(i, i ^ k) for i in range(n_ka)])  21.5 us
    ppermute x22, starting transfers between devices, swap(): return lax.ppermute(x, 'ka', [(i, i ^ k) for i in range(n_ka)])  16.9 us
    ppermute x3, starting transfers between devices, inward(): return lax.ppermute(x, 'pb', [(0, 1), (n_pb - 1, n_pb - 2)])  13.2 us
    ppermute x6, starting transfers between devices, exchange(): return lax.ppermute(x, 'pb', found) if found else None  11.2 us
    pallas_call x4, Pallas kernels, attend(): pl.pallas_call(functools.partial(attend_kernel, n_src, entry, first, mode...  11 us
    ppermute x2, waiting for transfers between devices, outward(): return lax.ppermute(x, 'pb', [(1, 0), (n_pb - 2, n_pb - 1)])  9.76 us
    pallas_call x2, Pallas kernels, pack(): pl.pallas_call(functools.partial(pack_kernel, n_ka, heads, c, len(masks))...  5.34 us
    ppermute x3, waiting for transfers between devices, inward(): return lax.ppermute(x, 'pb', [(0, 1), (n_pb - 1, n_pb - 2)])  4.79 us
  transfers between devices with their start and end apart: 33, of which 15 were waited for; matrix products, arithmetic and copies ran while one was open for 3% of the time, Pallas kernels for 17%

profile of v20, /device:TPU:0, one launch (start us, length us, event | category | flops | bytes accessed | tf_op | source)
XLA Modules:
  0.0 108.4 jit_solution(4048245552313405550)
XLA Ops:
  0.0 2.3 %pack_0.1 = (bf16[2,256,128]{2,1,0:T(8,128)(2,1)}, bf16[2,256,128]{2,1,0:T(8,128)(2,1)}, bf16[2,256,128]{2,1,0:T(8,128)(2,1)}, bf16[2,256,128]{2,1,0:T(8,128)(2,1)}) custom-call(s32[1]{0:T(128)} %bitcast.me_ref, bf16[128,2048]{1,0:T(8,128)(2,1)} %refs_2_.1, bf16[128,2048]{1,0:T(8,128)(2,1)} %refs_3_.1), custom_call_target="tpu_custom_call" | custom-call | bytes 262144 | tf_op jit(solution)/shard_map/pack_0/pallas_call | solution.py:77
  2.3 3.0 %collective-permute-start = (bf16[2,256,128]{2,1,0:T(8,128)(2,1)}, bf16[2,256,128]{2,1,0:T(8,128)(2,1)S(1)}, u32[]{:S(2)}, u32[]{:S(2)}) collective-permute-start(bf16[2,256,128]{2,1,0:T(8,128)(2,1)} %get-tuple-element.51), channel_id=1, source_target_pairs={{0,2},{1,3},{2,0},{3,1},{4,6},{5,7},{6,4},{7,5},{8,10},{9,11},{10,... | collective-permute-start | bytes 393224 | tf_op jit(solution)/shard_map/ppermute | solution.py:351
  6.9 3.9 %collective-permute-start.3 = (s32[4,8]{1,0:T(4,128)}, s32[4,8]{1,0:T(4,128)S(1)}, u32[]{:S(2)}, u32[]{:S(2)}) collective-permute-start(s32[4,8]{1,0:T(4,128)} %bitcast.12), channel_id=1, source_target_pairs={{0,8},{24,16},{1,9},{25,17},{2,10},{26,18},{3,11},{27,19},{4,12},{... | collective-permute-start | bytes 392 | tf_op jit(solution)/shard_map/ppermute | solution.py:367
  10.8 2.0 %turn.1 = (bf16[8,128,128]{2,1,0:T(8,128)(2,1)}, bf16[8,128,128]{2,1,0:T(8,128)(2,1)}) custom-call(s32[1]{0:T(128)} %bitcast.me_ref, bf16[1024,2048]{1,0:T(8,128)(2,1)} %q_all.1), custom_call_target="tpu_custom_call" | custom-call | bytes 131072 | tf_op jit(solution)/shard_map/turn/pallas_call | solution.py:105
  15.8 4.4 %collective-permute-start.8 = (bf16[8,2,128,128]{3,2,1,0:T(8,128)(2,1)S(1)}, bf16[8,2,128,128]{3,2,1,0:T(8,128)(2,1)S(1)}, u32[]{:S(2)}, u32[]{:S(2)}) collective-permute-start(bf16[8,2,128,128]{3,2,1,0:T(8,128)(2,1)S(1)} %bitcast.10), channel_id=1, source_target_pairs={{0,8},{8,0},{16,24},{24,16},{1,9},{9,1},{17,25},{25,17},{2,10},{10... | collective-permute-start | bytes 1572872 | tf_op jit(solution)/shard_map/ppermute | solution.py:364
  20.2 3.0 %pack_1.1 = (bf16[2,288,128]{2,1,0:T(8,128)(2,1)}, bf16[2,288,128]{2,1,0:T(8,128)(2,1)}, bf16[2,288,128]{2,1,0:T(8,128)(2,1)}, bf16[2,288,128]{2,1,0:T(8,128)(2,1)}) custom-call(s32[1]{0:T(128)} %bitcast.me_ref, s32[4,8]{1,0:T(4,128)} %bitcast.13, s32[4,8]{1,0:T(4,128)} %copy-done.5, bf16[128,2048]{1,0:T(8,128)(2,1)} %refs_2_.1, bf16[128,2048]{1,0:T(8,128)(2,1)} %refs_3_.1), custom_call_target="tpu_custom_call" | custom-call | bytes 262144 | tf_op jit(solution)/shard_map/pack_1/pallas_call | solution.py:77
  29.2 2.5 %collective-permute-done.5 = bf16[2,288,128]{2,1,0:T(8,128)(2,1)S(1)} collective-permute-done((bf16[2,288,128]{2,1,0:T(8,128)(2,1)}, bf16[2,288,128]{2,1,0:T(8,128)(2,1)S(1)}, u32[]{:S(2)}, u32[]{:S(2)}) %collective-permute-start.5) | collective-permute-done | bytes 147488 | tf_op jit(solution)/shard_map/ppermute | solution.py:351
  31.7 1.9 %collective-permute-done.6 = bf16[2,288,128]{2,1,0:T(8,128)(2,1)S(1)} collective-permute-done((bf16[2,288,128]{2,1,0:T(8,128)(2,1)}, bf16[2,288,128]{2,1,0:T(8,128)(2,1)S(1)}, u32[]{:S(2)}, u32[]{:S(2)}) %collective-permute-start.6) | collective-permute-done | bytes 147488 | tf_op jit(solution)/shard_map/ppermute | solution.py:351
  34.9 2.2 %collective-permute-start.11 = (bf16[8,128,128]{2,1,0:T(8,128)(2,1)S(1)}, bf16[8,128,128]{2,1,0:T(8,128)(2,1)S(1)}, u32[]{:S(2)}, u32[]{:S(2)}) collective-permute-start(bf16[8,128,128]{2,1,0:T(8,128)(2,1)S(1)} %copy-done.1), channel_id=1, source_target_pairs={{0,8},{24,16},{1,9},{25,17},{2,10},{26,18},{3,11},{27,19},{4,12},{... | collective-permute-start | bytes 786440 | tf_op jit(solution)/shard_map/ppermute | solution.py:367
  38.8 2.4 %plan.1 = (s32[2]{0:T(128)S(1)}, s32[432]{0:T(512)S(1)}, s32[176]{0:T(256)S(1)}) custom-call(s32[1]{0:T(128)} %bitcast.2.pb_ref, s32[256]{0:T(256)S(1)} %reshape.24.refs_0_, s32[256]{0:T(256)S(1)} %reshape.26.refs_1_), custom_call_target="tpu_custom_call" | custom-call | tf_op jit(solution)/shard_map/plan/pallas_call | solution.py:159
  41.2 2.1 %collective-permute-done.11.refs_0_ = bf16[8,128,128]{2,1,0:T(8,128)(2,1)S(1)} collective-permute-done((bf16[8,128,128]{2,1,0:T(8,128)(2,1)S(1)}, bf16[8,128,128]{2,1,0:T(8,128)(2,1)S(1)}, u32[]{:S(2)}, u32[]{:S(2)}) %collective-permute-start.11) | collective-permute-done | bytes 262176 | tf_op jit(solution)/shard_map/ppermute | solution.py:367
  43.3 2.5 %collective-permute-start.22 = (bf16[8,2,128,128]{3,2,1,0:T(8,128)(2,1)S(1)}, bf16[8,2,128,128]{3,2,1,0:T(8,128)(2,1)S(1)}, u32[]{:S(2)}, u32[]{:S(2)}) collective-permute-start(bf16[8,2,128,128]{3,2,1,0:T(8,128)(2,1)S(1)} %bitcast.6), channel_id=1, source_target_pairs={{0,8},{8,0},{16,24},{24,16},{1,9},{9,1},{17,25},{25,17},{2,10},{10... | collective-permute-start | bytes 1572872 | tf_op jit(solution)/shard_map/ppermute | solution.py:364
  46.5 3.4 %attend_0_0.1 = (f32[16,1,128]{2,1,0:T(1,128)S(1)}, f32[16,1,128]{2,1,0:T(1,128)S(1)}, f32[16,128,128]{2,1,0:T(8,128)S(1)}) custom-call(s32[2]{0:T(128)S(1)} %get-tuple-element.69.count_ref, s32[432]{0:T(512)S(1)} %get-tuple-element.73.live_ref, bf16[8,128,128]{2,1,0:T(8,128)(2,1)S(1)} %copy-done.1, ...), custom_call_target="tpu_custom_call" | custom-call | bytes 16384 | tf_op jit(solution)/shard_map/attend_0_0/pallas_call | solution.py:273
  49.9 2.4 %attend_0_1.1 = (f32[16,1,128]{2,1,0:T(1,128)S(1)}, f32[16,1,128]{2,1,0:T(1,128)S(1)}, f32[16,128,128]{2,1,0:T(8,128)S(1)}, bf16[8,144,128]{2,1,0:T(8,128)(2,1)}) custom-call(s32[2]{0:T(128)S(1)} %get-tuple-element.69.count_ref, s32[176]{0:T(256)S(1)} %get-tuple-element.70.live_ref, bf16[8,128,128]{2,1,0:T(8,128)(2,1)S(1)} %copy-done.1, ...), custom_call_target="tpu_custom_call" | custom-call | bytes 16384 | tf_op jit(solution)/shard_map/attend_0_1/pallas_call | solution.py:273
  53.7 7.1 %collective-permute-start.14 = (bf16[8,128,128]{2,1,0:T(8,128)(2,1)S(1)}, bf16[8,128,128]{2,1,0:T(8,128)(2,1)S(1)}, u32[]{:S(2)}, u32[]{:S(2)}) collective-permute-start(bf16[8,128,128]{2,1,0:T(8,128)(2,1)S(1)} %copy-done), channel_id=1, source_target_pairs={{0,8},{24,16},{1,9},{25,17},{2,10},{26,18},{3,11},{27,19},{4,12},{... | collective-permute-start | bytes 786440 | tf_op jit(solution)/shard_map/ppermute | solution.py:367
  63.1 2.7 %collective-permute-done.14.refs_0_ = bf16[8,128,128]{2,1,0:T(8,128)(2,1)S(1)} collective-permute-done((bf16[8,128,128]{2,1,0:T(8,128)(2,1)S(1)}, bf16[8,128,128]{2,1,0:T(8,128)(2,1)S(1)}, u32[]{:S(2)}, u32[]{:S(2)}) %collective-permute-start.14) | collective-permute-done | bytes 262176 | tf_op jit(solution)/shard_map/ppermute | solution.py:367
  70.6 3.4 %attend_1_0.1 = (f32[16,1,128]{2,1,0:T(1,128)S(1)}, f32[16,1,128]{2,1,0:T(1,128)S(1)}, f32[16,128,128]{2,1,0:T(8,128)S(1)}) custom-call(s32[2]{0:T(128)S(1)} %get-tuple-element.69.count_ref, s32[432]{0:T(512)S(1)} %get-tuple-element.73.live_ref, bf16[8,128,128]{2,1,0:T(8,128)(2,1)S(1)} %copy-done, bf16[8,128,128]{2,1,0:T(8,128)(2,1)S(1)} %collective-permute-done.14.refs_0_, ...), custom_call_target="tpu_custom_call" | custom-call | bytes 16384 | tf_op jit(solution)/shard_map/attend_1_0/pallas_call | solution.py:273
  74.4 2.1 %collective-permute-done.16.refs_2_ = bf16[1024,128]{1,0:T(8,128)(2,1)S(1)} collective-permute-done((bf16[1024,128]{1,0:T(8,128)(2,1)S(1)}, bf16[1024,128]{1,0:T(8,128)(2,1)S(1)}, u32[]{:S(2)}, u32[]{:S(2)}) %collective-permute-start.16) | collective-permute-done | bytes 262176 | tf_op jit(solution)/shard_map/ppermute | solution.py:351
  76.5 1.7 %attend_1_1.1 = (f32[16,1,128]{2,1,0:T(1,128)S(1)}, f32[16,1,128]{2,1,0:T(1,128)S(1)}, f32[16,128,128]{2,1,0:T(8,128)S(1)}, bf16[8,144,128]{2,1,0:T(8,128)(2,1)S(1)}) custom-call(s32[2]{0:T(128)S(1)} %get-tuple-element.69.count_ref, s32[176]{0:T(256)S(1)} %get-tuple-element.70.live_ref, bf16[8,128,128]{2,1,0:T(8,128)(2,1)S(1)} %copy-done, ...), custom_call_target="tpu_custom_call" | custom-call | bytes 16384 | tf_op jit(solution)/shard_map/attend_1_1/pallas_call | solution.py:273
  81.4 9.8 %collective-permute-done.25.part_ref = bf16[8,144,128]{2,1,0:T(8,128)(2,1)S(1)} collective-permute-done((bf16[8,144,128]{2,1,0:T(8,128)(2,1)S(1)}, bf16[8,144,128]{2,1,0:T(8,128)(2,1)S(1)}, u32[]{:S(2)}, u32[]{:S(2)}) %collective-permute-start.25) | collective-permute-done | bytes 294944 | tf_op jit(solution)/shard_map/ppermute | solution.py:370
  91.3 1.8 %collective-permute-start.31 = (bf16[1024,128]{1,0:T(8,128)(2,1)S(1)}, bf16[1024,128]{1,0:T(8,128)(2,1)S(1)}, u32[]{:S(2)}, u32[]{:S(2)}) collective-permute-start(bf16[1024,128]{1,0:T(8,128)(2,1)S(1)} %merge_1.1.refs_8_), channel_id=1, source_target_pairs={{0,6},{1,7},{2,4},{3,5},{4,2},{5,3},{6,0},{7,1},{8,14},{9,15},{10,... | collective-permute-start | bytes 786440 | tf_op jit(solution)/shard_map/ppermute | solution.py:351
  95.4 6.1 %collective-permute-done.31.refs_14_ = bf16[1024,128]{1,0:T(8,128)(2,1)S(1)} collective-permute-done((bf16[1024,128]{1,0:T(8,128)(2,1)S(1)}, bf16[1024,128]{1,0:T(8,128)(2,1)S(1)}, u32[]{:S(2)}, u32[]{:S(2)}) %collective-permute-start.31) | collective-permute-done | bytes 262176 | tf_op jit(solution)/shard_map/ppermute | solution.py:351
  101.6 2.8 %collective-permute-done.29.refs_12_ = bf16[1024,128]{1,0:T(8,128)(2,1)S(1)} collective-permute-done((bf16[1024,128]{1,0:T(8,128)(2,1)S(1)}, bf16[1024,128]{1,0:T(8,128)(2,1)S(1)}, u32[]{:S(2)}, u32[]{:S(2)}) %collective-permute-start.29) | collective-permute-done | bytes 262176 | tf_op jit(solution)/shard_map/ppermute | solution.py:351
  106.2 2.1 %place.1 = bf16[1024,2048]{1,0:T(8,128)(2,1)} custom-call(s32[1]{0:T(128)} %bitcast.me_ref, bf16[1024,128]{1,0:T(8,128)(2,1)S(1)} %merge_0.1.refs_0_, bf16[1024,128]{1,0:T(8,128)(2,1)S(1)} %collective-permute-done.15.refs_1_, bf16[1024,128]{1,0:T(8,128)(2,1)S(1)} %collective-permute-done.16.refs_2_, bf16[1024,128]{1,0:T(8,128)(2,1)S(1)} %collective-permute-done.17.refs_3_, ...), custom_call_target="tpu_custom_call" | custom-call | tf_op jit(solution)/shard_map/place/pallas_call | solution.py:330
  (89 shorter events, 30.3 us)
Async XLA Ops:
  2.3 10.5 %collective-permute-start = (bf16[2,256,128]{2,1,0:T(8,128)(2,1)}, bf16[2,256,128]{2,1,0:T(8,128)(2,1)S(1)}, u32[]{:S(2)}, u32[]{:S(2)}) collective-permute-start(bf16[2,256,128]{2,1,0:T(8,128)(2,1)} %get-tuple-element.51), channel_id=1, source_target_pairs={{0,2},{1,3},{2,0},{3,1},{4,6},{5,7},{6,4},{7,5},{8,10},{9,11},{10,... | collective-permute-start | bytes 393224 | tf_op jit(solution)/shard_map/ppermute | solution.py:351
  5.3 8.0 %collective-permute-start.1 = (bf16[2,256,128]{2,1,0:T(8,128)(2,1)}, bf16[2,256,128]{2,1,0:T(8,128)(2,1)S(1)}, u32[]{:S(2)}, u32[]{:S(2)}) collective-permute-start(bf16[2,256,128]{2,1,0:T(8,128)(2,1)} %get-tuple-element.52), channel_id=1, source_target_pairs={{0,4},{1,5},{2,6},{3,7},{4,0},{5,1},{6,2},{7,3},{8,12},{9,13},{10,... | collective-permute-start | bytes 393224 | tf_op jit(solution)/shard_map/ppermute | solution.py:351
  15.1 19.7 %collective-permute-start.9 = (bf16[8,2,128,128]{3,2,1,0:T(8,128)(2,1)S(1)}, bf16[8,2,128,128]{3,2,1,0:T(8,128)(2,1)S(1)}, u32[]{:S(2)}, u32[]{:S(2)}) collective-permute-start(bf16[8,2,128,128]{3,2,1,0:T(8,128)(2,1)S(1)} %bitcast.9), channel_id=1, source_target_pairs={{8,16},{16,8},{9,17},{17,9},{10,18},{18,10},{11,19},{19,11},{12,20... | collective-permute-start | bytes 1572872 | tf_op jit(solution)/shard_map/ppermute | solution.py:364
  15.8 19.0 %collective-permute-start.8 = (bf16[8,2,128,128]{3,2,1,0:T(8,128)(2,1)S(1)}, bf16[8,2,128,128]{3,2,1,0:T(8,128)(2,1)S(1)}, u32[]{:S(2)}, u32[]{:S(2)}) collective-permute-start(bf16[8,2,128,128]{3,2,1,0:T(8,128)(2,1)S(1)} %bitcast.10), channel_id=1, source_target_pairs={{0,8},{8,0},{16,24},{24,16},{1,9},{9,1},{17,25},{25,17},{2,10},{10... | collective-permute-start | bytes 1572872 | tf_op jit(solution)/shard_map/ppermute | solution.py:364
  26.2 7.4 %collective-permute-start.6 = (bf16[2,288,128]{2,1,0:T(8,128)(2,1)}, bf16[2,288,128]{2,1,0:T(8,128)(2,1)S(1)}, u32[]{:S(2)}, u32[]{:S(2)}) collective-permute-start(bf16[2,288,128]{2,1,0:T(8,128)(2,1)} %get-tuple-element.66), channel_id=1, source_target_pairs={{0,4},{1,5},{2,6},{3,7},{4,0},{5,1},{6,2},{7,3},{8,12},{9,13},{10,... | collective-permute-start | bytes 442376 | tf_op jit(solution)/shard_map/ppermute | solution.py:351
  34.9 8.4 %collective-permute-start.11 = (bf16[8,128,128]{2,1,0:T(8,128)(2,1)S(1)}, bf16[8,128,128]{2,1,0:T(8,128)(2,1)S(1)}, u32[]{:S(2)}, u32[]{:S(2)}) collective-permute-start(bf16[8,128,128]{2,1,0:T(8,128)(2,1)S(1)} %copy-done.1), channel_id=1, source_target_pairs={{0,8},{24,16},{1,9},{25,17},{2,10},{26,18},{3,11},{27,19},{4,12},{... | collective-permute-start | bytes 786440 | tf_op jit(solution)/shard_map/ppermute | solution.py:367
  37.1 12.8 %collective-permute-start.12 = (bf16[8,2,128,128]{3,2,1,0:T(8,128)(2,1)S(1)}, bf16[8,2,128,128]{3,2,1,0:T(8,128)(2,1)}, u32[]{:S(2)}, u32[]{:S(2)}) collective-permute-start(bf16[8,2,128,128]{3,2,1,0:T(8,128)(2,1)S(1)} %collective-permute-done.8.refs_2_), channel_id=1, source_target_pairs={{8,16},{16,8},{9,17},{17,9},{10,18},{18,10},{11,19},{19,11},{12,20... | collective-permute-start | bytes 1572872 | tf_op jit(solution)/shard_map/ppermute | solution.py:364
  43.3 17.5 %collective-permute-start.22 = (bf16[8,2,128,128]{3,2,1,0:T(8,128)(2,1)S(1)}, bf16[8,2,128,128]{3,2,1,0:T(8,128)(2,1)S(1)}, u32[]{:S(2)}, u32[]{:S(2)}) collective-permute-start(bf16[8,2,128,128]{3,2,1,0:T(8,128)(2,1)S(1)} %bitcast.6), channel_id=1, source_target_pairs={{0,8},{8,0},{16,24},{24,16},{1,9},{9,1},{17,25},{25,17},{2,10},{10... | collective-permute-start | bytes 1572872 | tf_op jit(solution)/shard_map/ppermute | solution.py:364
  45.8 15.0 %collective-permute-start.23 = (bf16[8,2,128,128]{3,2,1,0:T(8,128)(2,1)S(1)}, bf16[8,2,128,128]{3,2,1,0:T(8,128)(2,1)S(1)}, u32[]{:S(2)}, u32[]{:S(2)}) collective-permute-start(bf16[8,2,128,128]{3,2,1,0:T(8,128)(2,1)S(1)} %bitcast.7), channel_id=1, source_target_pairs={{8,16},{16,8},{9,17},{17,9},{10,18},{18,10},{11,19},{19,11},{12,20... | collective-permute-start | bytes 1572872 | tf_op jit(solution)/shard_map/ppermute | solution.py:364
  52.4 13.4 %collective-permute-start.13 = (bf16[8,144,128]{2,1,0:T(8,128)(2,1)}, bf16[8,144,128]{2,1,0:T(8,128)(2,1)S(1)}, u32[]{:S(2)}, u32[]{:S(2)}) collective-permute-start(bf16[8,144,128]{2,1,0:T(8,128)(2,1)} %get-tuple-element.80), channel_id=1, source_target_pairs={{8,0},{16,24},{9,1},{17,25},{10,2},{18,26},{11,3},{19,27},{12,4},{... | collective-permute-start | bytes 884744 | tf_op jit(solution)/shard_map/ppermute | solution.py:370
  53.7 12.1 %collective-permute-start.14 = (bf16[8,128,128]{2,1,0:T(8,128)(2,1)S(1)}, bf16[8,128,128]{2,1,0:T(8,128)(2,1)S(1)}, u32[]{:S(2)}, u32[]{:S(2)}) collective-permute-start(bf16[8,128,128]{2,1,0:T(8,128)(2,1)S(1)} %copy-done), channel_id=1, source_target_pairs={{0,8},{24,16},{1,9},{25,17},{2,10},{26,18},{3,11},{27,19},{4,12},{... | collective-permute-start | bytes 786440 | tf_op jit(solution)/shard_map/ppermute | solution.py:367
  61.6 14.9 %collective-permute-start.24 = (bf16[8,2,128,128]{3,2,1,0:T(8,128)(2,1)S(1)}, bf16[8,2,128,128]{3,2,1,0:T(8,128)(2,1)}, u32[]{:S(2)}, u32[]{:S(2)}) collective-permute-start(bf16[8,2,128,128]{3,2,1,0:T(8,128)(2,1)S(1)} %collective-permute-done.22.refs_2_), channel_id=1, source_target_pairs={{8,16},{16,8},{9,17},{17,9},{10,18},{18,10},{11,19},{19,11},{12,20... | collective-permute-start | bytes 1572872 | tf_op jit(solution)/shard_map/ppermute | solution.py:364
  66.0 8.4 %collective-permute-start.18 = (bf16[1024,128]{1,0:T(8,128)(2,1)S(1)}, bf16[1024,128]{1,0:T(8,128)(2,1)S(1)}, u32[]{:S(2)}, u32[]{:S(2)}) collective-permute-start(bf16[1024,128]{1,0:T(8,128)(2,1)S(1)} %merge_0.1.refs_0_), channel_id=1, source_target_pairs={{0,4},{1,5},{2,6},{3,7},{4,0},{5,1},{6,2},{7,3},{8,12},{9,13},{10,... | collective-permute-start | bytes 786440 | tf_op jit(solution)/shard_map/ppermute | solution.py:351
  67.4 9.1 %collective-permute-start.16 = (bf16[1024,128]{1,0:T(8,128)(2,1)S(1)}, bf16[1024,128]{1,0:T(8,128)(2,1)S(1)}, u32[]{:S(2)}, u32[]{:S(2)}) collective-permute-start(bf16[1024,128]{1,0:T(8,128)(2,1)S(1)} %merge_0.1.refs_0_), channel_id=1, source_target_pairs={{0,2},{1,3},{2,0},{3,1},{4,6},{5,7},{6,4},{7,5},{8,10},{9,11},{10,... | collective-permute-start | bytes 786440 | tf_op jit(solution)/shard_map/ppermute | solution.py:351
  68.4 11.0 %collective-permute-start.20 = (bf16[1024,128]{1,0:T(8,128)(2,1)S(1)}, bf16[1024,128]{1,0:T(8,128)(2,1)S(1)}, u32[]{:S(2)}, u32[]{:S(2)}) collective-permute-start(bf16[1024,128]{1,0:T(8,128)(2,1)S(1)} %merge_0.1.refs_0_), channel_id=1, source_target_pairs={{0,6},{1,7},{2,4},{3,5},{4,2},{5,3},{6,0},{7,1},{8,14},{9,15},{10,... | collective-permute-start | bytes 786440 | tf_op jit(solution)/shard_map/ppermute | solution.py:351
  79.4 11.7 %collective-permute-start.25 = (bf16[8,144,128]{2,1,0:T(8,128)(2,1)S(1)}, bf16[8,144,128]{2,1,0:T(8,128)(2,1)S(1)}, u32[]{:S(2)}, u32[]{:S(2)}) collective-permute-start(bf16[8,144,128]{2,1,0:T(8,128)(2,1)S(1)} %get-tuple-element.94), channel_id=1, source_target_pairs={{8,0},{16,24},{9,1},{17,25},{10,2},{18,26},{11,3},{19,27},{12,4},{... | collective-permute-start | bytes 884744 | tf_op jit(solution)/shard_map/ppermute | solution.py:370
  80.7 13.1 %collective-permute-start.15 = (bf16[1024,128]{1,0:T(8,128)(2,1)S(1)}, bf16[1024,128]{1,0:T(8,128)(2,1)S(1)}, u32[]{:S(2)}, u32[]{:S(2)}) collective-permute-start(bf16[1024,128]{1,0:T(8,128)(2,1)S(1)} %merge_0.1.refs_0_), channel_id=1, source_target_pairs={{0,1},{1,0},{2,3},{3,2},{4,5},{5,4},{6,7},{7,6},{8,9},{9,8},{10,11... | collective-permute-start | bytes 786440 | tf_op jit(solution)/shard_map/ppermute | solution.py:351
  80.8 14.1 %collective-permute-start.21 = (bf16[1024,128]{1,0:T(8,128)(2,1)S(1)}, bf16[1024,128]{1,0:T(8,128)(2,1)S(1)}, u32[]{:S(2)}, u32[]{:S(2)}) collective-permute-start(bf16[1024,128]{1,0:T(8,128)(2,1)S(1)} %collective-permute-done.20.refs_6_), channel_id=1, source_target_pairs={{0,1},{1,0},{2,3},{3,2},{4,5},{5,4},{6,7},{7,6},{8,9},{9,8},{10,11... | collective-permute-start | bytes 786440 | tf_op jit(solution)/shard_map/ppermute | solution.py:351
  81.3 13.6 %collective-permute-start.19 = (bf16[1024,128]{1,0:T(8,128)(2,1)S(1)}, bf16[1024,128]{1,0:T(8,128)(2,1)S(1)}, u32[]{:S(2)}, u32[]{:S(2)}) collective-permute-start(bf16[1024,128]{1,0:T(8,128)(2,1)S(1)} %collective-permute-done.18.refs_4_), channel_id=1, source_target_pairs={{0,1},{1,0},{2,3},{3,2},{4,5},{5,4},{6,7},{7,6},{8,9},{9,8},{10,11... | collective-permute-start | bytes 786440 | tf_op jit(solution)/shard_map/ppermute | solution.py:351
  91.3 10.2 %collective-permute-start.31 = (bf16[1024,128]{1,0:T(8,128)(2,1)S(1)}, bf16[1024,128]{1,0:T(8,128)(2,1)S(1)}, u32[]{:S(2)}, u32[]{:S(2)}) collective-permute-start(bf16[1024,128]{1,0:T(8,128)(2,1)S(1)} %merge_1.1.refs_8_), channel_id=1, source_target_pairs={{0,6},{1,7},{2,4},{3,5},{4,2},{5,3},{6,0},{7,1},{8,14},{9,15},{10,... | collective-permute-start | bytes 786440 | tf_op jit(solution)/shard_map/ppermute | solution.py:351
  93.2 11.1 %collective-permute-start.29 = (bf16[1024,128]{1,0:T(8,128)(2,1)S(1)}, bf16[1024,128]{1,0:T(8,128)(2,1)S(1)}, u32[]{:S(2)}, u32[]{:S(2)}) collective-permute-start(bf16[1024,128]{1,0:T(8,128)(2,1)S(1)} %merge_1.1.refs_8_), channel_id=1, source_target_pairs={{0,4},{1,5},{2,6},{3,7},{4,0},{5,1},{6,2},{7,3},{8,12},{9,13},{10,... | collective-permute-start | bytes 786440 | tf_op jit(solution)/shard_map/ppermute | solution.py:351
  93.9 10.4 %collective-permute-start.27 = (bf16[1024,128]{1,0:T(8,128)(2,1)S(1)}, bf16[1024,128]{1,0:T(8,128)(2,1)S(1)}, u32[]{:S(2)}, u32[]{:S(2)}) collective-permute-start(bf16[1024,128]{1,0:T(8,128)(2,1)S(1)} %merge_1.1.refs_8_), channel_id=1, source_target_pairs={{0,2},{1,3},{2,0},{3,1},{4,6},{5,7},{6,4},{7,5},{8,10},{9,11},{10,... | collective-permute-start | bytes 786440 | tf_op jit(solution)/shard_map/ppermute | solution.py:351
  94.9 9.9 %collective-permute-start.17 = (bf16[1024,128]{1,0:T(8,128)(2,1)S(1)}, bf16[1024,128]{1,0:T(8,128)(2,1)S(1)}, u32[]{:S(2)}, u32[]{:S(2)}) collective-permute-start(bf16[1024,128]{1,0:T(8,128)(2,1)S(1)} %collective-permute-done.16.refs_2_), channel_id=1, source_target_pairs={{0,1},{1,0},{2,3},{3,2},{4,5},{5,4},{6,7},{7,6},{8,9},{9,8},{10,11... | collective-permute-start | bytes 786440 | tf_op jit(solution)/shard_map/ppermute | solution.py:351
  94.9 9.9 %collective-permute-start.26 = (bf16[1024,128]{1,0:T(8,128)(2,1)S(1)}, bf16[1024,128]{1,0:T(8,128)(2,1)S(1)}, u32[]{:S(2)}, u32[]{:S(2)}) collective-permute-start(bf16[1024,128]{1,0:T(8,128)(2,1)S(1)} %merge_1.1.refs_8_), channel_id=1, source_target_pairs={{0,1},{1,0},{2,3},{3,2},{4,5},{5,4},{6,7},{7,6},{8,9},{9,8},{10,11... | collective-permute-start | bytes 786440 | tf_op jit(solution)/shard_map/ppermute | solution.py:351
  (15 other events, 120.5 us)
